TPU v7x, 32 devices: a whole 2x2x4 slice. The times are simulated.
32 devices in a mesh: fsdp: 4 (over z), proto: 4 (over y, core), dp: 2 (over x).
Axes of the slice: x: 2, y: 2, z: 4, core: 2. Of those that a mesh axis runs over, the one named last changes fastest.
Arguments:
- teacher_weight: float32 [192, 65536], P(None, ('proto', 'fsdp')), may hold values from -0.4375 to 0.4375
- student_weight: float32 [192, 65536], P(None, ('proto', 'fsdp')), may hold values from -0.4375 to 0.4375
- teacher_feats: bfloat16 [2, 1024, 192], P('dp', 'fsdp'), may hold values from -6 to 6
- student_feats: bfloat16 [2, 1024, 192], P('dp', 'fsdp'), may hold values from -6 to 6
- pairing: int32 [2, 1024], P('dp', 'fsdp'), may hold values from 0 to 255
- center: float32 [65536], P('proto'), may hold values from -10.3 to -3.7
Outputs:
- teacher_new: float32 [192, 65536], P(None, ('proto', 'fsdp'))
- student_grad: float32 [192, 65536], P(None, ('proto', 'fsdp', 'dp'))
Inputs may be any that keep to these rules, and one draw needn't show every extreme that they name: pairing[v, r] indexes a crop of the other view in the same block of 256 crops.
All inputs are finite; a program needn't handle non-finite values.
Results may differ from a plain program's by a relative error of at most 0.012.
Values may be sent and summed in bfloat16 or wider, within the bound.
No kernel may reach another device: no remote copies, remote signals or barrier semaphores. Data moves between devices by JAX's collectives and lax.ppermute only.
A program may use at most 128 MiB of HBM per device.

v0:
```python
import jax
import jax.numpy as jnp
from jax import lax
from jax.sharding import PartitionSpec as P


def from_partner(shard, axis, apart):
    return lax.ppermute(shard, axis, [(i, i ^ 1 << apart) for i in range(lax.axis_size(axis))])


def normalize_cols(weights):
    return weights * lax.rsqrt(jnp.sum(weights * weights, axis=0, keepdims=True) + 1e-06)


def normalize_rows(feats):
    values = feats.astype(jnp.float32)
    return values * lax.rsqrt(jnp.sum(values * values, axis=-1, keepdims=True) + 1e-06)


def shards(teacher_weight, student_weight, teacher_feats, student_feats, pairing, center):
    teacher_new = 0.994 * teacher_weight + 0.006 * student_weight
    w_teacher = normalize_cols(teacher_new).astype(jnp.bfloat16)
    w_student = normalize_cols(student_weight).astype(jnp.bfloat16)
    z_teacher = normalize_rows(teacher_feats[0]).astype(jnp.bfloat16)
    z_student = normalize_rows(student_feats[0]).astype(jnp.bfloat16)
    swapped = from_partner(z_teacher, "dp", 0)
    paired = jnp.take(swapped, pairing[0], axis=0)
    logits_t = jnp.dot(
        paired,
        lax.all_gather(w_teacher, "fsdp", axis=1, tiled=True),
        preferred_element_type=jnp.float32,
    )
    logits_s = jnp.dot(
        z_student,
        lax.all_gather(w_student, "fsdp", axis=1, tiled=True),
        preferred_element_type=jnp.float32,
    )
    scores_t = (logits_t - center[None, :]) / 0.04
    scores_s = logits_s / 0.1
    local_max_t = jnp.max(scores_t, axis=1)
    local_max_s = jnp.max(scores_s, axis=1)
    max_t, max_s = lax.pmax((local_max_t, local_max_s), "proto")
    exp_t = jnp.exp(scores_t - max_t[:, None])
    exp_s = jnp.exp(scores_s - max_s[:, None])
    total_t, total_s = lax.psum((jnp.sum(exp_t, axis=1), jnp.sum(exp_s, axis=1)), "proto")
    derivs = ((exp_s / total_s[:, None] - exp_t / total_t[:, None]) / 0.1).astype(jnp.bfloat16)
    grad_rows_mine = lax.psum_scatter(
        lax.dot_general(
            derivs, z_student, (((0,), (0,)), ((), ())), preferred_element_type=jnp.float32
        ),
        ("fsdp", "dp"),
        scatter_dimension=0,
        tiled=True,
    )
    grad_part = grad_rows_mine.T
    width = grad_part.shape[1]
    offset = lax.axis_index("dp") * width
    student_part = lax.dynamic_slice_in_dim(student_weight, offset, width, 1)
    norms = jnp.sqrt(jnp.sum(student_part * student_part, axis=0, keepdims=True) + 1e-06)
    unit = student_part / norms
    student_grad = (grad_part - unit * jnp.sum(unit * grad_part, axis=0, keepdims=True)) / norms
    return (teacher_new, student_grad)


def solution(mesh):
    placed = (
        P(None, ("proto", "fsdp")),
        P(None, ("proto", "fsdp")),
        P("dp", "fsdp", None),
        P("dp", "fsdp", None),
        P("dp", "fsdp"),
        P("proto"),
    )
    return jax.shard_map(
        shards,
        mesh=mesh,
        in_specs=placed,
        out_specs=(P(None, ("proto", "fsdp")), P(None, ("proto", "fsdp", "dp"))),
        check_vma=False,
    )
```

profile of v0, /device:TPU:0, one launch (start us, length us, event | category | flops | bytes accessed | tf_op | source)
XLA Modules:
  0.0 516.1 jit_solution(15650996628455921244)
XLA Ops:
  7.2 2.2 multiply_reduce_fusion.1
  9.4 4.7 multiply_reduce_fusion
  14.2 0.0 all-gather.5.cloned.1.call-start
  14.2 1.7 multiply_convert_fusion.2
  15.9 0.0 reduce-scatter.2.cloned.1.call-start
  16.0 0.1 copy.9
  16.1 0.1 fusion.6
  16.2 0.1 fusion.7
  16.3 3.0 collective-permute-start
  19.4 3.4 collective-permute-done
  22.8 1.2 gather_fusion
  24.0 108.4 %all-gather.3.cloned.1.call-done = bf16[192,16384]{1,0:T(8,128)(2,1)} async-done(((bf16[192,4096]{1,0:T(8,128)(2,1)}), bf16[192,16384]{1,0:T(8,128)(2,1)}) %all-gather.3.cloned.1.call-update) | async-done | bytes 6291472 | tf_op jit(solution)/shard_map/all_gather | solution.py:35
  132.4 12.3 %fusion.18 = (f32[256]{0:T(256)S(1)}, f32[256,16384]{1,0:T(8,128)}) fusion(bf16[192,16384]{1,0:T(8,128)(2,1)} %all-gather.3.cloned.1.call-done, bf16[1,256,192]{1,2,0:T(8,128)(2,1)S(1)} %copy-done.2, f32[256]{0:T(256)S(1)} %add_rsqrt_fusion.3), kind=kOutput, calls=%fused_computation.44 | convolution fusion | flops 1619148544 | bytes 23169024 | tf_op jit(solution)/shard_map/dot_general | solution.py:33
  144.7 102.8 %all-gather.5.cloned.1.call-done = bf16[192,16384]{1,0:T(8,128)(2,1)} async-done(((bf16[192,4096]{1,0:T(8,128)(2,1)}), bf16[192,16384]{1,0:T(8,128)(2,1)}) %all-gather.5.cloned.1.call-update) | async-done | bytes 6291472 | tf_op jit(solution)/shard_map/all_gather | solution.py:30
  247.5 10.0 %fusion.17 = (f32[256]{0:T(256)S(1)}, f32[256,16384]{1,0:T(8,128)}) fusion(f32[16384]{0:T(1024)S(1)} %copy-done.3, bf16[192,16384]{1,0:T(8,128)(2,1)} %all-gather.5.cloned.1.call-done, bf16[256,192]{1,0:T(8,128)(2,1)S(1)} %gather_fusion, pred[256]{0:T(512)(128)(4,1)S(1)} %compare_and_fusion), kind=kOutput, calls=%fused_computation.43 | convolution fusion | flops 1623244544 | bytes 23233792 | tf_op jit(solution)/shard_map/dot_general | solution.py:28
  257.5 6.8 %all-reduce.1 = (f32[256]{0:T(256)S(1)}, f32[256]{0:T(256)S(1)}) all-reduce(f32[256]{0:T(256)S(1)} %get-tuple-element.9, f32[256]{0:T(256)S(1)} %get-tuple-element.11), channel_id=1, replica_groups=mesh['fsdp'=4,'proto'=4,'dp'=2] {'proto'}, use_global_device_ids=true, to_apply=%region_9.10 | all-reduce | flops 512 | bytes 4096 | tf_op jit(solution)/shard_map/pmax | solution.py:42
  264.3 12.1 %fusion.1 = (f32[256]{0:T(256)S(1)}, f32[256]{0:T(256)S(1)}) fusion(f32[256,16384]{1,0:T(8,128)} %get-tuple-element.12, f32[256]{0:T(256)S(1)} %get-tuple-element.5, f32[256,16384]{1,0:T(8,128)} %get-tuple-element.10, f32[256]{0:T(256)S(1)} %get-tuple-element.4), kind=kLoop, calls=%fused_computation.7 | loop fusion | flops 16776704 | bytes 33558528 | tf_op jit(solution)/shard_map/reduce_sum | solution.py:45
  276.5 6.1 %all-reduce = (f32[256]{0:T(256)S(1)}, f32[256]{0:T(256)S(1)}) all-reduce(f32[256]{0:T(256)S(1)} %get-tuple-element.14, f32[256]{0:T(256)S(1)} %get-tuple-element.13), channel_id=1, replica_groups=mesh['fsdp'=4,'proto'=4,'dp'=2] {'proto'}, use_global_device_ids=true, to_apply=%region_11.12 | all-reduce | flops 512 | bytes 4096 | tf_op jit(solution)/shard_map/psum | solution.py:45
  282.6 17.4 %fusion.3 = f32[16384,192]{0,1:T(8,128)} fusion(f32[256,16384]{1,0:T(8,128)} %get-tuple-element.12, f32[256,16384]{1,0:T(8,128)} %get-tuple-element.10, f32[256]{0:T(256)S(1)} %get-tuple-element.2, f32[256]{0:T(256)S(1)} %get-tuple-element.4, f32[256]{0:T(256)S(1)} %get-tuple-element.3, f32[256]{0:T(256)S(1)} %get-tuple-element.5, ...), kind=kOutput, calls=%fused_computation.9 | convolution fusion | flops 1640120320 | bytes 46240768 | tf_op jit(solution)/shard_map/dot_general | solution.py:48
  300.0 1.9 copy-done
  301.9 0.1 multiply_reduce_fusion.2
  302.0 203.1 %reduce-scatter.2.cloned.1.call-done = f32[2048,192]{0,1:T(8,128)} async-done(((f32[16384,192]{0,1:T(8,128)}), f32[2048,192]{0,1:T(8,128)}) %reduce-scatter.2.cloned.1.call-update) | async-done | bytes 1572880 | tf_op jit(solution)/shard_map/reduce_scatter | solution.py:47
  505.1 1.6 fusion.4
  506.7 2.9 fusion.5
  (24 shorter events, 0.2 us)
Async XLA Ops:
  7.2 125.2 %all-gather.3.cloned.1.call-start = ((), (), s32[]{:S(2)}) async-start(), calls=%async_computation.1 | async-start | bytes 7864320 | tf_op jit(solution)/shard_map/all_gather | solution.py:35
  14.1 130.6 %copy-start.1 = (f32[192,4096]{1,0:T(8,128)}, f32[192,4096]{1,0:T(8,128)S(1)}, u32[]{:S(2)}) copy-start(f32[192,4096]{1,0:T(8,128)S(1)} %get-tuple-element.7) | copy-start | bytes 9437188
  14.1 1.8 copy-start.4
  14.1 5.2 %copy-start.2 = (bf16[1,256,192]{1,2,0:T(8,128)(2,1)S(1)}, bf16[1,256,192]{1,2,0:T(8,128)(2,1)}, u32[]{:S(2)}) copy-start(bf16[1,256,192]{1,2,0:T(8,128)(2,1)} %param.9) | copy-start | bytes 294916
  14.1 5.2 %copy-start.5 = (s32[1,256]{1,0:T(1,128)S(1)}, s32[1,256]{1,0:T(1,128)}, u32[]{:S(2)}) copy-start(s32[1,256]{1,0:T(1,128)} %param.10) | copy-start | bytes 3076
  14.2 233.3 %all-gather.5.cloned.1.call-start = ((), (), s32[]{:S(2)}) async-start(), calls=%async_computation.2 | async-start | bytes 7864320 | tf_op jit(solution)/shard_map/all_gather | solution.py:30
  15.9 489.2 %reduce-scatter.2.cloned.1.call-start = ((), (), s32[]{:S(2)}) async-start(), calls=%async_computation.3 | async-start | bytes 14155776 | tf_op jit(solution)/shard_map/reduce_scatter | solution.py:47
  16.3 6.5 %collective-permute-start = (bf16[256,192]{1,0:T(8,128)(2,1)S(1)}, bf16[256,192]{1,0:T(8,128)(2,1)S(1)}, u32[]{:S(2)}, u32[]{:S(2)}) collective-permute-start(bf16[256,192]{1,0:T(8,128)(2,1)S(1)} %fusion.7), channel_id=1, source_target_pairs={{0,1},{1,0},{2,3},{3,2},{4,5},{5,4},{6,7},{7,6},{8,9},{9,8},{10,11... | collective-permute-start | bytes 294920 | tf_op jit(solution)/shard_map/ppermute | solution.py:8
  24.0 223.5 %copy-start.3 = (f32[16384]{0:T(1024)S(1)}, f32[16384]{0:T(1024)}, u32[]{:S(2)}) copy-start(f32[16384]{0:T(1024)} %param.11) | copy-start | bytes 196612
  300.0 1.9 copy-start
Sparse Core Ops, SparseCore 0:
  14.3 118.0 all-gather.2
  133.9 113.5 all-gather.4
  300.1 204.9 reduce-scatter.1
where the time goes:
time: 516 us
  waiting for transfers between devices  418 us (81%)
  matrix products  39.8 us (8%)
  other arithmetic  25.6 us (5%)
  between operations  13.9 us (3%)
  blocking collectives  12.9 us (2%)
    reduce_scatter x1, waiting for transfers between devices, shards(): lax.psum_scatter(lax.dot_general(derivs, z_student, (((0,), (0,)), ((), (...  203 us
    all_gather x1, waiting for transfers between devices, shards(): lax.all_gather(w_student, 'fsdp', axis=1, tiled=True)  108 us
    all_gather x1, waiting for transfers between devices, shards(): lax.all_gather(w_teacher, 'fsdp', axis=1, tiled=True)  103 us
    dot_general x1, matrix products, shards(): lax.dot_general(derivs, z_student, (((0,), (0,)), ((), ())), preferred_el...  17.4 us
    dot_general x1, matrix products, shards(): jnp.dot(z_student, lax.all_gather(w_student, 'fsdp', axis=1, tiled=True),...  12.3 us
    reduce_sum x1, other arithmetic, shards(): jnp.sum(exp_s, axis=1)  12.1 us
  transfers between devices with their start and end apart: 4, of which 4 were waited for; matrix products, arithmetic and copies ran while one was open for 3% of the time, Pallas kernels for 0%

commit v1 on v0

v1 whole, which is shorter than its diff:
```python
import functools
import math

import jax
import jax.numpy as jnp
from jax import lax
from jax.experimental import pallas as pl
from jax.experimental.pallas import tpu as pltpu
from jax.sharding import PartitionSpec as P

EPS = 1e-06
DEPTH = 256
ROWS = 256
LOG2E = math.log2(math.e)
GAIN_T = LOG2E / 0.04
GAIN_S = LOG2E / 0.1
LEVELS = (5.35, 8.65)
SPLIT = 7.0
VMEM = 56 * 1024 * 1024


def cast_split(row):
    high = row.astype(jnp.bfloat16).astype(jnp.float32)
    mid = (row - high).astype(jnp.bfloat16).astype(jnp.float32)
    return high, mid, row - high - mid


def prep_kernel(n_own, which, teacher_ref, student_ref, center_ref, all_center_ref, new_ref, wt_ref, ws_ref):
    student = student_ref[...]
    new = 0.994 * teacher_ref[...] + 0.006 * student
    new_ref[...] = new

    @pl.when(pl.program_id(0) < n_own)
    def _():
        bot, width = new.shape
        peak = jnp.max(-all_center_ref[...], axis=1, keepdims=True)
        high, mid, low = cast_split(-center_ref[...] - peak)
        row = lax.broadcasted_iota(jnp.int32, (DEPTH - bot, width), 0)
        zero = jnp.zeros((DEPTH - bot, width), jnp.float32)
        extra = jnp.where(row == 0, high, jnp.where(row == 1, mid, jnp.where(row == 2, low, zero)))
        unit_t = new * lax.rsqrt(jnp.sum(new * new, axis=0, keepdims=True) + EPS)
        unit_s = student * lax.rsqrt(jnp.sum(student * student, axis=0, keepdims=True) + EPS)
        wt_ref[...] = jnp.concatenate([unit_t, extra], axis=0).astype(jnp.bfloat16).T
        ws_ref[...] = jnp.concatenate([unit_s, zero], axis=0).astype(jnp.bfloat16).T


def prepare(teacher_weight, student_weight, center_own, dp, n_dp):
    bot, cols = teacher_weight.shape
    own = cols // n_dp
    width = min(512, own)
    n_own, n_all = own // width, cols // width
    which = jnp.reshape(dp, (1,)).astype(jnp.int32)

    def place(i, which):
        return (0, lax.rem(i + which[0] * n_own, n_all))

    def held(i, which):
        return (lax.min(i, n_own - 1), 0)

    return pl.pallas_call(
        functools.partial(prep_kernel, n_own),
        grid_spec=pltpu.PrefetchScalarGridSpec(
            num_scalar_prefetch=1,
            grid=(n_all,),
            in_specs=[
                pl.BlockSpec((bot, width), place),
                pl.BlockSpec((bot, width), place),
                pl.BlockSpec((1, width), lambda i, which: (0, lax.min(i, n_own - 1))),
                pl.BlockSpec((1, own), lambda i, which: (0, 0)),
            ],
            out_specs=[
                pl.BlockSpec((bot, width), place),
                pl.BlockSpec((width, DEPTH), held),
                pl.BlockSpec((width, DEPTH), held),
            ],
        ),
        out_shape=[
            jax.ShapeDtypeStruct((bot, cols), jnp.float32),
            jax.ShapeDtypeStruct((own, DEPTH), jnp.bfloat16),
            jax.ShapeDtypeStruct((own, DEPTH), jnp.bfloat16),
        ],
        compiler_params=pltpu.CompilerParams(vmem_limit_bytes=VMEM),
        cost_estimate=pl.CostEstimate(flops=20 * bot * cols, bytes_accessed=12 * bot * cols, transcendentals=0),
        name="prep",
    )(which, teacher_weight, student_weight, center_own, center_own)


def score_kernel(teacher, gain, feats_ref, w_ref, *rest):
    if teacher:
        center_ref, exp_ref, total_ref, lhs = rest
    else:
        exp_ref, total_ref, trans_ref, lhs = rest
    bot = feats_ref.shape[1]

    @pl.when(pl.program_id(0) == 0)
    def _():
        half = DEPTH // 2
        lane = lax.broadcasted_iota(jnp.int32, (ROWS, half), 1) + half
        ones = jnp.where((lane >= bot) & (lane < bot + 3), 1.0, 0.0)
        lhs[:, half:] = ones.astype(jnp.bfloat16)

    values = feats_ref[...].astype(jnp.float32)
    unit = (values * lax.rsqrt(jnp.sum(values * values, axis=1, keepdims=True) + EPS)).astype(jnp.bfloat16)
    lhs[:, :bot] = unit
    if not teacher:
        trans_ref[...] = unit.T
    stationary = lhs[...]
    cols = w_ref.shape[0]
    step = min(256, cols)
    total = jnp.zeros((8, ROWS), jnp.float32)
    for at in range(0, cols, step):
        score = lax.dot_general(
            w_ref[at:at + step, :], stationary, (((1,), (1,)), ((), ())), preferred_element_type=jnp.float32
        )
        exps = jnp.exp2(score * gain)
        total = total + jnp.sum(exps.reshape(step // 8, 8, ROWS), axis=0)
        exp_ref[at:at + step, :] = exps.astype(jnp.bfloat16)
    total = jnp.sum(total, axis=0, keepdims=True)
    if teacher:
        peak = jnp.max(-center_ref[...], axis=1, keepdims=True)
        upper = peak >= SPLIT
        scaled = total * jnp.exp2((peak - jnp.where(upper, LEVELS[1], LEVELS[0])) * GAIN_T)
        total_ref[0:1, :] = jnp.where(upper, 0.0, scaled)
        total_ref[1:2, :] = jnp.where(upper, scaled, 0.0)
    else:
        total_ref[...] = total


def scores(teacher, feats, weights, center_own=None):
    rows, bot = feats.shape
    cols = weights.shape[0]
    steps = rows // ROWS
    half = steps // 2 if teacher else 0

    def source(i):
        return (lax.rem(i + half, steps), 0)

    in_specs = [pl.BlockSpec((ROWS, bot), source), pl.BlockSpec((cols, DEPTH), lambda i: (0, 0))]
    args = [feats, weights]
    exp_spec = pl.BlockSpec((cols, ROWS), lambda i: (0, i))
    exp_shape = jax.ShapeDtypeStruct((cols, rows), jnp.bfloat16)
    if teacher:
        in_specs.append(pl.BlockSpec((1, cols), lambda i: (0, 0)))
        args.append(center_own)
        out_specs = [exp_spec, pl.BlockSpec((2, ROWS), lambda i: (0, i))]
        out_shape = [exp_shape, jax.ShapeDtypeStruct((2, rows), jnp.float32)]
    else:
        out_specs = [exp_spec, pl.BlockSpec((1, ROWS), lambda i: (0, i)), pl.BlockSpec((bot, ROWS), lambda i: (0, i))]
        out_shape = [
            exp_shape,
            jax.ShapeDtypeStruct((1, rows), jnp.float32),
            jax.ShapeDtypeStruct((bot, rows), jnp.bfloat16),
        ]
    return pl.pallas_call(
        functools.partial(score_kernel, teacher, GAIN_T if teacher else GAIN_S),
        grid=(steps,),
        in_specs=in_specs,
        out_specs=out_specs,
        out_shape=out_shape,
        scratch_shapes=[pltpu.VMEM((ROWS, DEPTH), jnp.bfloat16)],
        compiler_params=pltpu.CompilerParams(vmem_limit_bytes=VMEM),
        cost_estimate=pl.CostEstimate(
            flops=2 * rows * cols * DEPTH, bytes_accessed=2 * rows * cols, transcendentals=rows * cols
        ),
        name="scores_t" if teacher else "scores_s",
    )(*args)


def grad_kernel(which, exp_s_ref, exp_t_ref, trans_ref, total_s_ref, total_t_ref, center_ref, weight_ref, out_ref, feats_s, feats_t):
    @pl.when(pl.program_id(0) == 0)
    def _():
        feats = trans_ref[...].astype(jnp.float32)
        feats_s[...] = (feats * (10.0 / total_s_ref[...])).astype(jnp.bfloat16)
        peak = jnp.max(-center_ref[...], axis=1, keepdims=True)
        low = jnp.log2(total_t_ref[0:1, :]) + GAIN_T * LEVELS[0]
        high = jnp.log2(total_t_ref[1:2, :]) + GAIN_T * LEVELS[1]
        top = jnp.maximum(low, high)
        log_total = top + jnp.log2(jnp.exp2(low - top) + jnp.exp2(high - top))
        feats_t[...] = (feats * (-10.0 * jnp.exp2(GAIN_T * peak - log_total))).astype(jnp.bfloat16)

    contract = (((1,), (1,)), ((), ()))
    grad = lax.dot_general(exp_s_ref[...], feats_s[...], contract, preferred_element_type=jnp.float32)
    grad = grad + lax.dot_general(exp_t_ref[...], feats_t[...], contract, preferred_element_type=jnp.float32)
    grad = grad.T
    weight = weight_ref[...]
    scale = lax.rsqrt(jnp.sum(weight * weight, axis=0, keepdims=True) + EPS)
    unit = weight * scale
    out_ref[...] = (grad - unit * jnp.sum(unit * grad, axis=0, keepdims=True)) * scale


def gradient(exp_s, exp_t, trans, total_s, total_t, center_own, student_weight, dp):
    cols, rows = exp_s.shape
    bot = trans.shape[0]
    width = min(cols, max(128, (1 << 19) // rows))
    steps = cols // width
    which = jnp.reshape(dp, (1,)).astype(jnp.int32)
    whole = lambda i, which: (0, 0)
    return pl.pallas_call(
        grad_kernel,
        grid_spec=pltpu.PrefetchScalarGridSpec(
            num_scalar_prefetch=1,
            grid=(steps,),
            in_specs=[
                pl.BlockSpec((width, rows), lambda i, which: (i, 0)),
                pl.BlockSpec((width, rows), lambda i, which: (i, 0)),
                pl.BlockSpec((bot, rows), whole),
                pl.BlockSpec((1, rows), whole),
                pl.BlockSpec((2, rows), whole),
                pl.BlockSpec((1, cols), whole),
                pl.BlockSpec((bot, width), lambda i, which: (0, which[0] * steps + i)),
            ],
            out_specs=pl.BlockSpec((bot, width), lambda i, which: (0, i)),
            scratch_shapes=[pltpu.VMEM((bot, rows), jnp.bfloat16), pltpu.VMEM((bot, rows), jnp.bfloat16)],
        ),
        out_shape=jax.ShapeDtypeStruct((bot, cols), jnp.float32),
        compiler_params=pltpu.CompilerParams(vmem_limit_bytes=VMEM),
        cost_estimate=pl.CostEstimate(
            flops=4 * rows * cols * DEPTH, bytes_accessed=4 * rows * cols, transcendentals=0
        ),
        name="gradient",
    )(which, exp_s, exp_t, trans, total_s, total_t, center_own, student_weight)


def shards(teacher_weight, student_weight, teacher_feats, student_feats, pairing, center):
    n_dp = lax.axis_size("dp")
    n_proto = lax.axis_size("proto")
    dp = lax.axis_index("dp")
    everyone = ("dp", "fsdp", "proto")
    crops = student_feats.shape[1]
    share = crops // n_proto
    mine = lax.axis_index("proto") * share

    partner = [(i, i ^ 1) for i in range(n_dp)]
    index = lax.ppermute(lax.dynamic_slice_in_dim(pairing[0], mine, share, 0), "dp", partner)
    feats_s = lax.all_gather(lax.dynamic_slice_in_dim(student_feats[0], mine, share, 0), everyone, axis=0, tiled=True)
    feats_t = lax.all_gather(jnp.take(teacher_feats[0], index, axis=0), everyone, axis=0, tiled=True)

    own = teacher_weight.shape[1] // n_dp
    first = (lax.axis_index("fsdp") * n_dp + dp) * own
    center_own = lax.dynamic_slice_in_dim(center, first, own, 0)[None, :]
    teacher_new, w_t, w_s = prepare(teacher_weight, student_weight, center_own, dp, n_dp)
    exp_s, total_s, trans = scores(False, feats_s, w_s)
    exp_t, total_t = scores(True, feats_t, w_t, center_own)
    total_s, total_t = lax.psum((total_s, total_t), everyone)
    student_grad = gradient(exp_s, exp_t, trans, total_s, total_t, center_own, student_weight, dp)
    return (teacher_new, student_grad)


def solution(mesh):
    placed = (
        P(None, ("proto", "fsdp")),
        P(None, ("proto", "fsdp")),
        P("dp", "fsdp", None),
        P("dp", "fsdp", None),
        P("dp", "fsdp"),
        P("proto"),
    )
    return jax.shard_map(
        shards,
        mesh=mesh,
        in_specs=placed,
        out_specs=(P(None, ("proto", "fsdp")), P(None, ("proto", "fsdp", "dp"))),
        check_vma=False,
    )
```

time: 516 us -> 175 us (0.34)
  waiting for transfers between devices: 418 us -> 0.01 us
  blocking collectives: 12.9 us -> 127 us
  matrix products: 39.8 us -> 0 us
  Pallas kernels: 0 us -> 39.5 us
  other arithmetic: 25.6 us -> 0.09 us
  between operations: 13.9 us -> 0.71 us
    all_gather x2 -> x0, waiting for transfers between devices: 211 us -> none  [the longest x1 108 us: shards(): lax.all_gather(w_student, 'fsdp', axis=1, tiled=True)]
    reduce_scatter x1 -> x0, waiting for transfers between devices: 203 us -> none  [shards(): lax.psum_scatter(lax.dot_general(derivs, z_student, (((0,), (0,)), ((), (...]
    all_gather x0 -> x2, blocking collectives: none -> 88.8 us  [the longest x1 46.5 us: shards(): lax.all_gather(lax.dynamic_slice_in_dim(student_feats[0], mine, share, 0)...]
    dot_general x3 -> x0, matrix products: 39.8 us -> none  [the longest x1 17.4 us: shards(): lax.dot_general(derivs, z_student, (((0,), (0,)), ((), ())), preferred_el...]
    pallas_call x0 -> x4, Pallas kernels: none -> 39.5 us  [the longest x2 18.1 us: scores(): pl.pallas_call(functools.partial(score_kernel, teacher, GAIN_T if teacher...]
    psum x1, blocking collectives: 6.1 us -> 38.5 us  [shards(): total_s, total_t = lax.psum((total_s, total_t), everyone)]
    reduce_sum x7 -> x0, other arithmetic: 20.9 us -> none  [the longest x1 12.1 us: shards(): jnp.sum(exp_s, axis=1)]
    pmax x1 -> x0, blocking collectives: 6.82 us -> none  [shards(): max_t, max_s = lax.pmax((local_max_t, local_max_s), 'proto')]
  transfers between devices with their start and end apart: 4 -> 1, of which waited for: 4 -> 0; matrix products, arithmetic and copies ran while one was open for 3% -> 1% of each run, Pallas kernels for 0% -> 10%
where the time goes in v1:
time: 175 us; the launch traced here: 174 us
  blocking collectives  127 us (73%)
  Pallas kernels  39.5 us (23%)
  local copies, waits for them, and re-layouts  3.05 us (2%)
  starting transfers between devices  2.94 us (2%)
    all_gather x1, blocking collectives, shards(): lax.all_gather(lax.dynamic_slice_in_dim(student_feats[0], mine, share, 0)...  46.5 us
    all_gather x1, blocking collectives, shards(): lax.all_gather(jnp.take(teacher_feats[0], index, axis=0), everyone, axis=...  42.3 us
    psum x1, blocking collectives, shards(): total_s, total_t = lax.psum((total_s, total_t), everyone)  38.5 us
    pallas_call x2, Pallas kernels, scores(): pl.pallas_call(functools.partial(score_kernel, teacher, GAIN_T if teacher...  18.1 us
    pallas_call x1, Pallas kernels, gradient(): pl.pallas_call(grad_kernel, grid_spec=pltpu.PrefetchScalarGridSpec(num_sc...  13.1 us
    pallas_call x1, Pallas kernels, prepare(): pl.pallas_call(functools.partial(prep_kernel, n_own), grid_spec=pltpu.Pre...  8.3 us
  transfers between devices with their start and end apart: 1, of which 0 were waited for; matrix products, arithmetic and copies ran while one was open for 1% of the time, Pallas kernels for 10%

profile of v1, /device:TPU:0, one launch (start us, length us, event | category | flops | bytes accessed | tf_op | source)
XLA Modules:
  0.0 173.6 jit_solution(4983776814836662748)
XLA Ops:
  0.6 0.0 copy-start
  0.7 0.8 dynamic-slice_bitcast_fusion
  1.4 2.9 %collective-permute-start = (s32[64]{0:T(128)S(1)}, s32[64]{0:T(128)S(1)}, u32[]{:S(2)}, u32[]{:S(2)}) collective-permute-start(s32[64]{0:T(128)S(1)} %dynamic-slice_bitcast_fusion), channel_id=1, source_target_pairs={{0,1},{1,0},{2,3},{3,2},{4,5},{5,4},{6,7},{7,6},{8,9},{9,8},{10,11... | collective-permute-start | bytes 776 | tf_op jit(solution)/shard_map/ppermute | solution.py:234
  4.4 0.0 copy-done
  4.4 0.1 constant_dynamic-slice_fusion
  4.4 0.1 copy.10
  4.5 46.5 %all-gather = bf16[1,2048,192]{2,1,0:T(8,128)(2,1)} all-gather(bf16[1,64,192]{2,1,0:T(8,128)(2,1)S(1)} %copy.10), channel_id=2, replica_groups=mesh['fsdp'=4,'proto'=4,'dp'=2] {'dp','fsdp','proto'}, dimensions={1}, use_global_device_ids=true | all-gather | bytes 811008 | tf_op jit(solution)/shard_map/all_gather | solution.py:235
  51.0 1.3 dynamic_slice.13
  52.3 8.3 %prep.1 = (f32[192,4096]{1,0:T(8,128)}, bf16[2048,256]{1,0:T(8,128)(2,1)}, bf16[2048,256]{1,0:T(8,128)(2,1)}) custom-call(s32[1]{0:T(128)} %bitcast.which, f32[192,4096]{1,0:T(8,128)} %teacher_ref.1, f32[192,4096]{1,0:T(8,128)} %weight_ref.1, f32[1,2048]{1,0:T(1,128)} %bitcast.8, f32[1,2048]{1,0:T(1,128)} %bitcast.9), custom_call_target="tpu_custom_call" | custom-call | flops 15728640 | bytes 9437184 | tf_op jit(solution)/shard_map/prep/pallas_call | solution.py:60
  60.6 0.0 copy-start.1
  60.6 9.1 %scores_s.1 = (bf16[2048,2048]{1,0:T(8,128)(2,1)}, f32[1,2048]{1,0:T(1,128)}, bf16[192,2048]{1,0:T(8,128)(2,1)}) custom-call(bf16[2048,192]{1,0:T(8,128)(2,1)} %bitcast.7, bf16[2048,256]{1,0:T(8,128)(2,1)} %get-tuple-element.11.w_ref), custom_call_target="tpu_custom_call" | custom-call | flops 2147483648 | bytes 8388608 | tf_op jit(solution)/shard_map/scores_s/pallas_call | solution.py:154
  69.7 0.0 copy-done.1
  69.7 0.1 copy.9
  69.8 0.0 collective-permute-done
  69.9 0.7 gather_fusion
  70.6 0.1 broadcast_select_fusion
  70.7 42.3 %all_gather.7.feats_ref = bf16[2048,192]{1,0:T(8,128)(2,1)} all-gather(bf16[64,192]{1,0:T(8,128)(2,1)S(1)} %broadcast_select_fusion), channel_id=1, replica_groups=mesh['fsdp'=4,'proto'=4,'dp'=2] {'dp','fsdp','proto'}, dimensions={0}, use_global_device_ids=true | all-gather | bytes 811008 | tf_op jit(solution)/shard_map/all_gather | solution.py:236
  112.9 0.0 copy-start.2
  112.9 9.0 %scores_t.1 = (bf16[2048,2048]{1,0:T(8,128)(2,1)}, f32[2,2048]{1,0:T(2,128)}) custom-call(bf16[2048,192]{1,0:T(8,128)(2,1)} %all_gather.7.feats_ref, bf16[2048,256]{1,0:T(8,128)(2,1)} %get-tuple-element.13.w_ref, f32[1,2048]{1,0:T(1,128)} %bitcast.10), custom_call_target="tpu_custom_call" | custom-call | flops 2147483648 | bytes 8388608 | tf_op jit(solution)/shard_map/scores_t/pallas_call | solution.py:154
  122.0 0.0 copy-done.2
  122.0 38.5 %all-reduce = (f32[1,2048]{1,0:T(1,128)}, f32[2,2048]{1,0:T(2,128)}) all-reduce(f32[1,2048]{1,0:T(1,128)S(1)} %copy-done.2, f32[2,2048]{1,0:T(2,128)} %get-tuple-element.17), channel_id=1, replica_groups=mesh['fsdp'=4,'proto'=4,'dp'=2] {'dp','fsdp','proto'}, use_global_device_ids=true, to_apply=%region_0.1 | all-reduce | flops 6144 | bytes 49152 | tf_op jit(solution)/shard_map/psum | solution.py:244
  160.4 13.1 %gradient.1 = f32[192,2048]{1,0:T(8,128)} custom-call(s32[1]{0:T(128)} %bitcast.which, bf16[2048,2048]{1,0:T(8,128)(2,1)} %get-tuple-element.12.exp_s_ref, bf16[2048,2048]{1,0:T(8,128)(2,1)} %get-tuple-element.14.exp_t_ref, bf16[192,2048]{1,0:T(8,128)(2,1)} %get-tuple-element.15.trans_ref, f32[1,2048]{1,0:T(1,128)} %get-tuple-element.18.total_s_ref, ...), custom_call_target="tpu_custom_call" | custom-call | flops 4294967296 | bytes 16777216 | tf_op jit(solution)/shard_map/gradient/pallas_call | solution.py:198
  (3 shorter events, 0.0 us)
Async XLA Ops:
  0.6 3.7 %copy-start = (bf16[1,256,192]{1,2,0:T(8,128)(2,1)S(1)}, bf16[1,256,192]{1,2,0:T(8,128)(2,1)}, u32[]{:S(2)}) copy-start(bf16[1,256,192]{1,2,0:T(8,128)(2,1)} %param.9) | copy-start | bytes 294916
  1.4 68.4 %collective-permute-start = (s32[64]{0:T(128)S(1)}, s32[64]{0:T(128)S(1)}, u32[]{:S(2)}, u32[]{:S(2)}) collective-permute-start(s32[64]{0:T(128)S(1)} %dynamic-slice_bitcast_fusion), channel_id=1, source_target_pairs={{0,1},{1,0},{2,3},{3,2},{4,5},{5,4},{6,7},{7,6},{8,9},{9,8},{10,11... | collective-permute-start | bytes 776 | tf_op jit(solution)/shard_map/ppermute | solution.py:234
  60.6 9.1 %copy-start.1 = (bf16[1,256,192]{1,2,0:T(8,128)(2,1)S(1)}, bf16[1,256,192]{1,2,0:T(8,128)(2,1)}, u32[]{:S(2)}) copy-start(bf16[1,256,192]{1,2,0:T(8,128)(2,1)} %param.8) | copy-start | bytes 294916
  112.9 9.0 %copy-start.2 = (f32[1,2048]{1,0:T(1,128)S(1)}, f32[1,2048]{1,0:T(1,128)}, u32[]{:S(2)}) copy-start(f32[1,2048]{1,0:T(1,128)} %get-tuple-element.16) | copy-start | bytes 24580

commit v2 on v1

--- a/solution.py
+++ b/solution.py
@@ -10,7 +10,7 @@
 
 EPS = 1e-06
 DEPTH = 256
-ROWS = 256
+ROWS = 512
 LOG2E = math.log2(math.e)
 GAIN_T = LOG2E / 0.04
 GAIN_S = LOG2E / 0.1
@@ -47,7 +47,7 @@
 def prepare(teacher_weight, student_weight, center_own, dp, n_dp):
     bot, cols = teacher_weight.shape
     own = cols // n_dp
-    width = min(512, own)
+    width = min(1024, own)
     n_own, n_all = own // width, cols // width
     which = jnp.reshape(dp, (1,)).astype(jnp.int32)
 
@@ -85,12 +85,13 @@
     )(which, teacher_weight, student_weight, center_own, center_own)
 
 
-def score_kernel(teacher, gain, feats_ref, w_ref, *rest):
+def score_kernel(teacher, gain, core, mine_ref, pair_ref, w_ref, *rest):
     if teacher:
         center_ref, exp_ref, total_ref, lhs = rest
     else:
         exp_ref, total_ref, trans_ref, lhs = rest
-    bot = feats_ref.shape[1]
+    bot = mine_ref.shape[1]
+    own_half = (pl.program_id(0) * 2 >= pl.num_programs(0)) == (core[0] == 1)
 
     @pl.when(pl.program_id(0) == 0)
     def _():
@@ -99,7 +100,7 @@
         ones = jnp.where((lane >= bot) & (lane < bot + 3), 1.0, 0.0)
         lhs[:, half:] = ones.astype(jnp.bfloat16)
 
-    values = feats_ref[...].astype(jnp.float32)
+    values = jnp.where(own_half, mine_ref[...], pair_ref[...]).astype(jnp.float32)
     unit = (values * lax.rsqrt(jnp.sum(values * values, axis=1, keepdims=True) + EPS)).astype(jnp.bfloat16)
     lhs[:, :bot] = unit
     if not teacher:
@@ -114,7 +115,7 @@
         )
         exps = jnp.exp2(score * gain)
         total = total + jnp.sum(exps.reshape(step // 8, 8, ROWS), axis=0)
-        exp_ref[at:at + step, :] = exps.astype(jnp.bfloat16)
+        exp_ref[0, at:at + step, :] = exps.astype(jnp.bfloat16)
     total = jnp.sum(total, axis=0, keepdims=True)
     if teacher:
         peak = jnp.max(-center_ref[...], axis=1, keepdims=True)
@@ -126,26 +127,34 @@
         total_ref[...] = total
 
 
-def scores(teacher, feats, weights, center_own=None):
-    rows, bot = feats.shape
+def scores(teacher, core, feats, weights, center_own=None):
+    held, bot = feats[0].shape
     cols = weights.shape[0]
+    rows = 2 * held
     steps = rows // ROWS
-    half = steps // 2 if teacher else 0
-
-    def source(i):
-        return (lax.rem(i + half, steps), 0)
-
-    in_specs = [pl.BlockSpec((ROWS, bot), source), pl.BlockSpec((cols, DEPTH), lambda i: (0, 0))]
-    args = [feats, weights]
-    exp_spec = pl.BlockSpec((cols, ROWS), lambda i: (0, i))
-    exp_shape = jax.ShapeDtypeStruct((cols, rows), jnp.bfloat16)
+    halves = steps // 2
+    turn = halves // 2 if teacher else 0
+
+    def source(i, core):
+        return (lax.rem(lax.rem(i, halves) + turn, halves), 0)
+
+    def whole(i, core):
+        return (0, 0)
+
+    def along(i, core):
+        return (0, i)
+
+    in_specs = [pl.BlockSpec((ROWS, bot), source), pl.BlockSpec((ROWS, bot), source), pl.BlockSpec((cols, DEPTH), whole)]
+    args = [*feats, weights]
+    exp_spec = pl.BlockSpec((1, cols, ROWS), lambda i, core: (i, 0, 0))
+    exp_shape = jax.ShapeDtypeStruct((steps, cols, ROWS), jnp.bfloat16)
     if teacher:
-        in_specs.append(pl.BlockSpec((1, cols), lambda i: (0, 0)))
+        in_specs.append(pl.BlockSpec((1, cols), whole))
         args.append(center_own)
-        out_specs = [exp_spec, pl.BlockSpec((2, ROWS), lambda i: (0, i))]
+        out_specs = [exp_spec, pl.BlockSpec((2, ROWS), along)]
         out_shape = [exp_shape, jax.ShapeDtypeStruct((2, rows), jnp.float32)]
     else:
-        out_specs = [exp_spec, pl.BlockSpec((1, ROWS), lambda i: (0, i)), pl.BlockSpec((bot, ROWS), lambda i: (0, i))]
+        out_specs = [exp_spec, pl.BlockSpec((1, ROWS), along), pl.BlockSpec((bot, ROWS), along)]
         out_shape = [
             exp_shape,
             jax.ShapeDtypeStruct((1, rows), jnp.float32),
@@ -153,64 +162,77 @@
         ]
     return pl.pallas_call(
         functools.partial(score_kernel, teacher, GAIN_T if teacher else GAIN_S),
-        grid=(steps,),
-        in_specs=in_specs,
-        out_specs=out_specs,
+        grid_spec=pltpu.PrefetchScalarGridSpec(
+            num_scalar_prefetch=1,
+            grid=(steps,),
+            in_specs=in_specs,
+            out_specs=out_specs,
+            scratch_shapes=[pltpu.VMEM((ROWS, DEPTH), jnp.bfloat16)],
+        ),
         out_shape=out_shape,
-        scratch_shapes=[pltpu.VMEM((ROWS, DEPTH), jnp.bfloat16)],
         compiler_params=pltpu.CompilerParams(vmem_limit_bytes=VMEM),
         cost_estimate=pl.CostEstimate(
             flops=2 * rows * cols * DEPTH, bytes_accessed=2 * rows * cols, transcendentals=rows * cols
         ),
         name="scores_t" if teacher else "scores_s",
-    )(*args)
-
-
-def grad_kernel(which, exp_s_ref, exp_t_ref, trans_ref, total_s_ref, total_t_ref, center_ref, weight_ref, out_ref, feats_s, feats_t):
-    @pl.when(pl.program_id(0) == 0)
+    )(jnp.reshape(core, (1,)).astype(jnp.int32), *args)
+
+
+def grad_kernel(which, exp_s_ref, exp_t_ref, trans_ref, total_s_ref, total_t_ref, center_ref, weight_ref, out_ref, acc):
+    feats = trans_ref[...].astype(jnp.float32)
+    feats_s = (feats * (10.0 / total_s_ref[...])).astype(jnp.bfloat16)
+    peak = jnp.max(-center_ref[...], axis=1, keepdims=True)
+    low = jnp.log2(total_t_ref[0:1, :]) + GAIN_T * LEVELS[0]
+    high = jnp.log2(total_t_ref[1:2, :]) + GAIN_T * LEVELS[1]
+    top = jnp.maximum(low, high)
+    log_total = top + jnp.log2(jnp.exp2(low - top) + jnp.exp2(high - top))
+    feats_t = (feats * (-10.0 * jnp.exp2(GAIN_T * peak - log_total))).astype(jnp.bfloat16)
+    cols = acc.shape[0]
+    step = min(256, cols)
+    first, last = pl.program_id(0) == 0, pl.program_id(0) == pl.num_programs(0) - 1
+
+    @pl.when(first)
     def _():
-        feats = trans_ref[...].astype(jnp.float32)
-        feats_s[...] = (feats * (10.0 / total_s_ref[...])).astype(jnp.bfloat16)
-        peak = jnp.max(-center_ref[...], axis=1, keepdims=True)
-        low = jnp.log2(total_t_ref[0:1, :]) + GAIN_T * LEVELS[0]
-        high = jnp.log2(total_t_ref[1:2, :]) + GAIN_T * LEVELS[1]
-        top = jnp.maximum(low, high)
-        log_total = top + jnp.log2(jnp.exp2(low - top) + jnp.exp2(high - top))
-        feats_t[...] = (feats * (-10.0 * jnp.exp2(GAIN_T * peak - log_total))).astype(jnp.bfloat16)
+        acc[...] = jnp.zeros_like(acc)
 
     contract = (((1,), (1,)), ((), ()))
-    grad = lax.dot_general(exp_s_ref[...], feats_s[...], contract, preferred_element_type=jnp.float32)
-    grad = grad + lax.dot_general(exp_t_ref[...], feats_t[...], contract, preferred_element_type=jnp.float32)
-    grad = grad.T
-    weight = weight_ref[...]
-    scale = lax.rsqrt(jnp.sum(weight * weight, axis=0, keepdims=True) + EPS)
-    unit = weight * scale
-    out_ref[...] = (grad - unit * jnp.sum(unit * grad, axis=0, keepdims=True)) * scale
+    for at in range(0, cols, step):
+        part = lax.dot_general(exp_s_ref[0, at:at + step, :], feats_s, contract, preferred_element_type=jnp.float32)
+        part = part + lax.dot_general(exp_t_ref[0, at:at + step, :], feats_t, contract, preferred_element_type=jnp.float32)
+        acc[at:at + step, :] += part
+
+    @pl.when(last)
+    def _():
+        for at in range(0, cols, step):
+            grad = acc[at:at + step, :].T
+            weight = weight_ref[:, at:at + step]
+            scale = lax.rsqrt(jnp.sum(weight * weight, axis=0, keepdims=True) + EPS)
+            unit = weight * scale
+            out_ref[:, at:at + step] = (grad - unit * jnp.sum(unit * grad, axis=0, keepdims=True)) * scale
 
 
 def gradient(exp_s, exp_t, trans, total_s, total_t, center_own, student_weight, dp):
-    cols, rows = exp_s.shape
-    bot = trans.shape[0]
-    width = min(cols, max(128, (1 << 19) // rows))
-    steps = cols // width
+    steps, cols, _ = exp_s.shape
+    bot, rows = trans.shape
     which = jnp.reshape(dp, (1,)).astype(jnp.int32)
-    whole = lambda i, which: (0, 0)
+    block = lambda i, which: (i, 0, 0)
+    along = lambda i, which: (0, i)
     return pl.pallas_call(
         grad_kernel,
         grid_spec=pltpu.PrefetchScalarGridSpec(
             num_scalar_prefetch=1,
             grid=(steps,),
             in_specs=[
-                pl.BlockSpec((width, rows), lambda i, which: (i, 0)),
-                pl.BlockSpec((width, rows), lambda i, which: (i, 0)),
-                pl.BlockSpec((bot, rows), whole),
-                pl.BlockSpec((1, rows), whole),
-                pl.BlockSpec((2, rows), whole),
-                pl.BlockSpec((1, cols), whole),
-                pl.BlockSpec((bot, width), lambda i, which: (0, which[0] * steps + i)),
+                pl.BlockSpec((1, cols, ROWS), block),
+                pl.BlockSpec((1, cols, ROWS), block),
+                pl.BlockSpec((bot, ROWS), along),
+                pl.BlockSpec((1, ROWS), along),
+                pl.BlockSpec((2, ROWS), along),
+                pl.BlockSpec((1, cols), lambda i, which: (0, 0)),
+                pl.BlockSpec((bot, cols), lambda i, which: (0, which[0])),
             ],
-            out_specs=pl.BlockSpec((bot, width), lambda i, which: (0, i)),
-            scratch_shapes=[pltpu.VMEM((bot, rows), jnp.bfloat16), pltpu.VMEM((bot, rows), jnp.bfloat16)],
+            out_specs=pl.BlockSpec((bot, cols), lambda i, which: (0, 0)),
+            scratch_shapes=[pltpu.VMEM((cols, bot), jnp.float32)],
         ),
         out_shape=jax.ShapeDtypeStruct((bot, cols), jnp.float32),
         compiler_params=pltpu.CompilerParams(vmem_limit_bytes=VMEM),
@@ -221,27 +243,42 @@
     )(which, exp_s, exp_t, trans, total_s, total_t, center_own, student_weight)
 
 
+def spread(shard, axes, n):
+    return lax.all_to_all(jnp.broadcast_to(shard[None], (n, *shard.shape)), axes, 0, 0, tiled=True)
+
+
 def shards(teacher_weight, student_weight, teacher_feats, student_feats, pairing, center):
     n_dp = lax.axis_size("dp")
     n_proto = lax.axis_size("proto")
     dp = lax.axis_index("dp")
-    everyone = ("dp", "fsdp", "proto")
-    crops = student_feats.shape[1]
-    share = crops // n_proto
-    mine = lax.axis_index("proto") * share
+    others = ("dp", "fsdp")
+    n_others = n_dp * lax.axis_size("fsdp")
+    crops, bot = student_feats.shape[1:]
+    share = crops // 2
+    core = lax.rem(lax.axis_index("proto"), 2)
+    mine = core * share
 
     partner = [(i, i ^ 1) for i in range(n_dp)]
+    pair = [(i, i ^ 1) for i in range(n_proto)]
     index = lax.ppermute(lax.dynamic_slice_in_dim(pairing[0], mine, share, 0), "dp", partner)
-    feats_s = lax.all_gather(lax.dynamic_slice_in_dim(student_feats[0], mine, share, 0), everyone, axis=0, tiled=True)
-    feats_t = lax.all_gather(jnp.take(teacher_feats[0], index, axis=0), everyone, axis=0, tiled=True)
+
+    def collect(shard):
+        held = spread(shard, others, n_others).reshape(n_others * share, bot)
+        return held, lax.ppermute(held, "proto", pair)
+
+    feats_s = collect(lax.dynamic_slice_in_dim(student_feats[0], mine, share, 0))
+    feats_t = collect(jnp.take(teacher_feats[0], index, axis=0))
 
     own = teacher_weight.shape[1] // n_dp
     first = (lax.axis_index("fsdp") * n_dp + dp) * own
     center_own = lax.dynamic_slice_in_dim(center, first, own, 0)[None, :]
     teacher_new, w_t, w_s = prepare(teacher_weight, student_weight, center_own, dp, n_dp)
-    exp_s, total_s, trans = scores(False, feats_s, w_s)
-    exp_t, total_t = scores(True, feats_t, w_t, center_own)
-    total_s, total_t = lax.psum((total_s, total_t), everyone)
+    exp_s, total_s, trans = scores(False, core, feats_s, w_s)
+    exp_t, total_t = scores(True, core, feats_t, w_t, center_own)
+    totals = jnp.concatenate([total_s, total_t], axis=0)
+    totals = jnp.sum(spread(totals, "proto", n_proto), axis=0)
+    totals = jnp.sum(spread(totals, others, n_others), axis=0)
+    total_s, total_t = totals[:1], totals[1:]
     student_grad = gradient(exp_s, exp_t, trans, total_s, total_t, center_own, student_weight, dp)
     return (teacher_new, student_grad)
 

time: 175 us -> 96.6 us (0.55)
  blocking collectives: 127 us -> 19.5 us
  waiting for transfers between devices: 0.01 us -> 21.1 us
  starting transfers between devices: 2.94 us -> 11.4 us
  Pallas kernels: 39.5 us -> 33.2 us
  local copies, waits for them, and re-layouts: 3.05 us -> 8.88 us
    all_gather x2 -> x0, blocking collectives: 88.8 us -> none  [the longest x1 46.5 us: shards(): lax.all_gather(lax.dynamic_slice_in_dim(student_feats[0], mine, share, 0)...]
    psum x1 -> x0, blocking collectives: 38.5 us -> none  [shards(): total_s, total_t = lax.psum((total_s, total_t), everyone)]
    all_to_all x0 -> x2, waiting for transfers between devices: none -> 21.1 us  [spread(): lax.all_to_all(jnp.broadcast_to(shard[None], (n, *shard.shape)), axes, 0,...]
    all_to_all x0 -> x2, blocking collectives: none -> 19.5 us  [spread(): lax.all_to_all(jnp.broadcast_to(shard[None], (n, *shard.shape)), axes, 0,...]
    all_to_all x0 -> x2, starting transfers between devices: none -> 8.33 us  [spread(): lax.all_to_all(jnp.broadcast_to(shard[None], (n, *shard.shape)), axes, 0,...]
    pallas_call x2, Pallas kernels: 18.1 us -> 14.6 us  [scores(): pl.pallas_call(functools.partial(score_kernel, teacher, GAIN_T if teacher...]
    unnamed x8 -> x13, local copies, waits for them, and re-layouts: 0.2 us -> 2.62 us
    pallas_call x1, Pallas kernels: 8.3 us -> 6.51 us  [prepare(): pl.pallas_call(functools.partial(prep_kernel, n_own), grid_spec=pltpu.Pre...]
  transfers between devices with their start and end apart: 1 -> 5, of which waited for: 0 -> 2; matrix products, arithmetic and copies ran while one was open for 1% -> 5% of each run, Pallas kernels for 10% -> 15%
where the time goes in v2:
time: 96.6 us; the launch traced here: 95.8 us
  Pallas kernels  33.2 us (34%)
  waiting for transfers between devices  21.1 us (22%)
  blocking collectives  19.5 us (20%)
  starting transfers between devices  11.4 us (12%)
  local copies, waits for them, and re-layouts  8.88 us (9%)
    all_to_all x2, waiting for transfers between devices, spread(): lax.all_to_all(jnp.broadcast_to(shard[None], (n, *shard.shape)), axes, 0,...  21.1 us
    all_to_all x2, blocking collectives, spread(): lax.all_to_all(jnp.broadcast_to(shard[None], (n, *shard.shape)), axes, 0,...  19.5 us
    pallas_call x2, Pallas kernels, scores(): pl.pallas_call(functools.partial(score_kernel, teacher, GAIN_T if teacher...  14.6 us
    pallas_call x1, Pallas kernels, gradient(): pl.pallas_call(grad_kernel, grid_spec=pltpu.PrefetchScalarGridSpec(num_sc...  12.1 us
    all_to_all x2, starting transfers between devices, spread(): lax.all_to_all(jnp.broadcast_to(shard[None], (n, *shard.shape)), axes, 0,...  8.33 us
    pallas_call x1, Pallas kernels, prepare(): pl.pallas_call(functools.partial(prep_kernel, n_own), grid_spec=pltpu.Pre...  6.51 us
    ppermute x1, starting transfers between devices, shards(): lax.ppermute(lax.dynamic_slice_in_dim(pairing[0], mine, share, 0), 'dp',...  2.94 us
    unnamed x13, local copies, waits for them, and re-layouts  2.62 us
  transfers between devices with their start and end apart: 5, of which 2 were waited for; matrix products, arithmetic and copies ran while one was open for 5% of the time, Pallas kernels for 15%

profile of v2, /device:TPU:0, one launch (start us, length us, event | category | flops | bytes accessed | tf_op | source)
XLA Modules:
  0.0 95.8 jit_solution(2761826243010623510)
XLA Ops:
  0.7 0.7 dynamic-slice_bitcast_fusion.1
  1.3 2.9 %collective-permute-start.1 = (s32[128]{0:T(128)S(1)}, s32[128]{0:T(128)S(1)}, u32[]{:S(2)}, u32[]{:S(2)}) collective-permute-start(s32[128]{0:T(128)S(1)} %dynamic-slice_bitcast_fusion.1), channel_id=1, source_target_pairs={{0,1},{1,0},{2,3},{3,2},{4,5},{5,4},{6,7},{7,6},{8,9},{9,8},{10,11... | collective-permute-start | bytes 1544 | tf_op jit(solution)/shard_map/ppermute | solution.py:263
  4.3 0.8 broadcast_in_dim.43
  5.1 4.9 %all-to-all-start = ((bf16[8,128,192]{1,2,0:T(8,128)(2,1)}), bf16[8,128,192]{1,2,0:T(8,128)(2,1)S(1)}, u32[]{:S(2)}, u32[]{:S(2)}) async-start(bf16[8,128,192]{1,2,0:T(8,128)(2,1)} %broadcast_in_dim.43), calls=%async_computation | async-start | bytes 786432 | tf_op jit(solution)/shard_map/all_to_all | solution.py:247
  10.0 1.0 %copy.20 = bf16[1,256,192]{2,1,0:T(8,128)(2,1)S(1)} copy(bf16[1,256,192]{1,2,0:T(8,128)(2,1)} %param.8) | data formatting | bytes 196608 | tf_op args[2]
  11.0 0.8 gather_fusion
  12.1 10.2 %all-to-all-done = bf16[8,128,192]{1,2,0:T(8,128)(2,1)S(1)} async-done(((bf16[8,128,192]{1,2,0:T(8,128)(2,1)}), bf16[8,128,192]{1,2,0:T(8,128)(2,1)S(1)}, u32[]{:S(2)}, u32[]{:S(2)}) %all-to-all-start) | async-done | bytes 393248 | tf_op jit(solution)/shard_map/all_to_all | solution.py:247
  22.3 0.8 broadcast_in_dim.47
  23.1 3.5 %all-to-all-start.1 = ((bf16[8,128,192]{1,2,0:T(8,128)(2,1)}), bf16[8,128,192]{1,2,0:T(8,128)(2,1)S(1)}, u32[]{:S(2)}, u32[]{:S(2)}) async-start(bf16[8,128,192]{1,2,0:T(8,128)(2,1)} %broadcast_in_dim.47), calls=%async_computation.1 | async-start | bytes 786432 | tf_op jit(solution)/shard_map/all_to_all | solution.py:247
  26.5 0.2 copy.19
  26.8 10.9 %all-to-all-done.1 = bf16[8,128,192]{1,2,0:T(8,128)(2,1)S(1)} async-done(((bf16[8,128,192]{1,2,0:T(8,128)(2,1)}), bf16[8,128,192]{1,2,0:T(8,128)(2,1)S(1)}, u32[]{:S(2)}, u32[]{:S(2)}) %all-to-all-start.1) | async-done | bytes 393248 | tf_op jit(solution)/shard_map/all_to_all | solution.py:247
  37.7 0.2 copy.22
  38.0 1.3 %dynamic_slice.11 = f32[2048]{0:T(1024)} dynamic-slice(f32[16384]{0:T(1024)} %param.11, s32[]{:T(128)S(6)} %select_n.20), dynamic_slice_sizes={2048} | dynamic-slice | bytes 16388 | tf_op jit(solution)/shard_map/dynamic_slice | solution.py:274
  39.4 6.5 %prep.1 = (f32[192,4096]{1,0:T(8,128)}, bf16[2048,256]{1,0:T(8,128)(2,1)}, bf16[2048,256]{1,0:T(8,128)(2,1)}) custom-call(s32[1]{0:T(128)} %bitcast.which, f32[192,4096]{1,0:T(8,128)} %teacher_ref.1, f32[192,4096]{1,0:T(8,128)} %weight_ref.1, f32[1,2048]{1,0:T(1,128)} %bitcast.15, f32[1,2048]{1,0:T(1,128)} %bitcast.16), custom_call_target="tpu_custom_call" | custom-call | flops 15728640 | bytes 9437184 | tf_op jit(solution)/shard_map/prep/pallas_call | solution.py:60
  45.9 0.8 copy-done.4
  46.7 7.4 %scores_s.1 = (bf16[4,2048,512]{2,1,0:T(8,128)(2,1)}, f32[1,2048]{1,0:T(1,128)}, bf16[192,2048]{1,0:T(8,128)(2,1)}) custom-call(s32[1]{0:T(128)} %bitcast.2.core, bf16[1024,192]{1,0:T(8,128)(2,1)} %bitcast.12, bf16[1024,192]{1,0:T(8,128)(2,1)} %copy-done.4, bf16[2048,256]{1,0:T(8,128)(2,1)} %get-tuple-element.11.w_ref), custom_call_target="tpu_custom_call" | custom-call | flops 2147483648 | bytes 8388608 | tf_op jit(solution)/shard_map/scores_s/pallas_call | solution.py:163
  54.1 0.8 copy-done.5
  54.9 7.2 %scores_t.1 = (bf16[4,2048,512]{2,1,0:T(8,128)(2,1)}, f32[2,2048]{1,0:T(2,128)}) custom-call(s32[1]{0:T(128)} %bitcast.2.core, bf16[1024,192]{1,0:T(8,128)(2,1)} %bitcast.14, bf16[1024,192]{1,0:T(8,128)(2,1)} %copy-done.5, bf16[2048,256]{1,0:T(8,128)(2,1)} %get-tuple-element.13.w_ref, f32[1,2048]{1,0:T(1,128)} %bitcast.17), custom_call_target="tpu_custom_call" | custom-call | flops 2147483648 | bytes 8388608 | tf_op jit(solution)/shard_map/scores_t/pallas_call | solution.py:163
  62.1 0.7 pad_maximum_fusion
  62.9 7.3 %all_to_all.20 = f32[4,3,2048]{2,1,0:T(4,128)S(1)} all-to-all(f32[4,3,2048]{2,1,0:T(4,128)S(1)} %broadcast_in_dim.48), channel_id=1, replica_groups=mesh['fsdp'=4,'proto'=4,'dp'=2] {'proto'}, dimensions={0} | all-to-all | bytes 196608 | tf_op jit(solution)/shard_map/all_to_all | solution.py:247
  70.2 12.2 %all_to_all.21 = f32[8,3,2048]{2,1,0:T(4,128)S(1)} all-to-all(f32[8,3,2048]{2,1,0:T(4,128)S(1)} %broadcast_in_dim.49), channel_id=1, replica_groups=mesh['fsdp'=4,'proto'=4,'dp'=2] {'dp','fsdp'}, dimensions={0} | all-to-all | bytes 393216 | tf_op jit(solution)/shard_map/all_to_all | solution.py:247
  82.5 0.6 slice.10.total_s_ref
  83.1 0.6 slice.11.total_t_ref
  83.7 12.1 %gradient.1 = f32[192,2048]{1,0:T(8,128)} custom-call(s32[1]{0:T(128)} %bitcast.which, bf16[4,2048,512]{2,1,0:T(8,128)(2,1)} %get-tuple-element.12.exp_s_ref, bf16[4,2048,512]{2,1,0:T(8,128)(2,1)} %get-tuple-element.14.exp_t_ref, bf16[192,2048]{1,0:T(8,128)(2,1)} %get-tuple-element.15.trans_ref, f32[1,2048]{1,0:T(1,128)} %slice.10.total_s_ref, ...), custom_call_target="tpu_custom_call" | custom-call | flops 4294967296 | bytes 16777216 | tf_op jit(solution)/shard_map/gradient/pallas_call | solution.py:220
  (25 shorter events, 0.5 us)
Async XLA Ops:
  0.6 3.7 %copy-start = (bf16[1,256,192]{1,2,0:T(8,128)(2,1)S(1)}, bf16[1,256,192]{1,2,0:T(8,128)(2,1)}, u32[]{:S(2)}) copy-start(bf16[1,256,192]{1,2,0:T(8,128)(2,1)} %param.9) | copy-start | bytes 294916
  1.3 9.6 %collective-permute-start.1 = (s32[128]{0:T(128)S(1)}, s32[128]{0:T(128)S(1)}, u32[]{:S(2)}, u32[]{:S(2)}) collective-permute-start(s32[128]{0:T(128)S(1)} %dynamic-slice_bitcast_fusion.1), channel_id=1, source_target_pairs={{0,1},{1,0},{2,3},{3,2},{4,5},{5,4},{6,7},{7,6},{8,9},{9,8},{10,11... | collective-permute-start | bytes 1544 | tf_op jit(solution)/shard_map/ppermute | solution.py:263
  5.1 17.2 %all-to-all-start = ((bf16[8,128,192]{1,2,0:T(8,128)(2,1)}), bf16[8,128,192]{1,2,0:T(8,128)(2,1)S(1)}, u32[]{:S(2)}, u32[]{:S(2)}) async-start(bf16[8,128,192]{1,2,0:T(8,128)(2,1)} %broadcast_in_dim.43), calls=%async_computation | async-start | bytes 786432 | tf_op jit(solution)/shard_map/all_to_all | solution.py:247
  23.1 14.6 %all-to-all-start.1 = ((bf16[8,128,192]{1,2,0:T(8,128)(2,1)}), bf16[8,128,192]{1,2,0:T(8,128)(2,1)S(1)}, u32[]{:S(2)}, u32[]{:S(2)}) async-start(bf16[8,128,192]{1,2,0:T(8,128)(2,1)} %broadcast_in_dim.47), calls=%async_computation.1 | async-start | bytes 786432 | tf_op jit(solution)/shard_map/all_to_all | solution.py:247
  26.7 19.1 %copy-start.1 = (bf16[8,128,192]{2,1,0:T(8,128)(2,1)}, bf16[8,128,192]{2,1,0:T(8,128)(2,1)S(1)}, u32[]{:S(2)}) copy-start(bf16[8,128,192]{2,1,0:T(8,128)(2,1)S(1)} %copy.19) | copy-start | bytes 1179652
  26.8 19.1 %collective-permute-start = (bf16[1024,192]{1,0:T(8,128)(2,1)S(1)}, bf16[1024,192]{1,0:T(8,128)(2,1)S(1)}, u32[]{:S(2)}, u32[]{:S(2)}) collective-permute-start(bf16[1024,192]{1,0:T(8,128)(2,1)S(1)} %bitcast.11), channel_id=1, source_target_pairs={{0,2},{2,0},{4,6},{6,4},{1,3},{3,1},{5,7},{7,5},{8,10},{10,8},{12,... | collective-permute-start | bytes 1179656 | tf_op jit(solution)/shard_map/ppermute | solution.py:267
  37.9 7.9 %copy-start.2 = (bf16[8,128,192]{2,1,0:T(8,128)(2,1)}, bf16[8,128,192]{2,1,0:T(8,128)(2,1)S(1)}, u32[]{:S(2)}) copy-start(bf16[8,128,192]{2,1,0:T(8,128)(2,1)S(1)} %copy.22) | copy-start | bytes 1179652
  37.9 16.1 %collective-permute-start.2 = (bf16[1024,192]{1,0:T(8,128)(2,1)S(1)}, bf16[1024,192]{1,0:T(8,128)(2,1)S(1)}, u32[]{:S(2)}, u32[]{:S(2)}) collective-permute-start(bf16[1024,192]{1,0:T(8,128)(2,1)S(1)} %bitcast.13), channel_id=1, source_target_pairs={{0,2},{2,0},{4,6},{6,4},{1,3},{3,1},{5,7},{7,5},{8,10},{10,8},{12,... | collective-permute-start | bytes 1179656 | tf_op jit(solution)/shard_map/ppermute | solution.py:267
  45.9 0.8 copy-start.4
  54.1 0.8 copy-start.5
  54.9 7.2 %copy-start.3 = (f32[1,2048]{1,0:T(1,128)S(1)}, f32[1,2048]{1,0:T(1,128)}, u32[]{:S(2)}) copy-start(f32[1,2048]{1,0:T(1,128)} %get-tuple-element.16) | copy-start | bytes 24580

commit v3 on v0

v3 whole, which is shorter than its diff:
```python
import functools
import math

import jax
import jax.numpy as jnp
from jax import lax
from jax.experimental import pallas as pl
from jax.experimental.pallas import tpu as pltpu
from jax.sharding import PartitionSpec as P

EPS = 1e-06
DEPTH = 256
GROUP = 512
STEP = 256
LOG2E = math.log2(math.e)
GAIN_T = LOG2E / 0.04
GAIN_S = LOG2E / 0.1
LIMIT = 24 * 1024 * 1024
ON_CHIP = pl.BlockSpec(memory_space=pltpu.VMEM)
SCALARS = pl.BlockSpec(memory_space=pltpu.SMEM)


def shape(*dims, dtype=jnp.float32):
    return jax.ShapeDtypeStruct(dims, dtype)


def params():
    return pltpu.CompilerParams(vmem_limit_bytes=LIMIT)


def cost(flops=0, moved=0, exps=0):
    return pl.CostEstimate(flops=int(flops), bytes_accessed=int(moved), transcendentals=int(exps))


def cast_split(row):
    high = row.astype(jnp.bfloat16).astype(jnp.float32)
    mid = (row - high).astype(jnp.bfloat16).astype(jnp.float32)
    return high, mid, row - high - mid


def prep_kernel(n_own, which, teacher_ref, student_ref, center_ref, new_ref, wt_ref, ws_ref, peak_ref):
    student = student_ref[...]
    new = 0.994 * teacher_ref[...] + 0.006 * student
    new_ref[...] = new
    i = pl.program_id(0)

    @pl.when(i < n_own)
    def _():
        bot, width = new.shape
        peak = jnp.max(-center_ref[...], axis=1, keepdims=True)
        peak_ref[...] = jnp.broadcast_to(peak, peak_ref.shape)
        high, mid, low = cast_split(-center_ref[:, pl.ds(pl.multiple_of(i * width, width), width)] - peak)
        row = lax.broadcasted_iota(jnp.int32, (DEPTH - bot, width), 0)
        zero = jnp.zeros((DEPTH - bot, width), jnp.float32)
        extra = jnp.where(row == 0, high, jnp.where(row == 1, mid, jnp.where(row == 2, low, zero)))
        unit_t = new * lax.rsqrt(jnp.sum(new * new, axis=0, keepdims=True) + EPS)
        unit_s = student * lax.rsqrt(jnp.sum(student * student, axis=0, keepdims=True) + EPS)
        wt_ref[...] = jnp.concatenate([unit_t, extra], axis=0).astype(jnp.bfloat16).T
        ws_ref[...] = jnp.concatenate([unit_s, zero], axis=0).astype(jnp.bfloat16).T


def prepare(which, teacher_weight, student_weight, center, n_dp):
    bot, cols = teacher_weight.shape
    own = cols // n_dp
    width = min(1024, own)
    n_own, n_all = own // width, cols // width

    def place(i, which):
        return (0, lax.rem(i + which[0] * n_own, n_all))

    def held(i, which):
        return (lax.min(i, n_own - 1), 0)

    return pl.pallas_call(
        functools.partial(prep_kernel, n_own),
        grid_spec=pltpu.PrefetchScalarGridSpec(
            num_scalar_prefetch=1,
            grid=(n_all,),
            in_specs=[
                pl.BlockSpec((bot, width), place),
                pl.BlockSpec((bot, width), place),
                pl.BlockSpec((1, own), lambda i, which: (0, which[1])),
            ],
            out_specs=[
                pl.BlockSpec((bot, width), place),
                pl.BlockSpec((width, DEPTH), held),
                pl.BlockSpec((width, DEPTH), held),
                pl.BlockSpec((1, 128), lambda i, which: (0, 0)),
            ],
        ),
        out_shape=[
            shape(bot, cols),
            pltpu.VMEM((own, DEPTH), jnp.bfloat16),
            pltpu.VMEM((own, DEPTH), jnp.bfloat16),
            shape(1, 128),
        ],
        compiler_params=params(),
        cost_estimate=cost(20 * bot * cols, 12 * bot * cols),
        name="prep",
    )(which, teacher_weight, student_weight, center)


def pack_kernel(which, feats_ref, *rest):
    out_ref = rest[-1]
    half = out_ref.shape[2]
    lower = which[2] == 0
    if len(rest) == 2:
        index = rest[0][...]
        index = jnp.where(lower, index[:, :half], index[:, half:])
        row = lax.broadcasted_iota(jnp.int32, (feats_ref.shape[1], half), 0)
        pick = jnp.where(row == index, 1.0, 0.0).astype(jnp.bfloat16)
        mine = jnp.dot(feats_ref[...], pick, preferred_element_type=jnp.float32).astype(jnp.bfloat16)
    else:
        mine = jnp.where(lower, feats_ref[:, :half], feats_ref[:, half:])
    for i in range(out_ref.shape[0]):
        out_ref[i] = mine


def pack(which, n, feats, index=None):
    bot, crops = feats.shape
    args = [feats] if index is None else [feats, index]
    return pl.pallas_call(
        pack_kernel,
        in_specs=[SCALARS] + [ON_CHIP] * len(args),
        out_specs=ON_CHIP,
        out_shape=shape(n, bot, crops // 2, dtype=jnp.bfloat16),
        compiler_params=params(),
        cost_estimate=cost(2 * bot * crops * crops, n * bot * crops),
        name="pack_s" if index is None else "pack_t",
    )(which, *args)


def log_sum(parts):
    top = functools.reduce(jnp.maximum, parts)
    return top + jnp.log2(sum(jnp.exp2(part - top) for part in parts))


def score_kernel(teacher, last, *refs):
    if last:
        which, refs = refs[0], refs[1:]
        before, refs = refs[:3], refs[3:]
    feats_ref, w_ref, refs = refs[0], refs[1], refs[2:]
    if teacher:
        peak_ref, exp_ref, total_ref = refs
    else:
        exp_ref, total_ref, unit_ref = refs
    n, bot, width = feats_ref.shape
    cols = w_ref.shape[0]
    step = min(STEP, cols)
    per = max(1, min(n, GROUP // width))
    row = lax.broadcasted_iota(jnp.int32, (DEPTH - bot, per * width), 0)
    extra = jnp.where(row < (3 if teacher else 0), 1.0, 0.0).astype(jnp.bfloat16)
    turn = n // 2 if teacher else 0
    totals = []
    for group in range(n // per):
        values = [feats_ref[(group * per + k + turn) % n].astype(jnp.float32) for k in range(per)]
        values = jnp.concatenate(values, axis=1)
        unit = (values * lax.rsqrt(jnp.sum(values * values, axis=0, keepdims=True) + EPS)).astype(jnp.bfloat16)
        lanes = slice(group * per * width, (group + 1) * per * width)
        if not teacher:
            unit_ref[:, lanes] = unit
        held = jnp.concatenate([unit, extra], axis=0)
        total = jnp.zeros((8, per * width), jnp.float32)
        for at in range(0, cols, step):
            score = jnp.dot(w_ref[at:at + step, :], held, preferred_element_type=jnp.float32)
            exps = jnp.exp2(score * (GAIN_T if teacher else GAIN_S))
            total = total + jnp.sum(exps.reshape(step // 8, 8, per * width), axis=0)
            exp_ref[at:at + step, lanes] = exps.astype(jnp.bfloat16)
        totals.append(jnp.sum(total, axis=0, keepdims=True))
    total = jnp.concatenate(totals, axis=1)
    if teacher:
        total = jnp.log2(total) + GAIN_T * peak_ref[:, :1]
    if not last:
        total_ref[...] = total
        return
    lower = which[2] == 0
    s_mine, s_pair, t_mine = [ref[...] for ref in before]
    rows = [
        jnp.where(lower, s_mine, s_pair),
        jnp.where(lower, s_pair, s_mine),
        jnp.where(lower, t_mine, total),
        jnp.where(lower, total, t_mine),
    ]
    rows = jnp.concatenate(rows, axis=0)
    for i in range(total_ref.shape[0]):
        total_ref[i] = rows


def scores(teacher, feats, weights, peak=None, last=None):
    n, bot, width = feats.shape
    cols = weights.shape[0]
    rows = n * width
    args, in_specs = [feats, weights], [ON_CHIP] * 2
    if teacher:
        args, in_specs = args + [peak], in_specs + [ON_CHIP]
    if last is not None:
        which, copies, before = last
        args, in_specs = [which, *before, *args], [SCALARS] + [ON_CHIP] * 3 + in_specs
    out_shape = [
        pltpu.VMEM((cols, rows), jnp.bfloat16),
        shape(1, rows) if last is None else shape(copies, 4, rows),
    ]
    if not teacher:
        out_shape.append(pltpu.VMEM((bot, rows), jnp.bfloat16))
    return pl.pallas_call(
        functools.partial(score_kernel, teacher, last is not None),
        in_specs=in_specs,
        out_specs=[ON_CHIP] * len(out_shape),
        out_shape=out_shape,
        compiler_params=params(),
        cost_estimate=cost(2 * rows * cols * DEPTH, 2 * rows * cols, rows * cols),
        name="scores_t" if teacher else "scores_s",
    )(*args)


def combine(parts):
    total_s = sum(part[:2] for part in parts)
    return total_s, log_sum([part[2:] for part in parts])


def relay_kernel(in_ref, out_ref):
    rows = jnp.concatenate(combine([in_ref[i] for i in range(in_ref.shape[0])]), axis=0)
    for i in range(out_ref.shape[0]):
        out_ref[i] = rows


def relay(parts, copies):
    return pl.pallas_call(
        relay_kernel,
        in_specs=[ON_CHIP],
        out_specs=ON_CHIP,
        out_shape=shape(copies, *parts.shape[1:]),
        compiler_params=params(),
        cost_estimate=cost(0, copies * parts[0].size * 4),
        name="relay",
    )(parts)


def grad_kernel(which, totals_ref, peak_ref, unit_a, unit_b, exps_a, exps_b, expt_a, expt_b, weight_ref, out_ref):
    total_s, log_t = combine([totals_ref[i] for i in range(totals_ref.shape[0])])
    scale_s = 10.0 / total_s
    scale_t = -10.0 * jnp.exp2(GAIN_T * peak_ref[:, :1] - log_t)
    lower = which[2] == 0
    sides = []
    for at, unit_ref, exp_s, exp_t in ((0, unit_a, exps_a, expt_a), (1, unit_b, exps_b, expt_b)):
        unit = unit_ref[...].astype(jnp.float32)
        for scale, exp_ref in ((scale_s, exp_s), (scale_t, exp_t)):
            mine = jnp.where(lower, scale[at:at + 1], scale[1 - at:2 - at])
            sides.append(((unit * mine).astype(jnp.bfloat16), exp_ref))
    cols = weight_ref.shape[1]
    step = min(512, cols)
    for at in range(0, cols, step):
        grad = sum(
            lax.dot_general(
                exp_ref[at:at + step, :], feats, (((1,), (1,)), ((), ())), preferred_element_type=jnp.float32
            )
            for feats, exp_ref in sides
        )
        grad = grad.T
        weight = weight_ref[:, at:at + step]
        scale = lax.rsqrt(jnp.sum(weight * weight, axis=0, keepdims=True) + EPS)
        unit = weight * scale
        out_ref[:, at:at + step] = (grad - unit * jnp.sum(unit * grad, axis=0, keepdims=True)) * scale


def gradient(which, totals, peak, units, exps_s, exps_t, student_weight):
    cols, rows = exps_s[0].shape
    bot = units[0].shape[0]
    own = lambda i, which: (0, which[0])
    whole = ON_CHIP
    return pl.pallas_call(
        grad_kernel,
        grid_spec=pltpu.PrefetchScalarGridSpec(
            num_scalar_prefetch=1,
            grid=(1,),
            in_specs=[whole] * 8 + [pl.BlockSpec((bot, cols), own)],
            out_specs=pl.BlockSpec((bot, cols), lambda i, which: (0, 0)),
        ),
        out_shape=shape(bot, cols),
        compiler_params=params(),
        cost_estimate=cost(8 * rows * cols * DEPTH, 8 * bot * cols),
        name="gradient",
    )(which, totals, peak, *units, *exps_s, *exps_t, student_weight)


def shards(teacher_weight, student_weight, teacher_feats, student_feats, pairing, center):
    n_dp, n_fsdp, n_proto = [lax.axis_size(axis) for axis in ("dp", "fsdp", "proto")]
    dp = lax.axis_index("dp")
    others = ("dp", "fsdp")
    n_others = n_dp * n_fsdp
    core = lax.rem(lax.axis_index("proto"), 2)
    which = jnp.stack([dp, lax.axis_index("fsdp") * n_dp + dp, core]).astype(jnp.int32)

    def spread(copies, axes):
        return lax.all_to_all(copies, axes, 0, 0, tiled=True)

    def from_pair(mine):
        return lax.ppermute(mine, "proto", [(i, i ^ 1) for i in range(n_proto)])

    index = lax.ppermute(pairing, "dp", [(i, i ^ 1) for i in range(n_dp)])
    mine_s = spread(pack(which, n_others, student_feats[0].T), others)
    mine_t = spread(pack(which, n_others, teacher_feats[0].T, index), others)
    teacher_new, w_t, w_s, peak = prepare(which, teacher_weight, student_weight, center[None, :], n_dp)
    pair_s = from_pair(mine_s)
    exps_a, total_a, unit_a = scores(False, mine_s, w_s)
    exps_b, total_b, unit_b = scores(False, pair_s, w_s)
    pair_t = from_pair(mine_t)
    expt_a, total_c = scores(True, mine_t, w_t, peak)
    expt_b, totals = scores(True, pair_t, w_t, peak, (which, n_proto, (total_a, total_b, total_c)))
    totals = spread(relay(spread(totals, "proto"), n_others), others)
    student_grad = gradient(which, totals, peak, (unit_a, unit_b), (exps_a, exps_b), (expt_a, expt_b), student_weight)
    return (teacher_new, student_grad)


def solution(mesh):
    placed = (
        P(None, ("proto", "fsdp")),
        P(None, ("proto", "fsdp")),
        P("dp", "fsdp", None),
        P("dp", "fsdp", None),
        P("dp", "fsdp"),
        P("proto"),
    )
    return jax.shard_map(
        shards,
        mesh=mesh,
        in_specs=placed,
        out_specs=(P(None, ("proto", "fsdp")), P(None, ("proto", "fsdp", "dp"))),
        check_vma=False,
    )
```

time: 516 us -> 76.5 us (0.15)
  waiting for transfers between devices: 418 us -> 19.3 us
  matrix products: 39.8 us -> 0 us
  other arithmetic: 25.6 us -> 0.08 us
  Pallas kernels: 0 us -> 19.9 us
  between operations: 13.9 us -> 0.72 us
  starting transfers between devices: 3.13 us -> 12.8 us
    all_gather x2 -> x0, waiting for transfers between devices: 211 us -> none  [the longest x1 108 us: shards(): lax.all_gather(w_student, 'fsdp', axis=1, tiled=True)]
    reduce_scatter x1 -> x0, waiting for transfers between devices: 203 us -> none  [shards(): lax.psum_scatter(lax.dot_general(derivs, z_student, (((0,), (0,)), ((), (...]
    dot_general x3 -> x0, matrix products: 39.8 us -> none  [the longest x1 17.4 us: shards(): lax.dot_general(derivs, z_student, (((0,), (0,)), ((), ())), preferred_el...]
    reduce_sum x7 -> x0, other arithmetic: 20.9 us -> none  [the longest x1 12.1 us: shards(): jnp.sum(exp_s, axis=1)]
    pallas_call x0 -> x9, Pallas kernels: none -> 19.9 us  [the longest x1 6.71 us: gradient(): pl.pallas_call(grad_kernel, grid_spec=pltpu.PrefetchScalarGridSpec(num_sc...]
    all_to_all x0 -> x2, blocking collectives: none -> 16.8 us  [spread(): return lax.all_to_all(copies, axes, 0, 0, tiled=True)]
    all_to_all x0 -> x2, waiting for transfers between devices: none -> 16.4 us  [spread(): return lax.all_to_all(copies, axes, 0, 0, tiled=True)]
    all_to_all x0 -> x2, starting transfers between devices: none -> 10.7 us  [spread(): return lax.all_to_all(copies, axes, 0, 0, tiled=True)]
  transfers between devices with their start and end apart: 4 -> 5, of which waited for: 4 -> 3; matrix products, arithmetic and copies ran while one was open for 3% -> 0% of each run, Pallas kernels for 0% -> 13%
where the time goes in v3:
time: 76.5 us; the launch traced here: 76 us
  Pallas kernels  19.9 us (26%)
  waiting for transfers between devices  19.3 us (25%)
  blocking collectives  16.8 us (22%)
  starting transfers between devices  12.8 us (17%)
  local copies, waits for them, and re-layouts  6.41 us (8%)
    all_to_all x2, blocking collectives, spread(): return lax.all_to_all(copies, axes, 0, 0, tiled=True)  16.8 us
    all_to_all x2, waiting for transfers between devices, spread(): return lax.all_to_all(copies, axes, 0, 0, tiled=True)  16.4 us
    all_to_all x2, starting transfers between devices, spread(): return lax.all_to_all(copies, axes, 0, 0, tiled=True)  10.7 us
    pallas_call x1, Pallas kernels, gradient(): pl.pallas_call(grad_kernel, grid_spec=pltpu.PrefetchScalarGridSpec(num_sc...  6.71 us
    unnamed x12, local copies, waits for them, and re-layouts  6.41 us
    pallas_call x4, Pallas kernels, scores(): pl.pallas_call(functools.partial(score_kernel, teacher, last is not None)...  6.35 us
    pallas_call x1, Pallas kernels, prepare(): pl.pallas_call(functools.partial(prep_kernel, n_own), grid_spec=pltpu.Pre...  4.01 us
    ppermute x1, waiting for transfers between devices, shards(): index = lax.ppermute(pairing, 'dp', [(i, i ^ 1) for i in range(n_dp)])  2.85 us
  transfers between devices with their start and end apart: 5, of which 3 were waited for; matrix products, arithmetic and copies ran while one was open for 0% of the time, Pallas kernels for 13%

profile of v3, /device:TPU:0, one launch (start us, length us, event | category | flops | bytes accessed | tf_op | source)
XLA Modules:
  0.0 76.0 jit_solution(3207563137692754421)
XLA Ops:
  0.6 0.1 pad_add_fusion.which.refs_0_
  0.7 0.9 %copy-done.3 = bf16[1,256,192]{1,2,0:T(8,128)(2,1)S(1)} copy-done((bf16[1,256,192]{1,2,0:T(8,128)(2,1)S(1)}, bf16[1,256,192]{1,2,0:T(8,128)(2,1)}, u32[]{:S(2)}) %copy-start.3) | copy-done | bytes 98328
  1.6 1.3 %pack_s.1 = bf16[8,192,128]{2,1,0:T(8,128)(2,1)} custom-call(s32[3]{0:T(128)S(1)} %pad_add_fusion.which.refs_0_, bf16[192,256]{1,0:T(8,128)(2,1)S(1)} %bitcast.10), custom_call_target="tpu_custom_call" | custom-call | flops 25165824 | bytes 393216 | tf_op jit(solution)/shard_map/pack_s/pallas_call | solution.py:122
  3.0 7.3 %all-to-all-start = ((bf16[8,192,128]{2,1,0:T(8,128)(2,1)}), bf16[8,192,128]{2,1,0:T(8,128)(2,1)S(1)}, u32[]{:S(2)}, u32[]{:S(2)}) async-start(bf16[8,192,128]{2,1,0:T(8,128)(2,1)} %pack_s.1), calls=%async_computation | async-start | bytes 786432 | tf_op jit(solution)/shard_map/all_to_all | solution.py:295
  10.2 2.0 %collective-permute-start.1 = (s32[1,256]{1,0:T(1,128)}, s32[1,256]{1,0:T(1,128)S(1)}, u32[]{:S(2)}, u32[]{:S(2)}) collective-permute-start(s32[1,256]{1,0:T(1,128)} %param.10), channel_id=1, source_target_pairs={{0,1},{1,0},{2,3},{3,2},{4,5},{5,4},{6,7},{7,6},{8,9},{9,8},{10,11... | collective-permute-start | bytes 3080 | tf_op jit(solution)/shard_map/ppermute | solution.py:300
  12.2 2.8 %collective-permute-done.1.rest_0_ = s32[1,256]{1,0:T(1,128)S(1)} collective-permute-done((s32[1,256]{1,0:T(1,128)}, s32[1,256]{1,0:T(1,128)S(1)}, u32[]{:S(2)}, u32[]{:S(2)}) %collective-permute-start.1) | collective-permute-done | bytes 1056 | tf_op jit(solution)/shard_map/ppermute | solution.py:300
  15.1 0.9 %copy-done.4 = bf16[1,256,192]{1,2,0:T(8,128)(2,1)S(1)} copy-done((bf16[1,256,192]{1,2,0:T(8,128)(2,1)S(1)}, bf16[1,256,192]{1,2,0:T(8,128)(2,1)}, u32[]{:S(2)}) %copy-start.4) | copy-done | bytes 98328
  16.0 1.5 %pack_t.1 = bf16[8,192,128]{2,1,0:T(8,128)(2,1)} custom-call(s32[3]{0:T(128)S(1)} %pad_add_fusion.which.refs_0_, bf16[192,256]{1,0:T(8,128)(2,1)S(1)} %bitcast.11, s32[1,256]{1,0:T(1,128)S(1)} %collective-permute-done.1.rest_0_), custom_call_target="tpu_custom_call" | custom-call | flops 25165824 | bytes 393216 | tf_op jit(solution)/shard_map/pack_t/pallas_call | solution.py:122
  17.4 5.3 %all-to-all-done.refs_0_ = bf16[8,192,128]{2,1,0:T(8,128)(2,1)S(1)} async-done(((bf16[8,192,128]{2,1,0:T(8,128)(2,1)}), bf16[8,192,128]{2,1,0:T(8,128)(2,1)S(1)}, u32[]{:S(2)}, u32[]{:S(2)}) %all-to-all-start) | async-done | bytes 393248 | tf_op jit(solution)/shard_map/all_to_all | solution.py:295
  22.8 3.5 %all-to-all-start.1 = ((bf16[8,192,128]{2,1,0:T(8,128)(2,1)}), bf16[8,192,128]{2,1,0:T(8,128)(2,1)S(1)}, u32[]{:S(2)}, u32[]{:S(2)}) async-start(bf16[8,192,128]{2,1,0:T(8,128)(2,1)} %pack_t.1), calls=%async_computation.1 | async-start | bytes 786432 | tf_op jit(solution)/shard_map/all_to_all | solution.py:295
  26.2 0.1 collective-permute-start
  26.3 11.1 %all-to-all-done.1.refs_0_ = bf16[8,192,128]{2,1,0:T(8,128)(2,1)S(1)} async-done(((bf16[8,192,128]{2,1,0:T(8,128)(2,1)}), bf16[8,192,128]{2,1,0:T(8,128)(2,1)S(1)}, u32[]{:S(2)}, u32[]{:S(2)}) %all-to-all-start.1) | async-done | bytes 393248 | tf_op jit(solution)/shard_map/all_to_all | solution.py:295
  37.4 1.9 %copy-done = f32[192,4096]{1,0:T(8,128)S(1)} copy-done((f32[192,4096]{1,0:T(8,128)S(1)}, f32[192,4096]{1,0:T(8,128)}, u32[]{:S(2)}) %copy-start) | copy-done | bytes 3145752
  39.3 1.9 %copy-done.2 = f32[192,4096]{1,0:T(8,128)S(1)} copy-done((f32[192,4096]{1,0:T(8,128)S(1)}, f32[192,4096]{1,0:T(8,128)}, u32[]{:S(2)}) %copy-start.2) | copy-done | bytes 3145752
  41.2 0.8 %copy-done.5 = f32[16384]{0:T(1024)S(1)} copy-done((f32[16384]{0:T(1024)S(1)}, f32[16384]{0:T(1024)}, u32[]{:S(2)}) %copy-start.5) | copy-done | bytes 65560
  42.0 4.0 %prep.1 = (f32[192,4096]{1,0:T(8,128)}, bf16[2048,256]{1,0:T(8,128)(2,1)S(1)}, bf16[2048,256]{1,0:T(8,128)(2,1)S(1)}, f32[1,128]{1,0:T(1,128)S(1)}) custom-call(s32[3]{0:T(128)S(1)} %pad_add_fusion.which.refs_0_, f32[192,4096]{1,0:T(8,128)S(1)} %copy-done.2, f32[192,4096]{1,0:T(8,128)S(1)} %copy-done, f32[1,16384]{1,0:T(1,128)S(1)} %bitcast.12), custom_call_target="tpu_custom_call" | custom-call | flops 15728640 | bytes 9437184 | tf_op jit(solution)/shard_map/prep/pallas_call | solution.py:74
  46.0 1.5 %scores_s.2 = (bf16[2048,1024]{1,0:T(8,128)(2,1)S(1)}, f32[1,1024]{1,0:T(1,128)S(1)}, bf16[192,1024]{1,0:T(8,128)(2,1)S(1)}) custom-call(bf16[8,192,128]{2,1,0:T(8,128)(2,1)S(1)} %all-to-all-done.refs_0_, bf16[2048,256]{1,0:T(8,128)(2,1)S(1)} %get-tuple-element.17.refs_1_), custom_call_target="tpu_custom_call" | custom-call | flops 1073741824 | bytes 4194304 | tf_op jit(solution)/shard_map/scores_s/pallas_call | solution.py:205
  47.5 1.4 %scores_t.2 = (bf16[2048,1024]{1,0:T(8,128)(2,1)S(1)}, f32[1,1024]{1,0:T(1,128)S(1)}) custom-call(bf16[8,192,128]{2,1,0:T(8,128)(2,1)S(1)} %all-to-all-done.1.refs_0_, bf16[2048,256]{1,0:T(8,128)(2,1)S(1)} %get-tuple-element.20.refs_1_.refs_5_, f32[1,128]{1,0:T(1,128)S(1)} %get-tuple-element.21.refs_2_.refs_6_.peak_ref), custom_call_target="tpu_custom_call" | custom-call | flops 1073741824 | bytes 4194304 | tf_op jit(solution)/shard_map/scores_t/pallas_call | solution.py:205
  48.9 0.0 copy-start.1
  49.0 1.5 %scores_s.3 = (bf16[2048,1024]{1,0:T(8,128)(2,1)S(1)}, f32[1,1024]{1,0:T(1,128)S(1)}, bf16[192,1024]{1,0:T(8,128)(2,1)S(1)}) custom-call(bf16[8,192,128]{2,1,0:T(8,128)(2,1)S(1)} %collective-permute-done.refs_0_, bf16[2048,256]{1,0:T(8,128)(2,1)S(1)} %get-tuple-element.17.refs_1_), custom_call_target="tpu_custom_call" | custom-call | flops 1073741824 | bytes 4194304 | tf_op jit(solution)/shard_map/scores_s/pallas_call | solution.py:205
  50.4 2.0 %scores_t.3 = (bf16[2048,1024]{1,0:T(8,128)(2,1)S(1)}, f32[4,4,1024]{2,1,0:T(4,128)S(1)}) custom-call(s32[3]{0:T(128)S(1)} %pad_add_fusion.which.refs_0_, f32[1,1024]{1,0:T(1,128)S(1)} %get-tuple-element.18.refs_1_, f32[1,1024]{1,0:T(1,128)S(1)} %get-tuple-element.19.refs_2_, f32[1,1024]{1,0:T(1,128)S(1)} %get-tuple-element.22.refs_3_, ...), custom_call_target="tpu_custom_call" | custom-call | flops 1073741824 | bytes 4194304 | tf_op jit(solution)/shard_map/scores_t/pallas_call | solution.py:205
  52.4 6.8 %all_to_all.20.in_ref = f32[4,4,1024]{2,1,0:T(4,128)S(1)} all-to-all(f32[4,4,1024]{2,1,0:T(4,128)S(1)} %get-tuple-element.23), channel_id=1, replica_groups=mesh['fsdp'=4,'proto'=4,'dp'=2] {'proto'}, dimensions={0} | all-to-all | bytes 131072 | tf_op jit(solution)/shard_map/all_to_all | solution.py:295
  59.3 10.0 %all_to_all.21.totals_ref = f32[8,4,1024]{2,1,0:T(4,128)S(1)} all-to-all(f32[8,4,1024]{2,1,0:T(4,128)S(1)} %relay.1), channel_id=1, replica_groups=mesh['fsdp'=4,'proto'=4,'dp'=2] {'dp','fsdp'}, dimensions={0} | all-to-all | bytes 262144 | tf_op jit(solution)/shard_map/all_to_all | solution.py:295
  69.3 6.7 %gradient.1 = f32[192,2048]{1,0:T(8,128)} custom-call(s32[3]{0:T(128)S(1)} %pad_add_fusion.which.refs_0_, f32[8,4,1024]{2,1,0:T(4,128)S(1)} %all_to_all.21.totals_ref, f32[1,128]{1,0:T(1,128)S(1)} %get-tuple-element.21.refs_2_.refs_6_.peak_ref, bf16[192,1024]{1,0:T(8,128)(2,1)S(1)} %get-tuple-element.24.unit_a, ...), custom_call_target="tpu_custom_call" | custom-call | flops 4294967296 | bytes 3145728 | tf_op jit(solution)/shard_map/gradient/pallas_call | solution.py:271
  (10 shorter events, 0.1 us)
Async XLA Ops:
  0.7 0.9 %copy-start.3 = (bf16[1,256,192]{1,2,0:T(8,128)(2,1)S(1)}, bf16[1,256,192]{1,2,0:T(8,128)(2,1)}, u32[]{:S(2)}) copy-start(bf16[1,256,192]{1,2,0:T(8,128)(2,1)} %param.9) | copy-start | bytes 294916
  3.0 19.8 %all-to-all-start = ((bf16[8,192,128]{2,1,0:T(8,128)(2,1)}), bf16[8,192,128]{2,1,0:T(8,128)(2,1)S(1)}, u32[]{:S(2)}, u32[]{:S(2)}) async-start(bf16[8,192,128]{2,1,0:T(8,128)(2,1)} %pack_s.1), calls=%async_computation | async-start | bytes 786432 | tf_op jit(solution)/shard_map/all_to_all | solution.py:295
  10.2 4.9 %collective-permute-start.1 = (s32[1,256]{1,0:T(1,128)}, s32[1,256]{1,0:T(1,128)S(1)}, u32[]{:S(2)}, u32[]{:S(2)}) collective-permute-start(s32[1,256]{1,0:T(1,128)} %param.10), channel_id=1, source_target_pairs={{0,1},{1,0},{2,3},{3,2},{4,5},{5,4},{6,7},{7,6},{8,9},{9,8},{10,11... | collective-permute-start | bytes 3080 | tf_op jit(solution)/shard_map/ppermute | solution.py:300
  15.1 0.9 %copy-start.4 = (bf16[1,256,192]{1,2,0:T(8,128)(2,1)S(1)}, bf16[1,256,192]{1,2,0:T(8,128)(2,1)}, u32[]{:S(2)}) copy-start(bf16[1,256,192]{1,2,0:T(8,128)(2,1)} %param.8) | copy-start | bytes 294916
  22.8 14.6 %all-to-all-start.1 = ((bf16[8,192,128]{2,1,0:T(8,128)(2,1)}), bf16[8,192,128]{2,1,0:T(8,128)(2,1)S(1)}, u32[]{:S(2)}, u32[]{:S(2)}) async-start(bf16[8,192,128]{2,1,0:T(8,128)(2,1)} %pack_t.1), calls=%async_computation.1 | async-start | bytes 786432 | tf_op jit(solution)/shard_map/all_to_all | solution.py:295
  26.2 22.7 %collective-permute-start = (bf16[8,192,128]{2,1,0:T(8,128)(2,1)S(1)}, bf16[8,192,128]{2,1,0:T(8,128)(2,1)S(1)}, u32[]{:S(2)}, u32[]{:S(2)}) collective-permute-start(bf16[8,192,128]{2,1,0:T(8,128)(2,1)S(1)} %all-to-all-done.refs_0_), channel_id=1, source_target_pairs={{0,2},{2,0},{4,6},{6,4},{1,3},{3,1},{5,7},{7,5},{8,10},{10,8},{12,... | collective-permute-start | bytes 1179656 | tf_op jit(solution)/shard_map/ppermute | solution.py:298
  37.4 13.0 %collective-permute-start.2 = (bf16[8,192,128]{2,1,0:T(8,128)(2,1)S(1)}, bf16[8,192,128]{2,1,0:T(8,128)(2,1)S(1)}, u32[]{:S(2)}, u32[]{:S(2)}) collective-permute-start(bf16[8,192,128]{2,1,0:T(8,128)(2,1)S(1)} %all-to-all-done.1.refs_0_), channel_id=1, source_target_pairs={{0,2},{2,0},{4,6},{6,4},{1,3},{3,1},{5,7},{7,5},{8,10},{10,8},{12,... | collective-permute-start | bytes 1179656 | tf_op jit(solution)/shard_map/ppermute | solution.py:298
  37.4 1.9 %copy-start = (f32[192,4096]{1,0:T(8,128)S(1)}, f32[192,4096]{1,0:T(8,128)}, u32[]{:S(2)}) copy-start(f32[192,4096]{1,0:T(8,128)} %weight_ref.1) | copy-start | bytes 9437188
  39.3 1.9 %copy-start.2 = (f32[192,4096]{1,0:T(8,128)S(1)}, f32[192,4096]{1,0:T(8,128)}, u32[]{:S(2)}) copy-start(f32[192,4096]{1,0:T(8,128)} %teacher_ref.1) | copy-start | bytes 9437188
  41.2 0.8 %copy-start.5 = (f32[16384]{0:T(1024)S(1)}, f32[16384]{0:T(1024)}, u32[]{:S(2)}) copy-start(f32[16384]{0:T(1024)} %param.11) | copy-start | bytes 196612
  48.9 20.3 %copy-start.1 = (f32[192,4096]{1,0:T(8,128)S(1)}, f32[192,4096]{1,0:T(8,128)}, u32[]{:S(2)}) copy-start(f32[192,4096]{1,0:T(8,128)} %weight_ref.1) | copy-start | bytes 9437188

commit v4 on v3

--- a/solution.py
+++ b/solution.py
@@ -61,6 +61,8 @@
 
 def prepare(which, teacher_weight, student_weight, center, n_dp):
     bot, cols = teacher_weight.shape
+    teacher_weight = pltpu.with_memory_space_constraint(teacher_weight, pltpu.HBM)
+    student_weight = pltpu.with_memory_space_constraint(student_weight, pltpu.HBM)
     own = cols // n_dp
     width = min(1024, own)
     n_own, n_all = own // width, cols // width
@@ -104,7 +106,7 @@
     out_ref = rest[-1]
     half = out_ref.shape[2]
     lower = which[2] == 0
-    if len(rest) == 2:
+    if len(rest) > 1:
         index = rest[0][...]
         index = jnp.where(lower, index[:, :half], index[:, half:])
         row = lax.broadcasted_iota(jnp.int32, (feats_ref.shape[1], half), 0)
@@ -116,9 +118,9 @@
         out_ref[i] = mine
 
 
-def pack(which, n, feats, index=None):
+def pack(which, n, feats, index=None, after=None):
     bot, crops = feats.shape
-    args = [feats] if index is None else [feats, index]
+    args = [feats] if index is None else [feats, index, after]
     return pl.pallas_call(
         pack_kernel,
         in_specs=[SCALARS] + [ON_CHIP] * len(args),
@@ -130,30 +132,52 @@
     )(which, *args)
 
 
+def gate_kernel(feats_ref, after_ref, out_ref):
+    pass
+
+
+def gate(feats, after):
+    return pl.pallas_call(
+        gate_kernel,
+        in_specs=[pl.BlockSpec(memory_space=pl.ANY)] * 2,
+        out_specs=pl.BlockSpec(memory_space=pl.ANY),
+        out_shape=pltpu.VMEM(feats.shape, feats.dtype),
+        input_output_aliases={0: 0},
+        compiler_params=params(),
+        cost_estimate=cost(),
+        name="gate",
+    )(feats, after)
+
+
 def log_sum(parts):
     top = functools.reduce(jnp.maximum, parts)
     return top + jnp.log2(sum(jnp.exp2(part - top) for part in parts))
+
+
+def by_view(which, rows):
+    half = rows.shape[1] // 2
+    return jnp.where(which[0] == 0, rows, jnp.concatenate([rows[:, half:], rows[:, :half]], axis=1))
 
 
 def score_kernel(teacher, last, *refs):
     if last:
         which, refs = refs[0], refs[1:]
         before, refs = refs[:3], refs[3:]
-    feats_ref, w_ref, refs = refs[0], refs[1], refs[2:]
+    feats_refs, w_ref, refs = refs[:2], refs[2], refs[3:]
     if teacher:
         peak_ref, exp_ref, total_ref = refs
     else:
         exp_ref, total_ref, unit_ref = refs
-    n, bot, width = feats_ref.shape
+    n, bot, width = feats_refs[0].shape
     cols = w_ref.shape[0]
     step = min(STEP, cols)
     per = max(1, min(n, GROUP // width))
     row = lax.broadcasted_iota(jnp.int32, (DEPTH - bot, per * width), 0)
     extra = jnp.where(row < (3 if teacher else 0), 1.0, 0.0).astype(jnp.bfloat16)
-    turn = n // 2 if teacher else 0
     totals = []
-    for group in range(n // per):
-        values = [feats_ref[(group * per + k + turn) % n].astype(jnp.float32) for k in range(per)]
+    for group in range(2 * n // per):
+        at = [divmod(group * per + k, n) for k in range(per)]
+        values = [feats_refs[view][block].astype(jnp.float32) for view, block in at]
         values = jnp.concatenate(values, axis=1)
         unit = (values * lax.rsqrt(jnp.sum(values * values, axis=0, keepdims=True) + EPS)).astype(jnp.bfloat16)
         lanes = slice(group * per * width, (group + 1) * per * width)
@@ -181,16 +205,16 @@
         jnp.where(lower, t_mine, total),
         jnp.where(lower, total, t_mine),
     ]
-    rows = jnp.concatenate(rows, axis=0)
+    rows = by_view(which, jnp.concatenate(rows, axis=0))
     for i in range(total_ref.shape[0]):
         total_ref[i] = rows
 
 
 def scores(teacher, feats, weights, peak=None, last=None):
-    n, bot, width = feats.shape
+    n, bot, width = feats[0].shape
     cols = weights.shape[0]
-    rows = n * width
-    args, in_specs = [feats, weights], [ON_CHIP] * 2
+    rows = 2 * n * width
+    args, in_specs = [*feats, weights], [ON_CHIP] * 3
     if teacher:
         args, in_specs = args + [peak], in_specs + [ON_CHIP]
     if last is not None:
@@ -238,8 +262,8 @@
 
 def grad_kernel(which, totals_ref, peak_ref, unit_a, unit_b, exps_a, exps_b, expt_a, expt_b, weight_ref, out_ref):
     total_s, log_t = combine([totals_ref[i] for i in range(totals_ref.shape[0])])
-    scale_s = 10.0 / total_s
-    scale_t = -10.0 * jnp.exp2(GAIN_T * peak_ref[:, :1] - log_t)
+    scale_s = by_view(which, 10.0 / total_s)
+    scale_t = by_view(which, -10.0 * jnp.exp2(GAIN_T * peak_ref[:, :1] - log_t))
     lower = which[2] == 0
     sides = []
     for at, unit_ref, exp_s, exp_t in ((0, unit_a, exps_a, expt_a), (1, unit_b, exps_b, expt_b)):
@@ -297,16 +321,20 @@
     def from_pair(mine):
         return lax.ppermute(mine, "proto", [(i, i ^ 1) for i in range(n_proto)])
 
-    index = lax.ppermute(pairing, "dp", [(i, i ^ 1) for i in range(n_dp)])
-    mine_s = spread(pack(which, n_others, student_feats[0].T), others)
-    mine_t = spread(pack(which, n_others, teacher_feats[0].T, index), others)
+    def from_view(mine):
+        return lax.ppermute(mine, "dp", [(i, i ^ 1) for i in range(n_dp)])
+
+    index = from_view(pairing)
+    own_s = spread(pack(which, n_fsdp, student_feats[0].T), "fsdp")
     teacher_new, w_t, w_s, peak = prepare(which, teacher_weight, student_weight, center[None, :], n_dp)
-    pair_s = from_pair(mine_s)
-    exps_a, total_a, unit_a = scores(False, mine_s, w_s)
-    exps_b, total_b, unit_b = scores(False, pair_s, w_s)
-    pair_t = from_pair(mine_t)
-    expt_a, total_c = scores(True, mine_t, w_t, peak)
-    expt_b, totals = scores(True, pair_t, w_t, peak, (which, n_proto, (total_a, total_b, total_c)))
+    own_t = spread(pack(which, n_fsdp, teacher_feats[0].T, index, peak), "fsdp")
+    other_s = from_view(own_s)
+    exps_a, total_a, unit_a = scores(False, (own_s, other_s), w_s)
+    exps_b, total_b, unit_b = scores(False, (from_pair(own_s), from_pair(other_s)), w_s)
+    other_t = gate(from_view(own_t), total_b)
+    expt_a, total_c = scores(True, (other_t, own_t), w_t, peak)
+    last = (which, n_proto, (total_a, total_b, total_c))
+    expt_b, totals = scores(True, (from_pair(other_t), from_pair(own_t)), w_t, peak, last)
     totals = spread(relay(spread(totals, "proto"), n_others), others)
     student_grad = gradient(which, totals, peak, (unit_a, unit_b), (exps_a, exps_b), (expt_a, expt_b), student_weight)
     return (teacher_new, student_grad)

time: 76.5 us -> 67 us (0.88)
  waiting for transfers between devices: 19.3 us -> 8.46 us
  local copies, waits for them, and re-layouts: 6.41 us -> 1.74 us
  starting transfers between devices: 12.8 us -> 15.4 us
  Pallas kernels: 19.9 us -> 21.8 us
  blocking collectives: 16.8 us -> 18.3 us
    all_to_all x2, waiting for transfers between devices: 16.4 us -> 5.74 us  [spread(): return lax.all_to_all(copies, axes, 0, 0, tiled=True)]
    unnamed x12 -> x8, local copies, waits for them, and re-layouts: 6.41 us -> 1.74 us
    pallas_call x1, Pallas kernels: 4.01 us -> 6.04 us  [prepare(): pl.pallas_call(functools.partial(prep_kernel, n_own), grid_spec=pltpu.Pre...]
    ppermute x1 -> x3, starting transfers between devices: 2.02 us -> 3.61 us  [from_view(): return lax.ppermute(mine, 'dp', [(i, i ^ 1) for i in range(n_dp)])]
    all_to_all x2, blocking collectives: 16.8 us -> 18.3 us  [spread(): return lax.all_to_all(copies, axes, 0, 0, tiled=True)]
    ppermute x1 -> x3, waiting for transfers between devices: 2.85 us -> 2.71 us  [from_view(): return lax.ppermute(mine, 'dp', [(i, i ^ 1) for i in range(n_dp)])]
  transfers between devices with their start and end apart: 5 -> 9, of which waited for: 3 -> 2; matrix products, arithmetic and copies ran while one was open for 0% -> 0% of each run, Pallas kernels for 13% -> 18%
where the time goes in v4:
time: 67 us; the launch traced here: 66.5 us
  Pallas kernels  21.8 us (33%)
  blocking collectives  18.3 us (27%)
  starting transfers between devices  15.4 us (23%)
  waiting for transfers between devices  8.46 us (13%)
  local copies, waits for them, and re-layouts  1.74 us (3%)
  between operations  0.71 us (1%)
    all_to_all x2, blocking collectives, spread(): return lax.all_to_all(copies, axes, 0, 0, tiled=True)  18.3 us
    all_to_all x2, starting transfers between devices, spread(): return lax.all_to_all(copies, axes, 0, 0, tiled=True)  11.3 us
    pallas_call x1, Pallas kernels, gradient(): pl.pallas_call(grad_kernel, grid_spec=pltpu.PrefetchScalarGridSpec(num_sc...  6.73 us
    pallas_call x4, Pallas kernels, scores(): pl.pallas_call(functools.partial(score_kernel, teacher, last is not None)...  6.36 us
    pallas_call x1, Pallas kernels, prepare(): pl.pallas_call(functools.partial(prep_kernel, n_own), grid_spec=pltpu.Pre...  6.04 us
    all_to_all x2, waiting for transfers between devices, spread(): return lax.all_to_all(copies, axes, 0, 0, tiled=True)  5.74 us
    ppermute x3, starting transfers between devices, from_view(): return lax.ppermute(mine, 'dp', [(i, i ^ 1) for i in range(n_dp)])  3.61 us
    ppermute x3, waiting for transfers between devices, from_view(): return lax.ppermute(mine, 'dp', [(i, i ^ 1) for i in range(n_dp)])  2.71 us
  transfers between devices with their start and end apart: 9, of which 2 were waited for; matrix products, arithmetic and copies ran while one was open for 0% of the time, Pallas kernels for 18%

profile of v4, /device:TPU:0, one launch (start us, length us, event | category | flops | bytes accessed | tf_op | source)
XLA Modules:
  0.0 66.5 jit_solution(16812877260526137326)
XLA Ops:
  0.6 0.1 pad_add_fusion.which.refs_0_
  0.7 0.9 %copy-done.1 = bf16[1,256,192]{1,2,0:T(8,128)(2,1)S(1)} copy-done((bf16[1,256,192]{1,2,0:T(8,128)(2,1)S(1)}, bf16[1,256,192]{1,2,0:T(8,128)(2,1)}, u32[]{:S(2)}) %copy-start.1) | copy-done | bytes 98328
  1.6 1.2 %pack_s.1 = bf16[4,192,128]{2,1,0:T(8,128)(2,1)} custom-call(s32[3]{0:T(128)S(1)} %pad_add_fusion.which.refs_0_, bf16[192,256]{1,0:T(8,128)(2,1)S(1)} %bitcast.10), custom_call_target="tpu_custom_call" | custom-call | flops 25165824 | bytes 196608 | tf_op jit(solution)/shard_map/pack_s/pallas_call | solution.py:124
  2.9 6.3 %all-to-all-start = ((bf16[4,192,128]{2,1,0:T(8,128)(2,1)}), bf16[4,192,128]{2,1,0:T(8,128)(2,1)S(1)}, u32[]{:S(2)}, u32[]{:S(2)}) async-start(bf16[4,192,128]{2,1,0:T(8,128)(2,1)} %pack_s.1), calls=%async_computation | async-start | bytes 393216 | tf_op jit(solution)/shard_map/all_to_all | solution.py:319
  9.2 1.5 %collective-permute-start.3 = (s32[1,256]{1,0:T(1,128)}, s32[1,256]{1,0:T(1,128)S(1)}, u32[]{:S(2)}, u32[]{:S(2)}) collective-permute-start(s32[1,256]{1,0:T(1,128)} %param.10), channel_id=1, source_target_pairs={{0,1},{1,0},{2,3},{3,2},{4,5},{5,4},{6,7},{7,6},{8,9},{9,8},{10,11... | collective-permute-start | bytes 3080 | tf_op jit(solution)/shard_map/ppermute | solution.py:325
  10.7 0.8 %copy-done.3 = f32[16384]{0:T(1024)S(1)} copy-done((f32[16384]{0:T(1024)S(1)}, f32[16384]{0:T(1024)}, u32[]{:S(2)}) %copy-start.3) | copy-done | bytes 65560
  11.5 6.0 %prep.1 = (f32[192,4096]{1,0:T(8,128)}, bf16[2048,256]{1,0:T(8,128)(2,1)S(1)}, bf16[2048,256]{1,0:T(8,128)(2,1)S(1)}, f32[1,128]{1,0:T(1,128)S(1)}) custom-call(s32[3]{0:T(128)S(1)} %pad_add_fusion.which.refs_0_, f32[192,4096]{1,0:T(8,128)} %teacher_ref.1, f32[192,4096]{1,0:T(8,128)} %weight_ref.1, f32[1,16384]{1,0:T(1,128)S(1)} %bitcast.12), custom_call_target="tpu_custom_call" | custom-call | flops 15728640 | bytes 9437184 | tf_op jit(solution)/shard_map/prep/pallas_call | solution.py:76
  17.5 0.0 all-to-all-done.refs_0_
  17.5 0.6 collective-permute-start
  18.2 1.4 %pack_t.1 = bf16[4,192,128]{2,1,0:T(8,128)(2,1)} custom-call(s32[3]{0:T(128)S(1)} %pad_add_fusion.which.refs_0_, bf16[192,256]{1,0:T(8,128)(2,1)S(1)} %bitcast.11, s32[1,256]{1,0:T(1,128)S(1)} %collective-permute-done.3.rest_0_, f32[1,128]{1,0:T(1,128)S(1)} %get-tuple-element.20.rest_1_.refs_3_.refs_7_.peak_ref), custom_call_target="tpu_custom_call" | custom-call | flops 25165824 | bytes 196608 | tf_op jit(solution)/shard_map/pack_t/pallas_call | solution.py:124
  19.6 5.0 %all-to-all-start.1 = ((bf16[4,192,128]{2,1,0:T(8,128)(2,1)}), bf16[4,192,128]{2,1,0:T(8,128)(2,1)S(1)}, u32[]{:S(2)}, u32[]{:S(2)}) async-start(bf16[4,192,128]{2,1,0:T(8,128)(2,1)} %pack_t.1), calls=%async_computation.1 | async-start | bytes 393216 | tf_op jit(solution)/shard_map/all_to_all | solution.py:319
  24.6 0.5 collective-permute-start.2
  25.1 5.7 %all-to-all-done.1.refs_1_ = bf16[4,192,128]{2,1,0:T(8,128)(2,1)S(1)} async-done(((bf16[4,192,128]{2,1,0:T(8,128)(2,1)}), bf16[4,192,128]{2,1,0:T(8,128)(2,1)S(1)}, u32[]{:S(2)}, u32[]{:S(2)}) %all-to-all-start.1) | async-done | bytes 196640 | tf_op jit(solution)/shard_map/all_to_all | solution.py:319
  30.8 1.5 %collective-permute-start.4 = (bf16[4,192,128]{2,1,0:T(8,128)(2,1)S(1)}, bf16[4,192,128]{2,1,0:T(8,128)(2,1)S(1)}, u32[]{:S(2)}, u32[]{:S(2)}) collective-permute-start(bf16[4,192,128]{2,1,0:T(8,128)(2,1)S(1)} %all-to-all-done.1.refs_1_), channel_id=1, source_target_pairs={{0,1},{1,0},{2,3},{3,2},{4,5},{5,4},{6,7},{7,6},{8,9},{9,8},{10,11... | collective-permute-start | bytes 589832 | tf_op jit(solution)/shard_map/ppermute | solution.py:325
  32.3 0.0 collective-permute-done.2.refs_1_
  32.3 1.5 %scores_s.3 = (bf16[2048,1024]{1,0:T(8,128)(2,1)S(1)}, f32[1,1024]{1,0:T(1,128)S(1)}, bf16[192,1024]{1,0:T(8,128)(2,1)S(1)}) custom-call(bf16[4,192,128]{2,1,0:T(8,128)(2,1)S(1)} %collective-permute-done.1.refs_0_, bf16[4,192,128]{2,1,0:T(8,128)(2,1)S(1)} %collective-permute-done.2.refs_1_, bf16[2048,256]{1,0:T(8,128)(2,1)S(1)} %get-tuple-element.17.refs_2_), custom_call_target="tpu_custom_call" | custom-call | flops 1073741824 | bytes 4194304 | tf_op jit(solution)/shard_map/scores_s/pallas_call | solution.py:229
  33.8 2.7 %collective-permute-done.4.feats_ref = bf16[4,192,128]{2,1,0:T(8,128)(2,1)S(1)} collective-permute-done((bf16[4,192,128]{2,1,0:T(8,128)(2,1)S(1)}, bf16[4,192,128]{2,1,0:T(8,128)(2,1)S(1)}, u32[]{:S(2)}, u32[]{:S(2)}) %collective-permute-start.4) | collective-permute-done | bytes 196640 | tf_op jit(solution)/shard_map/ppermute | solution.py:325
  36.5 1.5 %scores_s.2 = (bf16[2048,1024]{1,0:T(8,128)(2,1)S(1)}, f32[1,1024]{1,0:T(1,128)S(1)}, bf16[192,1024]{1,0:T(8,128)(2,1)S(1)}) custom-call(bf16[4,192,128]{2,1,0:T(8,128)(2,1)S(1)} %all-to-all-done.refs_0_, bf16[4,192,128]{2,1,0:T(8,128)(2,1)S(1)} %collective-permute-done.refs_1_, bf16[2048,256]{1,0:T(8,128)(2,1)S(1)} %get-tuple-element.17.refs_2_), custom_call_target="tpu_custom_call" | custom-call | flops 1073741824 | bytes 4194304 | tf_op jit(solution)/shard_map/scores_s/pallas_call | solution.py:229
  38.0 0.0 copy-start
  38.0 1.4 %scores_t.2 = (bf16[2048,1024]{1,0:T(8,128)(2,1)S(1)}, f32[1,1024]{1,0:T(1,128)S(1)}) custom-call(bf16[4,192,128]{2,1,0:T(8,128)(2,1)S(1)} %gate.1.refs_0_, bf16[4,192,128]{2,1,0:T(8,128)(2,1)S(1)} %all-to-all-done.1.refs_1_, bf16[2048,256]{1,0:T(8,128)(2,1)S(1)} %get-tuple-element.21.refs_2_.refs_6_, ...), custom_call_target="tpu_custom_call" | custom-call | flops 1073741824 | bytes 4194304 | tf_op jit(solution)/shard_map/scores_t/pallas_call | solution.py:229
  39.5 2.0 %scores_t.3 = (bf16[2048,1024]{1,0:T(8,128)(2,1)S(1)}, f32[4,4,1024]{2,1,0:T(4,128)S(1)}) custom-call(s32[3]{0:T(128)S(1)} %pad_add_fusion.which.refs_0_, f32[1,1024]{1,0:T(1,128)S(1)} %get-tuple-element.18.refs_1_, f32[1,1024]{1,0:T(1,128)S(1)} %get-tuple-element.19.after_ref.refs_2_, f32[1,1024]{1,0:T(1,128)S(1)} %get-tuple-element.22.refs_3_, ...), custom_call_target="tpu_custom_call" | custom-call | flops 1073741824 | bytes 4194304 | tf_op jit(solution)/shard_map/scores_t/pallas_call | solution.py:229
  41.5 6.8 %all_to_all.20.in_ref = f32[4,4,1024]{2,1,0:T(4,128)S(1)} all-to-all(f32[4,4,1024]{2,1,0:T(4,128)S(1)} %get-tuple-element.23), channel_id=1, replica_groups=mesh['fsdp'=4,'proto'=4,'dp'=2] {'proto'}, dimensions={0} | all-to-all | bytes 131072 | tf_op jit(solution)/shard_map/all_to_all | solution.py:319
  48.3 11.5 %all_to_all.21.totals_ref = f32[8,4,1024]{2,1,0:T(4,128)S(1)} all-to-all(f32[8,4,1024]{2,1,0:T(4,128)S(1)} %relay.1), channel_id=1, replica_groups=mesh['fsdp'=4,'proto'=4,'dp'=2] {'dp','fsdp'}, dimensions={0} | all-to-all | bytes 262144 | tf_op jit(solution)/shard_map/all_to_all | solution.py:319
  59.8 6.7 %gradient.1 = f32[192,2048]{1,0:T(8,128)} custom-call(s32[3]{0:T(128)S(1)} %pad_add_fusion.which.refs_0_, f32[8,4,1024]{2,1,0:T(4,128)S(1)} %all_to_all.21.totals_ref, f32[1,128]{1,0:T(1,128)S(1)} %get-tuple-element.20.rest_1_.refs_3_.refs_7_.peak_ref, bf16[192,1024]{1,0:T(8,128)(2,1)S(1)} %get-tuple-element.24.unit_a, ...), custom_call_target="tpu_custom_call" | custom-call | flops 4294967296 | bytes 3145728 | tf_op jit(solution)/shard_map/gradient/pallas_call | solution.py:295
  (15 shorter events, 0.1 us)
Async XLA Ops:
  0.7 0.9 %copy-start.1 = (bf16[1,256,192]{1,2,0:T(8,128)(2,1)S(1)}, bf16[1,256,192]{1,2,0:T(8,128)(2,1)}, u32[]{:S(2)}) copy-start(bf16[1,256,192]{1,2,0:T(8,128)(2,1)} %param.9) | copy-start | bytes 294916
  1.6 16.6 %copy-start.2 = (bf16[1,256,192]{1,2,0:T(8,128)(2,1)S(1)}, bf16[1,256,192]{1,2,0:T(8,128)(2,1)}, u32[]{:S(2)}) copy-start(bf16[1,256,192]{1,2,0:T(8,128)(2,1)} %param.8) | copy-start | bytes 294916
  2.9 14.7 %all-to-all-start = ((bf16[4,192,128]{2,1,0:T(8,128)(2,1)}), bf16[4,192,128]{2,1,0:T(8,128)(2,1)S(1)}, u32[]{:S(2)}, u32[]{:S(2)}) async-start(bf16[4,192,128]{2,1,0:T(8,128)(2,1)} %pack_s.1), calls=%async_computation | async-start | bytes 393216 | tf_op jit(solution)/shard_map/all_to_all | solution.py:319
  9.2 9.0 %collective-permute-start.3 = (s32[1,256]{1,0:T(1,128)}, s32[1,256]{1,0:T(1,128)S(1)}, u32[]{:S(2)}, u32[]{:S(2)}) collective-permute-start(s32[1,256]{1,0:T(1,128)} %param.10), channel_id=1, source_target_pairs={{0,1},{1,0},{2,3},{3,2},{4,5},{5,4},{6,7},{7,6},{8,9},{9,8},{10,11... | collective-permute-start | bytes 3080 | tf_op jit(solution)/shard_map/ppermute | solution.py:325
  10.7 0.8 %copy-start.3 = (f32[16384]{0:T(1024)S(1)}, f32[16384]{0:T(1024)}, u32[]{:S(2)}) copy-start(f32[16384]{0:T(1024)} %param.11) | copy-start | bytes 196612
  17.5 7.0 %collective-permute-start = (bf16[4,192,128]{2,1,0:T(8,128)(2,1)S(1)}, bf16[4,192,128]{2,1,0:T(8,128)(2,1)S(1)}, u32[]{:S(2)}, u32[]{:S(2)}) collective-permute-start(bf16[4,192,128]{2,1,0:T(8,128)(2,1)S(1)} %all-to-all-done.refs_0_), channel_id=1, source_target_pairs={{0,1},{1,0},{2,3},{3,2},{4,5},{5,4},{6,7},{7,6},{8,9},{9,8},{10,11... | collective-permute-start | bytes 589832 | tf_op jit(solution)/shard_map/ppermute | solution.py:325
  19.6 11.2 %all-to-all-start.1 = ((bf16[4,192,128]{2,1,0:T(8,128)(2,1)}), bf16[4,192,128]{2,1,0:T(8,128)(2,1)S(1)}, u32[]{:S(2)}, u32[]{:S(2)}) async-start(bf16[4,192,128]{2,1,0:T(8,128)(2,1)} %pack_t.1), calls=%async_computation.1 | async-start | bytes 393216 | tf_op jit(solution)/shard_map/all_to_all | solution.py:319
  24.6 7.7 %collective-permute-start.1 = (bf16[4,192,128]{2,1,0:T(8,128)(2,1)S(1)}, bf16[4,192,128]{2,1,0:T(8,128)(2,1)S(1)}, u32[]{:S(2)}, u32[]{:S(2)}) collective-permute-start(bf16[4,192,128]{2,1,0:T(8,128)(2,1)S(1)} %all-to-all-done.refs_0_), channel_id=1, source_target_pairs={{0,2},{2,0},{4,6},{6,4},{1,3},{3,1},{5,7},{7,5},{8,10},{10,8},{12,... | collective-permute-start | bytes 589832 | tf_op jit(solution)/shard_map/ppermute | solution.py:322
  24.6 7.7 %collective-permute-start.2 = (bf16[4,192,128]{2,1,0:T(8,128)(2,1)S(1)}, bf16[4,192,128]{2,1,0:T(8,128)(2,1)S(1)}, u32[]{:S(2)}, u32[]{:S(2)}) collective-permute-start(bf16[4,192,128]{2,1,0:T(8,128)(2,1)S(1)} %collective-permute-done.refs_1_), channel_id=1, source_target_pairs={{0,2},{2,0},{4,6},{6,4},{1,3},{3,1},{5,7},{7,5},{8,10},{10,8},{12,... | collective-permute-start | bytes 589832 | tf_op jit(solution)/shard_map/ppermute | solution.py:322
  30.8 5.7 %collective-permute-start.4 = (bf16[4,192,128]{2,1,0:T(8,128)(2,1)S(1)}, bf16[4,192,128]{2,1,0:T(8,128)(2,1)S(1)}, u32[]{:S(2)}, u32[]{:S(2)}) collective-permute-start(bf16[4,192,128]{2,1,0:T(8,128)(2,1)S(1)} %all-to-all-done.1.refs_1_), channel_id=1, source_target_pairs={{0,1},{1,0},{2,3},{3,2},{4,5},{5,4},{6,7},{7,6},{8,9},{9,8},{10,11... | collective-permute-start | bytes 589832 | tf_op jit(solution)/shard_map/ppermute | solution.py:325
  32.3 7.1 %collective-permute-start.6 = (bf16[4,192,128]{2,1,0:T(8,128)(2,1)S(1)}, bf16[4,192,128]{2,1,0:T(8,128)(2,1)S(1)}, u32[]{:S(2)}, u32[]{:S(2)}) collective-permute-start(bf16[4,192,128]{2,1,0:T(8,128)(2,1)S(1)} %all-to-all-done.1.refs_1_), channel_id=1, source_target_pairs={{0,2},{2,0},{4,6},{6,4},{1,3},{3,1},{5,7},{7,5},{8,10},{10,8},{12,... | collective-permute-start | bytes 589832 | tf_op jit(solution)/shard_map/ppermute | solution.py:322
  36.5 2.9 %collective-permute-start.5 = (bf16[4,192,128]{2,1,0:T(8,128)(2,1)S(1)}, bf16[4,192,128]{2,1,0:T(8,128)(2,1)S(1)}, u32[]{:S(2)}, u32[]{:S(2)}) collective-permute-start(bf16[4,192,128]{2,1,0:T(8,128)(2,1)S(1)} %gate.1.refs_0_), channel_id=1, source_target_pairs={{0,2},{2,0},{4,6},{6,4},{1,3},{3,1},{5,7},{7,5},{8,10},{10,8},{12,... | collective-permute-start | bytes 589832 | tf_op jit(solution)/shard_map/ppermute | solution.py:322
  38.0 21.8 %copy-start = (f32[192,4096]{1,0:T(8,128)S(1)}, f32[192,4096]{1,0:T(8,128)}, u32[]{:S(2)}) copy-start(f32[192,4096]{1,0:T(8,128)} %weight_ref.1) | copy-start | bytes 9437188

commit v5 on v0

v5 whole, which is shorter than its diff:
```python
import functools
import math

import jax
import jax.numpy as jnp
from jax import lax
from jax.experimental import pallas as pl
from jax.experimental.pallas import tpu as pltpu
from jax.sharding import PartitionSpec as P

EPS = 1e-06
DEPTH = 256
GROUP = 512
STEP = 256
DIRECT = 8
LOG2E = math.log2(math.e)
GAIN_T = LOG2E / 0.04
GAIN_S = LOG2E / 0.1
LIMIT = 24 * 1024 * 1024
ON_CHIP = pl.BlockSpec(memory_space=pltpu.VMEM)
IN_HBM = pl.BlockSpec(memory_space=pl.ANY)


def shape(*dims, dtype=jnp.float32):
    return jax.ShapeDtypeStruct(dims, dtype)


def held(*dims, dtype=jnp.float32):
    return pltpu.VMEM(dims, dtype)


def call(kernel, name, out_shape, args, cost=(0, 0, 0), **more):
    many = isinstance(out_shape, (list, tuple))
    specs = dict(in_specs=[ON_CHIP] * len(args), out_specs=[ON_CHIP] * len(out_shape) if many else ON_CHIP)
    flops, moved, exps = map(int, cost)
    return pl.pallas_call(
        kernel,
        out_shape=out_shape,
        compiler_params=pltpu.CompilerParams(vmem_limit_bytes=LIMIT),
        cost_estimate=pl.CostEstimate(flops=flops, bytes_accessed=moved, transcendentals=exps),
        name=name,
        **{**specs, **more},
    )(*args)


def here():
    return lax.axis_index("dp"), lax.axis_index("fsdp"), lax.rem(lax.axis_index("proto"), 2)


def cast_split(row):
    high = row.astype(jnp.bfloat16).astype(jnp.float32)
    mid = (row - high).astype(jnp.bfloat16).astype(jnp.float32)
    return high, mid, row - high - mid


def prep_kernel(n_dp, teacher_hbm, student_hbm, center_ref, new_hbm, wt_ref, ws_ref, unit_ref, scale_ref, peak_ref, *scratch):
    teacher_buf, student_buf, new_buf, in_t, in_s, out = scratch
    chunks, bot, width = new_buf.shape
    own = chunks // n_dp
    dp, fsdp, _ = here()
    at = [slice(i * width, (i + 1) * width) for i in range(chunks)]
    loads = [
        (
            pltpu.make_async_copy(teacher_hbm.at[:, at[i]], teacher_buf.at[i], in_t.at[i]),
            pltpu.make_async_copy(student_hbm.at[:, at[i]], student_buf.at[i], in_s.at[i]),
        )
        for i in range(chunks)
    ]
    stores = [pltpu.make_async_copy(new_buf.at[i], new_hbm.at[:, at[i]], out.at[i]) for i in range(chunks)]
    for pair in loads:
        for load in pair:
            load.start()
    start = pl.multiple_of((fsdp * n_dp + dp) * (own * width), 128)
    center = center_ref[:, pl.ds(start, own * width)]
    peak = jnp.max(-center, axis=1, keepdims=True)
    peak_ref[...] = jnp.broadcast_to(peak, peak_ref.shape)
    splits = cast_split(-center - peak)
    for i in range(chunks):
        for load in loads[i]:
            load.wait()
        student = student_buf[i]
        new = 0.994 * teacher_buf[i] + 0.006 * student
        new_buf[i] = new
        stores[i].start()

        @pl.when(dp == i // own)
        def _():
            to = at[i % own]
            high, mid, low = [part[:, to] for part in splits]
            row = lax.broadcasted_iota(jnp.int32, (DEPTH - bot, width), 0)
            zero = jnp.zeros((DEPTH - bot, width), jnp.float32)
            extra = jnp.where(row == 0, high, jnp.where(row == 1, mid, jnp.where(row == 2, low, zero)))
            scale = lax.rsqrt(jnp.sum(student * student, axis=0, keepdims=True) + EPS)
            unit_s = student * scale
            unit_t = new * lax.rsqrt(jnp.sum(new * new, axis=0, keepdims=True) + EPS)
            wt_ref[to, :] = jnp.concatenate([unit_t, extra], axis=0).astype(jnp.bfloat16).T
            ws_ref[to, :] = jnp.concatenate([unit_s, zero], axis=0).astype(jnp.bfloat16).T
            unit_ref[:, to] = unit_s
            scale_ref[:, to] = scale

    for store in stores:
        store.wait()


def prepare(teacher_weight, student_weight, center, n_dp):
    bot, cols = teacher_weight.shape
    own = cols // n_dp
    width = min(512, own)
    chunks = cols // width
    teacher_weight = pltpu.with_memory_space_constraint(teacher_weight, pltpu.HBM)
    student_weight = pltpu.with_memory_space_constraint(student_weight, pltpu.HBM)
    return call(
        functools.partial(prep_kernel, n_dp),
        "prep",
        [
            pltpu.HBM((bot, cols), jnp.float32),
            held(own, DEPTH, dtype=jnp.bfloat16),
            held(own, DEPTH, dtype=jnp.bfloat16),
            held(bot, own),
            held(1, own),
            held(1, 128),
        ],
        (teacher_weight, student_weight, center),
        (20 * bot * cols, 12 * bot * cols, 0),
        in_specs=[IN_HBM, IN_HBM, ON_CHIP],
        out_specs=[IN_HBM] + [ON_CHIP] * 5,
        scratch_shapes=[held(chunks, bot, width)] * 3 + [pltpu.SemaphoreType.DMA((chunks,))] * 3,
    )


def pack_kernel(student_ref, teacher_ref, index_ref, out_ref):
    half = out_ref.shape[2]
    lower = here()[2] == 0
    out_ref[0] = jnp.where(lower, student_ref[:, :half], student_ref[:, half:])
    index = jnp.where(lower, index_ref[:, :half], index_ref[:, half:])
    row = lax.broadcasted_iota(jnp.int32, (teacher_ref.shape[1], half), 0)
    pick = jnp.where(row == index, 1.0, 0.0).astype(jnp.bfloat16)
    out_ref[1] = jnp.dot(teacher_ref[...], pick, preferred_element_type=jnp.float32).astype(jnp.bfloat16)


def pack(student, teacher, index):
    bot, crops = student.shape
    return call(pack_kernel, "pack", held(2, bot, crops // 2, dtype=jnp.bfloat16), (student, teacher, index))


def join_kernel(n_in, n_after, *refs):
    blocks = []
    for ref in refs[:n_in]:
        blocks += [ref] if len(ref.shape) == 3 else [ref.at[i] for i in range(ref.shape[0])]
    for ref in refs[n_in + n_after:]:
        skip = len(blocks) - ref.shape[0]
        for i in range(ref.shape[0]):
            ref[i] = blocks[skip + i][...]


def join(parts, counts, after):
    block = parts[0].shape[-3:]
    outs = [held(count, *block, dtype=jnp.bfloat16) for count in counts]
    kernel = functools.partial(join_kernel, len(parts), len(after))
    return call(kernel, "join", outs, (*parts, *after), in_specs=[ON_CHIP] * len(parts) + [IN_HBM] * len(after))


def log_sum(parts):
    top = functools.reduce(jnp.maximum, parts)
    return top + jnp.log2(sum(jnp.exp2(part - top) for part in parts))


def combine(parts):
    half = parts[0].shape[0] // 2
    return sum(part[:half] for part in parts), log_sum([part[half:] for part in parts])


def slot(k, n):
    return lax.axis_index("fsdp") ^ k if n <= DIRECT else k


def score_kernel(last, *refs):
    before, refs = (refs[:3], refs[3:]) if last else ((), refs)
    feats_ref, ws_ref, wt_ref, peak_ref, exps_ref, expt_ref, unit_ref, total_ref, *mine = refs
    own_ref = mine[0] if last else total_ref
    n, _, bot, width = feats_ref.shape
    cols = ws_ref.shape[0]
    step = min(STEP, cols)
    per = max(1, min(n, GROUP // width))
    row = lax.broadcasted_iota(jnp.int32, (DEPTH - bot, per * width), 0)
    for which, w_ref, exp_ref, gain in ((0, ws_ref, exps_ref, GAIN_S), (1, wt_ref, expt_ref, GAIN_T)):
        extra = jnp.where(row < 3 * which, 1.0, 0.0).astype(jnp.bfloat16)
        for group in range(n // per):
            values = [feats_ref[group * per + k, which].astype(jnp.float32) for k in range(per)]
            values = jnp.concatenate(values, axis=1)
            unit = (values * lax.rsqrt(jnp.sum(values * values, axis=0, keepdims=True) + EPS)).astype(jnp.bfloat16)
            lanes = slice(group * per * width, (group + 1) * per * width)
            if which == 0:
                unit_ref[:, lanes] = unit
            stationary = jnp.concatenate([unit, extra], axis=0)
            total = jnp.zeros((8, per * width), jnp.float32)
            for at in range(0, cols, step):
                score = jnp.dot(w_ref[at:at + step, :], stationary, preferred_element_type=jnp.float32)
                exps = jnp.exp2(score * gain)
                total = total + jnp.sum(exps.reshape(step // 8, 8, per * width), axis=0)
                exp_ref[at:at + step, lanes] = exps.astype(jnp.bfloat16)
            total = jnp.sum(total, axis=0, keepdims=True)
            if which == 1:
                total = jnp.log2(total) + GAIN_T * peak_ref[:, :1]
            own_ref[which:which + 1, lanes] = total
    if not last:
        return
    dp, _, core = here()
    own, pair, other = before
    parts = ((own, other), (pair, own_ref))
    rows = []
    for which in (0, 1):
        for half in (0, 1):
            pieces = []
            for view in (0, 1):
                first = (dp == view) if which == 0 else (dp != view)
                for place in range(n):
                    at = pl.ds(pl.multiple_of(slot(place, n) * width, width), width)
                    read = [[part[which:which + 1, at] for part in side] for side in parts]
                    mine, theirs = [jnp.where(first, *side) for side in read]
                    pieces.append(jnp.where(core == half, mine, theirs))
            rows.append(jnp.concatenate(pieces, axis=1))
    rows = jnp.concatenate(rows, axis=0)
    for i in range(total_ref.shape[0]):
        total_ref[i] = rows


def scores(feats, ws, wt, peak, last=None):
    n, _, bot, width = feats.shape
    cols, rows = ws.shape[0], n * width
    copies, before = last or (0, ())
    return call(
        functools.partial(score_kernel, last is not None),
        "scores",
        [
            held(cols, rows, dtype=jnp.bfloat16),
            held(cols, rows, dtype=jnp.bfloat16),
            held(bot, rows, dtype=jnp.bfloat16),
            held(copies, 4, 2 * rows) if last else held(2, rows),
        ],
        (*before, feats, ws, wt, peak),
        (4 * rows * cols * DEPTH, 4 * rows * cols, 2 * rows * cols),
        scratch_shapes=[held(2, rows)] if last else [],
    )


def relay_kernel(in_ref, out_ref):
    rows = jnp.concatenate(combine([in_ref[i] for i in range(in_ref.shape[0])]), axis=0)
    for i in range(out_ref.shape[0]):
        out_ref[i] = rows


def relay(parts, copies):
    return call(relay_kernel, "relay", held(copies, *parts.shape[1:]), (parts,))


def grad_kernel(here_ref, there_ref, peak_ref, weight_unit, weight_scale, *refs):
    units, exps, expt, out_ref, scales = refs[:4], refs[4:8], refs[8:12], refs[12], refs[13]
    dp, _, core = here()
    total_s, log_t = combine([here_ref[0], there_ref[0]])
    scales[0:2, :] = 10.0 / total_s
    scales[2:4, :] = -10.0 * jnp.exp2(GAIN_T * peak_ref[:, :1] - log_t)
    bot, rows = units[0].shape
    width = 128
    n = rows // width
    sides = []
    for part in range(4):
        view, half = divmod(part, 2)
        base = (dp ^ view) * rows
        at = [pl.ds(pl.multiple_of(base + slot(k, n) * width, width), width) for k in range(n)]
        unit = units[part][...].astype(jnp.float32)
        for which, exp_ref in ((0, exps[part]), (1, expt[part ^ 2])):
            picked = [
                jnp.where(core == half, scales[2 * which:2 * which + 1, where], scales[2 * which + 1:2 * which + 2, where])
                for where in at
            ]
            sides.append(((unit * jnp.concatenate(picked, axis=1)).astype(jnp.bfloat16), exp_ref))
    cols = out_ref.shape[1]
    step = min(512, cols)
    for at in range(0, cols, step):
        grad = sum(
            lax.dot_general(
                exp_ref[at:at + step, :], feats, (((1,), (1,)), ((), ())), preferred_element_type=jnp.float32
            )
            for feats, exp_ref in sides
        )
        grad = grad.T
        unit = weight_unit[:, at:at + step]
        proj = unit * jnp.sum(unit * grad, axis=0, keepdims=True)
        out_ref[:, at:at + step] = (grad - proj) * weight_scale[:, at:at + step]


def gradient(here_total, there_total, peak, weight_unit, weight_scale, units, exps, expt):
    cols, rows = exps[0].shape
    bot = units[0].shape[0]
    return call(
        grad_kernel,
        "gradient",
        shape(bot, cols),
        (here_total, there_total, peak, weight_unit, weight_scale, *units, *exps, *expt),
        (16 * rows * cols * DEPTH, 8 * bot * cols, 0),
        scratch_shapes=[held(4, 2 * rows)],
    )


def shards(teacher_weight, student_weight, teacher_feats, student_feats, pairing, center):
    n_dp, n_fsdp, n_proto = [lax.axis_size(axis) for axis in ("dp", "fsdp", "proto")]

    def spread(copies, axis):
        return lax.all_to_all(copies, axis, 0, 0, tiled=True)

    def swap(block, axis, apart=1):
        return lax.ppermute(block, axis, [(i, i ^ apart) for i in range(lax.axis_size(axis))])

    teacher_new, wt, ws, unit, scale, peak = prepare(teacher_weight, student_weight, center[None, :], n_dp)
    weights = (ws, wt, peak)
    mine = pack(student_feats[0].T, teacher_feats[0].T, swap(pairing, "dp"))
    if n_fsdp <= DIRECT:
        along = [swap(mine, "fsdp", k) for k in range(1, n_fsdp)]
        other = swap(mine, "dp")
        own, rest = join([mine, *along], [n_fsdp, n_fsdp - 1], (other, peak))
        parts = [scores(own, *weights), scores(swap(own, "proto"), *weights)]
        (other,) = join([other, swap(rest, "dp")], [n_fsdp], [part[3] for part in parts])
    else:
        own = spread(jnp.broadcast_to(mine[None], (n_fsdp, *mine.shape)), "fsdp")
        other = swap(own, "dp")
        parts = [scores(own, *weights), scores(swap(own, "proto"), *weights)]
    parts.append(scores(other, *weights))
    before = [part[3] for part in parts]
    parts.append(scores(swap(other, "proto"), *weights, last=(n_proto, before)))
    exps, expt, units, totals = zip(*parts)
    total = relay(spread(relay(spread(totals[3], "proto"), n_fsdp), "fsdp"), 1)
    student_grad = gradient(total, swap(total, "dp"), peak, unit, scale, units, exps, expt)
    return (teacher_new, student_grad)


def solution(mesh):
    placed = (
        P(None, ("proto", "fsdp")),
        P(None, ("proto", "fsdp")),
        P("dp", "fsdp", None),
        P("dp", "fsdp", None),
        P("dp", "fsdp"),
        P("proto"),
    )
    return jax.shard_map(
        shards,
        mesh=mesh,
        in_specs=placed,
        out_specs=(P(None, ("proto", "fsdp")), P(None, ("proto", "fsdp", "dp"))),
        check_vma=False,
    )
```

time: 516 us -> 59.4 us (0.12)
  waiting for transfers between devices: 418 us -> 11.8 us
  matrix products: 39.8 us -> 0 us
  other arithmetic: 25.6 us -> 0 us
  Pallas kernels: 0 us -> 16.6 us
  between operations: 13.9 us -> 0.73 us
  starting transfers between devices: 3.13 us -> 11.1 us
    all_gather x2 -> x0, waiting for transfers between devices: 211 us -> none  [the longest x1 108 us: shards(): lax.all_gather(w_student, 'fsdp', axis=1, tiled=True)]
    reduce_scatter x1 -> x0, waiting for transfers between devices: 203 us -> none  [shards(): lax.psum_scatter(lax.dot_general(derivs, z_student, (((0,), (0,)), ((), (...]
    dot_general x3 -> x0, matrix products: 39.8 us -> none  [the longest x1 17.4 us: shards(): lax.dot_general(derivs, z_student, (((0,), (0,)), ((), ())), preferred_el...]
    reduce_sum x7 -> x0, other arithmetic: 20.9 us -> none  [the longest x1 12.1 us: shards(): jnp.sum(exp_s, axis=1)]
    pallas_call x0 -> x11, Pallas kernels: none -> 16.6 us  [call(): pl.pallas_call(kernel, out_shape=out_shape, compiler_params=pltpu.Compile...]
    all_to_all x0 -> x2, blocking collectives: none -> 16.3 us  [spread(): return lax.all_to_all(copies, axis, 0, 0, tiled=True)]
    ppermute x1 -> x9, waiting for transfers between devices: 3.39 us -> 11.8 us  [swap(): lax.ppermute(block, axis, [(i, i ^ apart) for i in range(lax.axis_size(ax...]
    ppermute x1 -> x9, starting transfers between devices: 3 us -> 11.1 us  [swap(): lax.ppermute(block, axis, [(i, i ^ apart) for i in range(lax.axis_size(ax...]
  transfers between devices with their start and end apart: 4 -> 9, of which waited for: 4 -> 5; matrix products, arithmetic and copies ran while one was open for 3% -> 0% of each run, Pallas kernels for 0% -> 15%
where the time goes in v5:
time: 59.4 us; the launch traced here: 59.1 us
  Pallas kernels  16.6 us (28%)
  blocking collectives  16.3 us (27%)
  waiting for transfers between devices  11.8 us (20%)
  starting transfers between devices  11.1 us (19%)
  local copies, waits for them, and re-layouts  2.62 us (4%)
  between operations  0.73 us (1%)
    pallas_call x11, Pallas kernels, call(): pl.pallas_call(kernel, out_shape=out_shape, compiler_params=pltpu.Compile...  16.6 us
    all_to_all x2, blocking collectives, spread(): return lax.all_to_all(copies, axis, 0, 0, tiled=True)  16.3 us
    ppermute x9, waiting for transfers between devices, swap(): lax.ppermute(block, axis, [(i, i ^ apart) for i in range(lax.axis_size(ax...  11.8 us
    ppermute x9, starting transfers between devices, swap(): lax.ppermute(block, axis, [(i, i ^ apart) for i in range(lax.axis_size(ax...  11.1 us
    unnamed x6, local copies, waits for them, and re-layouts  2.62 us
  transfers between devices with their start and end apart: 9, of which 5 were waited for; matrix products, arithmetic and copies ran while one was open for 0% of the time, Pallas kernels for 15%

profile of v5, /device:TPU:0, one launch (start us, length us, event | category | flops | bytes accessed | tf_op | source)
XLA Modules:
  0.0 59.1 jit_solution(7987848387180511879)
XLA Ops:
  0.6 3.0 %collective-permute-start = (s32[1,256]{1,0:T(1,128)}, s32[1,256]{1,0:T(1,128)S(1)}, u32[]{:S(2)}, u32[]{:S(2)}) collective-permute-start(s32[1,256]{1,0:T(1,128)} %param.10), channel_id=1, source_target_pairs={{0,1},{1,0},{2,3},{3,2},{4,5},{5,4},{6,7},{7,6},{8,9},{9,8},{10,11... | collective-permute-start | bytes 3080 | tf_op jit(solution)/shard_map/ppermute | solution.py:313
  3.6 1.8 %collective-permute-done.index_ref = s32[1,256]{1,0:T(1,128)S(1)} collective-permute-done((s32[1,256]{1,0:T(1,128)}, s32[1,256]{1,0:T(1,128)S(1)}, u32[]{:S(2)}, u32[]{:S(2)}) %collective-permute-start) | collective-permute-done | bytes 1056 | tf_op jit(solution)/shard_map/ppermute | solution.py:313
  5.4 0.9 %copy-done = bf16[1,256,192]{1,2,0:T(8,128)(2,1)S(1)} copy-done((bf16[1,256,192]{1,2,0:T(8,128)(2,1)S(1)}, bf16[1,256,192]{1,2,0:T(8,128)(2,1)}, u32[]{:S(2)}) %copy-start) | copy-done | bytes 98328
  6.3 0.9 %copy-done.1 = bf16[1,256,192]{1,2,0:T(8,128)(2,1)S(1)} copy-done((bf16[1,256,192]{1,2,0:T(8,128)(2,1)S(1)}, bf16[1,256,192]{1,2,0:T(8,128)(2,1)}, u32[]{:S(2)}) %copy-start.1) | copy-done | bytes 98328
  7.2 0.2 pack.1.refs_0_
  7.3 2.1 %collective-permute-start.4 = (bf16[2,192,128]{2,1,0:T(8,128)(2,1)S(1)}, bf16[2,192,128]{2,1,0:T(8,128)(2,1)S(1)}, u32[]{:S(2)}, u32[]{:S(2)}) collective-permute-start(bf16[2,192,128]{2,1,0:T(8,128)(2,1)S(1)} %pack.1.refs_0_), channel_id=1, source_target_pairs={{0,1},{1,0},{2,3},{3,2},{4,5},{5,4},{6,7},{7,6},{8,9},{9,8},{10,11... | collective-permute-start | bytes 294920 | tf_op jit(solution)/shard_map/ppermute | solution.py:313
  9.4 3.6 %collective-permute-start.3 = (bf16[2,192,128]{2,1,0:T(8,128)(2,1)S(1)}, bf16[2,192,128]{2,1,0:T(8,128)(2,1)S(1)}, u32[]{:S(2)}, u32[]{:S(2)}) collective-permute-start(bf16[2,192,128]{2,1,0:T(8,128)(2,1)S(1)} %pack.1.refs_0_), channel_id=1, source_target_pairs={{0,24},{8,16},{16,8},{24,0},{1,25},{9,17},{17,9},{25,1},{2,26},{10... | collective-permute-start | bytes 294920 | tf_op jit(solution)/shard_map/ppermute | solution.py:313
  13.0 0.8 %collective-permute-start.1 = (bf16[2,192,128]{2,1,0:T(8,128)(2,1)S(1)}, bf16[2,192,128]{2,1,0:T(8,128)(2,1)S(1)}, u32[]{:S(2)}, u32[]{:S(2)}) collective-permute-start(bf16[2,192,128]{2,1,0:T(8,128)(2,1)S(1)} %pack.1.refs_0_), channel_id=1, source_target_pairs={{0,8},{8,0},{16,24},{24,16},{1,9},{9,1},{17,25},{25,17},{2,10},{10... | collective-permute-start | bytes 294920 | tf_op jit(solution)/shard_map/ppermute | solution.py:313
  13.8 0.8 %copy-done.2 = f32[16384]{0:T(1024)S(1)} copy-done((f32[16384]{0:T(1024)S(1)}, f32[16384]{0:T(1024)}, u32[]{:S(2)}) %copy-start.2) | copy-done | bytes 65560
  14.7 4.4 %prep.1 = (f32[192,4096]{1,0:T(8,128)}, bf16[2048,256]{1,0:T(8,128)(2,1)S(1)}, bf16[2048,256]{1,0:T(8,128)(2,1)S(1)}, f32[192,2048]{1,0:T(8,128)S(1)}, f32[1,2048]{1,0:T(1,128)S(1)}, /*index=5*/f32[1,128]{1,0:T(1,128)S(1)}) custom-call(f32[192,4096]{1,0:T(8,128)} %teacher_hbm.1, f32[192,4096]{1,0:T(8,128)} %student_hbm.1, f32[1,16384]{1,0:T(1,128)S(1)} %bitcast.9), custom_call_target="tpu_custom_call" | custom-call | flops 15728640 | bytes 9437184 | tf_op jit(solution)/shard_map/prep/pallas_call | solution.py:36
  19.1 0.9 %collective-permute-done.2.refs_2_ = bf16[2,192,128]{2,1,0:T(8,128)(2,1)S(1)} collective-permute-done((bf16[2,192,128]{2,1,0:T(8,128)(2,1)S(1)}, bf16[2,192,128]{2,1,0:T(8,128)(2,1)S(1)}, u32[]{:S(2)}, u32[]{:S(2)}) %collective-permute-start.2) | collective-permute-done | bytes 98336 | tf_op jit(solution)/shard_map/ppermute | solution.py:313
  20.0 0.1 join.2
  20.1 0.6 %collective-permute-start.6 = (bf16[3,2,192,128]{3,2,1,0:T(8,128)(2,1)S(1)}, bf16[3,2,192,128]{3,2,1,0:T(8,128)(2,1)S(1)}, u32[]{:S(2)}, u32[]{:S(2)}) collective-permute-start(bf16[3,2,192,128]{3,2,1,0:T(8,128)(2,1)S(1)} %get-tuple-element.33), channel_id=1, source_target_pairs={{0,1},{1,0},{2,3},{3,2},{4,5},{5,4},{6,7},{7,6},{8,9},{9,8},{10,11... | collective-permute-start | bytes 884744 | tf_op jit(solution)/shard_map/ppermute | solution.py:313
  20.7 1.4 %scores.4 = (bf16[2048,512]{1,0:T(8,128)(2,1)S(1)}, bf16[2048,512]{1,0:T(8,128)(2,1)S(1)}, bf16[192,512]{1,0:T(8,128)(2,1)S(1)}, f32[2,512]{1,0:T(2,128)S(1)}) custom-call(bf16[4,2,192,128]{3,2,1,0:T(8,128)(2,1)S(1)} %get-tuple-element.28.refs_0_, bf16[2048,256]{1,0:T(8,128)(2,1)S(1)} %get-tuple-element.29.refs_1_.refs_4_, ...), custom_call_target="tpu_custom_call" | custom-call | flops 1073741824 | bytes 4194304 | tf_op jit(solution)/shard_map/scores/pallas_call | solution.py:36
  22.2 1.4 %scores.5 = (bf16[2048,512]{1,0:T(8,128)(2,1)S(1)}, bf16[2048,512]{1,0:T(8,128)(2,1)S(1)}, bf16[192,512]{1,0:T(8,128)(2,1)S(1)}, f32[2,512]{1,0:T(2,128)S(1)}) custom-call(bf16[4,2,192,128]{3,2,1,0:T(8,128)(2,1)S(1)} %collective-permute-done.5.refs_0_, bf16[2048,256]{1,0:T(8,128)(2,1)S(1)} %get-tuple-element.29.refs_1_.refs_4_, ...), custom_call_target="tpu_custom_call" | custom-call | flops 1073741824 | bytes 4194304 | tf_op jit(solution)/shard_map/scores/pallas_call | solution.py:36
  23.6 5.9 %collective-permute-done.6.refs_1_ = bf16[3,2,192,128]{3,2,1,0:T(8,128)(2,1)S(1)} collective-permute-done((bf16[3,2,192,128]{3,2,1,0:T(8,128)(2,1)S(1)}, bf16[3,2,192,128]{3,2,1,0:T(8,128)(2,1)S(1)}, u32[]{:S(2)}, u32[]{:S(2)}) %collective-permute-start.6) | collective-permute-done | bytes 294944 | tf_op jit(solution)/shard_map/ppermute | solution.py:313
  29.7 1.4 %scores.6 = (bf16[2048,512]{1,0:T(8,128)(2,1)S(1)}, bf16[2048,512]{1,0:T(8,128)(2,1)S(1)}, bf16[192,512]{1,0:T(8,128)(2,1)S(1)}, f32[2,512]{1,0:T(2,128)S(1)}) custom-call(bf16[4,2,192,128]{3,2,1,0:T(8,128)(2,1)S(1)} %join.3.refs_0_, bf16[2048,256]{1,0:T(8,128)(2,1)S(1)} %get-tuple-element.29.refs_1_.refs_4_, ...), custom_call_target="tpu_custom_call" | custom-call | flops 1073741824 | bytes 4194304 | tf_op jit(solution)/shard_map/scores/pallas_call | solution.py:36
  31.1 0.3 collective-permute-done.7.refs_3_
  31.4 1.5 %scores.7 = (bf16[2048,512]{1,0:T(8,128)(2,1)S(1)}, bf16[2048,512]{1,0:T(8,128)(2,1)S(1)}, bf16[192,512]{1,0:T(8,128)(2,1)S(1)}, f32[4,4,1024]{2,1,0:T(4,128)S(1)}) custom-call(f32[2,512]{1,0:T(2,128)S(1)} %get-tuple-element.31.refs_2_.refs_0_, f32[2,512]{1,0:T(2,128)S(1)} %get-tuple-element.32.refs_3_.refs_1_, f32[2,512]{1,0:T(2,128)S(1)} %get-tuple-element.34.refs_2_, ...), custom_call_target="tpu_custom_call" | custom-call | flops 1073741824 | bytes 4194304 | tf_op jit(solution)/shard_map/scores/pallas_call | solution.py:36
  32.9 6.7 %all_to_all.10.in_ref = f32[4,4,1024]{2,1,0:T(4,128)S(1)} all-to-all(f32[4,4,1024]{2,1,0:T(4,128)S(1)} %get-tuple-element.35), channel_id=1, replica_groups=mesh['fsdp'=4,'proto'=4,'dp'=2] {'proto'}, dimensions={0} | all-to-all | bytes 131072 | tf_op jit(solution)/shard_map/all_to_all | solution.py:310
  39.6 9.5 %all_to_all.11.in_ref = f32[4,4,1024]{2,1,0:T(4,128)S(1)} all-to-all(f32[4,4,1024]{2,1,0:T(4,128)S(1)} %relay.2), channel_id=1, replica_groups=mesh['fsdp'=4,'proto'=4,'dp'=2] {'fsdp'}, dimensions={0} | all-to-all | bytes 131072 | tf_op jit(solution)/shard_map/all_to_all | solution.py:310
  49.2 0.8 %collective-permute-start.8 = (f32[1,4,1024]{2,1,0:T(4,128)S(1)}, f32[1,4,1024]{2,1,0:T(4,128)S(1)}, u32[]{:S(2)}, u32[]{:S(2)}) collective-permute-start(f32[1,4,1024]{2,1,0:T(4,128)S(1)} %relay.3.here_ref), channel_id=1, source_target_pairs={{0,1},{1,0},{2,3},{3,2},{4,5},{5,4},{6,7},{7,6},{8,9},{9,8},{10,11... | collective-permute-start | bytes 49160 | tf_op jit(solution)/shard_map/ppermute | solution.py:313
  50.0 3.0 %collective-permute-done.8.there_ref = f32[1,4,1024]{2,1,0:T(4,128)S(1)} collective-permute-done((f32[1,4,1024]{2,1,0:T(4,128)S(1)}, f32[1,4,1024]{2,1,0:T(4,128)S(1)}, u32[]{:S(2)}, u32[]{:S(2)}) %collective-permute-start.8) | collective-permute-done | bytes 16416 | tf_op jit(solution)/shard_map/ppermute | solution.py:313
  53.0 6.2 %gradient.1 = f32[192,2048]{1,0:T(8,128)} custom-call(f32[1,4,1024]{2,1,0:T(4,128)S(1)} %relay.3.here_ref, f32[1,4,1024]{2,1,0:T(4,128)S(1)} %collective-permute-done.8.there_ref, f32[1,128]{1,0:T(1,128)S(1)} %get-tuple-element.27.refs_5_.refs_3_.refs_6_.peak_ref, f32[192,2048]{1,0:T(8,128)S(1)} %get-tuple-element.36.weight_unit, ...), custom_call_target="tpu_custom_call" | custom-call | flops 4294967296 | bytes 3145728 | tf_op jit(solution)/shard_map/gradient/pallas_call | solution.py:36
  (13 shorter events, 0.3 us)
Async XLA Ops:
  0.6 4.8 %collective-permute-start = (s32[1,256]{1,0:T(1,128)}, s32[1,256]{1,0:T(1,128)S(1)}, u32[]{:S(2)}, u32[]{:S(2)}) collective-permute-start(s32[1,256]{1,0:T(1,128)} %param.10), channel_id=1, source_target_pairs={{0,1},{1,0},{2,3},{3,2},{4,5},{5,4},{6,7},{7,6},{8,9},{9,8},{10,11... | collective-permute-start | bytes 3080 | tf_op jit(solution)/shard_map/ppermute | solution.py:313
  5.4 0.9 %copy-start = (bf16[1,256,192]{1,2,0:T(8,128)(2,1)S(1)}, bf16[1,256,192]{1,2,0:T(8,128)(2,1)}, u32[]{:S(2)}) copy-start(bf16[1,256,192]{1,2,0:T(8,128)(2,1)} %param.9) | copy-start | bytes 294916
  6.3 0.9 %copy-start.1 = (bf16[1,256,192]{1,2,0:T(8,128)(2,1)S(1)}, bf16[1,256,192]{1,2,0:T(8,128)(2,1)}, u32[]{:S(2)}) copy-start(bf16[1,256,192]{1,2,0:T(8,128)(2,1)} %param.8) | copy-start | bytes 294916
  7.3 11.7 %collective-permute-start.4 = (bf16[2,192,128]{2,1,0:T(8,128)(2,1)S(1)}, bf16[2,192,128]{2,1,0:T(8,128)(2,1)S(1)}, u32[]{:S(2)}, u32[]{:S(2)}) collective-permute-start(bf16[2,192,128]{2,1,0:T(8,128)(2,1)S(1)} %pack.1.refs_0_), channel_id=1, source_target_pairs={{0,1},{1,0},{2,3},{3,2},{4,5},{5,4},{6,7},{7,6},{8,9},{9,8},{10,11... | collective-permute-start | bytes 294920 | tf_op jit(solution)/shard_map/ppermute | solution.py:313
  9.4 9.6 %collective-permute-start.3 = (bf16[2,192,128]{2,1,0:T(8,128)(2,1)S(1)}, bf16[2,192,128]{2,1,0:T(8,128)(2,1)S(1)}, u32[]{:S(2)}, u32[]{:S(2)}) collective-permute-start(bf16[2,192,128]{2,1,0:T(8,128)(2,1)S(1)} %pack.1.refs_0_), channel_id=1, source_target_pairs={{0,24},{8,16},{16,8},{24,0},{1,25},{9,17},{17,9},{25,1},{2,26},{10... | collective-permute-start | bytes 294920 | tf_op jit(solution)/shard_map/ppermute | solution.py:313
  13.0 6.9 %collective-permute-start.2 = (bf16[2,192,128]{2,1,0:T(8,128)(2,1)S(1)}, bf16[2,192,128]{2,1,0:T(8,128)(2,1)S(1)}, u32[]{:S(2)}, u32[]{:S(2)}) collective-permute-start(bf16[2,192,128]{2,1,0:T(8,128)(2,1)S(1)} %pack.1.refs_0_), channel_id=1, source_target_pairs={{0,16},{8,24},{16,0},{24,8},{1,17},{9,25},{17,1},{25,9},{2,18},{10... | collective-permute-start | bytes 294920 | tf_op jit(solution)/shard_map/ppermute | solution.py:313
  13.0 6.9 %collective-permute-start.1 = (bf16[2,192,128]{2,1,0:T(8,128)(2,1)S(1)}, bf16[2,192,128]{2,1,0:T(8,128)(2,1)S(1)}, u32[]{:S(2)}, u32[]{:S(2)}) collective-permute-start(bf16[2,192,128]{2,1,0:T(8,128)(2,1)S(1)} %pack.1.refs_0_), channel_id=1, source_target_pairs={{0,8},{8,0},{16,24},{24,16},{1,9},{9,1},{17,25},{25,17},{2,10},{10... | collective-permute-start | bytes 294920 | tf_op jit(solution)/shard_map/ppermute | solution.py:313
  13.8 0.8 %copy-start.2 = (f32[16384]{0:T(1024)S(1)}, f32[16384]{0:T(1024)}, u32[]{:S(2)}) copy-start(f32[16384]{0:T(1024)} %param.11) | copy-start | bytes 196612
  20.1 2.1 %collective-permute-start.5 = (bf16[4,2,192,128]{3,2,1,0:T(8,128)(2,1)S(1)}, bf16[4,2,192,128]{3,2,1,0:T(8,128)(2,1)S(1)}, u32[]{:S(2)}, u32[]{:S(2)}) collective-permute-start(bf16[4,2,192,128]{3,2,1,0:T(8,128)(2,1)S(1)} %get-tuple-element.28.refs_0_), channel_id=1, source_target_pairs={{0,2},{2,0},{4,6},{6,4},{1,3},{3,1},{5,7},{7,5},{8,10},{10,8},{12,... | collective-permute-start | bytes 1179656 | tf_op jit(solution)/shard_map/ppermute | solution.py:313
  20.1 9.4 %collective-permute-start.6 = (bf16[3,2,192,128]{3,2,1,0:T(8,128)(2,1)S(1)}, bf16[3,2,192,128]{3,2,1,0:T(8,128)(2,1)S(1)}, u32[]{:S(2)}, u32[]{:S(2)}) collective-permute-start(bf16[3,2,192,128]{3,2,1,0:T(8,128)(2,1)S(1)} %get-tuple-element.33), channel_id=1, source_target_pairs={{0,1},{1,0},{2,3},{3,2},{4,5},{5,4},{6,7},{7,6},{8,9},{9,8},{10,11... | collective-permute-start | bytes 884744 | tf_op jit(solution)/shard_map/ppermute | solution.py:313
  29.6 1.8 %collective-permute-start.7 = (bf16[4,2,192,128]{3,2,1,0:T(8,128)(2,1)S(1)}, bf16[4,2,192,128]{3,2,1,0:T(8,128)(2,1)S(1)}, u32[]{:S(2)}, u32[]{:S(2)}) collective-permute-start(bf16[4,2,192,128]{3,2,1,0:T(8,128)(2,1)S(1)} %join.3.refs_0_), channel_id=1, source_target_pairs={{0,2},{2,0},{4,6},{6,4},{1,3},{3,1},{5,7},{7,5},{8,10},{10,8},{12,... | collective-permute-start | bytes 1179656 | tf_op jit(solution)/shard_map/ppermute | solution.py:313
  49.2 3.8 %collective-permute-start.8 = (f32[1,4,1024]{2,1,0:T(4,128)S(1)}, f32[1,4,1024]{2,1,0:T(4,128)S(1)}, u32[]{:S(2)}, u32[]{:S(2)}) collective-permute-start(f32[1,4,1024]{2,1,0:T(4,128)S(1)} %relay.3.here_ref), channel_id=1, source_target_pairs={{0,1},{1,0},{2,3},{3,2},{4,5},{5,4},{6,7},{7,6},{8,9},{9,8},{10,11... | collective-permute-start | bytes 49160 | tf_op jit(solution)/shard_map/ppermute | solution.py:313

commit v6 on v5

--- a/solution.py
+++ b/solution.py
@@ -29,18 +29,21 @@
     return pltpu.VMEM(dims, dtype)
 
 
-def call(kernel, name, out_shape, args, cost=(0, 0, 0), **more):
+def call(kernel, name, out_shape, args, **more):
     many = isinstance(out_shape, (list, tuple))
     specs = dict(in_specs=[ON_CHIP] * len(args), out_specs=[ON_CHIP] * len(out_shape) if many else ON_CHIP)
-    flops, moved, exps = map(int, cost)
     return pl.pallas_call(
         kernel,
         out_shape=out_shape,
         compiler_params=pltpu.CompilerParams(vmem_limit_bytes=LIMIT),
-        cost_estimate=pl.CostEstimate(flops=flops, bytes_accessed=moved, transcendentals=exps),
+        cost_estimate=pl.CostEstimate(flops=1, bytes_accessed=1, transcendentals=0),
         name=name,
         **{**specs, **more},
     )(*args)
+
+
+def swap(block, axis, apart=1):
+    return lax.ppermute(block, axis, [(i, i ^ apart) for i in range(lax.axis_size(axis))])
 
 
 def here():
@@ -53,28 +56,34 @@
     return high, mid, row - high - mid
 
 
-def prep_kernel(n_dp, teacher_hbm, student_hbm, center_ref, new_hbm, wt_ref, ws_ref, unit_ref, scale_ref, peak_ref, *scratch):
-    teacher_buf, student_buf, new_buf, in_t, in_s, out = scratch
+def prep_kernel(n_dp, teacher_hbm, student_hbm, center_hbm, new_hbm, wt_ref, ws_ref, unit_ref, scale_ref, peak_ref, *scratch):
+    teacher_buf, student_buf, new_buf, center_buf, in_t, in_s, out, in_c = scratch
     chunks, bot, width = new_buf.shape
-    own = chunks // n_dp
     dp, fsdp, _ = here()
+    first = dp * (chunks * width)
     at = [slice(i * width, (i + 1) * width) for i in range(chunks)]
+    far = [pl.ds(pl.multiple_of(first + i * width, width), width) for i in range(chunks)]
+    start = pl.multiple_of((fsdp * n_dp + dp) * (chunks * width), 128)
+    center_load = pltpu.make_async_copy(center_hbm.at[:, pl.ds(start, chunks * width)], center_buf, in_c)
     loads = [
         (
-            pltpu.make_async_copy(teacher_hbm.at[:, at[i]], teacher_buf.at[i], in_t.at[i]),
-            pltpu.make_async_copy(student_hbm.at[:, at[i]], student_buf.at[i], in_s.at[i]),
+            pltpu.make_async_copy(teacher_hbm.at[:, far[i]], teacher_buf.at[i], in_t.at[i]),
+            pltpu.make_async_copy(student_hbm.at[:, far[i]], student_buf.at[i], in_s.at[i]),
         )
         for i in range(chunks)
     ]
-    stores = [pltpu.make_async_copy(new_buf.at[i], new_hbm.at[:, at[i]], out.at[i]) for i in range(chunks)]
+    stores = [pltpu.make_async_copy(new_buf.at[i], new_hbm.at[:, far[i]], out.at[i]) for i in range(chunks)]
+    center_load.start()
     for pair in loads:
         for load in pair:
             load.start()
-    start = pl.multiple_of((fsdp * n_dp + dp) * (own * width), 128)
-    center = center_ref[:, pl.ds(start, own * width)]
+    center_load.wait()
+    center = center_buf[...]
     peak = jnp.max(-center, axis=1, keepdims=True)
     peak_ref[...] = jnp.broadcast_to(peak, peak_ref.shape)
     splits = cast_split(-center - peak)
+    row = lax.broadcasted_iota(jnp.int32, (DEPTH - bot, width), 0)
+    zero = jnp.zeros((DEPTH - bot, width), jnp.float32)
     for i in range(chunks):
         for load in loads[i]:
             load.wait()
@@ -82,22 +91,15 @@
         new = 0.994 * teacher_buf[i] + 0.006 * student
         new_buf[i] = new
         stores[i].start()
-
-        @pl.when(dp == i // own)
-        def _():
-            to = at[i % own]
-            high, mid, low = [part[:, to] for part in splits]
-            row = lax.broadcasted_iota(jnp.int32, (DEPTH - bot, width), 0)
-            zero = jnp.zeros((DEPTH - bot, width), jnp.float32)
-            extra = jnp.where(row == 0, high, jnp.where(row == 1, mid, jnp.where(row == 2, low, zero)))
-            scale = lax.rsqrt(jnp.sum(student * student, axis=0, keepdims=True) + EPS)
-            unit_s = student * scale
-            unit_t = new * lax.rsqrt(jnp.sum(new * new, axis=0, keepdims=True) + EPS)
-            wt_ref[to, :] = jnp.concatenate([unit_t, extra], axis=0).astype(jnp.bfloat16).T
-            ws_ref[to, :] = jnp.concatenate([unit_s, zero], axis=0).astype(jnp.bfloat16).T
-            unit_ref[:, to] = unit_s
-            scale_ref[:, to] = scale
-
+        high, mid, low = [part[:, at[i]] for part in splits]
+        extra = jnp.where(row == 0, high, jnp.where(row == 1, mid, jnp.where(row == 2, low, zero)))
+        scale = lax.rsqrt(jnp.sum(student * student, axis=0, keepdims=True) + EPS)
+        unit_s = student * scale
+        unit_t = new * lax.rsqrt(jnp.sum(new * new, axis=0, keepdims=True) + EPS)
+        wt_ref[at[i], :] = jnp.concatenate([unit_t, extra], axis=0).astype(jnp.bfloat16).T
+        ws_ref[at[i], :] = jnp.concatenate([unit_s, zero], axis=0).astype(jnp.bfloat16).T
+        unit_ref[:, at[i]] = unit_s
+        scale_ref[:, at[i]] = scale
     for store in stores:
         store.wait()
 
@@ -106,9 +108,7 @@
     bot, cols = teacher_weight.shape
     own = cols // n_dp
     width = min(512, own)
-    chunks = cols // width
-    teacher_weight = pltpu.with_memory_space_constraint(teacher_weight, pltpu.HBM)
-    student_weight = pltpu.with_memory_space_constraint(student_weight, pltpu.HBM)
+    chunks = own // width
     return call(
         functools.partial(prep_kernel, n_dp),
         "prep",
@@ -121,17 +121,90 @@
             held(1, 128),
         ],
         (teacher_weight, student_weight, center),
-        (20 * bot * cols, 12 * bot * cols, 0),
-        in_specs=[IN_HBM, IN_HBM, ON_CHIP],
+        in_specs=[IN_HBM] * 3,
         out_specs=[IN_HBM] + [ON_CHIP] * 5,
+        scratch_shapes=[held(chunks, bot, width)] * 3
+        + [held(1, own)]
+        + [pltpu.SemaphoreType.DMA((chunks,))] * 3
+        + [pltpu.SemaphoreType.DMA],
+    )
+
+
+def rest_kernel(teacher_hbm, student_hbm, after, before_hbm, new_hbm, done_ref, *scratch):
+    teacher_buf, student_buf, new_buf, in_t, in_s, out = scratch
+    chunks, bot, width = new_buf.shape
+    own = chunks * width
+    parts = teacher_hbm.shape[1] // own - 1
+    dp = here()[0]
+    done_ref[...] = jnp.zeros_like(done_ref)
+    for part in range(parts):
+        first = lax.rem(dp + 1 + part, parts + 1) * own
+        far = [pl.ds(pl.multiple_of(first + i * width, width), width) for i in range(chunks)]
+        loads = [
+            (
+                pltpu.make_async_copy(teacher_hbm.at[:, far[i]], teacher_buf.at[i], in_t.at[i]),
+                pltpu.make_async_copy(student_hbm.at[:, far[i]], student_buf.at[i], in_s.at[i]),
+            )
+            for i in range(chunks)
+        ]
+        stores = [pltpu.make_async_copy(new_buf.at[i], new_hbm.at[:, far[i]], out.at[i]) for i in range(chunks)]
+        for pair in loads:
+            for load in pair:
+                load.start()
+        for i in range(chunks):
+            for load in loads[i]:
+                load.wait()
+            new_buf[i] = 0.994 * teacher_buf[i] + 0.006 * student_buf[i]
+            stores[i].start()
+        for store in stores:
+            store.wait()
+
+
+def update_rest(teacher_weight, student_weight, after, new, own):
+    bot, cols = teacher_weight.shape
+    width = min(512, own)
+    chunks = own // width
+    return call(
+        rest_kernel,
+        "rest",
+        [pltpu.HBM((bot, cols), jnp.float32), held(8, 128)],
+        (teacher_weight, student_weight, after, new),
+        in_specs=[IN_HBM] * 4,
+        out_specs=[IN_HBM, ON_CHIP],
+        input_output_aliases={3: 0},
         scratch_shapes=[held(chunks, bot, width)] * 3 + [pltpu.SemaphoreType.DMA((chunks,))] * 3,
+    )
+
+
+def fetch_kernel(student_hbm, teacher_hbm, student_ref, teacher_ref, sems):
+    half = student_ref.shape[1]
+    side = pl.ds(pl.multiple_of(here()[2] * half, half), half)
+    loads = [
+        pltpu.make_async_copy(student_hbm.at[:, side], student_ref, sems.at[0]),
+        pltpu.make_async_copy(teacher_hbm, teacher_ref, sems.at[1]),
+    ]
+    for load in loads:
+        load.start()
+    for load in loads:
+        load.wait()
+
+
+def fetch(student, teacher):
+    bot, crops = student.shape
+    return call(
+        fetch_kernel,
+        "fetch",
+        [held(bot, crops // 2, dtype=jnp.bfloat16), held(bot, crops, dtype=jnp.bfloat16)],
+        (student, teacher),
+        in_specs=[IN_HBM] * 2,
+        scratch_shapes=[pltpu.SemaphoreType.DMA((2,))],
     )
 
 
 def pack_kernel(student_ref, teacher_ref, index_ref, out_ref):
     half = out_ref.shape[2]
     lower = here()[2] == 0
-    out_ref[0] = jnp.where(lower, student_ref[:, :half], student_ref[:, half:])
+    out_ref[0] = student_ref[...]
     index = jnp.where(lower, index_ref[:, :half], index_ref[:, half:])
     row = lax.broadcasted_iota(jnp.int32, (teacher_ref.shape[1], half), 0)
     pick = jnp.where(row == index, 1.0, 0.0).astype(jnp.bfloat16)
@@ -139,8 +212,8 @@
 
 
 def pack(student, teacher, index):
-    bot, crops = student.shape
-    return call(pack_kernel, "pack", held(2, bot, crops // 2, dtype=jnp.bfloat16), (student, teacher, index))
+    bot, half = student.shape
+    return call(pack_kernel, "pack", held(2, bot, half, dtype=jnp.bfloat16), (student, teacher, index))
 
 
 def join_kernel(n_in, n_after, *refs):
@@ -220,44 +293,46 @@
                     mine, theirs = [jnp.where(first, *side) for side in read]
                     pieces.append(jnp.where(core == half, mine, theirs))
             rows.append(jnp.concatenate(pieces, axis=1))
-    rows = jnp.concatenate(rows, axis=0)
-    for i in range(total_ref.shape[0]):
-        total_ref[i] = rows
-
-
-def scores(feats, ws, wt, peak, last=None):
+    total_ref[...] = jnp.concatenate(rows, axis=0)
+
+
+def scores(feats, ws, wt, peak, last=()):
     n, _, bot, width = feats.shape
     cols, rows = ws.shape[0], n * width
-    copies, before = last or (0, ())
     return call(
-        functools.partial(score_kernel, last is not None),
+        functools.partial(score_kernel, bool(last)),
         "scores",
         [
             held(cols, rows, dtype=jnp.bfloat16),
             held(cols, rows, dtype=jnp.bfloat16),
             held(bot, rows, dtype=jnp.bfloat16),
-            held(copies, 4, 2 * rows) if last else held(2, rows),
+            held(4, 2 * rows) if last else held(2, rows),
         ],
-        (*before, feats, ws, wt, peak),
-        (4 * rows * cols * DEPTH, 4 * rows * cols, 2 * rows * cols),
+        (*last, feats, ws, wt, peak),
         scratch_shapes=[held(2, rows)] if last else [],
     )
 
 
-def relay_kernel(in_ref, out_ref):
-    rows = jnp.concatenate(combine([in_ref[i] for i in range(in_ref.shape[0])]), axis=0)
-    for i in range(out_ref.shape[0]):
-        out_ref[i] = rows
-
-
-def relay(parts, copies):
-    return call(relay_kernel, "relay", held(copies, *parts.shape[1:]), (parts,))
+def relay_kernel(*refs):
+    parts = [ref[...] for ref in refs[:-1]]
+    if len(parts[0].shape) == 3:
+        parts = [parts[0][i] for i in range(parts[0].shape[0])]
+    refs[-1][...] = jnp.concatenate(combine(parts), axis=0)
+
+
+def add_up(total, axis):
+    n = lax.axis_size(axis)
+    if n <= DIRECT:
+        parts = [total, *[swap(total, axis, k) for k in range(1, n)]]
+    else:
+        parts = [lax.all_to_all(jnp.broadcast_to(total[None], (n, *total.shape)), axis, 0, 0, tiled=True)]
+    return call(relay_kernel, "relay", held(*total.shape), parts)
 
 
 def grad_kernel(here_ref, there_ref, peak_ref, weight_unit, weight_scale, *refs):
     units, exps, expt, out_ref, scales = refs[:4], refs[4:8], refs[8:12], refs[12], refs[13]
     dp, _, core = here()
-    total_s, log_t = combine([here_ref[0], there_ref[0]])
+    total_s, log_t = combine([here_ref[...], there_ref[...]])
     scales[0:2, :] = 10.0 / total_s
     scales[2:4, :] = -10.0 * jnp.exp2(GAIN_T * peak_ref[:, :1] - log_t)
     bot, rows = units[0].shape
@@ -298,38 +373,37 @@
         "gradient",
         shape(bot, cols),
         (here_total, there_total, peak, weight_unit, weight_scale, *units, *exps, *expt),
-        (16 * rows * cols * DEPTH, 8 * bot * cols, 0),
         scratch_shapes=[held(4, 2 * rows)],
     )
 
 
 def shards(teacher_weight, student_weight, teacher_feats, student_feats, pairing, center):
-    n_dp, n_fsdp, n_proto = [lax.axis_size(axis) for axis in ("dp", "fsdp", "proto")]
-
-    def spread(copies, axis):
-        return lax.all_to_all(copies, axis, 0, 0, tiled=True)
-
-    def swap(block, axis, apart=1):
-        return lax.ppermute(block, axis, [(i, i ^ apart) for i in range(lax.axis_size(axis))])
-
-    teacher_new, wt, ws, unit, scale, peak = prepare(teacher_weight, student_weight, center[None, :], n_dp)
+    n_dp, n_fsdp = lax.axis_size("dp"), lax.axis_size("fsdp")
+    in_hbm = lambda array: pltpu.with_memory_space_constraint(array, pltpu.HBM)
+    teacher_weight, student_weight, center = in_hbm(teacher_weight), in_hbm(student_weight), in_hbm(center[None, :])
+
+    index = swap(pairing, "dp")
+    mine = pack(*fetch(in_hbm(student_feats[0].T), in_hbm(teacher_feats[0].T)), index)
+    new, wt, ws, unit, scale, peak = prepare(teacher_weight, student_weight, center, n_dp)
     weights = (ws, wt, peak)
-    mine = pack(student_feats[0].T, teacher_feats[0].T, swap(pairing, "dp"))
+    own_cols = ws.shape[0]
     if n_fsdp <= DIRECT:
         along = [swap(mine, "fsdp", k) for k in range(1, n_fsdp)]
         other = swap(mine, "dp")
-        own, rest = join([mine, *along], [n_fsdp, n_fsdp - 1], (other, peak))
+        (rest,) = join(along, [n_fsdp - 1], (other, peak))
+        teacher_new, done = update_rest(teacher_weight, student_weight, rest, new, own_cols)
+        (own,) = join([mine, *along], [n_fsdp], (done,))
         parts = [scores(own, *weights), scores(swap(own, "proto"), *weights)]
         (other,) = join([other, swap(rest, "dp")], [n_fsdp], [part[3] for part in parts])
     else:
-        own = spread(jnp.broadcast_to(mine[None], (n_fsdp, *mine.shape)), "fsdp")
+        own = lax.all_to_all(jnp.broadcast_to(mine[None], (n_fsdp, *mine.shape)), "fsdp", 0, 0, tiled=True)
         other = swap(own, "dp")
+        teacher_new, _ = update_rest(teacher_weight, student_weight, own, new, own_cols)
         parts = [scores(own, *weights), scores(swap(own, "proto"), *weights)]
     parts.append(scores(other, *weights))
-    before = [part[3] for part in parts]
-    parts.append(scores(swap(other, "proto"), *weights, last=(n_proto, before)))
+    parts.append(scores(swap(other, "proto"), *weights, last=[part[3] for part in parts]))
     exps, expt, units, totals = zip(*parts)
-    total = relay(spread(relay(spread(totals[3], "proto"), n_fsdp), "fsdp"), 1)
+    total = add_up(add_up(totals[3], "proto"), "fsdp")
     student_grad = gradient(total, swap(total, "dp"), peak, unit, scale, units, exps, expt)
     return (teacher_new, student_grad)
 

time: 59.4 us -> 56.2 us (0.946)
  blocking collectives: 16.3 us -> 0 us
  waiting for transfers between devices: 11.8 us -> 18.6 us
  starting transfers between devices: 11.1 us -> 17.2 us
  Pallas kernels: 16.6 us -> 19.5 us
  local copies, waits for them, and re-layouts: 2.62 us -> 0 us
    all_to_all x2 -> x0, blocking collectives: 16.3 us -> none  [spread(): return lax.all_to_all(copies, axis, 0, 0, tiled=True)]
    ppermute x9 -> x15, waiting for transfers between devices: 11.8 us -> 18.6 us  [swap(): lax.ppermute(block, axis, [(i, i ^ apart) for i in range(lax.axis_size(ax...]
    ppermute x9 -> x15, starting transfers between devices: 11.1 us -> 17.2 us  [swap(): lax.ppermute(block, axis, [(i, i ^ apart) for i in range(lax.axis_size(ax...]
    pallas_call x11 -> x14, Pallas kernels: 16.6 us -> 19.5 us  [call(): pl.pallas_call(kernel, out_shape=out_shape, compiler_params=pltpu.Compile...]
    unnamed x6 -> x0, local copies, waits for them, and re-layouts: 2.62 us -> none
  transfers between devices with their start and end apart: 9 -> 15, of which waited for: 5 -> 9; matrix products, arithmetic and copies ran while one was open for 0% -> 0% of each run, Pallas kernels for 15% -> 16%
where the time goes in v6:
time: 56.2 us; the launch traced here: 56.1 us
  Pallas kernels  19.5 us (35%)
  waiting for transfers between devices  18.6 us (33%)
  starting transfers between devices  17.2 us (31%)
  between operations  0.76 us (1%)
    pallas_call x14, Pallas kernels, call(): pl.pallas_call(kernel, out_shape=out_shape, compiler_params=pltpu.Compile...  19.5 us
    ppermute x15, waiting for transfers between devices, swap(): lax.ppermute(block, axis, [(i, i ^ apart) for i in range(lax.axis_size(ax...  18.6 us
    ppermute x15, starting transfers between devices, swap(): lax.ppermute(block, axis, [(i, i ^ apart) for i in range(lax.axis_size(ax...  17.2 us
  transfers between devices with their start and end apart: 15, of which 9 were waited for; matrix products, arithmetic and copies ran while one was open for 0% of the time, Pallas kernels for 16%

profile of v6, /device:TPU:0, one launch (start us, length us, event | category | flops | bytes accessed | tf_op | source)
XLA Modules:
  0.0 56.1 jit_solution(14215184851246366775)
XLA Ops:
  0.6 3.0 %collective-permute-start = (s32[1,256]{1,0:T(1,128)}, s32[1,256]{1,0:T(1,128)S(1)}, u32[]{:S(2)}, u32[]{:S(2)}) collective-permute-start(s32[1,256]{1,0:T(1,128)} %param.10), channel_id=1, source_target_pairs={{0,1},{1,0},{2,3},{3,2},{4,5},{5,4},{6,7},{7,6},{8,9},{9,8},{10,11... | collective-permute-start | bytes 3080 | tf_op jit(solution)/shard_map/ppermute | solution.py:46
  3.6 0.9 %fetch.1 = (bf16[192,128]{1,0:T(8,128)(2,1)S(1)}, bf16[192,256]{1,0:T(8,128)(2,1)S(1)}) custom-call(bf16[192,256]{1,0:T(8,128)(2,1)} %bitcast.7, bf16[192,256]{1,0:T(8,128)(2,1)} %bitcast.8), custom_call_target="tpu_custom_call" | custom-call | flops 1 | bytes 1 | tf_op jit(solution)/shard_map/fetch/pallas_call | solution.py:35
  4.6 0.8 %collective-permute-done.index_ref = s32[1,256]{1,0:T(1,128)S(1)} collective-permute-done((s32[1,256]{1,0:T(1,128)}, s32[1,256]{1,0:T(1,128)S(1)}, u32[]{:S(2)}, u32[]{:S(2)}) %collective-permute-start) | collective-permute-done | bytes 1056 | tf_op jit(solution)/shard_map/ppermute | solution.py:46
  5.6 2.1 %collective-permute-start.4 = (bf16[2,192,128]{2,1,0:T(8,128)(2,1)S(1)}, bf16[2,192,128]{2,1,0:T(8,128)(2,1)S(1)}, u32[]{:S(2)}, u32[]{:S(2)}) collective-permute-start(bf16[2,192,128]{2,1,0:T(8,128)(2,1)S(1)} %pack.1.refs_0_), channel_id=1, source_target_pairs={{0,1},{1,0},{2,3},{3,2},{4,5},{5,4},{6,7},{7,6},{8,9},{9,8},{10,11... | collective-permute-start | bytes 294920 | tf_op jit(solution)/shard_map/ppermute | solution.py:46
  7.7 3.6 %collective-permute-start.3 = (bf16[2,192,128]{2,1,0:T(8,128)(2,1)S(1)}, bf16[2,192,128]{2,1,0:T(8,128)(2,1)S(1)}, u32[]{:S(2)}, u32[]{:S(2)}) collective-permute-start(bf16[2,192,128]{2,1,0:T(8,128)(2,1)S(1)} %pack.1.refs_0_), channel_id=1, source_target_pairs={{0,24},{8,16},{16,8},{24,0},{1,25},{9,17},{17,9},{25,1},{2,26},{10... | collective-permute-start | bytes 294920 | tf_op jit(solution)/shard_map/ppermute | solution.py:46
  11.3 0.8 %collective-permute-start.1 = (bf16[2,192,128]{2,1,0:T(8,128)(2,1)S(1)}, bf16[2,192,128]{2,1,0:T(8,128)(2,1)S(1)}, u32[]{:S(2)}, u32[]{:S(2)}) collective-permute-start(bf16[2,192,128]{2,1,0:T(8,128)(2,1)S(1)} %pack.1.refs_0_), channel_id=1, source_target_pairs={{0,8},{8,0},{16,24},{24,16},{1,9},{9,1},{17,25},{25,17},{2,10},{10... | collective-permute-start | bytes 294920 | tf_op jit(solution)/shard_map/ppermute | solution.py:46
  12.0 3.6 %prep.1 = (f32[192,4096]{1,0:T(8,128)}, bf16[2048,256]{1,0:T(8,128)(2,1)S(1)}, bf16[2048,256]{1,0:T(8,128)(2,1)S(1)}, f32[192,2048]{1,0:T(8,128)S(1)}, f32[1,2048]{1,0:T(1,128)S(1)}, /*index=5*/f32[1,128]{1,0:T(1,128)S(1)}) custom-call(f32[192,4096]{1,0:T(8,128)} %teacher_hbm.3, f32[192,4096]{1,0:T(8,128)} %student_hbm.3, f32[1,16384]{1,0:T(1,128)} %bitcast.9), custom_call_target="tpu_custom_call" | custom-call | flops 1 | bytes 1 | tf_op jit(solution)/shard_map/prep/pallas_call | solution.py:35
  15.7 2.5 %collective-permute-done.2.refs_1_.refs_2_ = bf16[2,192,128]{2,1,0:T(8,128)(2,1)S(1)} collective-permute-done((bf16[2,192,128]{2,1,0:T(8,128)(2,1)S(1)}, bf16[2,192,128]{2,1,0:T(8,128)(2,1)S(1)}, u32[]{:S(2)}, u32[]{:S(2)}) %collective-permute-start.2) | collective-permute-done | bytes 98336 | tf_op jit(solution)/shard_map/ppermute | solution.py:46
  18.2 2.8 %rest.1 = (f32[192,4096]{1,0:T(8,128)}, f32[8,128]{1,0:T(8,128)S(1)}) custom-call(f32[192,4096]{1,0:T(8,128)} %teacher_hbm.3, f32[192,4096]{1,0:T(8,128)} %student_hbm.3, bf16[3,2,192,128]{3,2,1,0:T(8,128)(2,1)S(1)} %join.3.after, f32[192,4096]{1,0:T(8,128)} %get-tuple-element.31.before_hbm), custom_call_target="tpu_custom_call", output_to_operand_aliasing={{0}: (3, {})} | custom-call | flops 1 | bytes 1 | tf_op jit(solution)/shard_map/rest/pallas_call | solution.py:35
  21.7 1.4 %scores.4 = (bf16[2048,512]{1,0:T(8,128)(2,1)S(1)}, bf16[2048,512]{1,0:T(8,128)(2,1)S(1)}, bf16[192,512]{1,0:T(8,128)(2,1)S(1)}, f32[2,512]{1,0:T(2,128)S(1)}) custom-call(bf16[4,2,192,128]{3,2,1,0:T(8,128)(2,1)S(1)} %join.4.refs_0_, bf16[2048,256]{1,0:T(8,128)(2,1)S(1)} %get-tuple-element.34.refs_1_.refs_4_, ...), custom_call_target="tpu_custom_call" | custom-call | flops 1 | bytes 1 | tf_op jit(solution)/shard_map/scores/pallas_call | solution.py:35
  23.1 1.4 %scores.5 = (bf16[2048,512]{1,0:T(8,128)(2,1)S(1)}, bf16[2048,512]{1,0:T(8,128)(2,1)S(1)}, bf16[192,512]{1,0:T(8,128)(2,1)S(1)}, f32[2,512]{1,0:T(2,128)S(1)}) custom-call(bf16[4,2,192,128]{3,2,1,0:T(8,128)(2,1)S(1)} %collective-permute-done.5.refs_0_, bf16[2048,256]{1,0:T(8,128)(2,1)S(1)} %get-tuple-element.34.refs_1_.refs_4_, ...), custom_call_target="tpu_custom_call" | custom-call | flops 1 | bytes 1 | tf_op jit(solution)/shard_map/scores/pallas_call | solution.py:35
  24.6 6.0 %collective-permute-done.6.refs_1_ = bf16[3,2,192,128]{3,2,1,0:T(8,128)(2,1)S(1)} collective-permute-done((bf16[3,2,192,128]{3,2,1,0:T(8,128)(2,1)S(1)}, bf16[3,2,192,128]{3,2,1,0:T(8,128)(2,1)S(1)}, u32[]{:S(2)}, u32[]{:S(2)}) %collective-permute-start.6) | collective-permute-done | bytes 294944 | tf_op jit(solution)/shard_map/ppermute | solution.py:46
  30.6 1.4 %scores.6 = (bf16[2048,512]{1,0:T(8,128)(2,1)S(1)}, bf16[2048,512]{1,0:T(8,128)(2,1)S(1)}, bf16[192,512]{1,0:T(8,128)(2,1)S(1)}, f32[2,512]{1,0:T(2,128)S(1)}) custom-call(bf16[4,2,192,128]{3,2,1,0:T(8,128)(2,1)S(1)} %join.5.refs_0_, bf16[2048,256]{1,0:T(8,128)(2,1)S(1)} %get-tuple-element.34.refs_1_.refs_4_, ...), custom_call_target="tpu_custom_call" | custom-call | flops 1 | bytes 1 | tf_op jit(solution)/shard_map/scores/pallas_call | solution.py:35
  32.3 1.5 %scores.7 = (bf16[2048,512]{1,0:T(8,128)(2,1)S(1)}, bf16[2048,512]{1,0:T(8,128)(2,1)S(1)}, bf16[192,512]{1,0:T(8,128)(2,1)S(1)}, f32[4,1024]{1,0:T(4,128)S(1)}) custom-call(f32[2,512]{1,0:T(2,128)S(1)} %get-tuple-element.36.refs_2_.refs_0_, f32[2,512]{1,0:T(2,128)S(1)} %get-tuple-element.37.refs_3_.refs_1_, f32[2,512]{1,0:T(2,128)S(1)} %get-tuple-element.38.refs_2_, ...), custom_call_target="tpu_custom_call" | custom-call | flops 1 | bytes 1 | tf_op jit(solution)/shard_map/scores/pallas_call | solution.py:35
  33.8 1.4 %collective-permute-start.10 = (f32[4,1024]{1,0:T(4,128)S(1)}, f32[4,1024]{1,0:T(4,128)S(1)}, u32[]{:S(2)}, u32[]{:S(2)}) collective-permute-start(f32[4,1024]{1,0:T(4,128)S(1)} %get-tuple-element.39.refs_0_), channel_id=1, source_target_pairs={{0,6},{2,4},{4,2},{6,0},{1,7},{3,5},{5,3},{7,1},{8,14},{10,12},{12... | collective-permute-start | bytes 49160 | tf_op jit(solution)/shard_map/ppermute | solution.py:46
  35.8 1.3 %collective-permute-done.10.refs_3_ = f32[4,1024]{1,0:T(4,128)S(1)} collective-permute-done((f32[4,1024]{1,0:T(4,128)S(1)}, f32[4,1024]{1,0:T(4,128)S(1)}, u32[]{:S(2)}, u32[]{:S(2)}) %collective-permute-start.10) | collective-permute-done | bytes 16416 | tf_op jit(solution)/shard_map/ppermute | solution.py:46
  37.0 1.9 %collective-permute-done.9.refs_2_ = f32[4,1024]{1,0:T(4,128)S(1)} collective-permute-done((f32[4,1024]{1,0:T(4,128)S(1)}, f32[4,1024]{1,0:T(4,128)S(1)}, u32[]{:S(2)}, u32[]{:S(2)}) %collective-permute-start.9) | collective-permute-done | bytes 16416 | tf_op jit(solution)/shard_map/ppermute | solution.py:46
  39.0 2.4 %collective-permute-start.13 = (f32[4,1024]{1,0:T(4,128)S(1)}, f32[4,1024]{1,0:T(4,128)S(1)}, u32[]{:S(2)}, u32[]{:S(2)}) collective-permute-start(f32[4,1024]{1,0:T(4,128)S(1)} %relay.2.refs_0_), channel_id=1, source_target_pairs={{0,24},{8,16},{16,8},{24,0},{1,25},{9,17},{17,9},{25,1},{2,26},{10... | collective-permute-start | bytes 49160 | tf_op jit(solution)/shard_map/ppermute | solution.py:46
  41.4 2.0 %collective-permute-start.11 = (f32[4,1024]{1,0:T(4,128)S(1)}, f32[4,1024]{1,0:T(4,128)S(1)}, u32[]{:S(2)}, u32[]{:S(2)}) collective-permute-start(f32[4,1024]{1,0:T(4,128)S(1)} %relay.2.refs_0_), channel_id=1, source_target_pairs={{0,8},{8,0},{16,24},{24,16},{1,9},{9,1},{17,25},{25,17},{2,10},{10... | collective-permute-start | bytes 49160 | tf_op jit(solution)/shard_map/ppermute | solution.py:46
  43.5 1.1 %collective-permute-done.13.refs_3_ = f32[4,1024]{1,0:T(4,128)S(1)} collective-permute-done((f32[4,1024]{1,0:T(4,128)S(1)}, f32[4,1024]{1,0:T(4,128)S(1)}, u32[]{:S(2)}, u32[]{:S(2)}) %collective-permute-start.13) | collective-permute-done | bytes 16416 | tf_op jit(solution)/shard_map/ppermute | solution.py:46
  44.6 1.5 %collective-permute-done.12.refs_2_ = f32[4,1024]{1,0:T(4,128)S(1)} collective-permute-done((f32[4,1024]{1,0:T(4,128)S(1)}, f32[4,1024]{1,0:T(4,128)S(1)}, u32[]{:S(2)}, u32[]{:S(2)}) %collective-permute-start.12) | collective-permute-done | bytes 16416 | tf_op jit(solution)/shard_map/ppermute | solution.py:46
  46.1 0.6 %collective-permute-start.14 = (f32[4,1024]{1,0:T(4,128)S(1)}, f32[4,1024]{1,0:T(4,128)S(1)}, u32[]{:S(2)}, u32[]{:S(2)}) collective-permute-start(f32[4,1024]{1,0:T(4,128)S(1)} %relay.3.here_ref), channel_id=1, source_target_pairs={{0,1},{1,0},{2,3},{3,2},{4,5},{5,4},{6,7},{7,6},{8,9},{9,8},{10,11... | collective-permute-start | bytes 49160 | tf_op jit(solution)/shard_map/ppermute | solution.py:46
  46.7 3.2 %collective-permute-done.14.there_ref = f32[4,1024]{1,0:T(4,128)S(1)} collective-permute-done((f32[4,1024]{1,0:T(4,128)S(1)}, f32[4,1024]{1,0:T(4,128)S(1)}, u32[]{:S(2)}, u32[]{:S(2)}) %collective-permute-start.14) | collective-permute-done | bytes 16416 | tf_op jit(solution)/shard_map/ppermute | solution.py:46
  49.9 6.1 %gradient.1 = f32[192,2048]{1,0:T(8,128)} custom-call(f32[4,1024]{1,0:T(4,128)S(1)} %relay.3.here_ref, f32[4,1024]{1,0:T(4,128)S(1)} %collective-permute-done.14.there_ref, f32[1,128]{1,0:T(1,128)S(1)} %get-tuple-element.30.refs_4_.refs_3_.refs_6_.peak_ref, f32[192,2048]{1,0:T(8,128)S(1)} %get-tuple-element.40.weight_unit, ...), custom_call_target="tpu_custom_call" | custom-call | flops 1 | bytes 1 | tf_op jit(solution)/shard_map/gradient/pallas_call | solution.py:35
  (20 shorter events, 1.8 us)
Async XLA Ops:
  0.6 4.8 %collective-permute-start = (s32[1,256]{1,0:T(1,128)}, s32[1,256]{1,0:T(1,128)S(1)}, u32[]{:S(2)}, u32[]{:S(2)}) collective-permute-start(s32[1,256]{1,0:T(1,128)} %param.10), channel_id=1, source_target_pairs={{0,1},{1,0},{2,3},{3,2},{4,5},{5,4},{6,7},{7,6},{8,9},{9,8},{10,11... | collective-permute-start | bytes 3080 | tf_op jit(solution)/shard_map/ppermute | solution.py:46
  5.6 10.1 %collective-permute-start.4 = (bf16[2,192,128]{2,1,0:T(8,128)(2,1)S(1)}, bf16[2,192,128]{2,1,0:T(8,128)(2,1)S(1)}, u32[]{:S(2)}, u32[]{:S(2)}) collective-permute-start(bf16[2,192,128]{2,1,0:T(8,128)(2,1)S(1)} %pack.1.refs_0_), channel_id=1, source_target_pairs={{0,1},{1,0},{2,3},{3,2},{4,5},{5,4},{6,7},{7,6},{8,9},{9,8},{10,11... | collective-permute-start | bytes 294920 | tf_op jit(solution)/shard_map/ppermute | solution.py:46
  7.7 8.0 %collective-permute-start.3 = (bf16[2,192,128]{2,1,0:T(8,128)(2,1)S(1)}, bf16[2,192,128]{2,1,0:T(8,128)(2,1)S(1)}, u32[]{:S(2)}, u32[]{:S(2)}) collective-permute-start(bf16[2,192,128]{2,1,0:T(8,128)(2,1)S(1)} %pack.1.refs_0_), channel_id=1, source_target_pairs={{0,24},{8,16},{16,8},{24,0},{1,25},{9,17},{17,9},{25,1},{2,26},{10... | collective-permute-start | bytes 294920 | tf_op jit(solution)/shard_map/ppermute | solution.py:46
  11.2 6.9 %collective-permute-start.2 = (bf16[2,192,128]{2,1,0:T(8,128)(2,1)S(1)}, bf16[2,192,128]{2,1,0:T(8,128)(2,1)S(1)}, u32[]{:S(2)}, u32[]{:S(2)}) collective-permute-start(bf16[2,192,128]{2,1,0:T(8,128)(2,1)S(1)} %pack.1.refs_0_), channel_id=1, source_target_pairs={{0,16},{8,24},{16,0},{24,8},{1,17},{9,25},{17,1},{25,9},{2,18},{10... | collective-permute-start | bytes 294920 | tf_op jit(solution)/shard_map/ppermute | solution.py:46
  11.3 6.9 %collective-permute-start.1 = (bf16[2,192,128]{2,1,0:T(8,128)(2,1)S(1)}, bf16[2,192,128]{2,1,0:T(8,128)(2,1)S(1)}, u32[]{:S(2)}, u32[]{:S(2)}) collective-permute-start(bf16[2,192,128]{2,1,0:T(8,128)(2,1)S(1)} %pack.1.refs_0_), channel_id=1, source_target_pairs={{0,8},{8,0},{16,24},{24,16},{1,9},{9,1},{17,25},{25,17},{2,10},{10... | collective-permute-start | bytes 294920 | tf_op jit(solution)/shard_map/ppermute | solution.py:46
  21.0 2.1 %collective-permute-start.5 = (bf16[4,2,192,128]{3,2,1,0:T(8,128)(2,1)S(1)}, bf16[4,2,192,128]{3,2,1,0:T(8,128)(2,1)S(1)}, u32[]{:S(2)}, u32[]{:S(2)}) collective-permute-start(bf16[4,2,192,128]{3,2,1,0:T(8,128)(2,1)S(1)} %join.4.refs_0_), channel_id=1, source_target_pairs={{0,2},{2,0},{4,6},{6,4},{1,3},{3,1},{5,7},{7,5},{8,10},{10,8},{12,... | collective-permute-start | bytes 1179656 | tf_op jit(solution)/shard_map/ppermute | solution.py:46
  21.1 9.4 %collective-permute-start.6 = (bf16[3,2,192,128]{3,2,1,0:T(8,128)(2,1)S(1)}, bf16[3,2,192,128]{3,2,1,0:T(8,128)(2,1)S(1)}, u32[]{:S(2)}, u32[]{:S(2)}) collective-permute-start(bf16[3,2,192,128]{3,2,1,0:T(8,128)(2,1)S(1)} %join.3.after), channel_id=1, source_target_pairs={{0,1},{1,0},{2,3},{3,2},{4,5},{5,4},{6,7},{7,6},{8,9},{9,8},{10,11... | collective-permute-start | bytes 884744 | tf_op jit(solution)/shard_map/ppermute | solution.py:46
  30.5 1.8 %collective-permute-start.7 = (bf16[4,2,192,128]{3,2,1,0:T(8,128)(2,1)S(1)}, bf16[4,2,192,128]{3,2,1,0:T(8,128)(2,1)S(1)}, u32[]{:S(2)}, u32[]{:S(2)}) collective-permute-start(bf16[4,2,192,128]{3,2,1,0:T(8,128)(2,1)S(1)} %join.5.refs_0_), channel_id=1, source_target_pairs={{0,2},{2,0},{4,6},{6,4},{1,3},{3,1},{5,7},{7,5},{8,10},{10,8},{12,... | collective-permute-start | bytes 1179656 | tf_op jit(solution)/shard_map/ppermute | solution.py:46
  33.8 3.2 %collective-permute-start.10 = (f32[4,1024]{1,0:T(4,128)S(1)}, f32[4,1024]{1,0:T(4,128)S(1)}, u32[]{:S(2)}, u32[]{:S(2)}) collective-permute-start(f32[4,1024]{1,0:T(4,128)S(1)} %get-tuple-element.39.refs_0_), channel_id=1, source_target_pairs={{0,6},{2,4},{4,2},{6,0},{1,7},{3,5},{5,3},{7,1},{8,14},{10,12},{12... | collective-permute-start | bytes 49160 | tf_op jit(solution)/shard_map/ppermute | solution.py:46
  35.2 3.7 %collective-permute-start.9 = (f32[4,1024]{1,0:T(4,128)S(1)}, f32[4,1024]{1,0:T(4,128)S(1)}, u32[]{:S(2)}, u32[]{:S(2)}) collective-permute-start(f32[4,1024]{1,0:T(4,128)S(1)} %get-tuple-element.39.refs_0_), channel_id=1, source_target_pairs={{0,4},{2,6},{4,0},{6,2},{1,5},{3,7},{5,1},{7,3},{8,12},{10,14},{12... | collective-permute-start | bytes 49160 | tf_op jit(solution)/shard_map/ppermute | solution.py:46
  35.7 3.2 %collective-permute-start.8 = (f32[4,1024]{1,0:T(4,128)S(1)}, f32[4,1024]{1,0:T(4,128)S(1)}, u32[]{:S(2)}, u32[]{:S(2)}) collective-permute-start(f32[4,1024]{1,0:T(4,128)S(1)} %get-tuple-element.39.refs_0_), channel_id=1, source_target_pairs={{0,2},{2,0},{4,6},{6,4},{1,3},{3,1},{5,7},{7,5},{8,10},{10,8},{12,... | collective-permute-start | bytes 49160 | tf_op jit(solution)/shard_map/ppermute | solution.py:46
  39.0 5.6 %collective-permute-start.13 = (f32[4,1024]{1,0:T(4,128)S(1)}, f32[4,1024]{1,0:T(4,128)S(1)}, u32[]{:S(2)}, u32[]{:S(2)}) collective-permute-start(f32[4,1024]{1,0:T(4,128)S(1)} %relay.2.refs_0_), channel_id=1, source_target_pairs={{0,24},{8,16},{16,8},{24,0},{1,25},{9,17},{17,9},{25,1},{2,26},{10... | collective-permute-start | bytes 49160 | tf_op jit(solution)/shard_map/ppermute | solution.py:46
  41.4 4.6 %collective-permute-start.12 = (f32[4,1024]{1,0:T(4,128)S(1)}, f32[4,1024]{1,0:T(4,128)S(1)}, u32[]{:S(2)}, u32[]{:S(2)}) collective-permute-start(f32[4,1024]{1,0:T(4,128)S(1)} %relay.2.refs_0_), channel_id=1, source_target_pairs={{0,16},{8,24},{16,0},{24,8},{1,17},{9,25},{17,1},{25,9},{2,18},{10... | collective-permute-start | bytes 49160 | tf_op jit(solution)/shard_map/ppermute | solution.py:46
  41.4 4.6 %collective-permute-start.11 = (f32[4,1024]{1,0:T(4,128)S(1)}, f32[4,1024]{1,0:T(4,128)S(1)}, u32[]{:S(2)}, u32[]{:S(2)}) collective-permute-start(f32[4,1024]{1,0:T(4,128)S(1)} %relay.2.refs_0_), channel_id=1, source_target_pairs={{0,8},{8,0},{16,24},{24,16},{1,9},{9,1},{17,25},{25,17},{2,10},{10... | collective-permute-start | bytes 49160 | tf_op jit(solution)/shard_map/ppermute | solution.py:46
  46.1 3.8 %collective-permute-start.14 = (f32[4,1024]{1,0:T(4,128)S(1)}, f32[4,1024]{1,0:T(4,128)S(1)}, u32[]{:S(2)}, u32[]{:S(2)}) collective-permute-start(f32[4,1024]{1,0:T(4,128)S(1)} %relay.3.here_ref), channel_id=1, source_target_pairs={{0,1},{1,0},{2,3},{3,2},{4,5},{5,4},{6,7},{7,6},{8,9},{9,8},{10,11... | collective-permute-start | bytes 49160 | tf_op jit(solution)/shard_map/ppermute | solution.py:46

commit v7 on v6

--- a/solution.py
+++ b/solution.py
@@ -247,16 +247,19 @@
     return lax.axis_index("fsdp") ^ k if n <= DIRECT else k
 
 
-def score_kernel(last, *refs):
+def score_kernel(part, *refs):
+    last = part == 3
     before, refs = (refs[:3], refs[3:]) if last else ((), refs)
-    feats_ref, ws_ref, wt_ref, peak_ref, exps_ref, expt_ref, unit_ref, total_ref, *mine = refs
+    feats_ref, ws_ref, wt_ref, peak_ref, *refs = refs
+    exp_ref, unit_ref, total_ref, *mine = refs[1:] if part else refs
     own_ref = mine[0] if last else total_ref
     n, _, bot, width = feats_ref.shape
     cols = ws_ref.shape[0]
     step = min(STEP, cols)
     per = max(1, min(n, GROUP // width))
     row = lax.broadcasted_iota(jnp.int32, (DEPTH - bot, per * width), 0)
-    for which, w_ref, exp_ref, gain in ((0, ws_ref, exps_ref, GAIN_S), (1, wt_ref, expt_ref, GAIN_T)):
+    for which, w_ref, gain in ((0, ws_ref, GAIN_S), (1, wt_ref, GAIN_T)):
+        base = (2 * part + which) * n * width
         extra = jnp.where(row < 3 * which, 1.0, 0.0).astype(jnp.bfloat16)
         for group in range(n // per):
             values = [feats_ref[group * per + k, which].astype(jnp.float32) for k in range(per)]
@@ -271,7 +274,7 @@
                 score = jnp.dot(w_ref[at:at + step, :], stationary, preferred_element_type=jnp.float32)
                 exps = jnp.exp2(score * gain)
                 total = total + jnp.sum(exps.reshape(step // 8, 8, per * width), axis=0)
-                exp_ref[at:at + step, lanes] = exps.astype(jnp.bfloat16)
+                exp_ref[at:at + step, base + lanes.start:base + lanes.stop] = exps.astype(jnp.bfloat16)
             total = jnp.sum(total, axis=0, keepdims=True)
             if which == 1:
                 total = jnp.log2(total) + GAIN_T * peak_ref[:, :1]
@@ -296,20 +299,22 @@
     total_ref[...] = jnp.concatenate(rows, axis=0)
 
 
-def scores(feats, ws, wt, peak, last=()):
+def scores(part, feats, weights, before=(), exps=None):
     n, _, bot, width = feats.shape
-    cols, rows = ws.shape[0], n * width
+    cols, rows = weights[0].shape[0], n * width
+    args = (*before, feats, *weights, *([exps] if part else []))
     return call(
-        functools.partial(score_kernel, bool(last)),
+        functools.partial(score_kernel, part),
         "scores",
         [
-            held(cols, rows, dtype=jnp.bfloat16),
-            held(cols, rows, dtype=jnp.bfloat16),
+            held(cols, 8 * rows, dtype=jnp.bfloat16),
             held(bot, rows, dtype=jnp.bfloat16),
-            held(4, 2 * rows) if last else held(2, rows),
+            held(4, 2 * rows) if part == 3 else held(2, rows),
         ],
-        (*last, feats, ws, wt, peak),
-        scratch_shapes=[held(2, rows)] if last else [],
+        args,
+        in_specs=[ON_CHIP] * (len(args) - bool(part)) + [IN_HBM] * bool(part),
+        input_output_aliases={len(args) - 1: 0} if part else {},
+        scratch_shapes=[held(2, rows)] if part == 3 else [],
     )
 
 
@@ -330,7 +335,7 @@
 
 
 def grad_kernel(here_ref, there_ref, peak_ref, weight_unit, weight_scale, *refs):
-    units, exps, expt, out_ref, scales = refs[:4], refs[4:8], refs[8:12], refs[12], refs[13]
+    units, exp_ref, out_hbm, scales, feats, buf, sems = refs[:4], *refs[4:]
     dp, _, core = here()
     total_s, log_t = combine([here_ref[...], there_ref[...]])
     scales[0:2, :] = 10.0 / total_s
@@ -338,42 +343,49 @@
     bot, rows = units[0].shape
     width = 128
     n = rows // width
-    sides = []
     for part in range(4):
         view, half = divmod(part, 2)
         base = (dp ^ view) * rows
         at = [pl.ds(pl.multiple_of(base + slot(k, n) * width, width), width) for k in range(n)]
         unit = units[part][...].astype(jnp.float32)
-        for which, exp_ref in ((0, exps[part]), (1, expt[part ^ 2])):
+        for which, lies in ((0, part), (1, part ^ 2)):
             picked = [
                 jnp.where(core == half, scales[2 * which:2 * which + 1, where], scales[2 * which + 1:2 * which + 2, where])
                 for where in at
             ]
-            sides.append(((unit * jnp.concatenate(picked, axis=1)).astype(jnp.bfloat16), exp_ref))
-    cols = out_ref.shape[1]
+            scaled = (unit * jnp.concatenate(picked, axis=1)).astype(jnp.bfloat16)
+            feats[(2 * lies + which) * rows:(2 * lies + which + 1) * rows, :] = scaled.T
+    chunks, _, step = buf.shape
+    stores = []
+    for i in range(chunks):
+        at = slice(i * step, (i + 1) * step)
+        grad = jnp.dot(exp_ref[at, :], feats[...], preferred_element_type=jnp.float32).T
+        unit = weight_unit[:, at]
+        proj = unit * jnp.sum(unit * grad, axis=0, keepdims=True)
+        buf[i] = (grad - proj) * weight_scale[:, at]
+        stores.append(pltpu.make_async_copy(buf.at[i], out_hbm.at[:, at], sems.at[i]))
+        stores[i].start()
+    for store in stores:
+        store.wait()
+
+
+def gradient(here_total, there_total, peak, weight_unit, weight_scale, units, exps):
+    cols, all_rows = exps.shape
+    bot, rows = units[0].shape
     step = min(512, cols)
-    for at in range(0, cols, step):
-        grad = sum(
-            lax.dot_general(
-                exp_ref[at:at + step, :], feats, (((1,), (1,)), ((), ())), preferred_element_type=jnp.float32
-            )
-            for feats, exp_ref in sides
-        )
-        grad = grad.T
-        unit = weight_unit[:, at:at + step]
-        proj = unit * jnp.sum(unit * grad, axis=0, keepdims=True)
-        out_ref[:, at:at + step] = (grad - proj) * weight_scale[:, at:at + step]
-
-
-def gradient(here_total, there_total, peak, weight_unit, weight_scale, units, exps, expt):
-    cols, rows = exps[0].shape
-    bot = units[0].shape[0]
+    args = (here_total, there_total, peak, weight_unit, weight_scale, *units, exps)
     return call(
         grad_kernel,
         "gradient",
-        shape(bot, cols),
-        (here_total, there_total, peak, weight_unit, weight_scale, *units, *exps, *expt),
-        scratch_shapes=[held(4, 2 * rows)],
+        pltpu.HBM((bot, cols), jnp.float32),
+        args,
+        out_specs=IN_HBM,
+        scratch_shapes=[
+            held(4, 2 * rows),
+            held(all_rows, bot, dtype=jnp.bfloat16),
+            held(cols // step, bot, step),
+            pltpu.SemaphoreType.DMA((cols // step,)),
+        ],
     )
 
 
@@ -388,23 +400,24 @@
     weights = (ws, wt, peak)
     own_cols = ws.shape[0]
     if n_fsdp <= DIRECT:
+        other = [swap(mine, "dp")]
         along = [swap(mine, "fsdp", k) for k in range(1, n_fsdp)]
-        other = swap(mine, "dp")
-        (rest,) = join(along, [n_fsdp - 1], (other, peak))
-        teacher_new, done = update_rest(teacher_weight, student_weight, rest, new, own_cols)
-        (own,) = join([mine, *along], [n_fsdp], (done,))
-        parts = [scores(own, *weights), scores(swap(own, "proto"), *weights)]
-        (other,) = join([other, swap(rest, "dp")], [n_fsdp], [part[3] for part in parts])
+        other.append(swap(other[0], "fsdp"))
+        own, far = join([mine, *along], [n_fsdp, n_fsdp - 2], (other[1], peak))
+        exps, unit_a, total_a = scores(0, own, weights)
+        teacher_new, done = update_rest(teacher_weight, student_weight, total_a, new, own_cols)
+        (other,) = join([*other, swap(far, "dp")], [n_fsdp], (done,))
     else:
         own = lax.all_to_all(jnp.broadcast_to(mine[None], (n_fsdp, *mine.shape)), "fsdp", 0, 0, tiled=True)
         other = swap(own, "dp")
         teacher_new, _ = update_rest(teacher_weight, student_weight, own, new, own_cols)
-        parts = [scores(own, *weights), scores(swap(own, "proto"), *weights)]
-    parts.append(scores(other, *weights))
-    parts.append(scores(swap(other, "proto"), *weights, last=[part[3] for part in parts]))
-    exps, expt, units, totals = zip(*parts)
-    total = add_up(add_up(totals[3], "proto"), "fsdp")
-    student_grad = gradient(total, swap(total, "dp"), peak, unit, scale, units, exps, expt)
+        exps, unit_a, total_a = scores(0, own, weights)
+    exps, unit_c, total_c = scores(2, other, weights, exps=exps)
+    exps, unit_b, total_b = scores(1, swap(own, "proto"), weights, exps=exps)
+    exps, unit_d, totals = scores(3, swap(other, "proto"), weights, (total_a, total_b, total_c), exps)
+    total = add_up(add_up(totals, "proto"), "fsdp")
+    units = (unit_a, unit_b, unit_c, unit_d)
+    student_grad = gradient(total, swap(total, "dp"), peak, unit, scale, units, exps)
     return (teacher_new, student_grad)
 
 

time: 56.2 us -> 52.1 us (0.927)
  waiting for transfers between devices: 18.6 us -> 13.1 us
  starting transfers between devices: 17.2 us -> 18.7 us
    ppermute x15 -> x16, waiting for transfers between devices: 18.6 us -> 13.1 us  [swap(): lax.ppermute(block, axis, [(i, i ^ apart) for i in range(lax.axis_size(ax...]
    ppermute x15 -> x16, starting transfers between devices: 17.2 us -> 18.7 us  [swap(): lax.ppermute(block, axis, [(i, i ^ apart) for i in range(lax.axis_size(ax...]
    pallas_call x14 -> x13, Pallas kernels: 19.5 us -> 19.4 us  [call(): pl.pallas_call(kernel, out_shape=out_shape, compiler_params=pltpu.Compile...]
  transfers between devices with their start and end apart: 15 -> 16, of which waited for: 9 -> 9; matrix products, arithmetic and copies ran while one was open for 0% -> 0% of each run, Pallas kernels for 16% -> 22%
where the time goes in v7:
time: 52.1 us; the launch traced here: 51.9 us
  Pallas kernels  19.4 us (37%)
  starting transfers between devices  18.7 us (36%)
  waiting for transfers between devices  13.1 us (25%)
  between operations  0.74 us (1%)
    pallas_call x13, Pallas kernels, call(): pl.pallas_call(kernel, out_shape=out_shape, compiler_params=pltpu.Compile...  19.4 us
    ppermute x16, starting transfers between devices, swap(): lax.ppermute(block, axis, [(i, i ^ apart) for i in range(lax.axis_size(ax...  18.7 us
    ppermute x16, waiting for transfers between devices, swap(): lax.ppermute(block, axis, [(i, i ^ apart) for i in range(lax.axis_size(ax...  13.1 us
  transfers between devices with their start and end apart: 16, of which 9 were waited for; matrix products, arithmetic and copies ran while one was open for 0% of the time, Pallas kernels for 22%

profile of v7, /device:TPU:0, one launch (start us, length us, event | category | flops | bytes accessed | tf_op | source)
XLA Modules:
  0.0 51.9 jit_solution(1409503761327273892)
XLA Ops:
  0.6 3.0 %collective-permute-start = (s32[1,256]{1,0:T(1,128)}, s32[1,256]{1,0:T(1,128)S(1)}, u32[]{:S(2)}, u32[]{:S(2)}) collective-permute-start(s32[1,256]{1,0:T(1,128)} %param.10), channel_id=1, source_target_pairs={{0,1},{1,0},{2,3},{3,2},{4,5},{5,4},{6,7},{7,6},{8,9},{9,8},{10,11... | collective-permute-start | bytes 3080 | tf_op jit(solution)/shard_map/ppermute | solution.py:46
  3.6 0.9 %fetch.1 = (bf16[192,128]{1,0:T(8,128)(2,1)S(1)}, bf16[192,256]{1,0:T(8,128)(2,1)S(1)}) custom-call(bf16[192,256]{1,0:T(8,128)(2,1)} %bitcast.7, bf16[192,256]{1,0:T(8,128)(2,1)} %bitcast.8), custom_call_target="tpu_custom_call" | custom-call | flops 1 | bytes 1 | tf_op jit(solution)/shard_map/fetch/pallas_call | solution.py:35
  4.6 0.8 %collective-permute-done.index_ref = s32[1,256]{1,0:T(1,128)S(1)} collective-permute-done((s32[1,256]{1,0:T(1,128)}, s32[1,256]{1,0:T(1,128)S(1)}, u32[]{:S(2)}, u32[]{:S(2)}) %collective-permute-start) | collective-permute-done | bytes 1056 | tf_op jit(solution)/shard_map/ppermute | solution.py:46
  5.6 2.1 %collective-permute-start.4 = (bf16[2,192,128]{2,1,0:T(8,128)(2,1)S(1)}, bf16[2,192,128]{2,1,0:T(8,128)(2,1)S(1)}, u32[]{:S(2)}, u32[]{:S(2)}) collective-permute-start(bf16[2,192,128]{2,1,0:T(8,128)(2,1)S(1)} %pack.1.refs_0_), channel_id=1, source_target_pairs={{0,1},{1,0},{2,3},{3,2},{4,5},{5,4},{6,7},{7,6},{8,9},{9,8},{10,11... | collective-permute-start | bytes 294920 | tf_op jit(solution)/shard_map/ppermute | solution.py:46
  7.7 3.6 %collective-permute-start.3 = (bf16[2,192,128]{2,1,0:T(8,128)(2,1)S(1)}, bf16[2,192,128]{2,1,0:T(8,128)(2,1)S(1)}, u32[]{:S(2)}, u32[]{:S(2)}) collective-permute-start(bf16[2,192,128]{2,1,0:T(8,128)(2,1)S(1)} %pack.1.refs_0_), channel_id=1, source_target_pairs={{0,24},{8,16},{16,8},{24,0},{1,25},{9,17},{17,9},{25,1},{2,26},{10... | collective-permute-start | bytes 294920 | tf_op jit(solution)/shard_map/ppermute | solution.py:46
  12.0 1.2 %collective-permute-start.5 = (bf16[2,192,128]{2,1,0:T(8,128)(2,1)S(1)}, bf16[2,192,128]{2,1,0:T(8,128)(2,1)S(1)}, u32[]{:S(2)}, u32[]{:S(2)}) collective-permute-start(bf16[2,192,128]{2,1,0:T(8,128)(2,1)S(1)} %collective-permute-done.4.refs_0_), channel_id=1, source_target_pairs={{0,8},{8,0},{16,24},{24,16},{1,9},{9,1},{17,25},{25,17},{2,10},{10... | collective-permute-start | bytes 294920 | tf_op jit(solution)/shard_map/ppermute | solution.py:46
  13.3 3.6 %prep.1 = (f32[192,4096]{1,0:T(8,128)}, bf16[2048,256]{1,0:T(8,128)(2,1)S(1)}, bf16[2048,256]{1,0:T(8,128)(2,1)S(1)}, f32[192,2048]{1,0:T(8,128)S(1)}, f32[1,2048]{1,0:T(1,128)S(1)}, /*index=5*/f32[1,128]{1,0:T(1,128)S(1)}) custom-call(f32[192,4096]{1,0:T(8,128)} %teacher_hbm.3, f32[192,4096]{1,0:T(8,128)} %student_hbm.3, f32[1,16384]{1,0:T(1,128)} %bitcast.9), custom_call_target="tpu_custom_call" | custom-call | flops 1 | bytes 1 | tf_op jit(solution)/shard_map/prep/pallas_call | solution.py:35
  16.9 1.4 %collective-permute-done.2.refs_2_ = bf16[2,192,128]{2,1,0:T(8,128)(2,1)S(1)} collective-permute-done((bf16[2,192,128]{2,1,0:T(8,128)(2,1)S(1)}, bf16[2,192,128]{2,1,0:T(8,128)(2,1)S(1)}, u32[]{:S(2)}, u32[]{:S(2)}) %collective-permute-start.2) | collective-permute-done | bytes 98336 | tf_op jit(solution)/shard_map/ppermute | solution.py:46
  18.3 1.1 %collective-permute-done.5.refs_4_.refs_1_ = bf16[2,192,128]{2,1,0:T(8,128)(2,1)S(1)} collective-permute-done((bf16[2,192,128]{2,1,0:T(8,128)(2,1)S(1)}, bf16[2,192,128]{2,1,0:T(8,128)(2,1)S(1)}, u32[]{:S(2)}, u32[]{:S(2)}) %collective-permute-start.5) | collective-permute-done | bytes 98336 | tf_op jit(solution)/shard_map/ppermute | solution.py:46
  20.0 1.4 %scores.4 = (bf16[2048,4096]{1,0:T(8,128)(2,1)S(1)}, bf16[192,512]{1,0:T(8,128)(2,1)S(1)}, f32[2,512]{1,0:T(2,128)S(1)}) custom-call(bf16[4,2,192,128]{3,2,1,0:T(8,128)(2,1)S(1)} %get-tuple-element.29.refs_0_, bf16[2048,256]{1,0:T(8,128)(2,1)S(1)} %get-tuple-element.30.refs_1_.refs_4_, bf16[2048,256]{1,0:T(8,128)(2,1)S(1)} %get-tuple-element.31.refs_2_.refs_5_, ...), custom_call_target="tpu_custom_call" | custom-call | flops 1 | bytes 1 | tf_op jit(solution)/shard_map/scores/pallas_call | solution.py:35
  21.5 2.8 %rest.1 = (f32[192,4096]{1,0:T(8,128)}, f32[8,128]{1,0:T(8,128)S(1)}) custom-call(f32[192,4096]{1,0:T(8,128)} %teacher_hbm.3, f32[192,4096]{1,0:T(8,128)} %student_hbm.3, f32[2,512]{1,0:T(2,128)S(1)} %get-tuple-element.32.after.refs_0_, f32[192,4096]{1,0:T(8,128)} %get-tuple-element.33.before_hbm), custom_call_target="tpu_custom_call", output_to_operand_aliasing={{0}: (3, {})} | custom-call | flops 1 | bytes 1 | tf_op jit(solution)/shard_map/rest/pallas_call | solution.py:35
  24.2 0.9 %collective-permute-done.7.refs_2_ = bf16[2,2,192,128]{3,2,1,0:T(8,128)(2,1)S(1)} collective-permute-done((bf16[2,2,192,128]{3,2,1,0:T(8,128)(2,1)S(1)}, bf16[2,2,192,128]{3,2,1,0:T(8,128)(2,1)S(1)}, u32[]{:S(2)}, u32[]{:S(2)}) %collective-permute-start.7) | collective-permute-done | bytes 196640 | tf_op jit(solution)/shard_map/ppermute | solution.py:46
  25.3 1.4 %scores.5 = (bf16[2048,4096]{1,0:T(8,128)(2,1)S(1)}, bf16[192,512]{1,0:T(8,128)(2,1)S(1)}, f32[2,512]{1,0:T(2,128)S(1)}) custom-call(bf16[4,2,192,128]{3,2,1,0:T(8,128)(2,1)S(1)} %join.3.refs_0_, bf16[2048,256]{1,0:T(8,128)(2,1)S(1)} %get-tuple-element.30.refs_1_.refs_4_, ...), custom_call_target="tpu_custom_call", output_to_operand_aliasing={{0}: (4, {})} | custom-call | flops 1 | bytes 1 | tf_op jit(solution)/shard_map/scores/pallas_call | solution.py:35
  26.7 1.4 %scores.6 = (bf16[2048,4096]{1,0:T(8,128)(2,1)S(1)}, bf16[192,512]{1,0:T(8,128)(2,1)S(1)}, f32[2,512]{1,0:T(2,128)S(1)}) custom-call(bf16[4,2,192,128]{3,2,1,0:T(8,128)(2,1)S(1)} %collective-permute-done.6.refs_0_, bf16[2048,256]{1,0:T(8,128)(2,1)S(1)} %get-tuple-element.30.refs_1_.refs_4_, ...), custom_call_target="tpu_custom_call", output_to_operand_aliasing={{0}: (4, {})} | custom-call | flops 1 | bytes 1 | tf_op jit(solution)/shard_map/scores/pallas_call | solution.py:35
  28.2 1.5 %scores.7 = (bf16[2048,4096]{1,0:T(8,128)(2,1)S(1)}, bf16[192,512]{1,0:T(8,128)(2,1)S(1)}, f32[4,1024]{1,0:T(4,128)S(1)}) custom-call(f32[2,512]{1,0:T(2,128)S(1)} %get-tuple-element.32.after.refs_0_, f32[2,512]{1,0:T(2,128)S(1)} %get-tuple-element.39.refs_1_, f32[2,512]{1,0:T(2,128)S(1)} %get-tuple-element.40.refs_2_, ...), custom_call_target="tpu_custom_call", output_to_operand_aliasing={{0}: (7, {})} | custom-call | flops 1 | bytes 1 | tf_op jit(solution)/shard_map/scores/pallas_call | solution.py:35
  29.7 1.7 %collective-permute-start.11 = (f32[4,1024]{1,0:T(4,128)S(1)}, f32[4,1024]{1,0:T(4,128)S(1)}, u32[]{:S(2)}, u32[]{:S(2)}) collective-permute-start(f32[4,1024]{1,0:T(4,128)S(1)} %get-tuple-element.42.refs_0_), channel_id=1, source_target_pairs={{0,6},{2,4},{4,2},{6,0},{1,7},{3,5},{5,3},{7,1},{8,14},{10,12},{12... | collective-permute-start | bytes 49160 | tf_op jit(solution)/shard_map/ppermute | solution.py:46
  31.9 1.0 %collective-permute-done.11.refs_3_ = f32[4,1024]{1,0:T(4,128)S(1)} collective-permute-done((f32[4,1024]{1,0:T(4,128)S(1)}, f32[4,1024]{1,0:T(4,128)S(1)}, u32[]{:S(2)}, u32[]{:S(2)}) %collective-permute-start.11) | collective-permute-done | bytes 16416 | tf_op jit(solution)/shard_map/ppermute | solution.py:46
  32.9 2.2 %collective-permute-done.10.refs_2_ = f32[4,1024]{1,0:T(4,128)S(1)} collective-permute-done((f32[4,1024]{1,0:T(4,128)S(1)}, f32[4,1024]{1,0:T(4,128)S(1)}, u32[]{:S(2)}, u32[]{:S(2)}) %collective-permute-start.10) | collective-permute-done | bytes 16416 | tf_op jit(solution)/shard_map/ppermute | solution.py:46
  35.1 2.3 %collective-permute-start.14 = (f32[4,1024]{1,0:T(4,128)S(1)}, f32[4,1024]{1,0:T(4,128)S(1)}, u32[]{:S(2)}, u32[]{:S(2)}) collective-permute-start(f32[4,1024]{1,0:T(4,128)S(1)} %relay.2.refs_0_), channel_id=1, source_target_pairs={{0,24},{8,16},{16,8},{24,0},{1,25},{9,17},{17,9},{25,1},{2,26},{10... | collective-permute-start | bytes 49160 | tf_op jit(solution)/shard_map/ppermute | solution.py:46
  38.0 1.6 %collective-permute-start.12 = (f32[4,1024]{1,0:T(4,128)S(1)}, f32[4,1024]{1,0:T(4,128)S(1)}, u32[]{:S(2)}, u32[]{:S(2)}) collective-permute-start(f32[4,1024]{1,0:T(4,128)S(1)} %relay.2.refs_0_), channel_id=1, source_target_pairs={{0,8},{8,0},{16,24},{24,16},{1,9},{9,1},{17,25},{25,17},{2,10},{10... | collective-permute-start | bytes 49160 | tf_op jit(solution)/shard_map/ppermute | solution.py:46
  39.6 1.2 %collective-permute-done.14.refs_3_ = f32[4,1024]{1,0:T(4,128)S(1)} collective-permute-done((f32[4,1024]{1,0:T(4,128)S(1)}, f32[4,1024]{1,0:T(4,128)S(1)}, u32[]{:S(2)}, u32[]{:S(2)}) %collective-permute-start.14) | collective-permute-done | bytes 16416 | tf_op jit(solution)/shard_map/ppermute | solution.py:46
  40.7 1.4 %collective-permute-done.13.refs_2_ = f32[4,1024]{1,0:T(4,128)S(1)} collective-permute-done((f32[4,1024]{1,0:T(4,128)S(1)}, f32[4,1024]{1,0:T(4,128)S(1)}, u32[]{:S(2)}, u32[]{:S(2)}) %collective-permute-start.13) | collective-permute-done | bytes 16416 | tf_op jit(solution)/shard_map/ppermute | solution.py:46
  42.8 3.1 %collective-permute-done.15.there_ref = f32[4,1024]{1,0:T(4,128)S(1)} collective-permute-done((f32[4,1024]{1,0:T(4,128)S(1)}, f32[4,1024]{1,0:T(4,128)S(1)}, u32[]{:S(2)}, u32[]{:S(2)}) %collective-permute-start.15) | collective-permute-done | bytes 16416 | tf_op jit(solution)/shard_map/ppermute | solution.py:46
  45.9 6.0 %gradient.1 = f32[192,2048]{1,0:T(8,128)} custom-call(f32[4,1024]{1,0:T(4,128)S(1)} %relay.3.here_ref, f32[4,1024]{1,0:T(4,128)S(1)} %collective-permute-done.15.there_ref, f32[1,128]{1,0:T(1,128)S(1)} %get-tuple-element.28.refs_5_.refs_3_.refs_6_.peak_ref, f32[192,2048]{1,0:T(8,128)S(1)} %get-tuple-element.43.weight_unit, ...), custom_call_target="tpu_custom_call" | custom-call | flops 1 | bytes 1 | tf_op jit(solution)/shard_map/gradient/pallas_call | solution.py:35
  (21 shorter events, 3.6 us)
Async XLA Ops:
  0.6 4.8 %collective-permute-start = (s32[1,256]{1,0:T(1,128)}, s32[1,256]{1,0:T(1,128)S(1)}, u32[]{:S(2)}, u32[]{:S(2)}) collective-permute-start(s32[1,256]{1,0:T(1,128)} %param.10), channel_id=1, source_target_pairs={{0,1},{1,0},{2,3},{3,2},{4,5},{5,4},{6,7},{7,6},{8,9},{9,8},{10,11... | collective-permute-start | bytes 3080 | tf_op jit(solution)/shard_map/ppermute | solution.py:46
  5.6 6.5 %collective-permute-start.4 = (bf16[2,192,128]{2,1,0:T(8,128)(2,1)S(1)}, bf16[2,192,128]{2,1,0:T(8,128)(2,1)S(1)}, u32[]{:S(2)}, u32[]{:S(2)}) collective-permute-start(bf16[2,192,128]{2,1,0:T(8,128)(2,1)S(1)} %pack.1.refs_0_), channel_id=1, source_target_pairs={{0,1},{1,0},{2,3},{3,2},{4,5},{5,4},{6,7},{7,6},{8,9},{9,8},{10,11... | collective-permute-start | bytes 294920 | tf_op jit(solution)/shard_map/ppermute | solution.py:46
  7.7 9.2 %collective-permute-start.3 = (bf16[2,192,128]{2,1,0:T(8,128)(2,1)S(1)}, bf16[2,192,128]{2,1,0:T(8,128)(2,1)S(1)}, u32[]{:S(2)}, u32[]{:S(2)}) collective-permute-start(bf16[2,192,128]{2,1,0:T(8,128)(2,1)S(1)} %pack.1.refs_0_), channel_id=1, source_target_pairs={{0,24},{8,16},{16,8},{24,0},{1,25},{9,17},{17,9},{25,1},{2,26},{10... | collective-permute-start | bytes 294920 | tf_op jit(solution)/shard_map/ppermute | solution.py:46
  11.2 7.0 %collective-permute-start.2 = (bf16[2,192,128]{2,1,0:T(8,128)(2,1)S(1)}, bf16[2,192,128]{2,1,0:T(8,128)(2,1)S(1)}, u32[]{:S(2)}, u32[]{:S(2)}) collective-permute-start(bf16[2,192,128]{2,1,0:T(8,128)(2,1)S(1)} %pack.1.refs_0_), channel_id=1, source_target_pairs={{0,16},{8,24},{16,0},{24,8},{1,17},{9,25},{17,1},{25,9},{2,18},{10... | collective-permute-start | bytes 294920 | tf_op jit(solution)/shard_map/ppermute | solution.py:46
  11.3 7.0 %collective-permute-start.1 = (bf16[2,192,128]{2,1,0:T(8,128)(2,1)S(1)}, bf16[2,192,128]{2,1,0:T(8,128)(2,1)S(1)}, u32[]{:S(2)}, u32[]{:S(2)}) collective-permute-start(bf16[2,192,128]{2,1,0:T(8,128)(2,1)S(1)} %pack.1.refs_0_), channel_id=1, source_target_pairs={{0,8},{8,0},{16,24},{24,16},{1,9},{9,1},{17,25},{25,17},{2,10},{10... | collective-permute-start | bytes 294920 | tf_op jit(solution)/shard_map/ppermute | solution.py:46
  12.0 7.3 %collective-permute-start.5 = (bf16[2,192,128]{2,1,0:T(8,128)(2,1)S(1)}, bf16[2,192,128]{2,1,0:T(8,128)(2,1)S(1)}, u32[]{:S(2)}, u32[]{:S(2)}) collective-permute-start(bf16[2,192,128]{2,1,0:T(8,128)(2,1)S(1)} %collective-permute-done.4.refs_0_), channel_id=1, source_target_pairs={{0,8},{8,0},{16,24},{24,16},{1,9},{9,1},{17,25},{25,17},{2,10},{10... | collective-permute-start | bytes 294920 | tf_op jit(solution)/shard_map/ppermute | solution.py:46
  19.4 5.7 %collective-permute-start.7 = (bf16[2,2,192,128]{3,2,1,0:T(8,128)(2,1)S(1)}, bf16[2,2,192,128]{3,2,1,0:T(8,128)(2,1)S(1)}, u32[]{:S(2)}, u32[]{:S(2)}) collective-permute-start(bf16[2,2,192,128]{3,2,1,0:T(8,128)(2,1)S(1)} %get-tuple-element.35), channel_id=1, source_target_pairs={{0,1},{1,0},{2,3},{3,2},{4,5},{5,4},{6,7},{7,6},{8,9},{9,8},{10,11... | collective-permute-start | bytes 589832 | tf_op jit(solution)/shard_map/ppermute | solution.py:46
  20.0 6.7 %collective-permute-start.6 = (bf16[4,2,192,128]{3,2,1,0:T(8,128)(2,1)S(1)}, bf16[4,2,192,128]{3,2,1,0:T(8,128)(2,1)S(1)}, u32[]{:S(2)}, u32[]{:S(2)}) collective-permute-start(bf16[4,2,192,128]{3,2,1,0:T(8,128)(2,1)S(1)} %get-tuple-element.29.refs_0_), channel_id=1, source_target_pairs={{0,2},{2,0},{4,6},{6,4},{1,3},{3,1},{5,7},{7,5},{8,10},{10,8},{12,... | collective-permute-start | bytes 1179656 | tf_op jit(solution)/shard_map/ppermute | solution.py:46
  25.2 3.0 %collective-permute-start.8 = (bf16[4,2,192,128]{3,2,1,0:T(8,128)(2,1)S(1)}, bf16[4,2,192,128]{3,2,1,0:T(8,128)(2,1)S(1)}, u32[]{:S(2)}, u32[]{:S(2)}) collective-permute-start(bf16[4,2,192,128]{3,2,1,0:T(8,128)(2,1)S(1)} %join.3.refs_0_), channel_id=1, source_target_pairs={{0,2},{2,0},{4,6},{6,4},{1,3},{3,1},{5,7},{7,5},{8,10},{10,8},{12,... | collective-permute-start | bytes 1179656 | tf_op jit(solution)/shard_map/ppermute | solution.py:46
  29.7 3.2 %collective-permute-start.11 = (f32[4,1024]{1,0:T(4,128)S(1)}, f32[4,1024]{1,0:T(4,128)S(1)}, u32[]{:S(2)}, u32[]{:S(2)}) collective-permute-start(f32[4,1024]{1,0:T(4,128)S(1)} %get-tuple-element.42.refs_0_), channel_id=1, source_target_pairs={{0,6},{2,4},{4,2},{6,0},{1,7},{3,5},{5,3},{7,1},{8,14},{10,12},{12... | collective-permute-start | bytes 49160 | tf_op jit(solution)/shard_map/ppermute | solution.py:46
  31.3 3.7 %collective-permute-start.10 = (f32[4,1024]{1,0:T(4,128)S(1)}, f32[4,1024]{1,0:T(4,128)S(1)}, u32[]{:S(2)}, u32[]{:S(2)}) collective-permute-start(f32[4,1024]{1,0:T(4,128)S(1)} %get-tuple-element.42.refs_0_), channel_id=1, source_target_pairs={{0,4},{2,6},{4,0},{6,2},{1,5},{3,7},{5,1},{7,3},{8,12},{10,14},{12... | collective-permute-start | bytes 49160 | tf_op jit(solution)/shard_map/ppermute | solution.py:46
  31.9 3.2 %collective-permute-start.9 = (f32[4,1024]{1,0:T(4,128)S(1)}, f32[4,1024]{1,0:T(4,128)S(1)}, u32[]{:S(2)}, u32[]{:S(2)}) collective-permute-start(f32[4,1024]{1,0:T(4,128)S(1)} %get-tuple-element.42.refs_0_), channel_id=1, source_target_pairs={{0,2},{2,0},{4,6},{6,4},{1,3},{3,1},{5,7},{7,5},{8,10},{10,8},{12,... | collective-permute-start | bytes 49160 | tf_op jit(solution)/shard_map/ppermute | solution.py:46
  35.1 5.6 %collective-permute-start.14 = (f32[4,1024]{1,0:T(4,128)S(1)}, f32[4,1024]{1,0:T(4,128)S(1)}, u32[]{:S(2)}, u32[]{:S(2)}) collective-permute-start(f32[4,1024]{1,0:T(4,128)S(1)} %relay.2.refs_0_), channel_id=1, source_target_pairs={{0,24},{8,16},{16,8},{24,0},{1,25},{9,17},{17,9},{25,1},{2,26},{10... | collective-permute-start | bytes 49160 | tf_op jit(solution)/shard_map/ppermute | solution.py:46
  37.5 4.6 %collective-permute-start.13 = (f32[4,1024]{1,0:T(4,128)S(1)}, f32[4,1024]{1,0:T(4,128)S(1)}, u32[]{:S(2)}, u32[]{:S(2)}) collective-permute-start(f32[4,1024]{1,0:T(4,128)S(1)} %relay.2.refs_0_), channel_id=1, source_target_pairs={{0,16},{8,24},{16,0},{24,8},{1,17},{9,25},{17,1},{25,9},{2,18},{10... | collective-permute-start | bytes 49160 | tf_op jit(solution)/shard_map/ppermute | solution.py:46
  38.0 4.1 %collective-permute-start.12 = (f32[4,1024]{1,0:T(4,128)S(1)}, f32[4,1024]{1,0:T(4,128)S(1)}, u32[]{:S(2)}, u32[]{:S(2)}) collective-permute-start(f32[4,1024]{1,0:T(4,128)S(1)} %relay.2.refs_0_), channel_id=1, source_target_pairs={{0,8},{8,0},{16,24},{24,16},{1,9},{9,1},{17,25},{25,17},{2,10},{10... | collective-permute-start | bytes 49160 | tf_op jit(solution)/shard_map/ppermute | solution.py:46
  42.1 3.8 %collective-permute-start.15 = (f32[4,1024]{1,0:T(4,128)S(1)}, f32[4,1024]{1,0:T(4,128)S(1)}, u32[]{:S(2)}, u32[]{:S(2)}) collective-permute-start(f32[4,1024]{1,0:T(4,128)S(1)} %relay.3.here_ref), channel_id=1, source_target_pairs={{0,1},{1,0},{2,3},{3,2},{4,5},{5,4},{6,7},{7,6},{8,9},{9,8},{10,11... | collective-permute-start | bytes 49160 | tf_op jit(solution)/shard_map/ppermute | solution.py:46

commit v8 on v7

--- a/solution.py
+++ b/solution.py
@@ -59,12 +59,14 @@
 def prep_kernel(n_dp, teacher_hbm, student_hbm, center_hbm, new_hbm, wt_ref, ws_ref, unit_ref, scale_ref, peak_ref, *scratch):
     teacher_buf, student_buf, new_buf, center_buf, in_t, in_s, out, in_c = scratch
     chunks, bot, width = new_buf.shape
+    own = chunks // n_dp
     dp, fsdp, _ = here()
-    first = dp * (chunks * width)
-    at = [slice(i * width, (i + 1) * width) for i in range(chunks)]
-    far = [pl.ds(pl.multiple_of(first + i * width, width), width) for i in range(chunks)]
-    start = pl.multiple_of((fsdp * n_dp + dp) * (chunks * width), 128)
-    center_load = pltpu.make_async_copy(center_hbm.at[:, pl.ds(start, chunks * width)], center_buf, in_c)
+    at = [slice(i * width, (i + 1) * width) for i in range(own)]
+    far = [
+        pl.ds(pl.multiple_of((lax.rem(dp + i // own, n_dp) * own + i % own) * width, width), width) for i in range(chunks)
+    ]
+    start = pl.multiple_of((fsdp * n_dp + dp) * (own * width), 128)
+    center_load = pltpu.make_async_copy(center_hbm.at[:, pl.ds(start, own * width)], center_buf, in_c)
     loads = [
         (
             pltpu.make_async_copy(teacher_hbm.at[:, far[i]], teacher_buf.at[i], in_t.at[i]),
@@ -91,6 +93,8 @@
         new = 0.994 * teacher_buf[i] + 0.006 * student
         new_buf[i] = new
         stores[i].start()
+        if i >= own:
+            continue
         high, mid, low = [part[:, at[i]] for part in splits]
         extra = jnp.where(row == 0, high, jnp.where(row == 1, mid, jnp.where(row == 2, low, zero)))
         scale = lax.rsqrt(jnp.sum(student * student, axis=0, keepdims=True) + EPS)
@@ -108,7 +112,7 @@
     bot, cols = teacher_weight.shape
     own = cols // n_dp
     width = min(512, own)
-    chunks = own // width
+    chunks = cols // width
     return call(
         functools.partial(prep_kernel, n_dp),
         "prep",
@@ -127,52 +131,6 @@
         + [held(1, own)]
         + [pltpu.SemaphoreType.DMA((chunks,))] * 3
         + [pltpu.SemaphoreType.DMA],
-    )
-
-
-def rest_kernel(teacher_hbm, student_hbm, after, before_hbm, new_hbm, done_ref, *scratch):
-    teacher_buf, student_buf, new_buf, in_t, in_s, out = scratch
-    chunks, bot, width = new_buf.shape
-    own = chunks * width
-    parts = teacher_hbm.shape[1] // own - 1
-    dp = here()[0]
-    done_ref[...] = jnp.zeros_like(done_ref)
-    for part in range(parts):
-        first = lax.rem(dp + 1 + part, parts + 1) * own
-        far = [pl.ds(pl.multiple_of(first + i * width, width), width) for i in range(chunks)]
-        loads = [
-            (
-                pltpu.make_async_copy(teacher_hbm.at[:, far[i]], teacher_buf.at[i], in_t.at[i]),
-                pltpu.make_async_copy(student_hbm.at[:, far[i]], student_buf.at[i], in_s.at[i]),
-            )
-            for i in range(chunks)
-        ]
-        stores = [pltpu.make_async_copy(new_buf.at[i], new_hbm.at[:, far[i]], out.at[i]) for i in range(chunks)]
-        for pair in loads:
-            for load in pair:
-                load.start()
-        for i in range(chunks):
-            for load in loads[i]:
-                load.wait()
-            new_buf[i] = 0.994 * teacher_buf[i] + 0.006 * student_buf[i]
-            stores[i].start()
-        for store in stores:
-            store.wait()
-
-
-def update_rest(teacher_weight, student_weight, after, new, own):
-    bot, cols = teacher_weight.shape
-    width = min(512, own)
-    chunks = own // width
-    return call(
-        rest_kernel,
-        "rest",
-        [pltpu.HBM((bot, cols), jnp.float32), held(8, 128)],
-        (teacher_weight, student_weight, after, new),
-        in_specs=[IN_HBM] * 4,
-        out_specs=[IN_HBM, ON_CHIP],
-        input_output_aliases={3: 0},
-        scratch_shapes=[held(chunks, bot, width)] * 3 + [pltpu.SemaphoreType.DMA((chunks,))] * 3,
     )
 
 
@@ -267,7 +225,7 @@
             unit = (values * lax.rsqrt(jnp.sum(values * values, axis=0, keepdims=True) + EPS)).astype(jnp.bfloat16)
             lanes = slice(group * per * width, (group + 1) * per * width)
             if which == 0:
-                unit_ref[:, lanes] = unit
+                unit_ref[lanes, :] = unit.T
             stationary = jnp.concatenate([unit, extra], axis=0)
             total = jnp.zeros((8, per * width), jnp.float32)
             for at in range(0, cols, step):
@@ -308,7 +266,7 @@
         "scores",
         [
             held(cols, 8 * rows, dtype=jnp.bfloat16),
-            held(bot, rows, dtype=jnp.bfloat16),
+            held(rows, bot, dtype=jnp.bfloat16),
             held(4, 2 * rows) if part == 3 else held(2, rows),
         ],
         args,
@@ -335,31 +293,38 @@
 
 
 def grad_kernel(here_ref, there_ref, peak_ref, weight_unit, weight_scale, *refs):
-    units, exp_ref, out_hbm, scales, feats, buf, sems = refs[:4], *refs[4:]
+    units, exp_ref, out_hbm, scales, buf, sems = refs[:4], *refs[4:]
     dp, _, core = here()
     total_s, log_t = combine([here_ref[...], there_ref[...]])
     scales[0:2, :] = 10.0 / total_s
-    scales[2:4, :] = -10.0 * jnp.exp2(GAIN_T * peak_ref[:, :1] - log_t)
-    bot, rows = units[0].shape
+    scales[2:4, :] = 10.0 * jnp.exp2(GAIN_T * peak_ref[:, :1] - log_t)
+    rows = units[0].shape[0]
     width = 128
     n = rows // width
+    factors = []
     for part in range(4):
         view, half = divmod(part, 2)
         base = (dp ^ view) * rows
         at = [pl.ds(pl.multiple_of(base + slot(k, n) * width, width), width) for k in range(n)]
-        unit = units[part][...].astype(jnp.float32)
-        for which, lies in ((0, part), (1, part ^ 2)):
+        for which in (0, 1):
             picked = [
                 jnp.where(core == half, scales[2 * which:2 * which + 1, where], scales[2 * which + 1:2 * which + 2, where])
                 for where in at
             ]
-            scaled = (unit * jnp.concatenate(picked, axis=1)).astype(jnp.bfloat16)
-            feats[(2 * lies + which) * rows:(2 * lies + which + 1) * rows, :] = scaled.T
+            factors.append(jnp.concatenate(picked, axis=1).astype(jnp.bfloat16))
+    feats = jnp.concatenate([unit[...] for unit in units], axis=0)
     chunks, _, step = buf.shape
     stores = []
     for i in range(chunks):
         at = slice(i * step, (i + 1) * step)
-        grad = jnp.dot(exp_ref[at, :], feats[...], preferred_element_type=jnp.float32).T
+        derivs = []
+        for part in range(4):
+            lies_s, lies_t = 2 * part * rows, (2 * (part ^ 2) + 1) * rows
+            probs_s = exp_ref[at, lies_s:lies_s + rows] * factors[2 * part]
+            probs_t = exp_ref[at, lies_t:lies_t + rows] * factors[2 * part + 1]
+            derivs.append(probs_s - probs_t)
+        derivs = jnp.concatenate(derivs, axis=1)
+        grad = jnp.dot(derivs, feats, preferred_element_type=jnp.float32).T
         unit = weight_unit[:, at]
         proj = unit * jnp.sum(unit * grad, axis=0, keepdims=True)
         buf[i] = (grad - proj) * weight_scale[:, at]
@@ -370,8 +335,8 @@
 
 
 def gradient(here_total, there_total, peak, weight_unit, weight_scale, units, exps):
-    cols, all_rows = exps.shape
-    bot, rows = units[0].shape
+    cols = exps.shape[0]
+    rows, bot = units[0].shape
     step = min(512, cols)
     args = (here_total, there_total, peak, weight_unit, weight_scale, *units, exps)
     return call(
@@ -380,12 +345,7 @@
         pltpu.HBM((bot, cols), jnp.float32),
         args,
         out_specs=IN_HBM,
-        scratch_shapes=[
-            held(4, 2 * rows),
-            held(all_rows, bot, dtype=jnp.bfloat16),
-            held(cols // step, bot, step),
-            pltpu.SemaphoreType.DMA((cols // step,)),
-        ],
+        scratch_shapes=[held(4, 2 * rows), held(cols // step, bot, step), pltpu.SemaphoreType.DMA((cols // step,))],
     )
 
 
@@ -396,21 +356,18 @@
 
     index = swap(pairing, "dp")
     mine = pack(*fetch(in_hbm(student_feats[0].T), in_hbm(teacher_feats[0].T)), index)
-    new, wt, ws, unit, scale, peak = prepare(teacher_weight, student_weight, center, n_dp)
+    teacher_new, wt, ws, unit, scale, peak = prepare(teacher_weight, student_weight, center, n_dp)
     weights = (ws, wt, peak)
-    own_cols = ws.shape[0]
     if n_fsdp <= DIRECT:
         other = [swap(mine, "dp")]
         along = [swap(mine, "fsdp", k) for k in range(1, n_fsdp)]
         other.append(swap(other[0], "fsdp"))
         own, far = join([mine, *along], [n_fsdp, n_fsdp - 2], (other[1], peak))
         exps, unit_a, total_a = scores(0, own, weights)
-        teacher_new, done = update_rest(teacher_weight, student_weight, total_a, new, own_cols)
-        (other,) = join([*other, swap(far, "dp")], [n_fsdp], (done,))
+        (other,) = join([*other, swap(far, "dp")], [n_fsdp], (total_a,))
     else:
         own = lax.all_to_all(jnp.broadcast_to(mine[None], (n_fsdp, *mine.shape)), "fsdp", 0, 0, tiled=True)
         other = swap(own, "dp")
-        teacher_new, _ = update_rest(teacher_weight, student_weight, own, new, own_cols)
         exps, unit_a, total_a = scores(0, own, weights)
     exps, unit_c, total_c = scores(2, other, weights, exps=exps)
     exps, unit_b, total_b = scores(1, swap(own, "proto"), weights, exps=exps)

time: 52.1 us -> 50 us (0.960)
  Pallas kernels: 19.4 us -> 16.2 us
  waiting for transfers between devices: 13.1 us -> 14.3 us
    pallas_call x13 -> x12, Pallas kernels: 19.4 us -> 16.2 us  [call(): pl.pallas_call(kernel, out_shape=out_shape, compiler_params=pltpu.Compile...]
    ppermute x16, waiting for transfers between devices: 13.1 us -> 14.3 us  [swap(): lax.ppermute(block, axis, [(i, i ^ apart) for i in range(lax.axis_size(ax...]
  transfers between devices with their start and end apart: 16 -> 16, of which waited for: 9 -> 8; matrix products, arithmetic and copies ran while one was open for 0% -> 0% of each run, Pallas kernels for 22% -> 21%
where the time goes in v8:
time: 50 us; the launch traced here: 49.9 us
  starting transfers between devices  18.7 us (37%)
  Pallas kernels  16.2 us (32%)
  waiting for transfers between devices  14.3 us (29%)
  between operations  0.75 us (2%)
    ppermute x16, starting transfers between devices, swap(): lax.ppermute(block, axis, [(i, i ^ apart) for i in range(lax.axis_size(ax...  18.7 us
    pallas_call x12, Pallas kernels, call(): pl.pallas_call(kernel, out_shape=out_shape, compiler_params=pltpu.Compile...  16.2 us
    ppermute x16, waiting for transfers between devices, swap(): lax.ppermute(block, axis, [(i, i ^ apart) for i in range(lax.axis_size(ax...  14.3 us
  transfers between devices with their start and end apart: 16, of which 8 were waited for; matrix products, arithmetic and copies ran while one was open for 0% of the time, Pallas kernels for 21%

profile of v8, /device:TPU:0, one launch (start us, length us, event | category | flops | bytes accessed | tf_op | source)
XLA Modules:
  0.0 49.9 jit_solution(7740780734436295600)
XLA Ops:
  0.6 3.0 %collective-permute-start = (s32[1,256]{1,0:T(1,128)}, s32[1,256]{1,0:T(1,128)S(1)}, u32[]{:S(2)}, u32[]{:S(2)}) collective-permute-start(s32[1,256]{1,0:T(1,128)} %param.10), channel_id=1, source_target_pairs={{0,1},{1,0},{2,3},{3,2},{4,5},{5,4},{6,7},{7,6},{8,9},{9,8},{10,11... | collective-permute-start | bytes 3080 | tf_op jit(solution)/shard_map/ppermute | solution.py:46
  3.6 0.9 %fetch.1 = (bf16[192,128]{1,0:T(8,128)(2,1)S(1)}, bf16[192,256]{1,0:T(8,128)(2,1)S(1)}) custom-call(bf16[192,256]{1,0:T(8,128)(2,1)} %bitcast.7, bf16[192,256]{1,0:T(8,128)(2,1)} %bitcast.8), custom_call_target="tpu_custom_call" | custom-call | flops 1 | bytes 1 | tf_op jit(solution)/shard_map/fetch/pallas_call | solution.py:35
  4.6 0.8 %collective-permute-done.index_ref = s32[1,256]{1,0:T(1,128)S(1)} collective-permute-done((s32[1,256]{1,0:T(1,128)}, s32[1,256]{1,0:T(1,128)S(1)}, u32[]{:S(2)}, u32[]{:S(2)}) %collective-permute-start) | collective-permute-done | bytes 1056 | tf_op jit(solution)/shard_map/ppermute | solution.py:46
  5.6 2.1 %collective-permute-start.4 = (bf16[2,192,128]{2,1,0:T(8,128)(2,1)S(1)}, bf16[2,192,128]{2,1,0:T(8,128)(2,1)S(1)}, u32[]{:S(2)}, u32[]{:S(2)}) collective-permute-start(bf16[2,192,128]{2,1,0:T(8,128)(2,1)S(1)} %pack.1.refs_0_), channel_id=1, source_target_pairs={{0,1},{1,0},{2,3},{3,2},{4,5},{5,4},{6,7},{7,6},{8,9},{9,8},{10,11... | collective-permute-start | bytes 294920 | tf_op jit(solution)/shard_map/ppermute | solution.py:46
  7.7 3.6 %collective-permute-start.3 = (bf16[2,192,128]{2,1,0:T(8,128)(2,1)S(1)}, bf16[2,192,128]{2,1,0:T(8,128)(2,1)S(1)}, u32[]{:S(2)}, u32[]{:S(2)}) collective-permute-start(bf16[2,192,128]{2,1,0:T(8,128)(2,1)S(1)} %pack.1.refs_0_), channel_id=1, source_target_pairs={{0,24},{8,16},{16,8},{24,0},{1,25},{9,17},{17,9},{25,1},{2,26},{10... | collective-permute-start | bytes 294920 | tf_op jit(solution)/shard_map/ppermute | solution.py:46
  11.3 0.8 %collective-permute-start.1 = (bf16[2,192,128]{2,1,0:T(8,128)(2,1)S(1)}, bf16[2,192,128]{2,1,0:T(8,128)(2,1)S(1)}, u32[]{:S(2)}, u32[]{:S(2)}) collective-permute-start(bf16[2,192,128]{2,1,0:T(8,128)(2,1)S(1)} %pack.1.refs_0_), channel_id=1, source_target_pairs={{0,8},{8,0},{16,24},{24,16},{1,9},{9,1},{17,25},{25,17},{2,10},{10... | collective-permute-start | bytes 294920 | tf_op jit(solution)/shard_map/ppermute | solution.py:46
  12.0 1.2 %collective-permute-start.5 = (bf16[2,192,128]{2,1,0:T(8,128)(2,1)S(1)}, bf16[2,192,128]{2,1,0:T(8,128)(2,1)S(1)}, u32[]{:S(2)}, u32[]{:S(2)}) collective-permute-start(bf16[2,192,128]{2,1,0:T(8,128)(2,1)S(1)} %collective-permute-done.4.refs_0_), channel_id=1, source_target_pairs={{0,8},{8,0},{16,24},{24,16},{1,9},{9,1},{17,25},{25,17},{2,10},{10... | collective-permute-start | bytes 294920 | tf_op jit(solution)/shard_map/ppermute | solution.py:46
  13.3 5.3 %prep.1 = (f32[192,4096]{1,0:T(8,128)}, bf16[2048,256]{1,0:T(8,128)(2,1)S(1)}, bf16[2048,256]{1,0:T(8,128)(2,1)S(1)}, f32[192,2048]{1,0:T(8,128)S(1)}, f32[1,2048]{1,0:T(1,128)S(1)}, /*index=5*/f32[1,128]{1,0:T(1,128)S(1)}) custom-call(f32[192,4096]{1,0:T(8,128)} %teacher_hbm.1, f32[192,4096]{1,0:T(8,128)} %student_hbm.1, f32[1,16384]{1,0:T(1,128)} %bitcast.9), custom_call_target="tpu_custom_call" | custom-call | flops 1 | bytes 1 | tf_op jit(solution)/shard_map/prep/pallas_call | solution.py:35
  18.6 0.7 %collective-permute-done.5.refs_4_.refs_1_ = bf16[2,192,128]{2,1,0:T(8,128)(2,1)S(1)} collective-permute-done((bf16[2,192,128]{2,1,0:T(8,128)(2,1)S(1)}, bf16[2,192,128]{2,1,0:T(8,128)(2,1)S(1)}, u32[]{:S(2)}, u32[]{:S(2)}) %collective-permute-start.5) | collective-permute-done | bytes 98336 | tf_op jit(solution)/shard_map/ppermute | solution.py:46
  20.0 1.5 %scores.4 = (bf16[2048,4096]{1,0:T(8,128)(2,1)S(1)}, bf16[512,192]{1,0:T(8,128)(2,1)S(1)}, f32[2,512]{1,0:T(2,128)S(1)}) custom-call(bf16[4,2,192,128]{3,2,1,0:T(8,128)(2,1)S(1)} %get-tuple-element.28.refs_0_, bf16[2048,256]{1,0:T(8,128)(2,1)S(1)} %get-tuple-element.29.refs_1_.refs_4_, bf16[2048,256]{1,0:T(8,128)(2,1)S(1)} %get-tuple-element.30.refs_2_.refs_5_, ...), custom_call_target="tpu_custom_call" | custom-call | flops 1 | bytes 1 | tf_op jit(solution)/shard_map/scores/pallas_call | solution.py:35
  21.5 3.7 %collective-permute-done.7.refs_2_ = bf16[2,2,192,128]{3,2,1,0:T(8,128)(2,1)S(1)} collective-permute-done((bf16[2,2,192,128]{3,2,1,0:T(8,128)(2,1)S(1)}, bf16[2,2,192,128]{3,2,1,0:T(8,128)(2,1)S(1)}, u32[]{:S(2)}, u32[]{:S(2)}) %collective-permute-start.7) | collective-permute-done | bytes 196640 | tf_op jit(solution)/shard_map/ppermute | solution.py:46
  25.3 1.5 %scores.5 = (bf16[2048,4096]{1,0:T(8,128)(2,1)S(1)}, bf16[512,192]{1,0:T(8,128)(2,1)S(1)}, f32[2,512]{1,0:T(2,128)S(1)}) custom-call(bf16[4,2,192,128]{3,2,1,0:T(8,128)(2,1)S(1)} %join.3.refs_0_, bf16[2048,256]{1,0:T(8,128)(2,1)S(1)} %get-tuple-element.29.refs_1_.refs_4_, ...), custom_call_target="tpu_custom_call", output_to_operand_aliasing={{0}: (4, {})} | custom-call | flops 1 | bytes 1 | tf_op jit(solution)/shard_map/scores/pallas_call | solution.py:35
  26.7 1.5 %scores.6 = (bf16[2048,4096]{1,0:T(8,128)(2,1)S(1)}, bf16[512,192]{1,0:T(8,128)(2,1)S(1)}, f32[2,512]{1,0:T(2,128)S(1)}) custom-call(bf16[4,2,192,128]{3,2,1,0:T(8,128)(2,1)S(1)} %collective-permute-done.6.refs_0_, bf16[2048,256]{1,0:T(8,128)(2,1)S(1)} %get-tuple-element.29.refs_1_.refs_4_, ...), custom_call_target="tpu_custom_call", output_to_operand_aliasing={{0}: (4, {})} | custom-call | flops 1 | bytes 1 | tf_op jit(solution)/shard_map/scores/pallas_call | solution.py:35
  28.2 1.5 %scores.7 = (bf16[2048,4096]{1,0:T(8,128)(2,1)S(1)}, bf16[512,192]{1,0:T(8,128)(2,1)S(1)}, f32[4,1024]{1,0:T(4,128)S(1)}) custom-call(f32[2,512]{1,0:T(2,128)S(1)} %get-tuple-element.31.refs_3_.refs_0_, f32[2,512]{1,0:T(2,128)S(1)} %get-tuple-element.35.refs_1_, f32[2,512]{1,0:T(2,128)S(1)} %get-tuple-element.36.refs_2_, ...), custom_call_target="tpu_custom_call", output_to_operand_aliasing={{0}: (7, {})} | custom-call | flops 1 | bytes 1 | tf_op jit(solution)/shard_map/scores/pallas_call | solution.py:35
  29.7 1.7 %collective-permute-start.11 = (f32[4,1024]{1,0:T(4,128)S(1)}, f32[4,1024]{1,0:T(4,128)S(1)}, u32[]{:S(2)}, u32[]{:S(2)}) collective-permute-start(f32[4,1024]{1,0:T(4,128)S(1)} %get-tuple-element.38.refs_0_), channel_id=1, source_target_pairs={{0,6},{2,4},{4,2},{6,0},{1,7},{3,5},{5,3},{7,1},{8,14},{10,12},{12... | collective-permute-start | bytes 49160 | tf_op jit(solution)/shard_map/ppermute | solution.py:46
  31.9 1.0 %collective-permute-done.11.refs_3_ = f32[4,1024]{1,0:T(4,128)S(1)} collective-permute-done((f32[4,1024]{1,0:T(4,128)S(1)}, f32[4,1024]{1,0:T(4,128)S(1)}, u32[]{:S(2)}, u32[]{:S(2)}) %collective-permute-start.11) | collective-permute-done | bytes 16416 | tf_op jit(solution)/shard_map/ppermute | solution.py:46
  32.9 2.2 %collective-permute-done.10.refs_2_ = f32[4,1024]{1,0:T(4,128)S(1)} collective-permute-done((f32[4,1024]{1,0:T(4,128)S(1)}, f32[4,1024]{1,0:T(4,128)S(1)}, u32[]{:S(2)}, u32[]{:S(2)}) %collective-permute-start.10) | collective-permute-done | bytes 16416 | tf_op jit(solution)/shard_map/ppermute | solution.py:46
  35.2 2.3 %collective-permute-start.14 = (f32[4,1024]{1,0:T(4,128)S(1)}, f32[4,1024]{1,0:T(4,128)S(1)}, u32[]{:S(2)}, u32[]{:S(2)}) collective-permute-start(f32[4,1024]{1,0:T(4,128)S(1)} %relay.2.refs_0_), channel_id=1, source_target_pairs={{0,24},{8,16},{16,8},{24,0},{1,25},{9,17},{17,9},{25,1},{2,26},{10... | collective-permute-start | bytes 49160 | tf_op jit(solution)/shard_map/ppermute | solution.py:46
  38.1 1.5 %collective-permute-start.12 = (f32[4,1024]{1,0:T(4,128)S(1)}, f32[4,1024]{1,0:T(4,128)S(1)}, u32[]{:S(2)}, u32[]{:S(2)}) collective-permute-start(f32[4,1024]{1,0:T(4,128)S(1)} %relay.2.refs_0_), channel_id=1, source_target_pairs={{0,8},{8,0},{16,24},{24,16},{1,9},{9,1},{17,25},{25,17},{2,10},{10... | collective-permute-start | bytes 49160 | tf_op jit(solution)/shard_map/ppermute | solution.py:46
  39.6 1.1 %collective-permute-done.14.refs_3_ = f32[4,1024]{1,0:T(4,128)S(1)} collective-permute-done((f32[4,1024]{1,0:T(4,128)S(1)}, f32[4,1024]{1,0:T(4,128)S(1)}, u32[]{:S(2)}, u32[]{:S(2)}) %collective-permute-start.14) | collective-permute-done | bytes 16416 | tf_op jit(solution)/shard_map/ppermute | solution.py:46
  40.8 1.5 %collective-permute-done.13.refs_2_ = f32[4,1024]{1,0:T(4,128)S(1)} collective-permute-done((f32[4,1024]{1,0:T(4,128)S(1)}, f32[4,1024]{1,0:T(4,128)S(1)}, u32[]{:S(2)}, u32[]{:S(2)}) %collective-permute-start.13) | collective-permute-done | bytes 16416 | tf_op jit(solution)/shard_map/ppermute | solution.py:46
  42.3 0.6 %collective-permute-start.15 = (f32[4,1024]{1,0:T(4,128)S(1)}, f32[4,1024]{1,0:T(4,128)S(1)}, u32[]{:S(2)}, u32[]{:S(2)}) collective-permute-start(f32[4,1024]{1,0:T(4,128)S(1)} %relay.3.here_ref), channel_id=1, source_target_pairs={{0,1},{1,0},{2,3},{3,2},{4,5},{5,4},{6,7},{7,6},{8,9},{9,8},{10,11... | collective-permute-start | bytes 49160 | tf_op jit(solution)/shard_map/ppermute | solution.py:46
  42.9 3.2 %collective-permute-done.15.there_ref = f32[4,1024]{1,0:T(4,128)S(1)} collective-permute-done((f32[4,1024]{1,0:T(4,128)S(1)}, f32[4,1024]{1,0:T(4,128)S(1)}, u32[]{:S(2)}, u32[]{:S(2)}) %collective-permute-start.15) | collective-permute-done | bytes 16416 | tf_op jit(solution)/shard_map/ppermute | solution.py:46
  46.1 3.7 %gradient.1 = f32[192,2048]{1,0:T(8,128)} custom-call(f32[4,1024]{1,0:T(4,128)S(1)} %relay.3.here_ref, f32[4,1024]{1,0:T(4,128)S(1)} %collective-permute-done.15.there_ref, f32[1,128]{1,0:T(1,128)S(1)} %get-tuple-element.27.refs_5_.refs_3_.refs_6_.peak_ref, f32[192,2048]{1,0:T(8,128)S(1)} %get-tuple-element.39.weight_unit, ...), custom_call_target="tpu_custom_call" | custom-call | flops 1 | bytes 1 | tf_op jit(solution)/shard_map/gradient/pallas_call | solution.py:35
  (20 shorter events, 2.1 us)
Async XLA Ops:
  0.6 4.8 %collective-permute-start = (s32[1,256]{1,0:T(1,128)}, s32[1,256]{1,0:T(1,128)S(1)}, u32[]{:S(2)}, u32[]{:S(2)}) collective-permute-start(s32[1,256]{1,0:T(1,128)} %param.10), channel_id=1, source_target_pairs={{0,1},{1,0},{2,3},{3,2},{4,5},{5,4},{6,7},{7,6},{8,9},{9,8},{10,11... | collective-permute-start | bytes 3080 | tf_op jit(solution)/shard_map/ppermute | solution.py:46
  5.6 6.5 %collective-permute-start.4 = (bf16[2,192,128]{2,1,0:T(8,128)(2,1)S(1)}, bf16[2,192,128]{2,1,0:T(8,128)(2,1)S(1)}, u32[]{:S(2)}, u32[]{:S(2)}) collective-permute-start(bf16[2,192,128]{2,1,0:T(8,128)(2,1)S(1)} %pack.1.refs_0_), channel_id=1, source_target_pairs={{0,1},{1,0},{2,3},{3,2},{4,5},{5,4},{6,7},{7,6},{8,9},{9,8},{10,11... | collective-permute-start | bytes 294920 | tf_op jit(solution)/shard_map/ppermute | solution.py:46
  7.7 11.0 %collective-permute-start.3 = (bf16[2,192,128]{2,1,0:T(8,128)(2,1)S(1)}, bf16[2,192,128]{2,1,0:T(8,128)(2,1)S(1)}, u32[]{:S(2)}, u32[]{:S(2)}) collective-permute-start(bf16[2,192,128]{2,1,0:T(8,128)(2,1)S(1)} %pack.1.refs_0_), channel_id=1, source_target_pairs={{0,24},{8,16},{16,8},{24,0},{1,25},{9,17},{17,9},{25,1},{2,26},{10... | collective-permute-start | bytes 294920 | tf_op jit(solution)/shard_map/ppermute | solution.py:46
  11.2 7.4 %collective-permute-start.2 = (bf16[2,192,128]{2,1,0:T(8,128)(2,1)S(1)}, bf16[2,192,128]{2,1,0:T(8,128)(2,1)S(1)}, u32[]{:S(2)}, u32[]{:S(2)}) collective-permute-start(bf16[2,192,128]{2,1,0:T(8,128)(2,1)S(1)} %pack.1.refs_0_), channel_id=1, source_target_pairs={{0,16},{8,24},{16,0},{24,8},{1,17},{9,25},{17,1},{25,9},{2,18},{10... | collective-permute-start | bytes 294920 | tf_op jit(solution)/shard_map/ppermute | solution.py:46
  11.3 7.4 %collective-permute-start.1 = (bf16[2,192,128]{2,1,0:T(8,128)(2,1)S(1)}, bf16[2,192,128]{2,1,0:T(8,128)(2,1)S(1)}, u32[]{:S(2)}, u32[]{:S(2)}) collective-permute-start(bf16[2,192,128]{2,1,0:T(8,128)(2,1)S(1)} %pack.1.refs_0_), channel_id=1, source_target_pairs={{0,8},{8,0},{16,24},{24,16},{1,9},{9,1},{17,25},{25,17},{2,10},{10... | collective-permute-start | bytes 294920 | tf_op jit(solution)/shard_map/ppermute | solution.py:46
  12.0 7.3 %collective-permute-start.5 = (bf16[2,192,128]{2,1,0:T(8,128)(2,1)S(1)}, bf16[2,192,128]{2,1,0:T(8,128)(2,1)S(1)}, u32[]{:S(2)}, u32[]{:S(2)}) collective-permute-start(bf16[2,192,128]{2,1,0:T(8,128)(2,1)S(1)} %collective-permute-done.4.refs_0_), channel_id=1, source_target_pairs={{0,8},{8,0},{16,24},{24,16},{1,9},{9,1},{17,25},{25,17},{2,10},{10... | collective-permute-start | bytes 294920 | tf_op jit(solution)/shard_map/ppermute | solution.py:46
  19.4 5.7 %collective-permute-start.7 = (bf16[2,2,192,128]{3,2,1,0:T(8,128)(2,1)S(1)}, bf16[2,2,192,128]{3,2,1,0:T(8,128)(2,1)S(1)}, u32[]{:S(2)}, u32[]{:S(2)}) collective-permute-start(bf16[2,2,192,128]{3,2,1,0:T(8,128)(2,1)S(1)} %get-tuple-element.32), channel_id=1, source_target_pairs={{0,1},{1,0},{2,3},{3,2},{4,5},{5,4},{6,7},{7,6},{8,9},{9,8},{10,11... | collective-permute-start | bytes 589832 | tf_op jit(solution)/shard_map/ppermute | solution.py:46
  20.0 6.7 %collective-permute-start.6 = (bf16[4,2,192,128]{3,2,1,0:T(8,128)(2,1)S(1)}, bf16[4,2,192,128]{3,2,1,0:T(8,128)(2,1)S(1)}, u32[]{:S(2)}, u32[]{:S(2)}) collective-permute-start(bf16[4,2,192,128]{3,2,1,0:T(8,128)(2,1)S(1)} %get-tuple-element.28.refs_0_), channel_id=1, source_target_pairs={{0,2},{2,0},{4,6},{6,4},{1,3},{3,1},{5,7},{7,5},{8,10},{10,8},{12,... | collective-permute-start | bytes 1179656 | tf_op jit(solution)/shard_map/ppermute | solution.py:46
  25.2 3.0 %collective-permute-start.8 = (bf16[4,2,192,128]{3,2,1,0:T(8,128)(2,1)S(1)}, bf16[4,2,192,128]{3,2,1,0:T(8,128)(2,1)S(1)}, u32[]{:S(2)}, u32[]{:S(2)}) collective-permute-start(bf16[4,2,192,128]{3,2,1,0:T(8,128)(2,1)S(1)} %join.3.refs_0_), channel_id=1, source_target_pairs={{0,2},{2,0},{4,6},{6,4},{1,3},{3,1},{5,7},{7,5},{8,10},{10,8},{12,... | collective-permute-start | bytes 1179656 | tf_op jit(solution)/shard_map/ppermute | solution.py:46
  29.7 3.2 %collective-permute-start.11 = (f32[4,1024]{1,0:T(4,128)S(1)}, f32[4,1024]{1,0:T(4,128)S(1)}, u32[]{:S(2)}, u32[]{:S(2)}) collective-permute-start(f32[4,1024]{1,0:T(4,128)S(1)} %get-tuple-element.38.refs_0_), channel_id=1, source_target_pairs={{0,6},{2,4},{4,2},{6,0},{1,7},{3,5},{5,3},{7,1},{8,14},{10,12},{12... | collective-permute-start | bytes 49160 | tf_op jit(solution)/shard_map/ppermute | solution.py:46
  31.4 3.7 %collective-permute-start.10 = (f32[4,1024]{1,0:T(4,128)S(1)}, f32[4,1024]{1,0:T(4,128)S(1)}, u32[]{:S(2)}, u32[]{:S(2)}) collective-permute-start(f32[4,1024]{1,0:T(4,128)S(1)} %get-tuple-element.38.refs_0_), channel_id=1, source_target_pairs={{0,4},{2,6},{4,0},{6,2},{1,5},{3,7},{5,1},{7,3},{8,12},{10,14},{12... | collective-permute-start | bytes 49160 | tf_op jit(solution)/shard_map/ppermute | solution.py:46
  31.9 3.2 %collective-permute-start.9 = (f32[4,1024]{1,0:T(4,128)S(1)}, f32[4,1024]{1,0:T(4,128)S(1)}, u32[]{:S(2)}, u32[]{:S(2)}) collective-permute-start(f32[4,1024]{1,0:T(4,128)S(1)} %get-tuple-element.38.refs_0_), channel_id=1, source_target_pairs={{0,2},{2,0},{4,6},{6,4},{1,3},{3,1},{5,7},{7,5},{8,10},{10,8},{12,... | collective-permute-start | bytes 49160 | tf_op jit(solution)/shard_map/ppermute | solution.py:46
  35.2 5.6 %collective-permute-start.14 = (f32[4,1024]{1,0:T(4,128)S(1)}, f32[4,1024]{1,0:T(4,128)S(1)}, u32[]{:S(2)}, u32[]{:S(2)}) collective-permute-start(f32[4,1024]{1,0:T(4,128)S(1)} %relay.2.refs_0_), channel_id=1, source_target_pairs={{0,24},{8,16},{16,8},{24,0},{1,25},{9,17},{17,9},{25,1},{2,26},{10... | collective-permute-start | bytes 49160 | tf_op jit(solution)/shard_map/ppermute | solution.py:46
  37.5 4.8 %collective-permute-start.13 = (f32[4,1024]{1,0:T(4,128)S(1)}, f32[4,1024]{1,0:T(4,128)S(1)}, u32[]{:S(2)}, u32[]{:S(2)}) collective-permute-start(f32[4,1024]{1,0:T(4,128)S(1)} %relay.2.refs_0_), channel_id=1, source_target_pairs={{0,16},{8,24},{16,0},{24,8},{1,17},{9,25},{17,1},{25,9},{2,18},{10... | collective-permute-start | bytes 49160 | tf_op jit(solution)/shard_map/ppermute | solution.py:46
  38.1 4.2 %collective-permute-start.12 = (f32[4,1024]{1,0:T(4,128)S(1)}, f32[4,1024]{1,0:T(4,128)S(1)}, u32[]{:S(2)}, u32[]{:S(2)}) collective-permute-start(f32[4,1024]{1,0:T(4,128)S(1)} %relay.2.refs_0_), channel_id=1, source_target_pairs={{0,8},{8,0},{16,24},{24,16},{1,9},{9,1},{17,25},{25,17},{2,10},{10... | collective-permute-start | bytes 49160 | tf_op jit(solution)/shard_map/ppermute | solution.py:46
  42.3 3.8 %collective-permute-start.15 = (f32[4,1024]{1,0:T(4,128)S(1)}, f32[4,1024]{1,0:T(4,128)S(1)}, u32[]{:S(2)}, u32[]{:S(2)}) collective-permute-start(f32[4,1024]{1,0:T(4,128)S(1)} %relay.3.here_ref), channel_id=1, source_target_pairs={{0,1},{1,0},{2,3},{3,2},{4,5},{5,4},{6,7},{7,6},{8,9},{9,8},{10,11... | collective-permute-start | bytes 49160 | tf_op jit(solution)/shard_map/ppermute | solution.py:46

commit v9 on v8

--- a/solution.py
+++ b/solution.py
@@ -285,18 +285,26 @@
 
 def add_up(total, axis):
     n = lax.axis_size(axis)
-    if n <= DIRECT:
-        parts = [total, *[swap(total, axis, k) for k in range(1, n)]]
+    if axis == "proto":
+        pairs = lambda k: [(i, i ^ k) for i in range(n) if (i ^ k) % 2]
+        parts = [total, *[lax.ppermute(total, axis, pairs(k)) for k in range(1, n)]]
+    elif n <= DIRECT:
+        n_proto = lax.axis_size("proto")
+        axes = ("fsdp", "proto") if axis == "fsdp" else ("proto", "dp")
+        place = (lambda i, p: i * n_proto + p) if axis == "fsdp" else (lambda i, p: p * n + i)
+        pairs = lambda k: [(place(i, p), place(i ^ k, p)) for p in range(1, n_proto, 2) for i in range(n)]
+        parts = [total, *[lax.ppermute(total, axes, pairs(k)) for k in range(1, n)]]
     else:
         parts = [lax.all_to_all(jnp.broadcast_to(total[None], (n, *total.shape)), axis, 0, 0, tiled=True)]
     return call(relay_kernel, "relay", held(*total.shape), parts)
 
 
-def grad_kernel(here_ref, there_ref, peak_ref, weight_unit, weight_scale, *refs):
+def grad_kernel(led_ref, given_ref, peak_ref, weight_unit, weight_scale, *refs):
     units, exp_ref, out_hbm, scales, buf, sems = refs[:4], *refs[4:]
     dp, _, core = here()
-    total_s, log_t = combine([here_ref[...], there_ref[...]])
-    scales[0:2, :] = 10.0 / total_s
+    total = jnp.where(core == 1, led_ref[...], given_ref[...])
+    scales[0:2, :] = 10.0 / total[:2]
+    log_t = total[2:]
     scales[2:4, :] = 10.0 * jnp.exp2(GAIN_T * peak_ref[:, :1] - log_t)
     rows = units[0].shape[0]
     width = 128
@@ -334,11 +342,11 @@
         store.wait()
 
 
-def gradient(here_total, there_total, peak, weight_unit, weight_scale, units, exps):
+def gradient(led, given, peak, weight_unit, weight_scale, units, exps):
     cols = exps.shape[0]
     rows, bot = units[0].shape
     step = min(512, cols)
-    args = (here_total, there_total, peak, weight_unit, weight_scale, *units, exps)
+    args = (led, given, peak, weight_unit, weight_scale, *units, exps)
     return call(
         grad_kernel,
         "gradient",
@@ -363,18 +371,19 @@
         along = [swap(mine, "fsdp", k) for k in range(1, n_fsdp)]
         other.append(swap(other[0], "fsdp"))
         own, far = join([mine, *along], [n_fsdp, n_fsdp - 2], (other[1], peak))
-        exps, unit_a, total_a = scores(0, own, weights)
-        (other,) = join([*other, swap(far, "dp")], [n_fsdp], (total_a,))
     else:
         own = lax.all_to_all(jnp.broadcast_to(mine[None], (n_fsdp, *mine.shape)), "fsdp", 0, 0, tiled=True)
         other = swap(own, "dp")
-        exps, unit_a, total_a = scores(0, own, weights)
+    exps, unit_a, total_a = scores(0, own, weights)
+    exps, unit_b, total_b = scores(1, swap(own, "proto"), weights, exps=exps)
+    if n_fsdp <= DIRECT:
+        (other,) = join([*other, swap(far, "dp")], [n_fsdp], (total_b,))
     exps, unit_c, total_c = scores(2, other, weights, exps=exps)
-    exps, unit_b, total_b = scores(1, swap(own, "proto"), weights, exps=exps)
-    exps, unit_d, totals = scores(3, swap(other, "proto"), weights, (total_a, total_b, total_c), exps)
-    total = add_up(add_up(totals, "proto"), "fsdp")
-    units = (unit_a, unit_b, unit_c, unit_d)
-    student_grad = gradient(total, swap(total, "dp"), peak, unit, scale, units, exps)
+    exps, unit_d, total = scores(3, swap(other, "proto"), weights, (total_a, total_b, total_c), exps)
+    for axis in ("proto", "fsdp", "dp"):
+        total = add_up(total, axis)
+    given = lax.ppermute(total, "proto", [(i, i ^ 1) for i in range(1, lax.axis_size("proto"), 2)])
+    student_grad = gradient(total, given, peak, unit, scale, (unit_a, unit_b, unit_c, unit_d), exps)
     return (teacher_new, student_grad)
 
 

time: 50 us -> 59.1 us (1.18)
  waiting for transfers between devices: 14.3 us -> 19.7 us
  starting transfers between devices: 18.7 us -> 22 us
    ppermute x0 -> x8, waiting for transfers between devices: none -> 14.2 us  [the longest x1 13.3 us: shards(): lax.ppermute(total, 'proto', [(i, i ^ 1) for i in range(1, lax.axis_size(...]
    ppermute x0 -> x8, starting transfers between devices: none -> 10.5 us  [the longest x3 6.61 us: add_up(): parts = [total, *[lax.ppermute(total, axis, pairs(k)) for k in range(1, n)]]]
    ppermute x16 -> x9, waiting for transfers between devices: 14.3 us -> 5.55 us  [swap(): lax.ppermute(block, axis, [(i, i ^ apart) for i in range(lax.axis_size(ax...]
    ppermute x16 -> x9, starting transfers between devices: 18.7 us -> 11.5 us  [swap(): lax.ppermute(block, axis, [(i, i ^ apart) for i in range(lax.axis_size(ax...]
    pallas_call x12 -> x13, Pallas kernels: 16.2 us -> 16.2 us  [call(): pl.pallas_call(kernel, out_shape=out_shape, compiler_params=pltpu.Compile...]
  transfers between devices with their start and end apart: 16 -> 17, of which waited for: 8 -> 6; matrix products, arithmetic and copies ran while one was open for 0% -> 0% of each run, Pallas kernels for 21% -> 18%
where the time goes in v9:
time: 59.1 us; the launch traced here: 58.8 us
  starting transfers between devices  22 us (37%)
  waiting for transfers between devices  19.7 us (33%)
  Pallas kernels  16.2 us (27%)
  between operations  0.86 us (1%)
    pallas_call x13, Pallas kernels, call(): pl.pallas_call(kernel, out_shape=out_shape, compiler_params=pltpu.Compile...  16.2 us
    ppermute x1, waiting for transfers between devices, shards(): lax.ppermute(total, 'proto', [(i, i ^ 1) for i in range(1, lax.axis_size(...  13.3 us
    ppermute x9, starting transfers between devices, swap(): lax.ppermute(block, axis, [(i, i ^ apart) for i in range(lax.axis_size(ax...  11.5 us
    ppermute x3, starting transfers between devices, add_up(): parts = [total, *[lax.ppermute(total, axis, pairs(k)) for k in range(1, n)]]  6.61 us
    ppermute x9, waiting for transfers between devices, swap(): lax.ppermute(block, axis, [(i, i ^ apart) for i in range(lax.axis_size(ax...  5.55 us
    ppermute x4, starting transfers between devices, add_up(): parts = [total, *[lax.ppermute(total, axes, pairs(k)) for k in range(1, n)]]  2.65 us
    ppermute x1, starting transfers between devices, shards(): lax.ppermute(total, 'proto', [(i, i ^ 1) for i in range(1, lax.axis_size(...  1.29 us
  transfers between devices with their start and end apart: 17, of which 6 were waited for; matrix products, arithmetic and copies ran while one was open for 0% of the time, Pallas kernels for 18%

profile of v9, /device:TPU:0, one launch (start us, length us, event | category | flops | bytes accessed | tf_op | source)
XLA Modules:
  0.0 58.8 jit_solution(115877664261783627)
XLA Ops:
  0.6 3.0 %collective-permute-start = (s32[1,256]{1,0:T(1,128)}, s32[1,256]{1,0:T(1,128)S(1)}, u32[]{:S(2)}, u32[]{:S(2)}) collective-permute-start(s32[1,256]{1,0:T(1,128)} %param.10), channel_id=1, source_target_pairs={{0,1},{1,0},{2,3},{3,2},{4,5},{5,4},{6,7},{7,6},{8,9},{9,8},{10,11... | collective-permute-start | bytes 3080 | tf_op jit(solution)/shard_map/ppermute | solution.py:46
  3.6 0.9 %fetch.1 = (bf16[192,128]{1,0:T(8,128)(2,1)S(1)}, bf16[192,256]{1,0:T(8,128)(2,1)S(1)}) custom-call(bf16[192,256]{1,0:T(8,128)(2,1)} %bitcast.7, bf16[192,256]{1,0:T(8,128)(2,1)} %bitcast.8), custom_call_target="tpu_custom_call" | custom-call | flops 1 | bytes 1 | tf_op jit(solution)/shard_map/fetch/pallas_call | solution.py:35
  4.6 0.8 %collective-permute-done.index_ref = s32[1,256]{1,0:T(1,128)S(1)} collective-permute-done((s32[1,256]{1,0:T(1,128)}, s32[1,256]{1,0:T(1,128)S(1)}, u32[]{:S(2)}, u32[]{:S(2)}) %collective-permute-start) | collective-permute-done | bytes 1056 | tf_op jit(solution)/shard_map/ppermute | solution.py:46
  5.6 2.1 %collective-permute-start.4 = (bf16[2,192,128]{2,1,0:T(8,128)(2,1)S(1)}, bf16[2,192,128]{2,1,0:T(8,128)(2,1)S(1)}, u32[]{:S(2)}, u32[]{:S(2)}) collective-permute-start(bf16[2,192,128]{2,1,0:T(8,128)(2,1)S(1)} %pack.1.refs_0_), channel_id=1, source_target_pairs={{0,1},{1,0},{2,3},{3,2},{4,5},{5,4},{6,7},{7,6},{8,9},{9,8},{10,11... | collective-permute-start | bytes 294920 | tf_op jit(solution)/shard_map/ppermute | solution.py:46
  7.7 3.6 %collective-permute-start.3 = (bf16[2,192,128]{2,1,0:T(8,128)(2,1)S(1)}, bf16[2,192,128]{2,1,0:T(8,128)(2,1)S(1)}, u32[]{:S(2)}, u32[]{:S(2)}) collective-permute-start(bf16[2,192,128]{2,1,0:T(8,128)(2,1)S(1)} %pack.1.refs_0_), channel_id=1, source_target_pairs={{0,24},{8,16},{16,8},{24,0},{1,25},{9,17},{17,9},{25,1},{2,26},{10... | collective-permute-start | bytes 294920 | tf_op jit(solution)/shard_map/ppermute | solution.py:46
  11.3 0.8 %collective-permute-start.1 = (bf16[2,192,128]{2,1,0:T(8,128)(2,1)S(1)}, bf16[2,192,128]{2,1,0:T(8,128)(2,1)S(1)}, u32[]{:S(2)}, u32[]{:S(2)}) collective-permute-start(bf16[2,192,128]{2,1,0:T(8,128)(2,1)S(1)} %pack.1.refs_0_), channel_id=1, source_target_pairs={{0,8},{8,0},{16,24},{24,16},{1,9},{9,1},{17,25},{25,17},{2,10},{10... | collective-permute-start | bytes 294920 | tf_op jit(solution)/shard_map/ppermute | solution.py:46
  12.0 1.2 %collective-permute-start.5 = (bf16[2,192,128]{2,1,0:T(8,128)(2,1)S(1)}, bf16[2,192,128]{2,1,0:T(8,128)(2,1)S(1)}, u32[]{:S(2)}, u32[]{:S(2)}) collective-permute-start(bf16[2,192,128]{2,1,0:T(8,128)(2,1)S(1)} %collective-permute-done.4.refs_0_), channel_id=1, source_target_pairs={{0,8},{8,0},{16,24},{24,16},{1,9},{9,1},{17,25},{25,17},{2,10},{10... | collective-permute-start | bytes 294920 | tf_op jit(solution)/shard_map/ppermute | solution.py:46
  13.3 5.3 %prep.1 = (f32[192,4096]{1,0:T(8,128)}, bf16[2048,256]{1,0:T(8,128)(2,1)S(1)}, bf16[2048,256]{1,0:T(8,128)(2,1)S(1)}, f32[192,2048]{1,0:T(8,128)S(1)}, f32[1,2048]{1,0:T(1,128)S(1)}, /*index=5*/f32[1,128]{1,0:T(1,128)S(1)}) custom-call(f32[192,4096]{1,0:T(8,128)} %teacher_hbm.1, f32[192,4096]{1,0:T(8,128)} %student_hbm.1, f32[1,16384]{1,0:T(1,128)} %bitcast.9), custom_call_target="tpu_custom_call" | custom-call | flops 1 | bytes 1 | tf_op jit(solution)/shard_map/prep/pallas_call | solution.py:35
  18.6 0.7 %collective-permute-done.5.refs_4_.refs_1_ = bf16[2,192,128]{2,1,0:T(8,128)(2,1)S(1)} collective-permute-done((bf16[2,192,128]{2,1,0:T(8,128)(2,1)S(1)}, bf16[2,192,128]{2,1,0:T(8,128)(2,1)S(1)}, u32[]{:S(2)}, u32[]{:S(2)}) %collective-permute-start.5) | collective-permute-done | bytes 98336 | tf_op jit(solution)/shard_map/ppermute | solution.py:46
  20.1 1.5 %scores.4 = (bf16[2048,4096]{1,0:T(8,128)(2,1)S(1)}, bf16[512,192]{1,0:T(8,128)(2,1)S(1)}, f32[2,512]{1,0:T(2,128)S(1)}) custom-call(bf16[4,2,192,128]{3,2,1,0:T(8,128)(2,1)S(1)} %get-tuple-element.28.refs_0_, bf16[2048,256]{1,0:T(8,128)(2,1)S(1)} %get-tuple-element.29.refs_1_.refs_4_, bf16[2048,256]{1,0:T(8,128)(2,1)S(1)} %get-tuple-element.30.refs_2_.refs_5_, ...), custom_call_target="tpu_custom_call" | custom-call | flops 1 | bytes 1 | tf_op jit(solution)/shard_map/scores/pallas_call | solution.py:35
  21.6 1.5 %scores.5 = (bf16[2048,4096]{1,0:T(8,128)(2,1)S(1)}, bf16[512,192]{1,0:T(8,128)(2,1)S(1)}, f32[2,512]{1,0:T(2,128)S(1)}) custom-call(bf16[4,2,192,128]{3,2,1,0:T(8,128)(2,1)S(1)} %collective-permute-done.6.refs_0_, bf16[2048,256]{1,0:T(8,128)(2,1)S(1)} %get-tuple-element.29.refs_1_.refs_4_, ...), custom_call_target="tpu_custom_call", output_to_operand_aliasing={{0}: (4, {})} | custom-call | flops 1 | bytes 1 | tf_op jit(solution)/shard_map/scores/pallas_call | solution.py:35
  23.0 3.8 %collective-permute-done.7.refs_2_ = bf16[2,2,192,128]{3,2,1,0:T(8,128)(2,1)S(1)} collective-permute-done((bf16[2,2,192,128]{3,2,1,0:T(8,128)(2,1)S(1)}, bf16[2,2,192,128]{3,2,1,0:T(8,128)(2,1)S(1)}, u32[]{:S(2)}, u32[]{:S(2)}) %collective-permute-start.7) | collective-permute-done | bytes 196640 | tf_op jit(solution)/shard_map/ppermute | solution.py:46
  26.9 1.5 %scores.6 = (bf16[2048,4096]{1,0:T(8,128)(2,1)S(1)}, bf16[512,192]{1,0:T(8,128)(2,1)S(1)}, f32[2,512]{1,0:T(2,128)S(1)}) custom-call(bf16[4,2,192,128]{3,2,1,0:T(8,128)(2,1)S(1)} %join.3.refs_0_, bf16[2048,256]{1,0:T(8,128)(2,1)S(1)} %get-tuple-element.29.refs_1_.refs_4_, ...), custom_call_target="tpu_custom_call", output_to_operand_aliasing={{0}: (4, {})} | custom-call | flops 1 | bytes 1 | tf_op jit(solution)/shard_map/scores/pallas_call | solution.py:35
  28.6 1.5 %scores.7 = (bf16[2048,4096]{1,0:T(8,128)(2,1)S(1)}, bf16[512,192]{1,0:T(8,128)(2,1)S(1)}, f32[4,1024]{1,0:T(4,128)S(1)}) custom-call(f32[2,512]{1,0:T(2,128)S(1)} %get-tuple-element.31.refs_0_, f32[2,512]{1,0:T(2,128)S(1)} %get-tuple-element.33.refs_3_.refs_1_, f32[2,512]{1,0:T(2,128)S(1)} %get-tuple-element.36.refs_2_, ...), custom_call_target="tpu_custom_call", output_to_operand_aliasing={{0}: (7, {})} | custom-call | flops 1 | bytes 1 | tf_op jit(solution)/shard_map/scores/pallas_call | solution.py:35
  30.1 3.3 %collective-permute-start.11 = (f32[4,1024]{1,0:T(4,128)S(1)}, f32[4,1024]{1,0:T(4,128)S(1)}, u32[]{:S(2)}, u32[]{:S(2)}) collective-permute-start(f32[4,1024]{1,0:T(4,128)S(1)} %get-tuple-element.38.refs_0_), channel_id=1, source_target_pairs={{0,6},{4,2},{1,7},{5,3},{8,14},{12,10},{9,15},{13,11},{16,22},{20,... | collective-permute-start | bytes 49160 | tf_op jit(solution)/shard_map/ppermute | solution.py:290
  33.4 0.7 %collective-permute-start.10 = (f32[4,1024]{1,0:T(4,128)S(1)}, f32[4,1024]{1,0:T(4,128)S(1)}, u32[]{:S(2)}, u32[]{:S(2)}) collective-permute-start(f32[4,1024]{1,0:T(4,128)S(1)} %get-tuple-element.38.refs_0_), channel_id=1, source_target_pairs={{2,6},{6,2},{3,7},{7,3},{10,14},{14,10},{11,15},{15,11},{18,22},{2... | collective-permute-start | bytes 49160 | tf_op jit(solution)/shard_map/ppermute | solution.py:290
  34.1 2.7 %collective-permute-start.9 = (f32[4,1024]{1,0:T(4,128)S(1)}, f32[4,1024]{1,0:T(4,128)S(1)}, u32[]{:S(2)}, u32[]{:S(2)}) collective-permute-start(f32[4,1024]{1,0:T(4,128)S(1)} %get-tuple-element.38.refs_0_), channel_id=1, source_target_pairs={{0,2},{4,6},{1,3},{5,7},{8,10},{12,14},{9,11},{13,15},{16,18},{20,... | collective-permute-start | bytes 49160 | tf_op jit(solution)/shard_map/ppermute | solution.py:290
  36.8 0.8 %collective-permute-done.9.refs_1_ = f32[4,1024]{1,0:T(4,128)S(1)} collective-permute-done((f32[4,1024]{1,0:T(4,128)S(1)}, f32[4,1024]{1,0:T(4,128)S(1)}, u32[]{:S(2)}, u32[]{:S(2)}) %collective-permute-start.9) | collective-permute-done | bytes 16416 | tf_op jit(solution)/shard_map/ppermute | solution.py:290
  37.6 0.7 %collective-permute-start.14 = (f32[4,1024]{1,0:T(4,128)S(1)}, f32[4,1024]{1,0:T(4,128)S(1)}, u32[]{:S(2)}, u32[]{:S(2)}) collective-permute-start(f32[4,1024]{1,0:T(4,128)S(1)} %relay.3.refs_0_), channel_id=1, source_target_pairs={{2,26},{10,18},{18,10},{26,2},{6,30},{14,22},{22,14},{30,6},{3,27}... | collective-permute-start | bytes 49160 | tf_op jit(solution)/shard_map/ppermute | solution.py:296
  38.3 0.7 %collective-permute-start.13 = (f32[4,1024]{1,0:T(4,128)S(1)}, f32[4,1024]{1,0:T(4,128)S(1)}, u32[]{:S(2)}, u32[]{:S(2)}) collective-permute-start(f32[4,1024]{1,0:T(4,128)S(1)} %relay.3.refs_0_), channel_id=1, source_target_pairs={{2,18},{10,26},{18,2},{26,10},{6,22},{14,30},{22,6},{30,14},{3,19}... | collective-permute-start | bytes 49160 | tf_op jit(solution)/shard_map/ppermute | solution.py:296
  38.9 0.7 %collective-permute-start.12 = (f32[4,1024]{1,0:T(4,128)S(1)}, f32[4,1024]{1,0:T(4,128)S(1)}, u32[]{:S(2)}, u32[]{:S(2)}) collective-permute-start(f32[4,1024]{1,0:T(4,128)S(1)} %relay.3.refs_0_), channel_id=1, source_target_pairs={{2,10},{10,2},{18,26},{26,18},{6,14},{14,6},{22,30},{30,22},{3,11}... | collective-permute-start | bytes 49160 | tf_op jit(solution)/shard_map/ppermute | solution.py:296
  40.4 1.3 %collective-permute-start.16 = (f32[4,1024]{1,0:T(4,128)S(1)}, f32[4,1024]{1,0:T(4,128)S(1)}, u32[]{:S(2)}, u32[]{:S(2)}) collective-permute-start(f32[4,1024]{1,0:T(4,128)S(1)} %relay.5.led_ref), channel_id=1, source_target_pairs={{2,0},{6,4},{3,1},{7,5},{10,8},{14,12},{11,9},{15,13},{18,16},{22,... | collective-permute-start | bytes 49160 | tf_op jit(solution)/shard_map/ppermute | solution.py:385
  41.7 13.3 %collective-permute-done.16.given_ref = f32[4,1024]{1,0:T(4,128)S(1)} collective-permute-done((f32[4,1024]{1,0:T(4,128)S(1)}, f32[4,1024]{1,0:T(4,128)S(1)}, u32[]{:S(2)}, u32[]{:S(2)}) %collective-permute-start.16) | collective-permute-done | bytes 16416 | tf_op jit(solution)/shard_map/ppermute | solution.py:385
  55.0 3.7 %gradient.1 = f32[192,2048]{1,0:T(8,128)} custom-call(f32[4,1024]{1,0:T(4,128)S(1)} %relay.5.led_ref, f32[4,1024]{1,0:T(4,128)S(1)} %collective-permute-done.16.given_ref, f32[1,128]{1,0:T(1,128)S(1)} %get-tuple-element.27.refs_5_.refs_3_.refs_6_.peak_ref, f32[192,2048]{1,0:T(8,128)S(1)} %get-tuple-element.39.weight_unit, ...), custom_call_target="tpu_custom_call" | custom-call | flops 1 | bytes 1 | tf_op jit(solution)/shard_map/gradient/pallas_call | solution.py:35
  (23 shorter events, 2.0 us)
Async XLA Ops:
  0.6 4.8 %collective-permute-start = (s32[1,256]{1,0:T(1,128)}, s32[1,256]{1,0:T(1,128)S(1)}, u32[]{:S(2)}, u32[]{:S(2)}) collective-permute-start(s32[1,256]{1,0:T(1,128)} %param.10), channel_id=1, source_target_pairs={{0,1},{1,0},{2,3},{3,2},{4,5},{5,4},{6,7},{7,6},{8,9},{9,8},{10,11... | collective-permute-start | bytes 3080 | tf_op jit(solution)/shard_map/ppermute | solution.py:46
  5.6 6.5 %collective-permute-start.4 = (bf16[2,192,128]{2,1,0:T(8,128)(2,1)S(1)}, bf16[2,192,128]{2,1,0:T(8,128)(2,1)S(1)}, u32[]{:S(2)}, u32[]{:S(2)}) collective-permute-start(bf16[2,192,128]{2,1,0:T(8,128)(2,1)S(1)} %pack.1.refs_0_), channel_id=1, source_target_pairs={{0,1},{1,0},{2,3},{3,2},{4,5},{5,4},{6,7},{7,6},{8,9},{9,8},{10,11... | collective-permute-start | bytes 294920 | tf_op jit(solution)/shard_map/ppermute | solution.py:46
  7.7 11.0 %collective-permute-start.3 = (bf16[2,192,128]{2,1,0:T(8,128)(2,1)S(1)}, bf16[2,192,128]{2,1,0:T(8,128)(2,1)S(1)}, u32[]{:S(2)}, u32[]{:S(2)}) collective-permute-start(bf16[2,192,128]{2,1,0:T(8,128)(2,1)S(1)} %pack.1.refs_0_), channel_id=1, source_target_pairs={{0,24},{8,16},{16,8},{24,0},{1,25},{9,17},{17,9},{25,1},{2,26},{10... | collective-permute-start | bytes 294920 | tf_op jit(solution)/shard_map/ppermute | solution.py:46
  11.2 7.4 %collective-permute-start.2 = (bf16[2,192,128]{2,1,0:T(8,128)(2,1)S(1)}, bf16[2,192,128]{2,1,0:T(8,128)(2,1)S(1)}, u32[]{:S(2)}, u32[]{:S(2)}) collective-permute-start(bf16[2,192,128]{2,1,0:T(8,128)(2,1)S(1)} %pack.1.refs_0_), channel_id=1, source_target_pairs={{0,16},{8,24},{16,0},{24,8},{1,17},{9,25},{17,1},{25,9},{2,18},{10... | collective-permute-start | bytes 294920 | tf_op jit(solution)/shard_map/ppermute | solution.py:46
  11.3 7.4 %collective-permute-start.1 = (bf16[2,192,128]{2,1,0:T(8,128)(2,1)S(1)}, bf16[2,192,128]{2,1,0:T(8,128)(2,1)S(1)}, u32[]{:S(2)}, u32[]{:S(2)}) collective-permute-start(bf16[2,192,128]{2,1,0:T(8,128)(2,1)S(1)} %pack.1.refs_0_), channel_id=1, source_target_pairs={{0,8},{8,0},{16,24},{24,16},{1,9},{9,1},{17,25},{25,17},{2,10},{10... | collective-permute-start | bytes 294920 | tf_op jit(solution)/shard_map/ppermute | solution.py:46
  12.0 7.3 %collective-permute-start.5 = (bf16[2,192,128]{2,1,0:T(8,128)(2,1)S(1)}, bf16[2,192,128]{2,1,0:T(8,128)(2,1)S(1)}, u32[]{:S(2)}, u32[]{:S(2)}) collective-permute-start(bf16[2,192,128]{2,1,0:T(8,128)(2,1)S(1)} %collective-permute-done.4.refs_0_), channel_id=1, source_target_pairs={{0,8},{8,0},{16,24},{24,16},{1,9},{9,1},{17,25},{25,17},{2,10},{10... | collective-permute-start | bytes 294920 | tf_op jit(solution)/shard_map/ppermute | solution.py:46
  19.4 2.1 %collective-permute-start.6 = (bf16[4,2,192,128]{3,2,1,0:T(8,128)(2,1)S(1)}, bf16[4,2,192,128]{3,2,1,0:T(8,128)(2,1)S(1)}, u32[]{:S(2)}, u32[]{:S(2)}) collective-permute-start(bf16[4,2,192,128]{3,2,1,0:T(8,128)(2,1)S(1)} %get-tuple-element.28.refs_0_), channel_id=1, source_target_pairs={{0,2},{2,0},{4,6},{6,4},{1,3},{3,1},{5,7},{7,5},{8,10},{10,8},{12,... | collective-permute-start | bytes 1179656 | tf_op jit(solution)/shard_map/ppermute | solution.py:46
  19.5 7.3 %collective-permute-start.7 = (bf16[2,2,192,128]{3,2,1,0:T(8,128)(2,1)S(1)}, bf16[2,2,192,128]{3,2,1,0:T(8,128)(2,1)S(1)}, u32[]{:S(2)}, u32[]{:S(2)}) collective-permute-start(bf16[2,2,192,128]{3,2,1,0:T(8,128)(2,1)S(1)} %get-tuple-element.34), channel_id=1, source_target_pairs={{0,1},{1,0},{2,3},{3,2},{4,5},{5,4},{6,7},{7,6},{8,9},{9,8},{10,11... | collective-permute-start | bytes 589832 | tf_op jit(solution)/shard_map/ppermute | solution.py:46
  26.8 1.8 %collective-permute-start.8 = (bf16[4,2,192,128]{3,2,1,0:T(8,128)(2,1)S(1)}, bf16[4,2,192,128]{3,2,1,0:T(8,128)(2,1)S(1)}, u32[]{:S(2)}, u32[]{:S(2)}) collective-permute-start(bf16[4,2,192,128]{3,2,1,0:T(8,128)(2,1)S(1)} %join.3.refs_0_), channel_id=1, source_target_pairs={{0,2},{2,0},{4,6},{6,4},{1,3},{3,1},{5,7},{7,5},{8,10},{10,8},{12,... | collective-permute-start | bytes 1179656 | tf_op jit(solution)/shard_map/ppermute | solution.py:46
  30.1 6.6 %collective-permute-start.11 = (f32[4,1024]{1,0:T(4,128)S(1)}, f32[4,1024]{1,0:T(4,128)S(1)}, u32[]{:S(2)}, u32[]{:S(2)}) collective-permute-start(f32[4,1024]{1,0:T(4,128)S(1)} %get-tuple-element.38.refs_0_), channel_id=1, source_target_pairs={{0,6},{4,2},{1,7},{5,3},{8,14},{12,10},{9,15},{13,11},{16,22},{20,... | collective-permute-start | bytes 49160 | tf_op jit(solution)/shard_map/ppermute | solution.py:290
  33.4 3.3 %collective-permute-start.10 = (f32[4,1024]{1,0:T(4,128)S(1)}, f32[4,1024]{1,0:T(4,128)S(1)}, u32[]{:S(2)}, u32[]{:S(2)}) collective-permute-start(f32[4,1024]{1,0:T(4,128)S(1)} %get-tuple-element.38.refs_0_), channel_id=1, source_target_pairs={{2,6},{6,2},{3,7},{7,3},{10,14},{14,10},{11,15},{15,11},{18,22},{2... | collective-permute-start | bytes 49160 | tf_op jit(solution)/shard_map/ppermute | solution.py:290
  34.1 3.5 %collective-permute-start.9 = (f32[4,1024]{1,0:T(4,128)S(1)}, f32[4,1024]{1,0:T(4,128)S(1)}, u32[]{:S(2)}, u32[]{:S(2)}) collective-permute-start(f32[4,1024]{1,0:T(4,128)S(1)} %get-tuple-element.38.refs_0_), channel_id=1, source_target_pairs={{0,2},{4,6},{1,3},{5,7},{8,10},{12,14},{9,11},{13,15},{16,18},{20,... | collective-permute-start | bytes 49160 | tf_op jit(solution)/shard_map/ppermute | solution.py:290
  37.6 2.0 %collective-permute-start.14 = (f32[4,1024]{1,0:T(4,128)S(1)}, f32[4,1024]{1,0:T(4,128)S(1)}, u32[]{:S(2)}, u32[]{:S(2)}) collective-permute-start(f32[4,1024]{1,0:T(4,128)S(1)} %relay.3.refs_0_), channel_id=1, source_target_pairs={{2,26},{10,18},{18,10},{26,2},{6,30},{14,22},{22,14},{30,6},{3,27}... | collective-permute-start | bytes 49160 | tf_op jit(solution)/shard_map/ppermute | solution.py:296
  38.3 1.4 %collective-permute-start.13 = (f32[4,1024]{1,0:T(4,128)S(1)}, f32[4,1024]{1,0:T(4,128)S(1)}, u32[]{:S(2)}, u32[]{:S(2)}) collective-permute-start(f32[4,1024]{1,0:T(4,128)S(1)} %relay.3.refs_0_), channel_id=1, source_target_pairs={{2,18},{10,26},{18,2},{26,10},{6,22},{14,30},{22,6},{30,14},{3,19}... | collective-permute-start | bytes 49160 | tf_op jit(solution)/shard_map/ppermute | solution.py:296
  38.9 0.7 %collective-permute-start.12 = (f32[4,1024]{1,0:T(4,128)S(1)}, f32[4,1024]{1,0:T(4,128)S(1)}, u32[]{:S(2)}, u32[]{:S(2)}) collective-permute-start(f32[4,1024]{1,0:T(4,128)S(1)} %relay.3.refs_0_), channel_id=1, source_target_pairs={{2,10},{10,2},{18,26},{26,18},{6,14},{14,6},{22,30},{30,22},{3,11}... | collective-permute-start | bytes 49160 | tf_op jit(solution)/shard_map/ppermute | solution.py:296
  39.7 0.7 %collective-permute-start.15 = (f32[4,1024]{1,0:T(4,128)S(1)}, f32[4,1024]{1,0:T(4,128)S(1)}, u32[]{:S(2)}, u32[]{:S(2)}) collective-permute-start(f32[4,1024]{1,0:T(4,128)S(1)} %relay.4.refs_0_), channel_id=1, source_target_pairs={{2,3},{3,2},{6,7},{7,6},{10,11},{11,10},{14,15},{15,14},{18,19},{1... | collective-permute-start | bytes 49160 | tf_op jit(solution)/shard_map/ppermute | solution.py:296
  40.4 14.6 %collective-permute-start.16 = (f32[4,1024]{1,0:T(4,128)S(1)}, f32[4,1024]{1,0:T(4,128)S(1)}, u32[]{:S(2)}, u32[]{:S(2)}) collective-permute-start(f32[4,1024]{1,0:T(4,128)S(1)} %relay.5.led_ref), channel_id=1, source_target_pairs={{2,0},{6,4},{3,1},{7,5},{10,8},{14,12},{11,9},{15,13},{18,16},{22,... | collective-permute-start | bytes 49160 | tf_op jit(solution)/shard_map/ppermute | solution.py:385

commit v10 on v7

--- a/solution.py
+++ b/solution.py
@@ -267,7 +267,7 @@
             unit = (values * lax.rsqrt(jnp.sum(values * values, axis=0, keepdims=True) + EPS)).astype(jnp.bfloat16)
             lanes = slice(group * per * width, (group + 1) * per * width)
             if which == 0:
-                unit_ref[:, lanes] = unit
+                unit_ref[lanes, :] = unit.T
             stationary = jnp.concatenate([unit, extra], axis=0)
             total = jnp.zeros((8, per * width), jnp.float32)
             for at in range(0, cols, step):
@@ -308,7 +308,7 @@
         "scores",
         [
             held(cols, 8 * rows, dtype=jnp.bfloat16),
-            held(bot, rows, dtype=jnp.bfloat16),
+            held(rows, bot, dtype=jnp.bfloat16),
             held(4, 2 * rows) if part == 3 else held(2, rows),
         ],
         args,
@@ -325,41 +325,60 @@
     refs[-1][...] = jnp.concatenate(combine(parts), axis=0)
 
 
-def add_up(total, axis):
-    n = lax.axis_size(axis)
-    if n <= DIRECT:
-        parts = [total, *[swap(total, axis, k) for k in range(1, n)]]
-    else:
-        parts = [lax.all_to_all(jnp.broadcast_to(total[None], (n, *total.shape)), axis, 0, 0, tiled=True)]
-    return call(relay_kernel, "relay", held(*total.shape), parts)
-
-
-def grad_kernel(here_ref, there_ref, peak_ref, weight_unit, weight_scale, *refs):
-    units, exp_ref, out_hbm, scales, feats, buf, sems = refs[:4], *refs[4:]
+def add_up(total, *others):
+    return call(relay_kernel, "relay", held(*total.shape), [total, *others])
+
+
+def add_up_all(total):
+    n_proto, n_dp, n_fsdp = [lax.axis_size(axis) for axis in ("proto", "dp", "fsdp")]
+    total = add_up(total, swap(total, "proto"))
+
+    def across(up, over):
+        places = [(p, d) for p in range(n_proto) for d in range(n_dp)]
+        pairs = [(p * n_dp + d, (p ^ up) * n_dp + (d ^ over)) for p, d in places]
+        return lax.ppermute(total, ("proto", "dp"), pairs)
+
+    steps = [(up, over) for up in range(0, n_proto, 2) for over in range(n_dp)][1:]
+    total = add_up(total, *[across(*step) for step in steps])
+    if n_fsdp <= DIRECT:
+        return add_up(total, *[swap(total, "fsdp", k) for k in range(1, n_fsdp)])
+    copies = jnp.broadcast_to(total[None], (n_fsdp, *total.shape))
+    parts = lax.all_to_all(copies, "fsdp", 0, 0, tiled=True)
+    return call(relay_kernel, "relay", held(*total.shape), [parts])
+
+
+def grad_kernel(total_ref, peak_ref, weight_unit, weight_scale, *refs):
+    units, exp_ref, out_hbm, scales, buf, sems = refs[:4], *refs[4:]
     dp, _, core = here()
-    total_s, log_t = combine([here_ref[...], there_ref[...]])
-    scales[0:2, :] = 10.0 / total_s
-    scales[2:4, :] = -10.0 * jnp.exp2(GAIN_T * peak_ref[:, :1] - log_t)
-    bot, rows = units[0].shape
+    scales[0:2, :] = 10.0 / total_ref[0:2, :]
+    scales[2:4, :] = 10.0 * jnp.exp2(GAIN_T * peak_ref[:, :1] - total_ref[2:4, :])
+    rows = units[0].shape[0]
     width = 128
     n = rows // width
+    factors = []
     for part in range(4):
         view, half = divmod(part, 2)
         base = (dp ^ view) * rows
         at = [pl.ds(pl.multiple_of(base + slot(k, n) * width, width), width) for k in range(n)]
-        unit = units[part][...].astype(jnp.float32)
-        for which, lies in ((0, part), (1, part ^ 2)):
+        for which in (0, 1):
             picked = [
                 jnp.where(core == half, scales[2 * which:2 * which + 1, where], scales[2 * which + 1:2 * which + 2, where])
                 for where in at
             ]
-            scaled = (unit * jnp.concatenate(picked, axis=1)).astype(jnp.bfloat16)
-            feats[(2 * lies + which) * rows:(2 * lies + which + 1) * rows, :] = scaled.T
+            factors.append(jnp.concatenate(picked, axis=1).astype(jnp.bfloat16))
+    feats = jnp.concatenate([unit[...] for unit in units], axis=0)
     chunks, _, step = buf.shape
     stores = []
     for i in range(chunks):
         at = slice(i * step, (i + 1) * step)
-        grad = jnp.dot(exp_ref[at, :], feats[...], preferred_element_type=jnp.float32).T
+        derivs = []
+        for part in range(4):
+            lies_s, lies_t = 2 * part * rows, (2 * (part ^ 2) + 1) * rows
+            probs_s = exp_ref[at, lies_s:lies_s + rows] * factors[2 * part]
+            probs_t = exp_ref[at, lies_t:lies_t + rows] * factors[2 * part + 1]
+            derivs.append(probs_s - probs_t)
+        derivs = jnp.concatenate(derivs, axis=1)
+        grad = jnp.dot(derivs, feats, preferred_element_type=jnp.float32).T
         unit = weight_unit[:, at]
         proj = unit * jnp.sum(unit * grad, axis=0, keepdims=True)
         buf[i] = (grad - proj) * weight_scale[:, at]
@@ -369,23 +388,18 @@
         store.wait()
 
 
-def gradient(here_total, there_total, peak, weight_unit, weight_scale, units, exps):
-    cols, all_rows = exps.shape
-    bot, rows = units[0].shape
+def gradient(total, peak, weight_unit, weight_scale, units, exps):
+    cols = exps.shape[0]
+    rows, bot = units[0].shape
     step = min(512, cols)
-    args = (here_total, there_total, peak, weight_unit, weight_scale, *units, exps)
+    args = (total, peak, weight_unit, weight_scale, *units, exps)
     return call(
         grad_kernel,
         "gradient",
         pltpu.HBM((bot, cols), jnp.float32),
         args,
         out_specs=IN_HBM,
-        scratch_shapes=[
-            held(4, 2 * rows),
-            held(all_rows, bot, dtype=jnp.bfloat16),
-            held(cols // step, bot, step),
-            pltpu.SemaphoreType.DMA((cols // step,)),
-        ],
+        scratch_shapes=[held(4, 2 * rows), held(cols // step, bot, step), pltpu.SemaphoreType.DMA((cols // step,))],
     )
 
 
@@ -398,26 +412,22 @@
     mine = pack(*fetch(in_hbm(student_feats[0].T), in_hbm(teacher_feats[0].T)), index)
     new, wt, ws, unit, scale, peak = prepare(teacher_weight, student_weight, center, n_dp)
     weights = (ws, wt, peak)
-    own_cols = ws.shape[0]
     if n_fsdp <= DIRECT:
         other = [swap(mine, "dp")]
         along = [swap(mine, "fsdp", k) for k in range(1, n_fsdp)]
-        other.append(swap(other[0], "fsdp"))
-        own, far = join([mine, *along], [n_fsdp, n_fsdp - 2], (other[1], peak))
-        exps, unit_a, total_a = scores(0, own, weights)
-        teacher_new, done = update_rest(teacher_weight, student_weight, total_a, new, own_cols)
-        (other,) = join([*other, swap(far, "dp")], [n_fsdp], (done,))
+        own, far = join([mine, *along], [n_fsdp, n_fsdp - 2], (other[0], peak))
+        other += [swap(other[0], "fsdp"), swap(far, "dp")]
     else:
         own = lax.all_to_all(jnp.broadcast_to(mine[None], (n_fsdp, *mine.shape)), "fsdp", 0, 0, tiled=True)
-        other = swap(own, "dp")
-        teacher_new, _ = update_rest(teacher_weight, student_weight, own, new, own_cols)
-        exps, unit_a, total_a = scores(0, own, weights)
+        other = [swap(own, "dp")]
+    exps, unit_a, total_a = scores(0, own, weights)
+    teacher_new, done = update_rest(teacher_weight, student_weight, total_a, new, ws.shape[0])
+    (other,) = join(other, [n_fsdp], (done,))
     exps, unit_c, total_c = scores(2, other, weights, exps=exps)
     exps, unit_b, total_b = scores(1, swap(own, "proto"), weights, exps=exps)
-    exps, unit_d, totals = scores(3, swap(other, "proto"), weights, (total_a, total_b, total_c), exps)
-    total = add_up(add_up(totals, "proto"), "fsdp")
-    units = (unit_a, unit_b, unit_c, unit_d)
-    student_grad = gradient(total, swap(total, "dp"), peak, unit, scale, units, exps)
+    exps, unit_d, total = scores(3, swap(other, "proto"), weights, (total_a, total_b, total_c), exps)
+    total = add_up_all(total)
+    student_grad = gradient(total, peak, unit, scale, (unit_a, unit_b, unit_c, unit_d), exps)
     return (teacher_new, student_grad)
 
 

time: 52.1 us -> 47.5 us (0.912)
  waiting for transfers between devices: 13.1 us -> 10.2 us
  Pallas kernels: 19.4 us -> 17.2 us
    ppermute x16 -> x13, waiting for transfers between devices: 13.1 us -> 7.36 us  [swap(): lax.ppermute(block, axis, [(i, i ^ apart) for i in range(lax.axis_size(ax...]
    ppermute x0 -> x3, starting transfers between devices: none -> 3.55 us  [across(): return lax.ppermute(total, ('proto', 'dp'), pairs)]
    ppermute x16 -> x13, starting transfers between devices: 18.7 us -> 15.6 us  [swap(): lax.ppermute(block, axis, [(i, i ^ apart) for i in range(lax.axis_size(ax...]
    ppermute x0 -> x3, waiting for transfers between devices: none -> 2.87 us  [across(): return lax.ppermute(total, ('proto', 'dp'), pairs)]
    pallas_call x13 -> x14, Pallas kernels: 19.4 us -> 17.2 us  [call(): pl.pallas_call(kernel, out_shape=out_shape, compiler_params=pltpu.Compile...]
  transfers between devices with their start and end apart: 16 -> 16, of which waited for: 9 -> 10; matrix products, arithmetic and copies ran while one was open for 0% -> 0% of each run, Pallas kernels for 22% -> 25%
where the time goes in v10:
time: 47.5 us; the launch traced here: 47.4 us
  starting transfers between devices  19.2 us (40%)
  Pallas kernels  17.2 us (36%)
  waiting for transfers between devices  10.2 us (21%)
  between operations  0.76 us (2%)
    pallas_call x14, Pallas kernels, call(): pl.pallas_call(kernel, out_shape=out_shape, compiler_params=pltpu.Compile...  17.2 us
    ppermute x13, starting transfers between devices, swap(): lax.ppermute(block, axis, [(i, i ^ apart) for i in range(lax.axis_size(ax...  15.6 us
    ppermute x13, waiting for transfers between devices, swap(): lax.ppermute(block, axis, [(i, i ^ apart) for i in range(lax.axis_size(ax...  7.36 us
    ppermute x3, starting transfers between devices, across(): return lax.ppermute(total, ('proto', 'dp'), pairs)  3.55 us
    ppermute x3, waiting for transfers between devices, across(): return lax.ppermute(total, ('proto', 'dp'), pairs)  2.87 us
  transfers between devices with their start and end apart: 16, of which 10 were waited for; matrix products, arithmetic and copies ran while one was open for 0% of the time, Pallas kernels for 25%

profile of v10, /device:TPU:0, one launch (start us, length us, event | category | flops | bytes accessed | tf_op | source)
XLA Modules:
  0.0 47.4 jit_solution(1976504381777239104)
XLA Ops:
  0.6 3.0 %collective-permute-start = (s32[1,256]{1,0:T(1,128)}, s32[1,256]{1,0:T(1,128)S(1)}, u32[]{:S(2)}, u32[]{:S(2)}) collective-permute-start(s32[1,256]{1,0:T(1,128)} %param.10), channel_id=1, source_target_pairs={{0,1},{1,0},{2,3},{3,2},{4,5},{5,4},{6,7},{7,6},{8,9},{9,8},{10,11... | collective-permute-start | bytes 3080 | tf_op jit(solution)/shard_map/ppermute | solution.py:46
  3.6 0.9 %fetch.1 = (bf16[192,128]{1,0:T(8,128)(2,1)S(1)}, bf16[192,256]{1,0:T(8,128)(2,1)S(1)}) custom-call(bf16[192,256]{1,0:T(8,128)(2,1)} %bitcast.7, bf16[192,256]{1,0:T(8,128)(2,1)} %bitcast.8), custom_call_target="tpu_custom_call" | custom-call | flops 1 | bytes 1 | tf_op jit(solution)/shard_map/fetch/pallas_call | solution.py:35
  4.6 0.8 %collective-permute-done.index_ref = s32[1,256]{1,0:T(1,128)S(1)} collective-permute-done((s32[1,256]{1,0:T(1,128)}, s32[1,256]{1,0:T(1,128)S(1)}, u32[]{:S(2)}, u32[]{:S(2)}) %collective-permute-start) | collective-permute-done | bytes 1056 | tf_op jit(solution)/shard_map/ppermute | solution.py:46
  5.6 2.1 %collective-permute-start.4 = (bf16[2,192,128]{2,1,0:T(8,128)(2,1)S(1)}, bf16[2,192,128]{2,1,0:T(8,128)(2,1)S(1)}, u32[]{:S(2)}, u32[]{:S(2)}) collective-permute-start(bf16[2,192,128]{2,1,0:T(8,128)(2,1)S(1)} %pack.1.refs_0_), channel_id=1, source_target_pairs={{0,1},{1,0},{2,3},{3,2},{4,5},{5,4},{6,7},{7,6},{8,9},{9,8},{10,11... | collective-permute-start | bytes 294920 | tf_op jit(solution)/shard_map/ppermute | solution.py:46
  7.7 3.6 %collective-permute-start.3 = (bf16[2,192,128]{2,1,0:T(8,128)(2,1)S(1)}, bf16[2,192,128]{2,1,0:T(8,128)(2,1)S(1)}, u32[]{:S(2)}, u32[]{:S(2)}) collective-permute-start(bf16[2,192,128]{2,1,0:T(8,128)(2,1)S(1)} %pack.1.refs_0_), channel_id=1, source_target_pairs={{0,24},{8,16},{16,8},{24,0},{1,25},{9,17},{17,9},{25,1},{2,26},{10... | collective-permute-start | bytes 294920 | tf_op jit(solution)/shard_map/ppermute | solution.py:46
  11.3 0.8 %collective-permute-start.1 = (bf16[2,192,128]{2,1,0:T(8,128)(2,1)S(1)}, bf16[2,192,128]{2,1,0:T(8,128)(2,1)S(1)}, u32[]{:S(2)}, u32[]{:S(2)}) collective-permute-start(bf16[2,192,128]{2,1,0:T(8,128)(2,1)S(1)} %pack.1.refs_0_), channel_id=1, source_target_pairs={{0,8},{8,0},{16,24},{24,16},{1,9},{9,1},{17,25},{25,17},{2,10},{10... | collective-permute-start | bytes 294920 | tf_op jit(solution)/shard_map/ppermute | solution.py:46
  12.0 3.6 %prep.1 = (f32[192,4096]{1,0:T(8,128)}, bf16[2048,256]{1,0:T(8,128)(2,1)S(1)}, bf16[2048,256]{1,0:T(8,128)(2,1)S(1)}, f32[192,2048]{1,0:T(8,128)S(1)}, f32[1,2048]{1,0:T(1,128)S(1)}, /*index=5*/f32[1,128]{1,0:T(1,128)S(1)}) custom-call(f32[192,4096]{1,0:T(8,128)} %teacher_hbm.3, f32[192,4096]{1,0:T(8,128)} %student_hbm.3, f32[1,16384]{1,0:T(1,128)} %bitcast.9), custom_call_target="tpu_custom_call" | custom-call | flops 1 | bytes 1 | tf_op jit(solution)/shard_map/prep/pallas_call | solution.py:35
  15.7 2.5 %collective-permute-done.2.refs_2_ = bf16[2,192,128]{2,1,0:T(8,128)(2,1)S(1)} collective-permute-done((bf16[2,192,128]{2,1,0:T(8,128)(2,1)S(1)}, bf16[2,192,128]{2,1,0:T(8,128)(2,1)S(1)}, u32[]{:S(2)}, u32[]{:S(2)}) %collective-permute-start.2) | collective-permute-done | bytes 98336 | tf_op jit(solution)/shard_map/ppermute | solution.py:46
  19.3 1.4 %scores.4 = (bf16[2048,4096]{1,0:T(8,128)(2,1)S(1)}, bf16[512,192]{1,0:T(8,128)(2,1)S(1)}, f32[2,512]{1,0:T(2,128)S(1)}) custom-call(bf16[4,2,192,128]{3,2,1,0:T(8,128)(2,1)S(1)} %get-tuple-element.29.refs_0_, bf16[2048,256]{1,0:T(8,128)(2,1)S(1)} %get-tuple-element.30.refs_1_.refs_4_, bf16[2048,256]{1,0:T(8,128)(2,1)S(1)} %get-tuple-element.31.refs_2_.refs_5_, ...), custom_call_target="tpu_custom_call" | custom-call | flops 1 | bytes 1 | tf_op jit(solution)/shard_map/scores/pallas_call | solution.py:35
  20.7 2.8 %rest.1 = (f32[192,4096]{1,0:T(8,128)}, f32[8,128]{1,0:T(8,128)S(1)}) custom-call(f32[192,4096]{1,0:T(8,128)} %teacher_hbm.3, f32[192,4096]{1,0:T(8,128)} %student_hbm.3, f32[2,512]{1,0:T(2,128)S(1)} %get-tuple-element.32.after.refs_0_, f32[192,4096]{1,0:T(8,128)} %get-tuple-element.33.before_hbm), custom_call_target="tpu_custom_call", output_to_operand_aliasing={{0}: (3, {})} | custom-call | flops 1 | bytes 1 | tf_op jit(solution)/shard_map/rest/pallas_call | solution.py:35
  24.3 1.5 %scores.5 = (bf16[2048,4096]{1,0:T(8,128)(2,1)S(1)}, bf16[512,192]{1,0:T(8,128)(2,1)S(1)}, f32[2,512]{1,0:T(2,128)S(1)}) custom-call(bf16[4,2,192,128]{3,2,1,0:T(8,128)(2,1)S(1)} %join.3.refs_0_, bf16[2048,256]{1,0:T(8,128)(2,1)S(1)} %get-tuple-element.30.refs_1_.refs_4_, ...), custom_call_target="tpu_custom_call", output_to_operand_aliasing={{0}: (4, {})} | custom-call | flops 1 | bytes 1 | tf_op jit(solution)/shard_map/scores/pallas_call | solution.py:35
  25.8 1.5 %scores.6 = (bf16[2048,4096]{1,0:T(8,128)(2,1)S(1)}, bf16[512,192]{1,0:T(8,128)(2,1)S(1)}, f32[2,512]{1,0:T(2,128)S(1)}) custom-call(bf16[4,2,192,128]{3,2,1,0:T(8,128)(2,1)S(1)} %collective-permute-done.5.refs_0_, bf16[2048,256]{1,0:T(8,128)(2,1)S(1)} %get-tuple-element.30.refs_1_.refs_4_, ...), custom_call_target="tpu_custom_call", output_to_operand_aliasing={{0}: (4, {})} | custom-call | flops 1 | bytes 1 | tf_op jit(solution)/shard_map/scores/pallas_call | solution.py:35
  27.3 1.5 %scores.7 = (bf16[2048,4096]{1,0:T(8,128)(2,1)S(1)}, bf16[512,192]{1,0:T(8,128)(2,1)S(1)}, f32[4,1024]{1,0:T(4,128)S(1)}) custom-call(f32[2,512]{1,0:T(2,128)S(1)} %get-tuple-element.32.after.refs_0_, f32[2,512]{1,0:T(2,128)S(1)} %get-tuple-element.39.refs_1_, f32[2,512]{1,0:T(2,128)S(1)} %get-tuple-element.40.refs_2_, ...), custom_call_target="tpu_custom_call", output_to_operand_aliasing={{0}: (7, {})} | custom-call | flops 1 | bytes 1 | tf_op jit(solution)/shard_map/scores/pallas_call | solution.py:35
  29.3 0.8 %collective-permute-done.9.refs_1_ = f32[4,1024]{1,0:T(4,128)S(1)} collective-permute-done((f32[4,1024]{1,0:T(4,128)S(1)}, f32[4,1024]{1,0:T(4,128)S(1)}, u32[]{:S(2)}, u32[]{:S(2)}) %collective-permute-start.9) | collective-permute-done | bytes 16416 | tf_op jit(solution)/shard_map/ppermute | solution.py:46
  30.2 2.2 %collective-permute-start.12 = (f32[4,1024]{1,0:T(4,128)S(1)}, f32[4,1024]{1,0:T(4,128)S(1)}, u32[]{:S(2)}, u32[]{:S(2)}) collective-permute-start(f32[4,1024]{1,0:T(4,128)S(1)} %relay.3.refs_0_), channel_id=1, source_target_pairs={{0,5},{1,4},{2,7},{3,6},{4,1},{5,0},{6,3},{7,2},{8,13},{9,12},{10,... | collective-permute-start | bytes 49160 | tf_op jit(solution)/shard_map/ppermute | solution.py:339
  32.9 0.9 %collective-permute-start.10 = (f32[4,1024]{1,0:T(4,128)S(1)}, f32[4,1024]{1,0:T(4,128)S(1)}, u32[]{:S(2)}, u32[]{:S(2)}) collective-permute-start(f32[4,1024]{1,0:T(4,128)S(1)} %relay.3.refs_0_), channel_id=1, source_target_pairs={{0,1},{1,0},{2,3},{3,2},{4,5},{5,4},{6,7},{7,6},{8,9},{9,8},{10,11... | collective-permute-start | bytes 49160 | tf_op jit(solution)/shard_map/ppermute | solution.py:339
  33.8 1.1 %collective-permute-done.12.refs_3_ = f32[4,1024]{1,0:T(4,128)S(1)} collective-permute-done((f32[4,1024]{1,0:T(4,128)S(1)}, f32[4,1024]{1,0:T(4,128)S(1)}, u32[]{:S(2)}, u32[]{:S(2)}) %collective-permute-start.12) | collective-permute-done | bytes 16416 | tf_op jit(solution)/shard_map/ppermute | solution.py:339
  34.9 1.2 %collective-permute-done.11.refs_2_ = f32[4,1024]{1,0:T(4,128)S(1)} collective-permute-done((f32[4,1024]{1,0:T(4,128)S(1)}, f32[4,1024]{1,0:T(4,128)S(1)}, u32[]{:S(2)}, u32[]{:S(2)}) %collective-permute-start.11) | collective-permute-done | bytes 16416 | tf_op jit(solution)/shard_map/ppermute | solution.py:339
  36.7 2.1 %collective-permute-start.15 = (f32[4,1024]{1,0:T(4,128)S(1)}, f32[4,1024]{1,0:T(4,128)S(1)}, u32[]{:S(2)}, u32[]{:S(2)}) collective-permute-start(f32[4,1024]{1,0:T(4,128)S(1)} %relay.4.refs_0_), channel_id=1, source_target_pairs={{0,24},{8,16},{16,8},{24,0},{1,25},{9,17},{17,9},{25,1},{2,26},{10... | collective-permute-start | bytes 49160 | tf_op jit(solution)/shard_map/ppermute | solution.py:46
  38.8 1.0 %collective-permute-start.14 = (f32[4,1024]{1,0:T(4,128)S(1)}, f32[4,1024]{1,0:T(4,128)S(1)}, u32[]{:S(2)}, u32[]{:S(2)}) collective-permute-start(f32[4,1024]{1,0:T(4,128)S(1)} %relay.4.refs_0_), channel_id=1, source_target_pairs={{0,16},{8,24},{16,0},{24,8},{1,17},{9,25},{17,1},{25,9},{2,18},{10... | collective-permute-start | bytes 49160 | tf_op jit(solution)/shard_map/ppermute | solution.py:46
  39.8 1.3 %collective-permute-start.13 = (f32[4,1024]{1,0:T(4,128)S(1)}, f32[4,1024]{1,0:T(4,128)S(1)}, u32[]{:S(2)}, u32[]{:S(2)}) collective-permute-start(f32[4,1024]{1,0:T(4,128)S(1)} %relay.4.refs_0_), channel_id=1, source_target_pairs={{0,8},{8,0},{16,24},{24,16},{1,9},{9,1},{17,25},{25,17},{2,10},{10... | collective-permute-start | bytes 49160 | tf_op jit(solution)/shard_map/ppermute | solution.py:46
  41.1 1.1 %collective-permute-done.15.refs_3_ = f32[4,1024]{1,0:T(4,128)S(1)} collective-permute-done((f32[4,1024]{1,0:T(4,128)S(1)}, f32[4,1024]{1,0:T(4,128)S(1)}, u32[]{:S(2)}, u32[]{:S(2)}) %collective-permute-start.15) | collective-permute-done | bytes 16416 | tf_op jit(solution)/shard_map/ppermute | solution.py:46
  42.3 1.1 %collective-permute-done.14.refs_2_ = f32[4,1024]{1,0:T(4,128)S(1)} collective-permute-done((f32[4,1024]{1,0:T(4,128)S(1)}, f32[4,1024]{1,0:T(4,128)S(1)}, u32[]{:S(2)}, u32[]{:S(2)}) %collective-permute-start.14) | collective-permute-done | bytes 16416 | tf_op jit(solution)/shard_map/ppermute | solution.py:46
  43.6 3.8 %gradient.1 = f32[192,2048]{1,0:T(8,128)} custom-call(f32[4,1024]{1,0:T(4,128)S(1)} %relay.5.total_ref, f32[1,128]{1,0:T(1,128)S(1)} %get-tuple-element.28.refs_5_.refs_3_.refs_6_.peak_ref, f32[192,2048]{1,0:T(8,128)S(1)} %get-tuple-element.43.weight_unit, f32[1,2048]{1,0:T(1,128)S(1)} %get-tuple-element.44.weight_scale, ...), custom_call_target="tpu_custom_call" | custom-call | flops 1 | bytes 1 | tf_op jit(solution)/shard_map/gradient/pallas_call | solution.py:35
  (22 shorter events, 3.9 us)
Async XLA Ops:
  0.6 4.8 %collective-permute-start = (s32[1,256]{1,0:T(1,128)}, s32[1,256]{1,0:T(1,128)S(1)}, u32[]{:S(2)}, u32[]{:S(2)}) collective-permute-start(s32[1,256]{1,0:T(1,128)} %param.10), channel_id=1, source_target_pairs={{0,1},{1,0},{2,3},{3,2},{4,5},{5,4},{6,7},{7,6},{8,9},{9,8},{10,11... | collective-permute-start | bytes 3080 | tf_op jit(solution)/shard_map/ppermute | solution.py:46
  5.6 10.1 %collective-permute-start.4 = (bf16[2,192,128]{2,1,0:T(8,128)(2,1)S(1)}, bf16[2,192,128]{2,1,0:T(8,128)(2,1)S(1)}, u32[]{:S(2)}, u32[]{:S(2)}) collective-permute-start(bf16[2,192,128]{2,1,0:T(8,128)(2,1)S(1)} %pack.1.refs_0_), channel_id=1, source_target_pairs={{0,1},{1,0},{2,3},{3,2},{4,5},{5,4},{6,7},{7,6},{8,9},{9,8},{10,11... | collective-permute-start | bytes 294920 | tf_op jit(solution)/shard_map/ppermute | solution.py:46
  7.7 8.0 %collective-permute-start.3 = (bf16[2,192,128]{2,1,0:T(8,128)(2,1)S(1)}, bf16[2,192,128]{2,1,0:T(8,128)(2,1)S(1)}, u32[]{:S(2)}, u32[]{:S(2)}) collective-permute-start(bf16[2,192,128]{2,1,0:T(8,128)(2,1)S(1)} %pack.1.refs_0_), channel_id=1, source_target_pairs={{0,24},{8,16},{16,8},{24,0},{1,25},{9,17},{17,9},{25,1},{2,26},{10... | collective-permute-start | bytes 294920 | tf_op jit(solution)/shard_map/ppermute | solution.py:46
  11.2 6.9 %collective-permute-start.2 = (bf16[2,192,128]{2,1,0:T(8,128)(2,1)S(1)}, bf16[2,192,128]{2,1,0:T(8,128)(2,1)S(1)}, u32[]{:S(2)}, u32[]{:S(2)}) collective-permute-start(bf16[2,192,128]{2,1,0:T(8,128)(2,1)S(1)} %pack.1.refs_0_), channel_id=1, source_target_pairs={{0,16},{8,24},{16,0},{24,8},{1,17},{9,25},{17,1},{25,9},{2,18},{10... | collective-permute-start | bytes 294920 | tf_op jit(solution)/shard_map/ppermute | solution.py:46
  11.3 6.9 %collective-permute-start.1 = (bf16[2,192,128]{2,1,0:T(8,128)(2,1)S(1)}, bf16[2,192,128]{2,1,0:T(8,128)(2,1)S(1)}, u32[]{:S(2)}, u32[]{:S(2)}) collective-permute-start(bf16[2,192,128]{2,1,0:T(8,128)(2,1)S(1)} %pack.1.refs_0_), channel_id=1, source_target_pairs={{0,8},{8,0},{16,24},{24,16},{1,9},{9,1},{17,25},{25,17},{2,10},{10... | collective-permute-start | bytes 294920 | tf_op jit(solution)/shard_map/ppermute | solution.py:46
  18.3 6.0 %collective-permute-start.7 = (bf16[2,2,192,128]{3,2,1,0:T(8,128)(2,1)S(1)}, bf16[2,2,192,128]{3,2,1,0:T(8,128)(2,1)S(1)}, u32[]{:S(2)}, u32[]{:S(2)}) collective-permute-start(bf16[2,2,192,128]{3,2,1,0:T(8,128)(2,1)S(1)} %get-tuple-element.35), channel_id=1, source_target_pairs={{0,1},{1,0},{2,3},{3,2},{4,5},{5,4},{6,7},{7,6},{8,9},{9,8},{10,11... | collective-permute-start | bytes 589832 | tf_op jit(solution)/shard_map/ppermute | solution.py:46
  18.8 4.7 %collective-permute-start.6 = (bf16[2,192,128]{2,1,0:T(8,128)(2,1)S(1)}, bf16[2,192,128]{2,1,0:T(8,128)(2,1)S(1)}, u32[]{:S(2)}, u32[]{:S(2)}) collective-permute-start(bf16[2,192,128]{2,1,0:T(8,128)(2,1)S(1)} %collective-permute-done.4.refs_4_.refs_0_), channel_id=1, source_target_pairs={{0,8},{8,0},{16,24},{24,16},{1,9},{9,1},{17,25},{25,17},{2,10},{10... | collective-permute-start | bytes 294920 | tf_op jit(solution)/shard_map/ppermute | solution.py:46
  19.3 6.5 %collective-permute-start.5 = (bf16[4,2,192,128]{3,2,1,0:T(8,128)(2,1)S(1)}, bf16[4,2,192,128]{3,2,1,0:T(8,128)(2,1)S(1)}, u32[]{:S(2)}, u32[]{:S(2)}) collective-permute-start(bf16[4,2,192,128]{3,2,1,0:T(8,128)(2,1)S(1)} %get-tuple-element.29.refs_0_), channel_id=1, source_target_pairs={{0,2},{2,0},{4,6},{6,4},{1,3},{3,1},{5,7},{7,5},{8,10},{10,8},{12,... | collective-permute-start | bytes 1179656 | tf_op jit(solution)/shard_map/ppermute | solution.py:46
  24.3 3.0 %collective-permute-start.8 = (bf16[4,2,192,128]{3,2,1,0:T(8,128)(2,1)S(1)}, bf16[4,2,192,128]{3,2,1,0:T(8,128)(2,1)S(1)}, u32[]{:S(2)}, u32[]{:S(2)}) collective-permute-start(bf16[4,2,192,128]{3,2,1,0:T(8,128)(2,1)S(1)} %join.3.refs_0_), channel_id=1, source_target_pairs={{0,2},{2,0},{4,6},{6,4},{1,3},{3,1},{5,7},{7,5},{8,10},{10,8},{12,... | collective-permute-start | bytes 1179656 | tf_op jit(solution)/shard_map/ppermute | solution.py:46
  28.8 1.4 %collective-permute-start.9 = (f32[4,1024]{1,0:T(4,128)S(1)}, f32[4,1024]{1,0:T(4,128)S(1)}, u32[]{:S(2)}, u32[]{:S(2)}) collective-permute-start(f32[4,1024]{1,0:T(4,128)S(1)} %get-tuple-element.42.refs_0_), channel_id=1, source_target_pairs={{0,2},{2,0},{4,6},{6,4},{1,3},{3,1},{5,7},{7,5},{8,10},{10,8},{12,... | collective-permute-start | bytes 49160 | tf_op jit(solution)/shard_map/ppermute | solution.py:46
  30.2 4.7 %collective-permute-start.12 = (f32[4,1024]{1,0:T(4,128)S(1)}, f32[4,1024]{1,0:T(4,128)S(1)}, u32[]{:S(2)}, u32[]{:S(2)}) collective-permute-start(f32[4,1024]{1,0:T(4,128)S(1)} %relay.3.refs_0_), channel_id=1, source_target_pairs={{0,5},{1,4},{2,7},{3,6},{4,1},{5,0},{6,3},{7,2},{8,13},{9,12},{10,... | collective-permute-start | bytes 49160 | tf_op jit(solution)/shard_map/ppermute | solution.py:339
  32.4 3.7 %collective-permute-start.11 = (f32[4,1024]{1,0:T(4,128)S(1)}, f32[4,1024]{1,0:T(4,128)S(1)}, u32[]{:S(2)}, u32[]{:S(2)}) collective-permute-start(f32[4,1024]{1,0:T(4,128)S(1)} %relay.3.refs_0_), channel_id=1, source_target_pairs={{0,4},{1,5},{2,6},{3,7},{4,0},{5,1},{6,2},{7,3},{8,12},{9,13},{10,... | collective-permute-start | bytes 49160 | tf_op jit(solution)/shard_map/ppermute | solution.py:339
  32.9 3.7 %collective-permute-start.10 = (f32[4,1024]{1,0:T(4,128)S(1)}, f32[4,1024]{1,0:T(4,128)S(1)}, u32[]{:S(2)}, u32[]{:S(2)}) collective-permute-start(f32[4,1024]{1,0:T(4,128)S(1)} %relay.3.refs_0_), channel_id=1, source_target_pairs={{0,1},{1,0},{2,3},{3,2},{4,5},{5,4},{6,7},{7,6},{8,9},{9,8},{10,11... | collective-permute-start | bytes 49160 | tf_op jit(solution)/shard_map/ppermute | solution.py:339
  36.7 5.6 %collective-permute-start.15 = (f32[4,1024]{1,0:T(4,128)S(1)}, f32[4,1024]{1,0:T(4,128)S(1)}, u32[]{:S(2)}, u32[]{:S(2)}) collective-permute-start(f32[4,1024]{1,0:T(4,128)S(1)} %relay.4.refs_0_), channel_id=1, source_target_pairs={{0,24},{8,16},{16,8},{24,0},{1,25},{9,17},{17,9},{25,1},{2,26},{10... | collective-permute-start | bytes 49160 | tf_op jit(solution)/shard_map/ppermute | solution.py:46
  38.8 4.6 %collective-permute-start.14 = (f32[4,1024]{1,0:T(4,128)S(1)}, f32[4,1024]{1,0:T(4,128)S(1)}, u32[]{:S(2)}, u32[]{:S(2)}) collective-permute-start(f32[4,1024]{1,0:T(4,128)S(1)} %relay.4.refs_0_), channel_id=1, source_target_pairs={{0,16},{8,24},{16,0},{24,8},{1,17},{9,25},{17,1},{25,9},{2,18},{10... | collective-permute-start | bytes 49160 | tf_op jit(solution)/shard_map/ppermute | solution.py:46
  39.8 3.8 %collective-permute-start.13 = (f32[4,1024]{1,0:T(4,128)S(1)}, f32[4,1024]{1,0:T(4,128)S(1)}, u32[]{:S(2)}, u32[]{:S(2)}) collective-permute-start(f32[4,1024]{1,0:T(4,128)S(1)} %relay.4.refs_0_), channel_id=1, source_target_pairs={{0,8},{8,0},{16,24},{24,16},{1,9},{9,1},{17,25},{25,17},{2,10},{10... | collective-permute-start | bytes 49160 | tf_op jit(solution)/shard_map/ppermute | solution.py:46

commit v11 on v10

--- a/solution.py
+++ b/solution.py
@@ -338,7 +338,8 @@
         pairs = [(p * n_dp + d, (p ^ up) * n_dp + (d ^ over)) for p, d in places]
         return lax.ppermute(total, ("proto", "dp"), pairs)
 
-    steps = [(up, over) for up in range(0, n_proto, 2) for over in range(n_dp)][1:]
+    steps = [(up, 0) for up in range(2, n_proto, 2)]
+    steps += [(up, over) for over in range(1, n_dp) for up in range(n_proto - 2, -1, -2)]
     total = add_up(total, *[across(*step) for step in steps])
     if n_fsdp <= DIRECT:
         return add_up(total, *[swap(total, "fsdp", k) for k in range(1, n_fsdp)])
@@ -391,7 +392,7 @@
 def gradient(total, peak, weight_unit, weight_scale, units, exps):
     cols = exps.shape[0]
     rows, bot = units[0].shape
-    step = min(512, cols)
+    step = min(256, cols)
     args = (total, peak, weight_unit, weight_scale, *units, exps)
     return call(
         grad_kernel,

time: 47.5 us -> 47.9 us (level)
  waiting for transfers between devices: 10.2 us -> 10.7 us
  transfers between devices with their start and end apart: 16 -> 16, of which waited for: 10 -> 9; matrix products, arithmetic and copies ran while one was open for 0% -> 0% of each run, Pallas kernels for 25% -> 24%
where the time goes in v11:
time: 47.9 us; the launch traced here: 47.7 us
  starting transfers between devices  19.2 us (40%)
  Pallas kernels  17.1 us (36%)
  waiting for transfers between devices  10.7 us (22%)
  between operations  0.76 us (2%)
    pallas_call x14, Pallas kernels, call(): pl.pallas_call(kernel, out_shape=out_shape, compiler_params=pltpu.Compile...  17.1 us
    ppermute x13, starting transfers between devices, swap(): lax.ppermute(block, axis, [(i, i ^ apart) for i in range(lax.axis_size(ax...  15.6 us
    ppermute x13, waiting for transfers between devices, swap(): lax.ppermute(block, axis, [(i, i ^ apart) for i in range(lax.axis_size(ax...  7.52 us
    ppermute x3, starting transfers between devices, across(): return lax.ppermute(total, ('proto', 'dp'), pairs)  3.55 us
    ppermute x3, waiting for transfers between devices, across(): return lax.ppermute(total, ('proto', 'dp'), pairs)  3.23 us
  transfers between devices with their start and end apart: 16, of which 9 were waited for; matrix products, arithmetic and copies ran while one was open for 0% of the time, Pallas kernels for 24%

profile of v11, /device:TPU:0, one launch (start us, length us, event | category | flops | bytes accessed | tf_op | source)
XLA Modules:
  0.0 47.7 jit_solution(7915918533032738084)
XLA Ops:
  0.6 3.0 %collective-permute-start = (s32[1,256]{1,0:T(1,128)}, s32[1,256]{1,0:T(1,128)S(1)}, u32[]{:S(2)}, u32[]{:S(2)}) collective-permute-start(s32[1,256]{1,0:T(1,128)} %param.10), channel_id=1, source_target_pairs={{0,1},{1,0},{2,3},{3,2},{4,5},{5,4},{6,7},{7,6},{8,9},{9,8},{10,11... | collective-permute-start | bytes 3080 | tf_op jit(solution)/shard_map/ppermute | solution.py:46
  3.6 0.9 %fetch.1 = (bf16[192,128]{1,0:T(8,128)(2,1)S(1)}, bf16[192,256]{1,0:T(8,128)(2,1)S(1)}) custom-call(bf16[192,256]{1,0:T(8,128)(2,1)} %bitcast.7, bf16[192,256]{1,0:T(8,128)(2,1)} %bitcast.8), custom_call_target="tpu_custom_call" | custom-call | flops 1 | bytes 1 | tf_op jit(solution)/shard_map/fetch/pallas_call | solution.py:35
  4.6 0.8 %collective-permute-done.index_ref = s32[1,256]{1,0:T(1,128)S(1)} collective-permute-done((s32[1,256]{1,0:T(1,128)}, s32[1,256]{1,0:T(1,128)S(1)}, u32[]{:S(2)}, u32[]{:S(2)}) %collective-permute-start) | collective-permute-done | bytes 1056 | tf_op jit(solution)/shard_map/ppermute | solution.py:46
  5.6 2.1 %collective-permute-start.4 = (bf16[2,192,128]{2,1,0:T(8,128)(2,1)S(1)}, bf16[2,192,128]{2,1,0:T(8,128)(2,1)S(1)}, u32[]{:S(2)}, u32[]{:S(2)}) collective-permute-start(bf16[2,192,128]{2,1,0:T(8,128)(2,1)S(1)} %pack.1.refs_0_), channel_id=1, source_target_pairs={{0,1},{1,0},{2,3},{3,2},{4,5},{5,4},{6,7},{7,6},{8,9},{9,8},{10,11... | collective-permute-start | bytes 294920 | tf_op jit(solution)/shard_map/ppermute | solution.py:46
  7.7 3.6 %collective-permute-start.3 = (bf16[2,192,128]{2,1,0:T(8,128)(2,1)S(1)}, bf16[2,192,128]{2,1,0:T(8,128)(2,1)S(1)}, u32[]{:S(2)}, u32[]{:S(2)}) collective-permute-start(bf16[2,192,128]{2,1,0:T(8,128)(2,1)S(1)} %pack.1.refs_0_), channel_id=1, source_target_pairs={{0,24},{8,16},{16,8},{24,0},{1,25},{9,17},{17,9},{25,1},{2,26},{10... | collective-permute-start | bytes 294920 | tf_op jit(solution)/shard_map/ppermute | solution.py:46
  11.3 0.8 %collective-permute-start.1 = (bf16[2,192,128]{2,1,0:T(8,128)(2,1)S(1)}, bf16[2,192,128]{2,1,0:T(8,128)(2,1)S(1)}, u32[]{:S(2)}, u32[]{:S(2)}) collective-permute-start(bf16[2,192,128]{2,1,0:T(8,128)(2,1)S(1)} %pack.1.refs_0_), channel_id=1, source_target_pairs={{0,8},{8,0},{16,24},{24,16},{1,9},{9,1},{17,25},{25,17},{2,10},{10... | collective-permute-start | bytes 294920 | tf_op jit(solution)/shard_map/ppermute | solution.py:46
  12.0 3.6 %prep.1 = (f32[192,4096]{1,0:T(8,128)}, bf16[2048,256]{1,0:T(8,128)(2,1)S(1)}, bf16[2048,256]{1,0:T(8,128)(2,1)S(1)}, f32[192,2048]{1,0:T(8,128)S(1)}, f32[1,2048]{1,0:T(1,128)S(1)}, /*index=5*/f32[1,128]{1,0:T(1,128)S(1)}) custom-call(f32[192,4096]{1,0:T(8,128)} %teacher_hbm.3, f32[192,4096]{1,0:T(8,128)} %student_hbm.3, f32[1,16384]{1,0:T(1,128)} %bitcast.9), custom_call_target="tpu_custom_call" | custom-call | flops 1 | bytes 1 | tf_op jit(solution)/shard_map/prep/pallas_call | solution.py:35
  15.7 2.5 %collective-permute-done.2.refs_2_ = bf16[2,192,128]{2,1,0:T(8,128)(2,1)S(1)} collective-permute-done((bf16[2,192,128]{2,1,0:T(8,128)(2,1)S(1)}, bf16[2,192,128]{2,1,0:T(8,128)(2,1)S(1)}, u32[]{:S(2)}, u32[]{:S(2)}) %collective-permute-start.2) | collective-permute-done | bytes 98336 | tf_op jit(solution)/shard_map/ppermute | solution.py:46
  19.3 1.4 %scores.4 = (bf16[2048,4096]{1,0:T(8,128)(2,1)S(1)}, bf16[512,192]{1,0:T(8,128)(2,1)S(1)}, f32[2,512]{1,0:T(2,128)S(1)}) custom-call(bf16[4,2,192,128]{3,2,1,0:T(8,128)(2,1)S(1)} %get-tuple-element.29.refs_0_, bf16[2048,256]{1,0:T(8,128)(2,1)S(1)} %get-tuple-element.30.refs_1_.refs_4_, bf16[2048,256]{1,0:T(8,128)(2,1)S(1)} %get-tuple-element.31.refs_2_.refs_5_, ...), custom_call_target="tpu_custom_call" | custom-call | flops 1 | bytes 1 | tf_op jit(solution)/shard_map/scores/pallas_call | solution.py:35
  20.7 2.8 %rest.1 = (f32[192,4096]{1,0:T(8,128)}, f32[8,128]{1,0:T(8,128)S(1)}) custom-call(f32[192,4096]{1,0:T(8,128)} %teacher_hbm.3, f32[192,4096]{1,0:T(8,128)} %student_hbm.3, f32[2,512]{1,0:T(2,128)S(1)} %get-tuple-element.32.after.refs_0_, f32[192,4096]{1,0:T(8,128)} %get-tuple-element.33.before_hbm), custom_call_target="tpu_custom_call", output_to_operand_aliasing={{0}: (3, {})} | custom-call | flops 1 | bytes 1 | tf_op jit(solution)/shard_map/rest/pallas_call | solution.py:35
  23.5 0.7 %collective-permute-done.7.refs_2_ = bf16[2,2,192,128]{3,2,1,0:T(8,128)(2,1)S(1)} collective-permute-done((bf16[2,2,192,128]{3,2,1,0:T(8,128)(2,1)S(1)}, bf16[2,2,192,128]{3,2,1,0:T(8,128)(2,1)S(1)}, u32[]{:S(2)}, u32[]{:S(2)}) %collective-permute-start.7) | collective-permute-done | bytes 196640 | tf_op jit(solution)/shard_map/ppermute | solution.py:46
  24.3 1.5 %scores.5 = (bf16[2048,4096]{1,0:T(8,128)(2,1)S(1)}, bf16[512,192]{1,0:T(8,128)(2,1)S(1)}, f32[2,512]{1,0:T(2,128)S(1)}) custom-call(bf16[4,2,192,128]{3,2,1,0:T(8,128)(2,1)S(1)} %join.3.refs_0_, bf16[2048,256]{1,0:T(8,128)(2,1)S(1)} %get-tuple-element.30.refs_1_.refs_4_, ...), custom_call_target="tpu_custom_call", output_to_operand_aliasing={{0}: (4, {})} | custom-call | flops 1 | bytes 1 | tf_op jit(solution)/shard_map/scores/pallas_call | solution.py:35
  25.8 1.5 %scores.6 = (bf16[2048,4096]{1,0:T(8,128)(2,1)S(1)}, bf16[512,192]{1,0:T(8,128)(2,1)S(1)}, f32[2,512]{1,0:T(2,128)S(1)}) custom-call(bf16[4,2,192,128]{3,2,1,0:T(8,128)(2,1)S(1)} %collective-permute-done.5.refs_0_, bf16[2048,256]{1,0:T(8,128)(2,1)S(1)} %get-tuple-element.30.refs_1_.refs_4_, ...), custom_call_target="tpu_custom_call", output_to_operand_aliasing={{0}: (4, {})} | custom-call | flops 1 | bytes 1 | tf_op jit(solution)/shard_map/scores/pallas_call | solution.py:35
  27.3 1.5 %scores.7 = (bf16[2048,4096]{1,0:T(8,128)(2,1)S(1)}, bf16[512,192]{1,0:T(8,128)(2,1)S(1)}, f32[4,1024]{1,0:T(4,128)S(1)}) custom-call(f32[2,512]{1,0:T(2,128)S(1)} %get-tuple-element.32.after.refs_0_, f32[2,512]{1,0:T(2,128)S(1)} %get-tuple-element.39.refs_1_, f32[2,512]{1,0:T(2,128)S(1)} %get-tuple-element.40.refs_2_, ...), custom_call_target="tpu_custom_call", output_to_operand_aliasing={{0}: (7, {})} | custom-call | flops 1 | bytes 1 | tf_op jit(solution)/shard_map/scores/pallas_call | solution.py:35
  29.3 0.8 %collective-permute-done.9.refs_1_ = f32[4,1024]{1,0:T(4,128)S(1)} collective-permute-done((f32[4,1024]{1,0:T(4,128)S(1)}, f32[4,1024]{1,0:T(4,128)S(1)}, u32[]{:S(2)}, u32[]{:S(2)}) %collective-permute-start.9) | collective-permute-done | bytes 16416 | tf_op jit(solution)/shard_map/ppermute | solution.py:46
  30.2 1.2 %collective-permute-start.12 = (f32[4,1024]{1,0:T(4,128)S(1)}, f32[4,1024]{1,0:T(4,128)S(1)}, u32[]{:S(2)}, u32[]{:S(2)}) collective-permute-start(f32[4,1024]{1,0:T(4,128)S(1)} %relay.3.refs_0_), channel_id=1, source_target_pairs={{0,1},{1,0},{2,3},{3,2},{4,5},{5,4},{6,7},{7,6},{8,9},{9,8},{10,11... | collective-permute-start | bytes 49160 | tf_op jit(solution)/shard_map/ppermute | solution.py:339
  31.4 1.8 %collective-permute-start.11 = (f32[4,1024]{1,0:T(4,128)S(1)}, f32[4,1024]{1,0:T(4,128)S(1)}, u32[]{:S(2)}, u32[]{:S(2)}) collective-permute-start(f32[4,1024]{1,0:T(4,128)S(1)} %relay.3.refs_0_), channel_id=1, source_target_pairs={{0,5},{1,4},{2,7},{3,6},{4,1},{5,0},{6,3},{7,2},{8,13},{9,12},{10,... | collective-permute-start | bytes 49160 | tf_op jit(solution)/shard_map/ppermute | solution.py:339
  34.0 2.1 %collective-permute-done.11.refs_2_ = f32[4,1024]{1,0:T(4,128)S(1)} collective-permute-done((f32[4,1024]{1,0:T(4,128)S(1)}, f32[4,1024]{1,0:T(4,128)S(1)}, u32[]{:S(2)}, u32[]{:S(2)}) %collective-permute-start.11) | collective-permute-done | bytes 16416 | tf_op jit(solution)/shard_map/ppermute | solution.py:339
  36.1 0.9 %collective-permute-done.10.refs_1_ = f32[4,1024]{1,0:T(4,128)S(1)} collective-permute-done((f32[4,1024]{1,0:T(4,128)S(1)}, f32[4,1024]{1,0:T(4,128)S(1)}, u32[]{:S(2)}, u32[]{:S(2)}) %collective-permute-start.10) | collective-permute-done | bytes 16416 | tf_op jit(solution)/shard_map/ppermute | solution.py:339
  37.0 2.3 %collective-permute-start.15 = (f32[4,1024]{1,0:T(4,128)S(1)}, f32[4,1024]{1,0:T(4,128)S(1)}, u32[]{:S(2)}, u32[]{:S(2)}) collective-permute-start(f32[4,1024]{1,0:T(4,128)S(1)} %relay.4.refs_0_), channel_id=1, source_target_pairs={{0,24},{8,16},{16,8},{24,0},{1,25},{9,17},{17,9},{25,1},{2,26},{10... | collective-permute-start | bytes 49160 | tf_op jit(solution)/shard_map/ppermute | solution.py:46
  39.8 1.7 %collective-permute-start.13 = (f32[4,1024]{1,0:T(4,128)S(1)}, f32[4,1024]{1,0:T(4,128)S(1)}, u32[]{:S(2)}, u32[]{:S(2)}) collective-permute-start(f32[4,1024]{1,0:T(4,128)S(1)} %relay.4.refs_0_), channel_id=1, source_target_pairs={{0,8},{8,0},{16,24},{24,16},{1,9},{9,1},{17,25},{25,17},{2,10},{10... | collective-permute-start | bytes 49160 | tf_op jit(solution)/shard_map/ppermute | solution.py:46
  41.5 1.1 %collective-permute-done.15.refs_3_ = f32[4,1024]{1,0:T(4,128)S(1)} collective-permute-done((f32[4,1024]{1,0:T(4,128)S(1)}, f32[4,1024]{1,0:T(4,128)S(1)}, u32[]{:S(2)}, u32[]{:S(2)}) %collective-permute-start.15) | collective-permute-done | bytes 16416 | tf_op jit(solution)/shard_map/ppermute | solution.py:46
  42.6 1.5 %collective-permute-done.14.refs_2_ = f32[4,1024]{1,0:T(4,128)S(1)} collective-permute-done((f32[4,1024]{1,0:T(4,128)S(1)}, f32[4,1024]{1,0:T(4,128)S(1)}, u32[]{:S(2)}, u32[]{:S(2)}) %collective-permute-start.14) | collective-permute-done | bytes 16416 | tf_op jit(solution)/shard_map/ppermute | solution.py:46
  44.1 3.6 %gradient.1 = f32[192,2048]{1,0:T(8,128)} custom-call(f32[4,1024]{1,0:T(4,128)S(1)} %relay.5.total_ref, f32[1,128]{1,0:T(1,128)S(1)} %get-tuple-element.28.refs_5_.refs_3_.refs_6_.peak_ref, f32[192,2048]{1,0:T(8,128)S(1)} %get-tuple-element.43.weight_unit, f32[1,2048]{1,0:T(1,128)S(1)} %get-tuple-element.44.weight_scale, ...), custom_call_target="tpu_custom_call" | custom-call | flops 1 | bytes 1 | tf_op jit(solution)/shard_map/gradient/pallas_call | solution.py:35
  (22 shorter events, 3.3 us)
Async XLA Ops:
  0.6 4.8 %collective-permute-start = (s32[1,256]{1,0:T(1,128)}, s32[1,256]{1,0:T(1,128)S(1)}, u32[]{:S(2)}, u32[]{:S(2)}) collective-permute-start(s32[1,256]{1,0:T(1,128)} %param.10), channel_id=1, source_target_pairs={{0,1},{1,0},{2,3},{3,2},{4,5},{5,4},{6,7},{7,6},{8,9},{9,8},{10,11... | collective-permute-start | bytes 3080 | tf_op jit(solution)/shard_map/ppermute | solution.py:46
  5.6 10.1 %collective-permute-start.4 = (bf16[2,192,128]{2,1,0:T(8,128)(2,1)S(1)}, bf16[2,192,128]{2,1,0:T(8,128)(2,1)S(1)}, u32[]{:S(2)}, u32[]{:S(2)}) collective-permute-start(bf16[2,192,128]{2,1,0:T(8,128)(2,1)S(1)} %pack.1.refs_0_), channel_id=1, source_target_pairs={{0,1},{1,0},{2,3},{3,2},{4,5},{5,4},{6,7},{7,6},{8,9},{9,8},{10,11... | collective-permute-start | bytes 294920 | tf_op jit(solution)/shard_map/ppermute | solution.py:46
  7.7 8.0 %collective-permute-start.3 = (bf16[2,192,128]{2,1,0:T(8,128)(2,1)S(1)}, bf16[2,192,128]{2,1,0:T(8,128)(2,1)S(1)}, u32[]{:S(2)}, u32[]{:S(2)}) collective-permute-start(bf16[2,192,128]{2,1,0:T(8,128)(2,1)S(1)} %pack.1.refs_0_), channel_id=1, source_target_pairs={{0,24},{8,16},{16,8},{24,0},{1,25},{9,17},{17,9},{25,1},{2,26},{10... | collective-permute-start | bytes 294920 | tf_op jit(solution)/shard_map/ppermute | solution.py:46
  11.2 6.9 %collective-permute-start.2 = (bf16[2,192,128]{2,1,0:T(8,128)(2,1)S(1)}, bf16[2,192,128]{2,1,0:T(8,128)(2,1)S(1)}, u32[]{:S(2)}, u32[]{:S(2)}) collective-permute-start(bf16[2,192,128]{2,1,0:T(8,128)(2,1)S(1)} %pack.1.refs_0_), channel_id=1, source_target_pairs={{0,16},{8,24},{16,0},{24,8},{1,17},{9,25},{17,1},{25,9},{2,18},{10... | collective-permute-start | bytes 294920 | tf_op jit(solution)/shard_map/ppermute | solution.py:46
  11.3 6.9 %collective-permute-start.1 = (bf16[2,192,128]{2,1,0:T(8,128)(2,1)S(1)}, bf16[2,192,128]{2,1,0:T(8,128)(2,1)S(1)}, u32[]{:S(2)}, u32[]{:S(2)}) collective-permute-start(bf16[2,192,128]{2,1,0:T(8,128)(2,1)S(1)} %pack.1.refs_0_), channel_id=1, source_target_pairs={{0,8},{8,0},{16,24},{24,16},{1,9},{9,1},{17,25},{25,17},{2,10},{10... | collective-permute-start | bytes 294920 | tf_op jit(solution)/shard_map/ppermute | solution.py:46
  18.3 6.0 %collective-permute-start.7 = (bf16[2,2,192,128]{3,2,1,0:T(8,128)(2,1)S(1)}, bf16[2,2,192,128]{3,2,1,0:T(8,128)(2,1)S(1)}, u32[]{:S(2)}, u32[]{:S(2)}) collective-permute-start(bf16[2,2,192,128]{3,2,1,0:T(8,128)(2,1)S(1)} %get-tuple-element.35), channel_id=1, source_target_pairs={{0,1},{1,0},{2,3},{3,2},{4,5},{5,4},{6,7},{7,6},{8,9},{9,8},{10,11... | collective-permute-start | bytes 589832 | tf_op jit(solution)/shard_map/ppermute | solution.py:46
  18.8 4.7 %collective-permute-start.6 = (bf16[2,192,128]{2,1,0:T(8,128)(2,1)S(1)}, bf16[2,192,128]{2,1,0:T(8,128)(2,1)S(1)}, u32[]{:S(2)}, u32[]{:S(2)}) collective-permute-start(bf16[2,192,128]{2,1,0:T(8,128)(2,1)S(1)} %collective-permute-done.4.refs_4_.refs_0_), channel_id=1, source_target_pairs={{0,8},{8,0},{16,24},{24,16},{1,9},{9,1},{17,25},{25,17},{2,10},{10... | collective-permute-start | bytes 294920 | tf_op jit(solution)/shard_map/ppermute | solution.py:46
  19.3 6.5 %collective-permute-start.5 = (bf16[4,2,192,128]{3,2,1,0:T(8,128)(2,1)S(1)}, bf16[4,2,192,128]{3,2,1,0:T(8,128)(2,1)S(1)}, u32[]{:S(2)}, u32[]{:S(2)}) collective-permute-start(bf16[4,2,192,128]{3,2,1,0:T(8,128)(2,1)S(1)} %get-tuple-element.29.refs_0_), channel_id=1, source_target_pairs={{0,2},{2,0},{4,6},{6,4},{1,3},{3,1},{5,7},{7,5},{8,10},{10,8},{12,... | collective-permute-start | bytes 1179656 | tf_op jit(solution)/shard_map/ppermute | solution.py:46
  24.3 3.0 %collective-permute-start.8 = (bf16[4,2,192,128]{3,2,1,0:T(8,128)(2,1)S(1)}, bf16[4,2,192,128]{3,2,1,0:T(8,128)(2,1)S(1)}, u32[]{:S(2)}, u32[]{:S(2)}) collective-permute-start(bf16[4,2,192,128]{3,2,1,0:T(8,128)(2,1)S(1)} %join.3.refs_0_), channel_id=1, source_target_pairs={{0,2},{2,0},{4,6},{6,4},{1,3},{3,1},{5,7},{7,5},{8,10},{10,8},{12,... | collective-permute-start | bytes 1179656 | tf_op jit(solution)/shard_map/ppermute | solution.py:46
  28.8 1.4 %collective-permute-start.9 = (f32[4,1024]{1,0:T(4,128)S(1)}, f32[4,1024]{1,0:T(4,128)S(1)}, u32[]{:S(2)}, u32[]{:S(2)}) collective-permute-start(f32[4,1024]{1,0:T(4,128)S(1)} %get-tuple-element.42.refs_0_), channel_id=1, source_target_pairs={{0,2},{2,0},{4,6},{6,4},{1,3},{3,1},{5,7},{7,5},{8,10},{10,8},{12,... | collective-permute-start | bytes 49160 | tf_op jit(solution)/shard_map/ppermute | solution.py:46
  30.2 3.8 %collective-permute-start.12 = (f32[4,1024]{1,0:T(4,128)S(1)}, f32[4,1024]{1,0:T(4,128)S(1)}, u32[]{:S(2)}, u32[]{:S(2)}) collective-permute-start(f32[4,1024]{1,0:T(4,128)S(1)} %relay.3.refs_0_), channel_id=1, source_target_pairs={{0,1},{1,0},{2,3},{3,2},{4,5},{5,4},{6,7},{7,6},{8,9},{9,8},{10,11... | collective-permute-start | bytes 49160 | tf_op jit(solution)/shard_map/ppermute | solution.py:339
  31.4 4.6 %collective-permute-start.11 = (f32[4,1024]{1,0:T(4,128)S(1)}, f32[4,1024]{1,0:T(4,128)S(1)}, u32[]{:S(2)}, u32[]{:S(2)}) collective-permute-start(f32[4,1024]{1,0:T(4,128)S(1)} %relay.3.refs_0_), channel_id=1, source_target_pairs={{0,5},{1,4},{2,7},{3,6},{4,1},{5,0},{6,3},{7,2},{8,13},{9,12},{10,... | collective-permute-start | bytes 49160 | tf_op jit(solution)/shard_map/ppermute | solution.py:339
  33.2 3.7 %collective-permute-start.10 = (f32[4,1024]{1,0:T(4,128)S(1)}, f32[4,1024]{1,0:T(4,128)S(1)}, u32[]{:S(2)}, u32[]{:S(2)}) collective-permute-start(f32[4,1024]{1,0:T(4,128)S(1)} %relay.3.refs_0_), channel_id=1, source_target_pairs={{0,4},{1,5},{2,6},{3,7},{4,0},{5,1},{6,2},{7,3},{8,12},{9,13},{10,... | collective-permute-start | bytes 49160 | tf_op jit(solution)/shard_map/ppermute | solution.py:339
  37.0 5.6 %collective-permute-start.15 = (f32[4,1024]{1,0:T(4,128)S(1)}, f32[4,1024]{1,0:T(4,128)S(1)}, u32[]{:S(2)}, u32[]{:S(2)}) collective-permute-start(f32[4,1024]{1,0:T(4,128)S(1)} %relay.4.refs_0_), channel_id=1, source_target_pairs={{0,24},{8,16},{16,8},{24,0},{1,25},{9,17},{17,9},{25,1},{2,26},{10... | collective-permute-start | bytes 49160 | tf_op jit(solution)/shard_map/ppermute | solution.py:46
  39.3 4.8 %collective-permute-start.14 = (f32[4,1024]{1,0:T(4,128)S(1)}, f32[4,1024]{1,0:T(4,128)S(1)}, u32[]{:S(2)}, u32[]{:S(2)}) collective-permute-start(f32[4,1024]{1,0:T(4,128)S(1)} %relay.4.refs_0_), channel_id=1, source_target_pairs={{0,16},{8,24},{16,0},{24,8},{1,17},{9,25},{17,1},{25,9},{2,18},{10... | collective-permute-start | bytes 49160 | tf_op jit(solution)/shard_map/ppermute | solution.py:46
  39.8 4.3 %collective-permute-start.13 = (f32[4,1024]{1,0:T(4,128)S(1)}, f32[4,1024]{1,0:T(4,128)S(1)}, u32[]{:S(2)}, u32[]{:S(2)}) collective-permute-start(f32[4,1024]{1,0:T(4,128)S(1)} %relay.4.refs_0_), channel_id=1, source_target_pairs={{0,8},{8,0},{16,24},{24,16},{1,9},{9,1},{17,25},{25,17},{2,10},{10... | collective-permute-start | bytes 49160 | tf_op jit(solution)/shard_map/ppermute | solution.py:46

commit v12 on v10

--- a/solution.py
+++ b/solution.py
@@ -130,49 +130,45 @@
     )
 
 
-def rest_kernel(teacher_hbm, student_hbm, after, before_hbm, new_hbm, done_ref, *scratch):
+def rest_kernel(lo, hi, own, teacher_hbm, student_hbm, after, before_hbm, new_hbm, done_ref, *scratch):
     teacher_buf, student_buf, new_buf, in_t, in_s, out = scratch
-    chunks, bot, width = new_buf.shape
-    own = chunks * width
+    width = hi - lo
     parts = teacher_hbm.shape[1] // own - 1
     dp = here()[0]
     done_ref[...] = jnp.zeros_like(done_ref)
-    for part in range(parts):
-        first = lax.rem(dp + 1 + part, parts + 1) * own
-        far = [pl.ds(pl.multiple_of(first + i * width, width), width) for i in range(chunks)]
-        loads = [
-            (
-                pltpu.make_async_copy(teacher_hbm.at[:, far[i]], teacher_buf.at[i], in_t.at[i]),
-                pltpu.make_async_copy(student_hbm.at[:, far[i]], student_buf.at[i], in_s.at[i]),
-            )
-            for i in range(chunks)
-        ]
-        stores = [pltpu.make_async_copy(new_buf.at[i], new_hbm.at[:, far[i]], out.at[i]) for i in range(chunks)]
-        for pair in loads:
-            for load in pair:
-                load.start()
-        for i in range(chunks):
-            for load in loads[i]:
-                load.wait()
-            new_buf[i] = 0.994 * teacher_buf[i] + 0.006 * student_buf[i]
-            stores[i].start()
-        for store in stores:
-            store.wait()
-
-
-def update_rest(teacher_weight, student_weight, after, new, own):
+    far = [pl.ds(pl.multiple_of(lax.rem(dp + 1 + i, parts + 1) * own + lo, 128), width) for i in range(parts)]
+    loads = [
+        (
+            pltpu.make_async_copy(teacher_hbm.at[:, far[i]], teacher_buf.at[i], in_t.at[i]),
+            pltpu.make_async_copy(student_hbm.at[:, far[i]], student_buf.at[i], in_s.at[i]),
+        )
+        for i in range(parts)
+    ]
+    stores = [pltpu.make_async_copy(new_buf.at[i], new_hbm.at[:, far[i]], out.at[i]) for i in range(parts)]
+    for pair in loads:
+        for load in pair:
+            load.start()
+    for i in range(parts):
+        for load in loads[i]:
+            load.wait()
+        new_buf[i] = 0.994 * teacher_buf[i] + 0.006 * student_buf[i]
+        stores[i].start()
+    for store in stores:
+        store.wait()
+
+
+def update_rest(teacher_weight, student_weight, after, new, own, lo, hi):
     bot, cols = teacher_weight.shape
-    width = min(512, own)
-    chunks = own // width
+    parts = cols // own - 1
     return call(
-        rest_kernel,
+        functools.partial(rest_kernel, lo, hi, own),
         "rest",
         [pltpu.HBM((bot, cols), jnp.float32), held(8, 128)],
         (teacher_weight, student_weight, after, new),
         in_specs=[IN_HBM] * 4,
         out_specs=[IN_HBM, ON_CHIP],
         input_output_aliases={3: 0},
-        scratch_shapes=[held(chunks, bot, width)] * 3 + [pltpu.SemaphoreType.DMA((chunks,))] * 3,
+        scratch_shapes=[held(parts, bot, hi - lo)] * 3 + [pltpu.SemaphoreType.DMA((parts,))] * 3,
     )
 
 
@@ -216,21 +212,23 @@
     return call(pack_kernel, "pack", held(2, bot, half, dtype=jnp.bfloat16), (student, teacher, index))
 
 
-def join_kernel(n_in, n_after, *refs):
+def join_kernel(n_in, n_after, firsts, bot, *refs):
     blocks = []
     for ref in refs[:n_in]:
         blocks += [ref] if len(ref.shape) == 3 else [ref.at[i] for i in range(ref.shape[0])]
-    for ref in refs[n_in + n_after:]:
-        skip = len(blocks) - ref.shape[0]
+    for first, ref in zip(firsts, refs[n_in + n_after:]):
         for i in range(ref.shape[0]):
-            ref[i] = blocks[skip + i][...]
-
-
-def join(parts, counts, after):
-    block = parts[0].shape[-3:]
-    outs = [held(count, *block, dtype=jnp.bfloat16) for count in counts]
-    kernel = functools.partial(join_kernel, len(parts), len(after))
-    return call(kernel, "join", outs, (*parts, *after), in_specs=[ON_CHIP] * len(parts) + [IN_HBM] * len(after))
+            block = blocks[first + i][:, :bot, :]
+            ref[i, :, :bot, :] = block
+            if ref.shape[2] > bot:
+                ref[i, :, bot:, :] = block[:, :ref.shape[2] - bot]
+
+
+def join(parts, outs, after, bot):
+    width = parts[0].shape[-1]
+    shapes = [held(count, 2, rows, width, dtype=jnp.bfloat16) for _, count, rows in outs]
+    kernel = functools.partial(join_kernel, len(parts), len(after), [first for first, _, _ in outs], bot)
+    return call(kernel, "join", shapes, (*parts, *after), in_specs=[ON_CHIP] * len(parts) + [IN_HBM] * len(after))
 
 
 def log_sum(parts):
@@ -247,13 +245,14 @@
     return lax.axis_index("fsdp") ^ k if n <= DIRECT else k
 
 
-def score_kernel(part, *refs):
+def score_kernel(part, n_feats, *refs):
     last = part == 3
     before, refs = (refs[:3], refs[3:]) if last else ((), refs)
-    feats_ref, ws_ref, wt_ref, peak_ref, *refs = refs
+    feats_refs, (ws_ref, wt_ref, peak_ref, *refs) = refs[:n_feats], refs[n_feats:]
+    blocks = [ref.at[i] for ref in feats_refs for i in range(ref.shape[0])]
     exp_ref, unit_ref, total_ref, *mine = refs[1:] if part else refs
     own_ref = mine[0] if last else total_ref
-    n, _, bot, width = feats_ref.shape
+    n, (_, bot, width) = len(blocks), blocks[0].shape
     cols = ws_ref.shape[0]
     step = min(STEP, cols)
     per = max(1, min(n, GROUP // width))
@@ -262,7 +261,7 @@
         base = (2 * part + which) * n * width
         extra = jnp.where(row < 3 * which, 1.0, 0.0).astype(jnp.bfloat16)
         for group in range(n // per):
-            values = [feats_ref[group * per + k, which].astype(jnp.float32) for k in range(per)]
+            values = [blocks[group * per + k][which].astype(jnp.float32) for k in range(per)]
             values = jnp.concatenate(values, axis=1)
             unit = (values * lax.rsqrt(jnp.sum(values * values, axis=0, keepdims=True) + EPS)).astype(jnp.bfloat16)
             lanes = slice(group * per * width, (group + 1) * per * width)
@@ -300,11 +299,11 @@
 
 
 def scores(part, feats, weights, before=(), exps=None):
-    n, _, bot, width = feats.shape
-    cols, rows = weights[0].shape[0], n * width
-    args = (*before, feats, *weights, *([exps] if part else []))
+    _, _, bot, width = feats[0].shape
+    cols, rows = weights[0].shape[0], sum(part.shape[0] for part in feats) * width
+    args = (*before, *feats, *weights, *([exps] if part else []))
     return call(
-        functools.partial(score_kernel, part),
+        functools.partial(score_kernel, part, len(feats)),
         "scores",
         [
             held(cols, 8 * rows, dtype=jnp.bfloat16),
@@ -318,33 +317,31 @@
     )
 
 
-def relay_kernel(*refs):
-    parts = [ref[...] for ref in refs[:-1]]
+def relay_kernel(n_in, *refs):
+    parts = [ref[...] for ref in refs[:n_in]]
     if len(parts[0].shape) == 3:
         parts = [parts[0][i] for i in range(parts[0].shape[0])]
     refs[-1][...] = jnp.concatenate(combine(parts), axis=0)
 
 
-def add_up(total, *others):
-    return call(relay_kernel, "relay", held(*total.shape), [total, *others])
-
-
-def add_up_all(total):
-    n_proto, n_dp, n_fsdp = [lax.axis_size(axis) for axis in ("proto", "dp", "fsdp")]
-    total = add_up(total, swap(total, "proto"))
-
-    def across(up, over):
-        places = [(p, d) for p in range(n_proto) for d in range(n_dp)]
-        pairs = [(p * n_dp + d, (p ^ up) * n_dp + (d ^ over)) for p, d in places]
-        return lax.ppermute(total, ("proto", "dp"), pairs)
-
-    steps = [(up, over) for up in range(0, n_proto, 2) for over in range(n_dp)][1:]
-    total = add_up(total, *[across(*step) for step in steps])
-    if n_fsdp <= DIRECT:
-        return add_up(total, *[swap(total, "fsdp", k) for k in range(1, n_fsdp)])
-    copies = jnp.broadcast_to(total[None], (n_fsdp, *total.shape))
-    parts = lax.all_to_all(copies, "fsdp", 0, 0, tiled=True)
-    return call(relay_kernel, "relay", held(*total.shape), [parts])
+def add_up(parts, *after):
+    specs = [ON_CHIP] * len(parts) + [IN_HBM] * len(after)
+    out = held(*parts[0].shape[-2:])
+    return call(functools.partial(relay_kernel, len(parts)), "relay", out, (*parts, *after), in_specs=specs)
+
+
+def across(total, up, over):
+    n_proto, n_dp = lax.axis_size("proto"), lax.axis_size("dp")
+    places = [(p, d) for p in range(n_proto) for d in range(n_dp)]
+    pairs = [(p * n_dp + d, (p ^ up) * n_dp + (d ^ over)) for p, d in places]
+    return lax.ppermute(total, ("proto", "dp"), pairs)
+
+
+def along_fsdp(total):
+    n = lax.axis_size("fsdp")
+    if n <= DIRECT:
+        return [total, *[swap(total, "fsdp", k) for k in range(1, n)]]
+    return [lax.all_to_all(jnp.broadcast_to(total[None], (n, *total.shape)), "fsdp", 0, 0, tiled=True)]
 
 
 def grad_kernel(total_ref, peak_ref, weight_unit, weight_scale, *refs):
@@ -412,21 +409,30 @@
     mine = pack(*fetch(in_hbm(student_feats[0].T), in_hbm(teacher_feats[0].T)), index)
     new, wt, ws, unit, scale, peak = prepare(teacher_weight, student_weight, center, n_dp)
     weights = (ws, wt, peak)
+    bot = mine.shape[1]
     if n_fsdp <= DIRECT:
         other = [swap(mine, "dp")]
         along = [swap(mine, "fsdp", k) for k in range(1, n_fsdp)]
-        own, far = join([mine, *along], [n_fsdp, n_fsdp - 2], (other[0], peak))
+        half = n_fsdp // 2
+        outs = [(0, n_fsdp, bot), (2, n_fsdp - 2, bot + 16), (0, half, bot), (half, half, bot)]
+        own, far, *halves = join([mine, *along], outs, (other[0], peak), bot)
         other += [swap(other[0], "fsdp"), swap(far, "dp")]
     else:
         own = lax.all_to_all(jnp.broadcast_to(mine[None], (n_fsdp, *mine.shape)), "fsdp", 0, 0, tiled=True)
-        other = [swap(own, "dp")]
-    exps, unit_a, total_a = scores(0, own, weights)
-    teacher_new, done = update_rest(teacher_weight, student_weight, total_a, new, ws.shape[0])
-    (other,) = join(other, [n_fsdp], (done,))
-    exps, unit_c, total_c = scores(2, other, weights, exps=exps)
-    exps, unit_b, total_b = scores(1, swap(own, "proto"), weights, exps=exps)
-    exps, unit_d, total = scores(3, swap(other, "proto"), weights, (total_a, total_b, total_c), exps)
-    total = add_up_all(total)
+        other, halves = [swap(own, "dp")], [own]
+    exps, unit_a, total_a = scores(0, [own], weights)
+    exps, unit_b, total_b = scores(1, [swap(half, "proto") for half in halves], weights, exps=exps)
+    (other,) = join(other, [(0, n_fsdp, bot)], (total_b,), bot)
+    exps, unit_c, total_c = scores(2, [other], weights, exps=exps)
+    exps, unit_d, total = scores(3, [swap(other, "proto")], weights, (total_a, total_b, total_c), exps)
+    n_proto, own_cols = lax.axis_size("proto"), ws.shape[0]
+    middle = own_cols // 2
+    total = add_up([total, swap(total, "proto")])
+    new, done = update_rest(teacher_weight, student_weight, total, new, own_cols, 0, middle)
+    steps = [(up, over) for up in range(0, n_proto, 2) for over in range(n_dp)][1:]
+    total = add_up([total, *[across(total, *step) for step in steps]], done)
+    teacher_new, done = update_rest(teacher_weight, student_weight, total, new, own_cols, middle, own_cols)
+    total = add_up(along_fsdp(total), done)
     student_grad = gradient(total, peak, unit, scale, (unit_a, unit_b, unit_c, unit_d), exps)
     return (teacher_new, student_grad)
 

time: 47.5 us -> 46.6 us (0.981)
  waiting for transfers between devices: 10.2 us -> 6.82 us
  Pallas kernels: 17.2 us -> 19.3 us
    ppermute x3, waiting for transfers between devices: 2.87 us -> 0.26 us  [across(): return lax.ppermute(total, ('proto', 'dp'), pairs)]
    pallas_call x14 -> x15, Pallas kernels: 17.2 us -> 19.3 us  [call(): pl.pallas_call(kernel, out_shape=out_shape, compiler_params=pltpu.Compile...]
    ppermute x13 -> x14, waiting for transfers between devices: 7.36 us -> 6.56 us  [swap(): lax.ppermute(block, axis, [(i, i ^ apart) for i in range(lax.axis_size(ax...]
    ppermute x13 -> x14, starting transfers between devices: 15.6 us -> 15.9 us  [swap(): lax.ppermute(block, axis, [(i, i ^ apart) for i in range(lax.axis_size(ax...]
  transfers between devices with their start and end apart: 16 -> 17, of which waited for: 10 -> 8; matrix products, arithmetic and copies ran while one was open for 0% -> 0% of each run, Pallas kernels for 25% -> 30%
where the time goes in v12:
time: 46.6 us; the launch traced here: 46.4 us
  starting transfers between devices  19.4 us (42%)
  Pallas kernels  19.3 us (41%)
  waiting for transfers between devices  6.82 us (15%)
  between operations  0.79 us (2%)
    pallas_call x15, Pallas kernels, call(): pl.pallas_call(kernel, out_shape=out_shape, compiler_params=pltpu.Compile...  19.3 us
    ppermute x14, starting transfers between devices, swap(): lax.ppermute(block, axis, [(i, i ^ apart) for i in range(lax.axis_size(ax...  15.9 us
    ppermute x14, waiting for transfers between devices, swap(): lax.ppermute(block, axis, [(i, i ^ apart) for i in range(lax.axis_size(ax...  6.56 us
    ppermute x3, starting transfers between devices, across(): return lax.ppermute(total, ('proto', 'dp'), pairs)  3.55 us
  transfers between devices with their start and end apart: 17, of which 8 were waited for; matrix products, arithmetic and copies ran while one was open for 0% of the time, Pallas kernels for 30%

profile of v12, /device:TPU:0, one launch (start us, length us, event | category | flops | bytes accessed | tf_op | source)
XLA Modules:
  0.0 46.4 jit_solution(795754282958431503)
XLA Ops:
  0.6 3.0 %collective-permute-start = (s32[1,256]{1,0:T(1,128)}, s32[1,256]{1,0:T(1,128)S(1)}, u32[]{:S(2)}, u32[]{:S(2)}) collective-permute-start(s32[1,256]{1,0:T(1,128)} %param.10), channel_id=1, source_target_pairs={{0,1},{1,0},{2,3},{3,2},{4,5},{5,4},{6,7},{7,6},{8,9},{9,8},{10,11... | collective-permute-start | bytes 3080 | tf_op jit(solution)/shard_map/ppermute | solution.py:46
  3.6 0.9 %fetch.1 = (bf16[192,128]{1,0:T(8,128)(2,1)S(1)}, bf16[192,256]{1,0:T(8,128)(2,1)S(1)}) custom-call(bf16[192,256]{1,0:T(8,128)(2,1)} %bitcast.7, bf16[192,256]{1,0:T(8,128)(2,1)} %bitcast.8), custom_call_target="tpu_custom_call" | custom-call | flops 1 | bytes 1 | tf_op jit(solution)/shard_map/fetch/pallas_call | solution.py:35
  4.6 0.8 %collective-permute-done.index_ref = s32[1,256]{1,0:T(1,128)S(1)} collective-permute-done((s32[1,256]{1,0:T(1,128)}, s32[1,256]{1,0:T(1,128)S(1)}, u32[]{:S(2)}, u32[]{:S(2)}) %collective-permute-start) | collective-permute-done | bytes 1056 | tf_op jit(solution)/shard_map/ppermute | solution.py:46
  5.6 2.1 %collective-permute-start.4 = (bf16[2,192,128]{2,1,0:T(8,128)(2,1)S(1)}, bf16[2,192,128]{2,1,0:T(8,128)(2,1)S(1)}, u32[]{:S(2)}, u32[]{:S(2)}) collective-permute-start(bf16[2,192,128]{2,1,0:T(8,128)(2,1)S(1)} %pack.1.refs_0_), channel_id=1, source_target_pairs={{0,1},{1,0},{2,3},{3,2},{4,5},{5,4},{6,7},{7,6},{8,9},{9,8},{10,11... | collective-permute-start | bytes 294920 | tf_op jit(solution)/shard_map/ppermute | solution.py:46
  7.7 3.6 %collective-permute-start.3 = (bf16[2,192,128]{2,1,0:T(8,128)(2,1)S(1)}, bf16[2,192,128]{2,1,0:T(8,128)(2,1)S(1)}, u32[]{:S(2)}, u32[]{:S(2)}) collective-permute-start(bf16[2,192,128]{2,1,0:T(8,128)(2,1)S(1)} %pack.1.refs_0_), channel_id=1, source_target_pairs={{0,24},{8,16},{16,8},{24,0},{1,25},{9,17},{17,9},{25,1},{2,26},{10... | collective-permute-start | bytes 294920 | tf_op jit(solution)/shard_map/ppermute | solution.py:46
  11.3 0.8 %collective-permute-start.1 = (bf16[2,192,128]{2,1,0:T(8,128)(2,1)S(1)}, bf16[2,192,128]{2,1,0:T(8,128)(2,1)S(1)}, u32[]{:S(2)}, u32[]{:S(2)}) collective-permute-start(bf16[2,192,128]{2,1,0:T(8,128)(2,1)S(1)} %pack.1.refs_0_), channel_id=1, source_target_pairs={{0,8},{8,0},{16,24},{24,16},{1,9},{9,1},{17,25},{25,17},{2,10},{10... | collective-permute-start | bytes 294920 | tf_op jit(solution)/shard_map/ppermute | solution.py:46
  12.0 3.6 %prep.1 = (f32[192,4096]{1,0:T(8,128)}, bf16[2048,256]{1,0:T(8,128)(2,1)S(1)}, bf16[2048,256]{1,0:T(8,128)(2,1)S(1)}, f32[192,2048]{1,0:T(8,128)S(1)}, f32[1,2048]{1,0:T(1,128)S(1)}, /*index=5*/f32[1,128]{1,0:T(1,128)S(1)}) custom-call(f32[192,4096]{1,0:T(8,128)} %teacher_hbm.5, f32[192,4096]{1,0:T(8,128)} %student_hbm.5, f32[1,16384]{1,0:T(1,128)} %bitcast.9), custom_call_target="tpu_custom_call" | custom-call | flops 1 | bytes 1 | tf_op jit(solution)/shard_map/prep/pallas_call | solution.py:35
  15.7 2.5 %collective-permute-done.2.refs_2_ = bf16[2,192,128]{2,1,0:T(8,128)(2,1)S(1)} collective-permute-done((bf16[2,192,128]{2,1,0:T(8,128)(2,1)S(1)}, bf16[2,192,128]{2,1,0:T(8,128)(2,1)S(1)}, u32[]{:S(2)}, u32[]{:S(2)}) %collective-permute-start.2) | collective-permute-done | bytes 98336 | tf_op jit(solution)/shard_map/ppermute | solution.py:46
  18.3 0.6 %collective-permute-start.8 = (bf16[2,2,208,128]{3,2,1,0:T(8,128)(2,1)S(1)}, bf16[2,2,208,128]{3,2,1,0:T(8,128)(2,1)S(1)}, u32[]{:S(2)}, u32[]{:S(2)}) collective-permute-start(bf16[2,2,208,128]{3,2,1,0:T(8,128)(2,1)S(1)} %get-tuple-element.41), channel_id=1, source_target_pairs={{0,1},{1,0},{2,3},{3,2},{4,5},{5,4},{6,7},{7,6},{8,9},{9,8},{10,11... | collective-permute-start | bytes 638984 | tf_op jit(solution)/shard_map/ppermute | solution.py:46
  18.9 0.5 %collective-permute-start.6 = (bf16[2,2,192,128]{3,2,1,0:T(8,128)(2,1)S(1)}, bf16[2,2,192,128]{3,2,1,0:T(8,128)(2,1)S(1)}, u32[]{:S(2)}, u32[]{:S(2)}) collective-permute-start(bf16[2,2,192,128]{3,2,1,0:T(8,128)(2,1)S(1)} %get-tuple-element.38), channel_id=1, source_target_pairs={{0,2},{2,0},{4,6},{6,4},{1,3},{3,1},{5,7},{7,5},{8,10},{10,8},{12,... | collective-permute-start | bytes 589832 | tf_op jit(solution)/shard_map/ppermute | solution.py:46
  19.8 1.5 %scores.4 = (bf16[2048,4096]{1,0:T(8,128)(2,1)S(1)}, bf16[512,192]{1,0:T(8,128)(2,1)S(1)}, f32[2,512]{1,0:T(2,128)S(1)}) custom-call(bf16[4,2,192,128]{3,2,1,0:T(8,128)(2,1)S(1)} %get-tuple-element.33.refs_0_, bf16[2048,256]{1,0:T(8,128)(2,1)S(1)} %get-tuple-element.34.refs_1_.refs_2_.refs_4_, ...), custom_call_target="tpu_custom_call" | custom-call | flops 1 | bytes 1 | tf_op jit(solution)/shard_map/scores/pallas_call | solution.py:35
  21.3 1.5 %scores.5 = (bf16[2048,4096]{1,0:T(8,128)(2,1)S(1)}, bf16[512,192]{1,0:T(8,128)(2,1)S(1)}, f32[2,512]{1,0:T(2,128)S(1)}) custom-call(bf16[2,2,192,128]{3,2,1,0:T(8,128)(2,1)S(1)} %collective-permute-done.5.refs_0_, bf16[2,2,192,128]{3,2,1,0:T(8,128)(2,1)S(1)} %collective-permute-done.6.refs_1_, ...), custom_call_target="tpu_custom_call", output_to_operand_aliasing={{0}: (5, {})} | custom-call | flops 1 | bytes 1 | tf_op jit(solution)/shard_map/scores/pallas_call | solution.py:35
  22.8 1.3 %collective-permute-done.7.refs_1_ = bf16[2,192,128]{2,1,0:T(8,128)(2,1)S(1)} collective-permute-done((bf16[2,192,128]{2,1,0:T(8,128)(2,1)S(1)}, bf16[2,192,128]{2,1,0:T(8,128)(2,1)S(1)}, u32[]{:S(2)}, u32[]{:S(2)}) %collective-permute-start.7) | collective-permute-done | bytes 98336 | tf_op jit(solution)/shard_map/ppermute | solution.py:46
  24.1 0.5 %collective-permute-done.8.refs_2_ = bf16[2,2,208,128]{3,2,1,0:T(8,128)(2,1)S(1)} collective-permute-done((bf16[2,2,208,128]{3,2,1,0:T(8,128)(2,1)S(1)}, bf16[2,2,208,128]{3,2,1,0:T(8,128)(2,1)S(1)}, u32[]{:S(2)}, u32[]{:S(2)}) %collective-permute-start.8) | collective-permute-done | bytes 213024 | tf_op jit(solution)/shard_map/ppermute | solution.py:46
  24.7 1.5 %scores.6 = (bf16[2048,4096]{1,0:T(8,128)(2,1)S(1)}, bf16[512,192]{1,0:T(8,128)(2,1)S(1)}, f32[2,512]{1,0:T(2,128)S(1)}) custom-call(bf16[4,2,192,128]{3,2,1,0:T(8,128)(2,1)S(1)} %join.3.refs_0_, bf16[2048,256]{1,0:T(8,128)(2,1)S(1)} %get-tuple-element.34.refs_1_.refs_2_.refs_4_, ...), custom_call_target="tpu_custom_call", output_to_operand_aliasing={{0}: (4, {})} | custom-call | flops 1 | bytes 1 | tf_op jit(solution)/shard_map/scores/pallas_call | solution.py:35
  26.4 1.5 %scores.7 = (bf16[2048,4096]{1,0:T(8,128)(2,1)S(1)}, bf16[512,192]{1,0:T(8,128)(2,1)S(1)}, f32[4,1024]{1,0:T(4,128)S(1)}) custom-call(f32[2,512]{1,0:T(2,128)S(1)} %get-tuple-element.36.refs_0_, f32[2,512]{1,0:T(2,128)S(1)} %get-tuple-element.40.refs_3_.refs_1_, f32[2,512]{1,0:T(2,128)S(1)} %get-tuple-element.43.refs_2_, ...), custom_call_target="tpu_custom_call", output_to_operand_aliasing={{0}: (7, {})} | custom-call | flops 1 | bytes 1 | tf_op jit(solution)/shard_map/scores/pallas_call | solution.py:35
  28.3 0.9 %collective-permute-done.10.refs_1_ = f32[4,1024]{1,0:T(4,128)S(1)} collective-permute-done((f32[4,1024]{1,0:T(4,128)S(1)}, f32[4,1024]{1,0:T(4,128)S(1)}, u32[]{:S(2)}, u32[]{:S(2)}) %collective-permute-start.10) | collective-permute-done | bytes 16416 | tf_op jit(solution)/shard_map/ppermute | solution.py:46
  29.2 2.0 %collective-permute-start.13 = (f32[4,1024]{1,0:T(4,128)S(1)}, f32[4,1024]{1,0:T(4,128)S(1)}, u32[]{:S(2)}, u32[]{:S(2)}) collective-permute-start(f32[4,1024]{1,0:T(4,128)S(1)} %relay.3.after.refs_0_), channel_id=1, source_target_pairs={{0,5},{1,4},{2,7},{3,6},{4,1},{5,0},{6,3},{7,2},{8,13},{9,12},{10,... | collective-permute-start | bytes 49160 | tf_op jit(solution)/shard_map/ppermute | solution.py:337
  31.7 1.1 %collective-permute-start.11 = (f32[4,1024]{1,0:T(4,128)S(1)}, f32[4,1024]{1,0:T(4,128)S(1)}, u32[]{:S(2)}, u32[]{:S(2)}) collective-permute-start(f32[4,1024]{1,0:T(4,128)S(1)} %relay.3.after.refs_0_), channel_id=1, source_target_pairs={{0,1},{1,0},{2,3},{3,2},{4,5},{5,4},{6,7},{7,6},{8,9},{9,8},{10,11... | collective-permute-start | bytes 49160 | tf_op jit(solution)/shard_map/ppermute | solution.py:337
  32.7 2.4 %rest.2 = (f32[192,4096]{1,0:T(8,128)}, f32[8,128]{1,0:T(8,128)S(1)}) custom-call(f32[192,4096]{1,0:T(8,128)} %teacher_hbm.5, f32[192,4096]{1,0:T(8,128)} %student_hbm.5, f32[4,1024]{1,0:T(4,128)S(1)} %relay.3.after.refs_0_, f32[192,4096]{1,0:T(8,128)} %get-tuple-element.46.before_hbm), custom_call_target="tpu_custom_call", output_to_operand_aliasing={{0}: (3, {})} | custom-call | flops 1 | bytes 1 | tf_op jit(solution)/shard_map/rest/pallas_call | solution.py:35
  35.5 2.5 %collective-permute-start.16 = (f32[4,1024]{1,0:T(4,128)S(1)}, f32[4,1024]{1,0:T(4,128)S(1)}, u32[]{:S(2)}, u32[]{:S(2)}) collective-permute-start(f32[4,1024]{1,0:T(4,128)S(1)} %relay.4.after.refs_0_), channel_id=1, source_target_pairs={{0,24},{8,16},{16,8},{24,0},{1,25},{9,17},{17,9},{25,1},{2,26},{10... | collective-permute-start | bytes 49160 | tf_op jit(solution)/shard_map/ppermute | solution.py:46
  37.9 2.0 %collective-permute-start.14 = (f32[4,1024]{1,0:T(4,128)S(1)}, f32[4,1024]{1,0:T(4,128)S(1)}, u32[]{:S(2)}, u32[]{:S(2)}) collective-permute-start(f32[4,1024]{1,0:T(4,128)S(1)} %relay.4.after.refs_0_), channel_id=1, source_target_pairs={{0,8},{8,0},{16,24},{24,16},{1,9},{9,1},{17,25},{25,17},{2,10},{10... | collective-permute-start | bytes 49160 | tf_op jit(solution)/shard_map/ppermute | solution.py:46
  39.9 2.4 %rest.3 = (f32[192,4096]{1,0:T(8,128)}, f32[8,128]{1,0:T(8,128)S(1)}) custom-call(f32[192,4096]{1,0:T(8,128)} %teacher_hbm.5, f32[192,4096]{1,0:T(8,128)} %student_hbm.5, f32[4,1024]{1,0:T(4,128)S(1)} %relay.4.after.refs_0_, f32[192,4096]{1,0:T(8,128)} %get-tuple-element.48.before_hbm), custom_call_target="tpu_custom_call", output_to_operand_aliasing={{0}: (3, {})} | custom-call | flops 1 | bytes 1 | tf_op jit(solution)/shard_map/rest/pallas_call | solution.py:35
  42.6 3.8 %gradient.1 = f32[192,2048]{1,0:T(8,128)} custom-call(f32[4,1024]{1,0:T(4,128)S(1)} %relay.5.total_ref, f32[1,128]{1,0:T(1,128)S(1)} %get-tuple-element.32.refs_5_.refs_3_.refs_4_.refs_6_.peak_ref, f32[192,2048]{1,0:T(8,128)S(1)} %get-tuple-element.51.weight_unit, f32[1,2048]{1,0:T(1,128)S(1)} %get-tuple-element.52.weight_scale, ...), custom_call_target="tpu_custom_call" | custom-call | flops 1 | bytes 1 | tf_op jit(solution)/shard_map/gradient/pallas_call | solution.py:35
  (25 shorter events, 2.5 us)
Async XLA Ops:
  0.6 4.8 %collective-permute-start = (s32[1,256]{1,0:T(1,128)}, s32[1,256]{1,0:T(1,128)S(1)}, u32[]{:S(2)}, u32[]{:S(2)}) collective-permute-start(s32[1,256]{1,0:T(1,128)} %param.10), channel_id=1, source_target_pairs={{0,1},{1,0},{2,3},{3,2},{4,5},{5,4},{6,7},{7,6},{8,9},{9,8},{10,11... | collective-permute-start | bytes 3080 | tf_op jit(solution)/shard_map/ppermute | solution.py:46
  5.6 10.1 %collective-permute-start.4 = (bf16[2,192,128]{2,1,0:T(8,128)(2,1)S(1)}, bf16[2,192,128]{2,1,0:T(8,128)(2,1)S(1)}, u32[]{:S(2)}, u32[]{:S(2)}) collective-permute-start(bf16[2,192,128]{2,1,0:T(8,128)(2,1)S(1)} %pack.1.refs_0_), channel_id=1, source_target_pairs={{0,1},{1,0},{2,3},{3,2},{4,5},{5,4},{6,7},{7,6},{8,9},{9,8},{10,11... | collective-permute-start | bytes 294920 | tf_op jit(solution)/shard_map/ppermute | solution.py:46
  7.7 8.0 %collective-permute-start.3 = (bf16[2,192,128]{2,1,0:T(8,128)(2,1)S(1)}, bf16[2,192,128]{2,1,0:T(8,128)(2,1)S(1)}, u32[]{:S(2)}, u32[]{:S(2)}) collective-permute-start(bf16[2,192,128]{2,1,0:T(8,128)(2,1)S(1)} %pack.1.refs_0_), channel_id=1, source_target_pairs={{0,24},{8,16},{16,8},{24,0},{1,25},{9,17},{17,9},{25,1},{2,26},{10... | collective-permute-start | bytes 294920 | tf_op jit(solution)/shard_map/ppermute | solution.py:46
  11.2 6.9 %collective-permute-start.2 = (bf16[2,192,128]{2,1,0:T(8,128)(2,1)S(1)}, bf16[2,192,128]{2,1,0:T(8,128)(2,1)S(1)}, u32[]{:S(2)}, u32[]{:S(2)}) collective-permute-start(bf16[2,192,128]{2,1,0:T(8,128)(2,1)S(1)} %pack.1.refs_0_), channel_id=1, source_target_pairs={{0,16},{8,24},{16,0},{24,8},{1,17},{9,25},{17,1},{25,9},{2,18},{10... | collective-permute-start | bytes 294920 | tf_op jit(solution)/shard_map/ppermute | solution.py:46
  11.3 6.9 %collective-permute-start.1 = (bf16[2,192,128]{2,1,0:T(8,128)(2,1)S(1)}, bf16[2,192,128]{2,1,0:T(8,128)(2,1)S(1)}, u32[]{:S(2)}, u32[]{:S(2)}) collective-permute-start(bf16[2,192,128]{2,1,0:T(8,128)(2,1)S(1)} %pack.1.refs_0_), channel_id=1, source_target_pairs={{0,8},{8,0},{16,24},{24,16},{1,9},{9,1},{17,25},{25,17},{2,10},{10... | collective-permute-start | bytes 294920 | tf_op jit(solution)/shard_map/ppermute | solution.py:46
  18.3 6.3 %collective-permute-start.8 = (bf16[2,2,208,128]{3,2,1,0:T(8,128)(2,1)S(1)}, bf16[2,2,208,128]{3,2,1,0:T(8,128)(2,1)S(1)}, u32[]{:S(2)}, u32[]{:S(2)}) collective-permute-start(bf16[2,2,208,128]{3,2,1,0:T(8,128)(2,1)S(1)} %get-tuple-element.41), channel_id=1, source_target_pairs={{0,1},{1,0},{2,3},{3,2},{4,5},{5,4},{6,7},{7,6},{8,9},{9,8},{10,11... | collective-permute-start | bytes 638984 | tf_op jit(solution)/shard_map/ppermute | solution.py:46
  18.9 2.4 %collective-permute-start.5 = (bf16[2,2,192,128]{3,2,1,0:T(8,128)(2,1)S(1)}, bf16[2,2,192,128]{3,2,1,0:T(8,128)(2,1)S(1)}, u32[]{:S(2)}, u32[]{:S(2)}) collective-permute-start(bf16[2,2,192,128]{3,2,1,0:T(8,128)(2,1)S(1)} %get-tuple-element.37), channel_id=1, source_target_pairs={{0,2},{2,0},{4,6},{6,4},{1,3},{3,1},{5,7},{7,5},{8,10},{10,8},{12,... | collective-permute-start | bytes 589832 | tf_op jit(solution)/shard_map/ppermute | solution.py:46
  18.9 2.4 %collective-permute-start.6 = (bf16[2,2,192,128]{3,2,1,0:T(8,128)(2,1)S(1)}, bf16[2,2,192,128]{3,2,1,0:T(8,128)(2,1)S(1)}, u32[]{:S(2)}, u32[]{:S(2)}) collective-permute-start(bf16[2,2,192,128]{3,2,1,0:T(8,128)(2,1)S(1)} %get-tuple-element.38), channel_id=1, source_target_pairs={{0,2},{2,0},{4,6},{6,4},{1,3},{3,1},{5,7},{7,5},{8,10},{10,8},{12,... | collective-permute-start | bytes 589832 | tf_op jit(solution)/shard_map/ppermute | solution.py:46
  19.4 4.7 %collective-permute-start.7 = (bf16[2,192,128]{2,1,0:T(8,128)(2,1)S(1)}, bf16[2,192,128]{2,1,0:T(8,128)(2,1)S(1)}, u32[]{:S(2)}, u32[]{:S(2)}) collective-permute-start(bf16[2,192,128]{2,1,0:T(8,128)(2,1)S(1)} %collective-permute-done.4.refs_4_.refs_0_), channel_id=1, source_target_pairs={{0,8},{8,0},{16,24},{24,16},{1,9},{9,1},{17,25},{25,17},{2,10},{10... | collective-permute-start | bytes 294920 | tf_op jit(solution)/shard_map/ppermute | solution.py:46
  24.6 1.8 %collective-permute-start.9 = (bf16[4,2,192,128]{3,2,1,0:T(8,128)(2,1)S(1)}, bf16[4,2,192,128]{3,2,1,0:T(8,128)(2,1)S(1)}, u32[]{:S(2)}, u32[]{:S(2)}) collective-permute-start(bf16[4,2,192,128]{3,2,1,0:T(8,128)(2,1)S(1)} %join.3.refs_0_), channel_id=1, source_target_pairs={{0,2},{2,0},{4,6},{6,4},{1,3},{3,1},{5,7},{7,5},{8,10},{10,8},{12,... | collective-permute-start | bytes 1179656 | tf_op jit(solution)/shard_map/ppermute | solution.py:46
  27.9 1.2 %collective-permute-start.10 = (f32[4,1024]{1,0:T(4,128)S(1)}, f32[4,1024]{1,0:T(4,128)S(1)}, u32[]{:S(2)}, u32[]{:S(2)}) collective-permute-start(f32[4,1024]{1,0:T(4,128)S(1)} %get-tuple-element.45.refs_0_), channel_id=1, source_target_pairs={{0,2},{2,0},{4,6},{6,4},{1,3},{3,1},{5,7},{7,5},{8,10},{10,8},{12,... | collective-permute-start | bytes 49160 | tf_op jit(solution)/shard_map/ppermute | solution.py:46
  29.2 6.0 %collective-permute-start.13 = (f32[4,1024]{1,0:T(4,128)S(1)}, f32[4,1024]{1,0:T(4,128)S(1)}, u32[]{:S(2)}, u32[]{:S(2)}) collective-permute-start(f32[4,1024]{1,0:T(4,128)S(1)} %relay.3.after.refs_0_), channel_id=1, source_target_pairs={{0,5},{1,4},{2,7},{3,6},{4,1},{5,0},{6,3},{7,2},{8,13},{9,12},{10,... | collective-permute-start | bytes 49160 | tf_op jit(solution)/shard_map/ppermute | solution.py:337
  31.2 4.0 %collective-permute-start.12 = (f32[4,1024]{1,0:T(4,128)S(1)}, f32[4,1024]{1,0:T(4,128)S(1)}, u32[]{:S(2)}, u32[]{:S(2)}) collective-permute-start(f32[4,1024]{1,0:T(4,128)S(1)} %relay.3.after.refs_0_), channel_id=1, source_target_pairs={{0,4},{1,5},{2,6},{3,7},{4,0},{5,1},{6,2},{7,3},{8,12},{9,13},{10,... | collective-permute-start | bytes 49160 | tf_op jit(solution)/shard_map/ppermute | solution.py:337
  31.7 3.7 %collective-permute-start.11 = (f32[4,1024]{1,0:T(4,128)S(1)}, f32[4,1024]{1,0:T(4,128)S(1)}, u32[]{:S(2)}, u32[]{:S(2)}) collective-permute-start(f32[4,1024]{1,0:T(4,128)S(1)} %relay.3.after.refs_0_), channel_id=1, source_target_pairs={{0,1},{1,0},{2,3},{3,2},{4,5},{5,4},{6,7},{7,6},{8,9},{9,8},{10,11... | collective-permute-start | bytes 49160 | tf_op jit(solution)/shard_map/ppermute | solution.py:337
  35.5 6.9 %collective-permute-start.16 = (f32[4,1024]{1,0:T(4,128)S(1)}, f32[4,1024]{1,0:T(4,128)S(1)}, u32[]{:S(2)}, u32[]{:S(2)}) collective-permute-start(f32[4,1024]{1,0:T(4,128)S(1)} %relay.4.after.refs_0_), channel_id=1, source_target_pairs={{0,24},{8,16},{16,8},{24,0},{1,25},{9,17},{17,9},{25,1},{2,26},{10... | collective-permute-start | bytes 49160 | tf_op jit(solution)/shard_map/ppermute | solution.py:46
  37.9 4.6 %collective-permute-start.15 = (f32[4,1024]{1,0:T(4,128)S(1)}, f32[4,1024]{1,0:T(4,128)S(1)}, u32[]{:S(2)}, u32[]{:S(2)}) collective-permute-start(f32[4,1024]{1,0:T(4,128)S(1)} %relay.4.after.refs_0_), channel_id=1, source_target_pairs={{0,16},{8,24},{16,0},{24,8},{1,17},{9,25},{17,1},{25,9},{2,18},{10... | collective-permute-start | bytes 49160 | tf_op jit(solution)/shard_map/ppermute | solution.py:46
  37.9 4.6 %collective-permute-start.14 = (f32[4,1024]{1,0:T(4,128)S(1)}, f32[4,1024]{1,0:T(4,128)S(1)}, u32[]{:S(2)}, u32[]{:S(2)}) collective-permute-start(f32[4,1024]{1,0:T(4,128)S(1)} %relay.4.after.refs_0_), channel_id=1, source_target_pairs={{0,8},{8,0},{16,24},{24,16},{1,9},{9,1},{17,25},{25,17},{2,10},{10... | collective-permute-start | bytes 49160 | tf_op jit(solution)/shard_map/ppermute | solution.py:46

commit v13 on v12

--- a/solution.py
+++ b/solution.py
@@ -197,14 +197,18 @@
     )
 
 
+def normalize(values):
+    return (values * lax.rsqrt(jnp.sum(values * values, axis=0, keepdims=True) + EPS)).astype(jnp.bfloat16)
+
+
 def pack_kernel(student_ref, teacher_ref, index_ref, out_ref):
     half = out_ref.shape[2]
     lower = here()[2] == 0
-    out_ref[0] = student_ref[...]
+    out_ref[0] = normalize(student_ref[...].astype(jnp.float32))
     index = jnp.where(lower, index_ref[:, :half], index_ref[:, half:])
     row = lax.broadcasted_iota(jnp.int32, (teacher_ref.shape[1], half), 0)
     pick = jnp.where(row == index, 1.0, 0.0).astype(jnp.bfloat16)
-    out_ref[1] = jnp.dot(teacher_ref[...], pick, preferred_element_type=jnp.float32).astype(jnp.bfloat16)
+    out_ref[1] = normalize(jnp.dot(teacher_ref[...], pick, preferred_element_type=jnp.float32))
 
 
 def pack(student, teacher, index):
@@ -212,13 +216,14 @@
     return call(pack_kernel, "pack", held(2, bot, half, dtype=jnp.bfloat16), (student, teacher, index))
 
 
-def join_kernel(n_in, n_after, firsts, bot, *refs):
+def join_kernel(n_in, n_after, picks, bot, *refs):
+    refs = refs[n_after:]
     blocks = []
     for ref in refs[:n_in]:
         blocks += [ref] if len(ref.shape) == 3 else [ref.at[i] for i in range(ref.shape[0])]
-    for first, ref in zip(firsts, refs[n_in + n_after:]):
-        for i in range(ref.shape[0]):
-            block = blocks[first + i][:, :bot, :]
+    for pick, ref in zip(picks, refs[n_in:]):
+        for i, at in enumerate(pick):
+            block = blocks[at][:, :bot, :]
             ref[i, :, :bot, :] = block
             if ref.shape[2] > bot:
                 ref[i, :, bot:, :] = block[:, :ref.shape[2] - bot]
@@ -226,9 +231,9 @@
 
 def join(parts, outs, after, bot):
     width = parts[0].shape[-1]
-    shapes = [held(count, 2, rows, width, dtype=jnp.bfloat16) for _, count, rows in outs]
-    kernel = functools.partial(join_kernel, len(parts), len(after), [first for first, _, _ in outs], bot)
-    return call(kernel, "join", shapes, (*parts, *after), in_specs=[ON_CHIP] * len(parts) + [IN_HBM] * len(after))
+    shapes = [held(len(pick), 2, rows, width, dtype=jnp.bfloat16) for pick, rows in outs]
+    kernel = functools.partial(join_kernel, len(parts), len(after), [pick for pick, _ in outs], bot)
+    return call(kernel, "join", shapes, (*after, *parts), in_specs=[IN_HBM] * len(after) + [ON_CHIP] * len(parts))
 
 
 def log_sum(parts):
@@ -245,76 +250,97 @@
     return lax.axis_index("fsdp") ^ k if n <= DIRECT else k
 
 
-def score_kernel(part, n_feats, *refs):
-    last = part == 3
-    before, refs = (refs[:3], refs[3:]) if last else ((), refs)
-    feats_refs, (ws_ref, wt_ref, peak_ref, *refs) = refs[:n_feats], refs[n_feats:]
-    blocks = [ref.at[i] for ref in feats_refs for i in range(ref.shape[0])]
-    exp_ref, unit_ref, total_ref, *mine = refs[1:] if part else refs
-    own_ref = mine[0] if last else total_ref
-    n, (_, bot, width) = len(blocks), blocks[0].shape
+def place(half, j, n):
+    return half * 2 * n + j
+
+
+def score_kernel(n, plan, earlier, *refs):
+    before, refs = refs[:len(earlier)], refs[len(earlier):]
+    blocks, at = [], 0
+    while len(blocks) < len(plan):
+        blocks += [refs[at].at[i] for i in range(refs[at].shape[0])]
+        at += 1
+    ws_ref, wt_ref, peak_ref, *refs = refs[at:]
+    exp_ref, unit_ref, total_ref, *scratch = refs[2:] if refs[0].shape == refs[2].shape else refs
+    _, bot, width = blocks[0].shape
     cols = ws_ref.shape[0]
+    teacher_side = 4 * n * width
     step = min(STEP, cols)
-    per = max(1, min(n, GROUP // width))
-    row = lax.broadcasted_iota(jnp.int32, (DEPTH - bot, per * width), 0)
-    for which, w_ref, gain in ((0, ws_ref, GAIN_S), (1, wt_ref, GAIN_T)):
-        base = (2 * part + which) * n * width
-        extra = jnp.where(row < 3 * which, 1.0, 0.0).astype(jnp.bfloat16)
-        for group in range(n // per):
-            values = [blocks[group * per + k][which].astype(jnp.float32) for k in range(per)]
-            values = jnp.concatenate(values, axis=1)
-            unit = (values * lax.rsqrt(jnp.sum(values * values, axis=0, keepdims=True) + EPS)).astype(jnp.bfloat16)
-            lanes = slice(group * per * width, (group + 1) * per * width)
-            if which == 0:
-                unit_ref[lanes, :] = unit.T
+    per = max(1, min(len(plan), GROUP // width))
+    own = {}
+    for first in range(0, len(plan), per):
+        group = range(first, min(first + per, len(plan)))
+        size = len(group) * width
+        row = lax.broadcasted_iota(jnp.int32, (DEPTH - bot, size), 0)
+        for which, w_ref, gain in ((0, ws_ref, GAIN_S), (1, wt_ref, GAIN_T)):
+            extra = jnp.where(row < 3 * which, 1.0, 0.0).astype(jnp.bfloat16)
+            unit = jnp.concatenate([blocks[k][which] for k in group], axis=1)
             stationary = jnp.concatenate([unit, extra], axis=0)
-            total = jnp.zeros((8, per * width), jnp.float32)
+            total = jnp.zeros((8, size), jnp.float32)
             for at in range(0, cols, step):
                 score = jnp.dot(w_ref[at:at + step, :], stationary, preferred_element_type=jnp.float32)
                 exps = jnp.exp2(score * gain)
-                total = total + jnp.sum(exps.reshape(step // 8, 8, per * width), axis=0)
-                exp_ref[at:at + step, base + lanes.start:base + lanes.stop] = exps.astype(jnp.bfloat16)
+                total = total + jnp.sum(exps.reshape(step // 8, 8, size), axis=0)
+                exps = exps.astype(jnp.bfloat16)
+                for k in group:
+                    half, j = plan[k]
+                    lies = place(half, (j + which * n) % (2 * n), n) * width + which * teacher_side
+                    exp_ref[at:at + step, lies:lies + width] = exps[:, (k - first) * width:(k - first + 1) * width]
             total = jnp.sum(total, axis=0, keepdims=True)
             if which == 1:
                 total = jnp.log2(total) + GAIN_T * peak_ref[:, :1]
-            own_ref[which:which + 1, lanes] = total
-    if not last:
+            for k in group:
+                own[which, k] = total[:, (k - first) * width:(k - first + 1) * width]
+    for k, (half, j) in enumerate(plan):
+        lies = place(half, j, n) * width
+        unit_ref[lies:lies + width, :] = blocks[k][0].T
+    if not earlier:
+        for which, k in own:
+            total_ref[which:which + 1, k * width:(k + 1) * width] = own[which, k]
         return
+    (gathered,) = scratch
+    for known, ref in [*zip(earlier, before), (plan, None)]:
+        for k, (half, j) in enumerate(known):
+            for which in (0, 1):
+                lies = place(half, (j + which * n) % (2 * n), n) * width
+                part = own[which, k] if ref is None else ref[which:which + 1, k * width:(k + 1) * width]
+                gathered[which:which + 1, lies:lies + width] = part
     dp, _, core = here()
-    own, pair, other = before
-    parts = ((own, other), (pair, own_ref))
     rows = []
     for which in (0, 1):
         for half in (0, 1):
             pieces = []
             for view in (0, 1):
-                first = (dp == view) if which == 0 else (dp != view)
-                for place in range(n):
-                    at = pl.ds(pl.multiple_of(slot(place, n) * width, width), width)
-                    read = [[part[which:which + 1, at] for part in side] for side in parts]
-                    mine, theirs = [jnp.where(first, *side) for side in read]
+                for k in range(n):
+                    lies = ((dp ^ view) * n + slot(k, n)) * width
+                    mine, theirs = [
+                        gathered[which:which + 1, pl.ds(pl.multiple_of(side * 2 * n * width + lies, width), width)]
+                        for side in (0, 1)
+                    ]
                     pieces.append(jnp.where(core == half, mine, theirs))
             rows.append(jnp.concatenate(pieces, axis=1))
     total_ref[...] = jnp.concatenate(rows, axis=0)
 
 
-def scores(part, feats, weights, before=(), exps=None):
+def scores(n, plan, feats, weights, buffers=(), earlier=(), before=()):
     _, _, bot, width = feats[0].shape
-    cols, rows = weights[0].shape[0], sum(part.shape[0] for part in feats) * width
-    args = (*before, *feats, *weights, *([exps] if part else []))
-    return call(
-        functools.partial(score_kernel, part, len(feats)),
+    cols, rows = weights[0].shape[0], 4 * n * width
+    args = (*before, *feats, *weights, *buffers)
+    plain = len(args) - len(buffers)
+    exps, units, total = call(
+        functools.partial(score_kernel, n, plan, earlier),
         "scores",
         [
-            held(cols, 8 * rows, dtype=jnp.bfloat16),
+            held(cols, 2 * rows, dtype=jnp.bfloat16),
             held(rows, bot, dtype=jnp.bfloat16),
-            held(4, 2 * rows) if part == 3 else held(2, rows),
+            held(4, rows // 2) if earlier else held(2, len(plan) * width),
         ],
         args,
-        in_specs=[ON_CHIP] * (len(args) - bool(part)) + [IN_HBM] * bool(part),
-        input_output_aliases={len(args) - 1: 0} if part else {},
-        scratch_shapes=[held(2, rows)] if part == 3 else [],
-    )
+        in_specs=[ON_CHIP] * plain + [IN_HBM] * len(buffers),
+        input_output_aliases={plain + i: i for i in range(len(buffers))},
+        scratch_shapes=[held(2, rows)] if earlier else [],
+    )
+    return (exps, units), total
 
 
 def relay_kernel(n_in, *refs):
@@ -344,38 +370,30 @@
     return [lax.all_to_all(jnp.broadcast_to(total[None], (n, *total.shape)), "fsdp", 0, 0, tiled=True)]
 
 
-def grad_kernel(total_ref, peak_ref, weight_unit, weight_scale, *refs):
-    units, exp_ref, out_hbm, scales, buf, sems = refs[:4], *refs[4:]
+def grad_kernel(total_ref, peak_ref, weight_unit, weight_scale, unit_ref, exp_ref, out_hbm, scales, buf, sems):
     dp, _, core = here()
     scales[0:2, :] = 10.0 / total_ref[0:2, :]
     scales[2:4, :] = 10.0 * jnp.exp2(GAIN_T * peak_ref[:, :1] - total_ref[2:4, :])
-    rows = units[0].shape[0]
+    rows = unit_ref.shape[0]
     width = 128
-    n = rows // width
+    n = rows // width // 4
     factors = []
-    for part in range(4):
-        view, half = divmod(part, 2)
-        base = (dp ^ view) * rows
-        at = [pl.ds(pl.multiple_of(base + slot(k, n) * width, width), width) for k in range(n)]
-        for which in (0, 1):
-            picked = [
-                jnp.where(core == half, scales[2 * which:2 * which + 1, where], scales[2 * which + 1:2 * which + 2, where])
-                for where in at
-            ]
-            factors.append(jnp.concatenate(picked, axis=1).astype(jnp.bfloat16))
-    feats = jnp.concatenate([unit[...] for unit in units], axis=0)
+    for which in (0, 1):
+        picked = []
+        for half in (0, 1):
+            for j in range(2 * n):
+                lies = ((dp ^ (j // n)) * n + slot(j % n, n)) * width
+                upper, lower = [
+                    scales[2 * which + i:2 * which + i + 1, pl.ds(pl.multiple_of(lies, width), width)] for i in (0, 1)
+                ]
+                picked.append(jnp.where(core == half, upper, lower))
+        factors.append(jnp.concatenate(picked, axis=1).astype(jnp.bfloat16))
     chunks, _, step = buf.shape
     stores = []
     for i in range(chunks):
         at = slice(i * step, (i + 1) * step)
-        derivs = []
-        for part in range(4):
-            lies_s, lies_t = 2 * part * rows, (2 * (part ^ 2) + 1) * rows
-            probs_s = exp_ref[at, lies_s:lies_s + rows] * factors[2 * part]
-            probs_t = exp_ref[at, lies_t:lies_t + rows] * factors[2 * part + 1]
-            derivs.append(probs_s - probs_t)
-        derivs = jnp.concatenate(derivs, axis=1)
-        grad = jnp.dot(derivs, feats, preferred_element_type=jnp.float32).T
+        derivs = exp_ref[at, :rows] * factors[0] - exp_ref[at, rows:] * factors[1]
+        grad = jnp.dot(derivs, unit_ref[...], preferred_element_type=jnp.float32).T
         unit = weight_unit[:, at]
         proj = unit * jnp.sum(unit * grad, axis=0, keepdims=True)
         buf[i] = (grad - proj) * weight_scale[:, at]
@@ -387,16 +405,15 @@
 
 def gradient(total, peak, weight_unit, weight_scale, units, exps):
     cols = exps.shape[0]
-    rows, bot = units[0].shape
+    rows, bot = units.shape
     step = min(512, cols)
-    args = (total, peak, weight_unit, weight_scale, *units, exps)
     return call(
         grad_kernel,
         "gradient",
         pltpu.HBM((bot, cols), jnp.float32),
-        args,
+        (total, peak, weight_unit, weight_scale, units, exps),
         out_specs=IN_HBM,
-        scratch_shapes=[held(4, 2 * rows), held(cols // step, bot, step), pltpu.SemaphoreType.DMA((cols // step,))],
+        scratch_shapes=[held(4, rows // 2), held(cols // step, bot, step), pltpu.SemaphoreType.DMA((cols // step,))],
     )
 
 
@@ -410,21 +427,32 @@
     new, wt, ws, unit, scale, peak = prepare(teacher_weight, student_weight, center, n_dp)
     weights = (ws, wt, peak)
     bot = mine.shape[1]
-    if n_fsdp <= DIRECT:
-        other = [swap(mine, "dp")]
-        along = [swap(mine, "fsdp", k) for k in range(1, n_fsdp)]
-        half = n_fsdp // 2
-        outs = [(0, n_fsdp, bot), (2, n_fsdp - 2, bot + 16), (0, half, bot), (half, half, bot)]
-        own, far, *halves = join([mine, *along], outs, (other[0], peak), bot)
-        other += [swap(other[0], "fsdp"), swap(far, "dp")]
+    bot, n = mine.shape[1], n_fsdp
+    named = lambda half, js: [(half, j) for j in js]
+    if n <= DIRECT:
+        other = swap(mine, "dp")
+        along = [swap(mine, "fsdp", k) for k in range(1, n)]
+        order = range(n - 1, -1, -1)
+        outs = [(order, bot), (order[2:], bot + 16), (order[:n // 2], bot), (order[n // 2:], bot)]
+        own, far, *halves = join([*along[::-1], mine], outs, (other, peak), bot)
+        rest = [swap(other, "fsdp"), swap(far, "dp")]
+        early, late = [other[None], swap(other, "proto")[None]], range(n + 1, 2 * n)
+        first, second, third = named(0, range(n)), named(1, range(n)), [(0, n), (1, n)]
+        buffers, total_a = scores(n, first, [own], weights)
+        buffers, total_b = scores(n, second, [swap(half, "proto") for half in halves], weights, buffers)
+        buffers, total_c = scores(n, third, early, weights, buffers)
+        (rest,) = join(rest, [(range(n - 1), bot)], (total_c,), bot)
+        buffers, total_d = scores(n, named(0, late), [rest], weights, buffers)
+        earlier, before = [first, second, third, named(0, late)], [total_a, total_b, total_c, total_d]
     else:
-        own = lax.all_to_all(jnp.broadcast_to(mine[None], (n_fsdp, *mine.shape)), "fsdp", 0, 0, tiled=True)
-        other, halves = [swap(own, "dp")], [own]
-    exps, unit_a, total_a = scores(0, [own], weights)
-    exps, unit_b, total_b = scores(1, [swap(half, "proto") for half in halves], weights, exps=exps)
-    (other,) = join(other, [(0, n_fsdp, bot)], (total_b,), bot)
-    exps, unit_c, total_c = scores(2, [other], weights, exps=exps)
-    exps, unit_d, total = scores(3, [swap(other, "proto")], weights, (total_a, total_b, total_c), exps)
+        own = lax.all_to_all(jnp.broadcast_to(mine[None], (n, *mine.shape)), "fsdp", 0, 0, tiled=True)
+        rest, late = swap(own, "dp"), range(n, 2 * n)
+        first, second = named(0, range(n)), named(1, range(n))
+        buffers, total_a = scores(n, first, [own], weights)
+        buffers, total_b = scores(n, second, [swap(own, "proto")], weights, buffers)
+        buffers, total_c = scores(n, named(0, late), [rest], weights, buffers)
+        earlier, before = [first, second, named(0, late)], [total_a, total_b, total_c]
+    (exps, units), total = scores(n, named(1, late), [swap(rest, "proto")], weights, buffers, earlier, before)
     n_proto, own_cols = lax.axis_size("proto"), ws.shape[0]
     middle = own_cols // 2
     total = add_up([total, swap(total, "proto")])
@@ -433,7 +461,7 @@
     total = add_up([total, *[across(total, *step) for step in steps]], done)
     teacher_new, done = update_rest(teacher_weight, student_weight, total, new, own_cols, middle, own_cols)
     total = add_up(along_fsdp(total), done)
-    student_grad = gradient(total, peak, unit, scale, (unit_a, unit_b, unit_c, unit_d), exps)
+    student_grad = gradient(total, peak, unit, scale, units, exps)
     return (teacher_new, student_grad)
 
 

time: 46.6 us -> 49.4 us (1.060)
  waiting for transfers between devices: 6.82 us -> 9.05 us
  Pallas kernels: 19.3 us -> 19.9 us
    ppermute x3, waiting for transfers between devices: 0.26 us -> 1.72 us  [across(): return lax.ppermute(total, ('proto', 'dp'), pairs)]
    ppermute x14 -> x15, waiting for transfers between devices: 6.56 us -> 7.33 us  [swap(): lax.ppermute(block, axis, [(i, i ^ apart) for i in range(lax.axis_size(ax...]
    pallas_call x15 -> x16, Pallas kernels: 19.3 us -> 19.9 us  [call(): pl.pallas_call(kernel, out_shape=out_shape, compiler_params=pltpu.Compile...]
    ppermute x14 -> x15, starting transfers between devices: 15.9 us -> 15.9 us  [swap(): lax.ppermute(block, axis, [(i, i ^ apart) for i in range(lax.axis_size(ax...]
  transfers between devices with their start and end apart: 17 -> 18, of which waited for: 8 -> 7; matrix products, arithmetic and copies ran while one was open for 0% -> 0% of each run, Pallas kernels for 30% -> 29%
where the time goes in v13:
time: 49.4 us; the launch traced here: 49.2 us
  Pallas kernels  19.9 us (40%)
  starting transfers between devices  19.4 us (39%)
  waiting for transfers between devices  9.05 us (18%)
  between operations  0.82 us (2%)
    pallas_call x16, Pallas kernels, call(): pl.pallas_call(kernel, out_shape=out_shape, compiler_params=pltpu.Compile...  19.9 us
    ppermute x15, starting transfers between devices, swap(): lax.ppermute(block, axis, [(i, i ^ apart) for i in range(lax.axis_size(ax...  15.9 us
    ppermute x15, waiting for transfers between devices, swap(): lax.ppermute(block, axis, [(i, i ^ apart) for i in range(lax.axis_size(ax...  7.33 us
    ppermute x3, starting transfers between devices, across(): return lax.ppermute(total, ('proto', 'dp'), pairs)  3.55 us
    ppermute x3, waiting for transfers between devices, across(): return lax.ppermute(total, ('proto', 'dp'), pairs)  1.72 us
  transfers between devices with their start and end apart: 18, of which 7 were waited for; matrix products, arithmetic and copies ran while one was open for 0% of the time, Pallas kernels for 29%

profile of v13, /device:TPU:0, one launch (start us, length us, event | category | flops | bytes accessed | tf_op | source)
XLA Modules:
  0.0 49.2 jit_solution(5363493066653438329)
XLA Ops:
  0.6 3.0 %collective-permute-start = (s32[1,256]{1,0:T(1,128)}, s32[1,256]{1,0:T(1,128)S(1)}, u32[]{:S(2)}, u32[]{:S(2)}) collective-permute-start(s32[1,256]{1,0:T(1,128)} %param.10), channel_id=1, source_target_pairs={{0,1},{1,0},{2,3},{3,2},{4,5},{5,4},{6,7},{7,6},{8,9},{9,8},{10,11... | collective-permute-start | bytes 3080 | tf_op jit(solution)/shard_map/ppermute | solution.py:46
  3.6 0.9 %fetch.1 = (bf16[192,128]{1,0:T(8,128)(2,1)S(1)}, bf16[192,256]{1,0:T(8,128)(2,1)S(1)}) custom-call(bf16[192,256]{1,0:T(8,128)(2,1)} %bitcast.11, bf16[192,256]{1,0:T(8,128)(2,1)} %bitcast.12), custom_call_target="tpu_custom_call" | custom-call | flops 1 | bytes 1 | tf_op jit(solution)/shard_map/fetch/pallas_call | solution.py:35
  4.6 0.8 %collective-permute-done.index_ref = s32[1,256]{1,0:T(1,128)S(1)} collective-permute-done((s32[1,256]{1,0:T(1,128)}, s32[1,256]{1,0:T(1,128)S(1)}, u32[]{:S(2)}, u32[]{:S(2)}) %collective-permute-start) | collective-permute-done | bytes 1056 | tf_op jit(solution)/shard_map/ppermute | solution.py:46
  5.6 2.1 %collective-permute-start.1 = (bf16[2,192,128]{2,1,0:T(8,128)(2,1)S(1)}, bf16[2,192,128]{2,1,0:T(8,128)(2,1)S(1)}, u32[]{:S(2)}, u32[]{:S(2)}) collective-permute-start(bf16[2,192,128]{2,1,0:T(8,128)(2,1)S(1)} %pack.1.refs_5_), channel_id=1, source_target_pairs={{0,1},{1,0},{2,3},{3,2},{4,5},{5,4},{6,7},{7,6},{8,9},{9,8},{10,11... | collective-permute-start | bytes 294920 | tf_op jit(solution)/shard_map/ppermute | solution.py:46
  7.7 3.6 %collective-permute-start.2 = (bf16[2,192,128]{2,1,0:T(8,128)(2,1)S(1)}, bf16[2,192,128]{2,1,0:T(8,128)(2,1)S(1)}, u32[]{:S(2)}, u32[]{:S(2)}) collective-permute-start(bf16[2,192,128]{2,1,0:T(8,128)(2,1)S(1)} %pack.1.refs_5_), channel_id=1, source_target_pairs={{0,24},{8,16},{16,8},{24,0},{1,25},{9,17},{17,9},{25,1},{2,26},{10... | collective-permute-start | bytes 294920 | tf_op jit(solution)/shard_map/ppermute | solution.py:46
  11.3 0.8 %collective-permute-start.4 = (bf16[2,192,128]{2,1,0:T(8,128)(2,1)S(1)}, bf16[2,192,128]{2,1,0:T(8,128)(2,1)S(1)}, u32[]{:S(2)}, u32[]{:S(2)}) collective-permute-start(bf16[2,192,128]{2,1,0:T(8,128)(2,1)S(1)} %pack.1.refs_5_), channel_id=1, source_target_pairs={{0,8},{8,0},{16,24},{24,16},{1,9},{9,1},{17,25},{25,17},{2,10},{10... | collective-permute-start | bytes 294920 | tf_op jit(solution)/shard_map/ppermute | solution.py:46
  12.1 3.6 %prep.1 = (f32[192,4096]{1,0:T(8,128)}, bf16[2048,256]{1,0:T(8,128)(2,1)S(1)}, bf16[2048,256]{1,0:T(8,128)(2,1)S(1)}, f32[192,2048]{1,0:T(8,128)S(1)}, f32[1,2048]{1,0:T(1,128)S(1)}, /*index=5*/f32[1,128]{1,0:T(1,128)S(1)}) custom-call(f32[192,4096]{1,0:T(8,128)} %teacher_hbm.5, f32[192,4096]{1,0:T(8,128)} %student_hbm.5, f32[1,16384]{1,0:T(1,128)} %bitcast.13), custom_call_target="tpu_custom_call" | custom-call | flops 1 | bytes 1 | tf_op jit(solution)/shard_map/prep/pallas_call | solution.py:35
  15.7 2.5 %collective-permute-done.3.refs_3_ = bf16[2,192,128]{2,1,0:T(8,128)(2,1)S(1)} collective-permute-done((bf16[2,192,128]{2,1,0:T(8,128)(2,1)S(1)}, bf16[2,192,128]{2,1,0:T(8,128)(2,1)S(1)}, u32[]{:S(2)}, u32[]{:S(2)}) %collective-permute-start.3) | collective-permute-done | bytes 98336 | tf_op jit(solution)/shard_map/ppermute | solution.py:46
  19.9 1.4 %scores.5 = (bf16[2048,4096]{1,0:T(8,128)(2,1)S(1)}, bf16[2048,192]{1,0:T(8,128)(2,1)S(1)}, f32[2,512]{1,0:T(2,128)S(1)}) custom-call(bf16[4,2,192,128]{3,2,1,0:T(8,128)(2,1)S(1)} %get-tuple-element.36.refs_0_, bf16[2048,256]{1,0:T(8,128)(2,1)S(1)} %get-tuple-element.37.refs_1_.refs_2_.refs_5_, ...), custom_call_target="tpu_custom_call" | custom-call | flops 1 | bytes 1 | tf_op jit(solution)/shard_map/scores/pallas_call | solution.py:35
  21.3 1.4 %scores.6 = (bf16[2048,4096]{1,0:T(8,128)(2,1)S(1)}, bf16[2048,192]{1,0:T(8,128)(2,1)S(1)}, f32[2,512]{1,0:T(2,128)S(1)}) custom-call(bf16[2,2,192,128]{3,2,1,0:T(8,128)(2,1)S(1)} %collective-permute-done.5.refs_0_, bf16[2,2,192,128]{3,2,1,0:T(8,128)(2,1)S(1)} %collective-permute-done.6.refs_1_, ...), custom_call_target="tpu_custom_call", output_to_operand_aliasing={{0}: (5, {}), {1}: (6, {})} | custom-call | flops 1 | bytes 1 | tf_op jit(solution)/shard_map/scores/pallas_call | solution.py:35
  22.7 0.8 %scores.7 = (bf16[2048,4096]{1,0:T(8,128)(2,1)S(1)}, bf16[2048,192]{1,0:T(8,128)(2,1)S(1)}, f32[2,256]{1,0:T(2,128)S(1)}) custom-call(bf16[1,2,192,128]{3,2,1,0:T(8,128)(2,1)S(1)} %bitcast.9, bf16[1,2,192,128]{3,2,1,0:T(8,128)(2,1)S(1)} %bitcast.10, ...), custom_call_target="tpu_custom_call", output_to_operand_aliasing={{0}: (5, {}), {1}: (6, {})} | custom-call | flops 1 | bytes 1 | tf_op jit(solution)/shard_map/scores/pallas_call | solution.py:35
  23.5 1.1 %collective-permute-done.8.refs_1_ = bf16[2,192,128]{2,1,0:T(8,128)(2,1)S(1)} collective-permute-done((bf16[2,192,128]{2,1,0:T(8,128)(2,1)S(1)}, bf16[2,192,128]{2,1,0:T(8,128)(2,1)S(1)}, u32[]{:S(2)}, u32[]{:S(2)}) %collective-permute-start.8) | collective-permute-done | bytes 98336 | tf_op jit(solution)/shard_map/ppermute | solution.py:46
  24.8 1.3 %scores.8 = (bf16[2048,4096]{1,0:T(8,128)(2,1)S(1)}, bf16[2048,192]{1,0:T(8,128)(2,1)S(1)}, f32[2,384]{1,0:T(2,128)S(1)}) custom-call(bf16[3,2,192,128]{3,2,1,0:T(8,128)(2,1)S(1)} %join.3.refs_0_, bf16[2048,256]{1,0:T(8,128)(2,1)S(1)} %get-tuple-element.37.refs_1_.refs_2_.refs_5_, ...), custom_call_target="tpu_custom_call", output_to_operand_aliasing={{0}: (4, {}), {1}: (5, {})} | custom-call | flops 1 | bytes 1 | tf_op jit(solution)/shard_map/scores/pallas_call | solution.py:35
  26.3 1.3 %scores.9 = (bf16[2048,4096]{1,0:T(8,128)(2,1)S(1)}, bf16[2048,192]{1,0:T(8,128)(2,1)S(1)}, f32[4,1024]{1,0:T(4,128)S(1)}) custom-call(f32[2,512]{1,0:T(2,128)S(1)} %get-tuple-element.39.refs_0_, f32[2,512]{1,0:T(2,128)S(1)} %get-tuple-element.44.refs_1_, ...), custom_call_target="tpu_custom_call", output_to_operand_aliasing={{0}: (8, {}), {1}: (9, {})} | custom-call | flops 1 | bytes 1 | tf_op jit(solution)/shard_map/scores/pallas_call | solution.py:35
  28.0 0.9 %collective-permute-done.11.refs_1_ = f32[4,1024]{1,0:T(4,128)S(1)} collective-permute-done((f32[4,1024]{1,0:T(4,128)S(1)}, f32[4,1024]{1,0:T(4,128)S(1)}, u32[]{:S(2)}, u32[]{:S(2)}) %collective-permute-start.11) | collective-permute-done | bytes 16416 | tf_op jit(solution)/shard_map/ppermute | solution.py:46
  28.9 1.5 %collective-permute-start.12 = (f32[4,1024]{1,0:T(4,128)S(1)}, f32[4,1024]{1,0:T(4,128)S(1)}, u32[]{:S(2)}, u32[]{:S(2)}) collective-permute-start(f32[4,1024]{1,0:T(4,128)S(1)} %relay.3.after.refs_0_), channel_id=1, source_target_pairs={{0,1},{1,0},{2,3},{3,2},{4,5},{5,4},{6,7},{7,6},{8,9},{9,8},{10,11... | collective-permute-start | bytes 49160 | tf_op jit(solution)/shard_map/ppermute | solution.py:363
  30.5 1.5 %collective-permute-start.13 = (f32[4,1024]{1,0:T(4,128)S(1)}, f32[4,1024]{1,0:T(4,128)S(1)}, u32[]{:S(2)}, u32[]{:S(2)}) collective-permute-start(f32[4,1024]{1,0:T(4,128)S(1)} %relay.3.after.refs_0_), channel_id=1, source_target_pairs={{0,4},{1,5},{2,6},{3,7},{4,0},{5,1},{6,2},{7,3},{8,12},{9,13},{10,... | collective-permute-start | bytes 49160 | tf_op jit(solution)/shard_map/ppermute | solution.py:363
  32.5 2.4 %rest.2 = (f32[192,4096]{1,0:T(8,128)}, f32[8,128]{1,0:T(8,128)S(1)}) custom-call(f32[192,4096]{1,0:T(8,128)} %teacher_hbm.5, f32[192,4096]{1,0:T(8,128)} %student_hbm.5, f32[4,1024]{1,0:T(4,128)S(1)} %relay.3.after.refs_0_, f32[192,4096]{1,0:T(8,128)} %get-tuple-element.55.before_hbm), custom_call_target="tpu_custom_call", output_to_operand_aliasing={{0}: (3, {})} | custom-call | flops 1 | bytes 1 | tf_op jit(solution)/shard_map/rest/pallas_call | solution.py:35
  34.9 1.7 %collective-permute-done.14.refs_3_ = f32[4,1024]{1,0:T(4,128)S(1)} collective-permute-done((f32[4,1024]{1,0:T(4,128)S(1)}, f32[4,1024]{1,0:T(4,128)S(1)}, u32[]{:S(2)}, u32[]{:S(2)}) %collective-permute-start.14) | collective-permute-done | bytes 16416 | tf_op jit(solution)/shard_map/ppermute | solution.py:363
  37.2 2.5 %collective-permute-start.16 = (f32[4,1024]{1,0:T(4,128)S(1)}, f32[4,1024]{1,0:T(4,128)S(1)}, u32[]{:S(2)}, u32[]{:S(2)}) collective-permute-start(f32[4,1024]{1,0:T(4,128)S(1)} %relay.4.after.refs_0_), channel_id=1, source_target_pairs={{0,16},{8,24},{16,0},{24,8},{1,17},{9,25},{17,1},{25,9},{2,18},{10... | collective-permute-start | bytes 49160 | tf_op jit(solution)/shard_map/ppermute | solution.py:46
  39.7 1.4 %collective-permute-start.17 = (f32[4,1024]{1,0:T(4,128)S(1)}, f32[4,1024]{1,0:T(4,128)S(1)}, u32[]{:S(2)}, u32[]{:S(2)}) collective-permute-start(f32[4,1024]{1,0:T(4,128)S(1)} %relay.4.after.refs_0_), channel_id=1, source_target_pairs={{0,24},{8,16},{16,8},{24,0},{1,25},{9,17},{17,9},{25,1},{2,26},{10... | collective-permute-start | bytes 49160 | tf_op jit(solution)/shard_map/ppermute | solution.py:46
  41.1 2.4 %rest.3 = (f32[192,4096]{1,0:T(8,128)}, f32[8,128]{1,0:T(8,128)S(1)}) custom-call(f32[192,4096]{1,0:T(8,128)} %teacher_hbm.5, f32[192,4096]{1,0:T(8,128)} %student_hbm.5, f32[4,1024]{1,0:T(4,128)S(1)} %relay.4.after.refs_0_, f32[192,4096]{1,0:T(8,128)} %get-tuple-element.57.before_hbm), custom_call_target="tpu_custom_call", output_to_operand_aliasing={{0}: (3, {})} | custom-call | flops 1 | bytes 1 | tf_op jit(solution)/shard_map/rest/pallas_call | solution.py:35
  43.5 1.7 %collective-permute-done.17.refs_3_ = f32[4,1024]{1,0:T(4,128)S(1)} collective-permute-done((f32[4,1024]{1,0:T(4,128)S(1)}, f32[4,1024]{1,0:T(4,128)S(1)}, u32[]{:S(2)}, u32[]{:S(2)}) %collective-permute-start.17) | collective-permute-done | bytes 16416 | tf_op jit(solution)/shard_map/ppermute | solution.py:46
  45.2 3.9 %gradient.1 = f32[192,2048]{1,0:T(8,128)} custom-call(f32[4,1024]{1,0:T(4,128)S(1)} %relay.5.total_ref, f32[1,128]{1,0:T(1,128)S(1)} %get-tuple-element.35.refs_1_.refs_3_.refs_4_.refs_7_.peak_ref, f32[192,2048]{1,0:T(8,128)S(1)} %get-tuple-element.60.weight_unit, f32[1,2048]{1,0:T(1,128)S(1)} %get-tuple-element.61.weight_scale, ...), custom_call_target="tpu_custom_call" | custom-call | flops 1 | bytes 1 | tf_op jit(solution)/shard_map/gradient/pallas_call | solution.py:35
  (28 shorter events, 3.7 us)
Async XLA Ops:
  0.6 4.8 %collective-permute-start = (s32[1,256]{1,0:T(1,128)}, s32[1,256]{1,0:T(1,128)S(1)}, u32[]{:S(2)}, u32[]{:S(2)}) collective-permute-start(s32[1,256]{1,0:T(1,128)} %param.10), channel_id=1, source_target_pairs={{0,1},{1,0},{2,3},{3,2},{4,5},{5,4},{6,7},{7,6},{8,9},{9,8},{10,11... | collective-permute-start | bytes 3080 | tf_op jit(solution)/shard_map/ppermute | solution.py:46
  5.6 10.1 %collective-permute-start.1 = (bf16[2,192,128]{2,1,0:T(8,128)(2,1)S(1)}, bf16[2,192,128]{2,1,0:T(8,128)(2,1)S(1)}, u32[]{:S(2)}, u32[]{:S(2)}) collective-permute-start(bf16[2,192,128]{2,1,0:T(8,128)(2,1)S(1)} %pack.1.refs_5_), channel_id=1, source_target_pairs={{0,1},{1,0},{2,3},{3,2},{4,5},{5,4},{6,7},{7,6},{8,9},{9,8},{10,11... | collective-permute-start | bytes 294920 | tf_op jit(solution)/shard_map/ppermute | solution.py:46
  7.7 8.0 %collective-permute-start.2 = (bf16[2,192,128]{2,1,0:T(8,128)(2,1)S(1)}, bf16[2,192,128]{2,1,0:T(8,128)(2,1)S(1)}, u32[]{:S(2)}, u32[]{:S(2)}) collective-permute-start(bf16[2,192,128]{2,1,0:T(8,128)(2,1)S(1)} %pack.1.refs_5_), channel_id=1, source_target_pairs={{0,24},{8,16},{16,8},{24,0},{1,25},{9,17},{17,9},{25,1},{2,26},{10... | collective-permute-start | bytes 294920 | tf_op jit(solution)/shard_map/ppermute | solution.py:46
  11.3 6.9 %collective-permute-start.3 = (bf16[2,192,128]{2,1,0:T(8,128)(2,1)S(1)}, bf16[2,192,128]{2,1,0:T(8,128)(2,1)S(1)}, u32[]{:S(2)}, u32[]{:S(2)}) collective-permute-start(bf16[2,192,128]{2,1,0:T(8,128)(2,1)S(1)} %pack.1.refs_5_), channel_id=1, source_target_pairs={{0,16},{8,24},{16,0},{24,8},{1,17},{9,25},{17,1},{25,9},{2,18},{10... | collective-permute-start | bytes 294920 | tf_op jit(solution)/shard_map/ppermute | solution.py:46
  11.3 6.9 %collective-permute-start.4 = (bf16[2,192,128]{2,1,0:T(8,128)(2,1)S(1)}, bf16[2,192,128]{2,1,0:T(8,128)(2,1)S(1)}, u32[]{:S(2)}, u32[]{:S(2)}) collective-permute-start(bf16[2,192,128]{2,1,0:T(8,128)(2,1)S(1)} %pack.1.refs_5_), channel_id=1, source_target_pairs={{0,8},{8,0},{16,24},{24,16},{1,9},{9,1},{17,25},{25,17},{2,10},{10... | collective-permute-start | bytes 294920 | tf_op jit(solution)/shard_map/ppermute | solution.py:46
  18.3 6.3 %collective-permute-start.9 = (bf16[2,2,208,128]{3,2,1,0:T(8,128)(2,1)S(1)}, bf16[2,2,208,128]{3,2,1,0:T(8,128)(2,1)S(1)}, u32[]{:S(2)}, u32[]{:S(2)}) collective-permute-start(bf16[2,2,208,128]{3,2,1,0:T(8,128)(2,1)S(1)} %get-tuple-element.48), channel_id=1, source_target_pairs={{0,1},{1,0},{2,3},{3,2},{4,5},{5,4},{6,7},{7,6},{8,9},{9,8},{10,11... | collective-permute-start | bytes 638984 | tf_op jit(solution)/shard_map/ppermute | solution.py:46
  18.9 2.4 %collective-permute-start.5 = (bf16[2,2,192,128]{3,2,1,0:T(8,128)(2,1)S(1)}, bf16[2,2,192,128]{3,2,1,0:T(8,128)(2,1)S(1)}, u32[]{:S(2)}, u32[]{:S(2)}) collective-permute-start(bf16[2,2,192,128]{3,2,1,0:T(8,128)(2,1)S(1)} %get-tuple-element.40), channel_id=1, source_target_pairs={{0,2},{2,0},{4,6},{6,4},{1,3},{3,1},{5,7},{7,5},{8,10},{10,8},{12,... | collective-permute-start | bytes 589832 | tf_op jit(solution)/shard_map/ppermute | solution.py:46
  18.9 2.4 %collective-permute-start.6 = (bf16[2,2,192,128]{3,2,1,0:T(8,128)(2,1)S(1)}, bf16[2,2,192,128]{3,2,1,0:T(8,128)(2,1)S(1)}, u32[]{:S(2)}, u32[]{:S(2)}) collective-permute-start(bf16[2,2,192,128]{3,2,1,0:T(8,128)(2,1)S(1)} %get-tuple-element.41), channel_id=1, source_target_pairs={{0,2},{2,0},{4,6},{6,4},{1,3},{3,1},{5,7},{7,5},{8,10},{10,8},{12,... | collective-permute-start | bytes 589832 | tf_op jit(solution)/shard_map/ppermute | solution.py:46
  19.4 3.3 %collective-permute-start.7 = (bf16[2,192,128]{2,1,0:T(8,128)(2,1)S(1)}, bf16[2,192,128]{2,1,0:T(8,128)(2,1)S(1)}, u32[]{:S(2)}, u32[]{:S(2)}) collective-permute-start(bf16[2,192,128]{2,1,0:T(8,128)(2,1)S(1)} %collective-permute-done.1.refs_0_), channel_id=1, source_target_pairs={{0,2},{2,0},{4,6},{6,4},{1,3},{3,1},{5,7},{7,5},{8,10},{10,8},{12,... | collective-permute-start | bytes 294920 | tf_op jit(solution)/shard_map/ppermute | solution.py:46
  19.4 5.2 %collective-permute-start.8 = (bf16[2,192,128]{2,1,0:T(8,128)(2,1)S(1)}, bf16[2,192,128]{2,1,0:T(8,128)(2,1)S(1)}, u32[]{:S(2)}, u32[]{:S(2)}) collective-permute-start(bf16[2,192,128]{2,1,0:T(8,128)(2,1)S(1)} %collective-permute-done.1.refs_0_), channel_id=1, source_target_pairs={{0,8},{8,0},{16,24},{24,16},{1,9},{9,1},{17,25},{25,17},{2,10},{10... | collective-permute-start | bytes 294920 | tf_op jit(solution)/shard_map/ppermute | solution.py:46
  24.7 1.6 %collective-permute-start.10 = (bf16[3,2,192,128]{3,2,1,0:T(8,128)(2,1)S(1)}, bf16[3,2,192,128]{3,2,1,0:T(8,128)(2,1)S(1)}, u32[]{:S(2)}, u32[]{:S(2)}) collective-permute-start(bf16[3,2,192,128]{3,2,1,0:T(8,128)(2,1)S(1)} %join.3.refs_0_), channel_id=1, source_target_pairs={{0,2},{2,0},{4,6},{6,4},{1,3},{3,1},{5,7},{7,5},{8,10},{10,8},{12,... | collective-permute-start | bytes 884744 | tf_op jit(solution)/shard_map/ppermute | solution.py:46
  27.6 1.2 %collective-permute-start.11 = (f32[4,1024]{1,0:T(4,128)S(1)}, f32[4,1024]{1,0:T(4,128)S(1)}, u32[]{:S(2)}, u32[]{:S(2)}) collective-permute-start(f32[4,1024]{1,0:T(4,128)S(1)} %get-tuple-element.54.refs_0_), channel_id=1, source_target_pairs={{0,2},{2,0},{4,6},{6,4},{1,3},{3,1},{5,7},{7,5},{8,10},{10,8},{12,... | collective-permute-start | bytes 49160 | tf_op jit(solution)/shard_map/ppermute | solution.py:46
  28.9 6.0 %collective-permute-start.12 = (f32[4,1024]{1,0:T(4,128)S(1)}, f32[4,1024]{1,0:T(4,128)S(1)}, u32[]{:S(2)}, u32[]{:S(2)}) collective-permute-start(f32[4,1024]{1,0:T(4,128)S(1)} %relay.3.after.refs_0_), channel_id=1, source_target_pairs={{0,1},{1,0},{2,3},{3,2},{4,5},{5,4},{6,7},{7,6},{8,9},{9,8},{10,11... | collective-permute-start | bytes 49160 | tf_op jit(solution)/shard_map/ppermute | solution.py:363
  30.5 4.4 %collective-permute-start.13 = (f32[4,1024]{1,0:T(4,128)S(1)}, f32[4,1024]{1,0:T(4,128)S(1)}, u32[]{:S(2)}, u32[]{:S(2)}) collective-permute-start(f32[4,1024]{1,0:T(4,128)S(1)} %relay.3.after.refs_0_), channel_id=1, source_target_pairs={{0,4},{1,5},{2,6},{3,7},{4,0},{5,1},{6,2},{7,3},{8,12},{9,13},{10,... | collective-permute-start | bytes 49160 | tf_op jit(solution)/shard_map/ppermute | solution.py:363
  32.0 4.6 %collective-permute-start.14 = (f32[4,1024]{1,0:T(4,128)S(1)}, f32[4,1024]{1,0:T(4,128)S(1)}, u32[]{:S(2)}, u32[]{:S(2)}) collective-permute-start(f32[4,1024]{1,0:T(4,128)S(1)} %relay.3.after.refs_0_), channel_id=1, source_target_pairs={{0,5},{1,4},{2,7},{3,6},{4,1},{5,0},{6,3},{7,2},{8,13},{9,12},{10,... | collective-permute-start | bytes 49160 | tf_op jit(solution)/shard_map/ppermute | solution.py:363
  36.7 6.9 %collective-permute-start.15 = (f32[4,1024]{1,0:T(4,128)S(1)}, f32[4,1024]{1,0:T(4,128)S(1)}, u32[]{:S(2)}, u32[]{:S(2)}) collective-permute-start(f32[4,1024]{1,0:T(4,128)S(1)} %relay.4.after.refs_0_), channel_id=1, source_target_pairs={{0,8},{8,0},{16,24},{24,16},{1,9},{9,1},{17,25},{25,17},{2,10},{10... | collective-permute-start | bytes 49160 | tf_op jit(solution)/shard_map/ppermute | solution.py:46
  37.2 6.3 %collective-permute-start.16 = (f32[4,1024]{1,0:T(4,128)S(1)}, f32[4,1024]{1,0:T(4,128)S(1)}, u32[]{:S(2)}, u32[]{:S(2)}) collective-permute-start(f32[4,1024]{1,0:T(4,128)S(1)} %relay.4.after.refs_0_), channel_id=1, source_target_pairs={{0,16},{8,24},{16,0},{24,8},{1,17},{9,25},{17,1},{25,9},{2,18},{10... | collective-permute-start | bytes 49160 | tf_op jit(solution)/shard_map/ppermute | solution.py:46
  39.7 5.5 %collective-permute-start.17 = (f32[4,1024]{1,0:T(4,128)S(1)}, f32[4,1024]{1,0:T(4,128)S(1)}, u32[]{:S(2)}, u32[]{:S(2)}) collective-permute-start(f32[4,1024]{1,0:T(4,128)S(1)} %relay.4.after.refs_0_), channel_id=1, source_target_pairs={{0,24},{8,16},{16,8},{24,0},{1,25},{9,17},{17,9},{25,1},{2,26},{10... | collective-permute-start | bytes 49160 | tf_op jit(solution)/shard_map/ppermute | solution.py:46

commit v14 on v12

--- a/solution.py
+++ b/solution.py
@@ -197,14 +197,18 @@
     )
 
 
+def normalize(values):
+    return (values * lax.rsqrt(jnp.sum(values * values, axis=0, keepdims=True) + EPS)).astype(jnp.bfloat16)
+
+
 def pack_kernel(student_ref, teacher_ref, index_ref, out_ref):
     half = out_ref.shape[2]
     lower = here()[2] == 0
-    out_ref[0] = student_ref[...]
+    out_ref[0] = normalize(student_ref[...].astype(jnp.float32))
     index = jnp.where(lower, index_ref[:, :half], index_ref[:, half:])
     row = lax.broadcasted_iota(jnp.int32, (teacher_ref.shape[1], half), 0)
     pick = jnp.where(row == index, 1.0, 0.0).astype(jnp.bfloat16)
-    out_ref[1] = jnp.dot(teacher_ref[...], pick, preferred_element_type=jnp.float32).astype(jnp.bfloat16)
+    out_ref[1] = normalize(jnp.dot(teacher_ref[...], pick, preferred_element_type=jnp.float32))
 
 
 def pack(student, teacher, index):
@@ -261,9 +265,7 @@
         base = (2 * part + which) * n * width
         extra = jnp.where(row < 3 * which, 1.0, 0.0).astype(jnp.bfloat16)
         for group in range(n // per):
-            values = [blocks[group * per + k][which].astype(jnp.float32) for k in range(per)]
-            values = jnp.concatenate(values, axis=1)
-            unit = (values * lax.rsqrt(jnp.sum(values * values, axis=0, keepdims=True) + EPS)).astype(jnp.bfloat16)
+            unit = jnp.concatenate([blocks[group * per + k][which] for k in range(per)], axis=1)
             lanes = slice(group * per * width, (group + 1) * per * width)
             if which == 0:
                 unit_ref[lanes, :] = unit.T
@@ -345,7 +347,7 @@
 
 
 def grad_kernel(total_ref, peak_ref, weight_unit, weight_scale, *refs):
-    units, exp_ref, out_hbm, scales, buf, sems = refs[:4], *refs[4:]
+    units, exp_ref, out_hbm, scales, feats, *derivs, buf, sems = refs[:4], *refs[4:]
     dp, _, core = here()
     scales[0:2, :] = 10.0 / total_ref[0:2, :]
     scales[2:4, :] = 10.0 * jnp.exp2(GAIN_T * peak_ref[:, :1] - total_ref[2:4, :])
@@ -363,19 +365,25 @@
                 for where in at
             ]
             factors.append(jnp.concatenate(picked, axis=1).astype(jnp.bfloat16))
-    feats = jnp.concatenate([unit[...] for unit in units], axis=0)
+    for part, unit in enumerate(units):
+        feats[part * rows:(part + 1) * rows, :] = unit[...]
     chunks, _, step = buf.shape
     stores = []
-    for i in range(chunks):
+
+    def derive(i):
         at = slice(i * step, (i + 1) * step)
-        derivs = []
         for part in range(4):
             lies_s, lies_t = 2 * part * rows, (2 * (part ^ 2) + 1) * rows
             probs_s = exp_ref[at, lies_s:lies_s + rows] * factors[2 * part]
             probs_t = exp_ref[at, lies_t:lies_t + rows] * factors[2 * part + 1]
-            derivs.append(probs_s - probs_t)
-        derivs = jnp.concatenate(derivs, axis=1)
-        grad = jnp.dot(derivs, feats, preferred_element_type=jnp.float32).T
+            derivs[i % 2][:, part * rows:(part + 1) * rows] = probs_s - probs_t
+
+    derive(0)
+    for i in range(chunks):
+        if i + 1 < chunks:
+            derive(i + 1)
+        at = slice(i * step, (i + 1) * step)
+        grad = jnp.dot(derivs[i % 2][...], feats[...], preferred_element_type=jnp.float32).T
         unit = weight_unit[:, at]
         proj = unit * jnp.sum(unit * grad, axis=0, keepdims=True)
         buf[i] = (grad - proj) * weight_scale[:, at]
@@ -388,7 +396,7 @@
 def gradient(total, peak, weight_unit, weight_scale, units, exps):
     cols = exps.shape[0]
     rows, bot = units[0].shape
-    step = min(512, cols)
+    step = min(256, cols)
     args = (total, peak, weight_unit, weight_scale, *units, exps)
     return call(
         grad_kernel,
@@ -396,7 +404,13 @@
         pltpu.HBM((bot, cols), jnp.float32),
         args,
         out_specs=IN_HBM,
-        scratch_shapes=[held(4, 2 * rows), held(cols // step, bot, step), pltpu.SemaphoreType.DMA((cols // step,))],
+        scratch_shapes=[
+            held(4, 2 * rows),
+            held(4 * rows, bot, dtype=jnp.bfloat16),
+            *[held(step, 4 * rows, dtype=jnp.bfloat16)] * 2,
+            held(cols // step, bot, step),
+            pltpu.SemaphoreType.DMA((cols // step,)),
+        ],
     )
 
 
@@ -411,12 +425,13 @@
     weights = (ws, wt, peak)
     bot = mine.shape[1]
     if n_fsdp <= DIRECT:
+        along = [swap(mine, "fsdp", k) for k in range(1, n_fsdp)]
         other = [swap(mine, "dp")]
-        along = [swap(mine, "fsdp", k) for k in range(1, n_fsdp)]
+        other.append(swap(other[0], "fsdp"))
         half = n_fsdp // 2
         outs = [(0, n_fsdp, bot), (2, n_fsdp - 2, bot + 16), (0, half, bot), (half, half, bot)]
-        own, far, *halves = join([mine, *along], outs, (other[0], peak), bot)
-        other += [swap(other[0], "fsdp"), swap(far, "dp")]
+        own, far, *halves = join([mine, *along], outs, (other[1], peak), bot)
+        other.append(swap(far, "dp"))
     else:
         own = lax.all_to_all(jnp.broadcast_to(mine[None], (n_fsdp, *mine.shape)), "fsdp", 0, 0, tiled=True)
         other, halves = [swap(own, "dp")], [own]

time: 46.6 us -> 46.6 us (level)
  Pallas kernels: 19.3 us -> 18.5 us
  starting transfers between devices: 19.4 us -> 20.1 us
    pallas_call x15, Pallas kernels: 19.3 us -> 18.5 us  [call(): pl.pallas_call(kernel, out_shape=out_shape, compiler_params=pltpu.Compile...]
    ppermute x14, starting transfers between devices: 15.9 us -> 16.6 us  [swap(): lax.ppermute(block, axis, [(i, i ^ apart) for i in range(lax.axis_size(ax...]
  transfers between devices with their start and end apart: 17 -> 17, of which waited for: 8 -> 7; matrix products, arithmetic and copies ran while one was open for 0% -> 0% of each run, Pallas kernels for 30% -> 29%
where the time goes in v14:
time: 46.6 us; the launch traced here: 46.4 us
  starting transfers between devices  20.1 us (43%)
  Pallas kernels  18.5 us (40%)
  waiting for transfers between devices  6.98 us (15%)
  between operations  0.79 us (2%)
    pallas_call x15, Pallas kernels, call(): pl.pallas_call(kernel, out_shape=out_shape, compiler_params=pltpu.Compile...  18.5 us
    ppermute x14, starting transfers between devices, swap(): lax.ppermute(block, axis, [(i, i ^ apart) for i in range(lax.axis_size(ax...  16.6 us
    ppermute x14, waiting for transfers between devices, swap(): lax.ppermute(block, axis, [(i, i ^ apart) for i in range(lax.axis_size(ax...  6.98 us
    ppermute x3, starting transfers between devices, across(): return lax.ppermute(total, ('proto', 'dp'), pairs)  3.55 us
  transfers between devices with their start and end apart: 17, of which 7 were waited for; matrix products, arithmetic and copies ran while one was open for 0% of the time, Pallas kernels for 29%

profile of v14, /device:TPU:0, one launch (start us, length us, event | category | flops | bytes accessed | tf_op | source)
XLA Modules:
  0.0 46.4 jit_solution(564313220857960263)
XLA Ops:
  0.6 3.0 %collective-permute-start = (s32[1,256]{1,0:T(1,128)}, s32[1,256]{1,0:T(1,128)S(1)}, u32[]{:S(2)}, u32[]{:S(2)}) collective-permute-start(s32[1,256]{1,0:T(1,128)} %param.10), channel_id=1, source_target_pairs={{0,1},{1,0},{2,3},{3,2},{4,5},{5,4},{6,7},{7,6},{8,9},{9,8},{10,11... | collective-permute-start | bytes 3080 | tf_op jit(solution)/shard_map/ppermute | solution.py:46
  3.6 0.9 %fetch.1 = (bf16[192,128]{1,0:T(8,128)(2,1)S(1)}, bf16[192,256]{1,0:T(8,128)(2,1)S(1)}) custom-call(bf16[192,256]{1,0:T(8,128)(2,1)} %bitcast.7, bf16[192,256]{1,0:T(8,128)(2,1)} %bitcast.8), custom_call_target="tpu_custom_call" | custom-call | flops 1 | bytes 1 | tf_op jit(solution)/shard_map/fetch/pallas_call | solution.py:35
  4.6 0.8 %collective-permute-done.index_ref = s32[1,256]{1,0:T(1,128)S(1)} collective-permute-done((s32[1,256]{1,0:T(1,128)}, s32[1,256]{1,0:T(1,128)S(1)}, u32[]{:S(2)}, u32[]{:S(2)}) %collective-permute-start) | collective-permute-done | bytes 1056 | tf_op jit(solution)/shard_map/ppermute | solution.py:46
  5.6 2.1 %collective-permute-start.4 = (bf16[2,192,128]{2,1,0:T(8,128)(2,1)S(1)}, bf16[2,192,128]{2,1,0:T(8,128)(2,1)S(1)}, u32[]{:S(2)}, u32[]{:S(2)}) collective-permute-start(bf16[2,192,128]{2,1,0:T(8,128)(2,1)S(1)} %pack.1.refs_0_), channel_id=1, source_target_pairs={{0,1},{1,0},{2,3},{3,2},{4,5},{5,4},{6,7},{7,6},{8,9},{9,8},{10,11... | collective-permute-start | bytes 294920 | tf_op jit(solution)/shard_map/ppermute | solution.py:46
  7.7 3.6 %collective-permute-start.3 = (bf16[2,192,128]{2,1,0:T(8,128)(2,1)S(1)}, bf16[2,192,128]{2,1,0:T(8,128)(2,1)S(1)}, u32[]{:S(2)}, u32[]{:S(2)}) collective-permute-start(bf16[2,192,128]{2,1,0:T(8,128)(2,1)S(1)} %pack.1.refs_0_), channel_id=1, source_target_pairs={{0,24},{8,16},{16,8},{24,0},{1,25},{9,17},{17,9},{25,1},{2,26},{10... | collective-permute-start | bytes 294920 | tf_op jit(solution)/shard_map/ppermute | solution.py:46
  11.3 0.8 %collective-permute-start.1 = (bf16[2,192,128]{2,1,0:T(8,128)(2,1)S(1)}, bf16[2,192,128]{2,1,0:T(8,128)(2,1)S(1)}, u32[]{:S(2)}, u32[]{:S(2)}) collective-permute-start(bf16[2,192,128]{2,1,0:T(8,128)(2,1)S(1)} %pack.1.refs_0_), channel_id=1, source_target_pairs={{0,8},{8,0},{16,24},{24,16},{1,9},{9,1},{17,25},{25,17},{2,10},{10... | collective-permute-start | bytes 294920 | tf_op jit(solution)/shard_map/ppermute | solution.py:46
  12.1 1.2 %collective-permute-start.5 = (bf16[2,192,128]{2,1,0:T(8,128)(2,1)S(1)}, bf16[2,192,128]{2,1,0:T(8,128)(2,1)S(1)}, u32[]{:S(2)}, u32[]{:S(2)}) collective-permute-start(bf16[2,192,128]{2,1,0:T(8,128)(2,1)S(1)} %collective-permute-done.4.refs_0_), channel_id=1, source_target_pairs={{0,8},{8,0},{16,24},{24,16},{1,9},{9,1},{17,25},{25,17},{2,10},{10... | collective-permute-start | bytes 294920 | tf_op jit(solution)/shard_map/ppermute | solution.py:46
  13.3 3.6 %prep.1 = (f32[192,4096]{1,0:T(8,128)}, bf16[2048,256]{1,0:T(8,128)(2,1)S(1)}, bf16[2048,256]{1,0:T(8,128)(2,1)S(1)}, f32[192,2048]{1,0:T(8,128)S(1)}, f32[1,2048]{1,0:T(1,128)S(1)}, /*index=5*/f32[1,128]{1,0:T(1,128)S(1)}) custom-call(f32[192,4096]{1,0:T(8,128)} %teacher_hbm.5, f32[192,4096]{1,0:T(8,128)} %student_hbm.5, f32[1,16384]{1,0:T(1,128)} %bitcast.9), custom_call_target="tpu_custom_call" | custom-call | flops 1 | bytes 1 | tf_op jit(solution)/shard_map/prep/pallas_call | solution.py:35
  16.9 1.4 %collective-permute-done.2.refs_2_ = bf16[2,192,128]{2,1,0:T(8,128)(2,1)S(1)} collective-permute-done((bf16[2,192,128]{2,1,0:T(8,128)(2,1)S(1)}, bf16[2,192,128]{2,1,0:T(8,128)(2,1)S(1)}, u32[]{:S(2)}, u32[]{:S(2)}) %collective-permute-start.2) | collective-permute-done | bytes 98336 | tf_op jit(solution)/shard_map/ppermute | solution.py:46
  18.3 1.1 %collective-permute-done.5.refs_4_.refs_1_ = bf16[2,192,128]{2,1,0:T(8,128)(2,1)S(1)} collective-permute-done((bf16[2,192,128]{2,1,0:T(8,128)(2,1)S(1)}, bf16[2,192,128]{2,1,0:T(8,128)(2,1)S(1)}, u32[]{:S(2)}, u32[]{:S(2)}) %collective-permute-start.5) | collective-permute-done | bytes 98336 | tf_op jit(solution)/shard_map/ppermute | solution.py:46
  19.5 0.6 %collective-permute-start.8 = (bf16[2,2,208,128]{3,2,1,0:T(8,128)(2,1)S(1)}, bf16[2,2,208,128]{3,2,1,0:T(8,128)(2,1)S(1)}, u32[]{:S(2)}, u32[]{:S(2)}) collective-permute-start(bf16[2,2,208,128]{3,2,1,0:T(8,128)(2,1)S(1)} %get-tuple-element.41), channel_id=1, source_target_pairs={{0,1},{1,0},{2,3},{3,2},{4,5},{5,4},{6,7},{7,6},{8,9},{9,8},{10,11... | collective-permute-start | bytes 638984 | tf_op jit(solution)/shard_map/ppermute | solution.py:46
  20.6 1.3 %scores.4 = (bf16[2048,4096]{1,0:T(8,128)(2,1)S(1)}, bf16[512,192]{1,0:T(8,128)(2,1)S(1)}, f32[2,512]{1,0:T(2,128)S(1)}) custom-call(bf16[4,2,192,128]{3,2,1,0:T(8,128)(2,1)S(1)} %get-tuple-element.33.refs_0_, bf16[2048,256]{1,0:T(8,128)(2,1)S(1)} %get-tuple-element.34.refs_1_.refs_2_.refs_4_, ...), custom_call_target="tpu_custom_call" | custom-call | flops 1 | bytes 1 | tf_op jit(solution)/shard_map/scores/pallas_call | solution.py:35
  21.9 1.3 %scores.5 = (bf16[2048,4096]{1,0:T(8,128)(2,1)S(1)}, bf16[512,192]{1,0:T(8,128)(2,1)S(1)}, f32[2,512]{1,0:T(2,128)S(1)}) custom-call(bf16[2,2,192,128]{3,2,1,0:T(8,128)(2,1)S(1)} %collective-permute-done.6.refs_0_, bf16[2,2,192,128]{3,2,1,0:T(8,128)(2,1)S(1)} %collective-permute-done.7.refs_1_, ...), custom_call_target="tpu_custom_call", output_to_operand_aliasing={{0}: (5, {})} | custom-call | flops 1 | bytes 1 | tf_op jit(solution)/shard_map/scores/pallas_call | solution.py:35
  23.2 2.1 %collective-permute-done.8.refs_2_ = bf16[2,2,208,128]{3,2,1,0:T(8,128)(2,1)S(1)} collective-permute-done((bf16[2,2,208,128]{3,2,1,0:T(8,128)(2,1)S(1)}, bf16[2,2,208,128]{3,2,1,0:T(8,128)(2,1)S(1)}, u32[]{:S(2)}, u32[]{:S(2)}) %collective-permute-start.8) | collective-permute-done | bytes 213024 | tf_op jit(solution)/shard_map/ppermute | solution.py:46
  25.5 1.3 %scores.6 = (bf16[2048,4096]{1,0:T(8,128)(2,1)S(1)}, bf16[512,192]{1,0:T(8,128)(2,1)S(1)}, f32[2,512]{1,0:T(2,128)S(1)}) custom-call(bf16[4,2,192,128]{3,2,1,0:T(8,128)(2,1)S(1)} %join.3.refs_0_, bf16[2048,256]{1,0:T(8,128)(2,1)S(1)} %get-tuple-element.34.refs_1_.refs_2_.refs_4_, ...), custom_call_target="tpu_custom_call", output_to_operand_aliasing={{0}: (4, {})} | custom-call | flops 1 | bytes 1 | tf_op jit(solution)/shard_map/scores/pallas_call | solution.py:35
  27.2 1.3 %scores.7 = (bf16[2048,4096]{1,0:T(8,128)(2,1)S(1)}, bf16[512,192]{1,0:T(8,128)(2,1)S(1)}, f32[4,1024]{1,0:T(4,128)S(1)}) custom-call(f32[2,512]{1,0:T(2,128)S(1)} %get-tuple-element.36.refs_0_, f32[2,512]{1,0:T(2,128)S(1)} %get-tuple-element.40.refs_3_.refs_1_, f32[2,512]{1,0:T(2,128)S(1)} %get-tuple-element.43.refs_2_, ...), custom_call_target="tpu_custom_call", output_to_operand_aliasing={{0}: (7, {})} | custom-call | flops 1 | bytes 1 | tf_op jit(solution)/shard_map/scores/pallas_call | solution.py:35
  28.8 1.0 %collective-permute-done.10.refs_1_ = f32[4,1024]{1,0:T(4,128)S(1)} collective-permute-done((f32[4,1024]{1,0:T(4,128)S(1)}, f32[4,1024]{1,0:T(4,128)S(1)}, u32[]{:S(2)}, u32[]{:S(2)}) %collective-permute-start.10) | collective-permute-done | bytes 16416 | tf_op jit(solution)/shard_map/ppermute | solution.py:46
  29.8 1.6 %collective-permute-start.13 = (f32[4,1024]{1,0:T(4,128)S(1)}, f32[4,1024]{1,0:T(4,128)S(1)}, u32[]{:S(2)}, u32[]{:S(2)}) collective-permute-start(f32[4,1024]{1,0:T(4,128)S(1)} %relay.3.after.refs_0_), channel_id=1, source_target_pairs={{0,5},{1,4},{2,7},{3,6},{4,1},{5,0},{6,3},{7,2},{8,13},{9,12},{10,... | collective-permute-start | bytes 49160 | tf_op jit(solution)/shard_map/ppermute | solution.py:339
  31.9 1.5 %collective-permute-start.11 = (f32[4,1024]{1,0:T(4,128)S(1)}, f32[4,1024]{1,0:T(4,128)S(1)}, u32[]{:S(2)}, u32[]{:S(2)}) collective-permute-start(f32[4,1024]{1,0:T(4,128)S(1)} %relay.3.after.refs_0_), channel_id=1, source_target_pairs={{0,1},{1,0},{2,3},{3,2},{4,5},{5,4},{6,7},{7,6},{8,9},{9,8},{10,11... | collective-permute-start | bytes 49160 | tf_op jit(solution)/shard_map/ppermute | solution.py:339
  33.4 2.4 %rest.2 = (f32[192,4096]{1,0:T(8,128)}, f32[8,128]{1,0:T(8,128)S(1)}) custom-call(f32[192,4096]{1,0:T(8,128)} %teacher_hbm.5, f32[192,4096]{1,0:T(8,128)} %student_hbm.5, f32[4,1024]{1,0:T(4,128)S(1)} %relay.3.after.refs_0_, f32[192,4096]{1,0:T(8,128)} %get-tuple-element.46.before_hbm), custom_call_target="tpu_custom_call", output_to_operand_aliasing={{0}: (3, {})} | custom-call | flops 1 | bytes 1 | tf_op jit(solution)/shard_map/rest/pallas_call | solution.py:35
  35.9 2.3 %collective-permute-start.16 = (f32[4,1024]{1,0:T(4,128)S(1)}, f32[4,1024]{1,0:T(4,128)S(1)}, u32[]{:S(2)}, u32[]{:S(2)}) collective-permute-start(f32[4,1024]{1,0:T(4,128)S(1)} %relay.4.after.refs_0_), channel_id=1, source_target_pairs={{0,24},{8,16},{16,8},{24,0},{1,25},{9,17},{17,9},{25,1},{2,26},{10... | collective-permute-start | bytes 49160 | tf_op jit(solution)/shard_map/ppermute | solution.py:46
  38.8 1.5 %collective-permute-start.14 = (f32[4,1024]{1,0:T(4,128)S(1)}, f32[4,1024]{1,0:T(4,128)S(1)}, u32[]{:S(2)}, u32[]{:S(2)}) collective-permute-start(f32[4,1024]{1,0:T(4,128)S(1)} %relay.4.after.refs_0_), channel_id=1, source_target_pairs={{0,8},{8,0},{16,24},{24,16},{1,9},{9,1},{17,25},{25,17},{2,10},{10... | collective-permute-start | bytes 49160 | tf_op jit(solution)/shard_map/ppermute | solution.py:46
  40.3 2.4 %rest.3 = (f32[192,4096]{1,0:T(8,128)}, f32[8,128]{1,0:T(8,128)S(1)}) custom-call(f32[192,4096]{1,0:T(8,128)} %teacher_hbm.5, f32[192,4096]{1,0:T(8,128)} %student_hbm.5, f32[4,1024]{1,0:T(4,128)S(1)} %relay.4.after.refs_0_, f32[192,4096]{1,0:T(8,128)} %get-tuple-element.48.before_hbm), custom_call_target="tpu_custom_call", output_to_operand_aliasing={{0}: (3, {})} | custom-call | flops 1 | bytes 1 | tf_op jit(solution)/shard_map/rest/pallas_call | solution.py:35
  42.9 3.5 %gradient.1 = f32[192,2048]{1,0:T(8,128)} custom-call(f32[4,1024]{1,0:T(4,128)S(1)} %relay.5.total_ref, f32[1,128]{1,0:T(1,128)S(1)} %get-tuple-element.32.refs_5_.refs_3_.refs_4_.refs_6_.peak_ref, f32[192,2048]{1,0:T(8,128)S(1)} %get-tuple-element.51.weight_unit, f32[1,2048]{1,0:T(1,128)S(1)} %get-tuple-element.52.weight_scale, ...), custom_call_target="tpu_custom_call" | custom-call | flops 1 | bytes 1 | tf_op jit(solution)/shard_map/gradient/pallas_call | solution.py:35
  (25 shorter events, 2.8 us)
Async XLA Ops:
  0.6 4.8 %collective-permute-start = (s32[1,256]{1,0:T(1,128)}, s32[1,256]{1,0:T(1,128)S(1)}, u32[]{:S(2)}, u32[]{:S(2)}) collective-permute-start(s32[1,256]{1,0:T(1,128)} %param.10), channel_id=1, source_target_pairs={{0,1},{1,0},{2,3},{3,2},{4,5},{5,4},{6,7},{7,6},{8,9},{9,8},{10,11... | collective-permute-start | bytes 3080 | tf_op jit(solution)/shard_map/ppermute | solution.py:46
  5.6 6.5 %collective-permute-start.4 = (bf16[2,192,128]{2,1,0:T(8,128)(2,1)S(1)}, bf16[2,192,128]{2,1,0:T(8,128)(2,1)S(1)}, u32[]{:S(2)}, u32[]{:S(2)}) collective-permute-start(bf16[2,192,128]{2,1,0:T(8,128)(2,1)S(1)} %pack.1.refs_0_), channel_id=1, source_target_pairs={{0,1},{1,0},{2,3},{3,2},{4,5},{5,4},{6,7},{7,6},{8,9},{9,8},{10,11... | collective-permute-start | bytes 294920 | tf_op jit(solution)/shard_map/ppermute | solution.py:46
  7.7 9.2 %collective-permute-start.3 = (bf16[2,192,128]{2,1,0:T(8,128)(2,1)S(1)}, bf16[2,192,128]{2,1,0:T(8,128)(2,1)S(1)}, u32[]{:S(2)}, u32[]{:S(2)}) collective-permute-start(bf16[2,192,128]{2,1,0:T(8,128)(2,1)S(1)} %pack.1.refs_0_), channel_id=1, source_target_pairs={{0,24},{8,16},{16,8},{24,0},{1,25},{9,17},{17,9},{25,1},{2,26},{10... | collective-permute-start | bytes 294920 | tf_op jit(solution)/shard_map/ppermute | solution.py:46
  11.3 7.0 %collective-permute-start.2 = (bf16[2,192,128]{2,1,0:T(8,128)(2,1)S(1)}, bf16[2,192,128]{2,1,0:T(8,128)(2,1)S(1)}, u32[]{:S(2)}, u32[]{:S(2)}) collective-permute-start(bf16[2,192,128]{2,1,0:T(8,128)(2,1)S(1)} %pack.1.refs_0_), channel_id=1, source_target_pairs={{0,16},{8,24},{16,0},{24,8},{1,17},{9,25},{17,1},{25,9},{2,18},{10... | collective-permute-start | bytes 294920 | tf_op jit(solution)/shard_map/ppermute | solution.py:46
  11.3 7.0 %collective-permute-start.1 = (bf16[2,192,128]{2,1,0:T(8,128)(2,1)S(1)}, bf16[2,192,128]{2,1,0:T(8,128)(2,1)S(1)}, u32[]{:S(2)}, u32[]{:S(2)}) collective-permute-start(bf16[2,192,128]{2,1,0:T(8,128)(2,1)S(1)} %pack.1.refs_0_), channel_id=1, source_target_pairs={{0,8},{8,0},{16,24},{24,16},{1,9},{9,1},{17,25},{25,17},{2,10},{10... | collective-permute-start | bytes 294920 | tf_op jit(solution)/shard_map/ppermute | solution.py:46
  12.1 7.3 %collective-permute-start.5 = (bf16[2,192,128]{2,1,0:T(8,128)(2,1)S(1)}, bf16[2,192,128]{2,1,0:T(8,128)(2,1)S(1)}, u32[]{:S(2)}, u32[]{:S(2)}) collective-permute-start(bf16[2,192,128]{2,1,0:T(8,128)(2,1)S(1)} %collective-permute-done.4.refs_0_), channel_id=1, source_target_pairs={{0,8},{8,0},{16,24},{24,16},{1,9},{9,1},{17,25},{25,17},{2,10},{10... | collective-permute-start | bytes 294920 | tf_op jit(solution)/shard_map/ppermute | solution.py:46
  19.5 5.9 %collective-permute-start.8 = (bf16[2,2,208,128]{3,2,1,0:T(8,128)(2,1)S(1)}, bf16[2,2,208,128]{3,2,1,0:T(8,128)(2,1)S(1)}, u32[]{:S(2)}, u32[]{:S(2)}) collective-permute-start(bf16[2,2,208,128]{3,2,1,0:T(8,128)(2,1)S(1)} %get-tuple-element.41), channel_id=1, source_target_pairs={{0,1},{1,0},{2,3},{3,2},{4,5},{5,4},{6,7},{7,6},{8,9},{9,8},{10,11... | collective-permute-start | bytes 638984 | tf_op jit(solution)/shard_map/ppermute | solution.py:46
  20.1 1.8 %collective-permute-start.6 = (bf16[2,2,192,128]{3,2,1,0:T(8,128)(2,1)S(1)}, bf16[2,2,192,128]{3,2,1,0:T(8,128)(2,1)S(1)}, u32[]{:S(2)}, u32[]{:S(2)}) collective-permute-start(bf16[2,2,192,128]{3,2,1,0:T(8,128)(2,1)S(1)} %get-tuple-element.37), channel_id=1, source_target_pairs={{0,2},{2,0},{4,6},{6,4},{1,3},{3,1},{5,7},{7,5},{8,10},{10,8},{12,... | collective-permute-start | bytes 589832 | tf_op jit(solution)/shard_map/ppermute | solution.py:46
  20.1 1.8 %collective-permute-start.7 = (bf16[2,2,192,128]{3,2,1,0:T(8,128)(2,1)S(1)}, bf16[2,2,192,128]{3,2,1,0:T(8,128)(2,1)S(1)}, u32[]{:S(2)}, u32[]{:S(2)}) collective-permute-start(bf16[2,2,192,128]{3,2,1,0:T(8,128)(2,1)S(1)} %get-tuple-element.38), channel_id=1, source_target_pairs={{0,2},{2,0},{4,6},{6,4},{1,3},{3,1},{5,7},{7,5},{8,10},{10,8},{12,... | collective-permute-start | bytes 589832 | tf_op jit(solution)/shard_map/ppermute | solution.py:46
  25.4 1.8 %collective-permute-start.9 = (bf16[4,2,192,128]{3,2,1,0:T(8,128)(2,1)S(1)}, bf16[4,2,192,128]{3,2,1,0:T(8,128)(2,1)S(1)}, u32[]{:S(2)}, u32[]{:S(2)}) collective-permute-start(bf16[4,2,192,128]{3,2,1,0:T(8,128)(2,1)S(1)} %join.3.refs_0_), channel_id=1, source_target_pairs={{0,2},{2,0},{4,6},{6,4},{1,3},{3,1},{5,7},{7,5},{8,10},{10,8},{12,... | collective-permute-start | bytes 1179656 | tf_op jit(solution)/shard_map/ppermute | solution.py:46
  28.6 1.2 %collective-permute-start.10 = (f32[4,1024]{1,0:T(4,128)S(1)}, f32[4,1024]{1,0:T(4,128)S(1)}, u32[]{:S(2)}, u32[]{:S(2)}) collective-permute-start(f32[4,1024]{1,0:T(4,128)S(1)} %get-tuple-element.45.refs_0_), channel_id=1, source_target_pairs={{0,2},{2,0},{4,6},{6,4},{1,3},{3,1},{5,7},{7,5},{8,10},{10,8},{12,... | collective-permute-start | bytes 49160 | tf_op jit(solution)/shard_map/ppermute | solution.py:46
  29.8 6.0 %collective-permute-start.13 = (f32[4,1024]{1,0:T(4,128)S(1)}, f32[4,1024]{1,0:T(4,128)S(1)}, u32[]{:S(2)}, u32[]{:S(2)}) collective-permute-start(f32[4,1024]{1,0:T(4,128)S(1)} %relay.3.after.refs_0_), channel_id=1, source_target_pairs={{0,5},{1,4},{2,7},{3,6},{4,1},{5,0},{6,3},{7,2},{8,13},{9,12},{10,... | collective-permute-start | bytes 49160 | tf_op jit(solution)/shard_map/ppermute | solution.py:339
  31.4 4.4 %collective-permute-start.12 = (f32[4,1024]{1,0:T(4,128)S(1)}, f32[4,1024]{1,0:T(4,128)S(1)}, u32[]{:S(2)}, u32[]{:S(2)}) collective-permute-start(f32[4,1024]{1,0:T(4,128)S(1)} %relay.3.after.refs_0_), channel_id=1, source_target_pairs={{0,4},{1,5},{2,6},{3,7},{4,0},{5,1},{6,2},{7,3},{8,12},{9,13},{10,... | collective-permute-start | bytes 49160 | tf_op jit(solution)/shard_map/ppermute | solution.py:339
  31.9 3.9 %collective-permute-start.11 = (f32[4,1024]{1,0:T(4,128)S(1)}, f32[4,1024]{1,0:T(4,128)S(1)}, u32[]{:S(2)}, u32[]{:S(2)}) collective-permute-start(f32[4,1024]{1,0:T(4,128)S(1)} %relay.3.after.refs_0_), channel_id=1, source_target_pairs={{0,1},{1,0},{2,3},{3,2},{4,5},{5,4},{6,7},{7,6},{8,9},{9,8},{10,11... | collective-permute-start | bytes 49160 | tf_op jit(solution)/shard_map/ppermute | solution.py:339
  35.9 6.9 %collective-permute-start.16 = (f32[4,1024]{1,0:T(4,128)S(1)}, f32[4,1024]{1,0:T(4,128)S(1)}, u32[]{:S(2)}, u32[]{:S(2)}) collective-permute-start(f32[4,1024]{1,0:T(4,128)S(1)} %relay.4.after.refs_0_), channel_id=1, source_target_pairs={{0,24},{8,16},{16,8},{24,0},{1,25},{9,17},{17,9},{25,1},{2,26},{10... | collective-permute-start | bytes 49160 | tf_op jit(solution)/shard_map/ppermute | solution.py:46
  38.2 4.6 %collective-permute-start.15 = (f32[4,1024]{1,0:T(4,128)S(1)}, f32[4,1024]{1,0:T(4,128)S(1)}, u32[]{:S(2)}, u32[]{:S(2)}) collective-permute-start(f32[4,1024]{1,0:T(4,128)S(1)} %relay.4.after.refs_0_), channel_id=1, source_target_pairs={{0,16},{8,24},{16,0},{24,8},{1,17},{9,25},{17,1},{25,9},{2,18},{10... | collective-permute-start | bytes 49160 | tf_op jit(solution)/shard_map/ppermute | solution.py:46
  38.8 4.1 %collective-permute-start.14 = (f32[4,1024]{1,0:T(4,128)S(1)}, f32[4,1024]{1,0:T(4,128)S(1)}, u32[]{:S(2)}, u32[]{:S(2)}) collective-permute-start(f32[4,1024]{1,0:T(4,128)S(1)} %relay.4.after.refs_0_), channel_id=1, source_target_pairs={{0,8},{8,0},{16,24},{24,16},{1,9},{9,1},{17,25},{25,17},{2,10},{10... | collective-permute-start | bytes 49160 | tf_op jit(solution)/shard_map/ppermute | solution.py:46

commit v15 on v14

--- a/solution.py
+++ b/solution.py
@@ -425,13 +425,12 @@
     weights = (ws, wt, peak)
     bot = mine.shape[1]
     if n_fsdp <= DIRECT:
+        other = [swap(mine, "dp")]
         along = [swap(mine, "fsdp", k) for k in range(1, n_fsdp)]
-        other = [swap(mine, "dp")]
-        other.append(swap(other[0], "fsdp"))
         half = n_fsdp // 2
         outs = [(0, n_fsdp, bot), (2, n_fsdp - 2, bot + 16), (0, half, bot), (half, half, bot)]
-        own, far, *halves = join([mine, *along], outs, (other[1], peak), bot)
-        other.append(swap(far, "dp"))
+        own, far, *halves = join([mine, *along], outs, (other[0], peak), bot)
+        other += [swap(other[0], "fsdp"), swap(far, "dp")]
     else:
         own = lax.all_to_all(jnp.broadcast_to(mine[None], (n_fsdp, *mine.shape)), "fsdp", 0, 0, tiled=True)
         other, halves = [swap(own, "dp")], [own]

time: 46.6 us -> 46.2 us (level)
  starting transfers between devices: 20.1 us -> 19.3 us
    ppermute x14, starting transfers between devices: 16.6 us -> 15.7 us  [swap(): lax.ppermute(block, axis, [(i, i ^ apart) for i in range(lax.axis_size(ax...]
  transfers between devices with their start and end apart: 17 -> 17, of which waited for: 7 -> 8; matrix products, arithmetic and copies ran while one was open for 0% -> 0% of each run, Pallas kernels for 29% -> 29%
where the time goes in v15:
time: 46.2 us; the launch traced here: 46 us
  starting transfers between devices  19.3 us (42%)
  Pallas kernels  18.5 us (40%)
  waiting for transfers between devices  7.41 us (16%)
  between operations  0.79 us (2%)
    pallas_call x15, Pallas kernels, call(): pl.pallas_call(kernel, out_shape=out_shape, compiler_params=pltpu.Compile...  18.5 us
    ppermute x14, starting transfers between devices, swap(): lax.ppermute(block, axis, [(i, i ^ apart) for i in range(lax.axis_size(ax...  15.7 us
    ppermute x14, waiting for transfers between devices, swap(): lax.ppermute(block, axis, [(i, i ^ apart) for i in range(lax.axis_size(ax...  7.15 us
    ppermute x3, starting transfers between devices, across(): return lax.ppermute(total, ('proto', 'dp'), pairs)  3.55 us
  transfers between devices with their start and end apart: 17, of which 8 were waited for; matrix products, arithmetic and copies ran while one was open for 0% of the time, Pallas kernels for 29%

profile of v15, /device:TPU:0, one launch (start us, length us, event | category | flops | bytes accessed | tf_op | source)
XLA Modules:
  0.0 46.0 jit_solution(18381994545089753123)
XLA Ops:
  0.6 3.0 %collective-permute-start = (s32[1,256]{1,0:T(1,128)}, s32[1,256]{1,0:T(1,128)S(1)}, u32[]{:S(2)}, u32[]{:S(2)}) collective-permute-start(s32[1,256]{1,0:T(1,128)} %param.10), channel_id=1, source_target_pairs={{0,1},{1,0},{2,3},{3,2},{4,5},{5,4},{6,7},{7,6},{8,9},{9,8},{10,11... | collective-permute-start | bytes 3080 | tf_op jit(solution)/shard_map/ppermute | solution.py:46
  3.6 0.9 %fetch.1 = (bf16[192,128]{1,0:T(8,128)(2,1)S(1)}, bf16[192,256]{1,0:T(8,128)(2,1)S(1)}) custom-call(bf16[192,256]{1,0:T(8,128)(2,1)} %bitcast.7, bf16[192,256]{1,0:T(8,128)(2,1)} %bitcast.8), custom_call_target="tpu_custom_call" | custom-call | flops 1 | bytes 1 | tf_op jit(solution)/shard_map/fetch/pallas_call | solution.py:35
  4.6 0.8 %collective-permute-done.index_ref = s32[1,256]{1,0:T(1,128)S(1)} collective-permute-done((s32[1,256]{1,0:T(1,128)}, s32[1,256]{1,0:T(1,128)S(1)}, u32[]{:S(2)}, u32[]{:S(2)}) %collective-permute-start) | collective-permute-done | bytes 1056 | tf_op jit(solution)/shard_map/ppermute | solution.py:46
  5.6 2.1 %collective-permute-start.4 = (bf16[2,192,128]{2,1,0:T(8,128)(2,1)S(1)}, bf16[2,192,128]{2,1,0:T(8,128)(2,1)S(1)}, u32[]{:S(2)}, u32[]{:S(2)}) collective-permute-start(bf16[2,192,128]{2,1,0:T(8,128)(2,1)S(1)} %pack.1.refs_0_), channel_id=1, source_target_pairs={{0,1},{1,0},{2,3},{3,2},{4,5},{5,4},{6,7},{7,6},{8,9},{9,8},{10,11... | collective-permute-start | bytes 294920 | tf_op jit(solution)/shard_map/ppermute | solution.py:46
  7.7 3.6 %collective-permute-start.3 = (bf16[2,192,128]{2,1,0:T(8,128)(2,1)S(1)}, bf16[2,192,128]{2,1,0:T(8,128)(2,1)S(1)}, u32[]{:S(2)}, u32[]{:S(2)}) collective-permute-start(bf16[2,192,128]{2,1,0:T(8,128)(2,1)S(1)} %pack.1.refs_0_), channel_id=1, source_target_pairs={{0,24},{8,16},{16,8},{24,0},{1,25},{9,17},{17,9},{25,1},{2,26},{10... | collective-permute-start | bytes 294920 | tf_op jit(solution)/shard_map/ppermute | solution.py:46
  11.3 0.8 %collective-permute-start.1 = (bf16[2,192,128]{2,1,0:T(8,128)(2,1)S(1)}, bf16[2,192,128]{2,1,0:T(8,128)(2,1)S(1)}, u32[]{:S(2)}, u32[]{:S(2)}) collective-permute-start(bf16[2,192,128]{2,1,0:T(8,128)(2,1)S(1)} %pack.1.refs_0_), channel_id=1, source_target_pairs={{0,8},{8,0},{16,24},{24,16},{1,9},{9,1},{17,25},{25,17},{2,10},{10... | collective-permute-start | bytes 294920 | tf_op jit(solution)/shard_map/ppermute | solution.py:46
  12.1 3.6 %prep.1 = (f32[192,4096]{1,0:T(8,128)}, bf16[2048,256]{1,0:T(8,128)(2,1)S(1)}, bf16[2048,256]{1,0:T(8,128)(2,1)S(1)}, f32[192,2048]{1,0:T(8,128)S(1)}, f32[1,2048]{1,0:T(1,128)S(1)}, /*index=5*/f32[1,128]{1,0:T(1,128)S(1)}) custom-call(f32[192,4096]{1,0:T(8,128)} %teacher_hbm.5, f32[192,4096]{1,0:T(8,128)} %student_hbm.5, f32[1,16384]{1,0:T(1,128)} %bitcast.9), custom_call_target="tpu_custom_call" | custom-call | flops 1 | bytes 1 | tf_op jit(solution)/shard_map/prep/pallas_call | solution.py:35
  15.7 2.5 %collective-permute-done.2.refs_2_ = bf16[2,192,128]{2,1,0:T(8,128)(2,1)S(1)} collective-permute-done((bf16[2,192,128]{2,1,0:T(8,128)(2,1)S(1)}, bf16[2,192,128]{2,1,0:T(8,128)(2,1)S(1)}, u32[]{:S(2)}, u32[]{:S(2)}) %collective-permute-start.2) | collective-permute-done | bytes 98336 | tf_op jit(solution)/shard_map/ppermute | solution.py:46
  18.3 0.6 %collective-permute-start.8 = (bf16[2,2,208,128]{3,2,1,0:T(8,128)(2,1)S(1)}, bf16[2,2,208,128]{3,2,1,0:T(8,128)(2,1)S(1)}, u32[]{:S(2)}, u32[]{:S(2)}) collective-permute-start(bf16[2,2,208,128]{3,2,1,0:T(8,128)(2,1)S(1)} %get-tuple-element.41), channel_id=1, source_target_pairs={{0,1},{1,0},{2,3},{3,2},{4,5},{5,4},{6,7},{7,6},{8,9},{9,8},{10,11... | collective-permute-start | bytes 638984 | tf_op jit(solution)/shard_map/ppermute | solution.py:46
  18.9 0.5 %collective-permute-start.6 = (bf16[2,2,192,128]{3,2,1,0:T(8,128)(2,1)S(1)}, bf16[2,2,192,128]{3,2,1,0:T(8,128)(2,1)S(1)}, u32[]{:S(2)}, u32[]{:S(2)}) collective-permute-start(bf16[2,2,192,128]{3,2,1,0:T(8,128)(2,1)S(1)} %get-tuple-element.38), channel_id=1, source_target_pairs={{0,2},{2,0},{4,6},{6,4},{1,3},{3,1},{5,7},{7,5},{8,10},{10,8},{12,... | collective-permute-start | bytes 589832 | tf_op jit(solution)/shard_map/ppermute | solution.py:46
  19.9 1.3 %scores.4 = (bf16[2048,4096]{1,0:T(8,128)(2,1)S(1)}, bf16[512,192]{1,0:T(8,128)(2,1)S(1)}, f32[2,512]{1,0:T(2,128)S(1)}) custom-call(bf16[4,2,192,128]{3,2,1,0:T(8,128)(2,1)S(1)} %get-tuple-element.33.refs_0_, bf16[2048,256]{1,0:T(8,128)(2,1)S(1)} %get-tuple-element.34.refs_1_.refs_2_.refs_4_, ...), custom_call_target="tpu_custom_call" | custom-call | flops 1 | bytes 1 | tf_op jit(solution)/shard_map/scores/pallas_call | solution.py:35
  21.2 1.3 %scores.5 = (bf16[2048,4096]{1,0:T(8,128)(2,1)S(1)}, bf16[512,192]{1,0:T(8,128)(2,1)S(1)}, f32[2,512]{1,0:T(2,128)S(1)}) custom-call(bf16[2,2,192,128]{3,2,1,0:T(8,128)(2,1)S(1)} %collective-permute-done.5.refs_0_, bf16[2,2,192,128]{3,2,1,0:T(8,128)(2,1)S(1)} %collective-permute-done.6.refs_1_, ...), custom_call_target="tpu_custom_call", output_to_operand_aliasing={{0}: (5, {})} | custom-call | flops 1 | bytes 1 | tf_op jit(solution)/shard_map/scores/pallas_call | solution.py:35
  22.5 1.6 %collective-permute-done.7.refs_1_ = bf16[2,192,128]{2,1,0:T(8,128)(2,1)S(1)} collective-permute-done((bf16[2,192,128]{2,1,0:T(8,128)(2,1)S(1)}, bf16[2,192,128]{2,1,0:T(8,128)(2,1)S(1)}, u32[]{:S(2)}, u32[]{:S(2)}) %collective-permute-start.7) | collective-permute-done | bytes 98336 | tf_op jit(solution)/shard_map/ppermute | solution.py:46
  24.1 0.5 %collective-permute-done.8.refs_2_ = bf16[2,2,208,128]{3,2,1,0:T(8,128)(2,1)S(1)} collective-permute-done((bf16[2,2,208,128]{3,2,1,0:T(8,128)(2,1)S(1)}, bf16[2,2,208,128]{3,2,1,0:T(8,128)(2,1)S(1)}, u32[]{:S(2)}, u32[]{:S(2)}) %collective-permute-start.8) | collective-permute-done | bytes 213024 | tf_op jit(solution)/shard_map/ppermute | solution.py:46
  24.8 1.3 %scores.6 = (bf16[2048,4096]{1,0:T(8,128)(2,1)S(1)}, bf16[512,192]{1,0:T(8,128)(2,1)S(1)}, f32[2,512]{1,0:T(2,128)S(1)}) custom-call(bf16[4,2,192,128]{3,2,1,0:T(8,128)(2,1)S(1)} %join.3.refs_0_, bf16[2048,256]{1,0:T(8,128)(2,1)S(1)} %get-tuple-element.34.refs_1_.refs_2_.refs_4_, ...), custom_call_target="tpu_custom_call", output_to_operand_aliasing={{0}: (4, {})} | custom-call | flops 1 | bytes 1 | tf_op jit(solution)/shard_map/scores/pallas_call | solution.py:35
  26.5 1.3 %scores.7 = (bf16[2048,4096]{1,0:T(8,128)(2,1)S(1)}, bf16[512,192]{1,0:T(8,128)(2,1)S(1)}, f32[4,1024]{1,0:T(4,128)S(1)}) custom-call(f32[2,512]{1,0:T(2,128)S(1)} %get-tuple-element.36.refs_0_, f32[2,512]{1,0:T(2,128)S(1)} %get-tuple-element.40.refs_3_.refs_1_, f32[2,512]{1,0:T(2,128)S(1)} %get-tuple-element.43.refs_2_, ...), custom_call_target="tpu_custom_call", output_to_operand_aliasing={{0}: (7, {})} | custom-call | flops 1 | bytes 1 | tf_op jit(solution)/shard_map/scores/pallas_call | solution.py:35
  28.0 1.0 %collective-permute-done.10.refs_1_ = f32[4,1024]{1,0:T(4,128)S(1)} collective-permute-done((f32[4,1024]{1,0:T(4,128)S(1)}, f32[4,1024]{1,0:T(4,128)S(1)}, u32[]{:S(2)}, u32[]{:S(2)}) %collective-permute-start.10) | collective-permute-done | bytes 16416 | tf_op jit(solution)/shard_map/ppermute | solution.py:46
  29.1 2.0 %collective-permute-start.13 = (f32[4,1024]{1,0:T(4,128)S(1)}, f32[4,1024]{1,0:T(4,128)S(1)}, u32[]{:S(2)}, u32[]{:S(2)}) collective-permute-start(f32[4,1024]{1,0:T(4,128)S(1)} %relay.3.after.refs_0_), channel_id=1, source_target_pairs={{0,5},{1,4},{2,7},{3,6},{4,1},{5,0},{6,3},{7,2},{8,13},{9,12},{10,... | collective-permute-start | bytes 49160 | tf_op jit(solution)/shard_map/ppermute | solution.py:339
  31.6 1.1 %collective-permute-start.11 = (f32[4,1024]{1,0:T(4,128)S(1)}, f32[4,1024]{1,0:T(4,128)S(1)}, u32[]{:S(2)}, u32[]{:S(2)}) collective-permute-start(f32[4,1024]{1,0:T(4,128)S(1)} %relay.3.after.refs_0_), channel_id=1, source_target_pairs={{0,1},{1,0},{2,3},{3,2},{4,5},{5,4},{6,7},{7,6},{8,9},{9,8},{10,11... | collective-permute-start | bytes 49160 | tf_op jit(solution)/shard_map/ppermute | solution.py:339
  32.6 2.4 %rest.2 = (f32[192,4096]{1,0:T(8,128)}, f32[8,128]{1,0:T(8,128)S(1)}) custom-call(f32[192,4096]{1,0:T(8,128)} %teacher_hbm.5, f32[192,4096]{1,0:T(8,128)} %student_hbm.5, f32[4,1024]{1,0:T(4,128)S(1)} %relay.3.after.refs_0_, f32[192,4096]{1,0:T(8,128)} %get-tuple-element.46.before_hbm), custom_call_target="tpu_custom_call", output_to_operand_aliasing={{0}: (3, {})} | custom-call | flops 1 | bytes 1 | tf_op jit(solution)/shard_map/rest/pallas_call | solution.py:35
  35.4 2.5 %collective-permute-start.16 = (f32[4,1024]{1,0:T(4,128)S(1)}, f32[4,1024]{1,0:T(4,128)S(1)}, u32[]{:S(2)}, u32[]{:S(2)}) collective-permute-start(f32[4,1024]{1,0:T(4,128)S(1)} %relay.4.after.refs_0_), channel_id=1, source_target_pairs={{0,24},{8,16},{16,8},{24,0},{1,25},{9,17},{17,9},{25,1},{2,26},{10... | collective-permute-start | bytes 49160 | tf_op jit(solution)/shard_map/ppermute | solution.py:46
  37.8 2.0 %collective-permute-start.14 = (f32[4,1024]{1,0:T(4,128)S(1)}, f32[4,1024]{1,0:T(4,128)S(1)}, u32[]{:S(2)}, u32[]{:S(2)}) collective-permute-start(f32[4,1024]{1,0:T(4,128)S(1)} %relay.4.after.refs_0_), channel_id=1, source_target_pairs={{0,8},{8,0},{16,24},{24,16},{1,9},{9,1},{17,25},{25,17},{2,10},{10... | collective-permute-start | bytes 49160 | tf_op jit(solution)/shard_map/ppermute | solution.py:46
  39.8 2.4 %rest.3 = (f32[192,4096]{1,0:T(8,128)}, f32[8,128]{1,0:T(8,128)S(1)}) custom-call(f32[192,4096]{1,0:T(8,128)} %teacher_hbm.5, f32[192,4096]{1,0:T(8,128)} %student_hbm.5, f32[4,1024]{1,0:T(4,128)S(1)} %relay.4.after.refs_0_, f32[192,4096]{1,0:T(8,128)} %get-tuple-element.48.before_hbm), custom_call_target="tpu_custom_call", output_to_operand_aliasing={{0}: (3, {})} | custom-call | flops 1 | bytes 1 | tf_op jit(solution)/shard_map/rest/pallas_call | solution.py:35
  42.5 3.5 %gradient.1 = f32[192,2048]{1,0:T(8,128)} custom-call(f32[4,1024]{1,0:T(4,128)S(1)} %relay.5.total_ref, f32[1,128]{1,0:T(1,128)S(1)} %get-tuple-element.32.refs_5_.refs_3_.refs_4_.refs_6_.peak_ref, f32[192,2048]{1,0:T(8,128)S(1)} %get-tuple-element.51.weight_unit, f32[1,2048]{1,0:T(1,128)S(1)} %get-tuple-element.52.weight_scale, ...), custom_call_target="tpu_custom_call" | custom-call | flops 1 | bytes 1 | tf_op jit(solution)/shard_map/gradient/pallas_call | solution.py:35
  (25 shorter events, 2.5 us)
Async XLA Ops:
  0.6 4.8 %collective-permute-start = (s32[1,256]{1,0:T(1,128)}, s32[1,256]{1,0:T(1,128)S(1)}, u32[]{:S(2)}, u32[]{:S(2)}) collective-permute-start(s32[1,256]{1,0:T(1,128)} %param.10), channel_id=1, source_target_pairs={{0,1},{1,0},{2,3},{3,2},{4,5},{5,4},{6,7},{7,6},{8,9},{9,8},{10,11... | collective-permute-start | bytes 3080 | tf_op jit(solution)/shard_map/ppermute | solution.py:46
  5.6 10.1 %collective-permute-start.4 = (bf16[2,192,128]{2,1,0:T(8,128)(2,1)S(1)}, bf16[2,192,128]{2,1,0:T(8,128)(2,1)S(1)}, u32[]{:S(2)}, u32[]{:S(2)}) collective-permute-start(bf16[2,192,128]{2,1,0:T(8,128)(2,1)S(1)} %pack.1.refs_0_), channel_id=1, source_target_pairs={{0,1},{1,0},{2,3},{3,2},{4,5},{5,4},{6,7},{7,6},{8,9},{9,8},{10,11... | collective-permute-start | bytes 294920 | tf_op jit(solution)/shard_map/ppermute | solution.py:46
  7.7 8.0 %collective-permute-start.3 = (bf16[2,192,128]{2,1,0:T(8,128)(2,1)S(1)}, bf16[2,192,128]{2,1,0:T(8,128)(2,1)S(1)}, u32[]{:S(2)}, u32[]{:S(2)}) collective-permute-start(bf16[2,192,128]{2,1,0:T(8,128)(2,1)S(1)} %pack.1.refs_0_), channel_id=1, source_target_pairs={{0,24},{8,16},{16,8},{24,0},{1,25},{9,17},{17,9},{25,1},{2,26},{10... | collective-permute-start | bytes 294920 | tf_op jit(solution)/shard_map/ppermute | solution.py:46
  11.3 6.9 %collective-permute-start.2 = (bf16[2,192,128]{2,1,0:T(8,128)(2,1)S(1)}, bf16[2,192,128]{2,1,0:T(8,128)(2,1)S(1)}, u32[]{:S(2)}, u32[]{:S(2)}) collective-permute-start(bf16[2,192,128]{2,1,0:T(8,128)(2,1)S(1)} %pack.1.refs_0_), channel_id=1, source_target_pairs={{0,16},{8,24},{16,0},{24,8},{1,17},{9,25},{17,1},{25,9},{2,18},{10... | collective-permute-start | bytes 294920 | tf_op jit(solution)/shard_map/ppermute | solution.py:46
  11.3 6.9 %collective-permute-start.1 = (bf16[2,192,128]{2,1,0:T(8,128)(2,1)S(1)}, bf16[2,192,128]{2,1,0:T(8,128)(2,1)S(1)}, u32[]{:S(2)}, u32[]{:S(2)}) collective-permute-start(bf16[2,192,128]{2,1,0:T(8,128)(2,1)S(1)} %pack.1.refs_0_), channel_id=1, source_target_pairs={{0,8},{8,0},{16,24},{24,16},{1,9},{9,1},{17,25},{25,17},{2,10},{10... | collective-permute-start | bytes 294920 | tf_op jit(solution)/shard_map/ppermute | solution.py:46
  18.3 6.3 %collective-permute-start.8 = (bf16[2,2,208,128]{3,2,1,0:T(8,128)(2,1)S(1)}, bf16[2,2,208,128]{3,2,1,0:T(8,128)(2,1)S(1)}, u32[]{:S(2)}, u32[]{:S(2)}) collective-permute-start(bf16[2,2,208,128]{3,2,1,0:T(8,128)(2,1)S(1)} %get-tuple-element.41), channel_id=1, source_target_pairs={{0,1},{1,0},{2,3},{3,2},{4,5},{5,4},{6,7},{7,6},{8,9},{9,8},{10,11... | collective-permute-start | bytes 638984 | tf_op jit(solution)/shard_map/ppermute | solution.py:46
  18.9 2.3 %collective-permute-start.5 = (bf16[2,2,192,128]{3,2,1,0:T(8,128)(2,1)S(1)}, bf16[2,2,192,128]{3,2,1,0:T(8,128)(2,1)S(1)}, u32[]{:S(2)}, u32[]{:S(2)}) collective-permute-start(bf16[2,2,192,128]{3,2,1,0:T(8,128)(2,1)S(1)} %get-tuple-element.37), channel_id=1, source_target_pairs={{0,2},{2,0},{4,6},{6,4},{1,3},{3,1},{5,7},{7,5},{8,10},{10,8},{12,... | collective-permute-start | bytes 589832 | tf_op jit(solution)/shard_map/ppermute | solution.py:46
  18.9 2.3 %collective-permute-start.6 = (bf16[2,2,192,128]{3,2,1,0:T(8,128)(2,1)S(1)}, bf16[2,2,192,128]{3,2,1,0:T(8,128)(2,1)S(1)}, u32[]{:S(2)}, u32[]{:S(2)}) collective-permute-start(bf16[2,2,192,128]{3,2,1,0:T(8,128)(2,1)S(1)} %get-tuple-element.38), channel_id=1, source_target_pairs={{0,2},{2,0},{4,6},{6,4},{1,3},{3,1},{5,7},{7,5},{8,10},{10,8},{12,... | collective-permute-start | bytes 589832 | tf_op jit(solution)/shard_map/ppermute | solution.py:46
  19.4 4.7 %collective-permute-start.7 = (bf16[2,192,128]{2,1,0:T(8,128)(2,1)S(1)}, bf16[2,192,128]{2,1,0:T(8,128)(2,1)S(1)}, u32[]{:S(2)}, u32[]{:S(2)}) collective-permute-start(bf16[2,192,128]{2,1,0:T(8,128)(2,1)S(1)} %collective-permute-done.4.refs_4_.refs_0_), channel_id=1, source_target_pairs={{0,8},{8,0},{16,24},{24,16},{1,9},{9,1},{17,25},{25,17},{2,10},{10... | collective-permute-start | bytes 294920 | tf_op jit(solution)/shard_map/ppermute | solution.py:46
  24.7 1.8 %collective-permute-start.9 = (bf16[4,2,192,128]{3,2,1,0:T(8,128)(2,1)S(1)}, bf16[4,2,192,128]{3,2,1,0:T(8,128)(2,1)S(1)}, u32[]{:S(2)}, u32[]{:S(2)}) collective-permute-start(bf16[4,2,192,128]{3,2,1,0:T(8,128)(2,1)S(1)} %join.3.refs_0_), channel_id=1, source_target_pairs={{0,2},{2,0},{4,6},{6,4},{1,3},{3,1},{5,7},{7,5},{8,10},{10,8},{12,... | collective-permute-start | bytes 1179656 | tf_op jit(solution)/shard_map/ppermute | solution.py:46
  27.8 1.2 %collective-permute-start.10 = (f32[4,1024]{1,0:T(4,128)S(1)}, f32[4,1024]{1,0:T(4,128)S(1)}, u32[]{:S(2)}, u32[]{:S(2)}) collective-permute-start(f32[4,1024]{1,0:T(4,128)S(1)} %get-tuple-element.45.refs_0_), channel_id=1, source_target_pairs={{0,2},{2,0},{4,6},{6,4},{1,3},{3,1},{5,7},{7,5},{8,10},{10,8},{12,... | collective-permute-start | bytes 49160 | tf_op jit(solution)/shard_map/ppermute | solution.py:46
  29.1 6.0 %collective-permute-start.13 = (f32[4,1024]{1,0:T(4,128)S(1)}, f32[4,1024]{1,0:T(4,128)S(1)}, u32[]{:S(2)}, u32[]{:S(2)}) collective-permute-start(f32[4,1024]{1,0:T(4,128)S(1)} %relay.3.after.refs_0_), channel_id=1, source_target_pairs={{0,5},{1,4},{2,7},{3,6},{4,1},{5,0},{6,3},{7,2},{8,13},{9,12},{10,... | collective-permute-start | bytes 49160 | tf_op jit(solution)/shard_map/ppermute | solution.py:339
  31.1 4.0 %collective-permute-start.12 = (f32[4,1024]{1,0:T(4,128)S(1)}, f32[4,1024]{1,0:T(4,128)S(1)}, u32[]{:S(2)}, u32[]{:S(2)}) collective-permute-start(f32[4,1024]{1,0:T(4,128)S(1)} %relay.3.after.refs_0_), channel_id=1, source_target_pairs={{0,4},{1,5},{2,6},{3,7},{4,0},{5,1},{6,2},{7,3},{8,12},{9,13},{10,... | collective-permute-start | bytes 49160 | tf_op jit(solution)/shard_map/ppermute | solution.py:339
  31.6 3.7 %collective-permute-start.11 = (f32[4,1024]{1,0:T(4,128)S(1)}, f32[4,1024]{1,0:T(4,128)S(1)}, u32[]{:S(2)}, u32[]{:S(2)}) collective-permute-start(f32[4,1024]{1,0:T(4,128)S(1)} %relay.3.after.refs_0_), channel_id=1, source_target_pairs={{0,1},{1,0},{2,3},{3,2},{4,5},{5,4},{6,7},{7,6},{8,9},{9,8},{10,11... | collective-permute-start | bytes 49160 | tf_op jit(solution)/shard_map/ppermute | solution.py:339
  35.4 6.9 %collective-permute-start.16 = (f32[4,1024]{1,0:T(4,128)S(1)}, f32[4,1024]{1,0:T(4,128)S(1)}, u32[]{:S(2)}, u32[]{:S(2)}) collective-permute-start(f32[4,1024]{1,0:T(4,128)S(1)} %relay.4.after.refs_0_), channel_id=1, source_target_pairs={{0,24},{8,16},{16,8},{24,0},{1,25},{9,17},{17,9},{25,1},{2,26},{10... | collective-permute-start | bytes 49160 | tf_op jit(solution)/shard_map/ppermute | solution.py:46
  37.8 4.6 %collective-permute-start.15 = (f32[4,1024]{1,0:T(4,128)S(1)}, f32[4,1024]{1,0:T(4,128)S(1)}, u32[]{:S(2)}, u32[]{:S(2)}) collective-permute-start(f32[4,1024]{1,0:T(4,128)S(1)} %relay.4.after.refs_0_), channel_id=1, source_target_pairs={{0,16},{8,24},{16,0},{24,8},{1,17},{9,25},{17,1},{25,9},{2,18},{10... | collective-permute-start | bytes 49160 | tf_op jit(solution)/shard_map/ppermute | solution.py:46
  37.8 4.6 %collective-permute-start.14 = (f32[4,1024]{1,0:T(4,128)S(1)}, f32[4,1024]{1,0:T(4,128)S(1)}, u32[]{:S(2)}, u32[]{:S(2)}) collective-permute-start(f32[4,1024]{1,0:T(4,128)S(1)} %relay.4.after.refs_0_), channel_id=1, source_target_pairs={{0,8},{8,0},{16,24},{24,16},{1,9},{9,1},{17,25},{25,17},{2,10},{10... | collective-permute-start | bytes 49160 | tf_op jit(solution)/shard_map/ppermute | solution.py:46

commit v16 on v15

--- a/solution.py
+++ b/solution.py
@@ -56,15 +56,18 @@
     return high, mid, row - high - mid
 
 
-def prep_kernel(n_dp, teacher_hbm, student_hbm, center_hbm, new_hbm, wt_ref, ws_ref, unit_ref, scale_ref, peak_ref, *scratch):
+def prep_kernel(n_dp, n_own, teacher_hbm, student_hbm, center_hbm, before_hbm, new_hbm, wt_ref, ws_ref, unit_ref, scale_ref, peak_ref, *scratch):
     teacher_buf, student_buf, new_buf, center_buf, in_t, in_s, out, in_c = scratch
     chunks, bot, width = new_buf.shape
     dp, fsdp, _ = here()
-    first = dp * (chunks * width)
-    at = [slice(i * width, (i + 1) * width) for i in range(chunks)]
-    far = [pl.ds(pl.multiple_of(first + i * width, width), width) for i in range(chunks)]
-    start = pl.multiple_of((fsdp * n_dp + dp) * (chunks * width), 128)
-    center_load = pltpu.make_async_copy(center_hbm.at[:, pl.ds(start, chunks * width)], center_buf, in_c)
+    own = n_own * width
+    at = [slice(i * width, (i + 1) * width) for i in range(n_own)]
+    firsts = [dp * own + i * width for i in range(n_own)]
+    more = (chunks - n_own) // (n_dp - 1) if n_dp > 1 else 0
+    firsts += [lax.rem(dp + 1 + i // more, n_dp) * own + (n_own - more + i % more) * width for i in range(chunks - n_own)]
+    far = [pl.ds(pl.multiple_of(first, width), width) for first in firsts]
+    start = pl.multiple_of((fsdp * n_dp + dp) * own, 128)
+    center_load = pltpu.make_async_copy(center_hbm.at[:, pl.ds(start, own)], center_buf, in_c)
     loads = [
         (
             pltpu.make_async_copy(teacher_hbm.at[:, far[i]], teacher_buf.at[i], in_t.at[i]),
@@ -91,6 +94,8 @@
         new = 0.994 * teacher_buf[i] + 0.006 * student
         new_buf[i] = new
         stores[i].start()
+        if i >= n_own:
+            continue
         high, mid, low = [part[:, at[i]] for part in splits]
         extra = jnp.where(row == 0, high, jnp.where(row == 1, mid, jnp.where(row == 2, low, zero)))
         scale = lax.rsqrt(jnp.sum(student * student, axis=0, keepdims=True) + EPS)
@@ -104,13 +109,14 @@
         store.wait()
 
 
-def prepare(teacher_weight, student_weight, center, n_dp):
+def prepare(teacher_weight, student_weight, center, new, n_dp, more):
     bot, cols = teacher_weight.shape
     own = cols // n_dp
-    width = min(512, own)
-    chunks = own // width
+    width = math.gcd(min(512, own), more)
+    n_own = own // width
+    chunks = n_own + (n_dp - 1) * (more // width)
     return call(
-        functools.partial(prep_kernel, n_dp),
+        functools.partial(prep_kernel, n_dp, n_own),
         "prep",
         [
             pltpu.HBM((bot, cols), jnp.float32),
@@ -120,9 +126,10 @@
             held(1, own),
             held(1, 128),
         ],
-        (teacher_weight, student_weight, center),
-        in_specs=[IN_HBM] * 3,
+        (teacher_weight, student_weight, center, new),
+        in_specs=[IN_HBM] * 4,
         out_specs=[IN_HBM] + [ON_CHIP] * 5,
+        input_output_aliases={3: 0},
         scratch_shapes=[held(chunks, bot, width)] * 3
         + [held(1, own)]
         + [pltpu.SemaphoreType.DMA((chunks,))] * 3
@@ -130,7 +137,7 @@
     )
 
 
-def rest_kernel(lo, hi, own, teacher_hbm, student_hbm, after, before_hbm, new_hbm, done_ref, *scratch):
+def rest_kernel(lo, hi, own, teacher_hbm, student_hbm, new_hbm, done_ref, *scratch):
     teacher_buf, student_buf, new_buf, in_t, in_s, out = scratch
     width = hi - lo
     parts = teacher_hbm.shape[1] // own - 1
@@ -157,17 +164,16 @@
         store.wait()
 
 
-def update_rest(teacher_weight, student_weight, after, new, own, lo, hi):
+def update_rest(teacher_weight, student_weight, own, lo, hi):
     bot, cols = teacher_weight.shape
     parts = cols // own - 1
     return call(
         functools.partial(rest_kernel, lo, hi, own),
         "rest",
         [pltpu.HBM((bot, cols), jnp.float32), held(8, 128)],
-        (teacher_weight, student_weight, after, new),
-        in_specs=[IN_HBM] * 4,
+        (teacher_weight, student_weight),
+        in_specs=[IN_HBM] * 2,
         out_specs=[IN_HBM, ON_CHIP],
-        input_output_aliases={3: 0},
         scratch_shapes=[held(parts, bot, hi - lo)] * 3 + [pltpu.SemaphoreType.DMA((parts,))] * 3,
     )
 
@@ -201,7 +207,7 @@
     return (values * lax.rsqrt(jnp.sum(values * values, axis=0, keepdims=True) + EPS)).astype(jnp.bfloat16)
 
 
-def pack_kernel(student_ref, teacher_ref, index_ref, out_ref):
+def pack_kernel(student_ref, teacher_ref, index_ref, after, out_ref):
     half = out_ref.shape[2]
     lower = here()[2] == 0
     out_ref[0] = normalize(student_ref[...].astype(jnp.float32))
@@ -211,9 +217,10 @@
     out_ref[1] = normalize(jnp.dot(teacher_ref[...], pick, preferred_element_type=jnp.float32))
 
 
-def pack(student, teacher, index):
+def pack(student, teacher, index, after):
     bot, half = student.shape
-    return call(pack_kernel, "pack", held(2, bot, half, dtype=jnp.bfloat16), (student, teacher, index))
+    out = held(2, bot, half, dtype=jnp.bfloat16)
+    return call(pack_kernel, "pack", out, (student, teacher, index, after), in_specs=[ON_CHIP] * 3 + [IN_HBM])
 
 
 def join_kernel(n_in, n_after, firsts, bot, *refs):
@@ -326,31 +333,32 @@
     refs[-1][...] = jnp.concatenate(combine(parts), axis=0)
 
 
-def add_up(parts, *after):
-    specs = [ON_CHIP] * len(parts) + [IN_HBM] * len(after)
-    out = held(*parts[0].shape[-2:])
-    return call(functools.partial(relay_kernel, len(parts)), "relay", out, (*parts, *after), in_specs=specs)
+def add_up(parts):
+    return call(functools.partial(relay_kernel, len(parts)), "relay", held(*parts[0].shape[-2:]), parts)
 
 
 def across(total, up, over):
     n_proto, n_dp = lax.axis_size("proto"), lax.axis_size("dp")
+    far = lambda p, d: (p ^ up, d ^ over) if p % 2 else (p, d)
     places = [(p, d) for p in range(n_proto) for d in range(n_dp)]
-    pairs = [(p * n_dp + d, (p ^ up) * n_dp + (d ^ over)) for p, d in places]
+    pairs = [(p * n_dp + d, far(p, d)[0] * n_dp + far(p, d)[1]) for p, d in places]
     return lax.ppermute(total, ("proto", "dp"), pairs)
 
 
 def along_fsdp(total):
-    n = lax.axis_size("fsdp")
+    n, n_proto = lax.axis_size("fsdp"), lax.axis_size("proto")
     if n <= DIRECT:
-        return [total, *[swap(total, "fsdp", k) for k in range(1, n)]]
+        pairs = lambda k: [(i * n_proto + p, (i ^ k if p % 2 else i) * n_proto + p) for i in range(n) for p in range(n_proto)]
+        return [total, *[lax.ppermute(total, ("fsdp", "proto"), pairs(k)) for k in range(1, n)]]
     return [lax.all_to_all(jnp.broadcast_to(total[None], (n, *total.shape)), "fsdp", 0, 0, tiled=True)]
 
 
-def grad_kernel(total_ref, peak_ref, weight_unit, weight_scale, *refs):
+def grad_kernel(led_ref, given_ref, peak_ref, weight_unit, weight_scale, *refs):
     units, exp_ref, out_hbm, scales, feats, *derivs, buf, sems = refs[:4], *refs[4:]
     dp, _, core = here()
-    scales[0:2, :] = 10.0 / total_ref[0:2, :]
-    scales[2:4, :] = 10.0 * jnp.exp2(GAIN_T * peak_ref[:, :1] - total_ref[2:4, :])
+    total = jnp.where(core == 1, led_ref[...], given_ref[...])
+    scales[0:2, :] = 10.0 / total[0:2]
+    scales[2:4, :] = 10.0 * jnp.exp2(GAIN_T * peak_ref[:, :1] - total[2:4])
     rows = units[0].shape[0]
     width = 128
     n = rows // width
@@ -393,11 +401,11 @@
         store.wait()
 
 
-def gradient(total, peak, weight_unit, weight_scale, units, exps):
+def gradient(led, given, peak, weight_unit, weight_scale, units, exps):
     cols = exps.shape[0]
     rows, bot = units[0].shape
     step = min(256, cols)
-    args = (total, peak, weight_unit, weight_scale, *units, exps)
+    args = (led, given, peak, weight_unit, weight_scale, *units, exps)
     return call(
         grad_kernel,
         "gradient",
@@ -420,8 +428,11 @@
     teacher_weight, student_weight, center = in_hbm(teacher_weight), in_hbm(student_weight), in_hbm(center[None, :])
 
     index = swap(pairing, "dp")
-    mine = pack(*fetch(in_hbm(student_feats[0].T), in_hbm(teacher_feats[0].T)), index)
-    new, wt, ws, unit, scale, peak = prepare(teacher_weight, student_weight, center, n_dp)
+    own_cols = teacher_weight.shape[1] // n_dp
+    middle = own_cols // 2
+    new, done = update_rest(teacher_weight, student_weight, own_cols, 0, middle)
+    mine = pack(*fetch(in_hbm(student_feats[0].T), in_hbm(teacher_feats[0].T)), index, done)
+    teacher_new, wt, ws, unit, scale, peak = prepare(teacher_weight, student_weight, center, new, n_dp, own_cols - middle)
     weights = (ws, wt, peak)
     bot = mine.shape[1]
     if n_fsdp <= DIRECT:
@@ -439,15 +450,12 @@
     (other,) = join(other, [(0, n_fsdp, bot)], (total_b,), bot)
     exps, unit_c, total_c = scores(2, [other], weights, exps=exps)
     exps, unit_d, total = scores(3, [swap(other, "proto")], weights, (total_a, total_b, total_c), exps)
-    n_proto, own_cols = lax.axis_size("proto"), ws.shape[0]
-    middle = own_cols // 2
     total = add_up([total, swap(total, "proto")])
-    new, done = update_rest(teacher_weight, student_weight, total, new, own_cols, 0, middle)
-    steps = [(up, over) for up in range(0, n_proto, 2) for over in range(n_dp)][1:]
-    total = add_up([total, *[across(total, *step) for step in steps]], done)
-    teacher_new, done = update_rest(teacher_weight, student_weight, total, new, own_cols, middle, own_cols)
-    total = add_up(along_fsdp(total), done)
-    student_grad = gradient(total, peak, unit, scale, (unit_a, unit_b, unit_c, unit_d), exps)
+    steps = [(up, over) for up in range(0, lax.axis_size("proto"), 2) for over in range(n_dp)][1:]
+    total = add_up([total, *[across(total, *step) for step in steps]])
+    total = add_up(along_fsdp(total))
+    units = (unit_a, unit_b, unit_c, unit_d)
+    student_grad = gradient(total, swap(total, "proto"), peak, unit, scale, units, exps)
     return (teacher_new, student_grad)
 
 

time: 46.2 us -> 56.2 us (1.22)
  starting transfers between devices: 19.3 us -> 31.6 us
  Pallas kernels: 18.5 us -> 17.1 us
  waiting for transfers between devices: 7.41 us -> 6.34 us
    ppermute x14 -> x12, starting transfers between devices: 15.7 us -> 27.6 us  [swap(): lax.ppermute(block, axis, [(i, i ^ apart) for i in range(lax.axis_size(ax...]
    ppermute x0 -> x3, starting transfers between devices: none -> 1.99 us  [along_fsdp(): lax.ppermute(total, ('fsdp', 'proto'), pairs(k))]
    ppermute x3, starting transfers between devices: 3.55 us -> 1.99 us  [across(): return lax.ppermute(total, ('proto', 'dp'), pairs)]
    pallas_call x15 -> x14, Pallas kernels: 18.5 us -> 17.1 us  [call(): pl.pallas_call(kernel, out_shape=out_shape, compiler_params=pltpu.Compile...]
    ppermute x14 -> x12, waiting for transfers between devices: 7.15 us -> 6.32 us  [swap(): lax.ppermute(block, axis, [(i, i ^ apart) for i in range(lax.axis_size(ax...]
  transfers between devices with their start and end apart: 17 -> 18, of which waited for: 8 -> 5; matrix products, arithmetic and copies ran while one was open for 0% -> 0% of each run, Pallas kernels for 29% -> 21%
where the time goes in v16:
time: 56.2 us; the launch traced here: 55.9 us
  starting transfers between devices  31.6 us (56%)
  Pallas kernels  17.1 us (30%)
  waiting for transfers between devices  6.34 us (11%)
  between operations  0.86 us (2%)
    ppermute x12, starting transfers between devices, swap(): lax.ppermute(block, axis, [(i, i ^ apart) for i in range(lax.axis_size(ax...  27.6 us
    pallas_call x14, Pallas kernels, call(): pl.pallas_call(kernel, out_shape=out_shape, compiler_params=pltpu.Compile...  17.1 us
    ppermute x12, waiting for transfers between devices, swap(): lax.ppermute(block, axis, [(i, i ^ apart) for i in range(lax.axis_size(ax...  6.32 us
    ppermute x3, starting transfers between devices, along_fsdp(): lax.ppermute(total, ('fsdp', 'proto'), pairs(k))  1.99 us
    ppermute x3, starting transfers between devices, across(): return lax.ppermute(total, ('proto', 'dp'), pairs)  1.99 us
  transfers between devices with their start and end apart: 18, of which 5 were waited for; matrix products, arithmetic and copies ran while one was open for 0% of the time, Pallas kernels for 21%

profile of v16, /device:TPU:0, one launch (start us, length us, event | category | flops | bytes accessed | tf_op | source)
XLA Modules:
  0.0 55.9 jit_solution(16889412125271286865)
XLA Ops:
  0.6 3.0 %collective-permute-start = (s32[1,256]{1,0:T(1,128)}, s32[1,256]{1,0:T(1,128)S(1)}, u32[]{:S(2)}, u32[]{:S(2)}) collective-permute-start(s32[1,256]{1,0:T(1,128)} %param.10), channel_id=1, source_target_pairs={{0,1},{1,0},{2,3},{3,2},{4,5},{5,4},{6,7},{7,6},{8,9},{9,8},{10,11... | collective-permute-start | bytes 3080 | tf_op jit(solution)/shard_map/ppermute | solution.py:46
  3.6 0.9 %fetch.1 = (bf16[192,128]{1,0:T(8,128)(2,1)S(1)}, bf16[192,256]{1,0:T(8,128)(2,1)S(1)}) custom-call(bf16[192,256]{1,0:T(8,128)(2,1)} %bitcast.7, bf16[192,256]{1,0:T(8,128)(2,1)} %bitcast.8), custom_call_target="tpu_custom_call" | custom-call | flops 1 | bytes 1 | tf_op jit(solution)/shard_map/fetch/pallas_call | solution.py:35
  4.6 2.4 %rest.1 = (f32[192,4096]{1,0:T(8,128)}, f32[8,128]{1,0:T(8,128)S(1)}) custom-call(f32[192,4096]{1,0:T(8,128)} %teacher_hbm.3, f32[192,4096]{1,0:T(8,128)} %student_hbm.3), custom_call_target="tpu_custom_call" | custom-call | flops 1 | bytes 1 | tf_op jit(solution)/shard_map/rest/pallas_call | solution.py:35
  7.7 3.7 %collective-permute-start.3 = (bf16[2,192,128]{2,1,0:T(8,128)(2,1)S(1)}, bf16[2,192,128]{2,1,0:T(8,128)(2,1)S(1)}, u32[]{:S(2)}, u32[]{:S(2)}) collective-permute-start(bf16[2,192,128]{2,1,0:T(8,128)(2,1)S(1)} %pack.1.refs_0_), channel_id=1, source_target_pairs={{0,24},{8,16},{16,8},{24,0},{1,25},{9,17},{17,9},{25,1},{2,26},{10... | collective-permute-start | bytes 294920 | tf_op jit(solution)/shard_map/ppermute | solution.py:46
  11.4 0.6 %collective-permute-start.1 = (bf16[2,192,128]{2,1,0:T(8,128)(2,1)S(1)}, bf16[2,192,128]{2,1,0:T(8,128)(2,1)S(1)}, u32[]{:S(2)}, u32[]{:S(2)}) collective-permute-start(bf16[2,192,128]{2,1,0:T(8,128)(2,1)S(1)} %pack.1.refs_0_), channel_id=1, source_target_pairs={{0,8},{8,0},{16,24},{24,16},{1,9},{9,1},{17,25},{25,17},{2,10},{10... | collective-permute-start | bytes 294920 | tf_op jit(solution)/shard_map/ppermute | solution.py:46
  12.1 4.5 %prep.1 = (f32[192,4096]{1,0:T(8,128)}, bf16[2048,256]{1,0:T(8,128)(2,1)S(1)}, bf16[2048,256]{1,0:T(8,128)(2,1)S(1)}, f32[192,2048]{1,0:T(8,128)S(1)}, f32[1,2048]{1,0:T(1,128)S(1)}, /*index=5*/f32[1,128]{1,0:T(1,128)S(1)}) custom-call(f32[192,4096]{1,0:T(8,128)} %teacher_hbm.3, f32[192,4096]{1,0:T(8,128)} %student_hbm.3, ...), custom_call_target="tpu_custom_call", output_to_operand_aliasing={{0}: (3, {})} | custom-call | flops 1 | bytes 1 | tf_op jit(solution)/shard_map/prep/pallas_call | solution.py:35
  16.6 2.5 %collective-permute-done.2.refs_2_ = bf16[2,192,128]{2,1,0:T(8,128)(2,1)S(1)} collective-permute-done((bf16[2,192,128]{2,1,0:T(8,128)(2,1)S(1)}, bf16[2,192,128]{2,1,0:T(8,128)(2,1)S(1)}, u32[]{:S(2)}, u32[]{:S(2)}) %collective-permute-start.2) | collective-permute-done | bytes 98336 | tf_op jit(solution)/shard_map/ppermute | solution.py:46
  19.2 1.6 %collective-permute-start.8 = (bf16[2,2,208,128]{3,2,1,0:T(8,128)(2,1)S(1)}, bf16[2,2,208,128]{3,2,1,0:T(8,128)(2,1)S(1)}, u32[]{:S(2)}, u32[]{:S(2)}) collective-permute-start(bf16[2,2,208,128]{3,2,1,0:T(8,128)(2,1)S(1)} %get-tuple-element.42), channel_id=1, source_target_pairs={{0,1},{1,0},{2,3},{3,2},{4,5},{5,4},{6,7},{7,6},{8,9},{9,8},{10,11... | collective-permute-start | bytes 638984 | tf_op jit(solution)/shard_map/ppermute | solution.py:46
  21.3 0.5 collective-permute-start.7
  21.8 1.3 %scores.4 = (bf16[2048,4096]{1,0:T(8,128)(2,1)S(1)}, bf16[512,192]{1,0:T(8,128)(2,1)S(1)}, f32[2,512]{1,0:T(2,128)S(1)}) custom-call(bf16[4,2,192,128]{3,2,1,0:T(8,128)(2,1)S(1)} %get-tuple-element.34.refs_0_, bf16[2048,256]{1,0:T(8,128)(2,1)S(1)} %get-tuple-element.35.refs_1_.refs_2_.refs_4_, ...), custom_call_target="tpu_custom_call" | custom-call | flops 1 | bytes 1 | tf_op jit(solution)/shard_map/scores/pallas_call | solution.py:35
  23.2 1.3 %scores.5 = (bf16[2048,4096]{1,0:T(8,128)(2,1)S(1)}, bf16[512,192]{1,0:T(8,128)(2,1)S(1)}, f32[2,512]{1,0:T(2,128)S(1)}) custom-call(bf16[2,2,192,128]{3,2,1,0:T(8,128)(2,1)S(1)} %collective-permute-done.5.refs_0_, bf16[2,2,192,128]{3,2,1,0:T(8,128)(2,1)S(1)} %collective-permute-done.6.refs_1_, ...), custom_call_target="tpu_custom_call", output_to_operand_aliasing={{0}: (5, {})} | custom-call | flops 1 | bytes 1 | tf_op jit(solution)/shard_map/scores/pallas_call | solution.py:35
  24.5 1.5 %collective-permute-done.7.refs_1_ = bf16[2,192,128]{2,1,0:T(8,128)(2,1)S(1)} collective-permute-done((bf16[2,192,128]{2,1,0:T(8,128)(2,1)S(1)}, bf16[2,192,128]{2,1,0:T(8,128)(2,1)S(1)}, u32[]{:S(2)}, u32[]{:S(2)}) %collective-permute-start.7) | collective-permute-done | bytes 98336 | tf_op jit(solution)/shard_map/ppermute | solution.py:46
  26.1 1.3 %scores.6 = (bf16[2048,4096]{1,0:T(8,128)(2,1)S(1)}, bf16[512,192]{1,0:T(8,128)(2,1)S(1)}, f32[2,512]{1,0:T(2,128)S(1)}) custom-call(bf16[4,2,192,128]{3,2,1,0:T(8,128)(2,1)S(1)} %join.3.refs_0_, bf16[2048,256]{1,0:T(8,128)(2,1)S(1)} %get-tuple-element.35.refs_1_.refs_2_.refs_4_, ...), custom_call_target="tpu_custom_call", output_to_operand_aliasing={{0}: (4, {})} | custom-call | flops 1 | bytes 1 | tf_op jit(solution)/shard_map/scores/pallas_call | solution.py:35
  27.8 1.3 %scores.7 = (bf16[2048,4096]{1,0:T(8,128)(2,1)S(1)}, bf16[512,192]{1,0:T(8,128)(2,1)S(1)}, f32[4,1024]{1,0:T(4,128)S(1)}) custom-call(f32[2,512]{1,0:T(2,128)S(1)} %get-tuple-element.37.refs_0_, f32[2,512]{1,0:T(2,128)S(1)} %get-tuple-element.41.refs_3_.refs_1_, f32[2,512]{1,0:T(2,128)S(1)} %get-tuple-element.44.refs_2_, ...), custom_call_target="tpu_custom_call", output_to_operand_aliasing={{0}: (7, {})} | custom-call | flops 1 | bytes 1 | tf_op jit(solution)/shard_map/scores/pallas_call | solution.py:35
  29.4 1.0 %collective-permute-done.10.refs_1_ = f32[4,1024]{1,0:T(4,128)S(1)} collective-permute-done((f32[4,1024]{1,0:T(4,128)S(1)}, f32[4,1024]{1,0:T(4,128)S(1)}, u32[]{:S(2)}, u32[]{:S(2)}) %collective-permute-start.10) | collective-permute-done | bytes 16416 | tf_op jit(solution)/shard_map/ppermute | solution.py:46
  30.4 0.7 %collective-permute-start.13 = (f32[4,1024]{1,0:T(4,128)S(1)}, f32[4,1024]{1,0:T(4,128)S(1)}, u32[]{:S(2)}, u32[]{:S(2)}) collective-permute-start(f32[4,1024]{1,0:T(4,128)S(1)} %relay.3.refs_0_), channel_id=1, source_target_pairs={{0,0},{1,1},{2,7},{3,6},{4,4},{5,5},{6,3},{7,2},{8,8},{9,9},{10,15... | collective-permute-start | bytes 49160 | tf_op jit(solution)/shard_map/ppermute | solution.py:345
  31.1 0.7 %collective-permute-start.12 = (f32[4,1024]{1,0:T(4,128)S(1)}, f32[4,1024]{1,0:T(4,128)S(1)}, u32[]{:S(2)}, u32[]{:S(2)}) collective-permute-start(f32[4,1024]{1,0:T(4,128)S(1)} %relay.3.refs_0_), channel_id=1, source_target_pairs={{0,0},{1,1},{2,6},{3,7},{4,4},{5,5},{6,2},{7,3},{8,8},{9,9},{10,14... | collective-permute-start | bytes 49160 | tf_op jit(solution)/shard_map/ppermute | solution.py:345
  31.8 0.7 %collective-permute-start.11 = (f32[4,1024]{1,0:T(4,128)S(1)}, f32[4,1024]{1,0:T(4,128)S(1)}, u32[]{:S(2)}, u32[]{:S(2)}) collective-permute-start(f32[4,1024]{1,0:T(4,128)S(1)} %relay.3.refs_0_), channel_id=1, source_target_pairs={{0,0},{1,1},{2,3},{3,2},{4,4},{5,5},{6,7},{7,6},{8,8},{9,9},{10,11... | collective-permute-start | bytes 49160 | tf_op jit(solution)/shard_map/ppermute | solution.py:345
  32.5 0.7 %collective-permute-start.16 = (f32[4,1024]{1,0:T(4,128)S(1)}, f32[4,1024]{1,0:T(4,128)S(1)}, u32[]{:S(2)}, u32[]{:S(2)}) collective-permute-start(f32[4,1024]{1,0:T(4,128)S(1)} %relay.4.refs_0_), channel_id=1, source_target_pairs={{0,0},{2,26},{4,4},{6,30},{8,8},{10,18},{12,12},{14,22},{16,16},{1... | collective-permute-start | bytes 49160 | tf_op jit(solution)/shard_map/ppermute | solution.py:352
  33.2 0.7 %collective-permute-start.15 = (f32[4,1024]{1,0:T(4,128)S(1)}, f32[4,1024]{1,0:T(4,128)S(1)}, u32[]{:S(2)}, u32[]{:S(2)}) collective-permute-start(f32[4,1024]{1,0:T(4,128)S(1)} %relay.4.refs_0_), channel_id=1, source_target_pairs={{0,0},{2,18},{4,4},{6,22},{8,8},{10,26},{12,12},{14,30},{16,16},{1... | collective-permute-start | bytes 49160 | tf_op jit(solution)/shard_map/ppermute | solution.py:352
  33.9 0.7 %collective-permute-start.14 = (f32[4,1024]{1,0:T(4,128)S(1)}, f32[4,1024]{1,0:T(4,128)S(1)}, u32[]{:S(2)}, u32[]{:S(2)}) collective-permute-start(f32[4,1024]{1,0:T(4,128)S(1)} %relay.4.refs_0_), channel_id=1, source_target_pairs={{0,0},{2,10},{4,4},{6,14},{8,8},{10,2},{12,12},{14,6},{16,16},{18,... | collective-permute-start | bytes 49160 | tf_op jit(solution)/shard_map/ppermute | solution.py:352
  34.6 16.9 %collective-permute-start.17 = (f32[4,1024]{1,0:T(4,128)S(1)}, f32[4,1024]{1,0:T(4,128)S(1)}, u32[]{:S(2)}, u32[]{:S(2)}) collective-permute-start(f32[4,1024]{1,0:T(4,128)S(1)} %relay.5.led_ref), channel_id=1, source_target_pairs={{0,2},{2,0},{4,6},{6,4},{1,3},{3,1},{5,7},{7,5},{8,10},{10,8},{12,... | collective-permute-start | bytes 49160 | tf_op jit(solution)/shard_map/ppermute | solution.py:46
  51.5 0.8 %collective-permute-done.17.given_ref = f32[4,1024]{1,0:T(4,128)S(1)} collective-permute-done((f32[4,1024]{1,0:T(4,128)S(1)}, f32[4,1024]{1,0:T(4,128)S(1)}, u32[]{:S(2)}, u32[]{:S(2)}) %collective-permute-start.17) | collective-permute-done | bytes 16416 | tf_op jit(solution)/shard_map/ppermute | solution.py:46
  52.4 3.5 %gradient.1 = f32[192,2048]{1,0:T(8,128)} custom-call(f32[4,1024]{1,0:T(4,128)S(1)} %relay.5.led_ref, f32[4,1024]{1,0:T(4,128)S(1)} %collective-permute-done.17.given_ref, f32[1,128]{1,0:T(1,128)S(1)} %get-tuple-element.33.refs_5_.refs_3_.refs_4_.refs_6_.peak_ref, f32[192,2048]{1,0:T(8,128)S(1)} %get-tuple-element.47.weight_unit, ...), custom_call_target="tpu_custom_call" | custom-call | flops 1 | bytes 1 | tf_op jit(solution)/shard_map/gradient/pallas_call | solution.py:35
  (26 shorter events, 2.1 us)
Async XLA Ops:
  0.6 6.4 %collective-permute-start = (s32[1,256]{1,0:T(1,128)}, s32[1,256]{1,0:T(1,128)S(1)}, u32[]{:S(2)}, u32[]{:S(2)}) collective-permute-start(s32[1,256]{1,0:T(1,128)} %param.10), channel_id=1, source_target_pairs={{0,1},{1,0},{2,3},{3,2},{4,5},{5,4},{6,7},{7,6},{8,9},{9,8},{10,11... | collective-permute-start | bytes 3080 | tf_op jit(solution)/shard_map/ppermute | solution.py:46
  7.2 9.4 %collective-permute-start.4 = (bf16[2,192,128]{2,1,0:T(8,128)(2,1)S(1)}, bf16[2,192,128]{2,1,0:T(8,128)(2,1)S(1)}, u32[]{:S(2)}, u32[]{:S(2)}) collective-permute-start(bf16[2,192,128]{2,1,0:T(8,128)(2,1)S(1)} %pack.1.refs_0_), channel_id=1, source_target_pairs={{0,1},{1,0},{2,3},{3,2},{4,5},{5,4},{6,7},{7,6},{8,9},{9,8},{10,11... | collective-permute-start | bytes 294920 | tf_op jit(solution)/shard_map/ppermute | solution.py:46
  7.7 8.9 %collective-permute-start.3 = (bf16[2,192,128]{2,1,0:T(8,128)(2,1)S(1)}, bf16[2,192,128]{2,1,0:T(8,128)(2,1)S(1)}, u32[]{:S(2)}, u32[]{:S(2)}) collective-permute-start(bf16[2,192,128]{2,1,0:T(8,128)(2,1)S(1)} %pack.1.refs_0_), channel_id=1, source_target_pairs={{0,24},{8,16},{16,8},{24,0},{1,25},{9,17},{17,9},{25,1},{2,26},{10... | collective-permute-start | bytes 294920 | tf_op jit(solution)/shard_map/ppermute | solution.py:46
  11.4 7.7 %collective-permute-start.2 = (bf16[2,192,128]{2,1,0:T(8,128)(2,1)S(1)}, bf16[2,192,128]{2,1,0:T(8,128)(2,1)S(1)}, u32[]{:S(2)}, u32[]{:S(2)}) collective-permute-start(bf16[2,192,128]{2,1,0:T(8,128)(2,1)S(1)} %pack.1.refs_0_), channel_id=1, source_target_pairs={{0,16},{8,24},{16,0},{24,8},{1,17},{9,25},{17,1},{25,9},{2,18},{10... | collective-permute-start | bytes 294920 | tf_op jit(solution)/shard_map/ppermute | solution.py:46
  11.4 7.7 %collective-permute-start.1 = (bf16[2,192,128]{2,1,0:T(8,128)(2,1)S(1)}, bf16[2,192,128]{2,1,0:T(8,128)(2,1)S(1)}, u32[]{:S(2)}, u32[]{:S(2)}) collective-permute-start(bf16[2,192,128]{2,1,0:T(8,128)(2,1)S(1)} %pack.1.refs_0_), channel_id=1, source_target_pairs={{0,8},{8,0},{16,24},{24,16},{1,9},{9,1},{17,25},{25,17},{2,10},{10... | collective-permute-start | bytes 294920 | tf_op jit(solution)/shard_map/ppermute | solution.py:46
  19.2 6.8 %collective-permute-start.8 = (bf16[2,2,208,128]{3,2,1,0:T(8,128)(2,1)S(1)}, bf16[2,2,208,128]{3,2,1,0:T(8,128)(2,1)S(1)}, u32[]{:S(2)}, u32[]{:S(2)}) collective-permute-start(bf16[2,2,208,128]{3,2,1,0:T(8,128)(2,1)S(1)} %get-tuple-element.42), channel_id=1, source_target_pairs={{0,1},{1,0},{2,3},{3,2},{4,5},{5,4},{6,7},{7,6},{8,9},{9,8},{10,11... | collective-permute-start | bytes 638984 | tf_op jit(solution)/shard_map/ppermute | solution.py:46
  20.8 2.4 %collective-permute-start.5 = (bf16[2,2,192,128]{3,2,1,0:T(8,128)(2,1)S(1)}, bf16[2,2,192,128]{3,2,1,0:T(8,128)(2,1)S(1)}, u32[]{:S(2)}, u32[]{:S(2)}) collective-permute-start(bf16[2,2,192,128]{3,2,1,0:T(8,128)(2,1)S(1)} %get-tuple-element.38), channel_id=1, source_target_pairs={{0,2},{2,0},{4,6},{6,4},{1,3},{3,1},{5,7},{7,5},{8,10},{10,8},{12,... | collective-permute-start | bytes 589832 | tf_op jit(solution)/shard_map/ppermute | solution.py:46
  20.8 2.4 %collective-permute-start.6 = (bf16[2,2,192,128]{3,2,1,0:T(8,128)(2,1)S(1)}, bf16[2,2,192,128]{3,2,1,0:T(8,128)(2,1)S(1)}, u32[]{:S(2)}, u32[]{:S(2)}) collective-permute-start(bf16[2,2,192,128]{3,2,1,0:T(8,128)(2,1)S(1)} %get-tuple-element.39), channel_id=1, source_target_pairs={{0,2},{2,0},{4,6},{6,4},{1,3},{3,1},{5,7},{7,5},{8,10},{10,8},{12,... | collective-permute-start | bytes 589832 | tf_op jit(solution)/shard_map/ppermute | solution.py:46
  21.3 4.7 %collective-permute-start.7 = (bf16[2,192,128]{2,1,0:T(8,128)(2,1)S(1)}, bf16[2,192,128]{2,1,0:T(8,128)(2,1)S(1)}, u32[]{:S(2)}, u32[]{:S(2)}) collective-permute-start(bf16[2,192,128]{2,1,0:T(8,128)(2,1)S(1)} %collective-permute-done.4.refs_4_.refs_0_), channel_id=1, source_target_pairs={{0,8},{8,0},{16,24},{24,16},{1,9},{9,1},{17,25},{25,17},{2,10},{10... | collective-permute-start | bytes 294920 | tf_op jit(solution)/shard_map/ppermute | solution.py:46
  26.0 1.8 %collective-permute-start.9 = (bf16[4,2,192,128]{3,2,1,0:T(8,128)(2,1)S(1)}, bf16[4,2,192,128]{3,2,1,0:T(8,128)(2,1)S(1)}, u32[]{:S(2)}, u32[]{:S(2)}) collective-permute-start(bf16[4,2,192,128]{3,2,1,0:T(8,128)(2,1)S(1)} %join.3.refs_0_), channel_id=1, source_target_pairs={{0,2},{2,0},{4,6},{6,4},{1,3},{3,1},{5,7},{7,5},{8,10},{10,8},{12,... | collective-permute-start | bytes 1179656 | tf_op jit(solution)/shard_map/ppermute | solution.py:46
  29.2 1.2 %collective-permute-start.10 = (f32[4,1024]{1,0:T(4,128)S(1)}, f32[4,1024]{1,0:T(4,128)S(1)}, u32[]{:S(2)}, u32[]{:S(2)}) collective-permute-start(f32[4,1024]{1,0:T(4,128)S(1)} %get-tuple-element.46.refs_0_), channel_id=1, source_target_pairs={{0,2},{2,0},{4,6},{6,4},{1,3},{3,1},{5,7},{7,5},{8,10},{10,8},{12,... | collective-permute-start | bytes 49160 | tf_op jit(solution)/shard_map/ppermute | solution.py:46
  30.4 2.0 %collective-permute-start.13 = (f32[4,1024]{1,0:T(4,128)S(1)}, f32[4,1024]{1,0:T(4,128)S(1)}, u32[]{:S(2)}, u32[]{:S(2)}) collective-permute-start(f32[4,1024]{1,0:T(4,128)S(1)} %relay.3.refs_0_), channel_id=1, source_target_pairs={{0,0},{1,1},{2,7},{3,6},{4,4},{5,5},{6,3},{7,2},{8,8},{9,9},{10,15... | collective-permute-start | bytes 49160 | tf_op jit(solution)/shard_map/ppermute | solution.py:345
  31.1 1.4 %collective-permute-start.12 = (f32[4,1024]{1,0:T(4,128)S(1)}, f32[4,1024]{1,0:T(4,128)S(1)}, u32[]{:S(2)}, u32[]{:S(2)}) collective-permute-start(f32[4,1024]{1,0:T(4,128)S(1)} %relay.3.refs_0_), channel_id=1, source_target_pairs={{0,0},{1,1},{2,6},{3,7},{4,4},{5,5},{6,2},{7,3},{8,8},{9,9},{10,14... | collective-permute-start | bytes 49160 | tf_op jit(solution)/shard_map/ppermute | solution.py:345
  31.8 0.7 %collective-permute-start.11 = (f32[4,1024]{1,0:T(4,128)S(1)}, f32[4,1024]{1,0:T(4,128)S(1)}, u32[]{:S(2)}, u32[]{:S(2)}) collective-permute-start(f32[4,1024]{1,0:T(4,128)S(1)} %relay.3.refs_0_), channel_id=1, source_target_pairs={{0,0},{1,1},{2,3},{3,2},{4,4},{5,5},{6,7},{7,6},{8,8},{9,9},{10,11... | collective-permute-start | bytes 49160 | tf_op jit(solution)/shard_map/ppermute | solution.py:345
  32.5 2.0 %collective-permute-start.16 = (f32[4,1024]{1,0:T(4,128)S(1)}, f32[4,1024]{1,0:T(4,128)S(1)}, u32[]{:S(2)}, u32[]{:S(2)}) collective-permute-start(f32[4,1024]{1,0:T(4,128)S(1)} %relay.4.refs_0_), channel_id=1, source_target_pairs={{0,0},{2,26},{4,4},{6,30},{8,8},{10,18},{12,12},{14,22},{16,16},{1... | collective-permute-start | bytes 49160 | tf_op jit(solution)/shard_map/ppermute | solution.py:352
  33.2 1.4 %collective-permute-start.15 = (f32[4,1024]{1,0:T(4,128)S(1)}, f32[4,1024]{1,0:T(4,128)S(1)}, u32[]{:S(2)}, u32[]{:S(2)}) collective-permute-start(f32[4,1024]{1,0:T(4,128)S(1)} %relay.4.refs_0_), channel_id=1, source_target_pairs={{0,0},{2,18},{4,4},{6,22},{8,8},{10,26},{12,12},{14,30},{16,16},{1... | collective-permute-start | bytes 49160 | tf_op jit(solution)/shard_map/ppermute | solution.py:352
  33.9 0.7 %collective-permute-start.14 = (f32[4,1024]{1,0:T(4,128)S(1)}, f32[4,1024]{1,0:T(4,128)S(1)}, u32[]{:S(2)}, u32[]{:S(2)}) collective-permute-start(f32[4,1024]{1,0:T(4,128)S(1)} %relay.4.refs_0_), channel_id=1, source_target_pairs={{0,0},{2,10},{4,4},{6,14},{8,8},{10,2},{12,12},{14,6},{16,16},{18,... | collective-permute-start | bytes 49160 | tf_op jit(solution)/shard_map/ppermute | solution.py:352
  34.6 17.7 %collective-permute-start.17 = (f32[4,1024]{1,0:T(4,128)S(1)}, f32[4,1024]{1,0:T(4,128)S(1)}, u32[]{:S(2)}, u32[]{:S(2)}) collective-permute-start(f32[4,1024]{1,0:T(4,128)S(1)} %relay.5.led_ref), channel_id=1, source_target_pairs={{0,2},{2,0},{4,6},{6,4},{1,3},{3,1},{5,7},{7,5},{8,10},{10,8},{12,... | collective-permute-start | bytes 49160 | tf_op jit(solution)/shard_map/ppermute | solution.py:46

commit v17 on v16

--- a/solution.py
+++ b/solution.py
@@ -56,7 +56,7 @@
     return high, mid, row - high - mid
 
 
-def prep_kernel(n_dp, n_own, teacher_hbm, student_hbm, center_hbm, before_hbm, new_hbm, wt_ref, ws_ref, unit_ref, scale_ref, peak_ref, *scratch):
+def prep_kernel(n_dp, n_own, teacher_hbm, student_hbm, center_hbm, new_hbm, wt_ref, ws_ref, unit_ref, scale_ref, peak_ref, *scratch):
     teacher_buf, student_buf, new_buf, center_buf, in_t, in_s, out, in_c = scratch
     chunks, bot, width = new_buf.shape
     dp, fsdp, _ = here()
@@ -109,7 +109,7 @@
         store.wait()
 
 
-def prepare(teacher_weight, student_weight, center, new, n_dp, more):
+def prepare(teacher_weight, student_weight, center, n_dp, more):
     bot, cols = teacher_weight.shape
     own = cols // n_dp
     width = math.gcd(min(512, own), more)
@@ -126,10 +126,9 @@
             held(1, own),
             held(1, 128),
         ],
-        (teacher_weight, student_weight, center, new),
-        in_specs=[IN_HBM] * 4,
+        (teacher_weight, student_weight, center),
+        in_specs=[IN_HBM] * 3,
         out_specs=[IN_HBM] + [ON_CHIP] * 5,
-        input_output_aliases={3: 0},
         scratch_shapes=[held(chunks, bot, width)] * 3
         + [held(1, own)]
         + [pltpu.SemaphoreType.DMA((chunks,))] * 3
@@ -137,7 +136,7 @@
     )
 
 
-def rest_kernel(lo, hi, own, teacher_hbm, student_hbm, new_hbm, done_ref, *scratch):
+def rest_kernel(lo, hi, own, teacher_hbm, student_hbm, after, before_hbm, new_hbm, done_ref, *scratch):
     teacher_buf, student_buf, new_buf, in_t, in_s, out = scratch
     width = hi - lo
     parts = teacher_hbm.shape[1] // own - 1
@@ -164,16 +163,17 @@
         store.wait()
 
 
-def update_rest(teacher_weight, student_weight, own, lo, hi):
+def update_rest(teacher_weight, student_weight, after, new, own, lo, hi):
     bot, cols = teacher_weight.shape
     parts = cols // own - 1
     return call(
         functools.partial(rest_kernel, lo, hi, own),
         "rest",
         [pltpu.HBM((bot, cols), jnp.float32), held(8, 128)],
-        (teacher_weight, student_weight),
-        in_specs=[IN_HBM] * 2,
+        (teacher_weight, student_weight, after, new),
+        in_specs=[IN_HBM] * 4,
         out_specs=[IN_HBM, ON_CHIP],
+        input_output_aliases={3: 0},
         scratch_shapes=[held(parts, bot, hi - lo)] * 3 + [pltpu.SemaphoreType.DMA((parts,))] * 3,
     )
 
@@ -207,7 +207,7 @@
     return (values * lax.rsqrt(jnp.sum(values * values, axis=0, keepdims=True) + EPS)).astype(jnp.bfloat16)
 
 
-def pack_kernel(student_ref, teacher_ref, index_ref, after, out_ref):
+def pack_kernel(student_ref, teacher_ref, index_ref, out_ref):
     half = out_ref.shape[2]
     lower = here()[2] == 0
     out_ref[0] = normalize(student_ref[...].astype(jnp.float32))
@@ -217,10 +217,9 @@
     out_ref[1] = normalize(jnp.dot(teacher_ref[...], pick, preferred_element_type=jnp.float32))
 
 
-def pack(student, teacher, index, after):
+def pack(student, teacher, index):
     bot, half = student.shape
-    out = held(2, bot, half, dtype=jnp.bfloat16)
-    return call(pack_kernel, "pack", out, (student, teacher, index, after), in_specs=[ON_CHIP] * 3 + [IN_HBM])
+    return call(pack_kernel, "pack", held(2, bot, half, dtype=jnp.bfloat16), (student, teacher, index))
 
 
 def join_kernel(n_in, n_after, firsts, bot, *refs):
@@ -337,9 +336,13 @@
     return call(functools.partial(relay_kernel, len(parts)), "relay", held(*parts[0].shape[-2:]), parts)
 
 
+def aside(p, n_proto):
+    return (p ^ 2) if n_proto % 4 == 0 else p ^ 1
+
+
 def across(total, up, over):
     n_proto, n_dp = lax.axis_size("proto"), lax.axis_size("dp")
-    far = lambda p, d: (p ^ up, d ^ over) if p % 2 else (p, d)
+    far = lambda p, d: (p ^ up, d ^ over) if p % 2 else (aside(p, n_proto), d)
     places = [(p, d) for p in range(n_proto) for d in range(n_dp)]
     pairs = [(p * n_dp + d, far(p, d)[0] * n_dp + far(p, d)[1]) for p, d in places]
     return lax.ppermute(total, ("proto", "dp"), pairs)
@@ -347,10 +350,11 @@
 
 def along_fsdp(total):
     n, n_proto = lax.axis_size("fsdp"), lax.axis_size("proto")
-    if n <= DIRECT:
-        pairs = lambda k: [(i * n_proto + p, (i ^ k if p % 2 else i) * n_proto + p) for i in range(n) for p in range(n_proto)]
-        return [total, *[lax.ppermute(total, ("fsdp", "proto"), pairs(k)) for k in range(1, n)]]
-    return [lax.all_to_all(jnp.broadcast_to(total[None], (n, *total.shape)), "fsdp", 0, 0, tiled=True)]
+    if n > DIRECT:
+        return [lax.all_to_all(jnp.broadcast_to(total[None], (n, *total.shape)), "fsdp", 0, 0, tiled=True)]
+    far = lambda i, p, k: (i ^ k) * n_proto + p if p % 2 else i * n_proto + aside(p, n_proto)
+    pairs = lambda k: [(i * n_proto + p, far(i, p, k)) for i in range(n) for p in range(n_proto)]
+    return [total, *[lax.ppermute(total, ("fsdp", "proto"), pairs(k)) for k in range(1, n)]]
 
 
 def grad_kernel(led_ref, given_ref, peak_ref, weight_unit, weight_scale, *refs):
@@ -428,11 +432,10 @@
     teacher_weight, student_weight, center = in_hbm(teacher_weight), in_hbm(student_weight), in_hbm(center[None, :])
 
     index = swap(pairing, "dp")
+    mine = pack(*fetch(in_hbm(student_feats[0].T), in_hbm(teacher_feats[0].T)), index)
     own_cols = teacher_weight.shape[1] // n_dp
     middle = own_cols // 2
-    new, done = update_rest(teacher_weight, student_weight, own_cols, 0, middle)
-    mine = pack(*fetch(in_hbm(student_feats[0].T), in_hbm(teacher_feats[0].T)), index, done)
-    teacher_new, wt, ws, unit, scale, peak = prepare(teacher_weight, student_weight, center, new, n_dp, own_cols - middle)
+    new, wt, ws, unit, scale, peak = prepare(teacher_weight, student_weight, center, n_dp, own_cols - middle)
     weights = (ws, wt, peak)
     bot = mine.shape[1]
     if n_fsdp <= DIRECT:
@@ -447,7 +450,8 @@
         other, halves = [swap(own, "dp")], [own]
     exps, unit_a, total_a = scores(0, [own], weights)
     exps, unit_b, total_b = scores(1, [swap(half, "proto") for half in halves], weights, exps=exps)
-    (other,) = join(other, [(0, n_fsdp, bot)], (total_b,), bot)
+    teacher_new, done = update_rest(teacher_weight, student_weight, total_a, new, own_cols, 0, middle)
+    (other,) = join(other, [(0, n_fsdp, bot)], (total_b, done), bot)
     exps, unit_c, total_c = scores(2, [other], weights, exps=exps)
     exps, unit_d, total = scores(3, [swap(other, "proto")], weights, (total_a, total_b, total_c), exps)
     total = add_up([total, swap(total, "proto")])

time: 56.2 us -> 46.1 us (0.82)
  starting transfers between devices: 31.6 us -> 18.6 us
  waiting for transfers between devices: 6.34 us -> 9.45 us
    ppermute x12, starting transfers between devices: 27.6 us -> 11.4 us  [swap(): lax.ppermute(block, axis, [(i, i ^ apart) for i in range(lax.axis_size(ax...]
    ppermute x3, waiting for transfers between devices: 0.01 us -> 2.22 us  [along_fsdp(): lax.ppermute(total, ('fsdp', 'proto'), pairs(k))]
    ppermute x3, waiting for transfers between devices: 0.01 us -> 2.22 us  [across(): return lax.ppermute(total, ('proto', 'dp'), pairs)]
    ppermute x3, starting transfers between devices: 1.99 us -> 3.61 us  [along_fsdp(): lax.ppermute(total, ('fsdp', 'proto'), pairs(k))]
    ppermute x3, starting transfers between devices: 1.99 us -> 3.61 us  [across(): return lax.ppermute(total, ('proto', 'dp'), pairs)]
    ppermute x12, waiting for transfers between devices: 6.32 us -> 5.02 us  [swap(): lax.ppermute(block, axis, [(i, i ^ apart) for i in range(lax.axis_size(ax...]
  transfers between devices with their start and end apart: 18 -> 18, of which waited for: 5 -> 11; matrix products, arithmetic and copies ran while one was open for 0% -> 0% of each run, Pallas kernels for 21% -> 26%
where the time goes in v17:
time: 46.1 us; the launch traced here: 45.9 us
  starting transfers between devices  18.6 us (40%)
  Pallas kernels  17.1 us (37%)
  waiting for transfers between devices  9.45 us (20%)
  between operations  0.79 us (2%)
    pallas_call x14, Pallas kernels, call(): pl.pallas_call(kernel, out_shape=out_shape, compiler_params=pltpu.Compile...  17.1 us
    ppermute x12, starting transfers between devices, swap(): lax.ppermute(block, axis, [(i, i ^ apart) for i in range(lax.axis_size(ax...  11.4 us
    ppermute x12, waiting for transfers between devices, swap(): lax.ppermute(block, axis, [(i, i ^ apart) for i in range(lax.axis_size(ax...  5.02 us
    ppermute x3, starting transfers between devices, along_fsdp(): lax.ppermute(total, ('fsdp', 'proto'), pairs(k))  3.61 us
    ppermute x3, starting transfers between devices, across(): return lax.ppermute(total, ('proto', 'dp'), pairs)  3.61 us
    ppermute x3, waiting for transfers between devices, along_fsdp(): lax.ppermute(total, ('fsdp', 'proto'), pairs(k))  2.22 us
    ppermute x3, waiting for transfers between devices, across(): return lax.ppermute(total, ('proto', 'dp'), pairs)  2.22 us
  transfers between devices with their start and end apart: 18, of which 11 were waited for; matrix products, arithmetic and copies ran while one was open for 0% of the time, Pallas kernels for 26%

profile of v17, /device:TPU:0, one launch (start us, length us, event | category | flops | bytes accessed | tf_op | source)
XLA Modules:
  0.0 45.9 jit_solution(8511261805910858421)
XLA Ops:
  0.6 3.0 %collective-permute-start = (s32[1,256]{1,0:T(1,128)}, s32[1,256]{1,0:T(1,128)S(1)}, u32[]{:S(2)}, u32[]{:S(2)}) collective-permute-start(s32[1,256]{1,0:T(1,128)} %param.10), channel_id=1, source_target_pairs={{0,1},{1,0},{2,3},{3,2},{4,5},{5,4},{6,7},{7,6},{8,9},{9,8},{10,11... | collective-permute-start | bytes 3080 | tf_op jit(solution)/shard_map/ppermute | solution.py:46
  3.6 0.9 %fetch.1 = (bf16[192,128]{1,0:T(8,128)(2,1)S(1)}, bf16[192,256]{1,0:T(8,128)(2,1)S(1)}) custom-call(bf16[192,256]{1,0:T(8,128)(2,1)} %bitcast.7, bf16[192,256]{1,0:T(8,128)(2,1)} %bitcast.8), custom_call_target="tpu_custom_call" | custom-call | flops 1 | bytes 1 | tf_op jit(solution)/shard_map/fetch/pallas_call | solution.py:35
  4.6 0.8 %collective-permute-done.index_ref = s32[1,256]{1,0:T(1,128)S(1)} collective-permute-done((s32[1,256]{1,0:T(1,128)}, s32[1,256]{1,0:T(1,128)S(1)}, u32[]{:S(2)}, u32[]{:S(2)}) %collective-permute-start) | collective-permute-done | bytes 1056 | tf_op jit(solution)/shard_map/ppermute | solution.py:46
  5.6 2.1 %collective-permute-start.4 = (bf16[2,192,128]{2,1,0:T(8,128)(2,1)S(1)}, bf16[2,192,128]{2,1,0:T(8,128)(2,1)S(1)}, u32[]{:S(2)}, u32[]{:S(2)}) collective-permute-start(bf16[2,192,128]{2,1,0:T(8,128)(2,1)S(1)} %pack.1.refs_0_), channel_id=1, source_target_pairs={{0,1},{1,0},{2,3},{3,2},{4,5},{5,4},{6,7},{7,6},{8,9},{9,8},{10,11... | collective-permute-start | bytes 294920 | tf_op jit(solution)/shard_map/ppermute | solution.py:46
  7.7 3.6 %collective-permute-start.3 = (bf16[2,192,128]{2,1,0:T(8,128)(2,1)S(1)}, bf16[2,192,128]{2,1,0:T(8,128)(2,1)S(1)}, u32[]{:S(2)}, u32[]{:S(2)}) collective-permute-start(bf16[2,192,128]{2,1,0:T(8,128)(2,1)S(1)} %pack.1.refs_0_), channel_id=1, source_target_pairs={{0,24},{8,16},{16,8},{24,0},{1,25},{9,17},{17,9},{25,1},{2,26},{10... | collective-permute-start | bytes 294920 | tf_op jit(solution)/shard_map/ppermute | solution.py:46
  11.3 0.8 %collective-permute-start.1 = (bf16[2,192,128]{2,1,0:T(8,128)(2,1)S(1)}, bf16[2,192,128]{2,1,0:T(8,128)(2,1)S(1)}, u32[]{:S(2)}, u32[]{:S(2)}) collective-permute-start(bf16[2,192,128]{2,1,0:T(8,128)(2,1)S(1)} %pack.1.refs_0_), channel_id=1, source_target_pairs={{0,8},{8,0},{16,24},{24,16},{1,9},{9,1},{17,25},{25,17},{2,10},{10... | collective-permute-start | bytes 294920 | tf_op jit(solution)/shard_map/ppermute | solution.py:46
  12.1 4.5 %prep.1 = (f32[192,4096]{1,0:T(8,128)}, bf16[2048,256]{1,0:T(8,128)(2,1)S(1)}, bf16[2048,256]{1,0:T(8,128)(2,1)S(1)}, f32[192,2048]{1,0:T(8,128)S(1)}, f32[1,2048]{1,0:T(1,128)S(1)}, /*index=5*/f32[1,128]{1,0:T(1,128)S(1)}) custom-call(f32[192,4096]{1,0:T(8,128)} %teacher_hbm.3, f32[192,4096]{1,0:T(8,128)} %student_hbm.3, f32[1,16384]{1,0:T(1,128)} %bitcast.9), custom_call_target="tpu_custom_call" | custom-call | flops 1 | bytes 1 | tf_op jit(solution)/shard_map/prep/pallas_call | solution.py:35
  16.6 1.6 %collective-permute-done.2.refs_2_ = bf16[2,192,128]{2,1,0:T(8,128)(2,1)S(1)} collective-permute-done((bf16[2,192,128]{2,1,0:T(8,128)(2,1)S(1)}, bf16[2,192,128]{2,1,0:T(8,128)(2,1)S(1)}, u32[]{:S(2)}, u32[]{:S(2)}) %collective-permute-start.2) | collective-permute-done | bytes 98336 | tf_op jit(solution)/shard_map/ppermute | solution.py:46
  18.3 0.6 %collective-permute-start.8 = (bf16[2,2,208,128]{3,2,1,0:T(8,128)(2,1)S(1)}, bf16[2,2,208,128]{3,2,1,0:T(8,128)(2,1)S(1)}, u32[]{:S(2)}, u32[]{:S(2)}) collective-permute-start(bf16[2,2,208,128]{3,2,1,0:T(8,128)(2,1)S(1)} %get-tuple-element.41), channel_id=1, source_target_pairs={{0,1},{1,0},{2,3},{3,2},{4,5},{5,4},{6,7},{7,6},{8,9},{9,8},{10,11... | collective-permute-start | bytes 638984 | tf_op jit(solution)/shard_map/ppermute | solution.py:46
  18.9 0.5 %collective-permute-start.6 = (bf16[2,2,192,128]{3,2,1,0:T(8,128)(2,1)S(1)}, bf16[2,2,192,128]{3,2,1,0:T(8,128)(2,1)S(1)}, u32[]{:S(2)}, u32[]{:S(2)}) collective-permute-start(bf16[2,2,192,128]{3,2,1,0:T(8,128)(2,1)S(1)} %get-tuple-element.38), channel_id=1, source_target_pairs={{0,2},{2,0},{4,6},{6,4},{1,3},{3,1},{5,7},{7,5},{8,10},{10,8},{12,... | collective-permute-start | bytes 589832 | tf_op jit(solution)/shard_map/ppermute | solution.py:46
  19.9 1.3 %scores.4 = (bf16[2048,4096]{1,0:T(8,128)(2,1)S(1)}, bf16[512,192]{1,0:T(8,128)(2,1)S(1)}, f32[2,512]{1,0:T(2,128)S(1)}) custom-call(bf16[4,2,192,128]{3,2,1,0:T(8,128)(2,1)S(1)} %get-tuple-element.31.refs_0_, bf16[2048,256]{1,0:T(8,128)(2,1)S(1)} %get-tuple-element.32.refs_1_.refs_2_.refs_4_, ...), custom_call_target="tpu_custom_call" | custom-call | flops 1 | bytes 1 | tf_op jit(solution)/shard_map/scores/pallas_call | solution.py:35
  21.2 2.4 %rest.1 = (f32[192,4096]{1,0:T(8,128)}, f32[8,128]{1,0:T(8,128)S(1)}) custom-call(f32[192,4096]{1,0:T(8,128)} %teacher_hbm.3, f32[192,4096]{1,0:T(8,128)} %student_hbm.3, f32[2,512]{1,0:T(2,128)S(1)} %get-tuple-element.34.after.refs_0_, f32[192,4096]{1,0:T(8,128)} %get-tuple-element.35.before_hbm), custom_call_target="tpu_custom_call", output_to_operand_aliasing={{0}: (3, {})} | custom-call | flops 1 | bytes 1 | tf_op jit(solution)/shard_map/rest/pallas_call | solution.py:35
  23.6 1.3 %scores.5 = (bf16[2048,4096]{1,0:T(8,128)(2,1)S(1)}, bf16[512,192]{1,0:T(8,128)(2,1)S(1)}, f32[2,512]{1,0:T(2,128)S(1)}) custom-call(bf16[2,2,192,128]{3,2,1,0:T(8,128)(2,1)S(1)} %collective-permute-done.5.refs_0_, bf16[2,2,192,128]{3,2,1,0:T(8,128)(2,1)S(1)} %collective-permute-done.6.refs_1_, ...), custom_call_target="tpu_custom_call", output_to_operand_aliasing={{0}: (5, {})} | custom-call | flops 1 | bytes 1 | tf_op jit(solution)/shard_map/scores/pallas_call | solution.py:35
  25.1 1.3 %scores.6 = (bf16[2048,4096]{1,0:T(8,128)(2,1)S(1)}, bf16[512,192]{1,0:T(8,128)(2,1)S(1)}, f32[2,512]{1,0:T(2,128)S(1)}) custom-call(bf16[4,2,192,128]{3,2,1,0:T(8,128)(2,1)S(1)} %join.3.refs_0_, bf16[2048,256]{1,0:T(8,128)(2,1)S(1)} %get-tuple-element.32.refs_1_.refs_2_.refs_4_, ...), custom_call_target="tpu_custom_call", output_to_operand_aliasing={{0}: (4, {})} | custom-call | flops 1 | bytes 1 | tf_op jit(solution)/shard_map/scores/pallas_call | solution.py:35
  26.8 1.3 %scores.7 = (bf16[2048,4096]{1,0:T(8,128)(2,1)S(1)}, bf16[512,192]{1,0:T(8,128)(2,1)S(1)}, f32[4,1024]{1,0:T(4,128)S(1)}) custom-call(f32[2,512]{1,0:T(2,128)S(1)} %get-tuple-element.34.after.refs_0_, f32[2,512]{1,0:T(2,128)S(1)} %get-tuple-element.40.refs_3_.refs_1_, f32[2,512]{1,0:T(2,128)S(1)} %get-tuple-element.44.refs_2_, ...), custom_call_target="tpu_custom_call", output_to_operand_aliasing={{0}: (7, {})} | custom-call | flops 1 | bytes 1 | tf_op jit(solution)/shard_map/scores/pallas_call | solution.py:35
  28.3 1.0 %collective-permute-done.10.refs_1_ = f32[4,1024]{1,0:T(4,128)S(1)} collective-permute-done((f32[4,1024]{1,0:T(4,128)S(1)}, f32[4,1024]{1,0:T(4,128)S(1)}, u32[]{:S(2)}, u32[]{:S(2)}) %collective-permute-start.10) | collective-permute-done | bytes 16416 | tf_op jit(solution)/shard_map/ppermute | solution.py:46
  29.4 1.6 %collective-permute-start.13 = (f32[4,1024]{1,0:T(4,128)S(1)}, f32[4,1024]{1,0:T(4,128)S(1)}, u32[]{:S(2)}, u32[]{:S(2)}) collective-permute-start(f32[4,1024]{1,0:T(4,128)S(1)} %relay.3.refs_0_), channel_id=1, source_target_pairs={{0,4},{1,5},{2,7},{3,6},{4,0},{5,1},{6,3},{7,2},{8,12},{9,13},{10,... | collective-permute-start | bytes 49160 | tf_op jit(solution)/shard_map/ppermute | solution.py:348
  31.5 1.5 %collective-permute-start.11 = (f32[4,1024]{1,0:T(4,128)S(1)}, f32[4,1024]{1,0:T(4,128)S(1)}, u32[]{:S(2)}, u32[]{:S(2)}) collective-permute-start(f32[4,1024]{1,0:T(4,128)S(1)} %relay.3.refs_0_), channel_id=1, source_target_pairs={{0,4},{1,5},{2,3},{3,2},{4,0},{5,1},{6,7},{7,6},{8,12},{9,13},{10,... | collective-permute-start | bytes 49160 | tf_op jit(solution)/shard_map/ppermute | solution.py:348
  33.2 1.5 %collective-permute-done.12.refs_2_ = f32[4,1024]{1,0:T(4,128)S(1)} collective-permute-done((f32[4,1024]{1,0:T(4,128)S(1)}, f32[4,1024]{1,0:T(4,128)S(1)}, u32[]{:S(2)}, u32[]{:S(2)}) %collective-permute-start.12) | collective-permute-done | bytes 16416 | tf_op jit(solution)/shard_map/ppermute | solution.py:348
  35.3 1.6 %collective-permute-start.16 = (f32[4,1024]{1,0:T(4,128)S(1)}, f32[4,1024]{1,0:T(4,128)S(1)}, u32[]{:S(2)}, u32[]{:S(2)}) collective-permute-start(f32[4,1024]{1,0:T(4,128)S(1)} %relay.4.refs_0_), channel_id=1, source_target_pairs={{0,4},{2,26},{4,0},{6,30},{8,12},{10,18},{12,8},{14,22},{16,20},{1... | collective-permute-start | bytes 49160 | tf_op jit(solution)/shard_map/ppermute | solution.py:357
  37.4 1.5 %collective-permute-start.14 = (f32[4,1024]{1,0:T(4,128)S(1)}, f32[4,1024]{1,0:T(4,128)S(1)}, u32[]{:S(2)}, u32[]{:S(2)}) collective-permute-start(f32[4,1024]{1,0:T(4,128)S(1)} %relay.4.refs_0_), channel_id=1, source_target_pairs={{0,4},{2,10},{4,0},{6,14},{8,12},{10,2},{12,8},{14,6},{16,20},{18,... | collective-permute-start | bytes 49160 | tf_op jit(solution)/shard_map/ppermute | solution.py:357
  39.1 1.5 %collective-permute-done.15.refs_2_ = f32[4,1024]{1,0:T(4,128)S(1)} collective-permute-done((f32[4,1024]{1,0:T(4,128)S(1)}, f32[4,1024]{1,0:T(4,128)S(1)}, u32[]{:S(2)}, u32[]{:S(2)}) %collective-permute-start.15) | collective-permute-done | bytes 16416 | tf_op jit(solution)/shard_map/ppermute | solution.py:357
  41.2 1.2 %collective-permute-done.17.given_ref = f32[4,1024]{1,0:T(4,128)S(1)} collective-permute-done((f32[4,1024]{1,0:T(4,128)S(1)}, f32[4,1024]{1,0:T(4,128)S(1)}, u32[]{:S(2)}, u32[]{:S(2)}) %collective-permute-start.17) | collective-permute-done | bytes 16416 | tf_op jit(solution)/shard_map/ppermute | solution.py:46
  42.4 3.5 %gradient.1 = f32[192,2048]{1,0:T(8,128)} custom-call(f32[4,1024]{1,0:T(4,128)S(1)} %relay.5.led_ref, f32[4,1024]{1,0:T(4,128)S(1)} %collective-permute-done.17.given_ref, f32[1,128]{1,0:T(1,128)S(1)} %get-tuple-element.30.refs_5_.refs_3_.refs_4_.refs_6_.peak_ref, f32[192,2048]{1,0:T(8,128)S(1)} %get-tuple-element.47.weight_unit, ...), custom_call_target="tpu_custom_call" | custom-call | flops 1 | bytes 1 | tf_op jit(solution)/shard_map/gradient/pallas_call | solution.py:35
  (26 shorter events, 4.0 us)
Async XLA Ops:
  0.6 4.8 %collective-permute-start = (s32[1,256]{1,0:T(1,128)}, s32[1,256]{1,0:T(1,128)S(1)}, u32[]{:S(2)}, u32[]{:S(2)}) collective-permute-start(s32[1,256]{1,0:T(1,128)} %param.10), channel_id=1, source_target_pairs={{0,1},{1,0},{2,3},{3,2},{4,5},{5,4},{6,7},{7,6},{8,9},{9,8},{10,11... | collective-permute-start | bytes 3080 | tf_op jit(solution)/shard_map/ppermute | solution.py:46
  5.6 11.0 %collective-permute-start.4 = (bf16[2,192,128]{2,1,0:T(8,128)(2,1)S(1)}, bf16[2,192,128]{2,1,0:T(8,128)(2,1)S(1)}, u32[]{:S(2)}, u32[]{:S(2)}) collective-permute-start(bf16[2,192,128]{2,1,0:T(8,128)(2,1)S(1)} %pack.1.refs_0_), channel_id=1, source_target_pairs={{0,1},{1,0},{2,3},{3,2},{4,5},{5,4},{6,7},{7,6},{8,9},{9,8},{10,11... | collective-permute-start | bytes 294920 | tf_op jit(solution)/shard_map/ppermute | solution.py:46
  7.7 8.9 %collective-permute-start.3 = (bf16[2,192,128]{2,1,0:T(8,128)(2,1)S(1)}, bf16[2,192,128]{2,1,0:T(8,128)(2,1)S(1)}, u32[]{:S(2)}, u32[]{:S(2)}) collective-permute-start(bf16[2,192,128]{2,1,0:T(8,128)(2,1)S(1)} %pack.1.refs_0_), channel_id=1, source_target_pairs={{0,24},{8,16},{16,8},{24,0},{1,25},{9,17},{17,9},{25,1},{2,26},{10... | collective-permute-start | bytes 294920 | tf_op jit(solution)/shard_map/ppermute | solution.py:46
  11.3 6.9 %collective-permute-start.2 = (bf16[2,192,128]{2,1,0:T(8,128)(2,1)S(1)}, bf16[2,192,128]{2,1,0:T(8,128)(2,1)S(1)}, u32[]{:S(2)}, u32[]{:S(2)}) collective-permute-start(bf16[2,192,128]{2,1,0:T(8,128)(2,1)S(1)} %pack.1.refs_0_), channel_id=1, source_target_pairs={{0,16},{8,24},{16,0},{24,8},{1,17},{9,25},{17,1},{25,9},{2,18},{10... | collective-permute-start | bytes 294920 | tf_op jit(solution)/shard_map/ppermute | solution.py:46
  11.3 6.9 %collective-permute-start.1 = (bf16[2,192,128]{2,1,0:T(8,128)(2,1)S(1)}, bf16[2,192,128]{2,1,0:T(8,128)(2,1)S(1)}, u32[]{:S(2)}, u32[]{:S(2)}) collective-permute-start(bf16[2,192,128]{2,1,0:T(8,128)(2,1)S(1)} %pack.1.refs_0_), channel_id=1, source_target_pairs={{0,8},{8,0},{16,24},{24,16},{1,9},{9,1},{17,25},{25,17},{2,10},{10... | collective-permute-start | bytes 294920 | tf_op jit(solution)/shard_map/ppermute | solution.py:46
  18.3 6.6 %collective-permute-start.8 = (bf16[2,2,208,128]{3,2,1,0:T(8,128)(2,1)S(1)}, bf16[2,2,208,128]{3,2,1,0:T(8,128)(2,1)S(1)}, u32[]{:S(2)}, u32[]{:S(2)}) collective-permute-start(bf16[2,2,208,128]{3,2,1,0:T(8,128)(2,1)S(1)} %get-tuple-element.41), channel_id=1, source_target_pairs={{0,1},{1,0},{2,3},{3,2},{4,5},{5,4},{6,7},{7,6},{8,9},{9,8},{10,11... | collective-permute-start | bytes 638984 | tf_op jit(solution)/shard_map/ppermute | solution.py:46
  18.9 4.7 %collective-permute-start.5 = (bf16[2,2,192,128]{3,2,1,0:T(8,128)(2,1)S(1)}, bf16[2,2,192,128]{3,2,1,0:T(8,128)(2,1)S(1)}, u32[]{:S(2)}, u32[]{:S(2)}) collective-permute-start(bf16[2,2,192,128]{3,2,1,0:T(8,128)(2,1)S(1)} %get-tuple-element.37), channel_id=1, source_target_pairs={{0,2},{2,0},{4,6},{6,4},{1,3},{3,1},{5,7},{7,5},{8,10},{10,8},{12,... | collective-permute-start | bytes 589832 | tf_op jit(solution)/shard_map/ppermute | solution.py:46
  18.9 4.7 %collective-permute-start.6 = (bf16[2,2,192,128]{3,2,1,0:T(8,128)(2,1)S(1)}, bf16[2,2,192,128]{3,2,1,0:T(8,128)(2,1)S(1)}, u32[]{:S(2)}, u32[]{:S(2)}) collective-permute-start(bf16[2,2,192,128]{3,2,1,0:T(8,128)(2,1)S(1)} %get-tuple-element.38), channel_id=1, source_target_pairs={{0,2},{2,0},{4,6},{6,4},{1,3},{3,1},{5,7},{7,5},{8,10},{10,8},{12,... | collective-permute-start | bytes 589832 | tf_op jit(solution)/shard_map/ppermute | solution.py:46
  19.4 5.5 %collective-permute-start.7 = (bf16[2,192,128]{2,1,0:T(8,128)(2,1)S(1)}, bf16[2,192,128]{2,1,0:T(8,128)(2,1)S(1)}, u32[]{:S(2)}, u32[]{:S(2)}) collective-permute-start(bf16[2,192,128]{2,1,0:T(8,128)(2,1)S(1)} %collective-permute-done.4.refs_4_.refs_0_), channel_id=1, source_target_pairs={{0,8},{8,0},{16,24},{24,16},{1,9},{9,1},{17,25},{25,17},{2,10},{10... | collective-permute-start | bytes 294920 | tf_op jit(solution)/shard_map/ppermute | solution.py:46
  25.0 1.8 %collective-permute-start.9 = (bf16[4,2,192,128]{3,2,1,0:T(8,128)(2,1)S(1)}, bf16[4,2,192,128]{3,2,1,0:T(8,128)(2,1)S(1)}, u32[]{:S(2)}, u32[]{:S(2)}) collective-permute-start(bf16[4,2,192,128]{3,2,1,0:T(8,128)(2,1)S(1)} %join.3.refs_0_), channel_id=1, source_target_pairs={{0,2},{2,0},{4,6},{6,4},{1,3},{3,1},{5,7},{7,5},{8,10},{10,8},{12,... | collective-permute-start | bytes 1179656 | tf_op jit(solution)/shard_map/ppermute | solution.py:46
  28.1 1.2 %collective-permute-start.10 = (f32[4,1024]{1,0:T(4,128)S(1)}, f32[4,1024]{1,0:T(4,128)S(1)}, u32[]{:S(2)}, u32[]{:S(2)}) collective-permute-start(f32[4,1024]{1,0:T(4,128)S(1)} %get-tuple-element.46.refs_0_), channel_id=1, source_target_pairs={{0,2},{2,0},{4,6},{6,4},{1,3},{3,1},{5,7},{7,5},{8,10},{10,8},{12,... | collective-permute-start | bytes 49160 | tf_op jit(solution)/shard_map/ppermute | solution.py:46
  29.4 3.8 %collective-permute-start.13 = (f32[4,1024]{1,0:T(4,128)S(1)}, f32[4,1024]{1,0:T(4,128)S(1)}, u32[]{:S(2)}, u32[]{:S(2)}) collective-permute-start(f32[4,1024]{1,0:T(4,128)S(1)} %relay.3.refs_0_), channel_id=1, source_target_pairs={{0,4},{1,5},{2,7},{3,6},{4,0},{5,1},{6,3},{7,2},{8,12},{9,13},{10,... | collective-permute-start | bytes 49160 | tf_op jit(solution)/shard_map/ppermute | solution.py:348
  31.0 3.8 %collective-permute-start.12 = (f32[4,1024]{1,0:T(4,128)S(1)}, f32[4,1024]{1,0:T(4,128)S(1)}, u32[]{:S(2)}, u32[]{:S(2)}) collective-permute-start(f32[4,1024]{1,0:T(4,128)S(1)} %relay.3.refs_0_), channel_id=1, source_target_pairs={{0,4},{1,5},{2,6},{3,7},{4,0},{5,1},{6,2},{7,3},{8,12},{9,13},{10,... | collective-permute-start | bytes 49160 | tf_op jit(solution)/shard_map/ppermute | solution.py:348
  31.5 3.7 %collective-permute-start.11 = (f32[4,1024]{1,0:T(4,128)S(1)}, f32[4,1024]{1,0:T(4,128)S(1)}, u32[]{:S(2)}, u32[]{:S(2)}) collective-permute-start(f32[4,1024]{1,0:T(4,128)S(1)} %relay.3.refs_0_), channel_id=1, source_target_pairs={{0,4},{1,5},{2,3},{3,2},{4,0},{5,1},{6,7},{7,6},{8,12},{9,13},{10,... | collective-permute-start | bytes 49160 | tf_op jit(solution)/shard_map/ppermute | solution.py:348
  35.3 3.8 %collective-permute-start.16 = (f32[4,1024]{1,0:T(4,128)S(1)}, f32[4,1024]{1,0:T(4,128)S(1)}, u32[]{:S(2)}, u32[]{:S(2)}) collective-permute-start(f32[4,1024]{1,0:T(4,128)S(1)} %relay.4.refs_0_), channel_id=1, source_target_pairs={{0,4},{2,26},{4,0},{6,30},{8,12},{10,18},{12,8},{14,22},{16,20},{1... | collective-permute-start | bytes 49160 | tf_op jit(solution)/shard_map/ppermute | solution.py:357
  36.9 3.7 %collective-permute-start.15 = (f32[4,1024]{1,0:T(4,128)S(1)}, f32[4,1024]{1,0:T(4,128)S(1)}, u32[]{:S(2)}, u32[]{:S(2)}) collective-permute-start(f32[4,1024]{1,0:T(4,128)S(1)} %relay.4.refs_0_), channel_id=1, source_target_pairs={{0,4},{2,18},{4,0},{6,22},{8,12},{10,26},{12,8},{14,30},{16,20},{1... | collective-permute-start | bytes 49160 | tf_op jit(solution)/shard_map/ppermute | solution.py:357
  37.4 3.7 %collective-permute-start.14 = (f32[4,1024]{1,0:T(4,128)S(1)}, f32[4,1024]{1,0:T(4,128)S(1)}, u32[]{:S(2)}, u32[]{:S(2)}) collective-permute-start(f32[4,1024]{1,0:T(4,128)S(1)} %relay.4.refs_0_), channel_id=1, source_target_pairs={{0,4},{2,10},{4,0},{6,14},{8,12},{10,2},{12,8},{14,6},{16,20},{18,... | collective-permute-start | bytes 49160 | tf_op jit(solution)/shard_map/ppermute | solution.py:357
  41.1 1.2 %collective-permute-start.17 = (f32[4,1024]{1,0:T(4,128)S(1)}, f32[4,1024]{1,0:T(4,128)S(1)}, u32[]{:S(2)}, u32[]{:S(2)}) collective-permute-start(f32[4,1024]{1,0:T(4,128)S(1)} %relay.5.led_ref), channel_id=1, source_target_pairs={{0,2},{2,0},{4,6},{6,4},{1,3},{3,1},{5,7},{7,5},{8,10},{10,8},{12,... | collective-permute-start | bytes 49160 | tf_op jit(solution)/shard_map/ppermute | solution.py:46

commit v18 on v15

--- a/solution.py
+++ b/solution.py
@@ -254,7 +254,7 @@
     before, refs = (refs[:3], refs[3:]) if last else ((), refs)
     feats_refs, (ws_ref, wt_ref, peak_ref, *refs) = refs[:n_feats], refs[n_feats:]
     blocks = [ref.at[i] for ref in feats_refs for i in range(ref.shape[0])]
-    exp_ref, unit_ref, total_ref, *mine = refs[1:] if part else refs
+    exp_ref, unit_ref, total_ref, *mine = refs[2:] if part else refs
     own_ref = mine[0] if last else total_ref
     n, (_, bot, width) = len(blocks), blocks[0].shape
     cols = ws_ref.shape[0]
@@ -268,7 +268,7 @@
             unit = jnp.concatenate([blocks[group * per + k][which] for k in range(per)], axis=1)
             lanes = slice(group * per * width, (group + 1) * per * width)
             if which == 0:
-                unit_ref[lanes, :] = unit.T
+                unit_ref[part * n * width + lanes.start:part * n * width + lanes.stop, :] = unit.T
             stationary = jnp.concatenate([unit, extra], axis=0)
             total = jnp.zeros((8, per * width), jnp.float32)
             for at in range(0, cols, step):
@@ -300,23 +300,25 @@
     total_ref[...] = jnp.concatenate(rows, axis=0)
 
 
-def scores(part, feats, weights, before=(), exps=None):
+def scores(part, feats, weights, before=(), buffers=()):
     _, _, bot, width = feats[0].shape
     cols, rows = weights[0].shape[0], sum(part.shape[0] for part in feats) * width
-    args = (*before, *feats, *weights, *([exps] if part else []))
-    return call(
+    args = (*before, *feats, *weights, *buffers)
+    plain = len(args) - len(buffers)
+    exps, units, total = call(
         functools.partial(score_kernel, part, len(feats)),
         "scores",
         [
             held(cols, 8 * rows, dtype=jnp.bfloat16),
-            held(rows, bot, dtype=jnp.bfloat16),
+            held(4 * rows, bot, dtype=jnp.bfloat16),
             held(4, 2 * rows) if part == 3 else held(2, rows),
         ],
         args,
-        in_specs=[ON_CHIP] * (len(args) - bool(part)) + [IN_HBM] * bool(part),
-        input_output_aliases={len(args) - 1: 0} if part else {},
+        in_specs=[ON_CHIP] * plain + [IN_HBM] * len(buffers),
+        input_output_aliases={plain + i: i for i in range(len(buffers))},
         scratch_shapes=[held(2, rows)] if part == 3 else [],
     )
+    return (exps, units), total
 
 
 def relay_kernel(n_in, *refs):
@@ -346,12 +348,12 @@
     return [lax.all_to_all(jnp.broadcast_to(total[None], (n, *total.shape)), "fsdp", 0, 0, tiled=True)]
 
 
-def grad_kernel(total_ref, peak_ref, weight_unit, weight_scale, *refs):
-    units, exp_ref, out_hbm, scales, feats, *derivs, buf, sems = refs[:4], *refs[4:]
+def grad_kernel(total_ref, peak_ref, weight_unit, weight_scale, unit_ref, exp_ref, out_hbm, scales, *refs):
+    *derivs, buf, sems = refs
     dp, _, core = here()
     scales[0:2, :] = 10.0 / total_ref[0:2, :]
     scales[2:4, :] = 10.0 * jnp.exp2(GAIN_T * peak_ref[:, :1] - total_ref[2:4, :])
-    rows = units[0].shape[0]
+    rows = unit_ref.shape[0] // 4
     width = 128
     n = rows // width
     factors = []
@@ -365,8 +367,6 @@
                 for where in at
             ]
             factors.append(jnp.concatenate(picked, axis=1).astype(jnp.bfloat16))
-    for part, unit in enumerate(units):
-        feats[part * rows:(part + 1) * rows, :] = unit[...]
     chunks, _, step = buf.shape
     stores = []
 
@@ -383,7 +383,7 @@
         if i + 1 < chunks:
             derive(i + 1)
         at = slice(i * step, (i + 1) * step)
-        grad = jnp.dot(derivs[i % 2][...], feats[...], preferred_element_type=jnp.float32).T
+        grad = jnp.dot(derivs[i % 2][...], unit_ref[...], preferred_element_type=jnp.float32).T
         unit = weight_unit[:, at]
         proj = unit * jnp.sum(unit * grad, axis=0, keepdims=True)
         buf[i] = (grad - proj) * weight_scale[:, at]
@@ -395,9 +395,10 @@
 
 def gradient(total, peak, weight_unit, weight_scale, units, exps):
     cols = exps.shape[0]
-    rows, bot = units[0].shape
+    all_rows, bot = units.shape
+    rows = all_rows // 4
     step = min(256, cols)
-    args = (total, peak, weight_unit, weight_scale, *units, exps)
+    args = (total, peak, weight_unit, weight_scale, units, exps)
     return call(
         grad_kernel,
         "gradient",
@@ -406,7 +407,6 @@
         out_specs=IN_HBM,
         scratch_shapes=[
             held(4, 2 * rows),
-            held(4 * rows, bot, dtype=jnp.bfloat16),
             *[held(step, 4 * rows, dtype=jnp.bfloat16)] * 2,
             held(cols // step, bot, step),
             pltpu.SemaphoreType.DMA((cols // step,)),
@@ -428,17 +428,17 @@
         other = [swap(mine, "dp")]
         along = [swap(mine, "fsdp", k) for k in range(1, n_fsdp)]
         half = n_fsdp // 2
-        outs = [(0, n_fsdp, bot), (2, n_fsdp - 2, bot + 16), (0, half, bot), (half, half, bot)]
+        outs = [(0, n_fsdp, bot), (1, n_fsdp - 1, bot), (0, half, bot), (half, n_fsdp - half, bot)]
         own, far, *halves = join([mine, *along], outs, (other[0], peak), bot)
-        other += [swap(other[0], "fsdp"), swap(far, "dp")]
+        other.append(swap(far, "dp"))
     else:
         own = lax.all_to_all(jnp.broadcast_to(mine[None], (n_fsdp, *mine.shape)), "fsdp", 0, 0, tiled=True)
         other, halves = [swap(own, "dp")], [own]
-    exps, unit_a, total_a = scores(0, [own], weights)
-    exps, unit_b, total_b = scores(1, [swap(half, "proto") for half in halves], weights, exps=exps)
+    buffers, total_a = scores(0, [own], weights)
+    buffers, total_b = scores(1, [swap(half, "proto") for half in halves], weights, (), buffers)
     (other,) = join(other, [(0, n_fsdp, bot)], (total_b,), bot)
-    exps, unit_c, total_c = scores(2, [other], weights, exps=exps)
-    exps, unit_d, total = scores(3, [swap(other, "proto")], weights, (total_a, total_b, total_c), exps)
+    buffers, total_c = scores(2, [other], weights, (), buffers)
+    (exps, units), total = scores(3, [swap(other, "proto")], weights, (total_a, total_b, total_c), buffers)
     n_proto, own_cols = lax.axis_size("proto"), ws.shape[0]
     middle = own_cols // 2
     total = add_up([total, swap(total, "proto")])
@@ -447,7 +447,7 @@
     total = add_up([total, *[across(total, *step) for step in steps]], done)
     teacher_new, done = update_rest(teacher_weight, student_weight, total, new, own_cols, middle, own_cols)
     total = add_up(along_fsdp(total), done)
-    student_grad = gradient(total, peak, unit, scale, (unit_a, unit_b, unit_c, unit_d), exps)
+    student_grad = gradient(total, peak, unit, scale, units, exps)
     return (teacher_new, student_grad)
 
 

time: 46.2 us -> 47.6 us (1.030)
  waiting for transfers between devices: 7.41 us -> 9.14 us
    ppermute x14 -> x13, waiting for transfers between devices: 7.15 us -> 9.13 us  [swap(): lax.ppermute(block, axis, [(i, i ^ apart) for i in range(lax.axis_size(ax...]
    ppermute x14 -> x13, starting transfers between devices: 15.7 us -> 15.3 us  [swap(): lax.ppermute(block, axis, [(i, i ^ apart) for i in range(lax.axis_size(ax...]
  transfers between devices with their start and end apart: 17 -> 16, of which waited for: 8 -> 5; matrix products, arithmetic and copies ran while one was open for 0% -> 0% of each run, Pallas kernels for 29% -> 28%
where the time goes in v18:
time: 47.6 us; the launch traced here: 47.4 us
  starting transfers between devices  18.9 us (40%)
  Pallas kernels  18.6 us (39%)
  waiting for transfers between devices  9.14 us (19%)
  between operations  0.82 us (2%)
    pallas_call x15, Pallas kernels, call(): pl.pallas_call(kernel, out_shape=out_shape, compiler_params=pltpu.Compile...  18.6 us
    ppermute x13, starting transfers between devices, swap(): lax.ppermute(block, axis, [(i, i ^ apart) for i in range(lax.axis_size(ax...  15.3 us
    ppermute x13, waiting for transfers between devices, swap(): lax.ppermute(block, axis, [(i, i ^ apart) for i in range(lax.axis_size(ax...  9.13 us
    ppermute x3, starting transfers between devices, across(): return lax.ppermute(total, ('proto', 'dp'), pairs)  3.55 us
  transfers between devices with their start and end apart: 16, of which 5 were waited for; matrix products, arithmetic and copies ran while one was open for 0% of the time, Pallas kernels for 28%

profile of v18, /device:TPU:0, one launch (start us, length us, event | category | flops | bytes accessed | tf_op | source)
XLA Modules:
  0.0 47.4 jit_solution(4163224206951398925)
XLA Ops:
  0.6 3.0 %collective-permute-start = (s32[1,256]{1,0:T(1,128)}, s32[1,256]{1,0:T(1,128)S(1)}, u32[]{:S(2)}, u32[]{:S(2)}) collective-permute-start(s32[1,256]{1,0:T(1,128)} %param.10), channel_id=1, source_target_pairs={{0,1},{1,0},{2,3},{3,2},{4,5},{5,4},{6,7},{7,6},{8,9},{9,8},{10,11... | collective-permute-start | bytes 3080 | tf_op jit(solution)/shard_map/ppermute | solution.py:46
  3.6 0.9 %fetch.1 = (bf16[192,128]{1,0:T(8,128)(2,1)S(1)}, bf16[192,256]{1,0:T(8,128)(2,1)S(1)}) custom-call(bf16[192,256]{1,0:T(8,128)(2,1)} %bitcast.7, bf16[192,256]{1,0:T(8,128)(2,1)} %bitcast.8), custom_call_target="tpu_custom_call" | custom-call | flops 1 | bytes 1 | tf_op jit(solution)/shard_map/fetch/pallas_call | solution.py:35
  4.6 0.8 %collective-permute-done.index_ref = s32[1,256]{1,0:T(1,128)S(1)} collective-permute-done((s32[1,256]{1,0:T(1,128)}, s32[1,256]{1,0:T(1,128)S(1)}, u32[]{:S(2)}, u32[]{:S(2)}) %collective-permute-start) | collective-permute-done | bytes 1056 | tf_op jit(solution)/shard_map/ppermute | solution.py:46
  5.6 2.1 %collective-permute-start.4 = (bf16[2,192,128]{2,1,0:T(8,128)(2,1)S(1)}, bf16[2,192,128]{2,1,0:T(8,128)(2,1)S(1)}, u32[]{:S(2)}, u32[]{:S(2)}) collective-permute-start(bf16[2,192,128]{2,1,0:T(8,128)(2,1)S(1)} %pack.1.refs_0_), channel_id=1, source_target_pairs={{0,1},{1,0},{2,3},{3,2},{4,5},{5,4},{6,7},{7,6},{8,9},{9,8},{10,11... | collective-permute-start | bytes 294920 | tf_op jit(solution)/shard_map/ppermute | solution.py:46
  7.7 3.6 %collective-permute-start.3 = (bf16[2,192,128]{2,1,0:T(8,128)(2,1)S(1)}, bf16[2,192,128]{2,1,0:T(8,128)(2,1)S(1)}, u32[]{:S(2)}, u32[]{:S(2)}) collective-permute-start(bf16[2,192,128]{2,1,0:T(8,128)(2,1)S(1)} %pack.1.refs_0_), channel_id=1, source_target_pairs={{0,24},{8,16},{16,8},{24,0},{1,25},{9,17},{17,9},{25,1},{2,26},{10... | collective-permute-start | bytes 294920 | tf_op jit(solution)/shard_map/ppermute | solution.py:46
  11.3 0.8 %collective-permute-start.1 = (bf16[2,192,128]{2,1,0:T(8,128)(2,1)S(1)}, bf16[2,192,128]{2,1,0:T(8,128)(2,1)S(1)}, u32[]{:S(2)}, u32[]{:S(2)}) collective-permute-start(bf16[2,192,128]{2,1,0:T(8,128)(2,1)S(1)} %pack.1.refs_0_), channel_id=1, source_target_pairs={{0,8},{8,0},{16,24},{24,16},{1,9},{9,1},{17,25},{25,17},{2,10},{10... | collective-permute-start | bytes 294920 | tf_op jit(solution)/shard_map/ppermute | solution.py:46
  12.1 3.6 %prep.1 = (f32[192,4096]{1,0:T(8,128)}, bf16[2048,256]{1,0:T(8,128)(2,1)S(1)}, bf16[2048,256]{1,0:T(8,128)(2,1)S(1)}, f32[192,2048]{1,0:T(8,128)S(1)}, f32[1,2048]{1,0:T(1,128)S(1)}, /*index=5*/f32[1,128]{1,0:T(1,128)S(1)}) custom-call(f32[192,4096]{1,0:T(8,128)} %teacher_hbm.5, f32[192,4096]{1,0:T(8,128)} %student_hbm.5, f32[1,16384]{1,0:T(1,128)} %bitcast.9), custom_call_target="tpu_custom_call" | custom-call | flops 1 | bytes 1 | tf_op jit(solution)/shard_map/prep/pallas_call | solution.py:35
  15.7 2.5 %collective-permute-done.2.refs_2_ = bf16[2,192,128]{2,1,0:T(8,128)(2,1)S(1)} collective-permute-done((bf16[2,192,128]{2,1,0:T(8,128)(2,1)S(1)}, bf16[2,192,128]{2,1,0:T(8,128)(2,1)S(1)}, u32[]{:S(2)}, u32[]{:S(2)}) %collective-permute-start.2) | collective-permute-done | bytes 98336 | tf_op jit(solution)/shard_map/ppermute | solution.py:46
  18.3 0.6 %collective-permute-start.7 = (bf16[3,2,192,128]{3,2,1,0:T(8,128)(2,1)S(1)}, bf16[3,2,192,128]{3,2,1,0:T(8,128)(2,1)S(1)}, u32[]{:S(2)}, u32[]{:S(2)}) collective-permute-start(bf16[3,2,192,128]{3,2,1,0:T(8,128)(2,1)S(1)} %get-tuple-element.42), channel_id=1, source_target_pairs={{0,1},{1,0},{2,3},{3,2},{4,5},{5,4},{6,7},{7,6},{8,9},{9,8},{10,11... | collective-permute-start | bytes 884744 | tf_op jit(solution)/shard_map/ppermute | solution.py:46
  18.9 0.5 %collective-permute-start.6 = (bf16[2,2,192,128]{3,2,1,0:T(8,128)(2,1)S(1)}, bf16[2,2,192,128]{3,2,1,0:T(8,128)(2,1)S(1)}, u32[]{:S(2)}, u32[]{:S(2)}) collective-permute-start(bf16[2,2,192,128]{3,2,1,0:T(8,128)(2,1)S(1)} %get-tuple-element.38), channel_id=1, source_target_pairs={{0,2},{2,0},{4,6},{6,4},{1,3},{3,1},{5,7},{7,5},{8,10},{10,8},{12,... | collective-permute-start | bytes 589832 | tf_op jit(solution)/shard_map/ppermute | solution.py:46
  19.4 1.3 %scores.4 = (bf16[2048,4096]{1,0:T(8,128)(2,1)S(1)}, bf16[2048,192]{1,0:T(8,128)(2,1)S(1)}, f32[2,512]{1,0:T(2,128)S(1)}) custom-call(bf16[4,2,192,128]{3,2,1,0:T(8,128)(2,1)S(1)} %get-tuple-element.33.refs_0_, bf16[2048,256]{1,0:T(8,128)(2,1)S(1)} %get-tuple-element.34.refs_1_.refs_2_.refs_4_, ...), custom_call_target="tpu_custom_call" | custom-call | flops 1 | bytes 1 | tf_op jit(solution)/shard_map/scores/pallas_call | solution.py:35
  20.8 1.3 %scores.5 = (bf16[2048,4096]{1,0:T(8,128)(2,1)S(1)}, bf16[2048,192]{1,0:T(8,128)(2,1)S(1)}, f32[2,512]{1,0:T(2,128)S(1)}) custom-call(bf16[2,2,192,128]{3,2,1,0:T(8,128)(2,1)S(1)} %collective-permute-done.5.refs_0_, bf16[2,2,192,128]{3,2,1,0:T(8,128)(2,1)S(1)} %collective-permute-done.6.refs_1_, ...), custom_call_target="tpu_custom_call", output_to_operand_aliasing={{0}: (5, {}), {1}: (6, {})} | custom-call | flops 1 | bytes 1 | tf_op jit(solution)/shard_map/scores/pallas_call | solution.py:35
  22.1 4.3 %collective-permute-done.7.refs_1_ = bf16[3,2,192,128]{3,2,1,0:T(8,128)(2,1)S(1)} collective-permute-done((bf16[3,2,192,128]{3,2,1,0:T(8,128)(2,1)S(1)}, bf16[3,2,192,128]{3,2,1,0:T(8,128)(2,1)S(1)}, u32[]{:S(2)}, u32[]{:S(2)}) %collective-permute-start.7) | collective-permute-done | bytes 294944 | tf_op jit(solution)/shard_map/ppermute | solution.py:46
  26.5 1.3 %scores.6 = (bf16[2048,4096]{1,0:T(8,128)(2,1)S(1)}, bf16[2048,192]{1,0:T(8,128)(2,1)S(1)}, f32[2,512]{1,0:T(2,128)S(1)}) custom-call(bf16[4,2,192,128]{3,2,1,0:T(8,128)(2,1)S(1)} %join.3.refs_0_, bf16[2048,256]{1,0:T(8,128)(2,1)S(1)} %get-tuple-element.34.refs_1_.refs_2_.refs_4_, ...), custom_call_target="tpu_custom_call", output_to_operand_aliasing={{0}: (4, {}), {1}: (5, {})} | custom-call | flops 1 | bytes 1 | tf_op jit(solution)/shard_map/scores/pallas_call | solution.py:35
  28.2 1.3 %scores.7 = (bf16[2048,4096]{1,0:T(8,128)(2,1)S(1)}, bf16[2048,192]{1,0:T(8,128)(2,1)S(1)}, f32[4,1024]{1,0:T(4,128)S(1)}) custom-call(f32[2,512]{1,0:T(2,128)S(1)} %get-tuple-element.36.refs_0_, f32[2,512]{1,0:T(2,128)S(1)} %get-tuple-element.41.refs_2_.refs_1_, ...), custom_call_target="tpu_custom_call", output_to_operand_aliasing={{0}: (7, {}), {1}: (8, {})} | custom-call | flops 1 | bytes 1 | tf_op jit(solution)/shard_map/scores/pallas_call | solution.py:35
  29.8 1.0 %collective-permute-done.9.refs_1_ = f32[4,1024]{1,0:T(4,128)S(1)} collective-permute-done((f32[4,1024]{1,0:T(4,128)S(1)}, f32[4,1024]{1,0:T(4,128)S(1)}, u32[]{:S(2)}, u32[]{:S(2)}) %collective-permute-start.9) | collective-permute-done | bytes 16416 | tf_op jit(solution)/shard_map/ppermute | solution.py:46
  30.8 1.6 %collective-permute-start.12 = (f32[4,1024]{1,0:T(4,128)S(1)}, f32[4,1024]{1,0:T(4,128)S(1)}, u32[]{:S(2)}, u32[]{:S(2)}) collective-permute-start(f32[4,1024]{1,0:T(4,128)S(1)} %relay.3.after.refs_0_), channel_id=1, source_target_pairs={{0,5},{1,4},{2,7},{3,6},{4,1},{5,0},{6,3},{7,2},{8,13},{9,12},{10,... | collective-permute-start | bytes 49160 | tf_op jit(solution)/shard_map/ppermute | solution.py:341
  32.4 0.5 %collective-permute-start.11 = (f32[4,1024]{1,0:T(4,128)S(1)}, f32[4,1024]{1,0:T(4,128)S(1)}, u32[]{:S(2)}, u32[]{:S(2)}) collective-permute-start(f32[4,1024]{1,0:T(4,128)S(1)} %relay.3.after.refs_0_), channel_id=1, source_target_pairs={{0,4},{1,5},{2,6},{3,7},{4,0},{5,1},{6,2},{7,3},{8,12},{9,13},{10,... | collective-permute-start | bytes 49160 | tf_op jit(solution)/shard_map/ppermute | solution.py:341
  32.9 1.5 %collective-permute-start.10 = (f32[4,1024]{1,0:T(4,128)S(1)}, f32[4,1024]{1,0:T(4,128)S(1)}, u32[]{:S(2)}, u32[]{:S(2)}) collective-permute-start(f32[4,1024]{1,0:T(4,128)S(1)} %relay.3.after.refs_0_), channel_id=1, source_target_pairs={{0,1},{1,0},{2,3},{3,2},{4,5},{5,4},{6,7},{7,6},{8,9},{9,8},{10,11... | collective-permute-start | bytes 49160 | tf_op jit(solution)/shard_map/ppermute | solution.py:341
  34.4 2.4 %rest.2 = (f32[192,4096]{1,0:T(8,128)}, f32[8,128]{1,0:T(8,128)S(1)}) custom-call(f32[192,4096]{1,0:T(8,128)} %teacher_hbm.5, f32[192,4096]{1,0:T(8,128)} %student_hbm.5, f32[4,1024]{1,0:T(4,128)S(1)} %relay.3.after.refs_0_, f32[192,4096]{1,0:T(8,128)} %get-tuple-element.49.before_hbm), custom_call_target="tpu_custom_call", output_to_operand_aliasing={{0}: (3, {})} | custom-call | flops 1 | bytes 1 | tf_op jit(solution)/shard_map/rest/pallas_call | solution.py:35
  36.9 1.2 %collective-permute-start.15 = (f32[4,1024]{1,0:T(4,128)S(1)}, f32[4,1024]{1,0:T(4,128)S(1)}, u32[]{:S(2)}, u32[]{:S(2)}) collective-permute-start(f32[4,1024]{1,0:T(4,128)S(1)} %relay.4.after.refs_0_), channel_id=1, source_target_pairs={{0,24},{8,16},{16,8},{24,0},{1,25},{9,17},{17,9},{25,1},{2,26},{10... | collective-permute-start | bytes 49160 | tf_op jit(solution)/shard_map/ppermute | solution.py:46
  38.0 3.3 %collective-permute-start.13 = (f32[4,1024]{1,0:T(4,128)S(1)}, f32[4,1024]{1,0:T(4,128)S(1)}, u32[]{:S(2)}, u32[]{:S(2)}) collective-permute-start(f32[4,1024]{1,0:T(4,128)S(1)} %relay.4.after.refs_0_), channel_id=1, source_target_pairs={{0,8},{8,0},{16,24},{24,16},{1,9},{9,1},{17,25},{25,17},{2,10},{10... | collective-permute-start | bytes 49160 | tf_op jit(solution)/shard_map/ppermute | solution.py:46
  41.3 2.4 %rest.3 = (f32[192,4096]{1,0:T(8,128)}, f32[8,128]{1,0:T(8,128)S(1)}) custom-call(f32[192,4096]{1,0:T(8,128)} %teacher_hbm.5, f32[192,4096]{1,0:T(8,128)} %student_hbm.5, f32[4,1024]{1,0:T(4,128)S(1)} %relay.4.after.refs_0_, f32[192,4096]{1,0:T(8,128)} %get-tuple-element.51.before_hbm), custom_call_target="tpu_custom_call", output_to_operand_aliasing={{0}: (3, {})} | custom-call | flops 1 | bytes 1 | tf_op jit(solution)/shard_map/rest/pallas_call | solution.py:35
  43.8 3.6 %gradient.1 = f32[192,2048]{1,0:T(8,128)} custom-call(f32[4,1024]{1,0:T(4,128)S(1)} %relay.5.total_ref, f32[1,128]{1,0:T(1,128)S(1)} %get-tuple-element.32.refs_5_.refs_3_.refs_4_.refs_6_.peak_ref, f32[192,2048]{1,0:T(8,128)S(1)} %get-tuple-element.54.weight_unit, f32[1,2048]{1,0:T(1,128)S(1)} %get-tuple-element.55.weight_scale, ...), custom_call_target="tpu_custom_call" | custom-call | flops 1 | bytes 1 | tf_op jit(solution)/shard_map/gradient/pallas_call | solution.py:35
  (23 shorter events, 1.1 us)
Async XLA Ops:
  0.6 4.8 %collective-permute-start = (s32[1,256]{1,0:T(1,128)}, s32[1,256]{1,0:T(1,128)S(1)}, u32[]{:S(2)}, u32[]{:S(2)}) collective-permute-start(s32[1,256]{1,0:T(1,128)} %param.10), channel_id=1, source_target_pairs={{0,1},{1,0},{2,3},{3,2},{4,5},{5,4},{6,7},{7,6},{8,9},{9,8},{10,11... | collective-permute-start | bytes 3080 | tf_op jit(solution)/shard_map/ppermute | solution.py:46
  5.6 10.1 %collective-permute-start.4 = (bf16[2,192,128]{2,1,0:T(8,128)(2,1)S(1)}, bf16[2,192,128]{2,1,0:T(8,128)(2,1)S(1)}, u32[]{:S(2)}, u32[]{:S(2)}) collective-permute-start(bf16[2,192,128]{2,1,0:T(8,128)(2,1)S(1)} %pack.1.refs_0_), channel_id=1, source_target_pairs={{0,1},{1,0},{2,3},{3,2},{4,5},{5,4},{6,7},{7,6},{8,9},{9,8},{10,11... | collective-permute-start | bytes 294920 | tf_op jit(solution)/shard_map/ppermute | solution.py:46
  7.7 8.0 %collective-permute-start.3 = (bf16[2,192,128]{2,1,0:T(8,128)(2,1)S(1)}, bf16[2,192,128]{2,1,0:T(8,128)(2,1)S(1)}, u32[]{:S(2)}, u32[]{:S(2)}) collective-permute-start(bf16[2,192,128]{2,1,0:T(8,128)(2,1)S(1)} %pack.1.refs_0_), channel_id=1, source_target_pairs={{0,24},{8,16},{16,8},{24,0},{1,25},{9,17},{17,9},{25,1},{2,26},{10... | collective-permute-start | bytes 294920 | tf_op jit(solution)/shard_map/ppermute | solution.py:46
  11.3 6.9 %collective-permute-start.2 = (bf16[2,192,128]{2,1,0:T(8,128)(2,1)S(1)}, bf16[2,192,128]{2,1,0:T(8,128)(2,1)S(1)}, u32[]{:S(2)}, u32[]{:S(2)}) collective-permute-start(bf16[2,192,128]{2,1,0:T(8,128)(2,1)S(1)} %pack.1.refs_0_), channel_id=1, source_target_pairs={{0,16},{8,24},{16,0},{24,8},{1,17},{9,25},{17,1},{25,9},{2,18},{10... | collective-permute-start | bytes 294920 | tf_op jit(solution)/shard_map/ppermute | solution.py:46
  11.3 6.9 %collective-permute-start.1 = (bf16[2,192,128]{2,1,0:T(8,128)(2,1)S(1)}, bf16[2,192,128]{2,1,0:T(8,128)(2,1)S(1)}, u32[]{:S(2)}, u32[]{:S(2)}) collective-permute-start(bf16[2,192,128]{2,1,0:T(8,128)(2,1)S(1)} %pack.1.refs_0_), channel_id=1, source_target_pairs={{0,8},{8,0},{16,24},{24,16},{1,9},{9,1},{17,25},{25,17},{2,10},{10... | collective-permute-start | bytes 294920 | tf_op jit(solution)/shard_map/ppermute | solution.py:46
  18.3 8.1 %collective-permute-start.7 = (bf16[3,2,192,128]{3,2,1,0:T(8,128)(2,1)S(1)}, bf16[3,2,192,128]{3,2,1,0:T(8,128)(2,1)S(1)}, u32[]{:S(2)}, u32[]{:S(2)}) collective-permute-start(bf16[3,2,192,128]{3,2,1,0:T(8,128)(2,1)S(1)} %get-tuple-element.42), channel_id=1, source_target_pairs={{0,1},{1,0},{2,3},{3,2},{4,5},{5,4},{6,7},{7,6},{8,9},{9,8},{10,11... | collective-permute-start | bytes 884744 | tf_op jit(solution)/shard_map/ppermute | solution.py:46
  18.9 1.8 %collective-permute-start.5 = (bf16[2,2,192,128]{3,2,1,0:T(8,128)(2,1)S(1)}, bf16[2,2,192,128]{3,2,1,0:T(8,128)(2,1)S(1)}, u32[]{:S(2)}, u32[]{:S(2)}) collective-permute-start(bf16[2,2,192,128]{3,2,1,0:T(8,128)(2,1)S(1)} %get-tuple-element.37), channel_id=1, source_target_pairs={{0,2},{2,0},{4,6},{6,4},{1,3},{3,1},{5,7},{7,5},{8,10},{10,8},{12,... | collective-permute-start | bytes 589832 | tf_op jit(solution)/shard_map/ppermute | solution.py:46
  18.9 1.8 %collective-permute-start.6 = (bf16[2,2,192,128]{3,2,1,0:T(8,128)(2,1)S(1)}, bf16[2,2,192,128]{3,2,1,0:T(8,128)(2,1)S(1)}, u32[]{:S(2)}, u32[]{:S(2)}) collective-permute-start(bf16[2,2,192,128]{3,2,1,0:T(8,128)(2,1)S(1)} %get-tuple-element.38), channel_id=1, source_target_pairs={{0,2},{2,0},{4,6},{6,4},{1,3},{3,1},{5,7},{7,5},{8,10},{10,8},{12,... | collective-permute-start | bytes 589832 | tf_op jit(solution)/shard_map/ppermute | solution.py:46
  26.5 1.8 %collective-permute-start.8 = (bf16[4,2,192,128]{3,2,1,0:T(8,128)(2,1)S(1)}, bf16[4,2,192,128]{3,2,1,0:T(8,128)(2,1)S(1)}, u32[]{:S(2)}, u32[]{:S(2)}) collective-permute-start(bf16[4,2,192,128]{3,2,1,0:T(8,128)(2,1)S(1)} %join.3.refs_0_), channel_id=1, source_target_pairs={{0,2},{2,0},{4,6},{6,4},{1,3},{3,1},{5,7},{7,5},{8,10},{10,8},{12,... | collective-permute-start | bytes 1179656 | tf_op jit(solution)/shard_map/ppermute | solution.py:46
  29.6 1.2 %collective-permute-start.9 = (f32[4,1024]{1,0:T(4,128)S(1)}, f32[4,1024]{1,0:T(4,128)S(1)}, u32[]{:S(2)}, u32[]{:S(2)}) collective-permute-start(f32[4,1024]{1,0:T(4,128)S(1)} %get-tuple-element.48.refs_0_), channel_id=1, source_target_pairs={{0,2},{2,0},{4,6},{6,4},{1,3},{3,1},{5,7},{7,5},{8,10},{10,8},{12,... | collective-permute-start | bytes 49160 | tf_op jit(solution)/shard_map/ppermute | solution.py:46
  30.8 6.0 %collective-permute-start.12 = (f32[4,1024]{1,0:T(4,128)S(1)}, f32[4,1024]{1,0:T(4,128)S(1)}, u32[]{:S(2)}, u32[]{:S(2)}) collective-permute-start(f32[4,1024]{1,0:T(4,128)S(1)} %relay.3.after.refs_0_), channel_id=1, source_target_pairs={{0,5},{1,4},{2,7},{3,6},{4,1},{5,0},{6,3},{7,2},{8,13},{9,12},{10,... | collective-permute-start | bytes 49160 | tf_op jit(solution)/shard_map/ppermute | solution.py:341
  32.4 4.4 %collective-permute-start.11 = (f32[4,1024]{1,0:T(4,128)S(1)}, f32[4,1024]{1,0:T(4,128)S(1)}, u32[]{:S(2)}, u32[]{:S(2)}) collective-permute-start(f32[4,1024]{1,0:T(4,128)S(1)} %relay.3.after.refs_0_), channel_id=1, source_target_pairs={{0,4},{1,5},{2,6},{3,7},{4,0},{5,1},{6,2},{7,3},{8,12},{9,13},{10,... | collective-permute-start | bytes 49160 | tf_op jit(solution)/shard_map/ppermute | solution.py:341
  32.9 3.9 %collective-permute-start.10 = (f32[4,1024]{1,0:T(4,128)S(1)}, f32[4,1024]{1,0:T(4,128)S(1)}, u32[]{:S(2)}, u32[]{:S(2)}) collective-permute-start(f32[4,1024]{1,0:T(4,128)S(1)} %relay.3.after.refs_0_), channel_id=1, source_target_pairs={{0,1},{1,0},{2,3},{3,2},{4,5},{5,4},{6,7},{7,6},{8,9},{9,8},{10,11... | collective-permute-start | bytes 49160 | tf_op jit(solution)/shard_map/ppermute | solution.py:341
  36.9 6.9 %collective-permute-start.15 = (f32[4,1024]{1,0:T(4,128)S(1)}, f32[4,1024]{1,0:T(4,128)S(1)}, u32[]{:S(2)}, u32[]{:S(2)}) collective-permute-start(f32[4,1024]{1,0:T(4,128)S(1)} %relay.4.after.refs_0_), channel_id=1, source_target_pairs={{0,24},{8,16},{16,8},{24,0},{1,25},{9,17},{17,9},{25,1},{2,26},{10... | collective-permute-start | bytes 49160 | tf_op jit(solution)/shard_map/ppermute | solution.py:46
  38.0 5.7 %collective-permute-start.14 = (f32[4,1024]{1,0:T(4,128)S(1)}, f32[4,1024]{1,0:T(4,128)S(1)}, u32[]{:S(2)}, u32[]{:S(2)}) collective-permute-start(f32[4,1024]{1,0:T(4,128)S(1)} %relay.4.after.refs_0_), channel_id=1, source_target_pairs={{0,16},{8,24},{16,0},{24,8},{1,17},{9,25},{17,1},{25,9},{2,18},{10... | collective-permute-start | bytes 49160 | tf_op jit(solution)/shard_map/ppermute | solution.py:46
  38.0 5.7 %collective-permute-start.13 = (f32[4,1024]{1,0:T(4,128)S(1)}, f32[4,1024]{1,0:T(4,128)S(1)}, u32[]{:S(2)}, u32[]{:S(2)}) collective-permute-start(f32[4,1024]{1,0:T(4,128)S(1)} %relay.4.after.refs_0_), channel_id=1, source_target_pairs={{0,8},{8,0},{16,24},{24,16},{1,9},{9,1},{17,25},{25,17},{2,10},{10... | collective-permute-start | bytes 49160 | tf_op jit(solution)/shard_map/ppermute | solution.py:46

commit v19 on v17

--- a/solution.py
+++ b/solution.py
@@ -336,33 +336,50 @@
     return call(functools.partial(relay_kernel, len(parts)), "relay", held(*parts[0].shape[-2:]), parts)
 
 
-def aside(p, n_proto):
-    return (p ^ 2) if n_proto % 4 == 0 else p ^ 1
+def exchange(total, axes, first, second):
+    sizes = [lax.axis_size(axis) for axis in axes]
+    proto = axes.index("proto")
+    places = [(i, j) for i in range(sizes[0]) for j in range(sizes[1])]
+
+    def permute(step):
+        flat = lambda place: place[0] * sizes[1] + place[1]
+        pairs = []
+        for place in places:
+            up = step(place[proto] % 2)
+            pairs.append((flat(place), flat((place[0] ^ up[0], place[1] ^ up[1]))))
+        return lax.ppermute(total, axes, pairs)
+
+    mine = permute(first)
+    return add_up([total, mine, swap(mine, "proto"), permute(second)])
 
 
 def across(total, up, over):
     n_proto, n_dp = lax.axis_size("proto"), lax.axis_size("dp")
-    far = lambda p, d: (p ^ up, d ^ over) if p % 2 else (aside(p, n_proto), d)
     places = [(p, d) for p in range(n_proto) for d in range(n_dp)]
-    pairs = [(p * n_dp + d, far(p, d)[0] * n_dp + far(p, d)[1]) for p, d in places]
+    pairs = [(p * n_dp + d, (p ^ up) * n_dp + (d ^ over)) for p, d in places]
     return lax.ppermute(total, ("proto", "dp"), pairs)
 
 
-def along_fsdp(total):
-    n, n_proto = lax.axis_size("fsdp"), lax.axis_size("proto")
-    if n > DIRECT:
-        return [lax.all_to_all(jnp.broadcast_to(total[None], (n, *total.shape)), "fsdp", 0, 0, tiled=True)]
-    far = lambda i, p, k: (i ^ k) * n_proto + p if p % 2 else i * n_proto + aside(p, n_proto)
-    pairs = lambda k: [(i * n_proto + p, far(i, p, k)) for i in range(n) for p in range(n_proto)]
-    return [total, *[lax.ppermute(total, ("fsdp", "proto"), pairs(k)) for k in range(1, n)]]
-
-
-def grad_kernel(led_ref, given_ref, peak_ref, weight_unit, weight_scale, *refs):
+def add_up_all(total):
+    n_proto, n_dp, n_fsdp = [lax.axis_size(axis) for axis in ("proto", "dp", "fsdp")]
+    total = add_up([total, swap(total, "proto")])
+    if n_proto == 4 and n_dp == 2:
+        total = exchange(total, ("proto", "dp"), lambda odd: (2 * odd, 1), lambda odd: (2, 0))
+    else:
+        steps = [(up, over) for up in range(0, n_proto, 2) for over in range(n_dp)][1:]
+        total = add_up([total, *[across(total, *step) for step in steps]])
+    if n_fsdp == 4:
+        return exchange(total, ("fsdp", "proto"), lambda odd: (1 + 2 * odd, 0), lambda odd: (2, 0))
+    if n_fsdp <= DIRECT:
+        return add_up([total, *[swap(total, "fsdp", k) for k in range(1, n_fsdp)]])
+    return add_up([lax.all_to_all(jnp.broadcast_to(total[None], (n_fsdp, *total.shape)), "fsdp", 0, 0, tiled=True)])
+
+
+def grad_kernel(total_ref, peak_ref, weight_unit, weight_scale, *refs):
     units, exp_ref, out_hbm, scales, feats, *derivs, buf, sems = refs[:4], *refs[4:]
     dp, _, core = here()
-    total = jnp.where(core == 1, led_ref[...], given_ref[...])
-    scales[0:2, :] = 10.0 / total[0:2]
-    scales[2:4, :] = 10.0 * jnp.exp2(GAIN_T * peak_ref[:, :1] - total[2:4])
+    scales[0:2, :] = 10.0 / total_ref[0:2, :]
+    scales[2:4, :] = 10.0 * jnp.exp2(GAIN_T * peak_ref[:, :1] - total_ref[2:4, :])
     rows = units[0].shape[0]
     width = 128
     n = rows // width
@@ -405,11 +422,11 @@
         store.wait()
 
 
-def gradient(led, given, peak, weight_unit, weight_scale, units, exps):
+def gradient(total, peak, weight_unit, weight_scale, units, exps):
     cols = exps.shape[0]
     rows, bot = units[0].shape
     step = min(256, cols)
-    args = (led, given, peak, weight_unit, weight_scale, *units, exps)
+    args = (total, peak, weight_unit, weight_scale, *units, exps)
     return call(
         grad_kernel,
         "gradient",
@@ -454,12 +471,9 @@
     (other,) = join(other, [(0, n_fsdp, bot)], (total_b, done), bot)
     exps, unit_c, total_c = scores(2, [other], weights, exps=exps)
     exps, unit_d, total = scores(3, [swap(other, "proto")], weights, (total_a, total_b, total_c), exps)
-    total = add_up([total, swap(total, "proto")])
-    steps = [(up, over) for up in range(0, lax.axis_size("proto"), 2) for over in range(n_dp)][1:]
-    total = add_up([total, *[across(total, *step) for step in steps]])
-    total = add_up(along_fsdp(total))
+    total = add_up_all(total)
     units = (unit_a, unit_b, unit_c, unit_d)
-    student_grad = gradient(total, swap(total, "proto"), peak, unit, scale, units, exps)
+    student_grad = gradient(total, peak, unit, scale, units, exps)
     return (teacher_new, student_grad)
 
 

time: 46.1 us -> 44.9 us (0.974)
  starting transfers between devices: 18.6 us -> 17.7 us
    ppermute x6 -> x4, starting transfers between devices: 7.22 us -> 5.74 us  [permute(): return lax.ppermute(total, axes, pairs)]
    ppermute x12 -> x13, waiting for transfers between devices: 5.02 us -> 3.85 us  [swap(): lax.ppermute(block, axis, [(i, i ^ apart) for i in range(lax.axis_size(ax...]
    ppermute x6 -> x4, waiting for transfers between devices: 4.43 us -> 5.31 us  [permute(): return lax.ppermute(total, axes, pairs)]
    ppermute x12 -> x13, starting transfers between devices: 11.4 us -> 11.9 us  [swap(): lax.ppermute(block, axis, [(i, i ^ apart) for i in range(lax.axis_size(ax...]
  transfers between devices with their start and end apart: 18 -> 17, of which waited for: 11 -> 8; matrix products, arithmetic and copies ran while one was open for 0% -> 0% of each run, Pallas kernels for 26% -> 26%
where the time goes in v19:
time: 44.9 us; the launch traced here: 44.7 us
  starting transfers between devices  17.7 us (39%)
  Pallas kernels  17.1 us (38%)
  waiting for transfers between devices  9.16 us (20%)
  between operations  0.78 us (2%)
    pallas_call x14, Pallas kernels, call(): pl.pallas_call(kernel, out_shape=out_shape, compiler_params=pltpu.Compile...  17.1 us
    ppermute x13, starting transfers between devices, swap(): lax.ppermute(block, axis, [(i, i ^ apart) for i in range(lax.axis_size(ax...  11.9 us
    ppermute x4, starting transfers between devices, permute(): return lax.ppermute(total, axes, pairs)  5.74 us
    ppermute x4, waiting for transfers between devices, permute(): return lax.ppermute(total, axes, pairs)  5.31 us
    ppermute x13, waiting for transfers between devices, swap(): lax.ppermute(block, axis, [(i, i ^ apart) for i in range(lax.axis_size(ax...  3.85 us
  transfers between devices with their start and end apart: 17, of which 8 were waited for; matrix products, arithmetic and copies ran while one was open for 0% of the time, Pallas kernels for 26%

profile of v19, /device:TPU:0, one launch (start us, length us, event | category | flops | bytes accessed | tf_op | source)
XLA Modules:
  0.0 44.7 jit_solution(4052463606532850732)
XLA Ops:
  0.6 3.0 %collective-permute-start = (s32[1,256]{1,0:T(1,128)}, s32[1,256]{1,0:T(1,128)S(1)}, u32[]{:S(2)}, u32[]{:S(2)}) collective-permute-start(s32[1,256]{1,0:T(1,128)} %param.10), channel_id=1, source_target_pairs={{0,1},{1,0},{2,3},{3,2},{4,5},{5,4},{6,7},{7,6},{8,9},{9,8},{10,11... | collective-permute-start | bytes 3080 | tf_op jit(solution)/shard_map/ppermute | solution.py:46
  3.6 0.9 %fetch.1 = (bf16[192,128]{1,0:T(8,128)(2,1)S(1)}, bf16[192,256]{1,0:T(8,128)(2,1)S(1)}) custom-call(bf16[192,256]{1,0:T(8,128)(2,1)} %bitcast.7, bf16[192,256]{1,0:T(8,128)(2,1)} %bitcast.8), custom_call_target="tpu_custom_call" | custom-call | flops 1 | bytes 1 | tf_op jit(solution)/shard_map/fetch/pallas_call | solution.py:35
  4.6 0.8 %collective-permute-done.index_ref = s32[1,256]{1,0:T(1,128)S(1)} collective-permute-done((s32[1,256]{1,0:T(1,128)}, s32[1,256]{1,0:T(1,128)S(1)}, u32[]{:S(2)}, u32[]{:S(2)}) %collective-permute-start) | collective-permute-done | bytes 1056 | tf_op jit(solution)/shard_map/ppermute | solution.py:46
  5.6 2.1 %collective-permute-start.4 = (bf16[2,192,128]{2,1,0:T(8,128)(2,1)S(1)}, bf16[2,192,128]{2,1,0:T(8,128)(2,1)S(1)}, u32[]{:S(2)}, u32[]{:S(2)}) collective-permute-start(bf16[2,192,128]{2,1,0:T(8,128)(2,1)S(1)} %pack.1.refs_0_), channel_id=1, source_target_pairs={{0,1},{1,0},{2,3},{3,2},{4,5},{5,4},{6,7},{7,6},{8,9},{9,8},{10,11... | collective-permute-start | bytes 294920 | tf_op jit(solution)/shard_map/ppermute | solution.py:46
  7.7 3.6 %collective-permute-start.3 = (bf16[2,192,128]{2,1,0:T(8,128)(2,1)S(1)}, bf16[2,192,128]{2,1,0:T(8,128)(2,1)S(1)}, u32[]{:S(2)}, u32[]{:S(2)}) collective-permute-start(bf16[2,192,128]{2,1,0:T(8,128)(2,1)S(1)} %pack.1.refs_0_), channel_id=1, source_target_pairs={{0,24},{8,16},{16,8},{24,0},{1,25},{9,17},{17,9},{25,1},{2,26},{10... | collective-permute-start | bytes 294920 | tf_op jit(solution)/shard_map/ppermute | solution.py:46
  11.3 0.8 %collective-permute-start.1 = (bf16[2,192,128]{2,1,0:T(8,128)(2,1)S(1)}, bf16[2,192,128]{2,1,0:T(8,128)(2,1)S(1)}, u32[]{:S(2)}, u32[]{:S(2)}) collective-permute-start(bf16[2,192,128]{2,1,0:T(8,128)(2,1)S(1)} %pack.1.refs_0_), channel_id=1, source_target_pairs={{0,8},{8,0},{16,24},{24,16},{1,9},{9,1},{17,25},{25,17},{2,10},{10... | collective-permute-start | bytes 294920 | tf_op jit(solution)/shard_map/ppermute | solution.py:46
  12.1 4.5 %prep.1 = (f32[192,4096]{1,0:T(8,128)}, bf16[2048,256]{1,0:T(8,128)(2,1)S(1)}, bf16[2048,256]{1,0:T(8,128)(2,1)S(1)}, f32[192,2048]{1,0:T(8,128)S(1)}, f32[1,2048]{1,0:T(1,128)S(1)}, /*index=5*/f32[1,128]{1,0:T(1,128)S(1)}) custom-call(f32[192,4096]{1,0:T(8,128)} %teacher_hbm.3, f32[192,4096]{1,0:T(8,128)} %student_hbm.3, f32[1,16384]{1,0:T(1,128)} %bitcast.9), custom_call_target="tpu_custom_call" | custom-call | flops 1 | bytes 1 | tf_op jit(solution)/shard_map/prep/pallas_call | solution.py:35
  16.6 1.6 %collective-permute-done.2.refs_2_ = bf16[2,192,128]{2,1,0:T(8,128)(2,1)S(1)} collective-permute-done((bf16[2,192,128]{2,1,0:T(8,128)(2,1)S(1)}, bf16[2,192,128]{2,1,0:T(8,128)(2,1)S(1)}, u32[]{:S(2)}, u32[]{:S(2)}) %collective-permute-start.2) | collective-permute-done | bytes 98336 | tf_op jit(solution)/shard_map/ppermute | solution.py:46
  19.9 1.3 %scores.4 = (bf16[2048,4096]{1,0:T(8,128)(2,1)S(1)}, bf16[512,192]{1,0:T(8,128)(2,1)S(1)}, f32[2,512]{1,0:T(2,128)S(1)}) custom-call(bf16[4,2,192,128]{3,2,1,0:T(8,128)(2,1)S(1)} %get-tuple-element.31.refs_0_, bf16[2048,256]{1,0:T(8,128)(2,1)S(1)} %get-tuple-element.32.refs_1_.refs_2_.refs_4_, ...), custom_call_target="tpu_custom_call" | custom-call | flops 1 | bytes 1 | tf_op jit(solution)/shard_map/scores/pallas_call | solution.py:35
  21.2 2.4 %rest.1 = (f32[192,4096]{1,0:T(8,128)}, f32[8,128]{1,0:T(8,128)S(1)}) custom-call(f32[192,4096]{1,0:T(8,128)} %teacher_hbm.3, f32[192,4096]{1,0:T(8,128)} %student_hbm.3, f32[2,512]{1,0:T(2,128)S(1)} %get-tuple-element.34.after.refs_0_, f32[192,4096]{1,0:T(8,128)} %get-tuple-element.35.before_hbm), custom_call_target="tpu_custom_call", output_to_operand_aliasing={{0}: (3, {})} | custom-call | flops 1 | bytes 1 | tf_op jit(solution)/shard_map/rest/pallas_call | solution.py:35
  23.6 1.3 %scores.5 = (bf16[2048,4096]{1,0:T(8,128)(2,1)S(1)}, bf16[512,192]{1,0:T(8,128)(2,1)S(1)}, f32[2,512]{1,0:T(2,128)S(1)}) custom-call(bf16[2,2,192,128]{3,2,1,0:T(8,128)(2,1)S(1)} %collective-permute-done.5.refs_0_, bf16[2,2,192,128]{3,2,1,0:T(8,128)(2,1)S(1)} %collective-permute-done.6.refs_1_, ...), custom_call_target="tpu_custom_call", output_to_operand_aliasing={{0}: (5, {})} | custom-call | flops 1 | bytes 1 | tf_op jit(solution)/shard_map/scores/pallas_call | solution.py:35
  25.1 1.3 %scores.6 = (bf16[2048,4096]{1,0:T(8,128)(2,1)S(1)}, bf16[512,192]{1,0:T(8,128)(2,1)S(1)}, f32[2,512]{1,0:T(2,128)S(1)}) custom-call(bf16[4,2,192,128]{3,2,1,0:T(8,128)(2,1)S(1)} %join.3.refs_0_, bf16[2048,256]{1,0:T(8,128)(2,1)S(1)} %get-tuple-element.32.refs_1_.refs_2_.refs_4_, ...), custom_call_target="tpu_custom_call", output_to_operand_aliasing={{0}: (4, {})} | custom-call | flops 1 | bytes 1 | tf_op jit(solution)/shard_map/scores/pallas_call | solution.py:35
  26.8 1.3 %scores.7 = (bf16[2048,4096]{1,0:T(8,128)(2,1)S(1)}, bf16[512,192]{1,0:T(8,128)(2,1)S(1)}, f32[4,1024]{1,0:T(4,128)S(1)}) custom-call(f32[2,512]{1,0:T(2,128)S(1)} %get-tuple-element.34.after.refs_0_, f32[2,512]{1,0:T(2,128)S(1)} %get-tuple-element.40.refs_3_.refs_1_, f32[2,512]{1,0:T(2,128)S(1)} %get-tuple-element.44.refs_2_, ...), custom_call_target="tpu_custom_call", output_to_operand_aliasing={{0}: (7, {})} | custom-call | flops 1 | bytes 1 | tf_op jit(solution)/shard_map/scores/pallas_call | solution.py:35
  28.3 1.0 %collective-permute-done.10.refs_1_ = f32[4,1024]{1,0:T(4,128)S(1)} collective-permute-done((f32[4,1024]{1,0:T(4,128)S(1)}, f32[4,1024]{1,0:T(4,128)S(1)}, u32[]{:S(2)}, u32[]{:S(2)}) %collective-permute-start.10) | collective-permute-done | bytes 16416 | tf_op jit(solution)/shard_map/ppermute | solution.py:46
  29.4 1.6 %collective-permute-start.11 = (f32[4,1024]{1,0:T(4,128)S(1)}, f32[4,1024]{1,0:T(4,128)S(1)}, u32[]{:S(2)}, u32[]{:S(2)}) collective-permute-start(f32[4,1024]{1,0:T(4,128)S(1)} %relay.3.refs_0_), channel_id=1, source_target_pairs={{0,1},{1,0},{2,7},{3,6},{4,5},{5,4},{6,3},{7,2},{8,9},{9,8},{10,15... | collective-permute-start | bytes 49160 | tf_op jit(solution)/shard_map/ppermute | solution.py:350
  31.0 1.5 %collective-permute-start.13 = (f32[4,1024]{1,0:T(4,128)S(1)}, f32[4,1024]{1,0:T(4,128)S(1)}, u32[]{:S(2)}, u32[]{:S(2)}) collective-permute-start(f32[4,1024]{1,0:T(4,128)S(1)} %relay.3.refs_0_), channel_id=1, source_target_pairs={{0,4},{1,5},{2,6},{3,7},{4,0},{5,1},{6,2},{7,3},{8,12},{9,13},{10,... | collective-permute-start | bytes 49160 | tf_op jit(solution)/shard_map/ppermute | solution.py:350
  32.5 0.7 %collective-permute-done.11.refs_1_ = f32[4,1024]{1,0:T(4,128)S(1)} collective-permute-done((f32[4,1024]{1,0:T(4,128)S(1)}, f32[4,1024]{1,0:T(4,128)S(1)}, u32[]{:S(2)}, u32[]{:S(2)}) %collective-permute-start.11) | collective-permute-done | bytes 16416 | tf_op jit(solution)/shard_map/ppermute | solution.py:350
  33.2 1.5 %collective-permute-done.13.refs_3_ = f32[4,1024]{1,0:T(4,128)S(1)} collective-permute-done((f32[4,1024]{1,0:T(4,128)S(1)}, f32[4,1024]{1,0:T(4,128)S(1)}, u32[]{:S(2)}, u32[]{:S(2)}) %collective-permute-start.13) | collective-permute-done | bytes 16416 | tf_op jit(solution)/shard_map/ppermute | solution.py:350
  34.8 1.7 %collective-permute-start.14 = (f32[4,1024]{1,0:T(4,128)S(1)}, f32[4,1024]{1,0:T(4,128)S(1)}, u32[]{:S(2)}, u32[]{:S(2)}) collective-permute-start(f32[4,1024]{1,0:T(4,128)S(1)} %relay.4.refs_0_), channel_id=1, source_target_pairs={{0,8},{2,26},{4,12},{6,30},{8,0},{10,18},{12,4},{14,22},{16,24},{1... | collective-permute-start | bytes 49160 | tf_op jit(solution)/shard_map/ppermute | solution.py:350
  36.5 1.0 %collective-permute-start.16 = (f32[4,1024]{1,0:T(4,128)S(1)}, f32[4,1024]{1,0:T(4,128)S(1)}, u32[]{:S(2)}, u32[]{:S(2)}) collective-permute-start(f32[4,1024]{1,0:T(4,128)S(1)} %relay.4.refs_0_), channel_id=1, source_target_pairs={{0,16},{2,18},{4,20},{6,22},{8,24},{10,26},{12,28},{14,30},{16,0},... | collective-permute-start | bytes 49160 | tf_op jit(solution)/shard_map/ppermute | solution.py:350
  37.5 1.1 %collective-permute-done.14.refs_1_ = f32[4,1024]{1,0:T(4,128)S(1)} collective-permute-done((f32[4,1024]{1,0:T(4,128)S(1)}, f32[4,1024]{1,0:T(4,128)S(1)}, u32[]{:S(2)}, u32[]{:S(2)}) %collective-permute-start.14) | collective-permute-done | bytes 16416 | tf_op jit(solution)/shard_map/ppermute | solution.py:350
  38.6 0.6 %collective-permute-start.15 = (f32[4,1024]{1,0:T(4,128)S(1)}, f32[4,1024]{1,0:T(4,128)S(1)}, u32[]{:S(2)}, u32[]{:S(2)}) collective-permute-start(f32[4,1024]{1,0:T(4,128)S(1)} %collective-permute-done.14.refs_1_), channel_id=1, source_target_pairs={{0,2},{2,0},{4,6},{6,4},{1,3},{3,1},{5,7},{7,5},{8,10},{10,8},{12,... | collective-permute-start | bytes 49160 | tf_op jit(solution)/shard_map/ppermute | solution.py:46
  39.2 1.9 %collective-permute-done.16.refs_3_ = f32[4,1024]{1,0:T(4,128)S(1)} collective-permute-done((f32[4,1024]{1,0:T(4,128)S(1)}, f32[4,1024]{1,0:T(4,128)S(1)}, u32[]{:S(2)}, u32[]{:S(2)}) %collective-permute-start.16) | collective-permute-done | bytes 16416 | tf_op jit(solution)/shard_map/ppermute | solution.py:350
  41.2 3.5 %gradient.1 = f32[192,2048]{1,0:T(8,128)} custom-call(f32[4,1024]{1,0:T(4,128)S(1)} %relay.5.total_ref, f32[1,128]{1,0:T(1,128)S(1)} %get-tuple-element.30.refs_5_.refs_3_.refs_4_.refs_6_.peak_ref, f32[192,2048]{1,0:T(8,128)S(1)} %get-tuple-element.47.weight_unit, f32[1,2048]{1,0:T(1,128)S(1)} %get-tuple-element.48.weight_scale, ...), custom_call_target="tpu_custom_call" | custom-call | flops 1 | bytes 1 | tf_op jit(solution)/shard_map/gradient/pallas_call | solution.py:35
  (24 shorter events, 2.7 us)
Async XLA Ops:
  0.6 4.8 %collective-permute-start = (s32[1,256]{1,0:T(1,128)}, s32[1,256]{1,0:T(1,128)S(1)}, u32[]{:S(2)}, u32[]{:S(2)}) collective-permute-start(s32[1,256]{1,0:T(1,128)} %param.10), channel_id=1, source_target_pairs={{0,1},{1,0},{2,3},{3,2},{4,5},{5,4},{6,7},{7,6},{8,9},{9,8},{10,11... | collective-permute-start | bytes 3080 | tf_op jit(solution)/shard_map/ppermute | solution.py:46
  5.6 11.0 %collective-permute-start.4 = (bf16[2,192,128]{2,1,0:T(8,128)(2,1)S(1)}, bf16[2,192,128]{2,1,0:T(8,128)(2,1)S(1)}, u32[]{:S(2)}, u32[]{:S(2)}) collective-permute-start(bf16[2,192,128]{2,1,0:T(8,128)(2,1)S(1)} %pack.1.refs_0_), channel_id=1, source_target_pairs={{0,1},{1,0},{2,3},{3,2},{4,5},{5,4},{6,7},{7,6},{8,9},{9,8},{10,11... | collective-permute-start | bytes 294920 | tf_op jit(solution)/shard_map/ppermute | solution.py:46
  7.7 8.9 %collective-permute-start.3 = (bf16[2,192,128]{2,1,0:T(8,128)(2,1)S(1)}, bf16[2,192,128]{2,1,0:T(8,128)(2,1)S(1)}, u32[]{:S(2)}, u32[]{:S(2)}) collective-permute-start(bf16[2,192,128]{2,1,0:T(8,128)(2,1)S(1)} %pack.1.refs_0_), channel_id=1, source_target_pairs={{0,24},{8,16},{16,8},{24,0},{1,25},{9,17},{17,9},{25,1},{2,26},{10... | collective-permute-start | bytes 294920 | tf_op jit(solution)/shard_map/ppermute | solution.py:46
  11.3 6.9 %collective-permute-start.2 = (bf16[2,192,128]{2,1,0:T(8,128)(2,1)S(1)}, bf16[2,192,128]{2,1,0:T(8,128)(2,1)S(1)}, u32[]{:S(2)}, u32[]{:S(2)}) collective-permute-start(bf16[2,192,128]{2,1,0:T(8,128)(2,1)S(1)} %pack.1.refs_0_), channel_id=1, source_target_pairs={{0,16},{8,24},{16,0},{24,8},{1,17},{9,25},{17,1},{25,9},{2,18},{10... | collective-permute-start | bytes 294920 | tf_op jit(solution)/shard_map/ppermute | solution.py:46
  11.3 6.9 %collective-permute-start.1 = (bf16[2,192,128]{2,1,0:T(8,128)(2,1)S(1)}, bf16[2,192,128]{2,1,0:T(8,128)(2,1)S(1)}, u32[]{:S(2)}, u32[]{:S(2)}) collective-permute-start(bf16[2,192,128]{2,1,0:T(8,128)(2,1)S(1)} %pack.1.refs_0_), channel_id=1, source_target_pairs={{0,8},{8,0},{16,24},{24,16},{1,9},{9,1},{17,25},{25,17},{2,10},{10... | collective-permute-start | bytes 294920 | tf_op jit(solution)/shard_map/ppermute | solution.py:46
  18.3 6.6 %collective-permute-start.8 = (bf16[2,2,208,128]{3,2,1,0:T(8,128)(2,1)S(1)}, bf16[2,2,208,128]{3,2,1,0:T(8,128)(2,1)S(1)}, u32[]{:S(2)}, u32[]{:S(2)}) collective-permute-start(bf16[2,2,208,128]{3,2,1,0:T(8,128)(2,1)S(1)} %get-tuple-element.41), channel_id=1, source_target_pairs={{0,1},{1,0},{2,3},{3,2},{4,5},{5,4},{6,7},{7,6},{8,9},{9,8},{10,11... | collective-permute-start | bytes 638984 | tf_op jit(solution)/shard_map/ppermute | solution.py:46
  18.9 4.7 %collective-permute-start.5 = (bf16[2,2,192,128]{3,2,1,0:T(8,128)(2,1)S(1)}, bf16[2,2,192,128]{3,2,1,0:T(8,128)(2,1)S(1)}, u32[]{:S(2)}, u32[]{:S(2)}) collective-permute-start(bf16[2,2,192,128]{3,2,1,0:T(8,128)(2,1)S(1)} %get-tuple-element.37), channel_id=1, source_target_pairs={{0,2},{2,0},{4,6},{6,4},{1,3},{3,1},{5,7},{7,5},{8,10},{10,8},{12,... | collective-permute-start | bytes 589832 | tf_op jit(solution)/shard_map/ppermute | solution.py:46
  18.9 4.7 %collective-permute-start.6 = (bf16[2,2,192,128]{3,2,1,0:T(8,128)(2,1)S(1)}, bf16[2,2,192,128]{3,2,1,0:T(8,128)(2,1)S(1)}, u32[]{:S(2)}, u32[]{:S(2)}) collective-permute-start(bf16[2,2,192,128]{3,2,1,0:T(8,128)(2,1)S(1)} %get-tuple-element.38), channel_id=1, source_target_pairs={{0,2},{2,0},{4,6},{6,4},{1,3},{3,1},{5,7},{7,5},{8,10},{10,8},{12,... | collective-permute-start | bytes 589832 | tf_op jit(solution)/shard_map/ppermute | solution.py:46
  19.4 5.5 %collective-permute-start.7 = (bf16[2,192,128]{2,1,0:T(8,128)(2,1)S(1)}, bf16[2,192,128]{2,1,0:T(8,128)(2,1)S(1)}, u32[]{:S(2)}, u32[]{:S(2)}) collective-permute-start(bf16[2,192,128]{2,1,0:T(8,128)(2,1)S(1)} %collective-permute-done.4.refs_4_.refs_0_), channel_id=1, source_target_pairs={{0,8},{8,0},{16,24},{24,16},{1,9},{9,1},{17,25},{25,17},{2,10},{10... | collective-permute-start | bytes 294920 | tf_op jit(solution)/shard_map/ppermute | solution.py:46
  25.0 1.8 %collective-permute-start.9 = (bf16[4,2,192,128]{3,2,1,0:T(8,128)(2,1)S(1)}, bf16[4,2,192,128]{3,2,1,0:T(8,128)(2,1)S(1)}, u32[]{:S(2)}, u32[]{:S(2)}) collective-permute-start(bf16[4,2,192,128]{3,2,1,0:T(8,128)(2,1)S(1)} %join.3.refs_0_), channel_id=1, source_target_pairs={{0,2},{2,0},{4,6},{6,4},{1,3},{3,1},{5,7},{7,5},{8,10},{10,8},{12,... | collective-permute-start | bytes 1179656 | tf_op jit(solution)/shard_map/ppermute | solution.py:46
  28.1 1.2 %collective-permute-start.10 = (f32[4,1024]{1,0:T(4,128)S(1)}, f32[4,1024]{1,0:T(4,128)S(1)}, u32[]{:S(2)}, u32[]{:S(2)}) collective-permute-start(f32[4,1024]{1,0:T(4,128)S(1)} %get-tuple-element.46.refs_0_), channel_id=1, source_target_pairs={{0,2},{2,0},{4,6},{6,4},{1,3},{3,1},{5,7},{7,5},{8,10},{10,8},{12,... | collective-permute-start | bytes 49160 | tf_op jit(solution)/shard_map/ppermute | solution.py:46
  29.4 3.8 %collective-permute-start.11 = (f32[4,1024]{1,0:T(4,128)S(1)}, f32[4,1024]{1,0:T(4,128)S(1)}, u32[]{:S(2)}, u32[]{:S(2)}) collective-permute-start(f32[4,1024]{1,0:T(4,128)S(1)} %relay.3.refs_0_), channel_id=1, source_target_pairs={{0,1},{1,0},{2,7},{3,6},{4,5},{5,4},{6,3},{7,2},{8,9},{9,8},{10,15... | collective-permute-start | bytes 49160 | tf_op jit(solution)/shard_map/ppermute | solution.py:350
  31.0 3.8 %collective-permute-start.13 = (f32[4,1024]{1,0:T(4,128)S(1)}, f32[4,1024]{1,0:T(4,128)S(1)}, u32[]{:S(2)}, u32[]{:S(2)}) collective-permute-start(f32[4,1024]{1,0:T(4,128)S(1)} %relay.3.refs_0_), channel_id=1, source_target_pairs={{0,4},{1,5},{2,6},{3,7},{4,0},{5,1},{6,2},{7,3},{8,12},{9,13},{10,... | collective-permute-start | bytes 49160 | tf_op jit(solution)/shard_map/ppermute | solution.py:350
  33.2 1.5 %collective-permute-start.12 = (f32[4,1024]{1,0:T(4,128)S(1)}, f32[4,1024]{1,0:T(4,128)S(1)}, u32[]{:S(2)}, u32[]{:S(2)}) collective-permute-start(f32[4,1024]{1,0:T(4,128)S(1)} %collective-permute-done.11.refs_1_), channel_id=1, source_target_pairs={{0,2},{2,0},{4,6},{6,4},{1,3},{3,1},{5,7},{7,5},{8,10},{10,8},{12,... | collective-permute-start | bytes 49160 | tf_op jit(solution)/shard_map/ppermute | solution.py:46
  34.8 3.8 %collective-permute-start.14 = (f32[4,1024]{1,0:T(4,128)S(1)}, f32[4,1024]{1,0:T(4,128)S(1)}, u32[]{:S(2)}, u32[]{:S(2)}) collective-permute-start(f32[4,1024]{1,0:T(4,128)S(1)} %relay.4.refs_0_), channel_id=1, source_target_pairs={{0,8},{2,26},{4,12},{6,30},{8,0},{10,18},{12,4},{14,22},{16,24},{1... | collective-permute-start | bytes 49160 | tf_op jit(solution)/shard_map/ppermute | solution.py:350
  36.5 4.7 %collective-permute-start.16 = (f32[4,1024]{1,0:T(4,128)S(1)}, f32[4,1024]{1,0:T(4,128)S(1)}, u32[]{:S(2)}, u32[]{:S(2)}) collective-permute-start(f32[4,1024]{1,0:T(4,128)S(1)} %relay.4.refs_0_), channel_id=1, source_target_pairs={{0,16},{2,18},{4,20},{6,22},{8,24},{10,26},{12,28},{14,30},{16,0},... | collective-permute-start | bytes 49160 | tf_op jit(solution)/shard_map/ppermute | solution.py:350
  38.6 2.5 %collective-permute-start.15 = (f32[4,1024]{1,0:T(4,128)S(1)}, f32[4,1024]{1,0:T(4,128)S(1)}, u32[]{:S(2)}, u32[]{:S(2)}) collective-permute-start(f32[4,1024]{1,0:T(4,128)S(1)} %collective-permute-done.14.refs_1_), channel_id=1, source_target_pairs={{0,2},{2,0},{4,6},{6,4},{1,3},{3,1},{5,7},{7,5},{8,10},{10,8},{12,... | collective-permute-start | bytes 49160 | tf_op jit(solution)/shard_map/ppermute | solution.py:46

commit v20 on v19

--- a/solution.py
+++ b/solution.py
@@ -332,11 +332,21 @@
     refs[-1][...] = jnp.concatenate(combine(parts), axis=0)
 
 
-def add_up(parts):
-    return call(functools.partial(relay_kernel, len(parts)), "relay", held(*parts[0].shape[-2:]), parts)
-
-
-def exchange(total, axes, first, second):
+def add_up(parts, after=()):
+    specs = [ON_CHIP] * len(parts) + [IN_HBM] * len(after)
+    out = held(*parts[0].shape[-2:])
+    return call(functools.partial(relay_kernel, len(parts)), "relay", out, (*parts, *after), in_specs=specs)
+
+
+def hold_kernel(in_ref, after, out_ref):
+    out_ref[...] = in_ref[...]
+
+
+def hold(array, after):
+    return call(hold_kernel, "hold", held(*array.shape), (array, after), in_specs=[ON_CHIP, IN_HBM])
+
+
+def exchange(total, axes, first, second, after=()):
     sizes = [lax.axis_size(axis) for axis in axes]
     proto = axes.index("proto")
     places = [(i, j) for i in range(sizes[0]) for j in range(sizes[1])]
@@ -350,7 +360,8 @@
         return lax.ppermute(total, axes, pairs)
 
     mine = permute(first)
-    return add_up([total, mine, swap(mine, "proto"), permute(second)])
+    passed = hold(mine, *after) if after else mine
+    return add_up([total, mine, swap(passed, "proto"), permute(second)])
 
 
 def across(total, up, over):
@@ -360,19 +371,22 @@
     return lax.ppermute(total, ("proto", "dp"), pairs)
 
 
-def add_up_all(total):
-    n_proto, n_dp, n_fsdp = [lax.axis_size(axis) for axis in ("proto", "dp", "fsdp")]
+def add_up_chip_and_across(total):
+    n_proto, n_dp = lax.axis_size("proto"), lax.axis_size("dp")
     total = add_up([total, swap(total, "proto")])
     if n_proto == 4 and n_dp == 2:
-        total = exchange(total, ("proto", "dp"), lambda odd: (2 * odd, 1), lambda odd: (2, 0))
-    else:
-        steps = [(up, over) for up in range(0, n_proto, 2) for over in range(n_dp)][1:]
-        total = add_up([total, *[across(total, *step) for step in steps]])
-    if n_fsdp == 4:
-        return exchange(total, ("fsdp", "proto"), lambda odd: (1 + 2 * odd, 0), lambda odd: (2, 0))
-    if n_fsdp <= DIRECT:
-        return add_up([total, *[swap(total, "fsdp", k) for k in range(1, n_fsdp)]])
-    return add_up([lax.all_to_all(jnp.broadcast_to(total[None], (n_fsdp, *total.shape)), "fsdp", 0, 0, tiled=True)])
+        return exchange(total, ("proto", "dp"), lambda odd: (2 * odd, 1), lambda odd: (2, 0))
+    steps = [(up, over) for up in range(0, n_proto, 2) for over in range(n_dp)][1:]
+    return add_up([total, *[across(total, *step) for step in steps]])
+
+
+def add_up_along(total, after):
+    n = lax.axis_size("fsdp")
+    if n == 4:
+        return exchange(total, ("fsdp", "proto"), lambda odd: (2 + odd, 0), lambda odd: (1, 0), after)
+    if n <= DIRECT:
+        return add_up([total, *[swap(total, "fsdp", k) for k in range(1, n)]], after)
+    return add_up([lax.all_to_all(jnp.broadcast_to(total[None], (n, *total.shape)), "fsdp", 0, 0, tiled=True)], after)
 
 
 def grad_kernel(total_ref, peak_ref, weight_unit, weight_scale, *refs):
@@ -467,11 +481,12 @@
         other, halves = [swap(own, "dp")], [own]
     exps, unit_a, total_a = scores(0, [own], weights)
     exps, unit_b, total_b = scores(1, [swap(half, "proto") for half in halves], weights, exps=exps)
-    teacher_new, done = update_rest(teacher_weight, student_weight, total_a, new, own_cols, 0, middle)
-    (other,) = join(other, [(0, n_fsdp, bot)], (total_b, done), bot)
+    (other,) = join(other, [(0, n_fsdp, bot)], (total_b,), bot)
     exps, unit_c, total_c = scores(2, [other], weights, exps=exps)
     exps, unit_d, total = scores(3, [swap(other, "proto")], weights, (total_a, total_b, total_c), exps)
-    total = add_up_all(total)
+    total = add_up_chip_and_across(total)
+    teacher_new, done = update_rest(teacher_weight, student_weight, total, new, own_cols, 0, middle)
+    total = add_up_along(total, (done,))
     units = (unit_a, unit_b, unit_c, unit_d)
     student_grad = gradient(total, peak, unit, scale, units, exps)
     return (teacher_new, student_grad)

time: 44.9 us -> 44.4 us (0.989)
  starting transfers between devices: 17.7 us -> 16.8 us
    ppermute x13, waiting for transfers between devices: 3.85 us -> 7.33 us  [swap(): lax.ppermute(block, axis, [(i, i ^ apart) for i in range(lax.axis_size(ax...]
    ppermute x4, waiting for transfers between devices: 5.31 us -> 2.27 us  [permute(): return lax.ppermute(total, axes, pairs)]
    ppermute x13, starting transfers between devices: 11.9 us -> 11.4 us  [swap(): lax.ppermute(block, axis, [(i, i ^ apart) for i in range(lax.axis_size(ax...]
    pallas_call x14 -> x15, Pallas kernels: 17.1 us -> 17.1 us  [call(): pl.pallas_call(kernel, out_shape=out_shape, compiler_params=pltpu.Compile...]
  transfers between devices with their start and end apart: 17 -> 17, of which waited for: 8 -> 10; matrix products, arithmetic and copies ran while one was open for 0% -> 0% of each run, Pallas kernels for 26% -> 27%
where the time goes in v20:
time: 44.4 us; the launch traced here: 44.2 us
  Pallas kernels  17.1 us (39%)
  starting transfers between devices  16.8 us (38%)
  waiting for transfers between devices  9.59 us (22%)
  between operations  0.79 us (2%)
    pallas_call x15, Pallas kernels, call(): pl.pallas_call(kernel, out_shape=out_shape, compiler_params=pltpu.Compile...  17.1 us
    ppermute x13, starting transfers between devices, swap(): lax.ppermute(block, axis, [(i, i ^ apart) for i in range(lax.axis_size(ax...  11.4 us
    ppermute x13, waiting for transfers between devices, swap(): lax.ppermute(block, axis, [(i, i ^ apart) for i in range(lax.axis_size(ax...  7.33 us
    ppermute x4, starting transfers between devices, permute(): return lax.ppermute(total, axes, pairs)  5.39 us
    ppermute x4, waiting for transfers between devices, permute(): return lax.ppermute(total, axes, pairs)  2.27 us
  transfers between devices with their start and end apart: 17, of which 10 were waited for; matrix products, arithmetic and copies ran while one was open for 0% of the time, Pallas kernels for 27%

profile of v20, /device:TPU:0, one launch (start us, length us, event | category | flops | bytes accessed | tf_op | source)
XLA Modules:
  0.0 44.2 jit_solution(10632860542651576123)
XLA Ops:
  0.6 3.0 %collective-permute-start = (s32[1,256]{1,0:T(1,128)}, s32[1,256]{1,0:T(1,128)S(1)}, u32[]{:S(2)}, u32[]{:S(2)}) collective-permute-start(s32[1,256]{1,0:T(1,128)} %param.10), channel_id=1, source_target_pairs={{0,1},{1,0},{2,3},{3,2},{4,5},{5,4},{6,7},{7,6},{8,9},{9,8},{10,11... | collective-permute-start | bytes 3080 | tf_op jit(solution)/shard_map/ppermute | solution.py:46
  3.6 0.9 %fetch.1 = (bf16[192,128]{1,0:T(8,128)(2,1)S(1)}, bf16[192,256]{1,0:T(8,128)(2,1)S(1)}) custom-call(bf16[192,256]{1,0:T(8,128)(2,1)} %bitcast.7, bf16[192,256]{1,0:T(8,128)(2,1)} %bitcast.8), custom_call_target="tpu_custom_call" | custom-call | flops 1 | bytes 1 | tf_op jit(solution)/shard_map/fetch/pallas_call | solution.py:35
  4.6 0.8 %collective-permute-done.index_ref = s32[1,256]{1,0:T(1,128)S(1)} collective-permute-done((s32[1,256]{1,0:T(1,128)}, s32[1,256]{1,0:T(1,128)S(1)}, u32[]{:S(2)}, u32[]{:S(2)}) %collective-permute-start) | collective-permute-done | bytes 1056 | tf_op jit(solution)/shard_map/ppermute | solution.py:46
  5.6 2.1 %collective-permute-start.4 = (bf16[2,192,128]{2,1,0:T(8,128)(2,1)S(1)}, bf16[2,192,128]{2,1,0:T(8,128)(2,1)S(1)}, u32[]{:S(2)}, u32[]{:S(2)}) collective-permute-start(bf16[2,192,128]{2,1,0:T(8,128)(2,1)S(1)} %pack.1.refs_0_), channel_id=1, source_target_pairs={{0,1},{1,0},{2,3},{3,2},{4,5},{5,4},{6,7},{7,6},{8,9},{9,8},{10,11... | collective-permute-start | bytes 294920 | tf_op jit(solution)/shard_map/ppermute | solution.py:46
  7.7 3.6 %collective-permute-start.3 = (bf16[2,192,128]{2,1,0:T(8,128)(2,1)S(1)}, bf16[2,192,128]{2,1,0:T(8,128)(2,1)S(1)}, u32[]{:S(2)}, u32[]{:S(2)}) collective-permute-start(bf16[2,192,128]{2,1,0:T(8,128)(2,1)S(1)} %pack.1.refs_0_), channel_id=1, source_target_pairs={{0,24},{8,16},{16,8},{24,0},{1,25},{9,17},{17,9},{25,1},{2,26},{10... | collective-permute-start | bytes 294920 | tf_op jit(solution)/shard_map/ppermute | solution.py:46
  11.3 0.8 %collective-permute-start.1 = (bf16[2,192,128]{2,1,0:T(8,128)(2,1)S(1)}, bf16[2,192,128]{2,1,0:T(8,128)(2,1)S(1)}, u32[]{:S(2)}, u32[]{:S(2)}) collective-permute-start(bf16[2,192,128]{2,1,0:T(8,128)(2,1)S(1)} %pack.1.refs_0_), channel_id=1, source_target_pairs={{0,8},{8,0},{16,24},{24,16},{1,9},{9,1},{17,25},{25,17},{2,10},{10... | collective-permute-start | bytes 294920 | tf_op jit(solution)/shard_map/ppermute | solution.py:46
  12.1 4.5 %prep.1 = (f32[192,4096]{1,0:T(8,128)}, bf16[2048,256]{1,0:T(8,128)(2,1)S(1)}, bf16[2048,256]{1,0:T(8,128)(2,1)S(1)}, f32[192,2048]{1,0:T(8,128)S(1)}, f32[1,2048]{1,0:T(1,128)S(1)}, /*index=5*/f32[1,128]{1,0:T(1,128)S(1)}) custom-call(f32[192,4096]{1,0:T(8,128)} %teacher_hbm.3, f32[192,4096]{1,0:T(8,128)} %student_hbm.3, f32[1,16384]{1,0:T(1,128)} %bitcast.9), custom_call_target="tpu_custom_call" | custom-call | flops 1 | bytes 1 | tf_op jit(solution)/shard_map/prep/pallas_call | solution.py:35
  16.6 1.6 %collective-permute-done.2.refs_2_ = bf16[2,192,128]{2,1,0:T(8,128)(2,1)S(1)} collective-permute-done((bf16[2,192,128]{2,1,0:T(8,128)(2,1)S(1)}, bf16[2,192,128]{2,1,0:T(8,128)(2,1)S(1)}, u32[]{:S(2)}, u32[]{:S(2)}) %collective-permute-start.2) | collective-permute-done | bytes 98336 | tf_op jit(solution)/shard_map/ppermute | solution.py:46
  18.3 0.6 %collective-permute-start.8 = (bf16[2,2,208,128]{3,2,1,0:T(8,128)(2,1)S(1)}, bf16[2,2,208,128]{3,2,1,0:T(8,128)(2,1)S(1)}, u32[]{:S(2)}, u32[]{:S(2)}) collective-permute-start(bf16[2,2,208,128]{3,2,1,0:T(8,128)(2,1)S(1)} %get-tuple-element.39), channel_id=1, source_target_pairs={{0,1},{1,0},{2,3},{3,2},{4,5},{5,4},{6,7},{7,6},{8,9},{9,8},{10,11... | collective-permute-start | bytes 638984 | tf_op jit(solution)/shard_map/ppermute | solution.py:46
  19.9 1.3 %scores.4 = (bf16[2048,4096]{1,0:T(8,128)(2,1)S(1)}, bf16[512,192]{1,0:T(8,128)(2,1)S(1)}, f32[2,512]{1,0:T(2,128)S(1)}) custom-call(bf16[4,2,192,128]{3,2,1,0:T(8,128)(2,1)S(1)} %get-tuple-element.31.refs_0_, bf16[2048,256]{1,0:T(8,128)(2,1)S(1)} %get-tuple-element.32.refs_1_.refs_2_.refs_4_, ...), custom_call_target="tpu_custom_call" | custom-call | flops 1 | bytes 1 | tf_op jit(solution)/shard_map/scores/pallas_call | solution.py:35
  21.2 1.3 %scores.5 = (bf16[2048,4096]{1,0:T(8,128)(2,1)S(1)}, bf16[512,192]{1,0:T(8,128)(2,1)S(1)}, f32[2,512]{1,0:T(2,128)S(1)}) custom-call(bf16[2,2,192,128]{3,2,1,0:T(8,128)(2,1)S(1)} %collective-permute-done.5.refs_0_, bf16[2,2,192,128]{3,2,1,0:T(8,128)(2,1)S(1)} %collective-permute-done.6.refs_1_, ...), custom_call_target="tpu_custom_call", output_to_operand_aliasing={{0}: (5, {})} | custom-call | flops 1 | bytes 1 | tf_op jit(solution)/shard_map/scores/pallas_call | solution.py:35
  22.5 1.6 %collective-permute-done.7.refs_1_ = bf16[2,192,128]{2,1,0:T(8,128)(2,1)S(1)} collective-permute-done((bf16[2,192,128]{2,1,0:T(8,128)(2,1)S(1)}, bf16[2,192,128]{2,1,0:T(8,128)(2,1)S(1)}, u32[]{:S(2)}, u32[]{:S(2)}) %collective-permute-start.7) | collective-permute-done | bytes 98336 | tf_op jit(solution)/shard_map/ppermute | solution.py:46
  24.8 1.3 %scores.6 = (bf16[2048,4096]{1,0:T(8,128)(2,1)S(1)}, bf16[512,192]{1,0:T(8,128)(2,1)S(1)}, f32[2,512]{1,0:T(2,128)S(1)}) custom-call(bf16[4,2,192,128]{3,2,1,0:T(8,128)(2,1)S(1)} %join.3.refs_0_, bf16[2048,256]{1,0:T(8,128)(2,1)S(1)} %get-tuple-element.32.refs_1_.refs_2_.refs_4_, ...), custom_call_target="tpu_custom_call", output_to_operand_aliasing={{0}: (4, {})} | custom-call | flops 1 | bytes 1 | tf_op jit(solution)/shard_map/scores/pallas_call | solution.py:35
  26.5 1.3 %scores.7 = (bf16[2048,4096]{1,0:T(8,128)(2,1)S(1)}, bf16[512,192]{1,0:T(8,128)(2,1)S(1)}, f32[4,1024]{1,0:T(4,128)S(1)}) custom-call(f32[2,512]{1,0:T(2,128)S(1)} %get-tuple-element.34.refs_0_, f32[2,512]{1,0:T(2,128)S(1)} %get-tuple-element.38.refs_3_.refs_1_, f32[2,512]{1,0:T(2,128)S(1)} %get-tuple-element.41.refs_2_, ...), custom_call_target="tpu_custom_call", output_to_operand_aliasing={{0}: (7, {})} | custom-call | flops 1 | bytes 1 | tf_op jit(solution)/shard_map/scores/pallas_call | solution.py:35
  28.0 1.0 %collective-permute-done.10.refs_1_ = f32[4,1024]{1,0:T(4,128)S(1)} collective-permute-done((f32[4,1024]{1,0:T(4,128)S(1)}, f32[4,1024]{1,0:T(4,128)S(1)}, u32[]{:S(2)}, u32[]{:S(2)}) %collective-permute-start.10) | collective-permute-done | bytes 16416 | tf_op jit(solution)/shard_map/ppermute | solution.py:46
  29.1 1.0 %collective-permute-start.11 = (f32[4,1024]{1,0:T(4,128)S(1)}, f32[4,1024]{1,0:T(4,128)S(1)}, u32[]{:S(2)}, u32[]{:S(2)}) collective-permute-start(f32[4,1024]{1,0:T(4,128)S(1)} %relay.3.refs_0_), channel_id=1, source_target_pairs={{0,1},{1,0},{2,7},{3,6},{4,5},{5,4},{6,3},{7,2},{8,9},{9,8},{10,15... | collective-permute-start | bytes 49160 | tf_op jit(solution)/shard_map/ppermute | solution.py:360
  30.1 1.5 %collective-permute-start.13 = (f32[4,1024]{1,0:T(4,128)S(1)}, f32[4,1024]{1,0:T(4,128)S(1)}, u32[]{:S(2)}, u32[]{:S(2)}) collective-permute-start(f32[4,1024]{1,0:T(4,128)S(1)} %relay.3.refs_0_), channel_id=1, source_target_pairs={{0,4},{1,5},{2,6},{3,7},{4,0},{5,1},{6,2},{7,3},{8,12},{9,13},{10,... | collective-permute-start | bytes 49160 | tf_op jit(solution)/shard_map/ppermute | solution.py:360
  31.7 1.3 %collective-permute-done.11.refs_1_ = f32[4,1024]{1,0:T(4,128)S(1)} collective-permute-done((f32[4,1024]{1,0:T(4,128)S(1)}, f32[4,1024]{1,0:T(4,128)S(1)}, u32[]{:S(2)}, u32[]{:S(2)}) %collective-permute-start.11) | collective-permute-done | bytes 16416 | tf_op jit(solution)/shard_map/ppermute | solution.py:360
  32.9 1.0 %collective-permute-done.13.refs_3_ = f32[4,1024]{1,0:T(4,128)S(1)} collective-permute-done((f32[4,1024]{1,0:T(4,128)S(1)}, f32[4,1024]{1,0:T(4,128)S(1)}, u32[]{:S(2)}, u32[]{:S(2)}) %collective-permute-start.13) | collective-permute-done | bytes 16416 | tf_op jit(solution)/shard_map/ppermute | solution.py:360
  34.1 1.1 %collective-permute-start.14 = (f32[4,1024]{1,0:T(4,128)S(1)}, f32[4,1024]{1,0:T(4,128)S(1)}, u32[]{:S(2)}, u32[]{:S(2)}) collective-permute-start(f32[4,1024]{1,0:T(4,128)S(1)} %relay.4.after.refs_0_), channel_id=1, source_target_pairs={{0,16},{2,26},{4,20},{6,30},{8,24},{10,18},{12,28},{14,22},{16,0},... | collective-permute-start | bytes 49160 | tf_op jit(solution)/shard_map/ppermute | solution.py:360
  35.2 1.7 %collective-permute-start.16 = (f32[4,1024]{1,0:T(4,128)S(1)}, f32[4,1024]{1,0:T(4,128)S(1)}, u32[]{:S(2)}, u32[]{:S(2)}) collective-permute-start(f32[4,1024]{1,0:T(4,128)S(1)} %relay.4.after.refs_0_), channel_id=1, source_target_pairs={{0,8},{2,10},{4,12},{6,14},{8,0},{10,2},{12,4},{14,6},{16,24},{18,... | collective-permute-start | bytes 49160 | tf_op jit(solution)/shard_map/ppermute | solution.py:360
  37.0 2.4 %rest.1 = (f32[192,4096]{1,0:T(8,128)}, f32[8,128]{1,0:T(8,128)S(1)}) custom-call(f32[192,4096]{1,0:T(8,128)} %teacher_hbm.3, f32[192,4096]{1,0:T(8,128)} %student_hbm.3, f32[4,1024]{1,0:T(4,128)S(1)} %relay.4.after.refs_0_, f32[192,4096]{1,0:T(8,128)} %get-tuple-element.44.before_hbm), custom_call_target="tpu_custom_call", output_to_operand_aliasing={{0}: (3, {})} | custom-call | flops 1 | bytes 1 | tf_op jit(solution)/shard_map/rest/pallas_call | solution.py:35
  39.5 1.2 %collective-permute-done.15.refs_2_ = f32[4,1024]{1,0:T(4,128)S(1)} collective-permute-done((f32[4,1024]{1,0:T(4,128)S(1)}, f32[4,1024]{1,0:T(4,128)S(1)}, u32[]{:S(2)}, u32[]{:S(2)}) %collective-permute-start.15) | collective-permute-done | bytes 16416 | tf_op jit(solution)/shard_map/ppermute | solution.py:46
  40.7 3.5 %gradient.1 = f32[192,2048]{1,0:T(8,128)} custom-call(f32[4,1024]{1,0:T(4,128)S(1)} %relay.5.total_ref, f32[1,128]{1,0:T(1,128)S(1)} %get-tuple-element.30.refs_5_.refs_3_.refs_4_.refs_6_.peak_ref, f32[192,2048]{1,0:T(8,128)S(1)} %get-tuple-element.47.weight_unit, f32[1,2048]{1,0:T(1,128)S(1)} %get-tuple-element.48.weight_scale, ...), custom_call_target="tpu_custom_call" | custom-call | flops 1 | bytes 1 | tf_op jit(solution)/shard_map/gradient/pallas_call | solution.py:35
  (25 shorter events, 2.8 us)
Async XLA Ops:
  0.6 4.8 %collective-permute-start = (s32[1,256]{1,0:T(1,128)}, s32[1,256]{1,0:T(1,128)S(1)}, u32[]{:S(2)}, u32[]{:S(2)}) collective-permute-start(s32[1,256]{1,0:T(1,128)} %param.10), channel_id=1, source_target_pairs={{0,1},{1,0},{2,3},{3,2},{4,5},{5,4},{6,7},{7,6},{8,9},{9,8},{10,11... | collective-permute-start | bytes 3080 | tf_op jit(solution)/shard_map/ppermute | solution.py:46
  5.6 11.0 %collective-permute-start.4 = (bf16[2,192,128]{2,1,0:T(8,128)(2,1)S(1)}, bf16[2,192,128]{2,1,0:T(8,128)(2,1)S(1)}, u32[]{:S(2)}, u32[]{:S(2)}) collective-permute-start(bf16[2,192,128]{2,1,0:T(8,128)(2,1)S(1)} %pack.1.refs_0_), channel_id=1, source_target_pairs={{0,1},{1,0},{2,3},{3,2},{4,5},{5,4},{6,7},{7,6},{8,9},{9,8},{10,11... | collective-permute-start | bytes 294920 | tf_op jit(solution)/shard_map/ppermute | solution.py:46
  7.7 8.9 %collective-permute-start.3 = (bf16[2,192,128]{2,1,0:T(8,128)(2,1)S(1)}, bf16[2,192,128]{2,1,0:T(8,128)(2,1)S(1)}, u32[]{:S(2)}, u32[]{:S(2)}) collective-permute-start(bf16[2,192,128]{2,1,0:T(8,128)(2,1)S(1)} %pack.1.refs_0_), channel_id=1, source_target_pairs={{0,24},{8,16},{16,8},{24,0},{1,25},{9,17},{17,9},{25,1},{2,26},{10... | collective-permute-start | bytes 294920 | tf_op jit(solution)/shard_map/ppermute | solution.py:46
  11.3 6.9 %collective-permute-start.2 = (bf16[2,192,128]{2,1,0:T(8,128)(2,1)S(1)}, bf16[2,192,128]{2,1,0:T(8,128)(2,1)S(1)}, u32[]{:S(2)}, u32[]{:S(2)}) collective-permute-start(bf16[2,192,128]{2,1,0:T(8,128)(2,1)S(1)} %pack.1.refs_0_), channel_id=1, source_target_pairs={{0,16},{8,24},{16,0},{24,8},{1,17},{9,25},{17,1},{25,9},{2,18},{10... | collective-permute-start | bytes 294920 | tf_op jit(solution)/shard_map/ppermute | solution.py:46
  11.3 6.9 %collective-permute-start.1 = (bf16[2,192,128]{2,1,0:T(8,128)(2,1)S(1)}, bf16[2,192,128]{2,1,0:T(8,128)(2,1)S(1)}, u32[]{:S(2)}, u32[]{:S(2)}) collective-permute-start(bf16[2,192,128]{2,1,0:T(8,128)(2,1)S(1)} %pack.1.refs_0_), channel_id=1, source_target_pairs={{0,8},{8,0},{16,24},{24,16},{1,9},{9,1},{17,25},{25,17},{2,10},{10... | collective-permute-start | bytes 294920 | tf_op jit(solution)/shard_map/ppermute | solution.py:46
  18.3 6.3 %collective-permute-start.8 = (bf16[2,2,208,128]{3,2,1,0:T(8,128)(2,1)S(1)}, bf16[2,2,208,128]{3,2,1,0:T(8,128)(2,1)S(1)}, u32[]{:S(2)}, u32[]{:S(2)}) collective-permute-start(bf16[2,2,208,128]{3,2,1,0:T(8,128)(2,1)S(1)} %get-tuple-element.39), channel_id=1, source_target_pairs={{0,1},{1,0},{2,3},{3,2},{4,5},{5,4},{6,7},{7,6},{8,9},{9,8},{10,11... | collective-permute-start | bytes 638984 | tf_op jit(solution)/shard_map/ppermute | solution.py:46
  18.9 2.3 %collective-permute-start.5 = (bf16[2,2,192,128]{3,2,1,0:T(8,128)(2,1)S(1)}, bf16[2,2,192,128]{3,2,1,0:T(8,128)(2,1)S(1)}, u32[]{:S(2)}, u32[]{:S(2)}) collective-permute-start(bf16[2,2,192,128]{3,2,1,0:T(8,128)(2,1)S(1)} %get-tuple-element.35), channel_id=1, source_target_pairs={{0,2},{2,0},{4,6},{6,4},{1,3},{3,1},{5,7},{7,5},{8,10},{10,8},{12,... | collective-permute-start | bytes 589832 | tf_op jit(solution)/shard_map/ppermute | solution.py:46
  18.9 2.3 %collective-permute-start.6 = (bf16[2,2,192,128]{3,2,1,0:T(8,128)(2,1)S(1)}, bf16[2,2,192,128]{3,2,1,0:T(8,128)(2,1)S(1)}, u32[]{:S(2)}, u32[]{:S(2)}) collective-permute-start(bf16[2,2,192,128]{3,2,1,0:T(8,128)(2,1)S(1)} %get-tuple-element.36), channel_id=1, source_target_pairs={{0,2},{2,0},{4,6},{6,4},{1,3},{3,1},{5,7},{7,5},{8,10},{10,8},{12,... | collective-permute-start | bytes 589832 | tf_op jit(solution)/shard_map/ppermute | solution.py:46
  19.4 4.7 %collective-permute-start.7 = (bf16[2,192,128]{2,1,0:T(8,128)(2,1)S(1)}, bf16[2,192,128]{2,1,0:T(8,128)(2,1)S(1)}, u32[]{:S(2)}, u32[]{:S(2)}) collective-permute-start(bf16[2,192,128]{2,1,0:T(8,128)(2,1)S(1)} %collective-permute-done.4.refs_4_.refs_0_), channel_id=1, source_target_pairs={{0,8},{8,0},{16,24},{24,16},{1,9},{9,1},{17,25},{25,17},{2,10},{10... | collective-permute-start | bytes 294920 | tf_op jit(solution)/shard_map/ppermute | solution.py:46
  24.7 1.8 %collective-permute-start.9 = (bf16[4,2,192,128]{3,2,1,0:T(8,128)(2,1)S(1)}, bf16[4,2,192,128]{3,2,1,0:T(8,128)(2,1)S(1)}, u32[]{:S(2)}, u32[]{:S(2)}) collective-permute-start(bf16[4,2,192,128]{3,2,1,0:T(8,128)(2,1)S(1)} %join.3.refs_0_), channel_id=1, source_target_pairs={{0,2},{2,0},{4,6},{6,4},{1,3},{3,1},{5,7},{7,5},{8,10},{10,8},{12,... | collective-permute-start | bytes 1179656 | tf_op jit(solution)/shard_map/ppermute | solution.py:46
  27.8 1.2 %collective-permute-start.10 = (f32[4,1024]{1,0:T(4,128)S(1)}, f32[4,1024]{1,0:T(4,128)S(1)}, u32[]{:S(2)}, u32[]{:S(2)}) collective-permute-start(f32[4,1024]{1,0:T(4,128)S(1)} %get-tuple-element.43.refs_0_), channel_id=1, source_target_pairs={{0,2},{2,0},{4,6},{6,4},{1,3},{3,1},{5,7},{7,5},{8,10},{10,8},{12,... | collective-permute-start | bytes 49160 | tf_op jit(solution)/shard_map/ppermute | solution.py:46
  29.1 3.8 %collective-permute-start.11 = (f32[4,1024]{1,0:T(4,128)S(1)}, f32[4,1024]{1,0:T(4,128)S(1)}, u32[]{:S(2)}, u32[]{:S(2)}) collective-permute-start(f32[4,1024]{1,0:T(4,128)S(1)} %relay.3.refs_0_), channel_id=1, source_target_pairs={{0,1},{1,0},{2,7},{3,6},{4,5},{5,4},{6,3},{7,2},{8,9},{9,8},{10,15... | collective-permute-start | bytes 49160 | tf_op jit(solution)/shard_map/ppermute | solution.py:360
  30.1 3.8 %collective-permute-start.13 = (f32[4,1024]{1,0:T(4,128)S(1)}, f32[4,1024]{1,0:T(4,128)S(1)}, u32[]{:S(2)}, u32[]{:S(2)}) collective-permute-start(f32[4,1024]{1,0:T(4,128)S(1)} %relay.3.refs_0_), channel_id=1, source_target_pairs={{0,4},{1,5},{2,6},{3,7},{4,0},{5,1},{6,2},{7,3},{8,12},{9,13},{10,... | collective-permute-start | bytes 49160 | tf_op jit(solution)/shard_map/ppermute | solution.py:360
  32.9 1.2 %collective-permute-start.12 = (f32[4,1024]{1,0:T(4,128)S(1)}, f32[4,1024]{1,0:T(4,128)S(1)}, u32[]{:S(2)}, u32[]{:S(2)}) collective-permute-start(f32[4,1024]{1,0:T(4,128)S(1)} %collective-permute-done.11.refs_1_), channel_id=1, source_target_pairs={{0,2},{2,0},{4,6},{6,4},{1,3},{3,1},{5,7},{7,5},{8,10},{10,8},{12,... | collective-permute-start | bytes 49160 | tf_op jit(solution)/shard_map/ppermute | solution.py:46
  34.1 5.2 %collective-permute-start.14 = (f32[4,1024]{1,0:T(4,128)S(1)}, f32[4,1024]{1,0:T(4,128)S(1)}, u32[]{:S(2)}, u32[]{:S(2)}) collective-permute-start(f32[4,1024]{1,0:T(4,128)S(1)} %relay.4.after.refs_0_), channel_id=1, source_target_pairs={{0,16},{2,26},{4,20},{6,30},{8,24},{10,18},{12,28},{14,22},{16,0},... | collective-permute-start | bytes 49160 | tf_op jit(solution)/shard_map/ppermute | solution.py:360
  35.2 4.3 %collective-permute-start.16 = (f32[4,1024]{1,0:T(4,128)S(1)}, f32[4,1024]{1,0:T(4,128)S(1)}, u32[]{:S(2)}, u32[]{:S(2)}) collective-permute-start(f32[4,1024]{1,0:T(4,128)S(1)} %relay.4.after.refs_0_), channel_id=1, source_target_pairs={{0,8},{2,10},{4,12},{6,14},{8,0},{10,2},{12,4},{14,6},{16,24},{18,... | collective-permute-start | bytes 49160 | tf_op jit(solution)/shard_map/ppermute | solution.py:360
  39.4 1.2 %collective-permute-start.15 = (f32[4,1024]{1,0:T(4,128)S(1)}, f32[4,1024]{1,0:T(4,128)S(1)}, u32[]{:S(2)}, u32[]{:S(2)}) collective-permute-start(f32[4,1024]{1,0:T(4,128)S(1)} %hold.1), channel_id=1, source_target_pairs={{0,2},{2,0},{4,6},{6,4},{1,3},{3,1},{5,7},{7,5},{8,10},{10,8},{12,... | collective-permute-start | bytes 49160 | tf_op jit(solution)/shard_map/ppermute | solution.py:46

commit v21 on v20

--- a/solution.py
+++ b/solution.py
@@ -56,15 +56,15 @@
     return high, mid, row - high - mid
 
 
-def prep_kernel(n_dp, n_own, teacher_hbm, student_hbm, center_hbm, new_hbm, wt_ref, ws_ref, unit_ref, scale_ref, peak_ref, *scratch):
+def prep_kernel(n_dp, teacher_hbm, student_hbm, center_hbm, new_hbm, wt_ref, ws_ref, unit_ref, scale_ref, peak_ref, *scratch):
     teacher_buf, student_buf, new_buf, center_buf, in_t, in_s, out, in_c = scratch
     chunks, bot, width = new_buf.shape
+    n_own = chunks // n_dp
     dp, fsdp, _ = here()
+    order = [*range(n_own - 1), *range(n_own, chunks), n_own - 1]
     own = n_own * width
     at = [slice(i * width, (i + 1) * width) for i in range(n_own)]
-    firsts = [dp * own + i * width for i in range(n_own)]
-    more = (chunks - n_own) // (n_dp - 1) if n_dp > 1 else 0
-    firsts += [lax.rem(dp + 1 + i // more, n_dp) * own + (n_own - more + i % more) * width for i in range(chunks - n_own)]
+    firsts = [lax.rem(dp + i // n_own, n_dp) * own + i % n_own * width for i in range(chunks)]
     far = [pl.ds(pl.multiple_of(first, width), width) for first in firsts]
     start = pl.multiple_of((fsdp * n_dp + dp) * own, 128)
     center_load = pltpu.make_async_copy(center_hbm.at[:, pl.ds(start, own)], center_buf, in_c)
@@ -77,8 +77,8 @@
     ]
     stores = [pltpu.make_async_copy(new_buf.at[i], new_hbm.at[:, far[i]], out.at[i]) for i in range(chunks)]
     center_load.start()
-    for pair in loads:
-        for load in pair:
+    for i in order:
+        for load in loads[i]:
             load.start()
     center_load.wait()
     center = center_buf[...]
@@ -87,7 +87,7 @@
     splits = cast_split(-center - peak)
     row = lax.broadcasted_iota(jnp.int32, (DEPTH - bot, width), 0)
     zero = jnp.zeros((DEPTH - bot, width), jnp.float32)
-    for i in range(chunks):
+    for i in order:
         for load in loads[i]:
             load.wait()
         student = student_buf[i]
@@ -109,14 +109,13 @@
         store.wait()
 
 
-def prepare(teacher_weight, student_weight, center, n_dp, more):
+def prepare(teacher_weight, student_weight, center, n_dp):
     bot, cols = teacher_weight.shape
     own = cols // n_dp
-    width = math.gcd(min(512, own), more)
-    n_own = own // width
-    chunks = n_own + (n_dp - 1) * (more // width)
+    width = min(512, own)
+    chunks = cols // width
     return call(
-        functools.partial(prep_kernel, n_dp, n_own),
+        functools.partial(prep_kernel, n_dp),
         "prep",
         [
             pltpu.HBM((bot, cols), jnp.float32),
@@ -133,48 +132,6 @@
         + [held(1, own)]
         + [pltpu.SemaphoreType.DMA((chunks,))] * 3
         + [pltpu.SemaphoreType.DMA],
-    )
-
-
-def rest_kernel(lo, hi, own, teacher_hbm, student_hbm, after, before_hbm, new_hbm, done_ref, *scratch):
-    teacher_buf, student_buf, new_buf, in_t, in_s, out = scratch
-    width = hi - lo
-    parts = teacher_hbm.shape[1] // own - 1
-    dp = here()[0]
-    done_ref[...] = jnp.zeros_like(done_ref)
-    far = [pl.ds(pl.multiple_of(lax.rem(dp + 1 + i, parts + 1) * own + lo, 128), width) for i in range(parts)]
-    loads = [
-        (
-            pltpu.make_async_copy(teacher_hbm.at[:, far[i]], teacher_buf.at[i], in_t.at[i]),
-            pltpu.make_async_copy(student_hbm.at[:, far[i]], student_buf.at[i], in_s.at[i]),
-        )
-        for i in range(parts)
-    ]
-    stores = [pltpu.make_async_copy(new_buf.at[i], new_hbm.at[:, far[i]], out.at[i]) for i in range(parts)]
-    for pair in loads:
-        for load in pair:
-            load.start()
-    for i in range(parts):
-        for load in loads[i]:
-            load.wait()
-        new_buf[i] = 0.994 * teacher_buf[i] + 0.006 * student_buf[i]
-        stores[i].start()
-    for store in stores:
-        store.wait()
-
-
-def update_rest(teacher_weight, student_weight, after, new, own, lo, hi):
-    bot, cols = teacher_weight.shape
-    parts = cols // own - 1
-    return call(
-        functools.partial(rest_kernel, lo, hi, own),
-        "rest",
-        [pltpu.HBM((bot, cols), jnp.float32), held(8, 128)],
-        (teacher_weight, student_weight, after, new),
-        in_specs=[IN_HBM] * 4,
-        out_specs=[IN_HBM, ON_CHIP],
-        input_output_aliases={3: 0},
-        scratch_shapes=[held(parts, bot, hi - lo)] * 3 + [pltpu.SemaphoreType.DMA((parts,))] * 3,
     )
 
 
@@ -332,21 +289,11 @@
     refs[-1][...] = jnp.concatenate(combine(parts), axis=0)
 
 
-def add_up(parts, after=()):
-    specs = [ON_CHIP] * len(parts) + [IN_HBM] * len(after)
-    out = held(*parts[0].shape[-2:])
-    return call(functools.partial(relay_kernel, len(parts)), "relay", out, (*parts, *after), in_specs=specs)
-
-
-def hold_kernel(in_ref, after, out_ref):
-    out_ref[...] = in_ref[...]
-
-
-def hold(array, after):
-    return call(hold_kernel, "hold", held(*array.shape), (array, after), in_specs=[ON_CHIP, IN_HBM])
-
-
-def exchange(total, axes, first, second, after=()):
+def add_up(parts):
+    return call(functools.partial(relay_kernel, len(parts)), "relay", held(*parts[0].shape[-2:]), parts)
+
+
+def exchange(total, axes, first, second):
     sizes = [lax.axis_size(axis) for axis in axes]
     proto = axes.index("proto")
     places = [(i, j) for i in range(sizes[0]) for j in range(sizes[1])]
@@ -360,8 +307,7 @@
         return lax.ppermute(total, axes, pairs)
 
     mine = permute(first)
-    passed = hold(mine, *after) if after else mine
-    return add_up([total, mine, swap(passed, "proto"), permute(second)])
+    return add_up([total, mine, swap(mine, "proto"), permute(second)])
 
 
 def across(total, up, over):
@@ -380,13 +326,13 @@
     return add_up([total, *[across(total, *step) for step in steps]])
 
 
-def add_up_along(total, after):
+def add_up_along(total):
     n = lax.axis_size("fsdp")
     if n == 4:
-        return exchange(total, ("fsdp", "proto"), lambda odd: (2 + odd, 0), lambda odd: (1, 0), after)
+        return exchange(total, ("fsdp", "proto"), lambda odd: (2 + odd, 0), lambda odd: (1, 0))
     if n <= DIRECT:
-        return add_up([total, *[swap(total, "fsdp", k) for k in range(1, n)]], after)
-    return add_up([lax.all_to_all(jnp.broadcast_to(total[None], (n, *total.shape)), "fsdp", 0, 0, tiled=True)], after)
+        return add_up([total, *[swap(total, "fsdp", k) for k in range(1, n)]])
+    return add_up([lax.all_to_all(jnp.broadcast_to(total[None], (n, *total.shape)), "fsdp", 0, 0, tiled=True)])
 
 
 def grad_kernel(total_ref, peak_ref, weight_unit, weight_scale, *refs):
@@ -464,9 +410,7 @@
 
     index = swap(pairing, "dp")
     mine = pack(*fetch(in_hbm(student_feats[0].T), in_hbm(teacher_feats[0].T)), index)
-    own_cols = teacher_weight.shape[1] // n_dp
-    middle = own_cols // 2
-    new, wt, ws, unit, scale, peak = prepare(teacher_weight, student_weight, center, n_dp, own_cols - middle)
+    teacher_new, wt, ws, unit, scale, peak = prepare(teacher_weight, student_weight, center, n_dp)
     weights = (ws, wt, peak)
     bot = mine.shape[1]
     if n_fsdp <= DIRECT:
@@ -485,8 +429,7 @@
     exps, unit_c, total_c = scores(2, [other], weights, exps=exps)
     exps, unit_d, total = scores(3, [swap(other, "proto")], weights, (total_a, total_b, total_c), exps)
     total = add_up_chip_and_across(total)
-    teacher_new, done = update_rest(teacher_weight, student_weight, total, new, own_cols, 0, middle)
-    total = add_up_along(total, (done,))
+    total = add_up_along(total)
     units = (unit_a, unit_b, unit_c, unit_d)
     student_grad = gradient(total, peak, unit, scale, units, exps)
     return (teacher_new, student_grad)

time: 44.4 us -> 43.8 us (0.986)
  Pallas kernels: 17.1 us -> 15.2 us
  waiting for transfers between devices: 9.59 us -> 10.7 us
    ppermute x4, waiting for transfers between devices: 2.27 us -> 4.42 us  [permute(): return lax.ppermute(total, axes, pairs)]
    pallas_call x15 -> x13, Pallas kernels: 17.1 us -> 15.2 us  [call(): pl.pallas_call(kernel, out_shape=out_shape, compiler_params=pltpu.Compile...]
    ppermute x13, waiting for transfers between devices: 7.33 us -> 6.27 us  [swap(): lax.ppermute(block, axis, [(i, i ^ apart) for i in range(lax.axis_size(ax...]
  transfers between devices with their start and end apart: 17 -> 17, of which waited for: 10 -> 12; matrix products, arithmetic and copies ran while one was open for 0% -> 0% of each run, Pallas kernels for 27% -> 23%
where the time goes in v21:
time: 43.8 us; the launch traced here: 43.6 us
  starting transfers between devices  16.9 us (39%)
  Pallas kernels  15.2 us (35%)
  waiting for transfers between devices  10.7 us (24%)
  between operations  0.75 us (2%)
    pallas_call x13, Pallas kernels, call(): pl.pallas_call(kernel, out_shape=out_shape, compiler_params=pltpu.Compile...  15.2 us
    ppermute x13, starting transfers between devices, swap(): lax.ppermute(block, axis, [(i, i ^ apart) for i in range(lax.axis_size(ax...  11.3 us
    ppermute x13, waiting for transfers between devices, swap(): lax.ppermute(block, axis, [(i, i ^ apart) for i in range(lax.axis_size(ax...  6.27 us
    ppermute x4, starting transfers between devices, permute(): return lax.ppermute(total, axes, pairs)  5.62 us
    ppermute x4, waiting for transfers between devices, permute(): return lax.ppermute(total, axes, pairs)  4.42 us
  transfers between devices with their start and end apart: 17, of which 12 were waited for; matrix products, arithmetic and copies ran while one was open for 0% of the time, Pallas kernels for 23%

profile of v21, /device:TPU:0, one launch (start us, length us, event | category | flops | bytes accessed | tf_op | source)
XLA Modules:
  0.0 43.6 jit_solution(12794887919910622653)
XLA Ops:
  0.6 3.0 %collective-permute-start = (s32[1,256]{1,0:T(1,128)}, s32[1,256]{1,0:T(1,128)S(1)}, u32[]{:S(2)}, u32[]{:S(2)}) collective-permute-start(s32[1,256]{1,0:T(1,128)} %param.10), channel_id=1, source_target_pairs={{0,1},{1,0},{2,3},{3,2},{4,5},{5,4},{6,7},{7,6},{8,9},{9,8},{10,11... | collective-permute-start | bytes 3080 | tf_op jit(solution)/shard_map/ppermute | solution.py:46
  3.6 0.9 %fetch.1 = (bf16[192,128]{1,0:T(8,128)(2,1)S(1)}, bf16[192,256]{1,0:T(8,128)(2,1)S(1)}) custom-call(bf16[192,256]{1,0:T(8,128)(2,1)} %bitcast.7, bf16[192,256]{1,0:T(8,128)(2,1)} %bitcast.8), custom_call_target="tpu_custom_call" | custom-call | flops 1 | bytes 1 | tf_op jit(solution)/shard_map/fetch/pallas_call | solution.py:35
  4.6 0.8 %collective-permute-done.index_ref = s32[1,256]{1,0:T(1,128)S(1)} collective-permute-done((s32[1,256]{1,0:T(1,128)}, s32[1,256]{1,0:T(1,128)S(1)}, u32[]{:S(2)}, u32[]{:S(2)}) %collective-permute-start) | collective-permute-done | bytes 1056 | tf_op jit(solution)/shard_map/ppermute | solution.py:46
  5.6 2.1 %collective-permute-start.4 = (bf16[2,192,128]{2,1,0:T(8,128)(2,1)S(1)}, bf16[2,192,128]{2,1,0:T(8,128)(2,1)S(1)}, u32[]{:S(2)}, u32[]{:S(2)}) collective-permute-start(bf16[2,192,128]{2,1,0:T(8,128)(2,1)S(1)} %pack.1.refs_0_), channel_id=1, source_target_pairs={{0,1},{1,0},{2,3},{3,2},{4,5},{5,4},{6,7},{7,6},{8,9},{9,8},{10,11... | collective-permute-start | bytes 294920 | tf_op jit(solution)/shard_map/ppermute | solution.py:46
  7.7 3.6 %collective-permute-start.3 = (bf16[2,192,128]{2,1,0:T(8,128)(2,1)S(1)}, bf16[2,192,128]{2,1,0:T(8,128)(2,1)S(1)}, u32[]{:S(2)}, u32[]{:S(2)}) collective-permute-start(bf16[2,192,128]{2,1,0:T(8,128)(2,1)S(1)} %pack.1.refs_0_), channel_id=1, source_target_pairs={{0,24},{8,16},{16,8},{24,0},{1,25},{9,17},{17,9},{25,1},{2,26},{10... | collective-permute-start | bytes 294920 | tf_op jit(solution)/shard_map/ppermute | solution.py:46
  11.3 0.8 %collective-permute-start.1 = (bf16[2,192,128]{2,1,0:T(8,128)(2,1)S(1)}, bf16[2,192,128]{2,1,0:T(8,128)(2,1)S(1)}, u32[]{:S(2)}, u32[]{:S(2)}) collective-permute-start(bf16[2,192,128]{2,1,0:T(8,128)(2,1)S(1)} %pack.1.refs_0_), channel_id=1, source_target_pairs={{0,8},{8,0},{16,24},{24,16},{1,9},{9,1},{17,25},{25,17},{2,10},{10... | collective-permute-start | bytes 294920 | tf_op jit(solution)/shard_map/ppermute | solution.py:46
  12.1 5.1 %prep.1 = (f32[192,4096]{1,0:T(8,128)}, bf16[2048,256]{1,0:T(8,128)(2,1)S(1)}, bf16[2048,256]{1,0:T(8,128)(2,1)S(1)}, f32[192,2048]{1,0:T(8,128)S(1)}, f32[1,2048]{1,0:T(1,128)S(1)}, /*index=5*/f32[1,128]{1,0:T(1,128)S(1)}) custom-call(f32[192,4096]{1,0:T(8,128)} %teacher_hbm.1, f32[192,4096]{1,0:T(8,128)} %student_hbm.1, f32[1,16384]{1,0:T(1,128)} %bitcast.9), custom_call_target="tpu_custom_call" | custom-call | flops 1 | bytes 1 | tf_op jit(solution)/shard_map/prep/pallas_call | solution.py:35
  17.2 1.0 %collective-permute-done.2.refs_2_ = bf16[2,192,128]{2,1,0:T(8,128)(2,1)S(1)} collective-permute-done((bf16[2,192,128]{2,1,0:T(8,128)(2,1)S(1)}, bf16[2,192,128]{2,1,0:T(8,128)(2,1)S(1)}, u32[]{:S(2)}, u32[]{:S(2)}) %collective-permute-start.2) | collective-permute-done | bytes 98336 | tf_op jit(solution)/shard_map/ppermute | solution.py:46
  18.3 0.6 %collective-permute-start.8 = (bf16[2,2,208,128]{3,2,1,0:T(8,128)(2,1)S(1)}, bf16[2,2,208,128]{3,2,1,0:T(8,128)(2,1)S(1)}, u32[]{:S(2)}, u32[]{:S(2)}) collective-permute-start(bf16[2,2,208,128]{3,2,1,0:T(8,128)(2,1)S(1)} %get-tuple-element.38), channel_id=1, source_target_pairs={{0,1},{1,0},{2,3},{3,2},{4,5},{5,4},{6,7},{7,6},{8,9},{9,8},{10,11... | collective-permute-start | bytes 638984 | tf_op jit(solution)/shard_map/ppermute | solution.py:46
  19.9 1.3 %scores.4 = (bf16[2048,4096]{1,0:T(8,128)(2,1)S(1)}, bf16[512,192]{1,0:T(8,128)(2,1)S(1)}, f32[2,512]{1,0:T(2,128)S(1)}) custom-call(bf16[4,2,192,128]{3,2,1,0:T(8,128)(2,1)S(1)} %get-tuple-element.30.refs_0_, bf16[2048,256]{1,0:T(8,128)(2,1)S(1)} %get-tuple-element.31.refs_1_.refs_2_.refs_4_, ...), custom_call_target="tpu_custom_call" | custom-call | flops 1 | bytes 1 | tf_op jit(solution)/shard_map/scores/pallas_call | solution.py:35
  21.2 1.3 %scores.5 = (bf16[2048,4096]{1,0:T(8,128)(2,1)S(1)}, bf16[512,192]{1,0:T(8,128)(2,1)S(1)}, f32[2,512]{1,0:T(2,128)S(1)}) custom-call(bf16[2,2,192,128]{3,2,1,0:T(8,128)(2,1)S(1)} %collective-permute-done.5.refs_0_, bf16[2,2,192,128]{3,2,1,0:T(8,128)(2,1)S(1)} %collective-permute-done.6.refs_1_, ...), custom_call_target="tpu_custom_call", output_to_operand_aliasing={{0}: (5, {})} | custom-call | flops 1 | bytes 1 | tf_op jit(solution)/shard_map/scores/pallas_call | solution.py:35
  22.5 1.6 %collective-permute-done.7.refs_1_ = bf16[2,192,128]{2,1,0:T(8,128)(2,1)S(1)} collective-permute-done((bf16[2,192,128]{2,1,0:T(8,128)(2,1)S(1)}, bf16[2,192,128]{2,1,0:T(8,128)(2,1)S(1)}, u32[]{:S(2)}, u32[]{:S(2)}) %collective-permute-start.7) | collective-permute-done | bytes 98336 | tf_op jit(solution)/shard_map/ppermute | solution.py:46
  24.8 1.3 %scores.6 = (bf16[2048,4096]{1,0:T(8,128)(2,1)S(1)}, bf16[512,192]{1,0:T(8,128)(2,1)S(1)}, f32[2,512]{1,0:T(2,128)S(1)}) custom-call(bf16[4,2,192,128]{3,2,1,0:T(8,128)(2,1)S(1)} %join.3.refs_0_, bf16[2048,256]{1,0:T(8,128)(2,1)S(1)} %get-tuple-element.31.refs_1_.refs_2_.refs_4_, ...), custom_call_target="tpu_custom_call", output_to_operand_aliasing={{0}: (4, {})} | custom-call | flops 1 | bytes 1 | tf_op jit(solution)/shard_map/scores/pallas_call | solution.py:35
  26.5 1.3 %scores.7 = (bf16[2048,4096]{1,0:T(8,128)(2,1)S(1)}, bf16[512,192]{1,0:T(8,128)(2,1)S(1)}, f32[4,1024]{1,0:T(4,128)S(1)}) custom-call(f32[2,512]{1,0:T(2,128)S(1)} %get-tuple-element.33.refs_0_, f32[2,512]{1,0:T(2,128)S(1)} %get-tuple-element.37.refs_3_.refs_1_, f32[2,512]{1,0:T(2,128)S(1)} %get-tuple-element.40.refs_2_, ...), custom_call_target="tpu_custom_call", output_to_operand_aliasing={{0}: (7, {})} | custom-call | flops 1 | bytes 1 | tf_op jit(solution)/shard_map/scores/pallas_call | solution.py:35
  28.0 1.0 %collective-permute-done.10.refs_1_ = f32[4,1024]{1,0:T(4,128)S(1)} collective-permute-done((f32[4,1024]{1,0:T(4,128)S(1)}, f32[4,1024]{1,0:T(4,128)S(1)}, u32[]{:S(2)}, u32[]{:S(2)}) %collective-permute-start.10) | collective-permute-done | bytes 16416 | tf_op jit(solution)/shard_map/ppermute | solution.py:46
  29.1 1.0 %collective-permute-start.11 = (f32[4,1024]{1,0:T(4,128)S(1)}, f32[4,1024]{1,0:T(4,128)S(1)}, u32[]{:S(2)}, u32[]{:S(2)}) collective-permute-start(f32[4,1024]{1,0:T(4,128)S(1)} %relay.3.refs_0_), channel_id=1, source_target_pairs={{0,1},{1,0},{2,7},{3,6},{4,5},{5,4},{6,3},{7,2},{8,9},{9,8},{10,15... | collective-permute-start | bytes 49160 | tf_op jit(solution)/shard_map/ppermute | solution.py:307
  30.1 1.5 %collective-permute-start.13 = (f32[4,1024]{1,0:T(4,128)S(1)}, f32[4,1024]{1,0:T(4,128)S(1)}, u32[]{:S(2)}, u32[]{:S(2)}) collective-permute-start(f32[4,1024]{1,0:T(4,128)S(1)} %relay.3.refs_0_), channel_id=1, source_target_pairs={{0,4},{1,5},{2,6},{3,7},{4,0},{5,1},{6,2},{7,3},{8,12},{9,13},{10,... | collective-permute-start | bytes 49160 | tf_op jit(solution)/shard_map/ppermute | solution.py:307
  31.7 1.3 %collective-permute-done.11.refs_1_ = f32[4,1024]{1,0:T(4,128)S(1)} collective-permute-done((f32[4,1024]{1,0:T(4,128)S(1)}, f32[4,1024]{1,0:T(4,128)S(1)}, u32[]{:S(2)}, u32[]{:S(2)}) %collective-permute-start.11) | collective-permute-done | bytes 16416 | tf_op jit(solution)/shard_map/ppermute | solution.py:307
  32.9 1.0 %collective-permute-done.13.refs_3_ = f32[4,1024]{1,0:T(4,128)S(1)} collective-permute-done((f32[4,1024]{1,0:T(4,128)S(1)}, f32[4,1024]{1,0:T(4,128)S(1)}, u32[]{:S(2)}, u32[]{:S(2)}) %collective-permute-start.13) | collective-permute-done | bytes 16416 | tf_op jit(solution)/shard_map/ppermute | solution.py:307
  34.1 1.3 %collective-permute-start.14 = (f32[4,1024]{1,0:T(4,128)S(1)}, f32[4,1024]{1,0:T(4,128)S(1)}, u32[]{:S(2)}, u32[]{:S(2)}) collective-permute-start(f32[4,1024]{1,0:T(4,128)S(1)} %relay.4.refs_0_), channel_id=1, source_target_pairs={{0,16},{2,26},{4,20},{6,30},{8,24},{10,18},{12,28},{14,22},{16,0},... | collective-permute-start | bytes 49160 | tf_op jit(solution)/shard_map/ppermute | solution.py:307
  35.5 1.7 %collective-permute-start.16 = (f32[4,1024]{1,0:T(4,128)S(1)}, f32[4,1024]{1,0:T(4,128)S(1)}, u32[]{:S(2)}, u32[]{:S(2)}) collective-permute-start(f32[4,1024]{1,0:T(4,128)S(1)} %relay.4.refs_0_), channel_id=1, source_target_pairs={{0,8},{2,10},{4,12},{6,14},{8,0},{10,2},{12,4},{14,6},{16,24},{18,... | collective-permute-start | bytes 49160 | tf_op jit(solution)/shard_map/ppermute | solution.py:307
  37.2 1.6 %collective-permute-done.14.refs_1_ = f32[4,1024]{1,0:T(4,128)S(1)} collective-permute-done((f32[4,1024]{1,0:T(4,128)S(1)}, f32[4,1024]{1,0:T(4,128)S(1)}, u32[]{:S(2)}, u32[]{:S(2)}) %collective-permute-start.14) | collective-permute-done | bytes 16416 | tf_op jit(solution)/shard_map/ppermute | solution.py:307
  39.4 0.7 %collective-permute-done.15.refs_2_ = f32[4,1024]{1,0:T(4,128)S(1)} collective-permute-done((f32[4,1024]{1,0:T(4,128)S(1)}, f32[4,1024]{1,0:T(4,128)S(1)}, u32[]{:S(2)}, u32[]{:S(2)}) %collective-permute-start.15) | collective-permute-done | bytes 16416 | tf_op jit(solution)/shard_map/ppermute | solution.py:46
  40.1 3.5 %gradient.1 = f32[192,2048]{1,0:T(8,128)} custom-call(f32[4,1024]{1,0:T(4,128)S(1)} %relay.5.total_ref, f32[1,128]{1,0:T(1,128)S(1)} %get-tuple-element.29.refs_5_.refs_3_.refs_4_.refs_6_.peak_ref, f32[192,2048]{1,0:T(8,128)S(1)} %get-tuple-element.43.weight_unit, f32[1,2048]{1,0:T(1,128)S(1)} %get-tuple-element.44.weight_scale, ...), custom_call_target="tpu_custom_call" | custom-call | flops 1 | bytes 1 | tf_op jit(solution)/shard_map/gradient/pallas_call | solution.py:35
  (23 shorter events, 3.3 us)
Async XLA Ops:
  0.6 4.8 %collective-permute-start = (s32[1,256]{1,0:T(1,128)}, s32[1,256]{1,0:T(1,128)S(1)}, u32[]{:S(2)}, u32[]{:S(2)}) collective-permute-start(s32[1,256]{1,0:T(1,128)} %param.10), channel_id=1, source_target_pairs={{0,1},{1,0},{2,3},{3,2},{4,5},{5,4},{6,7},{7,6},{8,9},{9,8},{10,11... | collective-permute-start | bytes 3080 | tf_op jit(solution)/shard_map/ppermute | solution.py:46
  5.6 11.6 %collective-permute-start.4 = (bf16[2,192,128]{2,1,0:T(8,128)(2,1)S(1)}, bf16[2,192,128]{2,1,0:T(8,128)(2,1)S(1)}, u32[]{:S(2)}, u32[]{:S(2)}) collective-permute-start(bf16[2,192,128]{2,1,0:T(8,128)(2,1)S(1)} %pack.1.refs_0_), channel_id=1, source_target_pairs={{0,1},{1,0},{2,3},{3,2},{4,5},{5,4},{6,7},{7,6},{8,9},{9,8},{10,11... | collective-permute-start | bytes 294920 | tf_op jit(solution)/shard_map/ppermute | solution.py:46
  7.7 9.5 %collective-permute-start.3 = (bf16[2,192,128]{2,1,0:T(8,128)(2,1)S(1)}, bf16[2,192,128]{2,1,0:T(8,128)(2,1)S(1)}, u32[]{:S(2)}, u32[]{:S(2)}) collective-permute-start(bf16[2,192,128]{2,1,0:T(8,128)(2,1)S(1)} %pack.1.refs_0_), channel_id=1, source_target_pairs={{0,24},{8,16},{16,8},{24,0},{1,25},{9,17},{17,9},{25,1},{2,26},{10... | collective-permute-start | bytes 294920 | tf_op jit(solution)/shard_map/ppermute | solution.py:46
  11.3 6.9 %collective-permute-start.2 = (bf16[2,192,128]{2,1,0:T(8,128)(2,1)S(1)}, bf16[2,192,128]{2,1,0:T(8,128)(2,1)S(1)}, u32[]{:S(2)}, u32[]{:S(2)}) collective-permute-start(bf16[2,192,128]{2,1,0:T(8,128)(2,1)S(1)} %pack.1.refs_0_), channel_id=1, source_target_pairs={{0,16},{8,24},{16,0},{24,8},{1,17},{9,25},{17,1},{25,9},{2,18},{10... | collective-permute-start | bytes 294920 | tf_op jit(solution)/shard_map/ppermute | solution.py:46
  11.3 6.9 %collective-permute-start.1 = (bf16[2,192,128]{2,1,0:T(8,128)(2,1)S(1)}, bf16[2,192,128]{2,1,0:T(8,128)(2,1)S(1)}, u32[]{:S(2)}, u32[]{:S(2)}) collective-permute-start(bf16[2,192,128]{2,1,0:T(8,128)(2,1)S(1)} %pack.1.refs_0_), channel_id=1, source_target_pairs={{0,8},{8,0},{16,24},{24,16},{1,9},{9,1},{17,25},{25,17},{2,10},{10... | collective-permute-start | bytes 294920 | tf_op jit(solution)/shard_map/ppermute | solution.py:46
  18.3 6.3 %collective-permute-start.8 = (bf16[2,2,208,128]{3,2,1,0:T(8,128)(2,1)S(1)}, bf16[2,2,208,128]{3,2,1,0:T(8,128)(2,1)S(1)}, u32[]{:S(2)}, u32[]{:S(2)}) collective-permute-start(bf16[2,2,208,128]{3,2,1,0:T(8,128)(2,1)S(1)} %get-tuple-element.38), channel_id=1, source_target_pairs={{0,1},{1,0},{2,3},{3,2},{4,5},{5,4},{6,7},{7,6},{8,9},{9,8},{10,11... | collective-permute-start | bytes 638984 | tf_op jit(solution)/shard_map/ppermute | solution.py:46
  18.9 2.3 %collective-permute-start.5 = (bf16[2,2,192,128]{3,2,1,0:T(8,128)(2,1)S(1)}, bf16[2,2,192,128]{3,2,1,0:T(8,128)(2,1)S(1)}, u32[]{:S(2)}, u32[]{:S(2)}) collective-permute-start(bf16[2,2,192,128]{3,2,1,0:T(8,128)(2,1)S(1)} %get-tuple-element.34), channel_id=1, source_target_pairs={{0,2},{2,0},{4,6},{6,4},{1,3},{3,1},{5,7},{7,5},{8,10},{10,8},{12,... | collective-permute-start | bytes 589832 | tf_op jit(solution)/shard_map/ppermute | solution.py:46
  18.9 2.3 %collective-permute-start.6 = (bf16[2,2,192,128]{3,2,1,0:T(8,128)(2,1)S(1)}, bf16[2,2,192,128]{3,2,1,0:T(8,128)(2,1)S(1)}, u32[]{:S(2)}, u32[]{:S(2)}) collective-permute-start(bf16[2,2,192,128]{3,2,1,0:T(8,128)(2,1)S(1)} %get-tuple-element.35), channel_id=1, source_target_pairs={{0,2},{2,0},{4,6},{6,4},{1,3},{3,1},{5,7},{7,5},{8,10},{10,8},{12,... | collective-permute-start | bytes 589832 | tf_op jit(solution)/shard_map/ppermute | solution.py:46
  19.4 4.7 %collective-permute-start.7 = (bf16[2,192,128]{2,1,0:T(8,128)(2,1)S(1)}, bf16[2,192,128]{2,1,0:T(8,128)(2,1)S(1)}, u32[]{:S(2)}, u32[]{:S(2)}) collective-permute-start(bf16[2,192,128]{2,1,0:T(8,128)(2,1)S(1)} %collective-permute-done.4.refs_4_.refs_0_), channel_id=1, source_target_pairs={{0,8},{8,0},{16,24},{24,16},{1,9},{9,1},{17,25},{25,17},{2,10},{10... | collective-permute-start | bytes 294920 | tf_op jit(solution)/shard_map/ppermute | solution.py:46
  24.7 1.8 %collective-permute-start.9 = (bf16[4,2,192,128]{3,2,1,0:T(8,128)(2,1)S(1)}, bf16[4,2,192,128]{3,2,1,0:T(8,128)(2,1)S(1)}, u32[]{:S(2)}, u32[]{:S(2)}) collective-permute-start(bf16[4,2,192,128]{3,2,1,0:T(8,128)(2,1)S(1)} %join.3.refs_0_), channel_id=1, source_target_pairs={{0,2},{2,0},{4,6},{6,4},{1,3},{3,1},{5,7},{7,5},{8,10},{10,8},{12,... | collective-permute-start | bytes 1179656 | tf_op jit(solution)/shard_map/ppermute | solution.py:46
  27.8 1.2 %collective-permute-start.10 = (f32[4,1024]{1,0:T(4,128)S(1)}, f32[4,1024]{1,0:T(4,128)S(1)}, u32[]{:S(2)}, u32[]{:S(2)}) collective-permute-start(f32[4,1024]{1,0:T(4,128)S(1)} %get-tuple-element.42.refs_0_), channel_id=1, source_target_pairs={{0,2},{2,0},{4,6},{6,4},{1,3},{3,1},{5,7},{7,5},{8,10},{10,8},{12,... | collective-permute-start | bytes 49160 | tf_op jit(solution)/shard_map/ppermute | solution.py:46
  29.1 3.8 %collective-permute-start.11 = (f32[4,1024]{1,0:T(4,128)S(1)}, f32[4,1024]{1,0:T(4,128)S(1)}, u32[]{:S(2)}, u32[]{:S(2)}) collective-permute-start(f32[4,1024]{1,0:T(4,128)S(1)} %relay.3.refs_0_), channel_id=1, source_target_pairs={{0,1},{1,0},{2,7},{3,6},{4,5},{5,4},{6,3},{7,2},{8,9},{9,8},{10,15... | collective-permute-start | bytes 49160 | tf_op jit(solution)/shard_map/ppermute | solution.py:307
  30.1 3.8 %collective-permute-start.13 = (f32[4,1024]{1,0:T(4,128)S(1)}, f32[4,1024]{1,0:T(4,128)S(1)}, u32[]{:S(2)}, u32[]{:S(2)}) collective-permute-start(f32[4,1024]{1,0:T(4,128)S(1)} %relay.3.refs_0_), channel_id=1, source_target_pairs={{0,4},{1,5},{2,6},{3,7},{4,0},{5,1},{6,2},{7,3},{8,12},{9,13},{10,... | collective-permute-start | bytes 49160 | tf_op jit(solution)/shard_map/ppermute | solution.py:307
  32.9 1.2 %collective-permute-start.12 = (f32[4,1024]{1,0:T(4,128)S(1)}, f32[4,1024]{1,0:T(4,128)S(1)}, u32[]{:S(2)}, u32[]{:S(2)}) collective-permute-start(f32[4,1024]{1,0:T(4,128)S(1)} %collective-permute-done.11.refs_1_), channel_id=1, source_target_pairs={{0,2},{2,0},{4,6},{6,4},{1,3},{3,1},{5,7},{7,5},{8,10},{10,8},{12,... | collective-permute-start | bytes 49160 | tf_op jit(solution)/shard_map/ppermute | solution.py:46
  34.1 4.7 %collective-permute-start.14 = (f32[4,1024]{1,0:T(4,128)S(1)}, f32[4,1024]{1,0:T(4,128)S(1)}, u32[]{:S(2)}, u32[]{:S(2)}) collective-permute-start(f32[4,1024]{1,0:T(4,128)S(1)} %relay.4.refs_0_), channel_id=1, source_target_pairs={{0,16},{2,26},{4,20},{6,30},{8,24},{10,18},{12,28},{14,22},{16,0},... | collective-permute-start | bytes 49160 | tf_op jit(solution)/shard_map/ppermute | solution.py:307
  35.5 3.9 %collective-permute-start.16 = (f32[4,1024]{1,0:T(4,128)S(1)}, f32[4,1024]{1,0:T(4,128)S(1)}, u32[]{:S(2)}, u32[]{:S(2)}) collective-permute-start(f32[4,1024]{1,0:T(4,128)S(1)} %relay.4.refs_0_), channel_id=1, source_target_pairs={{0,8},{2,10},{4,12},{6,14},{8,0},{10,2},{12,4},{14,6},{16,24},{18,... | collective-permute-start | bytes 49160 | tf_op jit(solution)/shard_map/ppermute | solution.py:307
  38.9 1.2 %collective-permute-start.15 = (f32[4,1024]{1,0:T(4,128)S(1)}, f32[4,1024]{1,0:T(4,128)S(1)}, u32[]{:S(2)}, u32[]{:S(2)}) collective-permute-start(f32[4,1024]{1,0:T(4,128)S(1)} %collective-permute-done.14.refs_1_), channel_id=1, source_target_pairs={{0,2},{2,0},{4,6},{6,4},{1,3},{3,1},{5,7},{7,5},{8,10},{10,8},{12,... | collective-permute-start | bytes 49160 | tf_op jit(solution)/shard_map/ppermute | solution.py:46

commit v22 on v21

--- a/solution.py
+++ b/solution.py
@@ -321,7 +321,7 @@
     n_proto, n_dp = lax.axis_size("proto"), lax.axis_size("dp")
     total = add_up([total, swap(total, "proto")])
     if n_proto == 4 and n_dp == 2:
-        return exchange(total, ("proto", "dp"), lambda odd: (2 * odd, 1), lambda odd: (2, 0))
+        return exchange(total, ("proto", "dp"), lambda odd: (2 * odd, 1 - odd), lambda odd: (2, 1))
     steps = [(up, over) for up in range(0, n_proto, 2) for over in range(n_dp)][1:]
     return add_up([total, *[across(total, *step) for step in steps]])
 
@@ -329,7 +329,7 @@
 def add_up_along(total):
     n = lax.axis_size("fsdp")
     if n == 4:
-        return exchange(total, ("fsdp", "proto"), lambda odd: (2 + odd, 0), lambda odd: (1, 0))
+        return exchange(total, ("fsdp", "proto"), lambda odd: (1 + odd, 0), lambda odd: (3, 0))
     if n <= DIRECT:
         return add_up([total, *[swap(total, "fsdp", k) for k in range(1, n)]])
     return add_up([lax.all_to_all(jnp.broadcast_to(total[None], (n, *total.shape)), "fsdp", 0, 0, tiled=True)])

time: 43.8 us -> 44.6 us (1.018)
    ppermute x4, waiting for transfers between devices: 4.42 us -> 5.69 us  [permute(): return lax.ppermute(total, axes, pairs)]
    ppermute x13, waiting for transfers between devices: 6.27 us -> 5.42 us  [swap(): lax.ppermute(block, axis, [(i, i ^ apart) for i in range(lax.axis_size(ax...]
  transfers between devices with their start and end apart: 17 -> 17, of which waited for: 12 -> 10; matrix products, arithmetic and copies ran while one was open for 0% -> 0% of each run, Pallas kernels for 23% -> 22%
where the time goes in v22:
time: 44.6 us; the launch traced here: 44.4 us
  starting transfers between devices  17.3 us (39%)
  Pallas kernels  15.2 us (34%)
  waiting for transfers between devices  11.1 us (25%)
  between operations  0.75 us (2%)
    pallas_call x13, Pallas kernels, call(): pl.pallas_call(kernel, out_shape=out_shape, compiler_params=pltpu.Compile...  15.2 us
    ppermute x13, starting transfers between devices, swap(): lax.ppermute(block, axis, [(i, i ^ apart) for i in range(lax.axis_size(ax...  11.3 us
    ppermute x4, starting transfers between devices, permute(): return lax.ppermute(total, axes, pairs)  6.01 us
    ppermute x4, waiting for transfers between devices, permute(): return lax.ppermute(total, axes, pairs)  5.69 us
    ppermute x13, waiting for transfers between devices, swap(): lax.ppermute(block, axis, [(i, i ^ apart) for i in range(lax.axis_size(ax...  5.42 us
  transfers between devices with their start and end apart: 17, of which 10 were waited for; matrix products, arithmetic and copies ran while one was open for 0% of the time, Pallas kernels for 22%

profile of v22, /device:TPU:0, one launch (start us, length us, event | category | flops | bytes accessed | tf_op | source)
XLA Modules:
  0.0 44.4 jit_solution(12101185934821994530)
XLA Ops:
  0.6 3.0 %collective-permute-start = (s32[1,256]{1,0:T(1,128)}, s32[1,256]{1,0:T(1,128)S(1)}, u32[]{:S(2)}, u32[]{:S(2)}) collective-permute-start(s32[1,256]{1,0:T(1,128)} %param.10), channel_id=1, source_target_pairs={{0,1},{1,0},{2,3},{3,2},{4,5},{5,4},{6,7},{7,6},{8,9},{9,8},{10,11... | collective-permute-start | bytes 3080 | tf_op jit(solution)/shard_map/ppermute | solution.py:46
  3.6 0.9 %fetch.1 = (bf16[192,128]{1,0:T(8,128)(2,1)S(1)}, bf16[192,256]{1,0:T(8,128)(2,1)S(1)}) custom-call(bf16[192,256]{1,0:T(8,128)(2,1)} %bitcast.7, bf16[192,256]{1,0:T(8,128)(2,1)} %bitcast.8), custom_call_target="tpu_custom_call" | custom-call | flops 1 | bytes 1 | tf_op jit(solution)/shard_map/fetch/pallas_call | solution.py:35
  4.6 0.8 %collective-permute-done.index_ref = s32[1,256]{1,0:T(1,128)S(1)} collective-permute-done((s32[1,256]{1,0:T(1,128)}, s32[1,256]{1,0:T(1,128)S(1)}, u32[]{:S(2)}, u32[]{:S(2)}) %collective-permute-start) | collective-permute-done | bytes 1056 | tf_op jit(solution)/shard_map/ppermute | solution.py:46
  5.6 2.1 %collective-permute-start.4 = (bf16[2,192,128]{2,1,0:T(8,128)(2,1)S(1)}, bf16[2,192,128]{2,1,0:T(8,128)(2,1)S(1)}, u32[]{:S(2)}, u32[]{:S(2)}) collective-permute-start(bf16[2,192,128]{2,1,0:T(8,128)(2,1)S(1)} %pack.1.refs_0_), channel_id=1, source_target_pairs={{0,1},{1,0},{2,3},{3,2},{4,5},{5,4},{6,7},{7,6},{8,9},{9,8},{10,11... | collective-permute-start | bytes 294920 | tf_op jit(solution)/shard_map/ppermute | solution.py:46
  7.7 3.6 %collective-permute-start.3 = (bf16[2,192,128]{2,1,0:T(8,128)(2,1)S(1)}, bf16[2,192,128]{2,1,0:T(8,128)(2,1)S(1)}, u32[]{:S(2)}, u32[]{:S(2)}) collective-permute-start(bf16[2,192,128]{2,1,0:T(8,128)(2,1)S(1)} %pack.1.refs_0_), channel_id=1, source_target_pairs={{0,24},{8,16},{16,8},{24,0},{1,25},{9,17},{17,9},{25,1},{2,26},{10... | collective-permute-start | bytes 294920 | tf_op jit(solution)/shard_map/ppermute | solution.py:46
  11.3 0.8 %collective-permute-start.1 = (bf16[2,192,128]{2,1,0:T(8,128)(2,1)S(1)}, bf16[2,192,128]{2,1,0:T(8,128)(2,1)S(1)}, u32[]{:S(2)}, u32[]{:S(2)}) collective-permute-start(bf16[2,192,128]{2,1,0:T(8,128)(2,1)S(1)} %pack.1.refs_0_), channel_id=1, source_target_pairs={{0,8},{8,0},{16,24},{24,16},{1,9},{9,1},{17,25},{25,17},{2,10},{10... | collective-permute-start | bytes 294920 | tf_op jit(solution)/shard_map/ppermute | solution.py:46
  12.1 5.1 %prep.1 = (f32[192,4096]{1,0:T(8,128)}, bf16[2048,256]{1,0:T(8,128)(2,1)S(1)}, bf16[2048,256]{1,0:T(8,128)(2,1)S(1)}, f32[192,2048]{1,0:T(8,128)S(1)}, f32[1,2048]{1,0:T(1,128)S(1)}, /*index=5*/f32[1,128]{1,0:T(1,128)S(1)}) custom-call(f32[192,4096]{1,0:T(8,128)} %teacher_hbm.1, f32[192,4096]{1,0:T(8,128)} %student_hbm.1, f32[1,16384]{1,0:T(1,128)} %bitcast.9), custom_call_target="tpu_custom_call" | custom-call | flops 1 | bytes 1 | tf_op jit(solution)/shard_map/prep/pallas_call | solution.py:35
  17.2 1.0 %collective-permute-done.2.refs_2_ = bf16[2,192,128]{2,1,0:T(8,128)(2,1)S(1)} collective-permute-done((bf16[2,192,128]{2,1,0:T(8,128)(2,1)S(1)}, bf16[2,192,128]{2,1,0:T(8,128)(2,1)S(1)}, u32[]{:S(2)}, u32[]{:S(2)}) %collective-permute-start.2) | collective-permute-done | bytes 98336 | tf_op jit(solution)/shard_map/ppermute | solution.py:46
  18.3 0.6 %collective-permute-start.8 = (bf16[2,2,208,128]{3,2,1,0:T(8,128)(2,1)S(1)}, bf16[2,2,208,128]{3,2,1,0:T(8,128)(2,1)S(1)}, u32[]{:S(2)}, u32[]{:S(2)}) collective-permute-start(bf16[2,2,208,128]{3,2,1,0:T(8,128)(2,1)S(1)} %get-tuple-element.38), channel_id=1, source_target_pairs={{0,1},{1,0},{2,3},{3,2},{4,5},{5,4},{6,7},{7,6},{8,9},{9,8},{10,11... | collective-permute-start | bytes 638984 | tf_op jit(solution)/shard_map/ppermute | solution.py:46
  19.9 1.3 %scores.4 = (bf16[2048,4096]{1,0:T(8,128)(2,1)S(1)}, bf16[512,192]{1,0:T(8,128)(2,1)S(1)}, f32[2,512]{1,0:T(2,128)S(1)}) custom-call(bf16[4,2,192,128]{3,2,1,0:T(8,128)(2,1)S(1)} %get-tuple-element.30.refs_0_, bf16[2048,256]{1,0:T(8,128)(2,1)S(1)} %get-tuple-element.31.refs_1_.refs_2_.refs_4_, ...), custom_call_target="tpu_custom_call" | custom-call | flops 1 | bytes 1 | tf_op jit(solution)/shard_map/scores/pallas_call | solution.py:35
  21.2 1.3 %scores.5 = (bf16[2048,4096]{1,0:T(8,128)(2,1)S(1)}, bf16[512,192]{1,0:T(8,128)(2,1)S(1)}, f32[2,512]{1,0:T(2,128)S(1)}) custom-call(bf16[2,2,192,128]{3,2,1,0:T(8,128)(2,1)S(1)} %collective-permute-done.5.refs_0_, bf16[2,2,192,128]{3,2,1,0:T(8,128)(2,1)S(1)} %collective-permute-done.6.refs_1_, ...), custom_call_target="tpu_custom_call", output_to_operand_aliasing={{0}: (5, {})} | custom-call | flops 1 | bytes 1 | tf_op jit(solution)/shard_map/scores/pallas_call | solution.py:35
  22.5 1.6 %collective-permute-done.7.refs_1_ = bf16[2,192,128]{2,1,0:T(8,128)(2,1)S(1)} collective-permute-done((bf16[2,192,128]{2,1,0:T(8,128)(2,1)S(1)}, bf16[2,192,128]{2,1,0:T(8,128)(2,1)S(1)}, u32[]{:S(2)}, u32[]{:S(2)}) %collective-permute-start.7) | collective-permute-done | bytes 98336 | tf_op jit(solution)/shard_map/ppermute | solution.py:46
  24.1 0.5 %collective-permute-done.8.refs_2_ = bf16[2,2,208,128]{3,2,1,0:T(8,128)(2,1)S(1)} collective-permute-done((bf16[2,2,208,128]{3,2,1,0:T(8,128)(2,1)S(1)}, bf16[2,2,208,128]{3,2,1,0:T(8,128)(2,1)S(1)}, u32[]{:S(2)}, u32[]{:S(2)}) %collective-permute-start.8) | collective-permute-done | bytes 213024 | tf_op jit(solution)/shard_map/ppermute | solution.py:46
  24.8 1.3 %scores.6 = (bf16[2048,4096]{1,0:T(8,128)(2,1)S(1)}, bf16[512,192]{1,0:T(8,128)(2,1)S(1)}, f32[2,512]{1,0:T(2,128)S(1)}) custom-call(bf16[4,2,192,128]{3,2,1,0:T(8,128)(2,1)S(1)} %join.3.refs_0_, bf16[2048,256]{1,0:T(8,128)(2,1)S(1)} %get-tuple-element.31.refs_1_.refs_2_.refs_4_, ...), custom_call_target="tpu_custom_call", output_to_operand_aliasing={{0}: (4, {})} | custom-call | flops 1 | bytes 1 | tf_op jit(solution)/shard_map/scores/pallas_call | solution.py:35
  26.5 1.3 %scores.7 = (bf16[2048,4096]{1,0:T(8,128)(2,1)S(1)}, bf16[512,192]{1,0:T(8,128)(2,1)S(1)}, f32[4,1024]{1,0:T(4,128)S(1)}) custom-call(f32[2,512]{1,0:T(2,128)S(1)} %get-tuple-element.33.refs_0_, f32[2,512]{1,0:T(2,128)S(1)} %get-tuple-element.37.refs_3_.refs_1_, f32[2,512]{1,0:T(2,128)S(1)} %get-tuple-element.40.refs_2_, ...), custom_call_target="tpu_custom_call", output_to_operand_aliasing={{0}: (7, {})} | custom-call | flops 1 | bytes 1 | tf_op jit(solution)/shard_map/scores/pallas_call | solution.py:35
  28.0 1.0 %collective-permute-done.10.refs_1_ = f32[4,1024]{1,0:T(4,128)S(1)} collective-permute-done((f32[4,1024]{1,0:T(4,128)S(1)}, f32[4,1024]{1,0:T(4,128)S(1)}, u32[]{:S(2)}, u32[]{:S(2)}) %collective-permute-start.10) | collective-permute-done | bytes 16416 | tf_op jit(solution)/shard_map/ppermute | solution.py:46
  29.1 1.0 %collective-permute-start.11 = (f32[4,1024]{1,0:T(4,128)S(1)}, f32[4,1024]{1,0:T(4,128)S(1)}, u32[]{:S(2)}, u32[]{:S(2)}) collective-permute-start(f32[4,1024]{1,0:T(4,128)S(1)} %relay.3.refs_0_), channel_id=1, source_target_pairs={{0,1},{1,0},{2,6},{3,7},{4,5},{5,4},{6,2},{7,3},{8,9},{9,8},{10,14... | collective-permute-start | bytes 49160 | tf_op jit(solution)/shard_map/ppermute | solution.py:307
  30.1 2.0 %collective-permute-start.13 = (f32[4,1024]{1,0:T(4,128)S(1)}, f32[4,1024]{1,0:T(4,128)S(1)}, u32[]{:S(2)}, u32[]{:S(2)}) collective-permute-start(f32[4,1024]{1,0:T(4,128)S(1)} %relay.3.refs_0_), channel_id=1, source_target_pairs={{0,5},{1,4},{2,7},{3,6},{4,1},{5,0},{6,3},{7,2},{8,13},{9,12},{10,... | collective-permute-start | bytes 49160 | tf_op jit(solution)/shard_map/ppermute | solution.py:307
  32.1 0.8 %collective-permute-done.11.refs_1_ = f32[4,1024]{1,0:T(4,128)S(1)} collective-permute-done((f32[4,1024]{1,0:T(4,128)S(1)}, f32[4,1024]{1,0:T(4,128)S(1)}, u32[]{:S(2)}, u32[]{:S(2)}) %collective-permute-start.11) | collective-permute-done | bytes 16416 | tf_op jit(solution)/shard_map/ppermute | solution.py:307
  32.9 1.9 %collective-permute-done.13.refs_3_ = f32[4,1024]{1,0:T(4,128)S(1)} collective-permute-done((f32[4,1024]{1,0:T(4,128)S(1)}, f32[4,1024]{1,0:T(4,128)S(1)}, u32[]{:S(2)}, u32[]{:S(2)}) %collective-permute-start.13) | collective-permute-done | bytes 16416 | tf_op jit(solution)/shard_map/ppermute | solution.py:307
  35.3 2.5 %collective-permute-start.16 = (f32[4,1024]{1,0:T(4,128)S(1)}, f32[4,1024]{1,0:T(4,128)S(1)}, u32[]{:S(2)}, u32[]{:S(2)}) collective-permute-start(f32[4,1024]{1,0:T(4,128)S(1)} %relay.4.refs_0_), channel_id=1, source_target_pairs={{0,24},{2,26},{4,28},{6,30},{8,16},{10,18},{12,20},{14,22},{16,8},... | collective-permute-start | bytes 49160 | tf_op jit(solution)/shard_map/ppermute | solution.py:307
  37.8 0.8 %collective-permute-done.14.refs_1_ = f32[4,1024]{1,0:T(4,128)S(1)} collective-permute-done((f32[4,1024]{1,0:T(4,128)S(1)}, f32[4,1024]{1,0:T(4,128)S(1)}, u32[]{:S(2)}, u32[]{:S(2)}) %collective-permute-start.14) | collective-permute-done | bytes 16416 | tf_op jit(solution)/shard_map/ppermute | solution.py:307
  38.6 2.2 %collective-permute-done.16.refs_3_ = f32[4,1024]{1,0:T(4,128)S(1)} collective-permute-done((f32[4,1024]{1,0:T(4,128)S(1)}, f32[4,1024]{1,0:T(4,128)S(1)}, u32[]{:S(2)}, u32[]{:S(2)}) %collective-permute-start.16) | collective-permute-done | bytes 16416 | tf_op jit(solution)/shard_map/ppermute | solution.py:307
  40.9 3.5 %gradient.1 = f32[192,2048]{1,0:T(8,128)} custom-call(f32[4,1024]{1,0:T(4,128)S(1)} %relay.5.total_ref, f32[1,128]{1,0:T(1,128)S(1)} %get-tuple-element.29.refs_5_.refs_3_.refs_4_.refs_6_.peak_ref, f32[192,2048]{1,0:T(8,128)S(1)} %get-tuple-element.43.weight_unit, f32[1,2048]{1,0:T(1,128)S(1)} %get-tuple-element.44.weight_scale, ...), custom_call_target="tpu_custom_call" | custom-call | flops 1 | bytes 1 | tf_op jit(solution)/shard_map/gradient/pallas_call | solution.py:35
  (23 shorter events, 2.5 us)
Async XLA Ops:
  0.6 4.8 %collective-permute-start = (s32[1,256]{1,0:T(1,128)}, s32[1,256]{1,0:T(1,128)S(1)}, u32[]{:S(2)}, u32[]{:S(2)}) collective-permute-start(s32[1,256]{1,0:T(1,128)} %param.10), channel_id=1, source_target_pairs={{0,1},{1,0},{2,3},{3,2},{4,5},{5,4},{6,7},{7,6},{8,9},{9,8},{10,11... | collective-permute-start | bytes 3080 | tf_op jit(solution)/shard_map/ppermute | solution.py:46
  5.6 11.6 %collective-permute-start.4 = (bf16[2,192,128]{2,1,0:T(8,128)(2,1)S(1)}, bf16[2,192,128]{2,1,0:T(8,128)(2,1)S(1)}, u32[]{:S(2)}, u32[]{:S(2)}) collective-permute-start(bf16[2,192,128]{2,1,0:T(8,128)(2,1)S(1)} %pack.1.refs_0_), channel_id=1, source_target_pairs={{0,1},{1,0},{2,3},{3,2},{4,5},{5,4},{6,7},{7,6},{8,9},{9,8},{10,11... | collective-permute-start | bytes 294920 | tf_op jit(solution)/shard_map/ppermute | solution.py:46
  7.7 9.5 %collective-permute-start.3 = (bf16[2,192,128]{2,1,0:T(8,128)(2,1)S(1)}, bf16[2,192,128]{2,1,0:T(8,128)(2,1)S(1)}, u32[]{:S(2)}, u32[]{:S(2)}) collective-permute-start(bf16[2,192,128]{2,1,0:T(8,128)(2,1)S(1)} %pack.1.refs_0_), channel_id=1, source_target_pairs={{0,24},{8,16},{16,8},{24,0},{1,25},{9,17},{17,9},{25,1},{2,26},{10... | collective-permute-start | bytes 294920 | tf_op jit(solution)/shard_map/ppermute | solution.py:46
  11.3 6.9 %collective-permute-start.2 = (bf16[2,192,128]{2,1,0:T(8,128)(2,1)S(1)}, bf16[2,192,128]{2,1,0:T(8,128)(2,1)S(1)}, u32[]{:S(2)}, u32[]{:S(2)}) collective-permute-start(bf16[2,192,128]{2,1,0:T(8,128)(2,1)S(1)} %pack.1.refs_0_), channel_id=1, source_target_pairs={{0,16},{8,24},{16,0},{24,8},{1,17},{9,25},{17,1},{25,9},{2,18},{10... | collective-permute-start | bytes 294920 | tf_op jit(solution)/shard_map/ppermute | solution.py:46
  11.3 6.9 %collective-permute-start.1 = (bf16[2,192,128]{2,1,0:T(8,128)(2,1)S(1)}, bf16[2,192,128]{2,1,0:T(8,128)(2,1)S(1)}, u32[]{:S(2)}, u32[]{:S(2)}) collective-permute-start(bf16[2,192,128]{2,1,0:T(8,128)(2,1)S(1)} %pack.1.refs_0_), channel_id=1, source_target_pairs={{0,8},{8,0},{16,24},{24,16},{1,9},{9,1},{17,25},{25,17},{2,10},{10... | collective-permute-start | bytes 294920 | tf_op jit(solution)/shard_map/ppermute | solution.py:46
  18.3 6.3 %collective-permute-start.8 = (bf16[2,2,208,128]{3,2,1,0:T(8,128)(2,1)S(1)}, bf16[2,2,208,128]{3,2,1,0:T(8,128)(2,1)S(1)}, u32[]{:S(2)}, u32[]{:S(2)}) collective-permute-start(bf16[2,2,208,128]{3,2,1,0:T(8,128)(2,1)S(1)} %get-tuple-element.38), channel_id=1, source_target_pairs={{0,1},{1,0},{2,3},{3,2},{4,5},{5,4},{6,7},{7,6},{8,9},{9,8},{10,11... | collective-permute-start | bytes 638984 | tf_op jit(solution)/shard_map/ppermute | solution.py:46
  18.9 2.3 %collective-permute-start.5 = (bf16[2,2,192,128]{3,2,1,0:T(8,128)(2,1)S(1)}, bf16[2,2,192,128]{3,2,1,0:T(8,128)(2,1)S(1)}, u32[]{:S(2)}, u32[]{:S(2)}) collective-permute-start(bf16[2,2,192,128]{3,2,1,0:T(8,128)(2,1)S(1)} %get-tuple-element.34), channel_id=1, source_target_pairs={{0,2},{2,0},{4,6},{6,4},{1,3},{3,1},{5,7},{7,5},{8,10},{10,8},{12,... | collective-permute-start | bytes 589832 | tf_op jit(solution)/shard_map/ppermute | solution.py:46
  18.9 2.3 %collective-permute-start.6 = (bf16[2,2,192,128]{3,2,1,0:T(8,128)(2,1)S(1)}, bf16[2,2,192,128]{3,2,1,0:T(8,128)(2,1)S(1)}, u32[]{:S(2)}, u32[]{:S(2)}) collective-permute-start(bf16[2,2,192,128]{3,2,1,0:T(8,128)(2,1)S(1)} %get-tuple-element.35), channel_id=1, source_target_pairs={{0,2},{2,0},{4,6},{6,4},{1,3},{3,1},{5,7},{7,5},{8,10},{10,8},{12,... | collective-permute-start | bytes 589832 | tf_op jit(solution)/shard_map/ppermute | solution.py:46
  19.4 4.7 %collective-permute-start.7 = (bf16[2,192,128]{2,1,0:T(8,128)(2,1)S(1)}, bf16[2,192,128]{2,1,0:T(8,128)(2,1)S(1)}, u32[]{:S(2)}, u32[]{:S(2)}) collective-permute-start(bf16[2,192,128]{2,1,0:T(8,128)(2,1)S(1)} %collective-permute-done.4.refs_4_.refs_0_), channel_id=1, source_target_pairs={{0,8},{8,0},{16,24},{24,16},{1,9},{9,1},{17,25},{25,17},{2,10},{10... | collective-permute-start | bytes 294920 | tf_op jit(solution)/shard_map/ppermute | solution.py:46
  24.7 1.8 %collective-permute-start.9 = (bf16[4,2,192,128]{3,2,1,0:T(8,128)(2,1)S(1)}, bf16[4,2,192,128]{3,2,1,0:T(8,128)(2,1)S(1)}, u32[]{:S(2)}, u32[]{:S(2)}) collective-permute-start(bf16[4,2,192,128]{3,2,1,0:T(8,128)(2,1)S(1)} %join.3.refs_0_), channel_id=1, source_target_pairs={{0,2},{2,0},{4,6},{6,4},{1,3},{3,1},{5,7},{7,5},{8,10},{10,8},{12,... | collective-permute-start | bytes 1179656 | tf_op jit(solution)/shard_map/ppermute | solution.py:46
  27.8 1.2 %collective-permute-start.10 = (f32[4,1024]{1,0:T(4,128)S(1)}, f32[4,1024]{1,0:T(4,128)S(1)}, u32[]{:S(2)}, u32[]{:S(2)}) collective-permute-start(f32[4,1024]{1,0:T(4,128)S(1)} %get-tuple-element.42.refs_0_), channel_id=1, source_target_pairs={{0,2},{2,0},{4,6},{6,4},{1,3},{3,1},{5,7},{7,5},{8,10},{10,8},{12,... | collective-permute-start | bytes 49160 | tf_op jit(solution)/shard_map/ppermute | solution.py:46
  29.1 3.8 %collective-permute-start.11 = (f32[4,1024]{1,0:T(4,128)S(1)}, f32[4,1024]{1,0:T(4,128)S(1)}, u32[]{:S(2)}, u32[]{:S(2)}) collective-permute-start(f32[4,1024]{1,0:T(4,128)S(1)} %relay.3.refs_0_), channel_id=1, source_target_pairs={{0,1},{1,0},{2,6},{3,7},{4,5},{5,4},{6,2},{7,3},{8,9},{9,8},{10,14... | collective-permute-start | bytes 49160 | tf_op jit(solution)/shard_map/ppermute | solution.py:307
  30.1 4.6 %collective-permute-start.13 = (f32[4,1024]{1,0:T(4,128)S(1)}, f32[4,1024]{1,0:T(4,128)S(1)}, u32[]{:S(2)}, u32[]{:S(2)}) collective-permute-start(f32[4,1024]{1,0:T(4,128)S(1)} %relay.3.refs_0_), channel_id=1, source_target_pairs={{0,5},{1,4},{2,7},{3,6},{4,1},{5,0},{6,3},{7,2},{8,13},{9,12},{10,... | collective-permute-start | bytes 49160 | tf_op jit(solution)/shard_map/ppermute | solution.py:307
  32.9 1.9 %collective-permute-start.12 = (f32[4,1024]{1,0:T(4,128)S(1)}, f32[4,1024]{1,0:T(4,128)S(1)}, u32[]{:S(2)}, u32[]{:S(2)}) collective-permute-start(f32[4,1024]{1,0:T(4,128)S(1)} %collective-permute-done.11.refs_1_), channel_id=1, source_target_pairs={{0,2},{2,0},{4,6},{6,4},{1,3},{3,1},{5,7},{7,5},{8,10},{10,8},{12,... | collective-permute-start | bytes 49160 | tf_op jit(solution)/shard_map/ppermute | solution.py:46
  34.8 3.8 %collective-permute-start.14 = (f32[4,1024]{1,0:T(4,128)S(1)}, f32[4,1024]{1,0:T(4,128)S(1)}, u32[]{:S(2)}, u32[]{:S(2)}) collective-permute-start(f32[4,1024]{1,0:T(4,128)S(1)} %relay.4.refs_0_), channel_id=1, source_target_pairs={{0,8},{2,18},{4,12},{6,22},{8,0},{10,26},{12,4},{14,30},{16,24},{1... | collective-permute-start | bytes 49160 | tf_op jit(solution)/shard_map/ppermute | solution.py:307
  35.3 5.5 %collective-permute-start.16 = (f32[4,1024]{1,0:T(4,128)S(1)}, f32[4,1024]{1,0:T(4,128)S(1)}, u32[]{:S(2)}, u32[]{:S(2)}) collective-permute-start(f32[4,1024]{1,0:T(4,128)S(1)} %relay.4.refs_0_), channel_id=1, source_target_pairs={{0,24},{2,26},{4,28},{6,30},{8,16},{10,18},{12,20},{14,22},{16,8},... | collective-permute-start | bytes 49160 | tf_op jit(solution)/shard_map/ppermute | solution.py:307
  38.6 2.2 %collective-permute-start.15 = (f32[4,1024]{1,0:T(4,128)S(1)}, f32[4,1024]{1,0:T(4,128)S(1)}, u32[]{:S(2)}, u32[]{:S(2)}) collective-permute-start(f32[4,1024]{1,0:T(4,128)S(1)} %collective-permute-done.14.refs_1_), channel_id=1, source_target_pairs={{0,2},{2,0},{4,6},{6,4},{1,3},{3,1},{5,7},{7,5},{8,10},{10,8},{12,... | collective-permute-start | bytes 49160 | tf_op jit(solution)/shard_map/ppermute | solution.py:46

commit v23 on v21

--- a/solution.py
+++ b/solution.py
@@ -11,7 +11,7 @@
 EPS = 1e-06
 DEPTH = 256
 GROUP = 512
-STEP = 256
+STEP = 512
 DIRECT = 8
 LOG2E = math.log2(math.e)
 GAIN_T = LOG2E / 0.04

time: 43.8 us -> 43.7 us (level)
  no operation moved by 1% of the time
where the time goes in v23:
time: 43.7 us; the launch traced here: 43.6 us
  starting transfers between devices  16.9 us (39%)
  Pallas kernels  15.2 us (35%)
  waiting for transfers between devices  10.7 us (24%)
  between operations  0.75 us (2%)
    pallas_call x13, Pallas kernels, call(): pl.pallas_call(kernel, out_shape=out_shape, compiler_params=pltpu.Compile...  15.2 us
    ppermute x13, starting transfers between devices, swap(): lax.ppermute(block, axis, [(i, i ^ apart) for i in range(lax.axis_size(ax...  11.3 us
    ppermute x13, waiting for transfers between devices, swap(): lax.ppermute(block, axis, [(i, i ^ apart) for i in range(lax.axis_size(ax...  6.3 us
    ppermute x4, starting transfers between devices, permute(): return lax.ppermute(total, axes, pairs)  5.63 us
    ppermute x4, waiting for transfers between devices, permute(): return lax.ppermute(total, axes, pairs)  4.42 us
  transfers between devices with their start and end apart: 17, of which 12 were waited for; matrix products, arithmetic and copies ran while one was open for 0% of the time, Pallas kernels for 23%

profile of v23, /device:TPU:0, one launch (start us, length us, event | category | flops | bytes accessed | tf_op | source)
XLA Modules:
  0.0 43.6 jit_solution(6785528770250477608)
XLA Ops:
  0.6 3.0 %collective-permute-start = (s32[1,256]{1,0:T(1,128)}, s32[1,256]{1,0:T(1,128)S(1)}, u32[]{:S(2)}, u32[]{:S(2)}) collective-permute-start(s32[1,256]{1,0:T(1,128)} %param.10), channel_id=1, source_target_pairs={{0,1},{1,0},{2,3},{3,2},{4,5},{5,4},{6,7},{7,6},{8,9},{9,8},{10,11... | collective-permute-start | bytes 3080 | tf_op jit(solution)/shard_map/ppermute | solution.py:46
  3.6 0.9 %fetch.1 = (bf16[192,128]{1,0:T(8,128)(2,1)S(1)}, bf16[192,256]{1,0:T(8,128)(2,1)S(1)}) custom-call(bf16[192,256]{1,0:T(8,128)(2,1)} %bitcast.7, bf16[192,256]{1,0:T(8,128)(2,1)} %bitcast.8), custom_call_target="tpu_custom_call" | custom-call | flops 1 | bytes 1 | tf_op jit(solution)/shard_map/fetch/pallas_call | solution.py:35
  4.6 0.8 %collective-permute-done.index_ref = s32[1,256]{1,0:T(1,128)S(1)} collective-permute-done((s32[1,256]{1,0:T(1,128)}, s32[1,256]{1,0:T(1,128)S(1)}, u32[]{:S(2)}, u32[]{:S(2)}) %collective-permute-start) | collective-permute-done | bytes 1056 | tf_op jit(solution)/shard_map/ppermute | solution.py:46
  5.6 2.1 %collective-permute-start.4 = (bf16[2,192,128]{2,1,0:T(8,128)(2,1)S(1)}, bf16[2,192,128]{2,1,0:T(8,128)(2,1)S(1)}, u32[]{:S(2)}, u32[]{:S(2)}) collective-permute-start(bf16[2,192,128]{2,1,0:T(8,128)(2,1)S(1)} %pack.1.refs_0_), channel_id=1, source_target_pairs={{0,1},{1,0},{2,3},{3,2},{4,5},{5,4},{6,7},{7,6},{8,9},{9,8},{10,11... | collective-permute-start | bytes 294920 | tf_op jit(solution)/shard_map/ppermute | solution.py:46
  7.7 3.6 %collective-permute-start.3 = (bf16[2,192,128]{2,1,0:T(8,128)(2,1)S(1)}, bf16[2,192,128]{2,1,0:T(8,128)(2,1)S(1)}, u32[]{:S(2)}, u32[]{:S(2)}) collective-permute-start(bf16[2,192,128]{2,1,0:T(8,128)(2,1)S(1)} %pack.1.refs_0_), channel_id=1, source_target_pairs={{0,24},{8,16},{16,8},{24,0},{1,25},{9,17},{17,9},{25,1},{2,26},{10... | collective-permute-start | bytes 294920 | tf_op jit(solution)/shard_map/ppermute | solution.py:46
  11.3 0.8 %collective-permute-start.1 = (bf16[2,192,128]{2,1,0:T(8,128)(2,1)S(1)}, bf16[2,192,128]{2,1,0:T(8,128)(2,1)S(1)}, u32[]{:S(2)}, u32[]{:S(2)}) collective-permute-start(bf16[2,192,128]{2,1,0:T(8,128)(2,1)S(1)} %pack.1.refs_0_), channel_id=1, source_target_pairs={{0,8},{8,0},{16,24},{24,16},{1,9},{9,1},{17,25},{25,17},{2,10},{10... | collective-permute-start | bytes 294920 | tf_op jit(solution)/shard_map/ppermute | solution.py:46
  12.1 5.1 %prep.1 = (f32[192,4096]{1,0:T(8,128)}, bf16[2048,256]{1,0:T(8,128)(2,1)S(1)}, bf16[2048,256]{1,0:T(8,128)(2,1)S(1)}, f32[192,2048]{1,0:T(8,128)S(1)}, f32[1,2048]{1,0:T(1,128)S(1)}, /*index=5*/f32[1,128]{1,0:T(1,128)S(1)}) custom-call(f32[192,4096]{1,0:T(8,128)} %teacher_hbm.1, f32[192,4096]{1,0:T(8,128)} %student_hbm.1, f32[1,16384]{1,0:T(1,128)} %bitcast.9), custom_call_target="tpu_custom_call" | custom-call | flops 1 | bytes 1 | tf_op jit(solution)/shard_map/prep/pallas_call | solution.py:35
  17.2 1.0 %collective-permute-done.2.refs_2_ = bf16[2,192,128]{2,1,0:T(8,128)(2,1)S(1)} collective-permute-done((bf16[2,192,128]{2,1,0:T(8,128)(2,1)S(1)}, bf16[2,192,128]{2,1,0:T(8,128)(2,1)S(1)}, u32[]{:S(2)}, u32[]{:S(2)}) %collective-permute-start.2) | collective-permute-done | bytes 98336 | tf_op jit(solution)/shard_map/ppermute | solution.py:46
  18.3 0.6 %collective-permute-start.8 = (bf16[2,2,208,128]{3,2,1,0:T(8,128)(2,1)S(1)}, bf16[2,2,208,128]{3,2,1,0:T(8,128)(2,1)S(1)}, u32[]{:S(2)}, u32[]{:S(2)}) collective-permute-start(bf16[2,2,208,128]{3,2,1,0:T(8,128)(2,1)S(1)} %get-tuple-element.38), channel_id=1, source_target_pairs={{0,1},{1,0},{2,3},{3,2},{4,5},{5,4},{6,7},{7,6},{8,9},{9,8},{10,11... | collective-permute-start | bytes 638984 | tf_op jit(solution)/shard_map/ppermute | solution.py:46
  19.9 1.3 %scores.4 = (bf16[2048,4096]{1,0:T(8,128)(2,1)S(1)}, bf16[512,192]{1,0:T(8,128)(2,1)S(1)}, f32[2,512]{1,0:T(2,128)S(1)}) custom-call(bf16[4,2,192,128]{3,2,1,0:T(8,128)(2,1)S(1)} %get-tuple-element.30.refs_0_, bf16[2048,256]{1,0:T(8,128)(2,1)S(1)} %get-tuple-element.31.refs_1_.refs_2_.refs_4_, ...), custom_call_target="tpu_custom_call" | custom-call | flops 1 | bytes 1 | tf_op jit(solution)/shard_map/scores/pallas_call | solution.py:35
  21.2 1.3 %scores.5 = (bf16[2048,4096]{1,0:T(8,128)(2,1)S(1)}, bf16[512,192]{1,0:T(8,128)(2,1)S(1)}, f32[2,512]{1,0:T(2,128)S(1)}) custom-call(bf16[2,2,192,128]{3,2,1,0:T(8,128)(2,1)S(1)} %collective-permute-done.5.refs_0_, bf16[2,2,192,128]{3,2,1,0:T(8,128)(2,1)S(1)} %collective-permute-done.6.refs_1_, ...), custom_call_target="tpu_custom_call", output_to_operand_aliasing={{0}: (5, {})} | custom-call | flops 1 | bytes 1 | tf_op jit(solution)/shard_map/scores/pallas_call | solution.py:35
  22.5 1.6 %collective-permute-done.7.refs_1_ = bf16[2,192,128]{2,1,0:T(8,128)(2,1)S(1)} collective-permute-done((bf16[2,192,128]{2,1,0:T(8,128)(2,1)S(1)}, bf16[2,192,128]{2,1,0:T(8,128)(2,1)S(1)}, u32[]{:S(2)}, u32[]{:S(2)}) %collective-permute-start.7) | collective-permute-done | bytes 98336 | tf_op jit(solution)/shard_map/ppermute | solution.py:46
  24.8 1.3 %scores.6 = (bf16[2048,4096]{1,0:T(8,128)(2,1)S(1)}, bf16[512,192]{1,0:T(8,128)(2,1)S(1)}, f32[2,512]{1,0:T(2,128)S(1)}) custom-call(bf16[4,2,192,128]{3,2,1,0:T(8,128)(2,1)S(1)} %join.3.refs_0_, bf16[2048,256]{1,0:T(8,128)(2,1)S(1)} %get-tuple-element.31.refs_1_.refs_2_.refs_4_, ...), custom_call_target="tpu_custom_call", output_to_operand_aliasing={{0}: (4, {})} | custom-call | flops 1 | bytes 1 | tf_op jit(solution)/shard_map/scores/pallas_call | solution.py:35
  26.5 1.3 %scores.7 = (bf16[2048,4096]{1,0:T(8,128)(2,1)S(1)}, bf16[512,192]{1,0:T(8,128)(2,1)S(1)}, f32[4,1024]{1,0:T(4,128)S(1)}) custom-call(f32[2,512]{1,0:T(2,128)S(1)} %get-tuple-element.33.refs_0_, f32[2,512]{1,0:T(2,128)S(1)} %get-tuple-element.37.refs_3_.refs_1_, f32[2,512]{1,0:T(2,128)S(1)} %get-tuple-element.40.refs_2_, ...), custom_call_target="tpu_custom_call", output_to_operand_aliasing={{0}: (7, {})} | custom-call | flops 1 | bytes 1 | tf_op jit(solution)/shard_map/scores/pallas_call | solution.py:35
  28.0 1.0 %collective-permute-done.10.refs_1_ = f32[4,1024]{1,0:T(4,128)S(1)} collective-permute-done((f32[4,1024]{1,0:T(4,128)S(1)}, f32[4,1024]{1,0:T(4,128)S(1)}, u32[]{:S(2)}, u32[]{:S(2)}) %collective-permute-start.10) | collective-permute-done | bytes 16416 | tf_op jit(solution)/shard_map/ppermute | solution.py:46
  29.1 1.0 %collective-permute-start.11 = (f32[4,1024]{1,0:T(4,128)S(1)}, f32[4,1024]{1,0:T(4,128)S(1)}, u32[]{:S(2)}, u32[]{:S(2)}) collective-permute-start(f32[4,1024]{1,0:T(4,128)S(1)} %relay.3.refs_0_), channel_id=1, source_target_pairs={{0,1},{1,0},{2,7},{3,6},{4,5},{5,4},{6,3},{7,2},{8,9},{9,8},{10,15... | collective-permute-start | bytes 49160 | tf_op jit(solution)/shard_map/ppermute | solution.py:307
  30.1 1.5 %collective-permute-start.13 = (f32[4,1024]{1,0:T(4,128)S(1)}, f32[4,1024]{1,0:T(4,128)S(1)}, u32[]{:S(2)}, u32[]{:S(2)}) collective-permute-start(f32[4,1024]{1,0:T(4,128)S(1)} %relay.3.refs_0_), channel_id=1, source_target_pairs={{0,4},{1,5},{2,6},{3,7},{4,0},{5,1},{6,2},{7,3},{8,12},{9,13},{10,... | collective-permute-start | bytes 49160 | tf_op jit(solution)/shard_map/ppermute | solution.py:307
  31.6 1.3 %collective-permute-done.11.refs_1_ = f32[4,1024]{1,0:T(4,128)S(1)} collective-permute-done((f32[4,1024]{1,0:T(4,128)S(1)}, f32[4,1024]{1,0:T(4,128)S(1)}, u32[]{:S(2)}, u32[]{:S(2)}) %collective-permute-start.11) | collective-permute-done | bytes 16416 | tf_op jit(solution)/shard_map/ppermute | solution.py:307
  32.9 1.0 %collective-permute-done.13.refs_3_ = f32[4,1024]{1,0:T(4,128)S(1)} collective-permute-done((f32[4,1024]{1,0:T(4,128)S(1)}, f32[4,1024]{1,0:T(4,128)S(1)}, u32[]{:S(2)}, u32[]{:S(2)}) %collective-permute-start.13) | collective-permute-done | bytes 16416 | tf_op jit(solution)/shard_map/ppermute | solution.py:307
  34.1 1.3 %collective-permute-start.14 = (f32[4,1024]{1,0:T(4,128)S(1)}, f32[4,1024]{1,0:T(4,128)S(1)}, u32[]{:S(2)}, u32[]{:S(2)}) collective-permute-start(f32[4,1024]{1,0:T(4,128)S(1)} %relay.4.refs_0_), channel_id=1, source_target_pairs={{0,16},{2,26},{4,20},{6,30},{8,24},{10,18},{12,28},{14,22},{16,0},... | collective-permute-start | bytes 49160 | tf_op jit(solution)/shard_map/ppermute | solution.py:307
  35.4 1.7 %collective-permute-start.16 = (f32[4,1024]{1,0:T(4,128)S(1)}, f32[4,1024]{1,0:T(4,128)S(1)}, u32[]{:S(2)}, u32[]{:S(2)}) collective-permute-start(f32[4,1024]{1,0:T(4,128)S(1)} %relay.4.refs_0_), channel_id=1, source_target_pairs={{0,8},{2,10},{4,12},{6,14},{8,0},{10,2},{12,4},{14,6},{16,24},{18,... | collective-permute-start | bytes 49160 | tf_op jit(solution)/shard_map/ppermute | solution.py:307
  37.2 1.6 %collective-permute-done.14.refs_1_ = f32[4,1024]{1,0:T(4,128)S(1)} collective-permute-done((f32[4,1024]{1,0:T(4,128)S(1)}, f32[4,1024]{1,0:T(4,128)S(1)}, u32[]{:S(2)}, u32[]{:S(2)}) %collective-permute-start.14) | collective-permute-done | bytes 16416 | tf_op jit(solution)/shard_map/ppermute | solution.py:307
  39.4 0.7 %collective-permute-done.15.refs_2_ = f32[4,1024]{1,0:T(4,128)S(1)} collective-permute-done((f32[4,1024]{1,0:T(4,128)S(1)}, f32[4,1024]{1,0:T(4,128)S(1)}, u32[]{:S(2)}, u32[]{:S(2)}) %collective-permute-start.15) | collective-permute-done | bytes 16416 | tf_op jit(solution)/shard_map/ppermute | solution.py:46
  40.1 3.5 %gradient.1 = f32[192,2048]{1,0:T(8,128)} custom-call(f32[4,1024]{1,0:T(4,128)S(1)} %relay.5.total_ref, f32[1,128]{1,0:T(1,128)S(1)} %get-tuple-element.29.refs_5_.refs_3_.refs_4_.refs_6_.peak_ref, f32[192,2048]{1,0:T(8,128)S(1)} %get-tuple-element.43.weight_unit, f32[1,2048]{1,0:T(1,128)S(1)} %get-tuple-element.44.weight_scale, ...), custom_call_target="tpu_custom_call" | custom-call | flops 1 | bytes 1 | tf_op jit(solution)/shard_map/gradient/pallas_call | solution.py:35
  (23 shorter events, 3.3 us)
Async XLA Ops:
  0.6 4.8 %collective-permute-start = (s32[1,256]{1,0:T(1,128)}, s32[1,256]{1,0:T(1,128)S(1)}, u32[]{:S(2)}, u32[]{:S(2)}) collective-permute-start(s32[1,256]{1,0:T(1,128)} %param.10), channel_id=1, source_target_pairs={{0,1},{1,0},{2,3},{3,2},{4,5},{5,4},{6,7},{7,6},{8,9},{9,8},{10,11... | collective-permute-start | bytes 3080 | tf_op jit(solution)/shard_map/ppermute | solution.py:46
  5.6 11.6 %collective-permute-start.4 = (bf16[2,192,128]{2,1,0:T(8,128)(2,1)S(1)}, bf16[2,192,128]{2,1,0:T(8,128)(2,1)S(1)}, u32[]{:S(2)}, u32[]{:S(2)}) collective-permute-start(bf16[2,192,128]{2,1,0:T(8,128)(2,1)S(1)} %pack.1.refs_0_), channel_id=1, source_target_pairs={{0,1},{1,0},{2,3},{3,2},{4,5},{5,4},{6,7},{7,6},{8,9},{9,8},{10,11... | collective-permute-start | bytes 294920 | tf_op jit(solution)/shard_map/ppermute | solution.py:46
  7.7 9.5 %collective-permute-start.3 = (bf16[2,192,128]{2,1,0:T(8,128)(2,1)S(1)}, bf16[2,192,128]{2,1,0:T(8,128)(2,1)S(1)}, u32[]{:S(2)}, u32[]{:S(2)}) collective-permute-start(bf16[2,192,128]{2,1,0:T(8,128)(2,1)S(1)} %pack.1.refs_0_), channel_id=1, source_target_pairs={{0,24},{8,16},{16,8},{24,0},{1,25},{9,17},{17,9},{25,1},{2,26},{10... | collective-permute-start | bytes 294920 | tf_op jit(solution)/shard_map/ppermute | solution.py:46
  11.3 6.9 %collective-permute-start.2 = (bf16[2,192,128]{2,1,0:T(8,128)(2,1)S(1)}, bf16[2,192,128]{2,1,0:T(8,128)(2,1)S(1)}, u32[]{:S(2)}, u32[]{:S(2)}) collective-permute-start(bf16[2,192,128]{2,1,0:T(8,128)(2,1)S(1)} %pack.1.refs_0_), channel_id=1, source_target_pairs={{0,16},{8,24},{16,0},{24,8},{1,17},{9,25},{17,1},{25,9},{2,18},{10... | collective-permute-start | bytes 294920 | tf_op jit(solution)/shard_map/ppermute | solution.py:46
  11.3 6.9 %collective-permute-start.1 = (bf16[2,192,128]{2,1,0:T(8,128)(2,1)S(1)}, bf16[2,192,128]{2,1,0:T(8,128)(2,1)S(1)}, u32[]{:S(2)}, u32[]{:S(2)}) collective-permute-start(bf16[2,192,128]{2,1,0:T(8,128)(2,1)S(1)} %pack.1.refs_0_), channel_id=1, source_target_pairs={{0,8},{8,0},{16,24},{24,16},{1,9},{9,1},{17,25},{25,17},{2,10},{10... | collective-permute-start | bytes 294920 | tf_op jit(solution)/shard_map/ppermute | solution.py:46
  18.3 6.3 %collective-permute-start.8 = (bf16[2,2,208,128]{3,2,1,0:T(8,128)(2,1)S(1)}, bf16[2,2,208,128]{3,2,1,0:T(8,128)(2,1)S(1)}, u32[]{:S(2)}, u32[]{:S(2)}) collective-permute-start(bf16[2,2,208,128]{3,2,1,0:T(8,128)(2,1)S(1)} %get-tuple-element.38), channel_id=1, source_target_pairs={{0,1},{1,0},{2,3},{3,2},{4,5},{5,4},{6,7},{7,6},{8,9},{9,8},{10,11... | collective-permute-start | bytes 638984 | tf_op jit(solution)/shard_map/ppermute | solution.py:46
  18.9 2.2 %collective-permute-start.5 = (bf16[2,2,192,128]{3,2,1,0:T(8,128)(2,1)S(1)}, bf16[2,2,192,128]{3,2,1,0:T(8,128)(2,1)S(1)}, u32[]{:S(2)}, u32[]{:S(2)}) collective-permute-start(bf16[2,2,192,128]{3,2,1,0:T(8,128)(2,1)S(1)} %get-tuple-element.34), channel_id=1, source_target_pairs={{0,2},{2,0},{4,6},{6,4},{1,3},{3,1},{5,7},{7,5},{8,10},{10,8},{12,... | collective-permute-start | bytes 589832 | tf_op jit(solution)/shard_map/ppermute | solution.py:46
  18.9 2.3 %collective-permute-start.6 = (bf16[2,2,192,128]{3,2,1,0:T(8,128)(2,1)S(1)}, bf16[2,2,192,128]{3,2,1,0:T(8,128)(2,1)S(1)}, u32[]{:S(2)}, u32[]{:S(2)}) collective-permute-start(bf16[2,2,192,128]{3,2,1,0:T(8,128)(2,1)S(1)} %get-tuple-element.35), channel_id=1, source_target_pairs={{0,2},{2,0},{4,6},{6,4},{1,3},{3,1},{5,7},{7,5},{8,10},{10,8},{12,... | collective-permute-start | bytes 589832 | tf_op jit(solution)/shard_map/ppermute | solution.py:46
  19.4 4.7 %collective-permute-start.7 = (bf16[2,192,128]{2,1,0:T(8,128)(2,1)S(1)}, bf16[2,192,128]{2,1,0:T(8,128)(2,1)S(1)}, u32[]{:S(2)}, u32[]{:S(2)}) collective-permute-start(bf16[2,192,128]{2,1,0:T(8,128)(2,1)S(1)} %collective-permute-done.4.refs_4_.refs_0_), channel_id=1, source_target_pairs={{0,8},{8,0},{16,24},{24,16},{1,9},{9,1},{17,25},{25,17},{2,10},{10... | collective-permute-start | bytes 294920 | tf_op jit(solution)/shard_map/ppermute | solution.py:46
  24.7 1.8 %collective-permute-start.9 = (bf16[4,2,192,128]{3,2,1,0:T(8,128)(2,1)S(1)}, bf16[4,2,192,128]{3,2,1,0:T(8,128)(2,1)S(1)}, u32[]{:S(2)}, u32[]{:S(2)}) collective-permute-start(bf16[4,2,192,128]{3,2,1,0:T(8,128)(2,1)S(1)} %join.3.refs_0_), channel_id=1, source_target_pairs={{0,2},{2,0},{4,6},{6,4},{1,3},{3,1},{5,7},{7,5},{8,10},{10,8},{12,... | collective-permute-start | bytes 1179656 | tf_op jit(solution)/shard_map/ppermute | solution.py:46
  27.8 1.2 %collective-permute-start.10 = (f32[4,1024]{1,0:T(4,128)S(1)}, f32[4,1024]{1,0:T(4,128)S(1)}, u32[]{:S(2)}, u32[]{:S(2)}) collective-permute-start(f32[4,1024]{1,0:T(4,128)S(1)} %get-tuple-element.42.refs_0_), channel_id=1, source_target_pairs={{0,2},{2,0},{4,6},{6,4},{1,3},{3,1},{5,7},{7,5},{8,10},{10,8},{12,... | collective-permute-start | bytes 49160 | tf_op jit(solution)/shard_map/ppermute | solution.py:46
  29.1 3.8 %collective-permute-start.11 = (f32[4,1024]{1,0:T(4,128)S(1)}, f32[4,1024]{1,0:T(4,128)S(1)}, u32[]{:S(2)}, u32[]{:S(2)}) collective-permute-start(f32[4,1024]{1,0:T(4,128)S(1)} %relay.3.refs_0_), channel_id=1, source_target_pairs={{0,1},{1,0},{2,7},{3,6},{4,5},{5,4},{6,3},{7,2},{8,9},{9,8},{10,15... | collective-permute-start | bytes 49160 | tf_op jit(solution)/shard_map/ppermute | solution.py:307
  30.1 3.8 %collective-permute-start.13 = (f32[4,1024]{1,0:T(4,128)S(1)}, f32[4,1024]{1,0:T(4,128)S(1)}, u32[]{:S(2)}, u32[]{:S(2)}) collective-permute-start(f32[4,1024]{1,0:T(4,128)S(1)} %relay.3.refs_0_), channel_id=1, source_target_pairs={{0,4},{1,5},{2,6},{3,7},{4,0},{5,1},{6,2},{7,3},{8,12},{9,13},{10,... | collective-permute-start | bytes 49160 | tf_op jit(solution)/shard_map/ppermute | solution.py:307
  32.9 1.2 %collective-permute-start.12 = (f32[4,1024]{1,0:T(4,128)S(1)}, f32[4,1024]{1,0:T(4,128)S(1)}, u32[]{:S(2)}, u32[]{:S(2)}) collective-permute-start(f32[4,1024]{1,0:T(4,128)S(1)} %collective-permute-done.11.refs_1_), channel_id=1, source_target_pairs={{0,2},{2,0},{4,6},{6,4},{1,3},{3,1},{5,7},{7,5},{8,10},{10,8},{12,... | collective-permute-start | bytes 49160 | tf_op jit(solution)/shard_map/ppermute | solution.py:46
  34.1 4.7 %collective-permute-start.14 = (f32[4,1024]{1,0:T(4,128)S(1)}, f32[4,1024]{1,0:T(4,128)S(1)}, u32[]{:S(2)}, u32[]{:S(2)}) collective-permute-start(f32[4,1024]{1,0:T(4,128)S(1)} %relay.4.refs_0_), channel_id=1, source_target_pairs={{0,16},{2,26},{4,20},{6,30},{8,24},{10,18},{12,28},{14,22},{16,0},... | collective-permute-start | bytes 49160 | tf_op jit(solution)/shard_map/ppermute | solution.py:307
  35.4 3.9 %collective-permute-start.16 = (f32[4,1024]{1,0:T(4,128)S(1)}, f32[4,1024]{1,0:T(4,128)S(1)}, u32[]{:S(2)}, u32[]{:S(2)}) collective-permute-start(f32[4,1024]{1,0:T(4,128)S(1)} %relay.4.refs_0_), channel_id=1, source_target_pairs={{0,8},{2,10},{4,12},{6,14},{8,0},{10,2},{12,4},{14,6},{16,24},{18,... | collective-permute-start | bytes 49160 | tf_op jit(solution)/shard_map/ppermute | solution.py:307
  38.8 1.2 %collective-permute-start.15 = (f32[4,1024]{1,0:T(4,128)S(1)}, f32[4,1024]{1,0:T(4,128)S(1)}, u32[]{:S(2)}, u32[]{:S(2)}) collective-permute-start(f32[4,1024]{1,0:T(4,128)S(1)} %collective-permute-done.14.refs_1_), channel_id=1, source_target_pairs={{0,2},{2,0},{4,6},{6,4},{1,3},{3,1},{5,7},{7,5},{8,10},{10,8},{12,... | collective-permute-start | bytes 49160 | tf_op jit(solution)/shard_map/ppermute | solution.py:46

commit v24 on v21

--- a/solution.py
+++ b/solution.py
@@ -317,9 +317,12 @@
     return lax.ppermute(total, ("proto", "dp"), pairs)
 
 
-def add_up_chip_and_across(total):
+def add_up_chip(total):
+    return add_up([total, swap(total, "proto")])
+
+
+def add_up_across(total):
     n_proto, n_dp = lax.axis_size("proto"), lax.axis_size("dp")
-    total = add_up([total, swap(total, "proto")])
     if n_proto == 4 and n_dp == 2:
         return exchange(total, ("proto", "dp"), lambda odd: (2 * odd, 1), lambda odd: (2, 0))
     steps = [(up, over) for up in range(0, n_proto, 2) for over in range(n_dp)][1:]
@@ -428,8 +431,7 @@
     (other,) = join(other, [(0, n_fsdp, bot)], (total_b,), bot)
     exps, unit_c, total_c = scores(2, [other], weights, exps=exps)
     exps, unit_d, total = scores(3, [swap(other, "proto")], weights, (total_a, total_b, total_c), exps)
-    total = add_up_chip_and_across(total)
-    total = add_up_along(total)
+    total = add_up_across(add_up_along(add_up_chip(total)))
     units = (unit_a, unit_b, unit_c, unit_d)
     student_grad = gradient(total, peak, unit, scale, units, exps)
     return (teacher_new, student_grad)

time: 43.8 us -> 43.8 us (level)
  transfers between devices with their start and end apart: 17 -> 17, of which waited for: 12 -> 11; matrix products, arithmetic and copies ran while one was open for 0% -> 0% of each run, Pallas kernels for 23% -> 23%
where the time goes in v24:
time: 43.8 us; the launch traced here: 43.6 us
  starting transfers between devices  16.9 us (39%)
  Pallas kernels  15.2 us (35%)
  waiting for transfers between devices  10.8 us (25%)
  between operations  0.75 us (2%)
    pallas_call x13, Pallas kernels, call(): pl.pallas_call(kernel, out_shape=out_shape, compiler_params=pltpu.Compile...  15.2 us
    ppermute x13, starting transfers between devices, swap(): lax.ppermute(block, axis, [(i, i ^ apart) for i in range(lax.axis_size(ax...  11.3 us
    ppermute x13, waiting for transfers between devices, swap(): lax.ppermute(block, axis, [(i, i ^ apart) for i in range(lax.axis_size(ax...  6.12 us
    ppermute x4, starting transfers between devices, permute(): return lax.ppermute(total, axes, pairs)  5.58 us
    ppermute x4, waiting for transfers between devices, permute(): return lax.ppermute(total, axes, pairs)  4.65 us
  transfers between devices with their start and end apart: 17, of which 11 were waited for; matrix products, arithmetic and copies ran while one was open for 0% of the time, Pallas kernels for 23%

profile of v24, /device:TPU:0, one launch (start us, length us, event | category | flops | bytes accessed | tf_op | source)
XLA Modules:
  0.0 43.6 jit_solution(2875282571915330252)
XLA Ops:
  0.6 3.0 %collective-permute-start = (s32[1,256]{1,0:T(1,128)}, s32[1,256]{1,0:T(1,128)S(1)}, u32[]{:S(2)}, u32[]{:S(2)}) collective-permute-start(s32[1,256]{1,0:T(1,128)} %param.10), channel_id=1, source_target_pairs={{0,1},{1,0},{2,3},{3,2},{4,5},{5,4},{6,7},{7,6},{8,9},{9,8},{10,11... | collective-permute-start | bytes 3080 | tf_op jit(solution)/shard_map/ppermute | solution.py:46
  3.6 0.9 %fetch.1 = (bf16[192,128]{1,0:T(8,128)(2,1)S(1)}, bf16[192,256]{1,0:T(8,128)(2,1)S(1)}) custom-call(bf16[192,256]{1,0:T(8,128)(2,1)} %bitcast.7, bf16[192,256]{1,0:T(8,128)(2,1)} %bitcast.8), custom_call_target="tpu_custom_call" | custom-call | flops 1 | bytes 1 | tf_op jit(solution)/shard_map/fetch/pallas_call | solution.py:35
  4.6 0.8 %collective-permute-done.index_ref = s32[1,256]{1,0:T(1,128)S(1)} collective-permute-done((s32[1,256]{1,0:T(1,128)}, s32[1,256]{1,0:T(1,128)S(1)}, u32[]{:S(2)}, u32[]{:S(2)}) %collective-permute-start) | collective-permute-done | bytes 1056 | tf_op jit(solution)/shard_map/ppermute | solution.py:46
  5.6 2.1 %collective-permute-start.4 = (bf16[2,192,128]{2,1,0:T(8,128)(2,1)S(1)}, bf16[2,192,128]{2,1,0:T(8,128)(2,1)S(1)}, u32[]{:S(2)}, u32[]{:S(2)}) collective-permute-start(bf16[2,192,128]{2,1,0:T(8,128)(2,1)S(1)} %pack.1.refs_0_), channel_id=1, source_target_pairs={{0,1},{1,0},{2,3},{3,2},{4,5},{5,4},{6,7},{7,6},{8,9},{9,8},{10,11... | collective-permute-start | bytes 294920 | tf_op jit(solution)/shard_map/ppermute | solution.py:46
  7.7 3.6 %collective-permute-start.3 = (bf16[2,192,128]{2,1,0:T(8,128)(2,1)S(1)}, bf16[2,192,128]{2,1,0:T(8,128)(2,1)S(1)}, u32[]{:S(2)}, u32[]{:S(2)}) collective-permute-start(bf16[2,192,128]{2,1,0:T(8,128)(2,1)S(1)} %pack.1.refs_0_), channel_id=1, source_target_pairs={{0,24},{8,16},{16,8},{24,0},{1,25},{9,17},{17,9},{25,1},{2,26},{10... | collective-permute-start | bytes 294920 | tf_op jit(solution)/shard_map/ppermute | solution.py:46
  11.3 0.8 %collective-permute-start.1 = (bf16[2,192,128]{2,1,0:T(8,128)(2,1)S(1)}, bf16[2,192,128]{2,1,0:T(8,128)(2,1)S(1)}, u32[]{:S(2)}, u32[]{:S(2)}) collective-permute-start(bf16[2,192,128]{2,1,0:T(8,128)(2,1)S(1)} %pack.1.refs_0_), channel_id=1, source_target_pairs={{0,8},{8,0},{16,24},{24,16},{1,9},{9,1},{17,25},{25,17},{2,10},{10... | collective-permute-start | bytes 294920 | tf_op jit(solution)/shard_map/ppermute | solution.py:46
  12.1 5.1 %prep.1 = (f32[192,4096]{1,0:T(8,128)}, bf16[2048,256]{1,0:T(8,128)(2,1)S(1)}, bf16[2048,256]{1,0:T(8,128)(2,1)S(1)}, f32[192,2048]{1,0:T(8,128)S(1)}, f32[1,2048]{1,0:T(1,128)S(1)}, /*index=5*/f32[1,128]{1,0:T(1,128)S(1)}) custom-call(f32[192,4096]{1,0:T(8,128)} %teacher_hbm.1, f32[192,4096]{1,0:T(8,128)} %student_hbm.1, f32[1,16384]{1,0:T(1,128)} %bitcast.9), custom_call_target="tpu_custom_call" | custom-call | flops 1 | bytes 1 | tf_op jit(solution)/shard_map/prep/pallas_call | solution.py:35
  17.2 1.0 %collective-permute-done.2.refs_2_ = bf16[2,192,128]{2,1,0:T(8,128)(2,1)S(1)} collective-permute-done((bf16[2,192,128]{2,1,0:T(8,128)(2,1)S(1)}, bf16[2,192,128]{2,1,0:T(8,128)(2,1)S(1)}, u32[]{:S(2)}, u32[]{:S(2)}) %collective-permute-start.2) | collective-permute-done | bytes 98336 | tf_op jit(solution)/shard_map/ppermute | solution.py:46
  18.3 0.6 %collective-permute-start.8 = (bf16[2,2,208,128]{3,2,1,0:T(8,128)(2,1)S(1)}, bf16[2,2,208,128]{3,2,1,0:T(8,128)(2,1)S(1)}, u32[]{:S(2)}, u32[]{:S(2)}) collective-permute-start(bf16[2,2,208,128]{3,2,1,0:T(8,128)(2,1)S(1)} %get-tuple-element.38), channel_id=1, source_target_pairs={{0,1},{1,0},{2,3},{3,2},{4,5},{5,4},{6,7},{7,6},{8,9},{9,8},{10,11... | collective-permute-start | bytes 638984 | tf_op jit(solution)/shard_map/ppermute | solution.py:46
  19.9 1.3 %scores.4 = (bf16[2048,4096]{1,0:T(8,128)(2,1)S(1)}, bf16[512,192]{1,0:T(8,128)(2,1)S(1)}, f32[2,512]{1,0:T(2,128)S(1)}) custom-call(bf16[4,2,192,128]{3,2,1,0:T(8,128)(2,1)S(1)} %get-tuple-element.30.refs_0_, bf16[2048,256]{1,0:T(8,128)(2,1)S(1)} %get-tuple-element.31.refs_1_.refs_2_.refs_4_, ...), custom_call_target="tpu_custom_call" | custom-call | flops 1 | bytes 1 | tf_op jit(solution)/shard_map/scores/pallas_call | solution.py:35
  21.2 1.3 %scores.5 = (bf16[2048,4096]{1,0:T(8,128)(2,1)S(1)}, bf16[512,192]{1,0:T(8,128)(2,1)S(1)}, f32[2,512]{1,0:T(2,128)S(1)}) custom-call(bf16[2,2,192,128]{3,2,1,0:T(8,128)(2,1)S(1)} %collective-permute-done.5.refs_0_, bf16[2,2,192,128]{3,2,1,0:T(8,128)(2,1)S(1)} %collective-permute-done.6.refs_1_, ...), custom_call_target="tpu_custom_call", output_to_operand_aliasing={{0}: (5, {})} | custom-call | flops 1 | bytes 1 | tf_op jit(solution)/shard_map/scores/pallas_call | solution.py:35
  22.5 1.6 %collective-permute-done.7.refs_1_ = bf16[2,192,128]{2,1,0:T(8,128)(2,1)S(1)} collective-permute-done((bf16[2,192,128]{2,1,0:T(8,128)(2,1)S(1)}, bf16[2,192,128]{2,1,0:T(8,128)(2,1)S(1)}, u32[]{:S(2)}, u32[]{:S(2)}) %collective-permute-start.7) | collective-permute-done | bytes 98336 | tf_op jit(solution)/shard_map/ppermute | solution.py:46
  24.8 1.3 %scores.6 = (bf16[2048,4096]{1,0:T(8,128)(2,1)S(1)}, bf16[512,192]{1,0:T(8,128)(2,1)S(1)}, f32[2,512]{1,0:T(2,128)S(1)}) custom-call(bf16[4,2,192,128]{3,2,1,0:T(8,128)(2,1)S(1)} %join.3.refs_0_, bf16[2048,256]{1,0:T(8,128)(2,1)S(1)} %get-tuple-element.31.refs_1_.refs_2_.refs_4_, ...), custom_call_target="tpu_custom_call", output_to_operand_aliasing={{0}: (4, {})} | custom-call | flops 1 | bytes 1 | tf_op jit(solution)/shard_map/scores/pallas_call | solution.py:35
  26.5 1.3 %scores.7 = (bf16[2048,4096]{1,0:T(8,128)(2,1)S(1)}, bf16[512,192]{1,0:T(8,128)(2,1)S(1)}, f32[4,1024]{1,0:T(4,128)S(1)}) custom-call(f32[2,512]{1,0:T(2,128)S(1)} %get-tuple-element.33.refs_0_, f32[2,512]{1,0:T(2,128)S(1)} %get-tuple-element.37.refs_3_.refs_1_, f32[2,512]{1,0:T(2,128)S(1)} %get-tuple-element.40.refs_2_, ...), custom_call_target="tpu_custom_call", output_to_operand_aliasing={{0}: (7, {})} | custom-call | flops 1 | bytes 1 | tf_op jit(solution)/shard_map/scores/pallas_call | solution.py:35
  28.0 1.0 %collective-permute-done.10.refs_1_ = f32[4,1024]{1,0:T(4,128)S(1)} collective-permute-done((f32[4,1024]{1,0:T(4,128)S(1)}, f32[4,1024]{1,0:T(4,128)S(1)}, u32[]{:S(2)}, u32[]{:S(2)}) %collective-permute-start.10) | collective-permute-done | bytes 16416 | tf_op jit(solution)/shard_map/ppermute | solution.py:46
  29.1 1.0 %collective-permute-start.11 = (f32[4,1024]{1,0:T(4,128)S(1)}, f32[4,1024]{1,0:T(4,128)S(1)}, u32[]{:S(2)}, u32[]{:S(2)}) collective-permute-start(f32[4,1024]{1,0:T(4,128)S(1)} %relay.3.refs_0_), channel_id=1, source_target_pairs={{0,16},{2,26},{4,20},{6,30},{8,24},{10,18},{12,28},{14,22},{16,0},... | collective-permute-start | bytes 49160 | tf_op jit(solution)/shard_map/ppermute | solution.py:307
  30.1 1.8 %collective-permute-start.13 = (f32[4,1024]{1,0:T(4,128)S(1)}, f32[4,1024]{1,0:T(4,128)S(1)}, u32[]{:S(2)}, u32[]{:S(2)}) collective-permute-start(f32[4,1024]{1,0:T(4,128)S(1)} %relay.3.refs_0_), channel_id=1, source_target_pairs={{0,8},{2,10},{4,12},{6,14},{8,0},{10,2},{12,4},{14,6},{16,24},{18,... | collective-permute-start | bytes 49160 | tf_op jit(solution)/shard_map/ppermute | solution.py:307
  31.9 1.9 %collective-permute-done.11.refs_1_ = f32[4,1024]{1,0:T(4,128)S(1)} collective-permute-done((f32[4,1024]{1,0:T(4,128)S(1)}, f32[4,1024]{1,0:T(4,128)S(1)}, u32[]{:S(2)}, u32[]{:S(2)}) %collective-permute-start.11) | collective-permute-done | bytes 16416 | tf_op jit(solution)/shard_map/ppermute | solution.py:307
  34.3 0.7 %collective-permute-done.12.refs_2_ = f32[4,1024]{1,0:T(4,128)S(1)} collective-permute-done((f32[4,1024]{1,0:T(4,128)S(1)}, f32[4,1024]{1,0:T(4,128)S(1)}, u32[]{:S(2)}, u32[]{:S(2)}) %collective-permute-start.12) | collective-permute-done | bytes 16416 | tf_op jit(solution)/shard_map/ppermute | solution.py:46
  35.0 1.2 %collective-permute-start.14 = (f32[4,1024]{1,0:T(4,128)S(1)}, f32[4,1024]{1,0:T(4,128)S(1)}, u32[]{:S(2)}, u32[]{:S(2)}) collective-permute-start(f32[4,1024]{1,0:T(4,128)S(1)} %relay.4.refs_0_), channel_id=1, source_target_pairs={{0,1},{1,0},{2,7},{3,6},{4,5},{5,4},{6,3},{7,2},{8,9},{9,8},{10,15... | collective-permute-start | bytes 49160 | tf_op jit(solution)/shard_map/ppermute | solution.py:307
  36.3 1.5 %collective-permute-start.16 = (f32[4,1024]{1,0:T(4,128)S(1)}, f32[4,1024]{1,0:T(4,128)S(1)}, u32[]{:S(2)}, u32[]{:S(2)}) collective-permute-start(f32[4,1024]{1,0:T(4,128)S(1)} %relay.4.refs_0_), channel_id=1, source_target_pairs={{0,4},{1,5},{2,6},{3,7},{4,0},{5,1},{6,2},{7,3},{8,12},{9,13},{10,... | collective-permute-start | bytes 49160 | tf_op jit(solution)/shard_map/ppermute | solution.py:307
  37.8 1.1 %collective-permute-done.14.refs_1_ = f32[4,1024]{1,0:T(4,128)S(1)} collective-permute-done((f32[4,1024]{1,0:T(4,128)S(1)}, f32[4,1024]{1,0:T(4,128)S(1)}, u32[]{:S(2)}, u32[]{:S(2)}) %collective-permute-start.14) | collective-permute-done | bytes 16416 | tf_op jit(solution)/shard_map/ppermute | solution.py:307
  38.9 1.2 %collective-permute-done.16.refs_3_ = f32[4,1024]{1,0:T(4,128)S(1)} collective-permute-done((f32[4,1024]{1,0:T(4,128)S(1)}, f32[4,1024]{1,0:T(4,128)S(1)}, u32[]{:S(2)}, u32[]{:S(2)}) %collective-permute-start.16) | collective-permute-done | bytes 16416 | tf_op jit(solution)/shard_map/ppermute | solution.py:307
  40.1 3.5 %gradient.1 = f32[192,2048]{1,0:T(8,128)} custom-call(f32[4,1024]{1,0:T(4,128)S(1)} %relay.5.total_ref, f32[1,128]{1,0:T(1,128)S(1)} %get-tuple-element.29.refs_5_.refs_3_.refs_4_.refs_6_.peak_ref, f32[192,2048]{1,0:T(8,128)S(1)} %get-tuple-element.43.weight_unit, f32[1,2048]{1,0:T(1,128)S(1)} %get-tuple-element.44.weight_scale, ...), custom_call_target="tpu_custom_call" | custom-call | flops 1 | bytes 1 | tf_op jit(solution)/shard_map/gradient/pallas_call | solution.py:35
  (23 shorter events, 3.0 us)
Async XLA Ops:
  0.6 4.8 %collective-permute-start = (s32[1,256]{1,0:T(1,128)}, s32[1,256]{1,0:T(1,128)S(1)}, u32[]{:S(2)}, u32[]{:S(2)}) collective-permute-start(s32[1,256]{1,0:T(1,128)} %param.10), channel_id=1, source_target_pairs={{0,1},{1,0},{2,3},{3,2},{4,5},{5,4},{6,7},{7,6},{8,9},{9,8},{10,11... | collective-permute-start | bytes 3080 | tf_op jit(solution)/shard_map/ppermute | solution.py:46
  5.6 11.6 %collective-permute-start.4 = (bf16[2,192,128]{2,1,0:T(8,128)(2,1)S(1)}, bf16[2,192,128]{2,1,0:T(8,128)(2,1)S(1)}, u32[]{:S(2)}, u32[]{:S(2)}) collective-permute-start(bf16[2,192,128]{2,1,0:T(8,128)(2,1)S(1)} %pack.1.refs_0_), channel_id=1, source_target_pairs={{0,1},{1,0},{2,3},{3,2},{4,5},{5,4},{6,7},{7,6},{8,9},{9,8},{10,11... | collective-permute-start | bytes 294920 | tf_op jit(solution)/shard_map/ppermute | solution.py:46
  7.7 9.5 %collective-permute-start.3 = (bf16[2,192,128]{2,1,0:T(8,128)(2,1)S(1)}, bf16[2,192,128]{2,1,0:T(8,128)(2,1)S(1)}, u32[]{:S(2)}, u32[]{:S(2)}) collective-permute-start(bf16[2,192,128]{2,1,0:T(8,128)(2,1)S(1)} %pack.1.refs_0_), channel_id=1, source_target_pairs={{0,24},{8,16},{16,8},{24,0},{1,25},{9,17},{17,9},{25,1},{2,26},{10... | collective-permute-start | bytes 294920 | tf_op jit(solution)/shard_map/ppermute | solution.py:46
  11.3 6.9 %collective-permute-start.2 = (bf16[2,192,128]{2,1,0:T(8,128)(2,1)S(1)}, bf16[2,192,128]{2,1,0:T(8,128)(2,1)S(1)}, u32[]{:S(2)}, u32[]{:S(2)}) collective-permute-start(bf16[2,192,128]{2,1,0:T(8,128)(2,1)S(1)} %pack.1.refs_0_), channel_id=1, source_target_pairs={{0,16},{8,24},{16,0},{24,8},{1,17},{9,25},{17,1},{25,9},{2,18},{10... | collective-permute-start | bytes 294920 | tf_op jit(solution)/shard_map/ppermute | solution.py:46
  11.3 6.9 %collective-permute-start.1 = (bf16[2,192,128]{2,1,0:T(8,128)(2,1)S(1)}, bf16[2,192,128]{2,1,0:T(8,128)(2,1)S(1)}, u32[]{:S(2)}, u32[]{:S(2)}) collective-permute-start(bf16[2,192,128]{2,1,0:T(8,128)(2,1)S(1)} %pack.1.refs_0_), channel_id=1, source_target_pairs={{0,8},{8,0},{16,24},{24,16},{1,9},{9,1},{17,25},{25,17},{2,10},{10... | collective-permute-start | bytes 294920 | tf_op jit(solution)/shard_map/ppermute | solution.py:46
  18.3 6.3 %collective-permute-start.8 = (bf16[2,2,208,128]{3,2,1,0:T(8,128)(2,1)S(1)}, bf16[2,2,208,128]{3,2,1,0:T(8,128)(2,1)S(1)}, u32[]{:S(2)}, u32[]{:S(2)}) collective-permute-start(bf16[2,2,208,128]{3,2,1,0:T(8,128)(2,1)S(1)} %get-tuple-element.38), channel_id=1, source_target_pairs={{0,1},{1,0},{2,3},{3,2},{4,5},{5,4},{6,7},{7,6},{8,9},{9,8},{10,11... | collective-permute-start | bytes 638984 | tf_op jit(solution)/shard_map/ppermute | solution.py:46
  18.9 2.3 %collective-permute-start.5 = (bf16[2,2,192,128]{3,2,1,0:T(8,128)(2,1)S(1)}, bf16[2,2,192,128]{3,2,1,0:T(8,128)(2,1)S(1)}, u32[]{:S(2)}, u32[]{:S(2)}) collective-permute-start(bf16[2,2,192,128]{3,2,1,0:T(8,128)(2,1)S(1)} %get-tuple-element.34), channel_id=1, source_target_pairs={{0,2},{2,0},{4,6},{6,4},{1,3},{3,1},{5,7},{7,5},{8,10},{10,8},{12,... | collective-permute-start | bytes 589832 | tf_op jit(solution)/shard_map/ppermute | solution.py:46
  18.9 2.3 %collective-permute-start.6 = (bf16[2,2,192,128]{3,2,1,0:T(8,128)(2,1)S(1)}, bf16[2,2,192,128]{3,2,1,0:T(8,128)(2,1)S(1)}, u32[]{:S(2)}, u32[]{:S(2)}) collective-permute-start(bf16[2,2,192,128]{3,2,1,0:T(8,128)(2,1)S(1)} %get-tuple-element.35), channel_id=1, source_target_pairs={{0,2},{2,0},{4,6},{6,4},{1,3},{3,1},{5,7},{7,5},{8,10},{10,8},{12,... | collective-permute-start | bytes 589832 | tf_op jit(solution)/shard_map/ppermute | solution.py:46
  19.4 4.7 %collective-permute-start.7 = (bf16[2,192,128]{2,1,0:T(8,128)(2,1)S(1)}, bf16[2,192,128]{2,1,0:T(8,128)(2,1)S(1)}, u32[]{:S(2)}, u32[]{:S(2)}) collective-permute-start(bf16[2,192,128]{2,1,0:T(8,128)(2,1)S(1)} %collective-permute-done.4.refs_4_.refs_0_), channel_id=1, source_target_pairs={{0,8},{8,0},{16,24},{24,16},{1,9},{9,1},{17,25},{25,17},{2,10},{10... | collective-permute-start | bytes 294920 | tf_op jit(solution)/shard_map/ppermute | solution.py:46
  24.7 1.8 %collective-permute-start.9 = (bf16[4,2,192,128]{3,2,1,0:T(8,128)(2,1)S(1)}, bf16[4,2,192,128]{3,2,1,0:T(8,128)(2,1)S(1)}, u32[]{:S(2)}, u32[]{:S(2)}) collective-permute-start(bf16[4,2,192,128]{3,2,1,0:T(8,128)(2,1)S(1)} %join.3.refs_0_), channel_id=1, source_target_pairs={{0,2},{2,0},{4,6},{6,4},{1,3},{3,1},{5,7},{7,5},{8,10},{10,8},{12,... | collective-permute-start | bytes 1179656 | tf_op jit(solution)/shard_map/ppermute | solution.py:46
  27.8 1.2 %collective-permute-start.10 = (f32[4,1024]{1,0:T(4,128)S(1)}, f32[4,1024]{1,0:T(4,128)S(1)}, u32[]{:S(2)}, u32[]{:S(2)}) collective-permute-start(f32[4,1024]{1,0:T(4,128)S(1)} %get-tuple-element.42.refs_0_), channel_id=1, source_target_pairs={{0,2},{2,0},{4,6},{6,4},{1,3},{3,1},{5,7},{7,5},{8,10},{10,8},{12,... | collective-permute-start | bytes 49160 | tf_op jit(solution)/shard_map/ppermute | solution.py:46
  29.1 4.7 %collective-permute-start.11 = (f32[4,1024]{1,0:T(4,128)S(1)}, f32[4,1024]{1,0:T(4,128)S(1)}, u32[]{:S(2)}, u32[]{:S(2)}) collective-permute-start(f32[4,1024]{1,0:T(4,128)S(1)} %relay.3.refs_0_), channel_id=1, source_target_pairs={{0,16},{2,26},{4,20},{6,30},{8,24},{10,18},{12,28},{14,22},{16,0},... | collective-permute-start | bytes 49160 | tf_op jit(solution)/shard_map/ppermute | solution.py:307
  30.1 4.2 %collective-permute-start.13 = (f32[4,1024]{1,0:T(4,128)S(1)}, f32[4,1024]{1,0:T(4,128)S(1)}, u32[]{:S(2)}, u32[]{:S(2)}) collective-permute-start(f32[4,1024]{1,0:T(4,128)S(1)} %relay.3.refs_0_), channel_id=1, source_target_pairs={{0,8},{2,10},{4,12},{6,14},{8,0},{10,2},{12,4},{14,6},{16,24},{18,... | collective-permute-start | bytes 49160 | tf_op jit(solution)/shard_map/ppermute | solution.py:307
  33.8 1.2 %collective-permute-start.12 = (f32[4,1024]{1,0:T(4,128)S(1)}, f32[4,1024]{1,0:T(4,128)S(1)}, u32[]{:S(2)}, u32[]{:S(2)}) collective-permute-start(f32[4,1024]{1,0:T(4,128)S(1)} %collective-permute-done.11.refs_1_), channel_id=1, source_target_pairs={{0,2},{2,0},{4,6},{6,4},{1,3},{3,1},{5,7},{7,5},{8,10},{10,8},{12,... | collective-permute-start | bytes 49160 | tf_op jit(solution)/shard_map/ppermute | solution.py:46
  35.0 3.8 %collective-permute-start.14 = (f32[4,1024]{1,0:T(4,128)S(1)}, f32[4,1024]{1,0:T(4,128)S(1)}, u32[]{:S(2)}, u32[]{:S(2)}) collective-permute-start(f32[4,1024]{1,0:T(4,128)S(1)} %relay.4.refs_0_), channel_id=1, source_target_pairs={{0,1},{1,0},{2,7},{3,6},{4,5},{5,4},{6,3},{7,2},{8,9},{9,8},{10,15... | collective-permute-start | bytes 49160 | tf_op jit(solution)/shard_map/ppermute | solution.py:307
  36.3 3.8 %collective-permute-start.16 = (f32[4,1024]{1,0:T(4,128)S(1)}, f32[4,1024]{1,0:T(4,128)S(1)}, u32[]{:S(2)}, u32[]{:S(2)}) collective-permute-start(f32[4,1024]{1,0:T(4,128)S(1)} %relay.4.refs_0_), channel_id=1, source_target_pairs={{0,4},{1,5},{2,6},{3,7},{4,0},{5,1},{6,2},{7,3},{8,12},{9,13},{10,... | collective-permute-start | bytes 49160 | tf_op jit(solution)/shard_map/ppermute | solution.py:307
  38.9 1.2 %collective-permute-start.15 = (f32[4,1024]{1,0:T(4,128)S(1)}, f32[4,1024]{1,0:T(4,128)S(1)}, u32[]{:S(2)}, u32[]{:S(2)}) collective-permute-start(f32[4,1024]{1,0:T(4,128)S(1)} %collective-permute-done.14.refs_1_), channel_id=1, source_target_pairs={{0,2},{2,0},{4,6},{6,4},{1,3},{3,1},{5,7},{7,5},{8,10},{10,8},{12,... | collective-permute-start | bytes 49160 | tf_op jit(solution)/shard_map/ppermute | solution.py:46

commit v25 on v20

--- a/solution.py
+++ b/solution.py
@@ -223,10 +223,11 @@
 
 
 def join_kernel(n_in, n_after, firsts, bot, *refs):
+    refs = refs[n_after:]
     blocks = []
     for ref in refs[:n_in]:
         blocks += [ref] if len(ref.shape) == 3 else [ref.at[i] for i in range(ref.shape[0])]
-    for first, ref in zip(firsts, refs[n_in + n_after:]):
+    for first, ref in zip(firsts, refs[n_in:]):
         for i in range(ref.shape[0]):
             block = blocks[first + i][:, :bot, :]
             ref[i, :, :bot, :] = block
@@ -238,7 +239,7 @@
     width = parts[0].shape[-1]
     shapes = [held(count, 2, rows, width, dtype=jnp.bfloat16) for _, count, rows in outs]
     kernel = functools.partial(join_kernel, len(parts), len(after), [first for first, _, _ in outs], bot)
-    return call(kernel, "join", shapes, (*parts, *after), in_specs=[ON_CHIP] * len(parts) + [IN_HBM] * len(after))
+    return call(kernel, "join", shapes, (*after, *parts), in_specs=[IN_HBM] * len(after) + [ON_CHIP] * len(parts))
 
 
 def log_sum(parts):

time: 44.4 us -> 44.1 us (level)
  waiting for transfers between devices: 9.59 us -> 7.79 us
  starting transfers between devices: 16.8 us -> 18.2 us
    ppermute x13, waiting for transfers between devices: 7.33 us -> 5.52 us  [swap(): lax.ppermute(block, axis, [(i, i ^ apart) for i in range(lax.axis_size(ax...]
    ppermute x13, starting transfers between devices: 11.4 us -> 12.3 us  [swap(): lax.ppermute(block, axis, [(i, i ^ apart) for i in range(lax.axis_size(ax...]
    ppermute x4, starting transfers between devices: 5.39 us -> 5.9 us  [permute(): return lax.ppermute(total, axes, pairs)]
  transfers between devices with their start and end apart: 17 -> 17, of which waited for: 10 -> 9; matrix products, arithmetic and copies ran while one was open for 0% -> 0% of each run, Pallas kernels for 27% -> 27%
where the time goes in v25:
time: 44.1 us; the launch traced here: 43.9 us
  starting transfers between devices  18.2 us (41%)
  Pallas kernels  17.1 us (39%)
  waiting for transfers between devices  7.79 us (18%)
  between operations  0.79 us (2%)
    pallas_call x15, Pallas kernels, call(): pl.pallas_call(kernel, out_shape=out_shape, compiler_params=pltpu.Compile...  17.1 us
    ppermute x13, starting transfers between devices, swap(): lax.ppermute(block, axis, [(i, i ^ apart) for i in range(lax.axis_size(ax...  12.3 us
    ppermute x4, starting transfers between devices, permute(): return lax.ppermute(total, axes, pairs)  5.9 us
    ppermute x13, waiting for transfers between devices, swap(): lax.ppermute(block, axis, [(i, i ^ apart) for i in range(lax.axis_size(ax...  5.52 us
    ppermute x4, waiting for transfers between devices, permute(): return lax.ppermute(total, axes, pairs)  2.27 us
  transfers between devices with their start and end apart: 17, of which 9 were waited for; matrix products, arithmetic and copies ran while one was open for 0% of the time, Pallas kernels for 27%

profile of v25, /device:TPU:0, one launch (start us, length us, event | category | flops | bytes accessed | tf_op | source)
XLA Modules:
  0.0 43.9 jit_solution(11131749974751393526)
XLA Ops:
  0.6 3.0 %collective-permute-start = (s32[1,256]{1,0:T(1,128)}, s32[1,256]{1,0:T(1,128)S(1)}, u32[]{:S(2)}, u32[]{:S(2)}) collective-permute-start(s32[1,256]{1,0:T(1,128)} %param.10), channel_id=1, source_target_pairs={{0,1},{1,0},{2,3},{3,2},{4,5},{5,4},{6,7},{7,6},{8,9},{9,8},{10,11... | collective-permute-start | bytes 3080 | tf_op jit(solution)/shard_map/ppermute | solution.py:46
  3.6 0.9 %fetch.1 = (bf16[192,128]{1,0:T(8,128)(2,1)S(1)}, bf16[192,256]{1,0:T(8,128)(2,1)S(1)}) custom-call(bf16[192,256]{1,0:T(8,128)(2,1)} %bitcast.7, bf16[192,256]{1,0:T(8,128)(2,1)} %bitcast.8), custom_call_target="tpu_custom_call" | custom-call | flops 1 | bytes 1 | tf_op jit(solution)/shard_map/fetch/pallas_call | solution.py:35
  4.6 0.8 %collective-permute-done.index_ref = s32[1,256]{1,0:T(1,128)S(1)} collective-permute-done((s32[1,256]{1,0:T(1,128)}, s32[1,256]{1,0:T(1,128)S(1)}, u32[]{:S(2)}, u32[]{:S(2)}) %collective-permute-start) | collective-permute-done | bytes 1056 | tf_op jit(solution)/shard_map/ppermute | solution.py:46
  5.6 4.2 %collective-permute-start.4 = (bf16[2,192,128]{2,1,0:T(8,128)(2,1)S(1)}, bf16[2,192,128]{2,1,0:T(8,128)(2,1)S(1)}, u32[]{:S(2)}, u32[]{:S(2)}) collective-permute-start(bf16[2,192,128]{2,1,0:T(8,128)(2,1)S(1)} %pack.1.refs_2_), channel_id=1, source_target_pairs={{0,24},{8,16},{16,8},{24,0},{1,25},{9,17},{17,9},{25,1},{2,26},{10... | collective-permute-start | bytes 294920 | tf_op jit(solution)/shard_map/ppermute | solution.py:46
  9.8 0.6 %collective-permute-start.2 = (bf16[2,192,128]{2,1,0:T(8,128)(2,1)S(1)}, bf16[2,192,128]{2,1,0:T(8,128)(2,1)S(1)}, u32[]{:S(2)}, u32[]{:S(2)}) collective-permute-start(bf16[2,192,128]{2,1,0:T(8,128)(2,1)S(1)} %pack.1.refs_2_), channel_id=1, source_target_pairs={{0,8},{8,0},{16,24},{24,16},{1,9},{9,1},{17,25},{25,17},{2,10},{10... | collective-permute-start | bytes 294920 | tf_op jit(solution)/shard_map/ppermute | solution.py:46
  10.4 1.6 %collective-permute-start.1 = (bf16[2,192,128]{2,1,0:T(8,128)(2,1)S(1)}, bf16[2,192,128]{2,1,0:T(8,128)(2,1)S(1)}, u32[]{:S(2)}, u32[]{:S(2)}) collective-permute-start(bf16[2,192,128]{2,1,0:T(8,128)(2,1)S(1)} %pack.1.refs_2_), channel_id=1, source_target_pairs={{0,1},{1,0},{2,3},{3,2},{4,5},{5,4},{6,7},{7,6},{8,9},{9,8},{10,11... | collective-permute-start | bytes 294920 | tf_op jit(solution)/shard_map/ppermute | solution.py:46
  12.1 4.5 %prep.1 = (f32[192,4096]{1,0:T(8,128)}, bf16[2048,256]{1,0:T(8,128)(2,1)S(1)}, bf16[2048,256]{1,0:T(8,128)(2,1)S(1)}, f32[192,2048]{1,0:T(8,128)S(1)}, f32[1,2048]{1,0:T(1,128)S(1)}, /*index=5*/f32[1,128]{1,0:T(1,128)S(1)}) custom-call(f32[192,4096]{1,0:T(8,128)} %teacher_hbm.3, f32[192,4096]{1,0:T(8,128)} %student_hbm.3, f32[1,16384]{1,0:T(1,128)} %bitcast.9), custom_call_target="tpu_custom_call" | custom-call | flops 1 | bytes 1 | tf_op jit(solution)/shard_map/prep/pallas_call | solution.py:35
  17.1 1.6 %collective-permute-start.8 = (bf16[2,2,208,128]{3,2,1,0:T(8,128)(2,1)S(1)}, bf16[2,2,208,128]{3,2,1,0:T(8,128)(2,1)S(1)}, u32[]{:S(2)}, u32[]{:S(2)}) collective-permute-start(bf16[2,2,208,128]{3,2,1,0:T(8,128)(2,1)S(1)} %get-tuple-element.39), channel_id=1, source_target_pairs={{0,1},{1,0},{2,3},{3,2},{4,5},{5,4},{6,7},{7,6},{8,9},{9,8},{10,11... | collective-permute-start | bytes 638984 | tf_op jit(solution)/shard_map/ppermute | solution.py:46
  18.7 0.5 %collective-permute-start.6 = (bf16[2,2,192,128]{3,2,1,0:T(8,128)(2,1)S(1)}, bf16[2,2,192,128]{3,2,1,0:T(8,128)(2,1)S(1)}, u32[]{:S(2)}, u32[]{:S(2)}) collective-permute-start(bf16[2,2,192,128]{3,2,1,0:T(8,128)(2,1)S(1)} %get-tuple-element.36), channel_id=1, source_target_pairs={{0,2},{2,0},{4,6},{6,4},{1,3},{3,1},{5,7},{7,5},{8,10},{10,8},{12,... | collective-permute-start | bytes 589832 | tf_op jit(solution)/shard_map/ppermute | solution.py:46
  19.6 1.3 %scores.4 = (bf16[2048,4096]{1,0:T(8,128)(2,1)S(1)}, bf16[512,192]{1,0:T(8,128)(2,1)S(1)}, f32[2,512]{1,0:T(2,128)S(1)}) custom-call(bf16[4,2,192,128]{3,2,1,0:T(8,128)(2,1)S(1)} %get-tuple-element.31.refs_0_, bf16[2048,256]{1,0:T(8,128)(2,1)S(1)} %get-tuple-element.32.refs_1_.refs_2_.refs_4_, ...), custom_call_target="tpu_custom_call" | custom-call | flops 1 | bytes 1 | tf_op jit(solution)/shard_map/scores/pallas_call | solution.py:35
  20.9 1.3 %scores.5 = (bf16[2048,4096]{1,0:T(8,128)(2,1)S(1)}, bf16[512,192]{1,0:T(8,128)(2,1)S(1)}, f32[2,512]{1,0:T(2,128)S(1)}) custom-call(bf16[2,2,192,128]{3,2,1,0:T(8,128)(2,1)S(1)} %collective-permute-done.5.refs_0_, bf16[2,2,192,128]{3,2,1,0:T(8,128)(2,1)S(1)} %collective-permute-done.6.refs_1_, ...), custom_call_target="tpu_custom_call", output_to_operand_aliasing={{0}: (5, {})} | custom-call | flops 1 | bytes 1 | tf_op jit(solution)/shard_map/scores/pallas_call | solution.py:35
  22.3 1.6 %collective-permute-done.7.refs_2_ = bf16[2,192,128]{2,1,0:T(8,128)(2,1)S(1)} collective-permute-done((bf16[2,192,128]{2,1,0:T(8,128)(2,1)S(1)}, bf16[2,192,128]{2,1,0:T(8,128)(2,1)S(1)}, u32[]{:S(2)}, u32[]{:S(2)}) %collective-permute-start.7) | collective-permute-done | bytes 98336 | tf_op jit(solution)/shard_map/ppermute | solution.py:46
  24.0 1.3 %scores.6 = (bf16[2048,4096]{1,0:T(8,128)(2,1)S(1)}, bf16[512,192]{1,0:T(8,128)(2,1)S(1)}, f32[2,512]{1,0:T(2,128)S(1)}) custom-call(bf16[4,2,192,128]{3,2,1,0:T(8,128)(2,1)S(1)} %join.3.refs_0_, bf16[2048,256]{1,0:T(8,128)(2,1)S(1)} %get-tuple-element.32.refs_1_.refs_2_.refs_4_, ...), custom_call_target="tpu_custom_call", output_to_operand_aliasing={{0}: (4, {})} | custom-call | flops 1 | bytes 1 | tf_op jit(solution)/shard_map/scores/pallas_call | solution.py:35
  25.7 1.3 %scores.7 = (bf16[2048,4096]{1,0:T(8,128)(2,1)S(1)}, bf16[512,192]{1,0:T(8,128)(2,1)S(1)}, f32[4,1024]{1,0:T(4,128)S(1)}) custom-call(f32[2,512]{1,0:T(2,128)S(1)} %get-tuple-element.34.refs_0_, f32[2,512]{1,0:T(2,128)S(1)} %get-tuple-element.38.refs_0_.refs_1_, f32[2,512]{1,0:T(2,128)S(1)} %get-tuple-element.41.refs_2_, ...), custom_call_target="tpu_custom_call", output_to_operand_aliasing={{0}: (7, {})} | custom-call | flops 1 | bytes 1 | tf_op jit(solution)/shard_map/scores/pallas_call | solution.py:35
  27.2 1.0 %collective-permute-done.10.refs_1_ = f32[4,1024]{1,0:T(4,128)S(1)} collective-permute-done((f32[4,1024]{1,0:T(4,128)S(1)}, f32[4,1024]{1,0:T(4,128)S(1)}, u32[]{:S(2)}, u32[]{:S(2)}) %collective-permute-start.10) | collective-permute-done | bytes 16416 | tf_op jit(solution)/shard_map/ppermute | solution.py:46
  28.3 1.1 %collective-permute-start.11 = (f32[4,1024]{1,0:T(4,128)S(1)}, f32[4,1024]{1,0:T(4,128)S(1)}, u32[]{:S(2)}, u32[]{:S(2)}) collective-permute-start(f32[4,1024]{1,0:T(4,128)S(1)} %relay.3.refs_0_), channel_id=1, source_target_pairs={{0,1},{1,0},{2,7},{3,6},{4,5},{5,4},{6,3},{7,2},{8,9},{9,8},{10,15... | collective-permute-start | bytes 49160 | tf_op jit(solution)/shard_map/ppermute | solution.py:361
  29.4 1.5 %collective-permute-start.13 = (f32[4,1024]{1,0:T(4,128)S(1)}, f32[4,1024]{1,0:T(4,128)S(1)}, u32[]{:S(2)}, u32[]{:S(2)}) collective-permute-start(f32[4,1024]{1,0:T(4,128)S(1)} %relay.3.refs_0_), channel_id=1, source_target_pairs={{0,4},{1,5},{2,6},{3,7},{4,0},{5,1},{6,2},{7,3},{8,12},{9,13},{10,... | collective-permute-start | bytes 49160 | tf_op jit(solution)/shard_map/ppermute | solution.py:361
  31.0 1.2 %collective-permute-done.11.refs_1_ = f32[4,1024]{1,0:T(4,128)S(1)} collective-permute-done((f32[4,1024]{1,0:T(4,128)S(1)}, f32[4,1024]{1,0:T(4,128)S(1)}, u32[]{:S(2)}, u32[]{:S(2)}) %collective-permute-start.11) | collective-permute-done | bytes 16416 | tf_op jit(solution)/shard_map/ppermute | solution.py:361
  32.2 1.1 %collective-permute-done.13.refs_3_ = f32[4,1024]{1,0:T(4,128)S(1)} collective-permute-done((f32[4,1024]{1,0:T(4,128)S(1)}, f32[4,1024]{1,0:T(4,128)S(1)}, u32[]{:S(2)}, u32[]{:S(2)}) %collective-permute-start.13) | collective-permute-done | bytes 16416 | tf_op jit(solution)/shard_map/ppermute | solution.py:361
  33.4 1.5 %collective-permute-start.14 = (f32[4,1024]{1,0:T(4,128)S(1)}, f32[4,1024]{1,0:T(4,128)S(1)}, u32[]{:S(2)}, u32[]{:S(2)}) collective-permute-start(f32[4,1024]{1,0:T(4,128)S(1)} %relay.4.after.refs_0_), channel_id=1, source_target_pairs={{0,16},{2,26},{4,20},{6,30},{8,24},{10,18},{12,28},{14,22},{16,0},... | collective-permute-start | bytes 49160 | tf_op jit(solution)/shard_map/ppermute | solution.py:361
  34.9 1.7 %collective-permute-start.16 = (f32[4,1024]{1,0:T(4,128)S(1)}, f32[4,1024]{1,0:T(4,128)S(1)}, u32[]{:S(2)}, u32[]{:S(2)}) collective-permute-start(f32[4,1024]{1,0:T(4,128)S(1)} %relay.4.after.refs_0_), channel_id=1, source_target_pairs={{0,8},{2,10},{4,12},{6,14},{8,0},{10,2},{12,4},{14,6},{16,24},{18,... | collective-permute-start | bytes 49160 | tf_op jit(solution)/shard_map/ppermute | solution.py:361
  36.6 2.4 %rest.1 = (f32[192,4096]{1,0:T(8,128)}, f32[8,128]{1,0:T(8,128)S(1)}) custom-call(f32[192,4096]{1,0:T(8,128)} %teacher_hbm.3, f32[192,4096]{1,0:T(8,128)} %student_hbm.3, f32[4,1024]{1,0:T(4,128)S(1)} %relay.4.after.refs_0_, f32[192,4096]{1,0:T(8,128)} %get-tuple-element.44.before_hbm), custom_call_target="tpu_custom_call", output_to_operand_aliasing={{0}: (3, {})} | custom-call | flops 1 | bytes 1 | tf_op jit(solution)/shard_map/rest/pallas_call | solution.py:35
  39.2 1.2 %collective-permute-done.15.refs_2_ = f32[4,1024]{1,0:T(4,128)S(1)} collective-permute-done((f32[4,1024]{1,0:T(4,128)S(1)}, f32[4,1024]{1,0:T(4,128)S(1)}, u32[]{:S(2)}, u32[]{:S(2)}) %collective-permute-start.15) | collective-permute-done | bytes 16416 | tf_op jit(solution)/shard_map/ppermute | solution.py:46
  40.4 3.5 %gradient.1 = f32[192,2048]{1,0:T(8,128)} custom-call(f32[4,1024]{1,0:T(4,128)S(1)} %relay.5.total_ref, f32[1,128]{1,0:T(1,128)S(1)} %get-tuple-element.30.refs_1_.refs_3_.refs_4_.refs_6_.peak_ref, f32[192,2048]{1,0:T(8,128)S(1)} %get-tuple-element.47.weight_unit, f32[1,2048]{1,0:T(1,128)S(1)} %get-tuple-element.48.weight_scale, ...), custom_call_target="tpu_custom_call" | custom-call | flops 1 | bytes 1 | tf_op jit(solution)/shard_map/gradient/pallas_call | solution.py:35
  (25 shorter events, 2.1 us)
Async XLA Ops:
  0.6 4.8 %collective-permute-start = (s32[1,256]{1,0:T(1,128)}, s32[1,256]{1,0:T(1,128)S(1)}, u32[]{:S(2)}, u32[]{:S(2)}) collective-permute-start(s32[1,256]{1,0:T(1,128)} %param.10), channel_id=1, source_target_pairs={{0,1},{1,0},{2,3},{3,2},{4,5},{5,4},{6,7},{7,6},{8,9},{9,8},{10,11... | collective-permute-start | bytes 3080 | tf_op jit(solution)/shard_map/ppermute | solution.py:46
  5.6 11.0 %collective-permute-start.4 = (bf16[2,192,128]{2,1,0:T(8,128)(2,1)S(1)}, bf16[2,192,128]{2,1,0:T(8,128)(2,1)S(1)}, u32[]{:S(2)}, u32[]{:S(2)}) collective-permute-start(bf16[2,192,128]{2,1,0:T(8,128)(2,1)S(1)} %pack.1.refs_2_), channel_id=1, source_target_pairs={{0,24},{8,16},{16,8},{24,0},{1,25},{9,17},{17,9},{25,1},{2,26},{10... | collective-permute-start | bytes 294920 | tf_op jit(solution)/shard_map/ppermute | solution.py:46
  9.8 7.2 %collective-permute-start.3 = (bf16[2,192,128]{2,1,0:T(8,128)(2,1)S(1)}, bf16[2,192,128]{2,1,0:T(8,128)(2,1)S(1)}, u32[]{:S(2)}, u32[]{:S(2)}) collective-permute-start(bf16[2,192,128]{2,1,0:T(8,128)(2,1)S(1)} %pack.1.refs_2_), channel_id=1, source_target_pairs={{0,16},{8,24},{16,0},{24,8},{1,17},{9,25},{17,1},{25,9},{2,18},{10... | collective-permute-start | bytes 294920 | tf_op jit(solution)/shard_map/ppermute | solution.py:46
  9.8 7.2 %collective-permute-start.2 = (bf16[2,192,128]{2,1,0:T(8,128)(2,1)S(1)}, bf16[2,192,128]{2,1,0:T(8,128)(2,1)S(1)}, u32[]{:S(2)}, u32[]{:S(2)}) collective-permute-start(bf16[2,192,128]{2,1,0:T(8,128)(2,1)S(1)} %pack.1.refs_2_), channel_id=1, source_target_pairs={{0,8},{8,0},{16,24},{24,16},{1,9},{9,1},{17,25},{25,17},{2,10},{10... | collective-permute-start | bytes 294920 | tf_op jit(solution)/shard_map/ppermute | solution.py:46
  10.4 6.6 %collective-permute-start.1 = (bf16[2,192,128]{2,1,0:T(8,128)(2,1)S(1)}, bf16[2,192,128]{2,1,0:T(8,128)(2,1)S(1)}, u32[]{:S(2)}, u32[]{:S(2)}) collective-permute-start(bf16[2,192,128]{2,1,0:T(8,128)(2,1)S(1)} %pack.1.refs_2_), channel_id=1, source_target_pairs={{0,1},{1,0},{2,3},{3,2},{4,5},{5,4},{6,7},{7,6},{8,9},{9,8},{10,11... | collective-permute-start | bytes 294920 | tf_op jit(solution)/shard_map/ppermute | solution.py:46
  17.1 6.8 %collective-permute-start.8 = (bf16[2,2,208,128]{3,2,1,0:T(8,128)(2,1)S(1)}, bf16[2,2,208,128]{3,2,1,0:T(8,128)(2,1)S(1)}, u32[]{:S(2)}, u32[]{:S(2)}) collective-permute-start(bf16[2,2,208,128]{3,2,1,0:T(8,128)(2,1)S(1)} %get-tuple-element.39), channel_id=1, source_target_pairs={{0,1},{1,0},{2,3},{3,2},{4,5},{5,4},{6,7},{7,6},{8,9},{9,8},{10,11... | collective-permute-start | bytes 638984 | tf_op jit(solution)/shard_map/ppermute | solution.py:46
  18.7 2.3 %collective-permute-start.5 = (bf16[2,2,192,128]{3,2,1,0:T(8,128)(2,1)S(1)}, bf16[2,2,192,128]{3,2,1,0:T(8,128)(2,1)S(1)}, u32[]{:S(2)}, u32[]{:S(2)}) collective-permute-start(bf16[2,2,192,128]{3,2,1,0:T(8,128)(2,1)S(1)} %get-tuple-element.35), channel_id=1, source_target_pairs={{0,2},{2,0},{4,6},{6,4},{1,3},{3,1},{5,7},{7,5},{8,10},{10,8},{12,... | collective-permute-start | bytes 589832 | tf_op jit(solution)/shard_map/ppermute | solution.py:46
  18.7 2.3 %collective-permute-start.6 = (bf16[2,2,192,128]{3,2,1,0:T(8,128)(2,1)S(1)}, bf16[2,2,192,128]{3,2,1,0:T(8,128)(2,1)S(1)}, u32[]{:S(2)}, u32[]{:S(2)}) collective-permute-start(bf16[2,2,192,128]{3,2,1,0:T(8,128)(2,1)S(1)} %get-tuple-element.36), channel_id=1, source_target_pairs={{0,2},{2,0},{4,6},{6,4},{1,3},{3,1},{5,7},{7,5},{8,10},{10,8},{12,... | collective-permute-start | bytes 589832 | tf_op jit(solution)/shard_map/ppermute | solution.py:46
  19.2 4.7 %collective-permute-start.7 = (bf16[2,192,128]{2,1,0:T(8,128)(2,1)S(1)}, bf16[2,192,128]{2,1,0:T(8,128)(2,1)S(1)}, u32[]{:S(2)}, u32[]{:S(2)}) collective-permute-start(bf16[2,192,128]{2,1,0:T(8,128)(2,1)S(1)} %collective-permute-done.1.refs_0_.refs_1_), channel_id=1, source_target_pairs={{0,8},{8,0},{16,24},{24,16},{1,9},{9,1},{17,25},{25,17},{2,10},{10... | collective-permute-start | bytes 294920 | tf_op jit(solution)/shard_map/ppermute | solution.py:46
  23.9 1.8 %collective-permute-start.9 = (bf16[4,2,192,128]{3,2,1,0:T(8,128)(2,1)S(1)}, bf16[4,2,192,128]{3,2,1,0:T(8,128)(2,1)S(1)}, u32[]{:S(2)}, u32[]{:S(2)}) collective-permute-start(bf16[4,2,192,128]{3,2,1,0:T(8,128)(2,1)S(1)} %join.3.refs_0_), channel_id=1, source_target_pairs={{0,2},{2,0},{4,6},{6,4},{1,3},{3,1},{5,7},{7,5},{8,10},{10,8},{12,... | collective-permute-start | bytes 1179656 | tf_op jit(solution)/shard_map/ppermute | solution.py:46
  27.0 1.2 %collective-permute-start.10 = (f32[4,1024]{1,0:T(4,128)S(1)}, f32[4,1024]{1,0:T(4,128)S(1)}, u32[]{:S(2)}, u32[]{:S(2)}) collective-permute-start(f32[4,1024]{1,0:T(4,128)S(1)} %get-tuple-element.43.refs_0_), channel_id=1, source_target_pairs={{0,2},{2,0},{4,6},{6,4},{1,3},{3,1},{5,7},{7,5},{8,10},{10,8},{12,... | collective-permute-start | bytes 49160 | tf_op jit(solution)/shard_map/ppermute | solution.py:46
  28.3 3.8 %collective-permute-start.11 = (f32[4,1024]{1,0:T(4,128)S(1)}, f32[4,1024]{1,0:T(4,128)S(1)}, u32[]{:S(2)}, u32[]{:S(2)}) collective-permute-start(f32[4,1024]{1,0:T(4,128)S(1)} %relay.3.refs_0_), channel_id=1, source_target_pairs={{0,1},{1,0},{2,7},{3,6},{4,5},{5,4},{6,3},{7,2},{8,9},{9,8},{10,15... | collective-permute-start | bytes 49160 | tf_op jit(solution)/shard_map/ppermute | solution.py:361
  29.4 3.8 %collective-permute-start.13 = (f32[4,1024]{1,0:T(4,128)S(1)}, f32[4,1024]{1,0:T(4,128)S(1)}, u32[]{:S(2)}, u32[]{:S(2)}) collective-permute-start(f32[4,1024]{1,0:T(4,128)S(1)} %relay.3.refs_0_), channel_id=1, source_target_pairs={{0,4},{1,5},{2,6},{3,7},{4,0},{5,1},{6,2},{7,3},{8,12},{9,13},{10,... | collective-permute-start | bytes 49160 | tf_op jit(solution)/shard_map/ppermute | solution.py:361
  32.1 1.2 %collective-permute-start.12 = (f32[4,1024]{1,0:T(4,128)S(1)}, f32[4,1024]{1,0:T(4,128)S(1)}, u32[]{:S(2)}, u32[]{:S(2)}) collective-permute-start(f32[4,1024]{1,0:T(4,128)S(1)} %collective-permute-done.11.refs_1_), channel_id=1, source_target_pairs={{0,2},{2,0},{4,6},{6,4},{1,3},{3,1},{5,7},{7,5},{8,10},{10,8},{12,... | collective-permute-start | bytes 49160 | tf_op jit(solution)/shard_map/ppermute | solution.py:46
  33.4 5.7 %collective-permute-start.14 = (f32[4,1024]{1,0:T(4,128)S(1)}, f32[4,1024]{1,0:T(4,128)S(1)}, u32[]{:S(2)}, u32[]{:S(2)}) collective-permute-start(f32[4,1024]{1,0:T(4,128)S(1)} %relay.4.after.refs_0_), channel_id=1, source_target_pairs={{0,16},{2,26},{4,20},{6,30},{8,24},{10,18},{12,28},{14,22},{16,0},... | collective-permute-start | bytes 49160 | tf_op jit(solution)/shard_map/ppermute | solution.py:361
  34.9 4.3 %collective-permute-start.16 = (f32[4,1024]{1,0:T(4,128)S(1)}, f32[4,1024]{1,0:T(4,128)S(1)}, u32[]{:S(2)}, u32[]{:S(2)}) collective-permute-start(f32[4,1024]{1,0:T(4,128)S(1)} %relay.4.after.refs_0_), channel_id=1, source_target_pairs={{0,8},{2,10},{4,12},{6,14},{8,0},{10,2},{12,4},{14,6},{16,24},{18,... | collective-permute-start | bytes 49160 | tf_op jit(solution)/shard_map/ppermute | solution.py:361
  39.1 1.2 %collective-permute-start.15 = (f32[4,1024]{1,0:T(4,128)S(1)}, f32[4,1024]{1,0:T(4,128)S(1)}, u32[]{:S(2)}, u32[]{:S(2)}) collective-permute-start(f32[4,1024]{1,0:T(4,128)S(1)} %hold.1), channel_id=1, source_target_pairs={{0,2},{2,0},{4,6},{6,4},{1,3},{3,1},{5,7},{7,5},{8,10},{10,8},{12,... | collective-permute-start | bytes 49160 | tf_op jit(solution)/shard_map/ppermute | solution.py:46

commit v26 on v21

--- a/solution.py
+++ b/solution.py
@@ -329,7 +329,7 @@
 def add_up_along(total):
     n = lax.axis_size("fsdp")
     if n == 4:
-        return exchange(total, ("fsdp", "proto"), lambda odd: (2 + odd, 0), lambda odd: (1, 0))
+        return exchange(total, ("fsdp", "proto"), lambda odd: (1 + 2 * odd, 0), lambda odd: (2, 0))
     if n <= DIRECT:
         return add_up([total, *[swap(total, "fsdp", k) for k in range(1, n)]])
     return add_up([lax.all_to_all(jnp.broadcast_to(total[None], (n, *total.shape)), "fsdp", 0, 0, tiled=True)])

time: 43.8 us -> 43.3 us (0.989)
  waiting for transfers between devices: 10.7 us -> 9.44 us
  starting transfers between devices: 16.9 us -> 17.7 us
    ppermute x4, waiting for transfers between devices: 4.42 us -> 3.53 us  [permute(): return lax.ppermute(total, axes, pairs)]
    ppermute x13, starting transfers between devices: 11.3 us -> 12.1 us  [swap(): lax.ppermute(block, axis, [(i, i ^ apart) for i in range(lax.axis_size(ax...]
where the time goes in v26:
time: 43.3 us; the launch traced here: 43.2 us
  starting transfers between devices  17.7 us (41%)
  Pallas kernels  15.2 us (35%)
  waiting for transfers between devices  9.44 us (22%)
  between operations  0.75 us (2%)
    pallas_call x13, Pallas kernels, call(): pl.pallas_call(kernel, out_shape=out_shape, compiler_params=pltpu.Compile...  15.2 us
    ppermute x13, starting transfers between devices, swap(): lax.ppermute(block, axis, [(i, i ^ apart) for i in range(lax.axis_size(ax...  12.1 us
    ppermute x13, waiting for transfers between devices, swap(): lax.ppermute(block, axis, [(i, i ^ apart) for i in range(lax.axis_size(ax...  5.91 us
    ppermute x4, starting transfers between devices, permute(): return lax.ppermute(total, axes, pairs)  5.62 us
    ppermute x4, waiting for transfers between devices, permute(): return lax.ppermute(total, axes, pairs)  3.53 us
  transfers between devices with their start and end apart: 17, of which 12 were waited for; matrix products, arithmetic and copies ran while one was open for 0% of the time, Pallas kernels for 23%

profile of v26, /device:TPU:0, one launch (start us, length us, event | category | flops | bytes accessed | tf_op | source)
XLA Modules:
  0.0 43.2 jit_solution(5275505545382573701)
XLA Ops:
  0.6 3.0 %collective-permute-start = (s32[1,256]{1,0:T(1,128)}, s32[1,256]{1,0:T(1,128)S(1)}, u32[]{:S(2)}, u32[]{:S(2)}) collective-permute-start(s32[1,256]{1,0:T(1,128)} %param.10), channel_id=1, source_target_pairs={{0,1},{1,0},{2,3},{3,2},{4,5},{5,4},{6,7},{7,6},{8,9},{9,8},{10,11... | collective-permute-start | bytes 3080 | tf_op jit(solution)/shard_map/ppermute | solution.py:46
  3.6 0.9 %fetch.1 = (bf16[192,128]{1,0:T(8,128)(2,1)S(1)}, bf16[192,256]{1,0:T(8,128)(2,1)S(1)}) custom-call(bf16[192,256]{1,0:T(8,128)(2,1)} %bitcast.7, bf16[192,256]{1,0:T(8,128)(2,1)} %bitcast.8), custom_call_target="tpu_custom_call" | custom-call | flops 1 | bytes 1 | tf_op jit(solution)/shard_map/fetch/pallas_call | solution.py:35
  4.6 0.8 %collective-permute-done.index_ref = s32[1,256]{1,0:T(1,128)S(1)} collective-permute-done((s32[1,256]{1,0:T(1,128)}, s32[1,256]{1,0:T(1,128)S(1)}, u32[]{:S(2)}, u32[]{:S(2)}) %collective-permute-start) | collective-permute-done | bytes 1056 | tf_op jit(solution)/shard_map/ppermute | solution.py:46
  5.6 2.1 %collective-permute-start.4 = (bf16[2,192,128]{2,1,0:T(8,128)(2,1)S(1)}, bf16[2,192,128]{2,1,0:T(8,128)(2,1)S(1)}, u32[]{:S(2)}, u32[]{:S(2)}) collective-permute-start(bf16[2,192,128]{2,1,0:T(8,128)(2,1)S(1)} %pack.1.refs_0_), channel_id=1, source_target_pairs={{0,1},{1,0},{2,3},{3,2},{4,5},{5,4},{6,7},{7,6},{8,9},{9,8},{10,11... | collective-permute-start | bytes 294920 | tf_op jit(solution)/shard_map/ppermute | solution.py:46
  7.7 3.6 %collective-permute-start.3 = (bf16[2,192,128]{2,1,0:T(8,128)(2,1)S(1)}, bf16[2,192,128]{2,1,0:T(8,128)(2,1)S(1)}, u32[]{:S(2)}, u32[]{:S(2)}) collective-permute-start(bf16[2,192,128]{2,1,0:T(8,128)(2,1)S(1)} %pack.1.refs_0_), channel_id=1, source_target_pairs={{0,24},{8,16},{16,8},{24,0},{1,25},{9,17},{17,9},{25,1},{2,26},{10... | collective-permute-start | bytes 294920 | tf_op jit(solution)/shard_map/ppermute | solution.py:46
  11.3 0.8 %collective-permute-start.1 = (bf16[2,192,128]{2,1,0:T(8,128)(2,1)S(1)}, bf16[2,192,128]{2,1,0:T(8,128)(2,1)S(1)}, u32[]{:S(2)}, u32[]{:S(2)}) collective-permute-start(bf16[2,192,128]{2,1,0:T(8,128)(2,1)S(1)} %pack.1.refs_0_), channel_id=1, source_target_pairs={{0,8},{8,0},{16,24},{24,16},{1,9},{9,1},{17,25},{25,17},{2,10},{10... | collective-permute-start | bytes 294920 | tf_op jit(solution)/shard_map/ppermute | solution.py:46
  12.1 5.1 %prep.1 = (f32[192,4096]{1,0:T(8,128)}, bf16[2048,256]{1,0:T(8,128)(2,1)S(1)}, bf16[2048,256]{1,0:T(8,128)(2,1)S(1)}, f32[192,2048]{1,0:T(8,128)S(1)}, f32[1,2048]{1,0:T(1,128)S(1)}, /*index=5*/f32[1,128]{1,0:T(1,128)S(1)}) custom-call(f32[192,4096]{1,0:T(8,128)} %teacher_hbm.1, f32[192,4096]{1,0:T(8,128)} %student_hbm.1, f32[1,16384]{1,0:T(1,128)} %bitcast.9), custom_call_target="tpu_custom_call" | custom-call | flops 1 | bytes 1 | tf_op jit(solution)/shard_map/prep/pallas_call | solution.py:35
  17.2 1.0 %collective-permute-done.2.refs_2_ = bf16[2,192,128]{2,1,0:T(8,128)(2,1)S(1)} collective-permute-done((bf16[2,192,128]{2,1,0:T(8,128)(2,1)S(1)}, bf16[2,192,128]{2,1,0:T(8,128)(2,1)S(1)}, u32[]{:S(2)}, u32[]{:S(2)}) %collective-permute-start.2) | collective-permute-done | bytes 98336 | tf_op jit(solution)/shard_map/ppermute | solution.py:46
  18.3 0.6 %collective-permute-start.8 = (bf16[2,2,208,128]{3,2,1,0:T(8,128)(2,1)S(1)}, bf16[2,2,208,128]{3,2,1,0:T(8,128)(2,1)S(1)}, u32[]{:S(2)}, u32[]{:S(2)}) collective-permute-start(bf16[2,2,208,128]{3,2,1,0:T(8,128)(2,1)S(1)} %get-tuple-element.38), channel_id=1, source_target_pairs={{0,1},{1,0},{2,3},{3,2},{4,5},{5,4},{6,7},{7,6},{8,9},{9,8},{10,11... | collective-permute-start | bytes 638984 | tf_op jit(solution)/shard_map/ppermute | solution.py:46
  19.9 1.3 %scores.4 = (bf16[2048,4096]{1,0:T(8,128)(2,1)S(1)}, bf16[512,192]{1,0:T(8,128)(2,1)S(1)}, f32[2,512]{1,0:T(2,128)S(1)}) custom-call(bf16[4,2,192,128]{3,2,1,0:T(8,128)(2,1)S(1)} %get-tuple-element.30.refs_0_, bf16[2048,256]{1,0:T(8,128)(2,1)S(1)} %get-tuple-element.31.refs_1_.refs_2_.refs_4_, ...), custom_call_target="tpu_custom_call" | custom-call | flops 1 | bytes 1 | tf_op jit(solution)/shard_map/scores/pallas_call | solution.py:35
  21.2 1.3 %scores.5 = (bf16[2048,4096]{1,0:T(8,128)(2,1)S(1)}, bf16[512,192]{1,0:T(8,128)(2,1)S(1)}, f32[2,512]{1,0:T(2,128)S(1)}) custom-call(bf16[2,2,192,128]{3,2,1,0:T(8,128)(2,1)S(1)} %collective-permute-done.5.refs_0_, bf16[2,2,192,128]{3,2,1,0:T(8,128)(2,1)S(1)} %collective-permute-done.6.refs_1_, ...), custom_call_target="tpu_custom_call", output_to_operand_aliasing={{0}: (5, {})} | custom-call | flops 1 | bytes 1 | tf_op jit(solution)/shard_map/scores/pallas_call | solution.py:35
  22.5 1.6 %collective-permute-done.7.refs_1_ = bf16[2,192,128]{2,1,0:T(8,128)(2,1)S(1)} collective-permute-done((bf16[2,192,128]{2,1,0:T(8,128)(2,1)S(1)}, bf16[2,192,128]{2,1,0:T(8,128)(2,1)S(1)}, u32[]{:S(2)}, u32[]{:S(2)}) %collective-permute-start.7) | collective-permute-done | bytes 98336 | tf_op jit(solution)/shard_map/ppermute | solution.py:46
  24.8 1.3 %scores.6 = (bf16[2048,4096]{1,0:T(8,128)(2,1)S(1)}, bf16[512,192]{1,0:T(8,128)(2,1)S(1)}, f32[2,512]{1,0:T(2,128)S(1)}) custom-call(bf16[4,2,192,128]{3,2,1,0:T(8,128)(2,1)S(1)} %join.3.refs_0_, bf16[2048,256]{1,0:T(8,128)(2,1)S(1)} %get-tuple-element.31.refs_1_.refs_2_.refs_4_, ...), custom_call_target="tpu_custom_call", output_to_operand_aliasing={{0}: (4, {})} | custom-call | flops 1 | bytes 1 | tf_op jit(solution)/shard_map/scores/pallas_call | solution.py:35
  26.5 1.3 %scores.7 = (bf16[2048,4096]{1,0:T(8,128)(2,1)S(1)}, bf16[512,192]{1,0:T(8,128)(2,1)S(1)}, f32[4,1024]{1,0:T(4,128)S(1)}) custom-call(f32[2,512]{1,0:T(2,128)S(1)} %get-tuple-element.33.refs_0_, f32[2,512]{1,0:T(2,128)S(1)} %get-tuple-element.37.refs_3_.refs_1_, f32[2,512]{1,0:T(2,128)S(1)} %get-tuple-element.40.refs_2_, ...), custom_call_target="tpu_custom_call", output_to_operand_aliasing={{0}: (7, {})} | custom-call | flops 1 | bytes 1 | tf_op jit(solution)/shard_map/scores/pallas_call | solution.py:35
  28.0 1.0 %collective-permute-done.10.refs_1_ = f32[4,1024]{1,0:T(4,128)S(1)} collective-permute-done((f32[4,1024]{1,0:T(4,128)S(1)}, f32[4,1024]{1,0:T(4,128)S(1)}, u32[]{:S(2)}, u32[]{:S(2)}) %collective-permute-start.10) | collective-permute-done | bytes 16416 | tf_op jit(solution)/shard_map/ppermute | solution.py:46
  29.1 1.0 %collective-permute-start.11 = (f32[4,1024]{1,0:T(4,128)S(1)}, f32[4,1024]{1,0:T(4,128)S(1)}, u32[]{:S(2)}, u32[]{:S(2)}) collective-permute-start(f32[4,1024]{1,0:T(4,128)S(1)} %relay.3.refs_0_), channel_id=1, source_target_pairs={{0,1},{1,0},{2,7},{3,6},{4,5},{5,4},{6,3},{7,2},{8,9},{9,8},{10,15... | collective-permute-start | bytes 49160 | tf_op jit(solution)/shard_map/ppermute | solution.py:307
  30.1 1.5 %collective-permute-start.13 = (f32[4,1024]{1,0:T(4,128)S(1)}, f32[4,1024]{1,0:T(4,128)S(1)}, u32[]{:S(2)}, u32[]{:S(2)}) collective-permute-start(f32[4,1024]{1,0:T(4,128)S(1)} %relay.3.refs_0_), channel_id=1, source_target_pairs={{0,4},{1,5},{2,6},{3,7},{4,0},{5,1},{6,2},{7,3},{8,12},{9,13},{10,... | collective-permute-start | bytes 49160 | tf_op jit(solution)/shard_map/ppermute | solution.py:307
  31.7 1.3 %collective-permute-done.11.refs_1_ = f32[4,1024]{1,0:T(4,128)S(1)} collective-permute-done((f32[4,1024]{1,0:T(4,128)S(1)}, f32[4,1024]{1,0:T(4,128)S(1)}, u32[]{:S(2)}, u32[]{:S(2)}) %collective-permute-start.11) | collective-permute-done | bytes 16416 | tf_op jit(solution)/shard_map/ppermute | solution.py:307
  32.9 1.0 %collective-permute-done.13.refs_3_ = f32[4,1024]{1,0:T(4,128)S(1)} collective-permute-done((f32[4,1024]{1,0:T(4,128)S(1)}, f32[4,1024]{1,0:T(4,128)S(1)}, u32[]{:S(2)}, u32[]{:S(2)}) %collective-permute-start.13) | collective-permute-done | bytes 16416 | tf_op jit(solution)/shard_map/ppermute | solution.py:307
  34.5 2.7 %collective-permute-start.16 = (f32[4,1024]{1,0:T(4,128)S(1)}, f32[4,1024]{1,0:T(4,128)S(1)}, u32[]{:S(2)}, u32[]{:S(2)}) collective-permute-start(f32[4,1024]{1,0:T(4,128)S(1)} %relay.4.refs_0_), channel_id=1, source_target_pairs={{0,16},{2,18},{4,20},{6,22},{8,24},{10,26},{12,28},{14,30},{16,0},... | collective-permute-start | bytes 49160 | tf_op jit(solution)/shard_map/ppermute | solution.py:307
  37.2 0.7 %collective-permute-done.14.refs_1_ = f32[4,1024]{1,0:T(4,128)S(1)} collective-permute-done((f32[4,1024]{1,0:T(4,128)S(1)}, f32[4,1024]{1,0:T(4,128)S(1)}, u32[]{:S(2)}, u32[]{:S(2)}) %collective-permute-start.14) | collective-permute-done | bytes 16416 | tf_op jit(solution)/shard_map/ppermute | solution.py:307
  37.9 0.8 %collective-permute-start.15 = (f32[4,1024]{1,0:T(4,128)S(1)}, f32[4,1024]{1,0:T(4,128)S(1)}, u32[]{:S(2)}, u32[]{:S(2)}) collective-permute-start(f32[4,1024]{1,0:T(4,128)S(1)} %collective-permute-done.14.refs_1_), channel_id=1, source_target_pairs={{0,2},{2,0},{4,6},{6,4},{1,3},{3,1},{5,7},{7,5},{8,10},{10,8},{12,... | collective-permute-start | bytes 49160 | tf_op jit(solution)/shard_map/ppermute | solution.py:46
  38.8 0.5 %collective-permute-done.16.refs_3_ = f32[4,1024]{1,0:T(4,128)S(1)} collective-permute-done((f32[4,1024]{1,0:T(4,128)S(1)}, f32[4,1024]{1,0:T(4,128)S(1)}, u32[]{:S(2)}, u32[]{:S(2)}) %collective-permute-start.16) | collective-permute-done | bytes 16416 | tf_op jit(solution)/shard_map/ppermute | solution.py:307
  39.6 3.5 %gradient.1 = f32[192,2048]{1,0:T(8,128)} custom-call(f32[4,1024]{1,0:T(4,128)S(1)} %relay.5.total_ref, f32[1,128]{1,0:T(1,128)S(1)} %get-tuple-element.29.refs_5_.refs_3_.refs_4_.refs_6_.peak_ref, f32[192,2048]{1,0:T(8,128)S(1)} %get-tuple-element.43.weight_unit, f32[1,2048]{1,0:T(1,128)S(1)} %get-tuple-element.44.weight_scale, ...), custom_call_target="tpu_custom_call" | custom-call | flops 1 | bytes 1 | tf_op jit(solution)/shard_map/gradient/pallas_call | solution.py:35
  (23 shorter events, 3.4 us)
Async XLA Ops:
  0.6 4.8 %collective-permute-start = (s32[1,256]{1,0:T(1,128)}, s32[1,256]{1,0:T(1,128)S(1)}, u32[]{:S(2)}, u32[]{:S(2)}) collective-permute-start(s32[1,256]{1,0:T(1,128)} %param.10), channel_id=1, source_target_pairs={{0,1},{1,0},{2,3},{3,2},{4,5},{5,4},{6,7},{7,6},{8,9},{9,8},{10,11... | collective-permute-start | bytes 3080 | tf_op jit(solution)/shard_map/ppermute | solution.py:46
  5.6 11.6 %collective-permute-start.4 = (bf16[2,192,128]{2,1,0:T(8,128)(2,1)S(1)}, bf16[2,192,128]{2,1,0:T(8,128)(2,1)S(1)}, u32[]{:S(2)}, u32[]{:S(2)}) collective-permute-start(bf16[2,192,128]{2,1,0:T(8,128)(2,1)S(1)} %pack.1.refs_0_), channel_id=1, source_target_pairs={{0,1},{1,0},{2,3},{3,2},{4,5},{5,4},{6,7},{7,6},{8,9},{9,8},{10,11... | collective-permute-start | bytes 294920 | tf_op jit(solution)/shard_map/ppermute | solution.py:46
  7.7 9.5 %collective-permute-start.3 = (bf16[2,192,128]{2,1,0:T(8,128)(2,1)S(1)}, bf16[2,192,128]{2,1,0:T(8,128)(2,1)S(1)}, u32[]{:S(2)}, u32[]{:S(2)}) collective-permute-start(bf16[2,192,128]{2,1,0:T(8,128)(2,1)S(1)} %pack.1.refs_0_), channel_id=1, source_target_pairs={{0,24},{8,16},{16,8},{24,0},{1,25},{9,17},{17,9},{25,1},{2,26},{10... | collective-permute-start | bytes 294920 | tf_op jit(solution)/shard_map/ppermute | solution.py:46
  11.3 6.9 %collective-permute-start.2 = (bf16[2,192,128]{2,1,0:T(8,128)(2,1)S(1)}, bf16[2,192,128]{2,1,0:T(8,128)(2,1)S(1)}, u32[]{:S(2)}, u32[]{:S(2)}) collective-permute-start(bf16[2,192,128]{2,1,0:T(8,128)(2,1)S(1)} %pack.1.refs_0_), channel_id=1, source_target_pairs={{0,16},{8,24},{16,0},{24,8},{1,17},{9,25},{17,1},{25,9},{2,18},{10... | collective-permute-start | bytes 294920 | tf_op jit(solution)/shard_map/ppermute | solution.py:46
  11.3 6.9 %collective-permute-start.1 = (bf16[2,192,128]{2,1,0:T(8,128)(2,1)S(1)}, bf16[2,192,128]{2,1,0:T(8,128)(2,1)S(1)}, u32[]{:S(2)}, u32[]{:S(2)}) collective-permute-start(bf16[2,192,128]{2,1,0:T(8,128)(2,1)S(1)} %pack.1.refs_0_), channel_id=1, source_target_pairs={{0,8},{8,0},{16,24},{24,16},{1,9},{9,1},{17,25},{25,17},{2,10},{10... | collective-permute-start | bytes 294920 | tf_op jit(solution)/shard_map/ppermute | solution.py:46
  18.3 6.3 %collective-permute-start.8 = (bf16[2,2,208,128]{3,2,1,0:T(8,128)(2,1)S(1)}, bf16[2,2,208,128]{3,2,1,0:T(8,128)(2,1)S(1)}, u32[]{:S(2)}, u32[]{:S(2)}) collective-permute-start(bf16[2,2,208,128]{3,2,1,0:T(8,128)(2,1)S(1)} %get-tuple-element.38), channel_id=1, source_target_pairs={{0,1},{1,0},{2,3},{3,2},{4,5},{5,4},{6,7},{7,6},{8,9},{9,8},{10,11... | collective-permute-start | bytes 638984 | tf_op jit(solution)/shard_map/ppermute | solution.py:46
  18.9 2.3 %collective-permute-start.5 = (bf16[2,2,192,128]{3,2,1,0:T(8,128)(2,1)S(1)}, bf16[2,2,192,128]{3,2,1,0:T(8,128)(2,1)S(1)}, u32[]{:S(2)}, u32[]{:S(2)}) collective-permute-start(bf16[2,2,192,128]{3,2,1,0:T(8,128)(2,1)S(1)} %get-tuple-element.34), channel_id=1, source_target_pairs={{0,2},{2,0},{4,6},{6,4},{1,3},{3,1},{5,7},{7,5},{8,10},{10,8},{12,... | collective-permute-start | bytes 589832 | tf_op jit(solution)/shard_map/ppermute | solution.py:46
  18.9 2.3 %collective-permute-start.6 = (bf16[2,2,192,128]{3,2,1,0:T(8,128)(2,1)S(1)}, bf16[2,2,192,128]{3,2,1,0:T(8,128)(2,1)S(1)}, u32[]{:S(2)}, u32[]{:S(2)}) collective-permute-start(bf16[2,2,192,128]{3,2,1,0:T(8,128)(2,1)S(1)} %get-tuple-element.35), channel_id=1, source_target_pairs={{0,2},{2,0},{4,6},{6,4},{1,3},{3,1},{5,7},{7,5},{8,10},{10,8},{12,... | collective-permute-start | bytes 589832 | tf_op jit(solution)/shard_map/ppermute | solution.py:46
  19.4 4.7 %collective-permute-start.7 = (bf16[2,192,128]{2,1,0:T(8,128)(2,1)S(1)}, bf16[2,192,128]{2,1,0:T(8,128)(2,1)S(1)}, u32[]{:S(2)}, u32[]{:S(2)}) collective-permute-start(bf16[2,192,128]{2,1,0:T(8,128)(2,1)S(1)} %collective-permute-done.4.refs_4_.refs_0_), channel_id=1, source_target_pairs={{0,8},{8,0},{16,24},{24,16},{1,9},{9,1},{17,25},{25,17},{2,10},{10... | collective-permute-start | bytes 294920 | tf_op jit(solution)/shard_map/ppermute | solution.py:46
  24.7 1.8 %collective-permute-start.9 = (bf16[4,2,192,128]{3,2,1,0:T(8,128)(2,1)S(1)}, bf16[4,2,192,128]{3,2,1,0:T(8,128)(2,1)S(1)}, u32[]{:S(2)}, u32[]{:S(2)}) collective-permute-start(bf16[4,2,192,128]{3,2,1,0:T(8,128)(2,1)S(1)} %join.3.refs_0_), channel_id=1, source_target_pairs={{0,2},{2,0},{4,6},{6,4},{1,3},{3,1},{5,7},{7,5},{8,10},{10,8},{12,... | collective-permute-start | bytes 1179656 | tf_op jit(solution)/shard_map/ppermute | solution.py:46
  27.8 1.2 %collective-permute-start.10 = (f32[4,1024]{1,0:T(4,128)S(1)}, f32[4,1024]{1,0:T(4,128)S(1)}, u32[]{:S(2)}, u32[]{:S(2)}) collective-permute-start(f32[4,1024]{1,0:T(4,128)S(1)} %get-tuple-element.42.refs_0_), channel_id=1, source_target_pairs={{0,2},{2,0},{4,6},{6,4},{1,3},{3,1},{5,7},{7,5},{8,10},{10,8},{12,... | collective-permute-start | bytes 49160 | tf_op jit(solution)/shard_map/ppermute | solution.py:46
  29.1 3.8 %collective-permute-start.11 = (f32[4,1024]{1,0:T(4,128)S(1)}, f32[4,1024]{1,0:T(4,128)S(1)}, u32[]{:S(2)}, u32[]{:S(2)}) collective-permute-start(f32[4,1024]{1,0:T(4,128)S(1)} %relay.3.refs_0_), channel_id=1, source_target_pairs={{0,1},{1,0},{2,7},{3,6},{4,5},{5,4},{6,3},{7,2},{8,9},{9,8},{10,15... | collective-permute-start | bytes 49160 | tf_op jit(solution)/shard_map/ppermute | solution.py:307
  30.1 3.8 %collective-permute-start.13 = (f32[4,1024]{1,0:T(4,128)S(1)}, f32[4,1024]{1,0:T(4,128)S(1)}, u32[]{:S(2)}, u32[]{:S(2)}) collective-permute-start(f32[4,1024]{1,0:T(4,128)S(1)} %relay.3.refs_0_), channel_id=1, source_target_pairs={{0,4},{1,5},{2,6},{3,7},{4,0},{5,1},{6,2},{7,3},{8,12},{9,13},{10,... | collective-permute-start | bytes 49160 | tf_op jit(solution)/shard_map/ppermute | solution.py:307
  32.9 1.2 %collective-permute-start.12 = (f32[4,1024]{1,0:T(4,128)S(1)}, f32[4,1024]{1,0:T(4,128)S(1)}, u32[]{:S(2)}, u32[]{:S(2)}) collective-permute-start(f32[4,1024]{1,0:T(4,128)S(1)} %collective-permute-done.11.refs_1_), channel_id=1, source_target_pairs={{0,2},{2,0},{4,6},{6,4},{1,3},{3,1},{5,7},{7,5},{8,10},{10,8},{12,... | collective-permute-start | bytes 49160 | tf_op jit(solution)/shard_map/ppermute | solution.py:46
  34.1 3.8 %collective-permute-start.14 = (f32[4,1024]{1,0:T(4,128)S(1)}, f32[4,1024]{1,0:T(4,128)S(1)}, u32[]{:S(2)}, u32[]{:S(2)}) collective-permute-start(f32[4,1024]{1,0:T(4,128)S(1)} %relay.4.refs_0_), channel_id=1, source_target_pairs={{0,8},{2,26},{4,12},{6,30},{8,0},{10,18},{12,4},{14,22},{16,24},{1... | collective-permute-start | bytes 49160 | tf_op jit(solution)/shard_map/ppermute | solution.py:307
  34.5 4.8 %collective-permute-start.16 = (f32[4,1024]{1,0:T(4,128)S(1)}, f32[4,1024]{1,0:T(4,128)S(1)}, u32[]{:S(2)}, u32[]{:S(2)}) collective-permute-start(f32[4,1024]{1,0:T(4,128)S(1)} %relay.4.refs_0_), channel_id=1, source_target_pairs={{0,16},{2,18},{4,20},{6,22},{8,24},{10,26},{12,28},{14,30},{16,0},... | collective-permute-start | bytes 49160 | tf_op jit(solution)/shard_map/ppermute | solution.py:307
  37.9 1.7 %collective-permute-start.15 = (f32[4,1024]{1,0:T(4,128)S(1)}, f32[4,1024]{1,0:T(4,128)S(1)}, u32[]{:S(2)}, u32[]{:S(2)}) collective-permute-start(f32[4,1024]{1,0:T(4,128)S(1)} %collective-permute-done.14.refs_1_), channel_id=1, source_target_pairs={{0,2},{2,0},{4,6},{6,4},{1,3},{3,1},{5,7},{7,5},{8,10},{10,8},{12,... | collective-permute-start | bytes 49160 | tf_op jit(solution)/shard_map/ppermute | solution.py:46

commit v27 on v26

--- a/solution.py
+++ b/solution.py
@@ -321,7 +321,7 @@
     n_proto, n_dp = lax.axis_size("proto"), lax.axis_size("dp")
     total = add_up([total, swap(total, "proto")])
     if n_proto == 4 and n_dp == 2:
-        return exchange(total, ("proto", "dp"), lambda odd: (2 * odd, 1), lambda odd: (2, 0))
+        return exchange(total, ("proto", "dp"), lambda odd: (2, odd), lambda odd: (0, 1))
     steps = [(up, over) for up in range(0, n_proto, 2) for over in range(n_dp)][1:]
     return add_up([total, *[across(total, *step) for step in steps]])
 

time: 43.3 us -> 43.3 us (level)
  waiting for transfers between devices: 9.44 us -> 9.98 us
  starting transfers between devices: 17.7 us -> 17.2 us
    ppermute x4, waiting for transfers between devices: 3.53 us -> 4.26 us  [permute(): return lax.ppermute(total, axes, pairs)]
  transfers between devices with their start and end apart: 17 -> 17, of which waited for: 12 -> 11; matrix products, arithmetic and copies ran while one was open for 0% -> 0% of each run, Pallas kernels for 23% -> 23%
where the time goes in v27:
time: 43.3 us; the launch traced here: 43.2 us
  starting transfers between devices  17.2 us (40%)
  Pallas kernels  15.3 us (35%)
  waiting for transfers between devices  9.98 us (23%)
  between operations  0.76 us (2%)
    pallas_call x13, Pallas kernels, call(): pl.pallas_call(kernel, out_shape=out_shape, compiler_params=pltpu.Compile...  15.3 us
    ppermute x13, starting transfers between devices, swap(): lax.ppermute(block, axis, [(i, i ^ apart) for i in range(lax.axis_size(ax...  11.8 us
    ppermute x13, waiting for transfers between devices, swap(): lax.ppermute(block, axis, [(i, i ^ apart) for i in range(lax.axis_size(ax...  5.73 us
    ppermute x4, starting transfers between devices, permute(): return lax.ppermute(total, axes, pairs)  5.39 us
    ppermute x4, waiting for transfers between devices, permute(): return lax.ppermute(total, axes, pairs)  4.26 us
  transfers between devices with their start and end apart: 17, of which 11 were waited for; matrix products, arithmetic and copies ran while one was open for 0% of the time, Pallas kernels for 23%

profile of v27, /device:TPU:0, one launch (start us, length us, event | category | flops | bytes accessed | tf_op | source)
XLA Modules:
  0.0 43.2 jit_solution(1684108490239923495)
XLA Ops:
  0.6 3.0 %collective-permute-start = (s32[1,256]{1,0:T(1,128)}, s32[1,256]{1,0:T(1,128)S(1)}, u32[]{:S(2)}, u32[]{:S(2)}) collective-permute-start(s32[1,256]{1,0:T(1,128)} %param.10), channel_id=1, source_target_pairs={{0,1},{1,0},{2,3},{3,2},{4,5},{5,4},{6,7},{7,6},{8,9},{9,8},{10,11... | collective-permute-start | bytes 3080 | tf_op jit(solution)/shard_map/ppermute | solution.py:46
  3.6 0.9 %fetch.1 = (bf16[192,128]{1,0:T(8,128)(2,1)S(1)}, bf16[192,256]{1,0:T(8,128)(2,1)S(1)}) custom-call(bf16[192,256]{1,0:T(8,128)(2,1)} %bitcast.7, bf16[192,256]{1,0:T(8,128)(2,1)} %bitcast.8), custom_call_target="tpu_custom_call" | custom-call | flops 1 | bytes 1 | tf_op jit(solution)/shard_map/fetch/pallas_call | solution.py:35
  4.6 0.8 %collective-permute-done.index_ref = s32[1,256]{1,0:T(1,128)S(1)} collective-permute-done((s32[1,256]{1,0:T(1,128)}, s32[1,256]{1,0:T(1,128)S(1)}, u32[]{:S(2)}, u32[]{:S(2)}) %collective-permute-start) | collective-permute-done | bytes 1056 | tf_op jit(solution)/shard_map/ppermute | solution.py:46
  5.6 2.1 %collective-permute-start.4 = (bf16[2,192,128]{2,1,0:T(8,128)(2,1)S(1)}, bf16[2,192,128]{2,1,0:T(8,128)(2,1)S(1)}, u32[]{:S(2)}, u32[]{:S(2)}) collective-permute-start(bf16[2,192,128]{2,1,0:T(8,128)(2,1)S(1)} %pack.1.refs_0_), channel_id=1, source_target_pairs={{0,1},{1,0},{2,3},{3,2},{4,5},{5,4},{6,7},{7,6},{8,9},{9,8},{10,11... | collective-permute-start | bytes 294920 | tf_op jit(solution)/shard_map/ppermute | solution.py:46
  7.7 3.6 %collective-permute-start.3 = (bf16[2,192,128]{2,1,0:T(8,128)(2,1)S(1)}, bf16[2,192,128]{2,1,0:T(8,128)(2,1)S(1)}, u32[]{:S(2)}, u32[]{:S(2)}) collective-permute-start(bf16[2,192,128]{2,1,0:T(8,128)(2,1)S(1)} %pack.1.refs_0_), channel_id=1, source_target_pairs={{0,24},{8,16},{16,8},{24,0},{1,25},{9,17},{17,9},{25,1},{2,26},{10... | collective-permute-start | bytes 294920 | tf_op jit(solution)/shard_map/ppermute | solution.py:46
  11.3 0.8 %collective-permute-start.1 = (bf16[2,192,128]{2,1,0:T(8,128)(2,1)S(1)}, bf16[2,192,128]{2,1,0:T(8,128)(2,1)S(1)}, u32[]{:S(2)}, u32[]{:S(2)}) collective-permute-start(bf16[2,192,128]{2,1,0:T(8,128)(2,1)S(1)} %pack.1.refs_0_), channel_id=1, source_target_pairs={{0,8},{8,0},{16,24},{24,16},{1,9},{9,1},{17,25},{25,17},{2,10},{10... | collective-permute-start | bytes 294920 | tf_op jit(solution)/shard_map/ppermute | solution.py:46
  12.1 5.1 %prep.1 = (f32[192,4096]{1,0:T(8,128)}, bf16[2048,256]{1,0:T(8,128)(2,1)S(1)}, bf16[2048,256]{1,0:T(8,128)(2,1)S(1)}, f32[192,2048]{1,0:T(8,128)S(1)}, f32[1,2048]{1,0:T(1,128)S(1)}, /*index=5*/f32[1,128]{1,0:T(1,128)S(1)}) custom-call(f32[192,4096]{1,0:T(8,128)} %teacher_hbm.1, f32[192,4096]{1,0:T(8,128)} %student_hbm.1, f32[1,16384]{1,0:T(1,128)} %bitcast.9), custom_call_target="tpu_custom_call" | custom-call | flops 1 | bytes 1 | tf_op jit(solution)/shard_map/prep/pallas_call | solution.py:35
  17.2 1.0 %collective-permute-done.2.refs_2_ = bf16[2,192,128]{2,1,0:T(8,128)(2,1)S(1)} collective-permute-done((bf16[2,192,128]{2,1,0:T(8,128)(2,1)S(1)}, bf16[2,192,128]{2,1,0:T(8,128)(2,1)S(1)}, u32[]{:S(2)}, u32[]{:S(2)}) %collective-permute-start.2) | collective-permute-done | bytes 98336 | tf_op jit(solution)/shard_map/ppermute | solution.py:46
  18.3 0.6 %collective-permute-start.8 = (bf16[2,2,208,128]{3,2,1,0:T(8,128)(2,1)S(1)}, bf16[2,2,208,128]{3,2,1,0:T(8,128)(2,1)S(1)}, u32[]{:S(2)}, u32[]{:S(2)}) collective-permute-start(bf16[2,2,208,128]{3,2,1,0:T(8,128)(2,1)S(1)} %get-tuple-element.38), channel_id=1, source_target_pairs={{0,1},{1,0},{2,3},{3,2},{4,5},{5,4},{6,7},{7,6},{8,9},{9,8},{10,11... | collective-permute-start | bytes 638984 | tf_op jit(solution)/shard_map/ppermute | solution.py:46
  19.9 1.3 %scores.4 = (bf16[2048,4096]{1,0:T(8,128)(2,1)S(1)}, bf16[512,192]{1,0:T(8,128)(2,1)S(1)}, f32[2,512]{1,0:T(2,128)S(1)}) custom-call(bf16[4,2,192,128]{3,2,1,0:T(8,128)(2,1)S(1)} %get-tuple-element.30.refs_0_, bf16[2048,256]{1,0:T(8,128)(2,1)S(1)} %get-tuple-element.31.refs_1_.refs_2_.refs_4_, ...), custom_call_target="tpu_custom_call" | custom-call | flops 1 | bytes 1 | tf_op jit(solution)/shard_map/scores/pallas_call | solution.py:35
  21.2 1.3 %scores.5 = (bf16[2048,4096]{1,0:T(8,128)(2,1)S(1)}, bf16[512,192]{1,0:T(8,128)(2,1)S(1)}, f32[2,512]{1,0:T(2,128)S(1)}) custom-call(bf16[2,2,192,128]{3,2,1,0:T(8,128)(2,1)S(1)} %collective-permute-done.5.refs_0_, bf16[2,2,192,128]{3,2,1,0:T(8,128)(2,1)S(1)} %collective-permute-done.6.refs_1_, ...), custom_call_target="tpu_custom_call", output_to_operand_aliasing={{0}: (5, {})} | custom-call | flops 1 | bytes 1 | tf_op jit(solution)/shard_map/scores/pallas_call | solution.py:35
  22.5 1.6 %collective-permute-done.7.refs_1_ = bf16[2,192,128]{2,1,0:T(8,128)(2,1)S(1)} collective-permute-done((bf16[2,192,128]{2,1,0:T(8,128)(2,1)S(1)}, bf16[2,192,128]{2,1,0:T(8,128)(2,1)S(1)}, u32[]{:S(2)}, u32[]{:S(2)}) %collective-permute-start.7) | collective-permute-done | bytes 98336 | tf_op jit(solution)/shard_map/ppermute | solution.py:46
  24.1 0.5 %collective-permute-done.8.refs_2_ = bf16[2,2,208,128]{3,2,1,0:T(8,128)(2,1)S(1)} collective-permute-done((bf16[2,2,208,128]{3,2,1,0:T(8,128)(2,1)S(1)}, bf16[2,2,208,128]{3,2,1,0:T(8,128)(2,1)S(1)}, u32[]{:S(2)}, u32[]{:S(2)}) %collective-permute-start.8) | collective-permute-done | bytes 213024 | tf_op jit(solution)/shard_map/ppermute | solution.py:46
  24.8 1.3 %scores.6 = (bf16[2048,4096]{1,0:T(8,128)(2,1)S(1)}, bf16[512,192]{1,0:T(8,128)(2,1)S(1)}, f32[2,512]{1,0:T(2,128)S(1)}) custom-call(bf16[4,2,192,128]{3,2,1,0:T(8,128)(2,1)S(1)} %join.3.refs_0_, bf16[2048,256]{1,0:T(8,128)(2,1)S(1)} %get-tuple-element.31.refs_1_.refs_2_.refs_4_, ...), custom_call_target="tpu_custom_call", output_to_operand_aliasing={{0}: (4, {})} | custom-call | flops 1 | bytes 1 | tf_op jit(solution)/shard_map/scores/pallas_call | solution.py:35
  26.5 1.3 %scores.7 = (bf16[2048,4096]{1,0:T(8,128)(2,1)S(1)}, bf16[512,192]{1,0:T(8,128)(2,1)S(1)}, f32[4,1024]{1,0:T(4,128)S(1)}) custom-call(f32[2,512]{1,0:T(2,128)S(1)} %get-tuple-element.33.refs_0_, f32[2,512]{1,0:T(2,128)S(1)} %get-tuple-element.37.refs_3_.refs_1_, f32[2,512]{1,0:T(2,128)S(1)} %get-tuple-element.40.refs_2_, ...), custom_call_target="tpu_custom_call", output_to_operand_aliasing={{0}: (7, {})} | custom-call | flops 1 | bytes 1 | tf_op jit(solution)/shard_map/scores/pallas_call | solution.py:35
  28.0 1.0 %collective-permute-done.10.refs_1_ = f32[4,1024]{1,0:T(4,128)S(1)} collective-permute-done((f32[4,1024]{1,0:T(4,128)S(1)}, f32[4,1024]{1,0:T(4,128)S(1)}, u32[]{:S(2)}, u32[]{:S(2)}) %collective-permute-start.10) | collective-permute-done | bytes 16416 | tf_op jit(solution)/shard_map/ppermute | solution.py:46
  29.1 1.6 %collective-permute-start.11 = (f32[4,1024]{1,0:T(4,128)S(1)}, f32[4,1024]{1,0:T(4,128)S(1)}, u32[]{:S(2)}, u32[]{:S(2)}) collective-permute-start(f32[4,1024]{1,0:T(4,128)S(1)} %relay.3.refs_0_), channel_id=1, source_target_pairs={{0,4},{1,5},{2,7},{3,6},{4,0},{5,1},{6,3},{7,2},{8,12},{9,13},{10,... | collective-permute-start | bytes 49160 | tf_op jit(solution)/shard_map/ppermute | solution.py:307
  30.7 1.0 %collective-permute-start.13 = (f32[4,1024]{1,0:T(4,128)S(1)}, f32[4,1024]{1,0:T(4,128)S(1)}, u32[]{:S(2)}, u32[]{:S(2)}) collective-permute-start(f32[4,1024]{1,0:T(4,128)S(1)} %relay.3.refs_0_), channel_id=1, source_target_pairs={{0,1},{1,0},{2,3},{3,2},{4,5},{5,4},{6,7},{7,6},{8,9},{9,8},{10,11... | collective-permute-start | bytes 49160 | tf_op jit(solution)/shard_map/ppermute | solution.py:307
  31.7 1.2 %collective-permute-done.11.refs_1_ = f32[4,1024]{1,0:T(4,128)S(1)} collective-permute-done((f32[4,1024]{1,0:T(4,128)S(1)}, f32[4,1024]{1,0:T(4,128)S(1)}, u32[]{:S(2)}, u32[]{:S(2)}) %collective-permute-start.11) | collective-permute-done | bytes 16416 | tf_op jit(solution)/shard_map/ppermute | solution.py:307
  32.9 1.5 %collective-permute-done.13.refs_3_ = f32[4,1024]{1,0:T(4,128)S(1)} collective-permute-done((f32[4,1024]{1,0:T(4,128)S(1)}, f32[4,1024]{1,0:T(4,128)S(1)}, u32[]{:S(2)}, u32[]{:S(2)}) %collective-permute-start.13) | collective-permute-done | bytes 16416 | tf_op jit(solution)/shard_map/ppermute | solution.py:307
  34.5 2.7 %collective-permute-start.16 = (f32[4,1024]{1,0:T(4,128)S(1)}, f32[4,1024]{1,0:T(4,128)S(1)}, u32[]{:S(2)}, u32[]{:S(2)}) collective-permute-start(f32[4,1024]{1,0:T(4,128)S(1)} %relay.4.refs_0_), channel_id=1, source_target_pairs={{0,16},{2,18},{4,20},{6,22},{8,24},{10,26},{12,28},{14,30},{16,0},... | collective-permute-start | bytes 49160 | tf_op jit(solution)/shard_map/ppermute | solution.py:307
  37.3 1.0 %collective-permute-done.14.refs_1_ = f32[4,1024]{1,0:T(4,128)S(1)} collective-permute-done((f32[4,1024]{1,0:T(4,128)S(1)}, f32[4,1024]{1,0:T(4,128)S(1)}, u32[]{:S(2)}, u32[]{:S(2)}) %collective-permute-start.14) | collective-permute-done | bytes 16416 | tf_op jit(solution)/shard_map/ppermute | solution.py:307
  38.7 0.5 %collective-permute-done.16.refs_3_ = f32[4,1024]{1,0:T(4,128)S(1)} collective-permute-done((f32[4,1024]{1,0:T(4,128)S(1)}, f32[4,1024]{1,0:T(4,128)S(1)}, u32[]{:S(2)}, u32[]{:S(2)}) %collective-permute-start.16) | collective-permute-done | bytes 16416 | tf_op jit(solution)/shard_map/ppermute | solution.py:307
  39.6 3.5 %gradient.1 = f32[192,2048]{1,0:T(8,128)} custom-call(f32[4,1024]{1,0:T(4,128)S(1)} %relay.5.total_ref, f32[1,128]{1,0:T(1,128)S(1)} %get-tuple-element.29.refs_5_.refs_3_.refs_4_.refs_6_.peak_ref, f32[192,2048]{1,0:T(8,128)S(1)} %get-tuple-element.43.weight_unit, f32[1,2048]{1,0:T(1,128)S(1)} %get-tuple-element.44.weight_scale, ...), custom_call_target="tpu_custom_call" | custom-call | flops 1 | bytes 1 | tf_op jit(solution)/shard_map/gradient/pallas_call | solution.py:35
  (23 shorter events, 2.9 us)
Async XLA Ops:
  0.6 4.8 %collective-permute-start = (s32[1,256]{1,0:T(1,128)}, s32[1,256]{1,0:T(1,128)S(1)}, u32[]{:S(2)}, u32[]{:S(2)}) collective-permute-start(s32[1,256]{1,0:T(1,128)} %param.10), channel_id=1, source_target_pairs={{0,1},{1,0},{2,3},{3,2},{4,5},{5,4},{6,7},{7,6},{8,9},{9,8},{10,11... | collective-permute-start | bytes 3080 | tf_op jit(solution)/shard_map/ppermute | solution.py:46
  5.6 11.6 %collective-permute-start.4 = (bf16[2,192,128]{2,1,0:T(8,128)(2,1)S(1)}, bf16[2,192,128]{2,1,0:T(8,128)(2,1)S(1)}, u32[]{:S(2)}, u32[]{:S(2)}) collective-permute-start(bf16[2,192,128]{2,1,0:T(8,128)(2,1)S(1)} %pack.1.refs_0_), channel_id=1, source_target_pairs={{0,1},{1,0},{2,3},{3,2},{4,5},{5,4},{6,7},{7,6},{8,9},{9,8},{10,11... | collective-permute-start | bytes 294920 | tf_op jit(solution)/shard_map/ppermute | solution.py:46
  7.7 9.5 %collective-permute-start.3 = (bf16[2,192,128]{2,1,0:T(8,128)(2,1)S(1)}, bf16[2,192,128]{2,1,0:T(8,128)(2,1)S(1)}, u32[]{:S(2)}, u32[]{:S(2)}) collective-permute-start(bf16[2,192,128]{2,1,0:T(8,128)(2,1)S(1)} %pack.1.refs_0_), channel_id=1, source_target_pairs={{0,24},{8,16},{16,8},{24,0},{1,25},{9,17},{17,9},{25,1},{2,26},{10... | collective-permute-start | bytes 294920 | tf_op jit(solution)/shard_map/ppermute | solution.py:46
  11.3 6.9 %collective-permute-start.2 = (bf16[2,192,128]{2,1,0:T(8,128)(2,1)S(1)}, bf16[2,192,128]{2,1,0:T(8,128)(2,1)S(1)}, u32[]{:S(2)}, u32[]{:S(2)}) collective-permute-start(bf16[2,192,128]{2,1,0:T(8,128)(2,1)S(1)} %pack.1.refs_0_), channel_id=1, source_target_pairs={{0,16},{8,24},{16,0},{24,8},{1,17},{9,25},{17,1},{25,9},{2,18},{10... | collective-permute-start | bytes 294920 | tf_op jit(solution)/shard_map/ppermute | solution.py:46
  11.3 6.9 %collective-permute-start.1 = (bf16[2,192,128]{2,1,0:T(8,128)(2,1)S(1)}, bf16[2,192,128]{2,1,0:T(8,128)(2,1)S(1)}, u32[]{:S(2)}, u32[]{:S(2)}) collective-permute-start(bf16[2,192,128]{2,1,0:T(8,128)(2,1)S(1)} %pack.1.refs_0_), channel_id=1, source_target_pairs={{0,8},{8,0},{16,24},{24,16},{1,9},{9,1},{17,25},{25,17},{2,10},{10... | collective-permute-start | bytes 294920 | tf_op jit(solution)/shard_map/ppermute | solution.py:46
  18.3 6.3 %collective-permute-start.8 = (bf16[2,2,208,128]{3,2,1,0:T(8,128)(2,1)S(1)}, bf16[2,2,208,128]{3,2,1,0:T(8,128)(2,1)S(1)}, u32[]{:S(2)}, u32[]{:S(2)}) collective-permute-start(bf16[2,2,208,128]{3,2,1,0:T(8,128)(2,1)S(1)} %get-tuple-element.38), channel_id=1, source_target_pairs={{0,1},{1,0},{2,3},{3,2},{4,5},{5,4},{6,7},{7,6},{8,9},{9,8},{10,11... | collective-permute-start | bytes 638984 | tf_op jit(solution)/shard_map/ppermute | solution.py:46
  18.9 2.3 %collective-permute-start.5 = (bf16[2,2,192,128]{3,2,1,0:T(8,128)(2,1)S(1)}, bf16[2,2,192,128]{3,2,1,0:T(8,128)(2,1)S(1)}, u32[]{:S(2)}, u32[]{:S(2)}) collective-permute-start(bf16[2,2,192,128]{3,2,1,0:T(8,128)(2,1)S(1)} %get-tuple-element.34), channel_id=1, source_target_pairs={{0,2},{2,0},{4,6},{6,4},{1,3},{3,1},{5,7},{7,5},{8,10},{10,8},{12,... | collective-permute-start | bytes 589832 | tf_op jit(solution)/shard_map/ppermute | solution.py:46
  18.9 2.3 %collective-permute-start.6 = (bf16[2,2,192,128]{3,2,1,0:T(8,128)(2,1)S(1)}, bf16[2,2,192,128]{3,2,1,0:T(8,128)(2,1)S(1)}, u32[]{:S(2)}, u32[]{:S(2)}) collective-permute-start(bf16[2,2,192,128]{3,2,1,0:T(8,128)(2,1)S(1)} %get-tuple-element.35), channel_id=1, source_target_pairs={{0,2},{2,0},{4,6},{6,4},{1,3},{3,1},{5,7},{7,5},{8,10},{10,8},{12,... | collective-permute-start | bytes 589832 | tf_op jit(solution)/shard_map/ppermute | solution.py:46
  19.4 4.7 %collective-permute-start.7 = (bf16[2,192,128]{2,1,0:T(8,128)(2,1)S(1)}, bf16[2,192,128]{2,1,0:T(8,128)(2,1)S(1)}, u32[]{:S(2)}, u32[]{:S(2)}) collective-permute-start(bf16[2,192,128]{2,1,0:T(8,128)(2,1)S(1)} %collective-permute-done.4.refs_4_.refs_0_), channel_id=1, source_target_pairs={{0,8},{8,0},{16,24},{24,16},{1,9},{9,1},{17,25},{25,17},{2,10},{10... | collective-permute-start | bytes 294920 | tf_op jit(solution)/shard_map/ppermute | solution.py:46
  24.7 1.8 %collective-permute-start.9 = (bf16[4,2,192,128]{3,2,1,0:T(8,128)(2,1)S(1)}, bf16[4,2,192,128]{3,2,1,0:T(8,128)(2,1)S(1)}, u32[]{:S(2)}, u32[]{:S(2)}) collective-permute-start(bf16[4,2,192,128]{3,2,1,0:T(8,128)(2,1)S(1)} %join.3.refs_0_), channel_id=1, source_target_pairs={{0,2},{2,0},{4,6},{6,4},{1,3},{3,1},{5,7},{7,5},{8,10},{10,8},{12,... | collective-permute-start | bytes 1179656 | tf_op jit(solution)/shard_map/ppermute | solution.py:46
  27.8 1.2 %collective-permute-start.10 = (f32[4,1024]{1,0:T(4,128)S(1)}, f32[4,1024]{1,0:T(4,128)S(1)}, u32[]{:S(2)}, u32[]{:S(2)}) collective-permute-start(f32[4,1024]{1,0:T(4,128)S(1)} %get-tuple-element.42.refs_0_), channel_id=1, source_target_pairs={{0,2},{2,0},{4,6},{6,4},{1,3},{3,1},{5,7},{7,5},{8,10},{10,8},{12,... | collective-permute-start | bytes 49160 | tf_op jit(solution)/shard_map/ppermute | solution.py:46
  29.1 3.8 %collective-permute-start.11 = (f32[4,1024]{1,0:T(4,128)S(1)}, f32[4,1024]{1,0:T(4,128)S(1)}, u32[]{:S(2)}, u32[]{:S(2)}) collective-permute-start(f32[4,1024]{1,0:T(4,128)S(1)} %relay.3.refs_0_), channel_id=1, source_target_pairs={{0,4},{1,5},{2,7},{3,6},{4,0},{5,1},{6,3},{7,2},{8,12},{9,13},{10,... | collective-permute-start | bytes 49160 | tf_op jit(solution)/shard_map/ppermute | solution.py:307
  30.7 3.7 %collective-permute-start.13 = (f32[4,1024]{1,0:T(4,128)S(1)}, f32[4,1024]{1,0:T(4,128)S(1)}, u32[]{:S(2)}, u32[]{:S(2)}) collective-permute-start(f32[4,1024]{1,0:T(4,128)S(1)} %relay.3.refs_0_), channel_id=1, source_target_pairs={{0,1},{1,0},{2,3},{3,2},{4,5},{5,4},{6,7},{7,6},{8,9},{9,8},{10,11... | collective-permute-start | bytes 49160 | tf_op jit(solution)/shard_map/ppermute | solution.py:307
  32.9 1.5 %collective-permute-start.12 = (f32[4,1024]{1,0:T(4,128)S(1)}, f32[4,1024]{1,0:T(4,128)S(1)}, u32[]{:S(2)}, u32[]{:S(2)}) collective-permute-start(f32[4,1024]{1,0:T(4,128)S(1)} %collective-permute-done.11.refs_1_), channel_id=1, source_target_pairs={{0,2},{2,0},{4,6},{6,4},{1,3},{3,1},{5,7},{7,5},{8,10},{10,8},{12,... | collective-permute-start | bytes 49160 | tf_op jit(solution)/shard_map/ppermute | solution.py:46
  34.5 3.8 %collective-permute-start.14 = (f32[4,1024]{1,0:T(4,128)S(1)}, f32[4,1024]{1,0:T(4,128)S(1)}, u32[]{:S(2)}, u32[]{:S(2)}) collective-permute-start(f32[4,1024]{1,0:T(4,128)S(1)} %relay.4.refs_0_), channel_id=1, source_target_pairs={{0,8},{2,26},{4,12},{6,30},{8,0},{10,18},{12,4},{14,22},{16,24},{1... | collective-permute-start | bytes 49160 | tf_op jit(solution)/shard_map/ppermute | solution.py:307
  34.5 4.7 %collective-permute-start.16 = (f32[4,1024]{1,0:T(4,128)S(1)}, f32[4,1024]{1,0:T(4,128)S(1)}, u32[]{:S(2)}, u32[]{:S(2)}) collective-permute-start(f32[4,1024]{1,0:T(4,128)S(1)} %relay.4.refs_0_), channel_id=1, source_target_pairs={{0,16},{2,18},{4,20},{6,22},{8,24},{10,26},{12,28},{14,30},{16,0},... | collective-permute-start | bytes 49160 | tf_op jit(solution)/shard_map/ppermute | solution.py:307
  38.3 1.3 %collective-permute-start.15 = (f32[4,1024]{1,0:T(4,128)S(1)}, f32[4,1024]{1,0:T(4,128)S(1)}, u32[]{:S(2)}, u32[]{:S(2)}) collective-permute-start(f32[4,1024]{1,0:T(4,128)S(1)} %collective-permute-done.14.refs_1_), channel_id=1, source_target_pairs={{0,2},{2,0},{4,6},{6,4},{1,3},{3,1},{5,7},{7,5},{8,10},{10,8},{12,... | collective-permute-start | bytes 49160 | tf_op jit(solution)/shard_map/ppermute | solution.py:46

commit v28 on v24

--- a/solution.py
+++ b/solution.py
@@ -332,7 +332,7 @@
 def add_up_along(total):
     n = lax.axis_size("fsdp")
     if n == 4:
-        return exchange(total, ("fsdp", "proto"), lambda odd: (2 + odd, 0), lambda odd: (1, 0))
+        return exchange(total, ("fsdp", "proto"), lambda odd: (1 + 2 * odd, 0), lambda odd: (2, 0))
     if n <= DIRECT:
         return add_up([total, *[swap(total, "fsdp", k) for k in range(1, n)]])
     return add_up([lax.all_to_all(jnp.broadcast_to(total[None], (n, *total.shape)), "fsdp", 0, 0, tiled=True)])

time: 43.8 us -> 43.4 us (level)
  waiting for transfers between devices: 10.8 us -> 9.61 us
  starting transfers between devices: 16.9 us -> 17.6 us
    ppermute x4, waiting for transfers between devices: 4.65 us -> 3.52 us  [permute(): return lax.ppermute(total, axes, pairs)]
    ppermute x13, starting transfers between devices: 11.3 us -> 12.3 us  [swap(): lax.ppermute(block, axis, [(i, i ^ apart) for i in range(lax.axis_size(ax...]
  transfers between devices with their start and end apart: 17 -> 17, of which waited for: 11 -> 12; matrix products, arithmetic and copies ran while one was open for 0% -> 0% of each run, Pallas kernels for 23% -> 23%
where the time goes in v28:
time: 43.4 us; the launch traced here: 43.2 us
  starting transfers between devices  17.6 us (41%)
  Pallas kernels  15.2 us (35%)
  waiting for transfers between devices  9.61 us (22%)
  between operations  0.75 us (2%)
    pallas_call x13, Pallas kernels, call(): pl.pallas_call(kernel, out_shape=out_shape, compiler_params=pltpu.Compile...  15.2 us
    ppermute x13, starting transfers between devices, swap(): lax.ppermute(block, axis, [(i, i ^ apart) for i in range(lax.axis_size(ax...  12.3 us
    ppermute x13, waiting for transfers between devices, swap(): lax.ppermute(block, axis, [(i, i ^ apart) for i in range(lax.axis_size(ax...  6.09 us
    ppermute x4, starting transfers between devices, permute(): return lax.ppermute(total, axes, pairs)  5.34 us
    ppermute x4, waiting for transfers between devices, permute(): return lax.ppermute(total, axes, pairs)  3.52 us
  transfers between devices with their start and end apart: 17, of which 12 were waited for; matrix products, arithmetic and copies ran while one was open for 0% of the time, Pallas kernels for 23%

profile of v28, /device:TPU:0, one launch (start us, length us, event | category | flops | bytes accessed | tf_op | source)
XLA Modules:
  0.0 43.2 jit_solution(1685184264884638369)
XLA Ops:
  0.6 3.0 %collective-permute-start = (s32[1,256]{1,0:T(1,128)}, s32[1,256]{1,0:T(1,128)S(1)}, u32[]{:S(2)}, u32[]{:S(2)}) collective-permute-start(s32[1,256]{1,0:T(1,128)} %param.10), channel_id=1, source_target_pairs={{0,1},{1,0},{2,3},{3,2},{4,5},{5,4},{6,7},{7,6},{8,9},{9,8},{10,11... | collective-permute-start | bytes 3080 | tf_op jit(solution)/shard_map/ppermute | solution.py:46
  3.6 0.9 %fetch.1 = (bf16[192,128]{1,0:T(8,128)(2,1)S(1)}, bf16[192,256]{1,0:T(8,128)(2,1)S(1)}) custom-call(bf16[192,256]{1,0:T(8,128)(2,1)} %bitcast.7, bf16[192,256]{1,0:T(8,128)(2,1)} %bitcast.8), custom_call_target="tpu_custom_call" | custom-call | flops 1 | bytes 1 | tf_op jit(solution)/shard_map/fetch/pallas_call | solution.py:35
  4.6 0.8 %collective-permute-done.index_ref = s32[1,256]{1,0:T(1,128)S(1)} collective-permute-done((s32[1,256]{1,0:T(1,128)}, s32[1,256]{1,0:T(1,128)S(1)}, u32[]{:S(2)}, u32[]{:S(2)}) %collective-permute-start) | collective-permute-done | bytes 1056 | tf_op jit(solution)/shard_map/ppermute | solution.py:46
  5.6 2.1 %collective-permute-start.4 = (bf16[2,192,128]{2,1,0:T(8,128)(2,1)S(1)}, bf16[2,192,128]{2,1,0:T(8,128)(2,1)S(1)}, u32[]{:S(2)}, u32[]{:S(2)}) collective-permute-start(bf16[2,192,128]{2,1,0:T(8,128)(2,1)S(1)} %pack.1.refs_0_), channel_id=1, source_target_pairs={{0,1},{1,0},{2,3},{3,2},{4,5},{5,4},{6,7},{7,6},{8,9},{9,8},{10,11... | collective-permute-start | bytes 294920 | tf_op jit(solution)/shard_map/ppermute | solution.py:46
  7.7 3.6 %collective-permute-start.3 = (bf16[2,192,128]{2,1,0:T(8,128)(2,1)S(1)}, bf16[2,192,128]{2,1,0:T(8,128)(2,1)S(1)}, u32[]{:S(2)}, u32[]{:S(2)}) collective-permute-start(bf16[2,192,128]{2,1,0:T(8,128)(2,1)S(1)} %pack.1.refs_0_), channel_id=1, source_target_pairs={{0,24},{8,16},{16,8},{24,0},{1,25},{9,17},{17,9},{25,1},{2,26},{10... | collective-permute-start | bytes 294920 | tf_op jit(solution)/shard_map/ppermute | solution.py:46
  11.3 0.8 %collective-permute-start.1 = (bf16[2,192,128]{2,1,0:T(8,128)(2,1)S(1)}, bf16[2,192,128]{2,1,0:T(8,128)(2,1)S(1)}, u32[]{:S(2)}, u32[]{:S(2)}) collective-permute-start(bf16[2,192,128]{2,1,0:T(8,128)(2,1)S(1)} %pack.1.refs_0_), channel_id=1, source_target_pairs={{0,8},{8,0},{16,24},{24,16},{1,9},{9,1},{17,25},{25,17},{2,10},{10... | collective-permute-start | bytes 294920 | tf_op jit(solution)/shard_map/ppermute | solution.py:46
  12.1 5.1 %prep.1 = (f32[192,4096]{1,0:T(8,128)}, bf16[2048,256]{1,0:T(8,128)(2,1)S(1)}, bf16[2048,256]{1,0:T(8,128)(2,1)S(1)}, f32[192,2048]{1,0:T(8,128)S(1)}, f32[1,2048]{1,0:T(1,128)S(1)}, /*index=5*/f32[1,128]{1,0:T(1,128)S(1)}) custom-call(f32[192,4096]{1,0:T(8,128)} %teacher_hbm.1, f32[192,4096]{1,0:T(8,128)} %student_hbm.1, f32[1,16384]{1,0:T(1,128)} %bitcast.9), custom_call_target="tpu_custom_call" | custom-call | flops 1 | bytes 1 | tf_op jit(solution)/shard_map/prep/pallas_call | solution.py:35
  17.2 1.0 %collective-permute-done.2.refs_2_ = bf16[2,192,128]{2,1,0:T(8,128)(2,1)S(1)} collective-permute-done((bf16[2,192,128]{2,1,0:T(8,128)(2,1)S(1)}, bf16[2,192,128]{2,1,0:T(8,128)(2,1)S(1)}, u32[]{:S(2)}, u32[]{:S(2)}) %collective-permute-start.2) | collective-permute-done | bytes 98336 | tf_op jit(solution)/shard_map/ppermute | solution.py:46
  18.3 0.6 %collective-permute-start.8 = (bf16[2,2,208,128]{3,2,1,0:T(8,128)(2,1)S(1)}, bf16[2,2,208,128]{3,2,1,0:T(8,128)(2,1)S(1)}, u32[]{:S(2)}, u32[]{:S(2)}) collective-permute-start(bf16[2,2,208,128]{3,2,1,0:T(8,128)(2,1)S(1)} %get-tuple-element.38), channel_id=1, source_target_pairs={{0,1},{1,0},{2,3},{3,2},{4,5},{5,4},{6,7},{7,6},{8,9},{9,8},{10,11... | collective-permute-start | bytes 638984 | tf_op jit(solution)/shard_map/ppermute | solution.py:46
  19.9 1.3 %scores.4 = (bf16[2048,4096]{1,0:T(8,128)(2,1)S(1)}, bf16[512,192]{1,0:T(8,128)(2,1)S(1)}, f32[2,512]{1,0:T(2,128)S(1)}) custom-call(bf16[4,2,192,128]{3,2,1,0:T(8,128)(2,1)S(1)} %get-tuple-element.30.refs_0_, bf16[2048,256]{1,0:T(8,128)(2,1)S(1)} %get-tuple-element.31.refs_1_.refs_2_.refs_4_, ...), custom_call_target="tpu_custom_call" | custom-call | flops 1 | bytes 1 | tf_op jit(solution)/shard_map/scores/pallas_call | solution.py:35
  21.2 1.3 %scores.5 = (bf16[2048,4096]{1,0:T(8,128)(2,1)S(1)}, bf16[512,192]{1,0:T(8,128)(2,1)S(1)}, f32[2,512]{1,0:T(2,128)S(1)}) custom-call(bf16[2,2,192,128]{3,2,1,0:T(8,128)(2,1)S(1)} %collective-permute-done.5.refs_0_, bf16[2,2,192,128]{3,2,1,0:T(8,128)(2,1)S(1)} %collective-permute-done.6.refs_1_, ...), custom_call_target="tpu_custom_call", output_to_operand_aliasing={{0}: (5, {})} | custom-call | flops 1 | bytes 1 | tf_op jit(solution)/shard_map/scores/pallas_call | solution.py:35
  22.5 1.6 %collective-permute-done.7.refs_1_ = bf16[2,192,128]{2,1,0:T(8,128)(2,1)S(1)} collective-permute-done((bf16[2,192,128]{2,1,0:T(8,128)(2,1)S(1)}, bf16[2,192,128]{2,1,0:T(8,128)(2,1)S(1)}, u32[]{:S(2)}, u32[]{:S(2)}) %collective-permute-start.7) | collective-permute-done | bytes 98336 | tf_op jit(solution)/shard_map/ppermute | solution.py:46
  24.1 0.5 %collective-permute-done.8.refs_2_ = bf16[2,2,208,128]{3,2,1,0:T(8,128)(2,1)S(1)} collective-permute-done((bf16[2,2,208,128]{3,2,1,0:T(8,128)(2,1)S(1)}, bf16[2,2,208,128]{3,2,1,0:T(8,128)(2,1)S(1)}, u32[]{:S(2)}, u32[]{:S(2)}) %collective-permute-start.8) | collective-permute-done | bytes 213024 | tf_op jit(solution)/shard_map/ppermute | solution.py:46
  24.8 1.3 %scores.6 = (bf16[2048,4096]{1,0:T(8,128)(2,1)S(1)}, bf16[512,192]{1,0:T(8,128)(2,1)S(1)}, f32[2,512]{1,0:T(2,128)S(1)}) custom-call(bf16[4,2,192,128]{3,2,1,0:T(8,128)(2,1)S(1)} %join.3.refs_0_, bf16[2048,256]{1,0:T(8,128)(2,1)S(1)} %get-tuple-element.31.refs_1_.refs_2_.refs_4_, ...), custom_call_target="tpu_custom_call", output_to_operand_aliasing={{0}: (4, {})} | custom-call | flops 1 | bytes 1 | tf_op jit(solution)/shard_map/scores/pallas_call | solution.py:35
  26.5 1.3 %scores.7 = (bf16[2048,4096]{1,0:T(8,128)(2,1)S(1)}, bf16[512,192]{1,0:T(8,128)(2,1)S(1)}, f32[4,1024]{1,0:T(4,128)S(1)}) custom-call(f32[2,512]{1,0:T(2,128)S(1)} %get-tuple-element.33.refs_0_, f32[2,512]{1,0:T(2,128)S(1)} %get-tuple-element.37.refs_3_.refs_1_, f32[2,512]{1,0:T(2,128)S(1)} %get-tuple-element.40.refs_2_, ...), custom_call_target="tpu_custom_call", output_to_operand_aliasing={{0}: (7, {})} | custom-call | flops 1 | bytes 1 | tf_op jit(solution)/shard_map/scores/pallas_call | solution.py:35
  28.0 1.0 %collective-permute-done.10.refs_1_ = f32[4,1024]{1,0:T(4,128)S(1)} collective-permute-done((f32[4,1024]{1,0:T(4,128)S(1)}, f32[4,1024]{1,0:T(4,128)S(1)}, u32[]{:S(2)}, u32[]{:S(2)}) %collective-permute-start.10) | collective-permute-done | bytes 16416 | tf_op jit(solution)/shard_map/ppermute | solution.py:46
  29.2 2.7 %collective-permute-start.13 = (f32[4,1024]{1,0:T(4,128)S(1)}, f32[4,1024]{1,0:T(4,128)S(1)}, u32[]{:S(2)}, u32[]{:S(2)}) collective-permute-start(f32[4,1024]{1,0:T(4,128)S(1)} %relay.3.refs_0_), channel_id=1, source_target_pairs={{0,16},{2,18},{4,20},{6,22},{8,24},{10,26},{12,28},{14,30},{16,0},... | collective-permute-start | bytes 49160 | tf_op jit(solution)/shard_map/ppermute | solution.py:307
  31.9 1.0 %collective-permute-done.11.refs_1_ = f32[4,1024]{1,0:T(4,128)S(1)} collective-permute-done((f32[4,1024]{1,0:T(4,128)S(1)}, f32[4,1024]{1,0:T(4,128)S(1)}, u32[]{:S(2)}, u32[]{:S(2)}) %collective-permute-start.11) | collective-permute-done | bytes 16416 | tf_op jit(solution)/shard_map/ppermute | solution.py:307
  32.9 0.9 %collective-permute-start.12 = (f32[4,1024]{1,0:T(4,128)S(1)}, f32[4,1024]{1,0:T(4,128)S(1)}, u32[]{:S(2)}, u32[]{:S(2)}) collective-permute-start(f32[4,1024]{1,0:T(4,128)S(1)} %collective-permute-done.11.refs_1_), channel_id=1, source_target_pairs={{0,2},{2,0},{4,6},{6,4},{1,3},{3,1},{5,7},{7,5},{8,10},{10,8},{12,... | collective-permute-start | bytes 49160 | tf_op jit(solution)/shard_map/ppermute | solution.py:46
  34.7 1.0 %collective-permute-start.14 = (f32[4,1024]{1,0:T(4,128)S(1)}, f32[4,1024]{1,0:T(4,128)S(1)}, u32[]{:S(2)}, u32[]{:S(2)}) collective-permute-start(f32[4,1024]{1,0:T(4,128)S(1)} %relay.4.refs_0_), channel_id=1, source_target_pairs={{0,1},{1,0},{2,7},{3,6},{4,5},{5,4},{6,3},{7,2},{8,9},{9,8},{10,15... | collective-permute-start | bytes 49160 | tf_op jit(solution)/shard_map/ppermute | solution.py:307
  35.7 1.5 %collective-permute-start.16 = (f32[4,1024]{1,0:T(4,128)S(1)}, f32[4,1024]{1,0:T(4,128)S(1)}, u32[]{:S(2)}, u32[]{:S(2)}) collective-permute-start(f32[4,1024]{1,0:T(4,128)S(1)} %relay.4.refs_0_), channel_id=1, source_target_pairs={{0,4},{1,5},{2,6},{3,7},{4,0},{5,1},{6,2},{7,3},{8,12},{9,13},{10,... | collective-permute-start | bytes 49160 | tf_op jit(solution)/shard_map/ppermute | solution.py:307
  37.2 1.3 %collective-permute-done.14.refs_1_ = f32[4,1024]{1,0:T(4,128)S(1)} collective-permute-done((f32[4,1024]{1,0:T(4,128)S(1)}, f32[4,1024]{1,0:T(4,128)S(1)}, u32[]{:S(2)}, u32[]{:S(2)}) %collective-permute-start.14) | collective-permute-done | bytes 16416 | tf_op jit(solution)/shard_map/ppermute | solution.py:307
  38.6 0.8 %collective-permute-done.16.refs_3_ = f32[4,1024]{1,0:T(4,128)S(1)} collective-permute-done((f32[4,1024]{1,0:T(4,128)S(1)}, f32[4,1024]{1,0:T(4,128)S(1)}, u32[]{:S(2)}, u32[]{:S(2)}) %collective-permute-start.16) | collective-permute-done | bytes 16416 | tf_op jit(solution)/shard_map/ppermute | solution.py:307
  39.7 3.5 %gradient.1 = f32[192,2048]{1,0:T(8,128)} custom-call(f32[4,1024]{1,0:T(4,128)S(1)} %relay.5.total_ref, f32[1,128]{1,0:T(1,128)S(1)} %get-tuple-element.29.refs_5_.refs_3_.refs_4_.refs_6_.peak_ref, f32[192,2048]{1,0:T(8,128)S(1)} %get-tuple-element.43.weight_unit, f32[1,2048]{1,0:T(1,128)S(1)} %get-tuple-element.44.weight_scale, ...), custom_call_target="tpu_custom_call" | custom-call | flops 1 | bytes 1 | tf_op jit(solution)/shard_map/gradient/pallas_call | solution.py:35
  (23 shorter events, 3.3 us)
Async XLA Ops:
  0.6 4.8 %collective-permute-start = (s32[1,256]{1,0:T(1,128)}, s32[1,256]{1,0:T(1,128)S(1)}, u32[]{:S(2)}, u32[]{:S(2)}) collective-permute-start(s32[1,256]{1,0:T(1,128)} %param.10), channel_id=1, source_target_pairs={{0,1},{1,0},{2,3},{3,2},{4,5},{5,4},{6,7},{7,6},{8,9},{9,8},{10,11... | collective-permute-start | bytes 3080 | tf_op jit(solution)/shard_map/ppermute | solution.py:46
  5.6 11.6 %collective-permute-start.4 = (bf16[2,192,128]{2,1,0:T(8,128)(2,1)S(1)}, bf16[2,192,128]{2,1,0:T(8,128)(2,1)S(1)}, u32[]{:S(2)}, u32[]{:S(2)}) collective-permute-start(bf16[2,192,128]{2,1,0:T(8,128)(2,1)S(1)} %pack.1.refs_0_), channel_id=1, source_target_pairs={{0,1},{1,0},{2,3},{3,2},{4,5},{5,4},{6,7},{7,6},{8,9},{9,8},{10,11... | collective-permute-start | bytes 294920 | tf_op jit(solution)/shard_map/ppermute | solution.py:46
  7.7 9.5 %collective-permute-start.3 = (bf16[2,192,128]{2,1,0:T(8,128)(2,1)S(1)}, bf16[2,192,128]{2,1,0:T(8,128)(2,1)S(1)}, u32[]{:S(2)}, u32[]{:S(2)}) collective-permute-start(bf16[2,192,128]{2,1,0:T(8,128)(2,1)S(1)} %pack.1.refs_0_), channel_id=1, source_target_pairs={{0,24},{8,16},{16,8},{24,0},{1,25},{9,17},{17,9},{25,1},{2,26},{10... | collective-permute-start | bytes 294920 | tf_op jit(solution)/shard_map/ppermute | solution.py:46
  11.3 6.9 %collective-permute-start.2 = (bf16[2,192,128]{2,1,0:T(8,128)(2,1)S(1)}, bf16[2,192,128]{2,1,0:T(8,128)(2,1)S(1)}, u32[]{:S(2)}, u32[]{:S(2)}) collective-permute-start(bf16[2,192,128]{2,1,0:T(8,128)(2,1)S(1)} %pack.1.refs_0_), channel_id=1, source_target_pairs={{0,16},{8,24},{16,0},{24,8},{1,17},{9,25},{17,1},{25,9},{2,18},{10... | collective-permute-start | bytes 294920 | tf_op jit(solution)/shard_map/ppermute | solution.py:46
  11.3 6.9 %collective-permute-start.1 = (bf16[2,192,128]{2,1,0:T(8,128)(2,1)S(1)}, bf16[2,192,128]{2,1,0:T(8,128)(2,1)S(1)}, u32[]{:S(2)}, u32[]{:S(2)}) collective-permute-start(bf16[2,192,128]{2,1,0:T(8,128)(2,1)S(1)} %pack.1.refs_0_), channel_id=1, source_target_pairs={{0,8},{8,0},{16,24},{24,16},{1,9},{9,1},{17,25},{25,17},{2,10},{10... | collective-permute-start | bytes 294920 | tf_op jit(solution)/shard_map/ppermute | solution.py:46
  18.3 6.3 %collective-permute-start.8 = (bf16[2,2,208,128]{3,2,1,0:T(8,128)(2,1)S(1)}, bf16[2,2,208,128]{3,2,1,0:T(8,128)(2,1)S(1)}, u32[]{:S(2)}, u32[]{:S(2)}) collective-permute-start(bf16[2,2,208,128]{3,2,1,0:T(8,128)(2,1)S(1)} %get-tuple-element.38), channel_id=1, source_target_pairs={{0,1},{1,0},{2,3},{3,2},{4,5},{5,4},{6,7},{7,6},{8,9},{9,8},{10,11... | collective-permute-start | bytes 638984 | tf_op jit(solution)/shard_map/ppermute | solution.py:46
  18.9 2.3 %collective-permute-start.5 = (bf16[2,2,192,128]{3,2,1,0:T(8,128)(2,1)S(1)}, bf16[2,2,192,128]{3,2,1,0:T(8,128)(2,1)S(1)}, u32[]{:S(2)}, u32[]{:S(2)}) collective-permute-start(bf16[2,2,192,128]{3,2,1,0:T(8,128)(2,1)S(1)} %get-tuple-element.34), channel_id=1, source_target_pairs={{0,2},{2,0},{4,6},{6,4},{1,3},{3,1},{5,7},{7,5},{8,10},{10,8},{12,... | collective-permute-start | bytes 589832 | tf_op jit(solution)/shard_map/ppermute | solution.py:46
  18.9 2.3 %collective-permute-start.6 = (bf16[2,2,192,128]{3,2,1,0:T(8,128)(2,1)S(1)}, bf16[2,2,192,128]{3,2,1,0:T(8,128)(2,1)S(1)}, u32[]{:S(2)}, u32[]{:S(2)}) collective-permute-start(bf16[2,2,192,128]{3,2,1,0:T(8,128)(2,1)S(1)} %get-tuple-element.35), channel_id=1, source_target_pairs={{0,2},{2,0},{4,6},{6,4},{1,3},{3,1},{5,7},{7,5},{8,10},{10,8},{12,... | collective-permute-start | bytes 589832 | tf_op jit(solution)/shard_map/ppermute | solution.py:46
  19.4 4.7 %collective-permute-start.7 = (bf16[2,192,128]{2,1,0:T(8,128)(2,1)S(1)}, bf16[2,192,128]{2,1,0:T(8,128)(2,1)S(1)}, u32[]{:S(2)}, u32[]{:S(2)}) collective-permute-start(bf16[2,192,128]{2,1,0:T(8,128)(2,1)S(1)} %collective-permute-done.4.refs_4_.refs_0_), channel_id=1, source_target_pairs={{0,8},{8,0},{16,24},{24,16},{1,9},{9,1},{17,25},{25,17},{2,10},{10... | collective-permute-start | bytes 294920 | tf_op jit(solution)/shard_map/ppermute | solution.py:46
  24.7 1.8 %collective-permute-start.9 = (bf16[4,2,192,128]{3,2,1,0:T(8,128)(2,1)S(1)}, bf16[4,2,192,128]{3,2,1,0:T(8,128)(2,1)S(1)}, u32[]{:S(2)}, u32[]{:S(2)}) collective-permute-start(bf16[4,2,192,128]{3,2,1,0:T(8,128)(2,1)S(1)} %join.3.refs_0_), channel_id=1, source_target_pairs={{0,2},{2,0},{4,6},{6,4},{1,3},{3,1},{5,7},{7,5},{8,10},{10,8},{12,... | collective-permute-start | bytes 1179656 | tf_op jit(solution)/shard_map/ppermute | solution.py:46
  27.8 1.2 %collective-permute-start.10 = (f32[4,1024]{1,0:T(4,128)S(1)}, f32[4,1024]{1,0:T(4,128)S(1)}, u32[]{:S(2)}, u32[]{:S(2)}) collective-permute-start(f32[4,1024]{1,0:T(4,128)S(1)} %get-tuple-element.42.refs_0_), channel_id=1, source_target_pairs={{0,2},{2,0},{4,6},{6,4},{1,3},{3,1},{5,7},{7,5},{8,10},{10,8},{12,... | collective-permute-start | bytes 49160 | tf_op jit(solution)/shard_map/ppermute | solution.py:46
  29.1 3.8 %collective-permute-start.11 = (f32[4,1024]{1,0:T(4,128)S(1)}, f32[4,1024]{1,0:T(4,128)S(1)}, u32[]{:S(2)}, u32[]{:S(2)}) collective-permute-start(f32[4,1024]{1,0:T(4,128)S(1)} %relay.3.refs_0_), channel_id=1, source_target_pairs={{0,8},{2,26},{4,12},{6,30},{8,0},{10,18},{12,4},{14,22},{16,24},{1... | collective-permute-start | bytes 49160 | tf_op jit(solution)/shard_map/ppermute | solution.py:307
  29.2 5.1 %collective-permute-start.13 = (f32[4,1024]{1,0:T(4,128)S(1)}, f32[4,1024]{1,0:T(4,128)S(1)}, u32[]{:S(2)}, u32[]{:S(2)}) collective-permute-start(f32[4,1024]{1,0:T(4,128)S(1)} %relay.3.refs_0_), channel_id=1, source_target_pairs={{0,16},{2,18},{4,20},{6,22},{8,24},{10,26},{12,28},{14,30},{16,0},... | collective-permute-start | bytes 49160 | tf_op jit(solution)/shard_map/ppermute | solution.py:307
  32.9 1.8 %collective-permute-start.12 = (f32[4,1024]{1,0:T(4,128)S(1)}, f32[4,1024]{1,0:T(4,128)S(1)}, u32[]{:S(2)}, u32[]{:S(2)}) collective-permute-start(f32[4,1024]{1,0:T(4,128)S(1)} %collective-permute-done.11.refs_1_), channel_id=1, source_target_pairs={{0,2},{2,0},{4,6},{6,4},{1,3},{3,1},{5,7},{7,5},{8,10},{10,8},{12,... | collective-permute-start | bytes 49160 | tf_op jit(solution)/shard_map/ppermute | solution.py:46
  34.7 3.8 %collective-permute-start.14 = (f32[4,1024]{1,0:T(4,128)S(1)}, f32[4,1024]{1,0:T(4,128)S(1)}, u32[]{:S(2)}, u32[]{:S(2)}) collective-permute-start(f32[4,1024]{1,0:T(4,128)S(1)} %relay.4.refs_0_), channel_id=1, source_target_pairs={{0,1},{1,0},{2,7},{3,6},{4,5},{5,4},{6,3},{7,2},{8,9},{9,8},{10,15... | collective-permute-start | bytes 49160 | tf_op jit(solution)/shard_map/ppermute | solution.py:307
  35.7 3.7 %collective-permute-start.16 = (f32[4,1024]{1,0:T(4,128)S(1)}, f32[4,1024]{1,0:T(4,128)S(1)}, u32[]{:S(2)}, u32[]{:S(2)}) collective-permute-start(f32[4,1024]{1,0:T(4,128)S(1)} %relay.4.refs_0_), channel_id=1, source_target_pairs={{0,4},{1,5},{2,6},{3,7},{4,0},{5,1},{6,2},{7,3},{8,12},{9,13},{10,... | collective-permute-start | bytes 49160 | tf_op jit(solution)/shard_map/ppermute | solution.py:307
  38.5 1.2 %collective-permute-start.15 = (f32[4,1024]{1,0:T(4,128)S(1)}, f32[4,1024]{1,0:T(4,128)S(1)}, u32[]{:S(2)}, u32[]{:S(2)}) collective-permute-start(f32[4,1024]{1,0:T(4,128)S(1)} %collective-permute-done.14.refs_1_), channel_id=1, source_target_pairs={{0,2},{2,0},{4,6},{6,4},{1,3},{3,1},{5,7},{7,5},{8,10},{10,8},{12,... | collective-permute-start | bytes 49160 | tf_op jit(solution)/shard_map/ppermute | solution.py:46
